TPU v7x, 32 devices: a whole 2x2x4 slice. The times are simulated.
32 devices in a mesh: row: 8 (over y, x, core), col: 4 (over z).
Axes of the slice: x: 2, y: 2, z: 4, core: 2. Of those that a mesh axis runs over, the one named last changes fastest.
Arguments:
- block_values: bfloat16 [8, 4, 192, 128, 128], P('row', 'col'), may hold values from -0.0625 to 0.0625
- block_rows: int32 [8, 4, 192], P('row', 'col'), may hold values from 0 to 511, as said below
- block_cols: int32 [8, 4, 192], P('row', 'col'), may hold values from 0 to 511, as said below
- block_counts: int32 [8, 4], P('row', 'col'), may hold values from 48 to 192, as said below
- precond: float32 [4, 128, 128, 128], P('col', 'row')
- right_side: float32 [4, 128, 32, 128], P('col', 'row'), may hold values from -6 to 6
Outputs:
- solution: float32 [4, 128, 32, 128], P('col', 'row')
Inputs may be any that keep to these rules, and one draw needn't show every extreme that they name: `block_rows`: the block rows of device (r, c) lie in [c * 128, (c + 1) * 128); positions may repeat; for each j, at most 36 of a device's 192 slots have (row mod 128) // 16 == j, and in every index of col some j has exactly 36 such slots on every device. `block_cols`: every block column q of device (r, c) has (q mod 128) // 16 == r; positions may repeat. `block_counts`: slots at or past a device's count are unused; some device uses all 192 slots.
All inputs are finite; a program needn't handle non-finite values.
Results may differ from a plain program's by a relative error of at most 0.00073.
Values may be sent and summed in bfloat16 or wider, within the bound.
No kernel may reach another device: no remote copies, remote signals or barrier semaphores. Data moves between devices by JAX's collectives and lax.ppermute only.
A program may use at most 64 MiB of HBM per device.

v0:
```python
import jax
import jax.numpy as jnp
from jax import lax
from jax.sharding import PartitionSpec as P

ITERS = 3


def apply_blocks(matrix, field):
    return jnp.einsum("poi,pki->pko", matrix, field, precision=lax.Precision.HIGHEST)


def block_terms(vectors, values, col_local):
    gathered = vectors[col_local]
    return jnp.einsum("ski,soi->sko", gathered, values, preferred_element_type=jnp.float32)


def per_device(block_values, block_rows, block_cols, block_counts, precond, right_side):
    owned = right_side.shape[1]
    row_devices = lax.axis_size("row")
    group = owned * row_devices
    slot_total = block_values.shape[2]
    values = block_values[0, 0]
    row_local = block_rows[0, 0] % group
    col_global = block_cols[0, 0]
    col_local = col_global // group * owned + col_global % owned
    used = block_counts[0, 0]
    live = jnp.arange(slot_total, dtype=jnp.int32) < used
    inverse = precond[0]
    rhs_own = right_side[0]
    solution = apply_blocks(inverse, rhs_own)
    for step in range(ITERS):
        pieces = lax.all_gather(solution.astype(jnp.bfloat16)[None], "col", axis=1, tiled=True)[0]
        terms = block_terms(pieces, values, col_local)
        terms = jnp.where(live[:, None, None], terms, jnp.zeros_like(terms))
        partial_value = jax.ops.segment_sum(terms, row_local, num_segments=group)
        product = lax.psum_scatter(partial_value, "row", scatter_dimension=0, tiled=True)
        residual = rhs_own - solution - product
        solution = solution + apply_blocks(inverse, residual)
    return solution[None]


def solution(mesh):
    placed = (
        P("row", "col", None, None, None),
        P("row", "col", None),
        P("row", "col", None),
        P("row", "col"),
        P("col", "row", None, None),
        P("col", "row", None, None),
    )
    return jax.shard_map(
        per_device,
        mesh=mesh,
        in_specs=placed,
        out_specs=P("col", "row", None, None),
        check_vma=False,
    )
```

profile of v0, /device:TPU:0, one launch (start us, length us, event | category | flops | bytes accessed | tf_op | source)
XLA Modules:
  0.0 288.2 jit_solution(14893506755444110047)
XLA Ops:
  6.5 0.8 and_select_fusion.2
  7.3 0.5 copy-done
  7.8 3.4 %fusion.30 = (bf16[16,32,128]{2,1,0:T(8,128)(2,1)S(1)}, f32[16,32,128]{2,1,0:T(8,128)}) fusion(f32[1,16,128,128]{3,2,1,0:T(8,128)S(1)} %copy-done, f32[1,16,32,128]{3,2,1,0:T(8,128)} %param.11), kind=kOutput, calls=%fused_computation.46 | convolution fusion | flops 100728832 | bytes 1703936 | tf_op jit(solution)/shard_map/poi,pki->pko/dot_general | solution.py:10
  11.2 17.3 %all-gather = bf16[64,32,128]{2,1,0:T(8,128)(2,1)S(1)} all-gather(bf16[16,32,128]{2,1,0:T(8,128)(2,1)S(1)} %get-tuple-element.5), channel_id=2, replica_groups=mesh['row'=8,'col'=4] {'col'}, dimensions={0}, use_global_device_ids=true | all-gather | bytes 655360 | tf_op jit(solution)/shard_map/all_gather | solution.py:33
  29.2 0.9 gather_fusion
  30.1 7.8 %fusion.6 = f32[192,32,128]{2,1,0:T(8,128)} fusion(bf16[192,32,128]{2,1,0:T(8,128)(2,1)S(1)} %gather_fusion, bf16[1,1,192,128,128]{4,3,2,1,0:T(8,128)(2,1)} %param.6, pred[192]{0:T(512)(128)(4,1)S(1)} %iota_compare_fusion), kind=kOutput, calls=%fused_computation.12 | convolution fusion | flops 202113024 | bytes 11010240 | tf_op jit(solution)/shard_map/ski,soi->sko/dot_general | solution.py:15
  37.9 0.2 broadcast.156.clone
  38.2 17.3 %scatter_fusion = f32[128,32,128]{2,1,0:T(8,128)S(1)} fusion(f32[128,32,128]{2,1,0:T(8,128)S(1)} %broadcast.156.clone, s32[192]{0:T(256)S(1)} %bitcast.73, f32[192,32,128]{2,1,0:T(8,128)} %fusion.6), kind=kCustom, calls=%fused_computation.3 | custom fusion | flops 786432 | bytes 9437952 | tf_op jit(solution)/shard_map/scatter-add | solution.py:36
  55.5 1.3 copy-done.2
  56.8 0.0 reduce-scatter.4.cloned.1.call-update
  56.9 0.0 reduce-scatter.6.cloned.1.call-start
  56.9 43.1 %reduce-scatter.4.cloned.1.call-done = f32[16,32,128]{2,1,0:T(8,128)} async-done(((f32[128,32,128]{2,1,0:T(8,128)}), f32[16,32,128]{2,1,0:T(8,128)}) %reduce-scatter.4.cloned.1.call-update) | async-done | bytes 262160 | tf_op jit(solution)/shard_map/reduce_scatter | solution.py:37
  100.0 3.6 %fusion.31 = (bf16[16,32,128]{2,1,0:T(8,128)(2,1)S(1)}, f32[16,32,128]{2,1,0:T(8,128)}) fusion(f32[16,32,128]{2,1,0:T(8,128)} %get-tuple-element.6, f32[1,16,128,128]{3,2,1,0:T(8,128)S(1)} %copy-done, f32[16,32,128]{2,1,0:T(8,128)} %reduce-scatter.4.cloned.1.call-done, f32[1,16,32,128]{3,2,1,0:T(8,128)S(1)} %copy-done.4), kind=kOutput, calls=%fused_computation.47 | convolution fusion | flops 100925440 | bytes 2228224 | tf_op jit(solution)/shard_map/poi,pki->pko/dot_general | solution.py:10
  103.6 15.6 %all-gather.1 = bf16[64,32,128]{2,1,0:T(8,128)(2,1)S(1)} all-gather(bf16[16,32,128]{2,1,0:T(8,128)(2,1)S(1)} %get-tuple-element.7), channel_id=3, replica_groups=mesh['row'=8,'col'=4] {'col'}, dimensions={0}, use_global_device_ids=true | all-gather | bytes 655360 | tf_op jit(solution)/shard_map/all_gather | solution.py:33
  119.2 0.9 gather_fusion.1
  120.1 7.8 %fusion.9 = f32[192,32,128]{2,1,0:T(8,128)} fusion(bf16[192,32,128]{2,1,0:T(8,128)(2,1)S(1)} %gather_fusion.1, bf16[1,1,192,128,128]{4,3,2,1,0:T(8,128)(2,1)} %param.6, pred[192]{0:T(512)(128)(4,1)S(1)} %iota_compare_fusion), kind=kOutput, calls=%fused_computation.13 | convolution fusion | flops 202113024 | bytes 11010240 | tf_op jit(solution)/shard_map/ski,soi->sko/dot_general | solution.py:15
  127.9 0.2 broadcast.156.clone.1
  128.2 17.3 %scatter_fusion.1 = f32[128,32,128]{2,1,0:T(8,128)S(1)} fusion(f32[128,32,128]{2,1,0:T(8,128)S(1)} %broadcast.156.clone.1, s32[192]{0:T(256)S(1)} %bitcast.74, f32[192,32,128]{2,1,0:T(8,128)} %fusion.9), kind=kCustom, calls=%fused_computation.4 | custom fusion | flops 786432 | bytes 9437952 | tf_op jit(solution)/shard_map/scatter-add | solution.py:36
  145.5 1.3 copy-done.3
  146.8 0.0 reduce-scatter.6.cloned.1.call-update
  146.8 0.0 reduce-scatter.8.cloned.1.call-start
  146.9 42.1 %reduce-scatter.6.cloned.1.call-done = f32[16,32,128]{2,1,0:T(8,128)} async-done(((f32[128,32,128]{2,1,0:T(8,128)}), f32[16,32,128]{2,1,0:T(8,128)}) %reduce-scatter.6.cloned.1.call-update) | async-done | bytes 262160 | tf_op jit(solution)/shard_map/reduce_scatter | solution.py:37
  189.0 3.6 %fusion.32 = (bf16[16,32,128]{2,1,0:T(8,128)(2,1)S(1)}, f32[16,32,128]{2,1,0:T(8,128)}) fusion(f32[16,32,128]{2,1,0:T(8,128)} %get-tuple-element.8, f32[1,16,128,128]{3,2,1,0:T(8,128)S(1)} %copy-done, f32[16,32,128]{2,1,0:T(8,128)} %reduce-scatter.6.cloned.1.call-done, f32[1,16,32,128]{3,2,1,0:T(8,128)S(1)} %copy-done.4), kind=kOutput, calls=%fused_computation.48 | convolution fusion | flops 100925440 | bytes 2228224 | tf_op jit(solution)/shard_map/poi,pki->pko/dot_general | solution.py:10
  192.6 15.8 %all-gather.2 = bf16[64,32,128]{2,1,0:T(8,128)(2,1)S(1)} all-gather(bf16[16,32,128]{2,1,0:T(8,128)(2,1)S(1)} %get-tuple-element.9), channel_id=4, replica_groups=mesh['row'=8,'col'=4] {'col'}, dimensions={0}, use_global_device_ids=true | all-gather | bytes 655360 | tf_op jit(solution)/shard_map/all_gather | solution.py:33
  208.4 0.9 gather_fusion.2
  209.3 7.8 %fusion.12 = f32[192,32,128]{2,1,0:T(8,128)} fusion(bf16[192,32,128]{2,1,0:T(8,128)(2,1)S(1)} %gather_fusion.2, bf16[1,1,192,128,128]{4,3,2,1,0:T(8,128)(2,1)} %param.6, pred[192]{0:T(512)(128)(4,1)S(1)} %iota_compare_fusion), kind=kOutput, calls=%fused_computation.14 | convolution fusion | flops 202113024 | bytes 11010240 | tf_op jit(solution)/shard_map/ski,soi->sko/dot_general | solution.py:15
  217.1 0.2 broadcast.156
  217.4 17.3 %scatter_fusion.2 = f32[128,32,128]{2,1,0:T(8,128)S(1)} fusion(f32[128,32,128]{2,1,0:T(8,128)S(1)} %broadcast.156, s32[192]{0:T(256)S(1)} %bitcast.75, f32[192,32,128]{2,1,0:T(8,128)} %fusion.12), kind=kCustom, calls=%fused_computation.5 | custom fusion | flops 786432 | bytes 9437952 | tf_op jit(solution)/shard_map/scatter-add | solution.py:36
  234.7 1.3 copy-done.1
  236.0 0.0 reduce-scatter.8.cloned.1.call-update
  236.0 42.1 %reduce-scatter.8.cloned.1.call-done = f32[16,32,128]{2,1,0:T(8,128)} async-done(((f32[128,32,128]{2,1,0:T(8,128)}), f32[16,32,128]{2,1,0:T(8,128)}) %reduce-scatter.8.cloned.1.call-update) | async-done | bytes 262160 | tf_op jit(solution)/shard_map/reduce_scatter | solution.py:37
  278.2 3.5 %fusion.15 = f32[1,16,32,128]{3,2,1,0:T(8,128)} fusion(f32[16,32,128]{2,1,0:T(8,128)} %get-tuple-element.10, f32[1,16,128,128]{3,2,1,0:T(8,128)S(1)} %copy-done, f32[16,32,128]{2,1,0:T(8,128)} %reduce-scatter.8.cloned.1.call-done, f32[1,16,32,128]{3,2,1,0:T(8,128)S(1)} %copy-done.4), kind=kOutput, calls=%fused_computation.16 | convolution fusion | flops 100859904 | bytes 2097152 | tf_op jit(solution)/shard_map/poi,pki->pko/dot_general | solution.py:10
  (12 shorter events, 0.0 us)
Async XLA Ops:
  6.5 1.2 copy-start
  6.5 22.0 %copy-start.5 = (s32[1,1,192]{2,1,0:T(1,128)S(1)}, s32[1,1,192]{2,1,0:T(1,128)}, u32[]{:S(2)}) copy-start(s32[1,1,192]{2,1,0:T(1,128)} %param.8) | copy-start | bytes 2308
  6.5 93.4 %reduce-scatter.4.cloned.1.call-start = ((), (), s32[]{:S(2)}) async-start(), calls=%async_computation.3 | async-start | bytes 2359296 | tf_op jit(solution)/shard_map/reduce_scatter | solution.py:37
  55.5 1.3 copy-start.2
  55.5 44.5 %copy-start.4 = (f32[1,16,32,128]{3,2,1,0:T(8,128)S(1)}, f32[1,16,32,128]{3,2,1,0:T(8,128)}, u32[]{:S(2)}) copy-start(f32[1,16,32,128]{3,2,1,0:T(8,128)} %param.11) | copy-start | bytes 786436
  56.9 132.2 %reduce-scatter.6.cloned.1.call-start = ((), (), s32[]{:S(2)}) async-start(), calls=%async_computation.4 | async-start | bytes 2359296 | tf_op jit(solution)/shard_map/reduce_scatter | solution.py:37
  145.5 1.3 copy-start.3
  146.8 131.3 %reduce-scatter.8.cloned.1.call-start = ((), (), s32[]{:S(2)}) async-start(), calls=%async_computation.5 | async-start | bytes 2359296 | tf_op jit(solution)/shard_map/reduce_scatter | solution.py:37
  234.6 1.3 copy-start.1
Sparse Core Ops, SparseCore 0:
  57.0 42.9 reduce-scatter.3
  147.0 41.9 reduce-scatter.5
  236.1 41.9 reduce-scatter.7
where the time goes:
time: 290 us; the launch traced here: 288 us
  waiting for transfers between devices  127 us (44%)
  other arithmetic  52.6 us (18%)
  blocking collectives  48.8 us (17%)
  matrix products  37.6 us (13%)
  between operations  13.9 us (5%)
  local copies, waits for them, and re-layouts  7.91 us (3%)
    reduce_scatter x3, waiting for transfers between devices, per_device(): lax.psum_scatter(partial_value, 'row', scatter_dimension=0, tiled=True)  127 us
    scatter-add x3, other arithmetic, per_device(): partial_value = jax.ops.segment_sum(terms, row_local, num_segments=group)  51.8 us
    all_gather x3, blocking collectives, per_device(): lax.all_gather(solution.astype(jnp.bfloat16)[None], 'col', axis=1, tiled=...  48.8 us
    dot_general x3, matrix products, block_terms(): jnp.einsum('ski,soi->sko', gathered, values, preferred_element_type=jnp.f...  23.5 us
    dot_general x4, matrix products, apply_blocks(): jnp.einsum('poi,pki->pko', matrix, field, precision=lax.Precision.HIGHEST)  14.1 us
  transfers between devices with their start and end apart: 3, of which 3 were waited for; matrix products, arithmetic and copies ran while one was open for 0% of the time, Pallas kernels for 0%

commit v1 on v0

v1 whole, which is shorter than its diff:
```python
import functools

import jax
import jax.numpy as jnp
from jax import lax
from jax.experimental import pallas as pl
from jax.experimental.pallas import tpu as pltpu
from jax.sharding import PartitionSpec as P

ITERS = 3
UNROLL = 8
CORES = 2
VMEM_LIMIT = 48 * 1024 * 1024

NT = (((1,), (1,)), ((), ()))


def in_vmem():
    return pl.BlockSpec(memory_space=pltpu.VMEM)


def in_smem():
    return pl.BlockSpec(memory_space=pltpu.SMEM)


def params():
    return pltpu.CompilerParams(vmem_limit_bytes=VMEM_LIMIT)


def split(value):
    high = value.astype(jnp.bfloat16)
    low = (value - high.astype(jnp.float32)).astype(jnp.bfloat16)
    return high, low


def times_block(field, high, low):
    field_high, field_low = split(field)
    rhs = field.shape[0]
    both = jnp.concatenate([field_high, field_low], axis=0)
    first = lax.dot_general(both, high, NT, preferred_element_type=jnp.float32)
    second = lax.dot_general(field_high, low, NT, preferred_element_type=jnp.float32)
    return first[:rhs] + (first[rhs:] + second)


def start_kernel(precond_ref, rhs_ref, high_ref, low_ref, sol_ref, rounded_ref):
    for p in range(rhs_ref.shape[0]):
        high, low = split(precond_ref[p])
        high_ref[p] = high
        low_ref[p] = low
        value = times_block(rhs_ref[p], high, low)
        sol_ref[p] = value
        rounded_ref[p] = value.astype(jnp.bfloat16)


def apply_kernel(pieces, high_ref, low_ref, rhs_ref, sol_ref, own_ref, *refs):
    piece_refs, (new_ref, rounded_ref) = refs[:pieces], refs[pieces:]
    for p in range(rhs_ref.shape[0]):
        product = own_ref[p]
        for piece_ref in piece_refs:
            product = product + piece_ref[p].astype(jnp.float32)
        before = sol_ref[p]
        residual = rhs_ref[p] - before - product
        value = before + times_block(residual, high_ref[p], low_ref[p])
        new_ref[p] = value
        rounded_ref[p] = value.astype(jnp.bfloat16)


def order_kernel(group, owned, groups, position_ref, count_ref, rows_ref, cols_ref,
                 slot_out, row_out, col_out, total_out):
    used = count_ref[0]
    core = lax.rem(position_ref[0], CORES)
    mine = position_ref[1]
    trash = group // CORES

    def fill(at, carry):
        for half in range(CORES):
            slot_out[half, at] = 0
            row_out[half, at] = trash
            col_out[half, at] = 0
        return carry

    lax.fori_loop(0, slot_out.shape[1], fill, 0)

    def place(slot, counts):
        row = lax.rem(rows_ref[slot], group)
        owner = lax.div(row, owned)
        half = jnp.where(lax.rem(owner, CORES) == core, 1, 0)
        at = jnp.where(half == 1, counts[1], counts[0])
        column = cols_ref[slot]
        source = lax.div(column, group)
        away = lax.rem(mine - source + groups, groups)
        slot_out[half, at] = slot
        row_out[half, at] = lax.div(owner, CORES) * owned + lax.rem(row, owned)
        col_out[half, at] = away * owned + lax.rem(column, owned)
        return counts[0] + (1 - half), counts[1] + half

    zero = jnp.int32(0)
    first, second = lax.fori_loop(0, used, place, (zero, zero))
    total_out[0] = first
    total_out[1] = second


def product_kernel(half, pieces, slot_ref, row_ref, col_ref, total_ref, values_ref, *refs):
    piece_refs, (out_ref, field, total) = refs[:pieces], refs[pieces:]
    owned = piece_refs[0].shape[0]
    for index, piece_ref in enumerate(piece_refs):
        field[pl.ds(index * owned, owned)] = piece_ref[...]
    total[...] = jnp.zeros_like(total)

    def step(chunk, carry):
        terms = []
        for lane in range(UNROLL):
            at = chunk * UNROLL + lane
            term = lax.dot_general(
                field[col_ref[half, at]], values_ref[slot_ref[half, at]], NT,
                preferred_element_type=jnp.float32)
            terms.append((row_ref[half, at], term))
        for row, term in terms:
            total[row] += term
        return carry

    chunks = lax.div(total_ref[half] + UNROLL - 1, UNROLL)
    lax.fori_loop(0, chunks, step, 0)
    out_ref[...] = total[pl.ds(0, out_ref.shape[0])].astype(out_ref.dtype)


def combine_kernel(chips, position_ref, own_ref, other_ref, keep_ref, *send_refs):
    chip = lax.div(position_ref[0], CORES)
    owned = keep_ref.shape[0]
    for shift in range(chips):
        dest = partner(chip, shift, chips)
        at = pl.ds(dest * owned, owned)
        value = own_ref[at] + other_ref[at].astype(jnp.float32)
        if shift == 0:
            keep_ref[...] = value
        else:
            send_refs[shift - 1][...] = value.astype(jnp.bfloat16)


def partner(chip, shift, chips):
    if chips & (chips - 1) == 0:
        return chip ^ shift
    return (chip + shift) % chips


def per_device(block_values, block_rows, block_cols, block_counts, precond, right_side):
    owned, rhs, size = right_side.shape[1:]
    row_devices = lax.axis_size("row")
    groups = lax.axis_size("col")
    chips = row_devices // CORES
    group = owned * row_devices
    half_rows = chips * owned
    slots = block_values.shape[2]
    padded = (slots + UNROLL - 1) // UNROLL * UNROLL
    values = block_values[0, 0]
    inverse = precond[0]
    rhs_own = right_side[0]
    position = jnp.stack([lax.axis_index("row"), lax.axis_index("col")]).astype(jnp.int32)

    field_type = jax.ShapeDtypeStruct((owned, rhs, size), jnp.float32)
    rounded_type = jax.ShapeDtypeStruct((owned, rhs, size), jnp.bfloat16)
    matrix_type = jax.ShapeDtypeStruct((owned, size, size), jnp.bfloat16)

    high, low, sol, rounded = pl.pallas_call(
        start_kernel,
        out_shape=[matrix_type, matrix_type, field_type, rounded_type],
        in_specs=[in_vmem()] * 2,
        out_specs=[in_vmem()] * 4,
        compiler_params=params(),
        name="start",
    )(inverse, rhs_own)

    index_type = jax.ShapeDtypeStruct((CORES, padded), jnp.int32)
    lists = pl.pallas_call(
        functools.partial(order_kernel, group, owned, groups),
        out_shape=[index_type] * 3 + [jax.ShapeDtypeStruct((CORES,), jnp.int32)],
        in_specs=[in_smem()] * 4,
        out_specs=[in_smem()] * 4,
        compiler_params=params(),
        name="order",
    )(position, block_counts[0], block_rows[0, 0], block_cols[0, 0])

    def product(half, dtype, fields):
        return pl.pallas_call(
            functools.partial(product_kernel, half, len(fields)),
            out_shape=jax.ShapeDtypeStruct((half_rows, rhs, size), dtype),
            in_specs=[in_smem()] * 4 + [in_vmem()] * (1 + len(fields)),
            out_specs=in_vmem(),
            scratch_shapes=[
                pltpu.VMEM((groups * owned, rhs, size), jnp.bfloat16),
                pltpu.VMEM((half_rows + 1, rhs, size), jnp.float32),
            ],
            compiler_params=params(),
            name="product%d" % half,
            cost_estimate=pl.CostEstimate(
                flops=slots * rhs * size * size, bytes_accessed=slots * size * size, transcendentals=0),
        )(*lists, values, *fields)

    swap = [(r, r ^ 1) for r in range(row_devices)]
    for step in range(ITERS):
        fields = [rounded]
        for shift in range(1, groups):
            ring = [(c, (c + shift) % groups) for c in range(groups)]
            fields.append(lax.ppermute(rounded, "col", ring))
        outgoing = product(0, jnp.bfloat16, fields)
        incoming = lax.ppermute(outgoing, "row", swap)
        own = product(1, jnp.float32, fields)
        keep, *sends = pl.pallas_call(
            functools.partial(combine_kernel, chips),
            out_shape=[field_type] + [rounded_type] * (chips - 1),
            in_specs=[in_smem()] + [in_vmem()] * 2,
            out_specs=[in_vmem()] * chips,
            compiler_params=params(),
            name="combine",
        )(position, own, incoming)
        pieces = []
        for shift in range(1, chips):
            pairs = [
                (chip * CORES + core, partner(chip, shift, chips) * CORES + core)
                for chip in range(chips) for core in range(CORES)
            ]
            pieces.append(lax.ppermute(sends[shift - 1], "row", pairs))
        sol, rounded = pl.pallas_call(
            functools.partial(apply_kernel, len(pieces)),
            out_shape=[field_type, rounded_type],
            in_specs=[in_vmem()] * (5 + len(pieces)),
            out_specs=[in_vmem()] * 2,
            compiler_params=params(),
            name="apply",
        )(high, low, rhs_own, sol, keep, *pieces)
    return sol[None]


def solution(mesh):
    placed = (
        P("row", "col", None, None, None),
        P("row", "col", None),
        P("row", "col", None),
        P("row", "col"),
        P("col", "row", None, None),
        P("col", "row", None, None),
    )
    return jax.shard_map(
        per_device,
        mesh=mesh,
        in_specs=placed,
        out_specs=P("col", "row", None, None),
        check_vma=False,
    )
```

time: 290 us -> 115 us (0.40)
  waiting for transfers between devices: 127 us -> 36.8 us
  other arithmetic: 52.6 us -> 0.08 us
  blocking collectives: 48.8 us -> 0 us
  Pallas kernels: 0 us -> 46.9 us
  matrix products: 37.6 us -> 0 us
  starting transfers between devices: 0.09 us -> 27.2 us
  between operations: 13.9 us -> 0.83 us
  local copies, waits for them, and re-layouts: 7.91 us -> 3.54 us
    reduce_scatter x3 -> x0, waiting for transfers between devices: 127 us -> none  [per_device(): lax.psum_scatter(partial_value, 'row', scatter_dimension=0, tiled=True)]
    scatter-add x3 -> x0, other arithmetic: 51.8 us -> none  [per_device(): partial_value = jax.ops.segment_sum(terms, row_local, num_segments=group)]
    all_gather x3 -> x0, blocking collectives: 48.8 us -> none  [per_device(): lax.all_gather(solution.astype(jnp.bfloat16)[None], 'col', axis=1, tiled=...]
    pallas_call x0 -> x14, Pallas kernels: none -> 46.9 us  [the longest x6 33.9 us: product(): pl.pallas_call(functools.partial(product_kernel, half, len(fields)), out_...]
    dot_general x7 -> x0, matrix products: 37.6 us -> none  [the longest x3 23.5 us: block_terms(): jnp.einsum('ski,soi->sko', gathered, values, preferred_element_type=jnp.f...]
    ppermute x0 -> x21, waiting for transfers between devices: none -> 36.8 us  [the longest x9 20.9 us: per_device(): fields.append(lax.ppermute(rounded, 'col', ring))]
    ppermute x0 -> x21, starting transfers between devices: none -> 27.2 us  [the longest x9 16.4 us: per_device(): fields.append(lax.ppermute(rounded, 'col', ring))]
  transfers between devices with their start and end apart: 3 -> 21, of which waited for: 3 -> 11; matrix products, arithmetic and copies ran while one was open for 0% -> 0% of each run, Pallas kernels for 0% -> 20%
where the time goes in v1:
time: 115 us
  Pallas kernels  46.9 us (41%)
  waiting for transfers between devices  36.8 us (32%)
  starting transfers between devices  27.2 us (24%)
  local copies, waits for them, and re-layouts  3.54 us (3%)
    pallas_call x6, Pallas kernels, product(): pl.pallas_call(functools.partial(product_kernel, half, len(fields)), out_...  33.9 us
    ppermute x9, waiting for transfers between devices, per_device(): fields.append(lax.ppermute(rounded, 'col', ring))  20.9 us
    ppermute x9, starting transfers between devices, per_device(): fields.append(lax.ppermute(rounded, 'col', ring))  16.4 us
    ppermute x9, waiting for transfers between devices, per_device(): pieces.append(lax.ppermute(sends[shift - 1], 'row', pairs))  15.9 us
    ppermute x9, starting transfers between devices, per_device(): pieces.append(lax.ppermute(sends[shift - 1], 'row', pairs))  10.6 us
    pallas_call x1, Pallas kernels, per_device(): pl.pallas_call(functools.partial(order_kernel, group, owned, groups), out...  7.46 us
    unnamed x10, local copies, waits for them, and re-layouts  3.54 us
    pallas_call x3, Pallas kernels, per_device(): pl.pallas_call(functools.partial(apply_kernel, len(pieces)), out_shape=[f...  2.94 us
  transfers between devices with their start and end apart: 21, of which 11 were waited for; matrix products, arithmetic and copies ran while one was open for 0% of the time, Pallas kernels for 20%

profile of v1, /device:TPU:0, one launch (start us, length us, event | category | flops | bytes accessed | tf_op | source)
XLA Modules:
  0.0 115.4 jit_solution(8909156791141383151)
XLA Ops:
  1.0 1.2 %copy-done.2 = f32[1,16,128,128]{3,2,1,0:T(8,128)S(1)} copy-done((f32[1,16,128,128]{3,2,1,0:T(8,128)S(1)}, f32[1,16,128,128]{3,2,1,0:T(8,128)}, u32[]{:S(2)}) %copy-start.2) | copy-done | bytes 1048600
  2.9 5.1 %collective-permute-start.2 = (bf16[16,32,128]{2,1,0:T(8,128)(2,1)S(1)}, bf16[16,32,128]{2,1,0:T(8,128)(2,1)S(1)}, u32[]{:S(2)}, u32[]{:S(2)}) collective-permute-start(bf16[16,32,128]{2,1,0:T(8,128)(2,1)S(1)} %get-tuple-element.37.refs_0_), channel_id=1, source_target_pairs={{0,3},{1,0},{2,1},{3,2},{4,7},{5,4},{6,5},{7,6},{8,11},{9,8},{10,9... | collective-permute-start | bytes 393224 | tf_op jit(solution)/shard_map/ppermute | solution.py:204
  8.0 1.0 collective-permute-start
  11.1 7.5 %order.1 = (s32[2,192]{1,0:T(2,128)S(1)}, s32[2,192]{1,0:T(2,128)S(1)}, s32[2,192]{1,0:T(2,128)S(1)}, s32[2]{0:T(128)S(1)}) custom-call(s32[2]{0:T(128)S(1)} %pad_add_fusion.position_ref, s32[1]{0:T(128)} %bitcast.9.count_ref, s32[192]{0:T(256)S(1)} %bitcast.15, s32[192]{0:T(256)S(1)} %bitcast.16), custom_call_target="tpu_custom_call" | custom-call | tf_op jit(solution)/shard_map/order/pallas_call | solution.py:174
  19.2 6.0 %product0.3 = bf16[64,32,128]{2,1,0:T(8,128)(2,1)S(1)} custom-call(s32[2,192]{1,0:T(2,128)S(1)} %get-tuple-element.33.slot_ref, s32[2,192]{1,0:T(2,128)S(1)} %get-tuple-element.34.row_ref, s32[2,192]{1,0:T(2,128)S(1)} %get-tuple-element.35.col_ref, s32[2]{0:T(128)S(1)} %get-tuple-element.36.total_ref, bf16[192,128,128]{2,1,0:T(8,128)(2,1)} %bitcast.17, ...), custom_call_target="tpu_custom_call" | custom-call | flops 100663296 | bytes 3145728 | tf_op jit(solution)/shard_map/product0/pallas_call | solution.py:184
  25.3 5.3 %product1.3.own_ref = f32[64,32,128]{2,1,0:T(8,128)S(1)} custom-call(s32[2,192]{1,0:T(2,128)S(1)} %get-tuple-element.33.slot_ref, s32[2,192]{1,0:T(2,128)S(1)} %get-tuple-element.34.row_ref, s32[2,192]{1,0:T(2,128)S(1)} %get-tuple-element.35.col_ref, s32[2]{0:T(128)S(1)} %get-tuple-element.36.total_ref, bf16[192,128,128]{2,1,0:T(8,128)(2,1)} %bitcast.18, ...), custom_call_target="tpu_custom_call" | custom-call | flops 100663296 | bytes 3145728 | tf_op jit(solution)/shard_map/product1/pallas_call | solution.py:184
  31.3 1.7 %collective-permute-start.5 = (bf16[16,32,128]{2,1,0:T(8,128)(2,1)S(1)}, bf16[16,32,128]{2,1,0:T(8,128)(2,1)S(1)}, u32[]{:S(2)}, u32[]{:S(2)}) collective-permute-start(bf16[16,32,128]{2,1,0:T(8,128)(2,1)S(1)} %get-tuple-element.40), channel_id=1, source_target_pairs={{0,16},{4,20},{8,24},{12,28},{16,0},{20,4},{24,8},{28,12},{1,17},{... | collective-permute-start | bytes 393224 | tf_op jit(solution)/shard_map/ppermute | solution.py:222
  33.0 1.8 %collective-permute-start.6 = (bf16[16,32,128]{2,1,0:T(8,128)(2,1)S(1)}, bf16[16,32,128]{2,1,0:T(8,128)(2,1)S(1)}, u32[]{:S(2)}, u32[]{:S(2)}) collective-permute-start(bf16[16,32,128]{2,1,0:T(8,128)(2,1)S(1)} %get-tuple-element.41), channel_id=1, source_target_pairs={{0,24},{4,28},{8,16},{12,20},{16,8},{20,12},{24,0},{28,4},{1,25},{... | collective-permute-start | bytes 393224 | tf_op jit(solution)/shard_map/ppermute | solution.py:222
  34.8 2.6 %collective-permute-done.4.refs_0_ = bf16[16,32,128]{2,1,0:T(8,128)(2,1)S(1)} collective-permute-done((bf16[16,32,128]{2,1,0:T(8,128)(2,1)S(1)}, bf16[16,32,128]{2,1,0:T(8,128)(2,1)S(1)}, u32[]{:S(2)}, u32[]{:S(2)}) %collective-permute-start.4) | collective-permute-done | bytes 131104 | tf_op jit(solution)/shard_map/ppermute | solution.py:222
  37.4 2.9 %collective-permute-done.5.refs_1_ = bf16[16,32,128]{2,1,0:T(8,128)(2,1)S(1)} collective-permute-done((bf16[16,32,128]{2,1,0:T(8,128)(2,1)S(1)}, bf16[16,32,128]{2,1,0:T(8,128)(2,1)S(1)}, u32[]{:S(2)}, u32[]{:S(2)}) %collective-permute-start.5) | collective-permute-done | bytes 131104 | tf_op jit(solution)/shard_map/ppermute | solution.py:222
  41.0 4.0 %collective-permute-start.9 = (bf16[16,32,128]{2,1,0:T(8,128)(2,1)S(1)}, bf16[16,32,128]{2,1,0:T(8,128)(2,1)S(1)}, u32[]{:S(2)}, u32[]{:S(2)}) collective-permute-start(bf16[16,32,128]{2,1,0:T(8,128)(2,1)S(1)} %get-tuple-element.43.refs_0_), channel_id=1, source_target_pairs={{0,3},{1,0},{2,1},{3,2},{4,7},{5,4},{6,5},{7,6},{8,11},{9,8},{10,9... | collective-permute-start | bytes 393224 | tf_op jit(solution)/shard_map/ppermute | solution.py:204
  45.0 1.8 %collective-permute-start.8 = (bf16[16,32,128]{2,1,0:T(8,128)(2,1)S(1)}, bf16[16,32,128]{2,1,0:T(8,128)(2,1)S(1)}, u32[]{:S(2)}, u32[]{:S(2)}) collective-permute-start(bf16[16,32,128]{2,1,0:T(8,128)(2,1)S(1)} %get-tuple-element.43.refs_0_), channel_id=1, source_target_pairs={{0,2},{1,3},{2,0},{3,1},{4,6},{5,7},{6,4},{7,5},{8,10},{9,11},{10,... | collective-permute-start | bytes 393224 | tf_op jit(solution)/shard_map/ppermute | solution.py:204
  46.8 2.1 %collective-permute-done.9.refs_3_ = bf16[16,32,128]{2,1,0:T(8,128)(2,1)S(1)} collective-permute-done((bf16[16,32,128]{2,1,0:T(8,128)(2,1)S(1)}, bf16[16,32,128]{2,1,0:T(8,128)(2,1)S(1)}, u32[]{:S(2)}, u32[]{:S(2)}) %collective-permute-start.9) | collective-permute-done | bytes 131104 | tf_op jit(solution)/shard_map/ppermute | solution.py:204
  48.9 8.8 %collective-permute-done.8.refs_2_ = bf16[16,32,128]{2,1,0:T(8,128)(2,1)S(1)} collective-permute-done((bf16[16,32,128]{2,1,0:T(8,128)(2,1)S(1)}, bf16[16,32,128]{2,1,0:T(8,128)(2,1)S(1)}, u32[]{:S(2)}, u32[]{:S(2)}) %collective-permute-start.8) | collective-permute-done | bytes 131104 | tf_op jit(solution)/shard_map/ppermute | solution.py:204
  57.7 6.0 %product0.4 = bf16[64,32,128]{2,1,0:T(8,128)(2,1)S(1)} custom-call(s32[2,192]{1,0:T(2,128)S(1)} %get-tuple-element.33.slot_ref, s32[2,192]{1,0:T(2,128)S(1)} %get-tuple-element.34.row_ref, s32[2,192]{1,0:T(2,128)S(1)} %get-tuple-element.35.col_ref, s32[2]{0:T(128)S(1)} %get-tuple-element.36.total_ref, bf16[192,128,128]{2,1,0:T(8,128)(2,1)} %bitcast.19, ...), custom_call_target="tpu_custom_call" | custom-call | flops 100663296 | bytes 3145728 | tf_op jit(solution)/shard_map/product0/pallas_call | solution.py:184
  63.8 5.3 %product1.4.own_ref = f32[64,32,128]{2,1,0:T(8,128)S(1)} custom-call(s32[2,192]{1,0:T(2,128)S(1)} %get-tuple-element.33.slot_ref, s32[2,192]{1,0:T(2,128)S(1)} %get-tuple-element.34.row_ref, s32[2,192]{1,0:T(2,128)S(1)} %get-tuple-element.35.col_ref, s32[2]{0:T(128)S(1)} %get-tuple-element.36.total_ref, bf16[192,128,128]{2,1,0:T(8,128)(2,1)} %bitcast.20, ...), custom_call_target="tpu_custom_call" | custom-call | flops 100663296 | bytes 3145728 | tf_op jit(solution)/shard_map/product1/pallas_call | solution.py:184
  70.0 1.4 %collective-permute-start.12 = (bf16[16,32,128]{2,1,0:T(8,128)(2,1)S(1)}, bf16[16,32,128]{2,1,0:T(8,128)(2,1)S(1)}, u32[]{:S(2)}, u32[]{:S(2)}) collective-permute-start(bf16[16,32,128]{2,1,0:T(8,128)(2,1)S(1)} %get-tuple-element.46), channel_id=1, source_target_pairs={{0,16},{4,20},{8,24},{12,28},{16,0},{20,4},{24,8},{28,12},{1,17},{... | collective-permute-start | bytes 393224 | tf_op jit(solution)/shard_map/ppermute | solution.py:222
  71.4 1.9 %collective-permute-start.13 = (bf16[16,32,128]{2,1,0:T(8,128)(2,1)S(1)}, bf16[16,32,128]{2,1,0:T(8,128)(2,1)S(1)}, u32[]{:S(2)}, u32[]{:S(2)}) collective-permute-start(bf16[16,32,128]{2,1,0:T(8,128)(2,1)S(1)} %get-tuple-element.47), channel_id=1, source_target_pairs={{0,24},{4,28},{8,16},{12,20},{16,8},{20,12},{24,0},{28,4},{1,25},{... | collective-permute-start | bytes 393224 | tf_op jit(solution)/shard_map/ppermute | solution.py:222
  73.3 2.6 %collective-permute-done.11.refs_0_ = bf16[16,32,128]{2,1,0:T(8,128)(2,1)S(1)} collective-permute-done((bf16[16,32,128]{2,1,0:T(8,128)(2,1)S(1)}, bf16[16,32,128]{2,1,0:T(8,128)(2,1)S(1)}, u32[]{:S(2)}, u32[]{:S(2)}) %collective-permute-start.11) | collective-permute-done | bytes 131104 | tf_op jit(solution)/shard_map/ppermute | solution.py:222
  75.9 2.5 %collective-permute-done.13.refs_2_ = bf16[16,32,128]{2,1,0:T(8,128)(2,1)S(1)} collective-permute-done((bf16[16,32,128]{2,1,0:T(8,128)(2,1)S(1)}, bf16[16,32,128]{2,1,0:T(8,128)(2,1)S(1)}, u32[]{:S(2)}, u32[]{:S(2)}) %collective-permute-start.13) | collective-permute-done | bytes 131104 | tf_op jit(solution)/shard_map/ppermute | solution.py:222
  79.2 1.0 collective-permute-start.16
  80.2 1.5 %collective-permute-start.15 = (bf16[16,32,128]{2,1,0:T(8,128)(2,1)S(1)}, bf16[16,32,128]{2,1,0:T(8,128)(2,1)S(1)}, u32[]{:S(2)}, u32[]{:S(2)}) collective-permute-start(bf16[16,32,128]{2,1,0:T(8,128)(2,1)S(1)} %get-tuple-element.49.refs_0_), channel_id=1, source_target_pairs={{0,2},{1,3},{2,0},{3,1},{4,6},{5,7},{6,4},{7,5},{8,10},{9,11},{10,... | collective-permute-start | bytes 393224 | tf_op jit(solution)/shard_map/ppermute | solution.py:204
  81.7 2.0 %collective-permute-start.14 = (bf16[16,32,128]{2,1,0:T(8,128)(2,1)S(1)}, bf16[16,32,128]{2,1,0:T(8,128)(2,1)S(1)}, u32[]{:S(2)}, u32[]{:S(2)}) collective-permute-start(bf16[16,32,128]{2,1,0:T(8,128)(2,1)S(1)} %get-tuple-element.49.refs_0_), channel_id=1, source_target_pairs={{0,1},{1,2},{2,3},{3,0},{4,5},{5,6},{6,7},{7,4},{8,9},{9,10},{10,1... | collective-permute-start | bytes 393224 | tf_op jit(solution)/shard_map/ppermute | solution.py:204
  83.6 2.5 %collective-permute-done.16.refs_3_ = bf16[16,32,128]{2,1,0:T(8,128)(2,1)S(1)} collective-permute-done((bf16[16,32,128]{2,1,0:T(8,128)(2,1)S(1)}, bf16[16,32,128]{2,1,0:T(8,128)(2,1)S(1)}, u32[]{:S(2)}, u32[]{:S(2)}) %collective-permute-start.16) | collective-permute-done | bytes 131104 | tf_op jit(solution)/shard_map/ppermute | solution.py:204
  86.1 6.9 %collective-permute-done.15.refs_2_ = bf16[16,32,128]{2,1,0:T(8,128)(2,1)S(1)} collective-permute-done((bf16[16,32,128]{2,1,0:T(8,128)(2,1)S(1)}, bf16[16,32,128]{2,1,0:T(8,128)(2,1)S(1)}, u32[]{:S(2)}, u32[]{:S(2)}) %collective-permute-start.15) | collective-permute-done | bytes 131104 | tf_op jit(solution)/shard_map/ppermute | solution.py:204
  93.0 6.0 %product0.5 = bf16[64,32,128]{2,1,0:T(8,128)(2,1)S(1)} custom-call(s32[2,192]{1,0:T(2,128)S(1)} %get-tuple-element.33.slot_ref, s32[2,192]{1,0:T(2,128)S(1)} %get-tuple-element.34.row_ref, s32[2,192]{1,0:T(2,128)S(1)} %get-tuple-element.35.col_ref, s32[2]{0:T(128)S(1)} %get-tuple-element.36.total_ref, bf16[192,128,128]{2,1,0:T(8,128)(2,1)} %bitcast.21, ...), custom_call_target="tpu_custom_call" | custom-call | flops 100663296 | bytes 3145728 | tf_op jit(solution)/shard_map/product0/pallas_call | solution.py:184
  99.1 5.3 %product1.5.own_ref = f32[64,32,128]{2,1,0:T(8,128)S(1)} custom-call(s32[2,192]{1,0:T(2,128)S(1)} %get-tuple-element.33.slot_ref, s32[2,192]{1,0:T(2,128)S(1)} %get-tuple-element.34.row_ref, s32[2,192]{1,0:T(2,128)S(1)} %get-tuple-element.35.col_ref, s32[2]{0:T(128)S(1)} %get-tuple-element.36.total_ref, bf16[192,128,128]{2,1,0:T(8,128)(2,1)} %bitcast.22, ...), custom_call_target="tpu_custom_call" | custom-call | flops 100663296 | bytes 3145728 | tf_op jit(solution)/shard_map/product1/pallas_call | solution.py:184
  105.1 1.3 %collective-permute-start.19 = (bf16[16,32,128]{2,1,0:T(8,128)(2,1)S(1)}, bf16[16,32,128]{2,1,0:T(8,128)(2,1)S(1)}, u32[]{:S(2)}, u32[]{:S(2)}) collective-permute-start(bf16[16,32,128]{2,1,0:T(8,128)(2,1)S(1)} %get-tuple-element.52), channel_id=1, source_target_pairs={{0,16},{4,20},{8,24},{12,28},{16,0},{20,4},{24,8},{28,12},{1,17},{... | collective-permute-start | bytes 393224 | tf_op jit(solution)/shard_map/ppermute | solution.py:222
  106.4 2.2 %collective-permute-start.20 = (bf16[16,32,128]{2,1,0:T(8,128)(2,1)S(1)}, bf16[16,32,128]{2,1,0:T(8,128)(2,1)S(1)}, u32[]{:S(2)}, u32[]{:S(2)}) collective-permute-start(bf16[16,32,128]{2,1,0:T(8,128)(2,1)S(1)} %get-tuple-element.53), channel_id=1, source_target_pairs={{0,24},{4,28},{8,16},{12,20},{16,8},{20,12},{24,0},{28,4},{1,25},{... | collective-permute-start | bytes 393224 | tf_op jit(solution)/shard_map/ppermute | solution.py:222
  108.6 2.6 %collective-permute-done.18.refs_0_ = bf16[16,32,128]{2,1,0:T(8,128)(2,1)S(1)} collective-permute-done((bf16[16,32,128]{2,1,0:T(8,128)(2,1)S(1)}, bf16[16,32,128]{2,1,0:T(8,128)(2,1)S(1)}, u32[]{:S(2)}, u32[]{:S(2)}) %collective-permute-start.18) | collective-permute-done | bytes 131104 | tf_op jit(solution)/shard_map/ppermute | solution.py:222
  111.2 2.7 %collective-permute-done.19.refs_1_ = bf16[16,32,128]{2,1,0:T(8,128)(2,1)S(1)} collective-permute-done((bf16[16,32,128]{2,1,0:T(8,128)(2,1)S(1)}, bf16[16,32,128]{2,1,0:T(8,128)(2,1)S(1)}, u32[]{:S(2)}, u32[]{:S(2)}) %collective-permute-start.19) | collective-permute-done | bytes 131104 | tf_op jit(solution)/shard_map/ppermute | solution.py:222
  113.9 1.5 %apply.5 = (f32[16,32,128]{2,1,0:T(8,128)}, bf16[16,32,128]{2,1,0:T(8,128)(2,1)}) custom-call(bf16[16,128,128]{2,1,0:T(8,128)(2,1)S(1)} %get-tuple-element.30.high_ref, bf16[16,128,128]{2,1,0:T(8,128)(2,1)S(1)} %get-tuple-element.31.low_ref, f32[16,32,128]{2,1,0:T(8,128)S(1)} %bitcast.13, f32[16,32,128]{2,1,0:T(8,128)S(1)} %get-tuple-element.48.sol_ref, ...), custom_call_target="tpu_custom_call" | custom-call | tf_op jit(solution)/shard_map/apply/pallas_call | solution.py:223
  (35 shorter events, 7.8 us)
Async XLA Ops:
  0.0 0.9 copy-start
  1.0 1.2 %copy-start.2 = (f32[1,16,128,128]{3,2,1,0:T(8,128)S(1)}, f32[1,16,128,128]{3,2,1,0:T(8,128)}, u32[]{:S(2)}) copy-start(f32[1,16,128,128]{3,2,1,0:T(8,128)} %param.10) | copy-start | bytes 3145732
  2.9 15.6 %collective-permute-start.2 = (bf16[16,32,128]{2,1,0:T(8,128)(2,1)S(1)}, bf16[16,32,128]{2,1,0:T(8,128)(2,1)S(1)}, u32[]{:S(2)}, u32[]{:S(2)}) collective-permute-start(bf16[16,32,128]{2,1,0:T(8,128)(2,1)S(1)} %get-tuple-element.37.refs_0_), channel_id=1, source_target_pairs={{0,3},{1,0},{2,1},{3,2},{4,7},{5,4},{6,5},{7,6},{8,11},{9,8},{10,9... | collective-permute-start | bytes 393224 | tf_op jit(solution)/shard_map/ppermute | solution.py:204
  8.0 11.2 %collective-permute-start.1 = (bf16[16,32,128]{2,1,0:T(8,128)(2,1)S(1)}, bf16[16,32,128]{2,1,0:T(8,128)(2,1)S(1)}, u32[]{:S(2)}, u32[]{:S(2)}) collective-permute-start(bf16[16,32,128]{2,1,0:T(8,128)(2,1)S(1)} %get-tuple-element.37.refs_0_), channel_id=1, source_target_pairs={{0,2},{1,3},{2,0},{3,1},{4,6},{5,7},{6,4},{7,5},{8,10},{9,11},{10,... | collective-permute-start | bytes 393224 | tf_op jit(solution)/shard_map/ppermute | solution.py:204
  8.0 11.2 %collective-permute-start = (bf16[16,32,128]{2,1,0:T(8,128)(2,1)S(1)}, bf16[16,32,128]{2,1,0:T(8,128)(2,1)S(1)}, u32[]{:S(2)}, u32[]{:S(2)}) collective-permute-start(bf16[16,32,128]{2,1,0:T(8,128)(2,1)S(1)} %get-tuple-element.37.refs_0_), channel_id=1, source_target_pairs={{0,1},{1,2},{2,3},{3,0},{4,5},{5,6},{6,7},{7,4},{8,9},{9,10},{10,1... | collective-permute-start | bytes 393224 | tf_op jit(solution)/shard_map/ppermute | solution.py:204
  9.7 0.7 copy-start.3
  10.4 0.7 copy-start.4
  25.2 15.1 %copy-start.1 = (f32[1,16,32,128]{3,2,1,0:T(8,128)S(1)}, f32[1,16,32,128]{3,2,1,0:T(8,128)}, u32[]{:S(2)}) copy-start(f32[1,16,32,128]{3,2,1,0:T(8,128)} %param.11) | copy-start | bytes 786436
  25.2 5.4 %collective-permute-start.3 = (bf16[64,32,128]{2,1,0:T(8,128)(2,1)S(1)}, bf16[64,32,128]{2,1,0:T(8,128)(2,1)S(1)}, u32[]{:S(2)}, u32[]{:S(2)}) collective-permute-start(bf16[64,32,128]{2,1,0:T(8,128)(2,1)S(1)} %product0.3), channel_id=1, source_target_pairs={{0,4},{4,0},{8,12},{12,8},{16,20},{20,16},{24,28},{28,24},{1,5},{5... | collective-permute-start | bytes 1572872 | tf_op jit(solution)/shard_map/ppermute | solution.py:206
  31.2 6.2 %collective-permute-start.4 = (bf16[16,32,128]{2,1,0:T(8,128)(2,1)S(1)}, bf16[16,32,128]{2,1,0:T(8,128)(2,1)S(1)}, u32[]{:S(2)}, u32[]{:S(2)}) collective-permute-start(bf16[16,32,128]{2,1,0:T(8,128)(2,1)S(1)} %get-tuple-element.39), channel_id=1, source_target_pairs={{0,8},{4,12},{8,0},{12,4},{16,24},{20,28},{24,16},{28,20},{1,9},{5... | collective-permute-start | bytes 393224 | tf_op jit(solution)/shard_map/ppermute | solution.py:222
  31.3 8.9 %collective-permute-start.5 = (bf16[16,32,128]{2,1,0:T(8,128)(2,1)S(1)}, bf16[16,32,128]{2,1,0:T(8,128)(2,1)S(1)}, u32[]{:S(2)}, u32[]{:S(2)}) collective-permute-start(bf16[16,32,128]{2,1,0:T(8,128)(2,1)S(1)} %get-tuple-element.40), channel_id=1, source_target_pairs={{0,16},{4,20},{8,24},{12,28},{16,0},{20,4},{24,8},{28,12},{1,17},{... | collective-permute-start | bytes 393224 | tf_op jit(solution)/shard_map/ppermute | solution.py:222
  33.0 7.2 %collective-permute-start.6 = (bf16[16,32,128]{2,1,0:T(8,128)(2,1)S(1)}, bf16[16,32,128]{2,1,0:T(8,128)(2,1)S(1)}, u32[]{:S(2)}, u32[]{:S(2)}) collective-permute-start(bf16[16,32,128]{2,1,0:T(8,128)(2,1)S(1)} %get-tuple-element.41), channel_id=1, source_target_pairs={{0,24},{4,28},{8,16},{12,20},{16,8},{20,12},{24,0},{28,4},{1,25},{... | collective-permute-start | bytes 393224 | tf_op jit(solution)/shard_map/ppermute | solution.py:222
  41.0 7.9 %collective-permute-start.9 = (bf16[16,32,128]{2,1,0:T(8,128)(2,1)S(1)}, bf16[16,32,128]{2,1,0:T(8,128)(2,1)S(1)}, u32[]{:S(2)}, u32[]{:S(2)}) collective-permute-start(bf16[16,32,128]{2,1,0:T(8,128)(2,1)S(1)} %get-tuple-element.43.refs_0_), channel_id=1, source_target_pairs={{0,3},{1,0},{2,1},{3,2},{4,7},{5,4},{6,5},{7,6},{8,11},{9,8},{10,9... | collective-permute-start | bytes 393224 | tf_op jit(solution)/shard_map/ppermute | solution.py:204
  45.0 12.7 %collective-permute-start.8 = (bf16[16,32,128]{2,1,0:T(8,128)(2,1)S(1)}, bf16[16,32,128]{2,1,0:T(8,128)(2,1)S(1)}, u32[]{:S(2)}, u32[]{:S(2)}) collective-permute-start(bf16[16,32,128]{2,1,0:T(8,128)(2,1)S(1)} %get-tuple-element.43.refs_0_), channel_id=1, source_target_pairs={{0,2},{1,3},{2,0},{3,1},{4,6},{5,7},{6,4},{7,5},{8,10},{9,11},{10,... | collective-permute-start | bytes 393224 | tf_op jit(solution)/shard_map/ppermute | solution.py:204
  46.8 10.9 %collective-permute-start.7 = (bf16[16,32,128]{2,1,0:T(8,128)(2,1)S(1)}, bf16[16,32,128]{2,1,0:T(8,128)(2,1)S(1)}, u32[]{:S(2)}, u32[]{:S(2)}) collective-permute-start(bf16[16,32,128]{2,1,0:T(8,128)(2,1)S(1)} %get-tuple-element.43.refs_0_), channel_id=1, source_target_pairs={{0,1},{1,2},{2,3},{3,0},{4,5},{5,6},{6,7},{7,4},{8,9},{9,10},{10,1... | collective-permute-start | bytes 393224 | tf_op jit(solution)/shard_map/ppermute | solution.py:204
  63.7 5.4 %collective-permute-start.10 = (bf16[64,32,128]{2,1,0:T(8,128)(2,1)S(1)}, bf16[64,32,128]{2,1,0:T(8,128)(2,1)S(1)}, u32[]{:S(2)}, u32[]{:S(2)}) collective-permute-start(bf16[64,32,128]{2,1,0:T(8,128)(2,1)S(1)} %product0.4), channel_id=1, source_target_pairs={{0,4},{4,0},{8,12},{12,8},{16,20},{20,16},{24,28},{28,24},{1,5},{5... | collective-permute-start | bytes 1572872 | tf_op jit(solution)/shard_map/ppermute | solution.py:206
  69.7 6.2 %collective-permute-start.11 = (bf16[16,32,128]{2,1,0:T(8,128)(2,1)S(1)}, bf16[16,32,128]{2,1,0:T(8,128)(2,1)S(1)}, u32[]{:S(2)}, u32[]{:S(2)}) collective-permute-start(bf16[16,32,128]{2,1,0:T(8,128)(2,1)S(1)} %get-tuple-element.45), channel_id=1, source_target_pairs={{0,8},{4,12},{8,0},{12,4},{16,24},{20,28},{24,16},{28,20},{1,9},{5... | collective-permute-start | bytes 393224 | tf_op jit(solution)/shard_map/ppermute | solution.py:222
  70.0 5.9 %collective-permute-start.12 = (bf16[16,32,128]{2,1,0:T(8,128)(2,1)S(1)}, bf16[16,32,128]{2,1,0:T(8,128)(2,1)S(1)}, u32[]{:S(2)}, u32[]{:S(2)}) collective-permute-start(bf16[16,32,128]{2,1,0:T(8,128)(2,1)S(1)} %get-tuple-element.46), channel_id=1, source_target_pairs={{0,16},{4,20},{8,24},{12,28},{16,0},{20,4},{24,8},{28,12},{1,17},{... | collective-permute-start | bytes 393224 | tf_op jit(solution)/shard_map/ppermute | solution.py:222
  71.4 7.0 %collective-permute-start.13 = (bf16[16,32,128]{2,1,0:T(8,128)(2,1)S(1)}, bf16[16,32,128]{2,1,0:T(8,128)(2,1)S(1)}, u32[]{:S(2)}, u32[]{:S(2)}) collective-permute-start(bf16[16,32,128]{2,1,0:T(8,128)(2,1)S(1)} %get-tuple-element.47), channel_id=1, source_target_pairs={{0,24},{4,28},{8,16},{12,20},{16,8},{20,12},{24,0},{28,4},{1,25},{... | collective-permute-start | bytes 393224 | tf_op jit(solution)/shard_map/ppermute | solution.py:222
  79.2 7.0 %collective-permute-start.16 = (bf16[16,32,128]{2,1,0:T(8,128)(2,1)S(1)}, bf16[16,32,128]{2,1,0:T(8,128)(2,1)S(1)}, u32[]{:S(2)}, u32[]{:S(2)}) collective-permute-start(bf16[16,32,128]{2,1,0:T(8,128)(2,1)S(1)} %get-tuple-element.49.refs_0_), channel_id=1, source_target_pairs={{0,3},{1,0},{2,1},{3,2},{4,7},{5,4},{6,5},{7,6},{8,11},{9,8},{10,9... | collective-permute-start | bytes 393224 | tf_op jit(solution)/shard_map/ppermute | solution.py:204
  80.2 12.8 %collective-permute-start.15 = (bf16[16,32,128]{2,1,0:T(8,128)(2,1)S(1)}, bf16[16,32,128]{2,1,0:T(8,128)(2,1)S(1)}, u32[]{:S(2)}, u32[]{:S(2)}) collective-permute-start(bf16[16,32,128]{2,1,0:T(8,128)(2,1)S(1)} %get-tuple-element.49.refs_0_), channel_id=1, source_target_pairs={{0,2},{1,3},{2,0},{3,1},{4,6},{5,7},{6,4},{7,5},{8,10},{9,11},{10,... | collective-permute-start | bytes 393224 | tf_op jit(solution)/shard_map/ppermute | solution.py:204
  81.7 11.3 %collective-permute-start.14 = (bf16[16,32,128]{2,1,0:T(8,128)(2,1)S(1)}, bf16[16,32,128]{2,1,0:T(8,128)(2,1)S(1)}, u32[]{:S(2)}, u32[]{:S(2)}) collective-permute-start(bf16[16,32,128]{2,1,0:T(8,128)(2,1)S(1)} %get-tuple-element.49.refs_0_), channel_id=1, source_target_pairs={{0,1},{1,2},{2,3},{3,0},{4,5},{5,6},{6,7},{7,4},{8,9},{9,10},{10,1... | collective-permute-start | bytes 393224 | tf_op jit(solution)/shard_map/ppermute | solution.py:204
  99.0 5.4 %collective-permute-start.17 = (bf16[64,32,128]{2,1,0:T(8,128)(2,1)S(1)}, bf16[64,32,128]{2,1,0:T(8,128)(2,1)S(1)}, u32[]{:S(2)}, u32[]{:S(2)}) collective-permute-start(bf16[64,32,128]{2,1,0:T(8,128)(2,1)S(1)} %product0.5), channel_id=1, source_target_pairs={{0,4},{4,0},{8,12},{12,8},{16,20},{20,16},{24,28},{28,24},{1,5},{5... | collective-permute-start | bytes 1572872 | tf_op jit(solution)/shard_map/ppermute | solution.py:206
  105.0 6.2 %collective-permute-start.18 = (bf16[16,32,128]{2,1,0:T(8,128)(2,1)S(1)}, bf16[16,32,128]{2,1,0:T(8,128)(2,1)S(1)}, u32[]{:S(2)}, u32[]{:S(2)}) collective-permute-start(bf16[16,32,128]{2,1,0:T(8,128)(2,1)S(1)} %get-tuple-element.51), channel_id=1, source_target_pairs={{0,8},{4,12},{8,0},{12,4},{16,24},{20,28},{24,16},{28,20},{1,9},{5... | collective-permute-start | bytes 393224 | tf_op jit(solution)/shard_map/ppermute | solution.py:222
  105.1 8.8 %collective-permute-start.19 = (bf16[16,32,128]{2,1,0:T(8,128)(2,1)S(1)}, bf16[16,32,128]{2,1,0:T(8,128)(2,1)S(1)}, u32[]{:S(2)}, u32[]{:S(2)}) collective-permute-start(bf16[16,32,128]{2,1,0:T(8,128)(2,1)S(1)} %get-tuple-element.52), channel_id=1, source_target_pairs={{0,16},{4,20},{8,24},{12,28},{16,0},{20,4},{24,8},{28,12},{1,17},{... | collective-permute-start | bytes 393224 | tf_op jit(solution)/shard_map/ppermute | solution.py:222
  106.4 7.5 %collective-permute-start.20 = (bf16[16,32,128]{2,1,0:T(8,128)(2,1)S(1)}, bf16[16,32,128]{2,1,0:T(8,128)(2,1)S(1)}, u32[]{:S(2)}, u32[]{:S(2)}) collective-permute-start(bf16[16,32,128]{2,1,0:T(8,128)(2,1)S(1)} %get-tuple-element.53), channel_id=1, source_target_pairs={{0,24},{4,28},{8,16},{12,20},{16,8},{20,12},{24,0},{28,4},{1,25},{... | collective-permute-start | bytes 393224 | tf_op jit(solution)/shard_map/ppermute | solution.py:222

commit v2 on v0

v2 whole, which is shorter than its diff:
```python
import functools

import jax
import jax.numpy as jnp
import numpy as np
from jax import lax
from jax.experimental import pallas as pl
from jax.experimental.pallas import tpu as pltpu
from jax.sharding import PartitionSpec as P

ITERS = 3
UNROLL = 8
CORES = 2
VMEM_LIMIT = 24 * 1024 * 1024

NT = (((1,), (1,)), ((), ()))


def in_vmem():
    return pl.BlockSpec(memory_space=pltpu.VMEM)


def in_hbm():
    return pl.BlockSpec(memory_space=pltpu.HBM)


def in_smem():
    return pl.BlockSpec(memory_space=pltpu.SMEM)


def stay_in_hbm(array):
    return pltpu.with_memory_space_constraint(array, pltpu.HBM)


def params():
    return pltpu.CompilerParams(vmem_limit_bytes=VMEM_LIMIT)


def split(value):
    high = value.astype(jnp.bfloat16)
    low = (value - high.astype(jnp.float32)).astype(jnp.bfloat16)
    return high, low


def times_block(field, high, low):
    field_high, field_low = split(field)
    rhs = field.shape[0]
    both = jnp.concatenate([field_high, field_low], axis=0)
    first = lax.dot_general(both, high, NT, preferred_element_type=jnp.float32)
    second = lax.dot_general(field_high, low, NT, preferred_element_type=jnp.float32)
    return first[:rhs] + (first[rhs:] + second)


def partner(chip, shift, chips):
    if chips & (chips - 1) == 0:
        return chip ^ shift
    return (chip + shift) % chips


def halves(value, size):
    if size & (size - 1) == 0:
        return lax.shift_right_logical(value, size.bit_length() - 1), value & (size - 1)
    return lax.div(value, size), lax.rem(value, size)


def gather_stages(groups, parts):
    near = sorted({shift for shift in (1, groups - 1) if 0 < shift < groups})
    far = [shift for shift in range(1, groups) if shift not in near]
    stages = [[(part, 0) for part in range(parts)]]
    for part in range(parts - 1):
        stages.append([(part, shift) for shift in near + far])
    stages.append([(parts - 1, shift) for shift in near])
    stages.append([(parts - 1, shift) for shift in far])
    return [stage for stage in stages if stage]


def start_kernel(parts, precond_hbm, rhs_hbm, high_ref, low_ref, *refs):
    sol_refs, refs = refs[:parts], refs[parts:]
    left_refs, refs = refs[:parts], refs[parts:]
    rounded_refs, (precond_ref, rhs_ref, sems) = refs[:parts], refs[parts:]
    owned = rhs_ref.shape[0]
    loads_total = sems.shape[0] - 1
    each = owned // loads_total
    loads = [pltpu.make_async_copy(rhs_hbm, rhs_ref, sems.at[loads_total])]
    for load in range(loads_total):
        at = pl.ds(load * each, each)
        loads.append(pltpu.make_async_copy(precond_hbm.at[at], precond_ref.at[at], sems.at[load]))
    for load in loads:
        load.start()
    loads[0].wait()
    for load in range(loads_total):
        loads[1 + load].wait()
        for p in range(load * each, (load + 1) * each):
            part, inner = divmod(p, owned // parts)
            high, low = split(precond_ref[p])
            high_ref[p] = high
            low_ref[p] = low
            value = times_block(rhs_ref[p], high, low)
            sol_refs[part][inner] = value
            left_refs[part][inner] = rhs_ref[p]
            rounded_refs[part][inner] = value.astype(jnp.bfloat16)


def updated(p, inner, pieces, high_ref, low_ref, left_ref, sol_ref, keep_ref):
    left = left_ref[inner]
    for piece_ref in pieces:
        left = left - piece_ref[inner].astype(jnp.float32)
    before = sol_ref[inner]
    residual = left - before - keep_ref[inner]
    return before + times_block(residual, high_ref[p], low_ref[p]), left


def apply_kernel(base, pieces, high_ref, low_ref, left_ref, sol_ref, keep_ref, *refs):
    piece_refs, (new_ref, new_left_ref, rounded_ref) = refs[:pieces], refs[pieces:]
    for inner in range(sol_ref.shape[0]):
        value, left = updated(base + inner, inner, piece_refs, high_ref, low_ref, left_ref, sol_ref, keep_ref)
        new_ref[inner] = value
        new_left_ref[inner] = left
        rounded_ref[inner] = value.astype(jnp.bfloat16)


def finish_kernel(base, pieces, earlier, high_ref, low_ref, left_ref, sol_ref, keep_ref, *refs):
    piece_refs, refs = refs[:pieces], refs[pieces:]
    done_refs, (out_hbm, value_ref, sems) = refs[:earlier], refs[earlier:]
    each = sol_ref.shape[0]
    stores = [
        pltpu.make_async_copy(done, out_hbm.at[pl.ds(part * each, each)], sems.at[part])
        for part, done in enumerate(done_refs)
    ]
    for store in stores:
        store.start()
    for inner in range(each):
        value_ref[inner], _ = updated(
            base + inner, inner, piece_refs, high_ref, low_ref, left_ref, sol_ref, keep_ref)
    last = pltpu.make_async_copy(value_ref, out_hbm.at[pl.ds(base, each)], sems.at[earlier])
    last.start()
    for store in stores:
        store.wait()
    last.wait()


def order_kernel(group, owned, groups, parts, bits, table_ref, position_ref, count_ref, rows_ref, cols_ref,
                 values_hbm, list_out, total_out, values_out, sem):
    load = pltpu.make_async_copy(values_hbm, values_out, sem)
    load.start()
    core = position_ref[0] & (CORES - 1)
    mine = position_ref[1]
    each = owned // parts
    row_bits, col_bits = bits
    lists = total_out.shape[0]
    trash = (group // CORES // parts) << col_bits

    def clear(index, carry):
        total_out[index] = 0
        return carry

    lax.fori_loop(0, lists, clear, 0)

    def place(slot, carry):
        owner, row_owned = halves(halves(rows_ref[0, 0, slot], group)[1], owned)
        row_part, row_inner = halves(row_owned, each)
        source, rest = halves(cols_ref[0, 0, slot], group)
        col_part, col_inner = halves(halves(rest, owned)[1], each)
        half = 1 - ((owner & (CORES - 1)) ^ core)
        shift = mine - source
        shift = jnp.where(shift < 0, shift + groups, shift)
        stage, base = halves(table_ref[col_part * groups + shift], 1 << col_bits)
        which = (stage * parts + row_part) * CORES + half
        row = lax.shift_right_logical(owner, 1) * each + row_inner
        at = total_out[which]
        list_out[which, at] = (((slot << row_bits) | row) << col_bits) | (base + col_inner)
        total_out[which] = at + 1
        return carry

    lax.fori_loop(0, count_ref[0, 0], place, 0)

    def close(index, carry):
        for extra in range(UNROLL):
            list_out[index, total_out[index] + extra] = trash
        return carry

    lax.fori_loop(0, lists, close, 0)
    load.wait()


def add_products(which, bits, list_ref, total_ref, values_ref, field_ref, total):
    row_bits, col_bits = bits

    def step(chunk, carry):
        terms = []
        for lane in range(UNROLL):
            entry = list_ref[which, chunk * UNROLL + lane]
            col = entry & ((1 << col_bits) - 1)
            row = lax.shift_right_logical(entry, col_bits) & ((1 << row_bits) - 1)
            slot = lax.shift_right_logical(entry, col_bits + row_bits)
            term = lax.dot_general(
                field_ref[col], values_ref[slot], NT, preferred_element_type=jnp.float32)
            terms.append((row, term))
        for row, term in terms:
            total[row] += term
        return carry

    lax.fori_loop(0, lax.div(total_ref[which] + UNROLL - 1, UNROLL), step, 0)


def join(pieces, field):
    each = pieces[0].shape[0]
    for index, piece in enumerate(pieces):
        field[pl.ds(index * each, each)] = piece[...]


def first_kernel(steps, parts, chips, bits, position_ref, list_ref, total_ref, values_ref, *refs):
    lists = parts * CORES
    piece_refs, refs = refs[:parts], refs[parts:]
    out_refs, refs = refs[:steps], refs[steps:]
    in_refs, refs = refs[:steps], refs[steps:]
    sent_refs, totals, field = refs[:-lists - 1], refs[-lists - 1:-1], refs[-1]
    chip = lax.shift_right_logical(position_ref[0], 1)
    join(piece_refs, field)
    for index, total in enumerate(totals):
        part, half = divmod(index, CORES)
        rows = total.shape[0] - 1
        each = rows // chips
        if steps == 0:
            total[...] = jnp.zeros(total.shape, jnp.float32)
        elif half == 0:
            at = pl.ds(part * rows, rows)
            total[pl.ds(0, rows)] = -sum(out_ref[at].astype(jnp.float32) for out_ref in out_refs)
        else:
            for shift in range(chips):
                at = partner(chip, shift, chips) * each
                value = sum(in_ref[pl.ds(part * rows + at, each)].astype(jnp.float32) for in_ref in in_refs)
                if shift > 0:
                    for step in range(steps):
                        value -= sent_refs[(step * parts + part) * (chips - 1) + shift - 1][...].astype(jnp.float32)
                total[pl.ds(at, each)] = value
        add_products(index, bits, list_ref, total_ref, values_ref, field, total)


def stage_kernel(stage, bits, pieces, lists, list_ref, total_ref, values_ref, *refs):
    piece_refs, refs = refs[:pieces], refs[pieces:]
    totals, field = refs[-lists - 1:-1], refs[-1]
    join(piece_refs, field)
    for index, total in enumerate(totals):
        add_products(stage * lists + index, bits, list_ref, total_ref, values_ref, field, total)


def last_kernel(stage, half, bits, pieces, parts, list_ref, total_ref, values_ref, *refs):
    piece_refs, refs = refs[:pieces], refs[pieces + parts:]
    totals, outs, field = refs[:parts], refs[parts:-1], refs[-1]
    join(piece_refs, field)
    for part, total in enumerate(totals):
        add_products(
            (stage * parts + part) * CORES + half, bits, list_ref, total_ref, values_ref, field, total)
        for out_ref in outs:
            rows = total.shape[0] - 1
            out_ref[pl.ds(part * rows, rows)] = total[pl.ds(0, rows)].astype(out_ref.dtype)


def combine_kernel(part, chips, position_ref, own_ref, other_ref, keep_ref, *send_refs):
    chip = lax.shift_right_logical(position_ref[0], 1)
    each = keep_ref.shape[0]
    for shift in range(chips):
        at = partner(chip, shift, chips) * each
        value = own_ref[pl.ds(at, each)] + other_ref[pl.ds(part * chips * each + at, each)].astype(jnp.float32)
        if shift == 0:
            keep_ref[...] = value
        else:
            send_refs[shift - 1][...] = value.astype(jnp.bfloat16)


def per_device(block_values, block_rows, block_cols, block_counts, precond, right_side):
    owned, rhs, size = right_side.shape[1:]
    row_devices = lax.axis_size("row")
    groups = lax.axis_size("col")
    chips = row_devices // CORES
    group = owned * row_devices
    slots = block_values.shape[2]
    parts = 2 if owned % 2 == 0 else 1
    each = owned // parts
    part_rows = chips * each
    position = jnp.stack([lax.axis_index("row"), lax.axis_index("col")]).astype(jnp.int32)

    stages = gather_stages(groups, parts)
    final = len(stages) - 1
    lists_each = parts * CORES
    widest = max(len(stage) for stage in stages) * each
    row_bits, col_bits = bits = part_rows.bit_length(), (widest - 1).bit_length()
    assert (slots - 1).bit_length() + row_bits + col_bits <= 31
    table = np.zeros(parts * groups, np.int32)
    for index, stage in enumerate(stages):
        for place, (part, shift) in enumerate(stage):
            table[part * groups + shift] = (index << col_bits) + place * each

    part_type = jax.ShapeDtypeStruct((each, rhs, size), jnp.float32)
    rounded_type = jax.ShapeDtypeStruct((each, rhs, size), jnp.bfloat16)
    matrix_type = jax.ShapeDtypeStruct((owned, size, size), jnp.bfloat16)
    total_type = jax.ShapeDtypeStruct((part_rows + 1, rhs, size), jnp.float32)

    loads = next(count for count in (4, 2, 1) if owned % count == 0)
    high, low, *fields = pl.pallas_call(
        functools.partial(start_kernel, parts),
        out_shape=[matrix_type] * 2 + [part_type] * (2 * parts) + [rounded_type] * parts,
        in_specs=[in_hbm()] * 2,
        out_specs=[in_vmem()] * (2 + 3 * parts),
        scratch_shapes=[
            pltpu.VMEM((owned, size, size), jnp.float32),
            pltpu.VMEM((owned, rhs, size), jnp.float32),
            pltpu.SemaphoreType.DMA((loads + 1,)),
        ],
        compiler_params=params(),
        name="start",
    )(stay_in_hbm(precond[0]), stay_in_hbm(right_side[0]))
    sols, lefts, rounded = fields[:parts], fields[parts:2 * parts], fields[2 * parts:]

    *lists, values = pl.pallas_call(
        functools.partial(order_kernel, group, owned, groups, parts, bits),
        out_shape=[
            jax.ShapeDtypeStruct((len(stages) * lists_each, slots + UNROLL), jnp.int32),
            jax.ShapeDtypeStruct((len(stages) * lists_each,), jnp.int32),
            pltpu.VMEM(block_values.shape[2:], block_values.dtype),
        ],
        in_specs=[in_smem()] * 5 + [in_hbm()],
        out_specs=[in_smem()] * 2 + [in_vmem()],
        scratch_shapes=[pltpu.SemaphoreType.DMA],
        compiler_params=params(),
        name="order",
    )(table, position, block_counts, block_rows, block_cols, stay_in_hbm(block_values[0, 0]))

    def cost(share):
        return pl.CostEstimate(
            flops=int(slots * share) * 2 * rhs * size * size,
            bytes_accessed=int(slots * share) * 2 * size * size, transcendentals=0)

    def field_scratch(pieces):
        return pltpu.VMEM((len(pieces) * each, rhs, size), jnp.bfloat16)

    def product_first(pieces, outs, ins, sent):
        return pl.pallas_call(
            functools.partial(first_kernel, len(outs), parts, chips, bits),
            out_shape=[total_type] * lists_each,
            in_specs=[in_smem()] * 3 + [in_vmem()] * (1 + len(pieces) + len(outs) + len(ins) + len(sent)),
            out_specs=[in_vmem()] * lists_each,
            scratch_shapes=[field_scratch(pieces)],
            compiler_params=params(),
            cost_estimate=cost(len(pieces) / groups / parts),
            name="stage0",
        )(position, *lists, values, *pieces, *outs, *ins, *sent)

    def product_stage(stage, pieces, totals):
        inputs = 3 + len(pieces)
        return pl.pallas_call(
            functools.partial(stage_kernel, stage, bits, len(pieces), lists_each),
            out_shape=[total_type] * lists_each,
            in_specs=[in_smem()] * 2 + [in_vmem()] * (1 + len(pieces) + len(totals)),
            out_specs=[in_vmem()] * lists_each,
            scratch_shapes=[field_scratch(pieces)],
            input_output_aliases={inputs + index: index for index in range(len(totals))},
            compiler_params=params(),
            cost_estimate=cost(len(pieces) / groups / parts),
            name="stage%d" % stage,
        )(*lists, values, *pieces, *totals)

    def product_last(half, pieces, totals):
        send = [jax.ShapeDtypeStruct((parts * part_rows, rhs, size), jnp.bfloat16)] if half == 0 else []
        inputs = 3 + len(pieces)
        return pl.pallas_call(
            functools.partial(last_kernel, final, half, bits, len(pieces), parts),
            out_shape=[total_type] * parts + send,
            in_specs=[in_smem()] * 2 + [in_vmem()] * (1 + len(pieces) + parts),
            out_specs=[in_vmem()] * (parts + len(send)),
            scratch_shapes=[field_scratch(pieces)],
            input_output_aliases={inputs + part: part for part in range(parts)},
            compiler_params=params(),
            cost_estimate=cost(len(pieces) / groups / parts / CORES),
            name="last%d" % half,
        )(*lists, values, *pieces, *totals)

    swap = [(r, r ^ 1) for r in range(row_devices)]
    outs, ins, sent = [], [], []
    for step in range(ITERS):
        gathered = {}
        for part in range(parts):
            gathered[part, 0] = rounded[part]
            for _, shift in [entry for stage in stages[1:] for entry in stage if entry[0] == part]:
                ring = [(c, (c + shift) % groups) for c in range(groups)]
                gathered[part, shift] = lax.ppermute(rounded[part], "col", ring)
        totals = product_first([gathered[entry] for entry in stages[0]], outs, ins, sent)
        for stage in range(1, final):
            totals = product_stage(stage, [gathered[entry] for entry in stages[stage]], totals)
        tail = [gathered[entry] for entry in stages[final]]
        outgoing = product_last(0, tail, totals[0::CORES])[-1]
        incoming = lax.ppermute(outgoing, "row", swap)
        own = product_last(1, tail, totals[1::CORES])
        outs.append(outgoing)
        ins.append(incoming)
        received = []
        for part in range(parts):
            keep, *sends = pl.pallas_call(
                functools.partial(combine_kernel, part, chips),
                out_shape=[part_type] + [rounded_type] * (chips - 1),
                in_specs=[in_smem()] + [in_vmem()] * 2,
                out_specs=[in_vmem()] * chips,
                compiler_params=params(),
                name="combine%d" % part,
            )(position, own[part], incoming)
            sent += sends
            pieces = []
            for shift in reversed(range(1, chips)):
                pairs = [
                    (chip * CORES + core, partner(chip, shift, chips) * CORES + core)
                    for chip in range(chips) for core in range(CORES)
                ]
                pieces.append(lax.ppermute(sends[shift - 1], "row", pairs))
            received.append([keep] + pieces)
        results = []
        for part in range(parts):
            base, inputs = part * each, received[part]
            if step == ITERS - 1 and part == parts - 1:
                return pl.pallas_call(
                    functools.partial(finish_kernel, base, len(inputs) - 1, parts - 1),
                    out_shape=jax.ShapeDtypeStruct((owned, rhs, size), jnp.float32),
                    in_specs=[in_vmem()] * (4 + len(inputs) + parts - 1),
                    out_specs=in_hbm(),
                    scratch_shapes=[
                        pltpu.VMEM((each, rhs, size), jnp.float32),
                        pltpu.SemaphoreType.DMA((parts,)),
                    ],
                    compiler_params=params(),
                    name="finish",
                )(high, low, lefts[part], sols[part], *inputs, *[result[0] for result in results])[None]
            results.append(pl.pallas_call(
                functools.partial(apply_kernel, base, len(inputs) - 1),
                out_shape=[part_type, part_type, rounded_type],
                in_specs=[in_vmem()] * (4 + len(inputs)),
                out_specs=[in_vmem()] * 3,
                compiler_params=params(),
                name="apply%d" % part,
            )(high, low, lefts[part], sols[part], *inputs))
        sols, lefts, rounded = [list(column) for column in zip(*results)]


def solution(mesh):
    placed = (
        P("row", "col", None, None, None),
        P("row", "col", None),
        P("row", "col", None),
        P("row", "col"),
        P("col", "row", None, None),
        P("col", "row", None, None),
    )
    return jax.shard_map(
        per_device,
        mesh=mesh,
        in_specs=placed,
        out_specs=P("col", "row", None, None),
        check_vma=False,
    )
```

time: 290 us -> 107 us (0.37)
  waiting for transfers between devices: 127 us -> 7.19 us
  starting transfers between devices: 0.09 us -> 56.7 us
  other arithmetic: 52.6 us -> 0.07 us
  blocking collectives: 48.8 us -> 0 us
  Pallas kernels: 0 us -> 39.2 us
  matrix products: 37.6 us -> 0 us
  between operations: 13.9 us -> 0.93 us
  local copies, waits for them, and re-layouts: 7.91 us -> 2.01 us
    reduce_scatter x3 -> x0, waiting for transfers between devices: 127 us -> none  [per_device(): lax.psum_scatter(partial_value, 'row', scatter_dimension=0, tiled=True)]
    ppermute x0 -> x39, starting transfers between devices: none -> 56.7 us  [the longest x18 28.7 us: per_device(): pieces.append(lax.ppermute(sends[shift - 1], 'row', pairs))]
    scatter-add x3 -> x0, other arithmetic: 51.8 us -> none  [per_device(): partial_value = jax.ops.segment_sum(terms, row_local, num_segments=group)]
    all_gather x3 -> x0, blocking collectives: 48.8 us -> none  [per_device(): lax.all_gather(solution.astype(jnp.bfloat16)[None], 'col', axis=1, tiled=...]
    pallas_call x0 -> x29, Pallas kernels: none -> 39.2 us  [the longest x6 11.8 us: product_stage(): pl.pallas_call(functools.partial(stage_kernel, stage, bits, len(pieces),...]
    dot_general x7 -> x0, matrix products: 37.6 us -> none  [the longest x3 23.5 us: block_terms(): jnp.einsum('ski,soi->sko', gathered, values, preferred_element_type=jnp.f...]
    ppermute x0 -> x39, waiting for transfers between devices: none -> 7.19 us  [the longest x18 3.89 us: per_device(): pieces.append(lax.ppermute(sends[shift - 1], 'row', pairs))]
  transfers between devices with their start and end apart: 3 -> 39, of which waited for: 3 -> 10; matrix products, arithmetic and copies ran while one was open for 0% -> 0% of each run, Pallas kernels for 0% -> 28%
where the time goes in v2:
time: 107 us; the launch traced here: 106 us
  starting transfers between devices  56.7 us (53%)
  Pallas kernels  39.2 us (37%)
  waiting for transfers between devices  7.19 us (7%)
  local copies, waits for them, and re-layouts  2.01 us (2%)
    ppermute x18, starting transfers between devices, per_device(): pieces.append(lax.ppermute(sends[shift - 1], 'row', pairs))  28.7 us
    ppermute x18, starting transfers between devices, per_device(): gathered[part, shift] = lax.ppermute(rounded[part], 'col', ring)  27.7 us
    pallas_call x6, Pallas kernels, product_stage(): pl.pallas_call(functools.partial(stage_kernel, stage, bits, len(pieces),...  11.8 us
    pallas_call x6, Pallas kernels, product_last(): pl.pallas_call(functools.partial(last_kernel, final, half, bits, len(piec...  7.38 us
    pallas_call x3, Pallas kernels, product_first(): pl.pallas_call(functools.partial(first_kernel, len(outs), parts, chips, b...  6.25 us
    pallas_call x1, Pallas kernels, per_device(): pl.pallas_call(functools.partial(order_kernel, group, owned, groups, part...  4.23 us
    ppermute x18, waiting for transfers between devices, per_device(): pieces.append(lax.ppermute(sends[shift - 1], 'row', pairs))  3.89 us
    pallas_call x6, Pallas kernels, per_device(): pl.pallas_call(functools.partial(combine_kernel, part, chips), out_shape=...  3.57 us
  transfers between devices with their start and end apart: 39, of which 10 were waited for; matrix products, arithmetic and copies ran while one was open for 0% of the time, Pallas kernels for 28%

profile of v2, /device:TPU:0, one launch (start us, length us, event | category | flops | bytes accessed | tf_op | source)
XLA Modules:
  0.0 106.1 jit_solution(8249785538863913107)
XLA Ops:
  0.0 2.2 %start.1 = (bf16[16,128,128]{2,1,0:T(8,128)(2,1)S(1)}, bf16[16,128,128]{2,1,0:T(8,128)(2,1)S(1)}, f32[8,32,128]{2,1,0:T(8,128)S(1)}, f32[8,32,128]{2,1,0:T(8,128...) custom-call(f32[16,128,128]{2,1,0:T(8,128)} %bitcast.7, ...), custom_call_target="tpu_custom_call" | custom-call | tf_op jit(solution)/shard_map/start/pallas_call | solution.py:301
  2.2 3.1 %collective-permute-start.3 = (bf16[8,32,128]{2,1,0:T(8,128)(2,1)S(1)}, bf16[8,32,128]{2,1,0:T(8,128)(2,1)S(1)}, u32[]{:S(2)}, u32[]{:S(2)}) collective-permute-start(bf16[8,32,128]{2,1,0:T(8,128)(2,1)S(1)} %get-tuple-element.106.refs_0_), channel_id=1, source_target_pairs={{0,1},{1,2},{2,3},{3,0},{4,5},{5,6},{6,7},{7,4},{8,9},{9,10},{10,1... | collective-permute-start | bytes 196616 | tf_op jit(solution)/shard_map/ppermute | solution.py:387
  5.3 2.1 %collective-permute-start.4 = (bf16[8,32,128]{2,1,0:T(8,128)(2,1)S(1)}, bf16[8,32,128]{2,1,0:T(8,128)(2,1)S(1)}, u32[]{:S(2)}, u32[]{:S(2)}) collective-permute-start(bf16[8,32,128]{2,1,0:T(8,128)(2,1)S(1)} %get-tuple-element.106.refs_0_), channel_id=1, source_target_pairs={{0,3},{1,0},{2,1},{3,2},{4,7},{5,4},{6,5},{7,6},{8,11},{9,8},{10,9... | collective-permute-start | bytes 196616 | tf_op jit(solution)/shard_map/ppermute | solution.py:387
  8.3 1.6 %collective-permute-start.1 = (bf16[8,32,128]{2,1,0:T(8,128)(2,1)S(1)}, bf16[8,32,128]{2,1,0:T(8,128)(2,1)S(1)}, u32[]{:S(2)}, u32[]{:S(2)}) collective-permute-start(bf16[8,32,128]{2,1,0:T(8,128)(2,1)S(1)} %get-tuple-element.105.refs_1_), channel_id=1, source_target_pairs={{0,1},{1,2},{2,3},{3,0},{4,5},{5,6},{6,7},{7,4},{8,9},{9,10},{10,1... | collective-permute-start | bytes 196616 | tf_op jit(solution)/shard_map/ppermute | solution.py:387
  9.9 2.2 %collective-permute-start.2 = (bf16[8,32,128]{2,1,0:T(8,128)(2,1)S(1)}, bf16[8,32,128]{2,1,0:T(8,128)(2,1)S(1)}, u32[]{:S(2)}, u32[]{:S(2)}) collective-permute-start(bf16[8,32,128]{2,1,0:T(8,128)(2,1)S(1)} %get-tuple-element.105.refs_1_), channel_id=1, source_target_pairs={{0,3},{1,0},{2,1},{3,2},{4,7},{5,4},{6,5},{7,6},{8,11},{9,8},{10,9... | collective-permute-start | bytes 196616 | tf_op jit(solution)/shard_map/ppermute | solution.py:387
  15.0 4.2 %order.1 = (s32[16,200]{1,0:T(8,128)S(1)}, s32[16]{0:T(128)S(1)}, bf16[192,128,128]{2,1,0:T(8,128)(2,1)S(1)}) custom-call(s32[8]{0:T(128)S(1)} %copy-done.2, s32[2]{0:T(128)S(1)} %pad_add_fusion.position_ref, s32[1,1]{1,0:T(1,128)S(6)} %copy.80.count_ref, s32[1,1,192]{2,1,0:T(1,128)S(1)} %copy-done, s32[1,1,192]{2,1,0:T(1,128)S(1)} %copy-done.1, ...), custom_call_target="tpu_custom_call" | custom-call | tf_op jit(solution)/shard_map/order/pallas_call | solution.py:316
  19.3 2.0 %stage0.3 = (f32[33,32,128]{2,1,0:T(8,128)S(1)}, f32[33,32,128]{2,1,0:T(8,128)S(1)}, f32[33,32,128]{2,1,0:T(8,128)S(1)}, f32[33,32,128]{2,1,0:T(8,128)S(1)}) custom-call(s32[2]{0:T(128)S(1)} %pad_add_fusion.position_ref, s32[16,200]{1,0:T(8,128)S(1)} %get-tuple-element.102.list_ref, s32[16]{0:T(128)S(1)} %get-tuple-element.103.total_ref, ...), custom_call_target="tpu_custom_call" | custom-call | flops 50331648 | bytes 1572864 | tf_op jit(solution)/shard_map/stage0/pallas_call | solution.py:339
  21.3 2.1 %stage1.3 = (f32[33,32,128]{2,1,0:T(8,128)S(1)}, f32[33,32,128]{2,1,0:T(8,128)S(1)}, f32[33,32,128]{2,1,0:T(8,128)S(1)}, f32[33,32,128]{2,1,0:T(8,128)S(1)}) custom-call(s32[16,200]{1,0:T(8,128)S(1)} %get-tuple-element.102.list_ref, s32[16]{0:T(128)S(1)} %get-tuple-element.103.total_ref, ...), custom_call_target="tpu_custom_call", output_to_operand_aliasing={{0}: (6, {}), {1}: (7, {}), {2}: (8, {}), {3}: (9, {})} | custom-call | flops 75497472 | bytes 2359296 | tf_op jit(solution)/shard_map/stage1/pallas_call | solution.py:352
  23.4 1.8 %stage2.3 = (f32[33,32,128]{2,1,0:T(8,128)S(1)}, f32[33,32,128]{2,1,0:T(8,128)S(1)}, f32[33,32,128]{2,1,0:T(8,128)S(1)}, f32[33,32,128]{2,1,0:T(8,128)S(1)}) custom-call(s32[16,200]{1,0:T(8,128)S(1)} %get-tuple-element.102.list_ref, s32[16]{0:T(128)S(1)} %get-tuple-element.103.total_ref, ...), custom_call_target="tpu_custom_call", output_to_operand_aliasing={{0}: (5, {}), {1}: (6, {}), {2}: (7, {}), {3}: (8, {})} | custom-call | flops 50331648 | bytes 1572864 | tf_op jit(solution)/shard_map/stage2/pallas_call | solution.py:352
  25.3 1.4 %last0.3 = (f32[33,32,128]{2,1,0:T(8,128)S(1)}, f32[33,32,128]{2,1,0:T(8,128)S(1)}, bf16[64,32,128]{2,1,0:T(8,128)(2,1)S(1)}) custom-call(s32[16,200]{1,0:T(8,128)S(1)} %get-tuple-element.102.list_ref, s32[16]{0:T(128)S(1)} %get-tuple-element.103.total_ref, ...), custom_call_target="tpu_custom_call", output_to_operand_aliasing={{0}: (4, {}), {1}: (5, {})} | custom-call | flops 12582912 | bytes 393216 | tf_op jit(solution)/shard_map/last0/pallas_call | solution.py:367
  29.3 1.9 %collective-permute-start.13 = (bf16[8,32,128]{2,1,0:T(8,128)(2,1)S(1)}, bf16[8,32,128]{2,1,0:T(8,128)(2,1)S(1)}, u32[]{:S(2)}, u32[]{:S(2)}) collective-permute-start(bf16[8,32,128]{2,1,0:T(8,128)(2,1)S(1)} %get-tuple-element.132.refs_6_.refs_8_), channel_id=1, source_target_pairs={{0,24},{4,28},{8,16},{12,20},{16,8},{20,12},{24,0},{28,4},{1,25},{... | collective-permute-start | bytes 196616 | tf_op jit(solution)/shard_map/ppermute | solution.py:414
  31.2 4.9 %collective-permute-start.14 = (bf16[8,32,128]{2,1,0:T(8,128)(2,1)S(1)}, bf16[8,32,128]{2,1,0:T(8,128)(2,1)S(1)}, u32[]{:S(2)}, u32[]{:S(2)}) collective-permute-start(bf16[8,32,128]{2,1,0:T(8,128)(2,1)S(1)} %get-tuple-element.133.refs_5_.refs_7_), channel_id=1, source_target_pairs={{0,16},{4,20},{8,24},{12,28},{16,0},{20,4},{24,8},{28,12},{1,17},{... | collective-permute-start | bytes 196616 | tf_op jit(solution)/shard_map/ppermute | solution.py:414
  36.7 1.5 %collective-permute-start.7 = (bf16[8,32,128]{2,1,0:T(8,128)(2,1)S(1)}, bf16[8,32,128]{2,1,0:T(8,128)(2,1)S(1)}, u32[]{:S(2)}, u32[]{:S(2)}) collective-permute-start(bf16[8,32,128]{2,1,0:T(8,128)(2,1)S(1)} %get-tuple-element.122.refs_9_.refs_11_), channel_id=1, source_target_pairs={{0,24},{4,28},{8,16},{12,20},{16,8},{20,12},{24,0},{28,4},{1,25},{... | collective-permute-start | bytes 196616 | tf_op jit(solution)/shard_map/ppermute | solution.py:414
  38.2 2.0 %collective-permute-start.8 = (bf16[8,32,128]{2,1,0:T(8,128)(2,1)S(1)}, bf16[8,32,128]{2,1,0:T(8,128)(2,1)S(1)}, u32[]{:S(2)}, u32[]{:S(2)}) collective-permute-start(bf16[8,32,128]{2,1,0:T(8,128)(2,1)S(1)} %get-tuple-element.123.refs_8_.refs_10_), channel_id=1, source_target_pairs={{0,16},{4,20},{8,24},{12,28},{16,0},{20,4},{24,8},{28,12},{1,17},{... | collective-permute-start | bytes 196616 | tf_op jit(solution)/shard_map/ppermute | solution.py:414
  42.5 2.7 %collective-permute-start.17 = (bf16[8,32,128]{2,1,0:T(8,128)(2,1)S(1)}, bf16[8,32,128]{2,1,0:T(8,128)(2,1)S(1)}, u32[]{:S(2)}, u32[]{:S(2)}) collective-permute-start(bf16[8,32,128]{2,1,0:T(8,128)(2,1)S(1)} %get-tuple-element.135.refs_0_), channel_id=1, source_target_pairs={{0,3},{1,0},{2,1},{3,2},{4,7},{5,4},{6,5},{7,6},{8,11},{9,8},{10,9... | collective-permute-start | bytes 196616 | tf_op jit(solution)/shard_map/ppermute | solution.py:387
  46.2 3.8 %collective-permute-start.12 = (bf16[8,32,128]{2,1,0:T(8,128)(2,1)S(1)}, bf16[8,32,128]{2,1,0:T(8,128)(2,1)S(1)}, u32[]{:S(2)}, u32[]{:S(2)}) collective-permute-start(bf16[8,32,128]{2,1,0:T(8,128)(2,1)S(1)} %get-tuple-element.127.refs_1_), channel_id=1, source_target_pairs={{0,3},{1,0},{2,1},{3,2},{4,7},{5,4},{6,5},{7,6},{8,11},{9,8},{10,9... | collective-permute-start | bytes 196616 | tf_op jit(solution)/shard_map/ppermute | solution.py:387
  50.6 2.0 %stage0.4 = (f32[33,32,128]{2,1,0:T(8,128)S(1)}, f32[33,32,128]{2,1,0:T(8,128)S(1)}, f32[33,32,128]{2,1,0:T(8,128)S(1)}, f32[33,32,128]{2,1,0:T(8,128)S(1)}) custom-call(s32[2]{0:T(128)S(1)} %pad_add_fusion.position_ref, s32[16,200]{1,0:T(8,128)S(1)} %get-tuple-element.102.list_ref, s32[16]{0:T(128)S(1)} %get-tuple-element.103.total_ref, ...), custom_call_target="tpu_custom_call" | custom-call | flops 50331648 | bytes 1572864 | tf_op jit(solution)/shard_map/stage0/pallas_call | solution.py:339
  53.1 2.1 %stage1.4 = (f32[33,32,128]{2,1,0:T(8,128)S(1)}, f32[33,32,128]{2,1,0:T(8,128)S(1)}, f32[33,32,128]{2,1,0:T(8,128)S(1)}, f32[33,32,128]{2,1,0:T(8,128)S(1)}) custom-call(s32[16,200]{1,0:T(8,128)S(1)} %get-tuple-element.102.list_ref, s32[16]{0:T(128)S(1)} %get-tuple-element.103.total_ref, ...), custom_call_target="tpu_custom_call", output_to_operand_aliasing={{0}: (6, {}), {1}: (7, {}), {2}: (8, {}), {3}: (9, {})} | custom-call | flops 75497472 | bytes 2359296 | tf_op jit(solution)/shard_map/stage1/pallas_call | solution.py:352
  55.2 1.8 %stage2.4 = (f32[33,32,128]{2,1,0:T(8,128)S(1)}, f32[33,32,128]{2,1,0:T(8,128)S(1)}, f32[33,32,128]{2,1,0:T(8,128)S(1)}, f32[33,32,128]{2,1,0:T(8,128)S(1)}) custom-call(s32[16,200]{1,0:T(8,128)S(1)} %get-tuple-element.102.list_ref, s32[16]{0:T(128)S(1)} %get-tuple-element.103.total_ref, ...), custom_call_target="tpu_custom_call", output_to_operand_aliasing={{0}: (5, {}), {1}: (6, {}), {2}: (7, {}), {3}: (8, {})} | custom-call | flops 50331648 | bytes 1572864 | tf_op jit(solution)/shard_map/stage2/pallas_call | solution.py:352
  57.1 1.4 %last0.4 = (f32[33,32,128]{2,1,0:T(8,128)S(1)}, f32[33,32,128]{2,1,0:T(8,128)S(1)}, bf16[64,32,128]{2,1,0:T(8,128)(2,1)S(1)}) custom-call(s32[16,200]{1,0:T(8,128)S(1)} %get-tuple-element.102.list_ref, s32[16]{0:T(128)S(1)} %get-tuple-element.103.total_ref, ...), custom_call_target="tpu_custom_call", output_to_operand_aliasing={{0}: (4, {}), {1}: (5, {})} | custom-call | flops 12582912 | bytes 393216 | tf_op jit(solution)/shard_map/last0/pallas_call | solution.py:367
  61.8 4.7 %collective-permute-start.27 = (bf16[8,32,128]{2,1,0:T(8,128)(2,1)S(1)}, bf16[8,32,128]{2,1,0:T(8,128)(2,1)S(1)}, u32[]{:S(2)}, u32[]{:S(2)}) collective-permute-start(bf16[8,32,128]{2,1,0:T(8,128)(2,1)S(1)} %get-tuple-element.162.refs_13_), channel_id=1, source_target_pairs={{0,16},{4,20},{8,24},{12,28},{16,0},{20,4},{24,8},{28,12},{1,17},{... | collective-permute-start | bytes 196616 | tf_op jit(solution)/shard_map/ppermute | solution.py:414
  67.3 1.5 %collective-permute-start.20 = (bf16[8,32,128]{2,1,0:T(8,128)(2,1)S(1)}, bf16[8,32,128]{2,1,0:T(8,128)(2,1)S(1)}, u32[]{:S(2)}, u32[]{:S(2)}) collective-permute-start(bf16[8,32,128]{2,1,0:T(8,128)(2,1)S(1)} %get-tuple-element.151.refs_17_), channel_id=1, source_target_pairs={{0,24},{4,28},{8,16},{12,20},{16,8},{20,12},{24,0},{28,4},{1,25},{... | collective-permute-start | bytes 196616 | tf_op jit(solution)/shard_map/ppermute | solution.py:414
  68.8 1.8 %collective-permute-start.21 = (bf16[8,32,128]{2,1,0:T(8,128)(2,1)S(1)}, bf16[8,32,128]{2,1,0:T(8,128)(2,1)S(1)}, u32[]{:S(2)}, u32[]{:S(2)}) collective-permute-start(bf16[8,32,128]{2,1,0:T(8,128)(2,1)S(1)} %get-tuple-element.152.refs_16_), channel_id=1, source_target_pairs={{0,16},{4,20},{8,24},{12,28},{16,0},{20,4},{24,8},{28,12},{1,17},{... | collective-permute-start | bytes 196616 | tf_op jit(solution)/shard_map/ppermute | solution.py:414
  71.4 3.7 %collective-permute-start.30 = (bf16[8,32,128]{2,1,0:T(8,128)(2,1)S(1)}, bf16[8,32,128]{2,1,0:T(8,128)(2,1)S(1)}, u32[]{:S(2)}, u32[]{:S(2)}) collective-permute-start(bf16[8,32,128]{2,1,0:T(8,128)(2,1)S(1)} %get-tuple-element.164.refs_0_), channel_id=1, source_target_pairs={{0,3},{1,0},{2,1},{3,2},{4,7},{5,4},{6,5},{7,6},{8,11},{9,8},{10,9... | collective-permute-start | bytes 196616 | tf_op jit(solution)/shard_map/ppermute | solution.py:387
  76.1 3.7 %collective-permute-start.25 = (bf16[8,32,128]{2,1,0:T(8,128)(2,1)S(1)}, bf16[8,32,128]{2,1,0:T(8,128)(2,1)S(1)}, u32[]{:S(2)}, u32[]{:S(2)}) collective-permute-start(bf16[8,32,128]{2,1,0:T(8,128)(2,1)S(1)} %get-tuple-element.156.refs_1_), channel_id=1, source_target_pairs={{0,3},{1,0},{2,1},{3,2},{4,7},{5,4},{6,5},{7,6},{8,11},{9,8},{10,9... | collective-permute-start | bytes 196616 | tf_op jit(solution)/shard_map/ppermute | solution.py:387
  80.5 2.2 %stage0.5 = (f32[33,32,128]{2,1,0:T(8,128)S(1)}, f32[33,32,128]{2,1,0:T(8,128)S(1)}, f32[33,32,128]{2,1,0:T(8,128)S(1)}, f32[33,32,128]{2,1,0:T(8,128)S(1)}) custom-call(s32[2]{0:T(128)S(1)} %pad_add_fusion.position_ref, s32[16,200]{1,0:T(8,128)S(1)} %get-tuple-element.102.list_ref, s32[16]{0:T(128)S(1)} %get-tuple-element.103.total_ref, ...), custom_call_target="tpu_custom_call" | custom-call | flops 50331648 | bytes 1572864 | tf_op jit(solution)/shard_map/stage0/pallas_call | solution.py:339
  83.0 2.1 %stage1.5 = (f32[33,32,128]{2,1,0:T(8,128)S(1)}, f32[33,32,128]{2,1,0:T(8,128)S(1)}, f32[33,32,128]{2,1,0:T(8,128)S(1)}, f32[33,32,128]{2,1,0:T(8,128)S(1)}) custom-call(s32[16,200]{1,0:T(8,128)S(1)} %get-tuple-element.102.list_ref, s32[16]{0:T(128)S(1)} %get-tuple-element.103.total_ref, ...), custom_call_target="tpu_custom_call", output_to_operand_aliasing={{0}: (6, {}), {1}: (7, {}), {2}: (8, {}), {3}: (9, {})} | custom-call | flops 75497472 | bytes 2359296 | tf_op jit(solution)/shard_map/stage1/pallas_call | solution.py:352
  85.1 1.8 %stage2.5 = (f32[33,32,128]{2,1,0:T(8,128)S(1)}, f32[33,32,128]{2,1,0:T(8,128)S(1)}, f32[33,32,128]{2,1,0:T(8,128)S(1)}, f32[33,32,128]{2,1,0:T(8,128)S(1)}) custom-call(s32[16,200]{1,0:T(8,128)S(1)} %get-tuple-element.102.list_ref, s32[16]{0:T(128)S(1)} %get-tuple-element.103.total_ref, ...), custom_call_target="tpu_custom_call", output_to_operand_aliasing={{0}: (5, {}), {1}: (6, {}), {2}: (7, {}), {3}: (8, {})} | custom-call | flops 50331648 | bytes 1572864 | tf_op jit(solution)/shard_map/stage2/pallas_call | solution.py:352
  92.3 4.3 %collective-permute-start.37 = (bf16[8,32,128]{2,1,0:T(8,128)(2,1)S(1)}, bf16[8,32,128]{2,1,0:T(8,128)(2,1)S(1)}, u32[]{:S(2)}, u32[]{:S(2)}) collective-permute-start(bf16[8,32,128]{2,1,0:T(8,128)(2,1)S(1)} %get-tuple-element.188), channel_id=1, source_target_pairs={{0,16},{4,20},{8,24},{12,28},{16,0},{20,4},{24,8},{28,12},{1,17},{... | collective-permute-start | bytes 196616 | tf_op jit(solution)/shard_map/ppermute | solution.py:414
  97.2 1.5 %collective-permute-start.33 = (bf16[8,32,128]{2,1,0:T(8,128)(2,1)S(1)}, bf16[8,32,128]{2,1,0:T(8,128)(2,1)S(1)}, u32[]{:S(2)}, u32[]{:S(2)}) collective-permute-start(bf16[8,32,128]{2,1,0:T(8,128)(2,1)S(1)} %get-tuple-element.180), channel_id=1, source_target_pairs={{0,24},{4,28},{8,16},{12,20},{16,8},{20,12},{24,0},{28,4},{1,25},{... | collective-permute-start | bytes 196616 | tf_op jit(solution)/shard_map/ppermute | solution.py:414
  98.7 2.0 %collective-permute-start.34 = (bf16[8,32,128]{2,1,0:T(8,128)(2,1)S(1)}, bf16[8,32,128]{2,1,0:T(8,128)(2,1)S(1)}, u32[]{:S(2)}, u32[]{:S(2)}) collective-permute-start(bf16[8,32,128]{2,1,0:T(8,128)(2,1)S(1)} %get-tuple-element.181), channel_id=1, source_target_pairs={{0,16},{4,20},{8,24},{12,28},{16,0},{20,4},{24,8},{28,12},{1,17},{... | collective-permute-start | bytes 196616 | tf_op jit(solution)/shard_map/ppermute | solution.py:414
  103.4 1.6 %collective-permute-done.35.refs_2_ = bf16[8,32,128]{2,1,0:T(8,128)(2,1)S(1)} collective-permute-done((bf16[8,32,128]{2,1,0:T(8,128)(2,1)S(1)}, bf16[8,32,128]{2,1,0:T(8,128)(2,1)S(1)}, u32[]{:S(2)}, u32[]{:S(2)}) %collective-permute-start.35) | collective-permute-done | bytes 65568 | tf_op jit(solution)/shard_map/ppermute | solution.py:414
  (82 shorter events, 27.3 us)
Async XLA Ops:
  2.2 9.9 %collective-permute-start.3 = (bf16[8,32,128]{2,1,0:T(8,128)(2,1)S(1)}, bf16[8,32,128]{2,1,0:T(8,128)(2,1)S(1)}, u32[]{:S(2)}, u32[]{:S(2)}) collective-permute-start(bf16[8,32,128]{2,1,0:T(8,128)(2,1)S(1)} %get-tuple-element.106.refs_0_), channel_id=1, source_target_pairs={{0,1},{1,2},{2,3},{3,0},{4,5},{5,6},{6,7},{7,4},{8,9},{9,10},{10,1... | collective-permute-start | bytes 196616 | tf_op jit(solution)/shard_map/ppermute | solution.py:387
  5.3 16.0 %collective-permute-start.4 = (bf16[8,32,128]{2,1,0:T(8,128)(2,1)S(1)}, bf16[8,32,128]{2,1,0:T(8,128)(2,1)S(1)}, u32[]{:S(2)}, u32[]{:S(2)}) collective-permute-start(bf16[8,32,128]{2,1,0:T(8,128)(2,1)S(1)} %get-tuple-element.106.refs_0_), channel_id=1, source_target_pairs={{0,3},{1,0},{2,1},{3,2},{4,7},{5,4},{6,5},{7,6},{8,11},{9,8},{10,9... | collective-permute-start | bytes 196616 | tf_op jit(solution)/shard_map/ppermute | solution.py:387
  7.3 14.0 %collective-permute-start.5 = (bf16[8,32,128]{2,1,0:T(8,128)(2,1)S(1)}, bf16[8,32,128]{2,1,0:T(8,128)(2,1)S(1)}, u32[]{:S(2)}, u32[]{:S(2)}) collective-permute-start(bf16[8,32,128]{2,1,0:T(8,128)(2,1)S(1)} %get-tuple-element.106.refs_0_), channel_id=1, source_target_pairs={{0,2},{1,3},{2,0},{3,1},{4,6},{5,7},{6,4},{7,5},{8,10},{9,11},{10,... | collective-permute-start | bytes 196616 | tf_op jit(solution)/shard_map/ppermute | solution.py:387
  8.3 15.1 %collective-permute-start.1 = (bf16[8,32,128]{2,1,0:T(8,128)(2,1)S(1)}, bf16[8,32,128]{2,1,0:T(8,128)(2,1)S(1)}, u32[]{:S(2)}, u32[]{:S(2)}) collective-permute-start(bf16[8,32,128]{2,1,0:T(8,128)(2,1)S(1)} %get-tuple-element.105.refs_1_), channel_id=1, source_target_pairs={{0,1},{1,2},{2,3},{3,0},{4,5},{5,6},{6,7},{7,4},{8,9},{9,10},{10,1... | collective-permute-start | bytes 196616 | tf_op jit(solution)/shard_map/ppermute | solution.py:387
  9.9 13.6 %collective-permute-start.2 = (bf16[8,32,128]{2,1,0:T(8,128)(2,1)S(1)}, bf16[8,32,128]{2,1,0:T(8,128)(2,1)S(1)}, u32[]{:S(2)}, u32[]{:S(2)}) collective-permute-start(bf16[8,32,128]{2,1,0:T(8,128)(2,1)S(1)} %get-tuple-element.105.refs_1_), channel_id=1, source_target_pairs={{0,3},{1,0},{2,1},{3,2},{4,7},{5,4},{6,5},{7,6},{8,11},{9,8},{10,9... | collective-permute-start | bytes 196616 | tf_op jit(solution)/shard_map/ppermute | solution.py:387
  12.1 13.2 %collective-permute-start = (bf16[8,32,128]{2,1,0:T(8,128)(2,1)S(1)}, bf16[8,32,128]{2,1,0:T(8,128)(2,1)S(1)}, u32[]{:S(2)}, u32[]{:S(2)}) collective-permute-start(bf16[8,32,128]{2,1,0:T(8,128)(2,1)S(1)} %get-tuple-element.105.refs_1_), channel_id=1, source_target_pairs={{0,2},{1,3},{2,0},{3,1},{4,6},{5,7},{6,4},{7,5},{8,10},{9,11},{10,... | collective-permute-start | bytes 196616 | tf_op jit(solution)/shard_map/ppermute | solution.py:387
  29.3 11.0 %collective-permute-start.13 = (bf16[8,32,128]{2,1,0:T(8,128)(2,1)S(1)}, bf16[8,32,128]{2,1,0:T(8,128)(2,1)S(1)}, u32[]{:S(2)}, u32[]{:S(2)}) collective-permute-start(bf16[8,32,128]{2,1,0:T(8,128)(2,1)S(1)} %get-tuple-element.132.refs_6_.refs_8_), channel_id=1, source_target_pairs={{0,24},{4,28},{8,16},{12,20},{16,8},{20,12},{24,0},{28,4},{1,25},{... | collective-permute-start | bytes 196616 | tf_op jit(solution)/shard_map/ppermute | solution.py:414
  31.2 9.1 %collective-permute-start.14 = (bf16[8,32,128]{2,1,0:T(8,128)(2,1)S(1)}, bf16[8,32,128]{2,1,0:T(8,128)(2,1)S(1)}, u32[]{:S(2)}, u32[]{:S(2)}) collective-permute-start(bf16[8,32,128]{2,1,0:T(8,128)(2,1)S(1)} %get-tuple-element.133.refs_5_.refs_7_), channel_id=1, source_target_pairs={{0,16},{4,20},{8,24},{12,28},{16,0},{20,4},{24,8},{28,12},{1,17},{... | collective-permute-start | bytes 196616 | tf_op jit(solution)/shard_map/ppermute | solution.py:414
  36.1 4.9 %collective-permute-start.15 = (bf16[8,32,128]{2,1,0:T(8,128)(2,1)S(1)}, bf16[8,32,128]{2,1,0:T(8,128)(2,1)S(1)}, u32[]{:S(2)}, u32[]{:S(2)}) collective-permute-start(bf16[8,32,128]{2,1,0:T(8,128)(2,1)S(1)} %get-tuple-element.134.refs_4_.refs_6_), channel_id=1, source_target_pairs={{0,8},{4,12},{8,0},{12,4},{16,24},{20,28},{24,16},{28,20},{1,9},{5... | collective-permute-start | bytes 196616 | tf_op jit(solution)/shard_map/ppermute | solution.py:414
  36.7 8.5 %collective-permute-start.7 = (bf16[8,32,128]{2,1,0:T(8,128)(2,1)S(1)}, bf16[8,32,128]{2,1,0:T(8,128)(2,1)S(1)}, u32[]{:S(2)}, u32[]{:S(2)}) collective-permute-start(bf16[8,32,128]{2,1,0:T(8,128)(2,1)S(1)} %get-tuple-element.122.refs_9_.refs_11_), channel_id=1, source_target_pairs={{0,24},{4,28},{8,16},{12,20},{16,8},{20,12},{24,0},{28,4},{1,25},{... | collective-permute-start | bytes 196616 | tf_op jit(solution)/shard_map/ppermute | solution.py:414
  38.2 7.5 %collective-permute-start.8 = (bf16[8,32,128]{2,1,0:T(8,128)(2,1)S(1)}, bf16[8,32,128]{2,1,0:T(8,128)(2,1)S(1)}, u32[]{:S(2)}, u32[]{:S(2)}) collective-permute-start(bf16[8,32,128]{2,1,0:T(8,128)(2,1)S(1)} %get-tuple-element.123.refs_8_.refs_10_), channel_id=1, source_target_pairs={{0,16},{4,20},{8,24},{12,28},{16,0},{20,4},{24,8},{28,12},{1,17},{... | collective-permute-start | bytes 196616 | tf_op jit(solution)/shard_map/ppermute | solution.py:414
  40.3 5.5 %collective-permute-start.9 = (bf16[8,32,128]{2,1,0:T(8,128)(2,1)S(1)}, bf16[8,32,128]{2,1,0:T(8,128)(2,1)S(1)}, u32[]{:S(2)}, u32[]{:S(2)}) collective-permute-start(bf16[8,32,128]{2,1,0:T(8,128)(2,1)S(1)} %get-tuple-element.124.refs_7_.refs_9_), channel_id=1, source_target_pairs={{0,8},{4,12},{8,0},{12,4},{16,24},{20,28},{24,16},{28,20},{1,9},{5... | collective-permute-start | bytes 196616 | tf_op jit(solution)/shard_map/ppermute | solution.py:414
  41.4 8.6 %collective-permute-start.16 = (bf16[8,32,128]{2,1,0:T(8,128)(2,1)S(1)}, bf16[8,32,128]{2,1,0:T(8,128)(2,1)S(1)}, u32[]{:S(2)}, u32[]{:S(2)}) collective-permute-start(bf16[8,32,128]{2,1,0:T(8,128)(2,1)S(1)} %get-tuple-element.135.refs_0_), channel_id=1, source_target_pairs={{0,1},{1,2},{2,3},{3,0},{4,5},{5,6},{6,7},{7,4},{8,9},{9,10},{10,1... | collective-permute-start | bytes 196616 | tf_op jit(solution)/shard_map/ppermute | solution.py:387
  42.5 10.1 %collective-permute-start.17 = (bf16[8,32,128]{2,1,0:T(8,128)(2,1)S(1)}, bf16[8,32,128]{2,1,0:T(8,128)(2,1)S(1)}, u32[]{:S(2)}, u32[]{:S(2)}) collective-permute-start(bf16[8,32,128]{2,1,0:T(8,128)(2,1)S(1)} %get-tuple-element.135.refs_0_), channel_id=1, source_target_pairs={{0,3},{1,0},{2,1},{3,2},{4,7},{5,4},{6,5},{7,6},{8,11},{9,8},{10,9... | collective-permute-start | bytes 196616 | tf_op jit(solution)/shard_map/ppermute | solution.py:387
  45.2 7.9 %collective-permute-start.18 = (bf16[8,32,128]{2,1,0:T(8,128)(2,1)S(1)}, bf16[8,32,128]{2,1,0:T(8,128)(2,1)S(1)}, u32[]{:S(2)}, u32[]{:S(2)}) collective-permute-start(bf16[8,32,128]{2,1,0:T(8,128)(2,1)S(1)} %get-tuple-element.135.refs_0_), channel_id=1, source_target_pairs={{0,2},{1,3},{2,0},{3,1},{4,6},{5,7},{6,4},{7,5},{8,10},{9,11},{10,... | collective-permute-start | bytes 196616 | tf_op jit(solution)/shard_map/ppermute | solution.py:387
  46.2 9.1 %collective-permute-start.11 = (bf16[8,32,128]{2,1,0:T(8,128)(2,1)S(1)}, bf16[8,32,128]{2,1,0:T(8,128)(2,1)S(1)}, u32[]{:S(2)}, u32[]{:S(2)}) collective-permute-start(bf16[8,32,128]{2,1,0:T(8,128)(2,1)S(1)} %get-tuple-element.127.refs_1_), channel_id=1, source_target_pairs={{0,1},{1,2},{2,3},{3,0},{4,5},{5,6},{6,7},{7,4},{8,9},{9,10},{10,1... | collective-permute-start | bytes 196616 | tf_op jit(solution)/shard_map/ppermute | solution.py:387
  46.2 9.0 %collective-permute-start.12 = (bf16[8,32,128]{2,1,0:T(8,128)(2,1)S(1)}, bf16[8,32,128]{2,1,0:T(8,128)(2,1)S(1)}, u32[]{:S(2)}, u32[]{:S(2)}) collective-permute-start(bf16[8,32,128]{2,1,0:T(8,128)(2,1)S(1)} %get-tuple-element.127.refs_1_), channel_id=1, source_target_pairs={{0,3},{1,0},{2,1},{3,2},{4,7},{5,4},{6,5},{7,6},{8,11},{9,8},{10,9... | collective-permute-start | bytes 196616 | tf_op jit(solution)/shard_map/ppermute | solution.py:387
  50.0 7.1 %collective-permute-start.10 = (bf16[8,32,128]{2,1,0:T(8,128)(2,1)S(1)}, bf16[8,32,128]{2,1,0:T(8,128)(2,1)S(1)}, u32[]{:S(2)}, u32[]{:S(2)}) collective-permute-start(bf16[8,32,128]{2,1,0:T(8,128)(2,1)S(1)} %get-tuple-element.127.refs_1_), channel_id=1, source_target_pairs={{0,2},{1,3},{2,0},{3,1},{4,6},{5,7},{6,4},{7,5},{8,10},{9,11},{10,... | collective-permute-start | bytes 196616 | tf_op jit(solution)/shard_map/ppermute | solution.py:387
  61.1 9.5 %collective-permute-start.26 = (bf16[8,32,128]{2,1,0:T(8,128)(2,1)S(1)}, bf16[8,32,128]{2,1,0:T(8,128)(2,1)S(1)}, u32[]{:S(2)}, u32[]{:S(2)}) collective-permute-start(bf16[8,32,128]{2,1,0:T(8,128)(2,1)S(1)} %get-tuple-element.161.refs_14_), channel_id=1, source_target_pairs={{0,24},{4,28},{8,16},{12,20},{16,8},{20,12},{24,0},{28,4},{1,25},{... | collective-permute-start | bytes 196616 | tf_op jit(solution)/shard_map/ppermute | solution.py:414
  61.8 9.1 %collective-permute-start.27 = (bf16[8,32,128]{2,1,0:T(8,128)(2,1)S(1)}, bf16[8,32,128]{2,1,0:T(8,128)(2,1)S(1)}, u32[]{:S(2)}, u32[]{:S(2)}) collective-permute-start(bf16[8,32,128]{2,1,0:T(8,128)(2,1)S(1)} %get-tuple-element.162.refs_13_), channel_id=1, source_target_pairs={{0,16},{4,20},{8,24},{12,28},{16,0},{20,4},{24,8},{28,12},{1,17},{... | collective-permute-start | bytes 196616 | tf_op jit(solution)/shard_map/ppermute | solution.py:414
  67.3 7.8 %collective-permute-start.20 = (bf16[8,32,128]{2,1,0:T(8,128)(2,1)S(1)}, bf16[8,32,128]{2,1,0:T(8,128)(2,1)S(1)}, u32[]{:S(2)}, u32[]{:S(2)}) collective-permute-start(bf16[8,32,128]{2,1,0:T(8,128)(2,1)S(1)} %get-tuple-element.151.refs_17_), channel_id=1, source_target_pairs={{0,24},{4,28},{8,16},{12,20},{16,8},{20,12},{24,0},{28,4},{1,25},{... | collective-permute-start | bytes 196616 | tf_op jit(solution)/shard_map/ppermute | solution.py:414
  68.8 6.8 %collective-permute-start.21 = (bf16[8,32,128]{2,1,0:T(8,128)(2,1)S(1)}, bf16[8,32,128]{2,1,0:T(8,128)(2,1)S(1)}, u32[]{:S(2)}, u32[]{:S(2)}) collective-permute-start(bf16[8,32,128]{2,1,0:T(8,128)(2,1)S(1)} %get-tuple-element.152.refs_16_), channel_id=1, source_target_pairs={{0,16},{4,20},{8,24},{12,28},{16,0},{20,4},{24,8},{28,12},{1,17},{... | collective-permute-start | bytes 196616 | tf_op jit(solution)/shard_map/ppermute | solution.py:414
  70.6 5.0 %collective-permute-start.22 = (bf16[8,32,128]{2,1,0:T(8,128)(2,1)S(1)}, bf16[8,32,128]{2,1,0:T(8,128)(2,1)S(1)}, u32[]{:S(2)}, u32[]{:S(2)}) collective-permute-start(bf16[8,32,128]{2,1,0:T(8,128)(2,1)S(1)} %get-tuple-element.153.refs_15_), channel_id=1, source_target_pairs={{0,8},{4,12},{8,0},{12,4},{16,24},{20,28},{24,16},{28,20},{1,9},{5... | collective-permute-start | bytes 196616 | tf_op jit(solution)/shard_map/ppermute | solution.py:414
  71.3 8.6 %collective-permute-start.29 = (bf16[8,32,128]{2,1,0:T(8,128)(2,1)S(1)}, bf16[8,32,128]{2,1,0:T(8,128)(2,1)S(1)}, u32[]{:S(2)}, u32[]{:S(2)}) collective-permute-start(bf16[8,32,128]{2,1,0:T(8,128)(2,1)S(1)} %get-tuple-element.164.refs_0_), channel_id=1, source_target_pairs={{0,1},{1,2},{2,3},{3,0},{4,5},{5,6},{6,7},{7,4},{8,9},{9,10},{10,1... | collective-permute-start | bytes 196616 | tf_op jit(solution)/shard_map/ppermute | solution.py:387
  71.4 11.3 %collective-permute-start.30 = (bf16[8,32,128]{2,1,0:T(8,128)(2,1)S(1)}, bf16[8,32,128]{2,1,0:T(8,128)(2,1)S(1)}, u32[]{:S(2)}, u32[]{:S(2)}) collective-permute-start(bf16[8,32,128]{2,1,0:T(8,128)(2,1)S(1)} %get-tuple-element.164.refs_0_), channel_id=1, source_target_pairs={{0,3},{1,0},{2,1},{3,2},{4,7},{5,4},{6,5},{7,6},{8,11},{9,8},{10,9... | collective-permute-start | bytes 196616 | tf_op jit(solution)/shard_map/ppermute | solution.py:387
  75.1 7.9 %collective-permute-start.31 = (bf16[8,32,128]{2,1,0:T(8,128)(2,1)S(1)}, bf16[8,32,128]{2,1,0:T(8,128)(2,1)S(1)}, u32[]{:S(2)}, u32[]{:S(2)}) collective-permute-start(bf16[8,32,128]{2,1,0:T(8,128)(2,1)S(1)} %get-tuple-element.164.refs_0_), channel_id=1, source_target_pairs={{0,2},{1,3},{2,0},{3,1},{4,6},{5,7},{6,4},{7,5},{8,10},{9,11},{10,... | collective-permute-start | bytes 196616 | tf_op jit(solution)/shard_map/ppermute | solution.py:387
  76.0 9.1 %collective-permute-start.24 = (bf16[8,32,128]{2,1,0:T(8,128)(2,1)S(1)}, bf16[8,32,128]{2,1,0:T(8,128)(2,1)S(1)}, u32[]{:S(2)}, u32[]{:S(2)}) collective-permute-start(bf16[8,32,128]{2,1,0:T(8,128)(2,1)S(1)} %get-tuple-element.156.refs_1_), channel_id=1, source_target_pairs={{0,1},{1,2},{2,3},{3,0},{4,5},{5,6},{6,7},{7,4},{8,9},{9,10},{10,1... | collective-permute-start | bytes 196616 | tf_op jit(solution)/shard_map/ppermute | solution.py:387
  76.1 9.0 %collective-permute-start.25 = (bf16[8,32,128]{2,1,0:T(8,128)(2,1)S(1)}, bf16[8,32,128]{2,1,0:T(8,128)(2,1)S(1)}, u32[]{:S(2)}, u32[]{:S(2)}) collective-permute-start(bf16[8,32,128]{2,1,0:T(8,128)(2,1)S(1)} %get-tuple-element.156.refs_1_), channel_id=1, source_target_pairs={{0,3},{1,0},{2,1},{3,2},{4,7},{5,4},{6,5},{7,6},{8,11},{9,8},{10,9... | collective-permute-start | bytes 196616 | tf_op jit(solution)/shard_map/ppermute | solution.py:387
  79.9 7.1 %collective-permute-start.23 = (bf16[8,32,128]{2,1,0:T(8,128)(2,1)S(1)}, bf16[8,32,128]{2,1,0:T(8,128)(2,1)S(1)}, u32[]{:S(2)}, u32[]{:S(2)}) collective-permute-start(bf16[8,32,128]{2,1,0:T(8,128)(2,1)S(1)} %get-tuple-element.156.refs_1_), channel_id=1, source_target_pairs={{0,2},{1,3},{2,0},{3,1},{4,6},{5,7},{6,4},{7,5},{8,10},{9,11},{10,... | collective-permute-start | bytes 196616 | tf_op jit(solution)/shard_map/ppermute | solution.py:387
  91.0 9.8 %collective-permute-start.36 = (bf16[8,32,128]{2,1,0:T(8,128)(2,1)S(1)}, bf16[8,32,128]{2,1,0:T(8,128)(2,1)S(1)}, u32[]{:S(2)}, u32[]{:S(2)}) collective-permute-start(bf16[8,32,128]{2,1,0:T(8,128)(2,1)S(1)} %get-tuple-element.187), channel_id=1, source_target_pairs={{0,24},{4,28},{8,16},{12,20},{16,8},{20,12},{24,0},{28,4},{1,25},{... | collective-permute-start | bytes 196616 | tf_op jit(solution)/shard_map/ppermute | solution.py:414
  92.3 8.5 %collective-permute-start.37 = (bf16[8,32,128]{2,1,0:T(8,128)(2,1)S(1)}, bf16[8,32,128]{2,1,0:T(8,128)(2,1)S(1)}, u32[]{:S(2)}, u32[]{:S(2)}) collective-permute-start(bf16[8,32,128]{2,1,0:T(8,128)(2,1)S(1)} %get-tuple-element.188), channel_id=1, source_target_pairs={{0,16},{4,20},{8,24},{12,28},{16,0},{20,4},{24,8},{28,12},{1,17},{... | collective-permute-start | bytes 196616 | tf_op jit(solution)/shard_map/ppermute | solution.py:414
  97.2 5.8 %collective-permute-start.33 = (bf16[8,32,128]{2,1,0:T(8,128)(2,1)S(1)}, bf16[8,32,128]{2,1,0:T(8,128)(2,1)S(1)}, u32[]{:S(2)}, u32[]{:S(2)}) collective-permute-start(bf16[8,32,128]{2,1,0:T(8,128)(2,1)S(1)} %get-tuple-element.180), channel_id=1, source_target_pairs={{0,24},{4,28},{8,16},{12,20},{16,8},{20,12},{24,0},{28,4},{1,25},{... | collective-permute-start | bytes 196616 | tf_op jit(solution)/shard_map/ppermute | solution.py:414
  (10 other events, 25.8 us)

commit v3 on v0

v3 whole, which is shorter than its diff:
```python
import functools

import jax
import jax.numpy as jnp
from jax import lax
from jax.experimental import pallas as pl
from jax.experimental.pallas import tpu as pltpu
from jax.sharding import PartitionSpec as P

ITERS = 3
UNROLL = 16
LANES = 4
DEPTH = 6
CORES = 2
VMEM_LIMIT = 24 * 1024 * 1024

NT = (((1,), (1,)), ((), ()))


def in_vmem():
    return pl.BlockSpec(memory_space=pltpu.VMEM)


def in_hbm():
    return pl.BlockSpec(memory_space=pltpu.HBM)


def in_smem():
    return pl.BlockSpec(memory_space=pltpu.SMEM)


def stay_in_hbm(array):
    return pltpu.with_memory_space_constraint(array, pltpu.HBM)


def params():
    return pltpu.CompilerParams(vmem_limit_bytes=VMEM_LIMIT)


def split(value):
    high = value.astype(jnp.bfloat16)
    low = (value - high.astype(jnp.float32)).astype(jnp.bfloat16)
    return high, low


def times_block(field, high, low):
    field_high, field_low = split(field)
    rhs = field.shape[0]
    both = jnp.concatenate([field_high, field_low], axis=0)
    first = lax.dot_general(both, high, NT, preferred_element_type=jnp.float32)
    second = lax.dot_general(field_high, low, NT, preferred_element_type=jnp.float32)
    return first[:rhs] + (first[rhs:] + second)


def partner(chip, shift, chips):
    if chips & (chips - 1) == 0:
        return chip ^ shift
    return (chip + shift) % chips


def halves(value, size):
    if size & (size - 1) == 0:
        return lax.shift_right_logical(value, size.bit_length() - 1), value & (size - 1)
    return lax.div(value, size), lax.rem(value, size)


def relative(mine, source, groups):
    if groups % 2:
        away = mine - source
        return jnp.where(away < 0, away + groups, away)
    other = (mine ^ source) & 1
    away = (mine ^ other) - source
    away = jnp.where(away < 0, away + groups, away)
    return other * (groups // 2) + lax.shift_right_logical(away, 1)


def gather_stages(groups):
    if groups % 2:
        return [[0], list(range(1, groups))]
    pairs = groups // 2
    stages = [[0], [pairs], list(range(1, pairs)), list(range(pairs + 1, groups))]
    return [stage for stage in stages if stage]


def gather(rounded, groups):
    def ring(step):
        return [(c, (c + step) % groups) for c in range(groups)]

    if groups % 2:
        return [rounded] + [lax.ppermute(rounded, "col", ring(step)) for step in range(1, groups)]
    far = [lax.ppermute(rounded, "col", ring(2 * step)) for step in range(1, groups // 2)]
    return [rounded] + far + [lax.ppermute(rounded, "col", neighbours(groups))]


def neighbours(count):
    return [(index, index ^ 1) for index in range(count)]


def hold_kernel(piece_ref, token_ref, out_ref):
    pass


def start_kernel(precond_hbm, rhs_hbm, high_ref, low_ref, sol_ref, left_ref, rounded_ref, precond_ref, sems):
    owned = left_ref.shape[0]
    parts = sems.shape[0] - 1
    each = owned // parts
    loads = [pltpu.make_async_copy(rhs_hbm, left_ref, sems.at[parts])]
    for part in range(parts):
        at = pl.ds(part * each, each)
        loads.append(pltpu.make_async_copy(precond_hbm.at[at], precond_ref.at[at], sems.at[part]))
    for load in loads:
        load.start()
    loads[0].wait()
    for part in range(parts):
        loads[1 + part].wait()
        for p in range(part * each, (part + 1) * each):
            high, low = split(precond_ref[p])
            high_ref[p] = high
            low_ref[p] = low
            value = times_block(left_ref[p], high, low)
            sol_ref[p] = value
            rounded_ref[p] = value.astype(jnp.bfloat16)


def apply_kernel(pieces, high_ref, low_ref, left_ref, sol_ref, base_ref, *refs):
    piece_refs, (new_ref, new_left_ref, rounded_ref) = refs[:pieces], refs[pieces:]
    for p in range(sol_ref.shape[0]):
        received = sum(piece_ref[p].astype(jnp.float32) for piece_ref in piece_refs)
        value = sol_ref[p] + times_block(base_ref[p] - received, high_ref[p], low_ref[p])
        new_ref[p] = value
        new_left_ref[p] = left_ref[p] - received
        rounded_ref[p] = value.astype(jnp.bfloat16)


def finish_kernel(pieces, high_ref, low_ref, sol_ref, base_ref, *refs):
    piece_refs, (out_hbm, value_ref, sems) = refs[:pieces], refs[pieces:]
    owned = sol_ref.shape[0]
    parts = sems.shape[0]
    each = owned // parts
    stores = []
    for part in range(parts):
        for p in range(part * each, (part + 1) * each):
            received = sum(piece_ref[p].astype(jnp.float32) for piece_ref in piece_refs)
            value_ref[p] = sol_ref[p] + times_block(base_ref[p] - received, high_ref[p], low_ref[p])
        at = pl.ds(part * each, each)
        stores.append(pltpu.make_async_copy(value_ref.at[at], out_hbm.at[at], sems.at[part]))
        stores[-1].start()
    for store in stores:
        store.wait()


def order_kernel(group, owned, groups, stages, bits, position_ref, count_ref, rows_hbm, cols_hbm, values_hbm,
                 list_out, total_out, values_out, rows_ref, cols_ref, table_ref, total_ref, sems):
    loads = [
        pltpu.make_async_copy(rows_hbm, rows_ref, sems.at[0]),
        pltpu.make_async_copy(cols_hbm, cols_ref, sems.at[1]),
        pltpu.make_async_copy(values_hbm, values_out, sems.at[2]),
    ]
    for load in loads:
        load.start()
    core = position_ref[0] & (CORES - 1)
    mine = position_ref[1]
    used = count_ref[0, 0]
    row_bits, col_bits = bits
    lists = len(stages) * CORES
    trash = (group // CORES) << col_bits
    for index, stage in enumerate(stages):
        for place, piece in enumerate(stage):
            table_ref[piece] = ((index * CORES) << col_bits) + place * owned
    for index in range(lists + 1):
        total_ref[index] = 0
    loads[0].wait()
    loads[1].wait()

    def place(chunk, carry):
        entries = []
        for lane in range(LANES):
            slot = chunk * LANES + lane
            owner, row_inner = halves(halves(rows_ref[0, 0, slot], group)[1], owned)
            source, rest = halves(cols_ref[0, 0, slot], group)
            half = 1 - ((owner & (CORES - 1)) ^ core)
            first, base = halves(table_ref[relative(mine, source, groups)], 1 << col_bits)
            which = jnp.where(slot < used, first + half, lists)
            row = lax.shift_right_logical(owner, 1) * owned + row_inner
            col = base + halves(rest, owned)[1]
            entries.append((which, (((slot << row_bits) | row) << col_bits) | col))
        for which, entry in entries:
            at = total_ref[which]
            list_out[which, at] = entry
            total_ref[which] = at + 1
        return carry

    lax.fori_loop(0, lax.div(used + LANES - 1, LANES), place, 0)
    for index in range(lists):
        total_out[index] = total_ref[index]

    def close(index, carry):
        for extra in range(UNROLL):
            list_out[index, total_ref[index] + extra] = trash
        return carry

    lax.fori_loop(0, lists, close, 0)
    loads[2].wait()


def add_products(which, bits, list_ref, total_ref, values_ref, field_ref, total):
    row_bits, col_bits = bits

    def step(chunk, carry):
        terms = []

        def store(row, term):
            total[row] += term

        for lane in range(UNROLL):
            entry = list_ref[which, chunk * UNROLL + lane]
            col = entry & ((1 << col_bits) - 1)
            row = lax.shift_right_logical(entry, col_bits) & ((1 << row_bits) - 1)
            slot = lax.shift_right_logical(entry, col_bits + row_bits)
            term = lax.dot_general(
                field_ref[col], values_ref[slot], NT, preferred_element_type=jnp.float32)
            terms.append((row, term))
            if len(terms) > DEPTH:
                store(*terms.pop(0))
        for row, term in terms:
            store(row, term)
        return carry

    lax.fori_loop(0, lax.div(total_ref[which] + UNROLL - 1, UNROLL), step, 0)


def join(pieces, field):
    each = pieces[0].shape[0]
    for index, piece in enumerate(pieces):
        field[pl.ds(index * each, each)] = piece[...]


def first_kernel(steps, chips, bits, position_ref, list_ref, total_ref, values_ref, field_ref, *refs):
    out_refs, refs = refs[:steps], refs[steps:]
    in_refs, refs = refs[:steps], refs[steps:]
    sent_refs, totals, token_ref = refs[:-CORES - 1], refs[-CORES - 1:-1], refs[-1]
    token_ref[...] = jnp.zeros_like(token_ref)
    chip = lax.shift_right_logical(position_ref[0], 1)
    for half, total in enumerate(totals):
        rows = total.shape[0] - 1
        owned = rows // chips
        if steps == 0:
            total[...] = jnp.zeros(total.shape, jnp.float32)
        elif half == 0:
            total[pl.ds(0, rows)] = -sum(out_ref[...].astype(jnp.float32) for out_ref in out_refs)
        else:
            for shift in range(chips):
                at = pl.ds(partner(chip, shift, chips) * owned, owned)
                value = sum(in_ref[at].astype(jnp.float32) for in_ref in in_refs)
                if shift > 0:
                    for step in range(steps):
                        value -= sent_refs[step * (chips - 1) + shift - 1][...].astype(jnp.float32)
                total[at] = value
        add_products(half, bits, list_ref, total_ref, values_ref, field_ref, total)


def stage_kernel(stage, bits, pieces, list_ref, total_ref, values_ref, *refs):
    piece_refs, refs = refs[:pieces], refs[pieces + CORES:]
    totals, field = refs[:CORES], refs[-1]
    join(piece_refs, field)
    for half, total in enumerate(totals):
        add_products(stage * CORES + half, bits, list_ref, total_ref, values_ref, field, total)


def last_kernel(stage, half, bits, pieces, list_ref, total_ref, values_ref, *refs):
    piece_refs, refs = refs[:pieces], refs[pieces + 1:]
    total, outs, field = refs[0], refs[1:-1], refs[-1]
    join(piece_refs, field)
    add_products(stage * CORES + half, bits, list_ref, total_ref, values_ref, field, total)
    for out_ref in outs:
        out_ref[...] = total[pl.ds(0, out_ref.shape[0])].astype(out_ref.dtype)


def chip_rows(shift, chips, position_ref, own_ref, other_ref, owned):
    chip = lax.shift_right_logical(position_ref[0], 1)
    at = pl.ds(partner(chip, shift, chips) * owned, owned)
    return own_ref[at] + other_ref[at].astype(jnp.float32)


def combine_kernel(shift, chips, position_ref, own_ref, other_ref, send_ref):
    send_ref[...] = chip_rows(
        shift, chips, position_ref, own_ref, other_ref, send_ref.shape[0]).astype(send_ref.dtype)


def keep_kernel(chips, position_ref, own_ref, other_ref, left_ref, sol_ref, base_ref):
    keep = chip_rows(0, chips, position_ref, own_ref, other_ref, base_ref.shape[0])
    base_ref[...] = left_ref[...] - sol_ref[...] - keep


def per_device(block_values, block_rows, block_cols, block_counts, precond, right_side):
    owned, rhs, size = right_side.shape[1:]
    row_devices = lax.axis_size("row")
    groups = lax.axis_size("col")
    chips = row_devices // CORES
    group = owned * row_devices
    half_rows = chips * owned
    slots = block_values.shape[2]
    position = jnp.stack([lax.axis_index("row"), lax.axis_index("col")]).astype(jnp.int32)

    stages = gather_stages(groups)
    final = len(stages) - 1
    lists_total = len(stages) * CORES
    widest = max(len(stage) for stage in stages) * owned
    row_bits, col_bits = bits = half_rows.bit_length(), (widest - 1).bit_length()
    assert (slots - 1).bit_length() + row_bits + col_bits <= 31
    assert slots % LANES == 0

    field_type = jax.ShapeDtypeStruct((owned, rhs, size), jnp.float32)
    rounded_type = jax.ShapeDtypeStruct((owned, rhs, size), jnp.bfloat16)
    matrix_type = jax.ShapeDtypeStruct((owned, size, size), jnp.bfloat16)
    total_type = jax.ShapeDtypeStruct((half_rows + 1, rhs, size), jnp.float32)
    index_type = pltpu.SMEM(block_rows.shape, jnp.int32)
    token_type = jax.ShapeDtypeStruct((8, 128), jnp.float32)
    parts = next(count for count in (4, 2, 1) if owned % count == 0)

    high, low, sol, left, rounded = pl.pallas_call(
        start_kernel,
        out_shape=[matrix_type] * 2 + [field_type] * 2 + [rounded_type],
        in_specs=[in_hbm()] * 2,
        out_specs=[in_vmem()] * 5,
        scratch_shapes=[
            pltpu.VMEM((owned, size, size), jnp.float32),
            pltpu.SemaphoreType.DMA((parts + 1,)),
        ],
        compiler_params=params(),
        name="start",
    )(stay_in_hbm(precond[0]), stay_in_hbm(right_side[0]))

    *lists, values = pl.pallas_call(
        functools.partial(order_kernel, group, owned, groups, stages, bits),
        out_shape=[
            jax.ShapeDtypeStruct((lists_total + 1, slots + UNROLL), jnp.int32),
            jax.ShapeDtypeStruct((lists_total,), jnp.int32),
            pltpu.VMEM(block_values.shape[2:], block_values.dtype),
        ],
        in_specs=[in_smem()] * 2 + [in_hbm()] * 3,
        out_specs=[in_smem()] * 2 + [in_vmem()],
        scratch_shapes=[
            index_type, index_type,
            pltpu.SMEM((groups,), jnp.int32), pltpu.SMEM((lists_total + 1,), jnp.int32),
            pltpu.SemaphoreType.DMA((3,)),
        ],
        compiler_params=params(),
        name="order",
    )(position, block_counts, *[stay_in_hbm(array) for array in (block_rows, block_cols, block_values[0, 0])])

    def cost(share):
        return pl.CostEstimate(
            flops=int(slots * share) * 2 * rhs * size * size,
            bytes_accessed=int(slots * share) * 2 * size * size, transcendentals=0)

    def field_scratch(pieces):
        return pltpu.VMEM((len(pieces) * owned, rhs, size), jnp.bfloat16)

    def product_first(field, outs, ins, sent):
        return pl.pallas_call(
            functools.partial(first_kernel, len(outs), chips, bits),
            out_shape=[total_type] * CORES + [token_type],
            in_specs=[in_smem()] * 3 + [in_vmem()] * (2 + len(outs) + len(ins) + len(sent)),
            out_specs=[in_vmem()] * (CORES + 1),
            compiler_params=params(),
            cost_estimate=cost(1 / groups),
            name="stage0",
        )(position, *lists, values, field, *outs, *ins, *sent)

    def product_stage(stage, pieces, totals):
        inputs = 3 + len(pieces)
        return pl.pallas_call(
            functools.partial(stage_kernel, stage, bits, len(pieces)),
            out_shape=[total_type] * CORES,
            in_specs=[in_smem()] * 2 + [in_vmem()] * (1 + len(pieces) + CORES),
            out_specs=[in_vmem()] * CORES,
            scratch_shapes=[field_scratch(pieces)],
            input_output_aliases={inputs + half: half for half in range(CORES)},
            compiler_params=params(),
            cost_estimate=cost(len(pieces) / groups),
            name="stage%d" % stage,
        )(*lists, values, *pieces, *totals)

    def product_last(half, pieces, total):
        send = [jax.ShapeDtypeStruct((half_rows, rhs, size), jnp.bfloat16)] if half == 0 else []
        return pl.pallas_call(
            functools.partial(last_kernel, final, half, bits, len(pieces)),
            out_shape=[total_type] + send,
            in_specs=[in_smem()] * 2 + [in_vmem()] * (2 + len(pieces)),
            out_specs=[in_vmem()] * (1 + len(send)),
            scratch_shapes=[field_scratch(pieces)],
            input_output_aliases={3 + len(pieces): 0},
            compiler_params=params(),
            cost_estimate=cost(len(pieces) / groups / CORES),
            name="last%d" % half,
        )(*lists, values, *pieces, total)[-1]

    def hold(piece, token):
        return pl.pallas_call(
            hold_kernel,
            out_shape=rounded_type,
            in_specs=[in_vmem()] * 2,
            out_specs=in_vmem(),
            input_output_aliases={0: 0},
            compiler_params=params(),
            name="hold",
        )(piece, token)

    outs, ins, sent = [], [], []
    for step in range(ITERS):
        fields = gather(rounded, groups)
        *totals, token = product_first(rounded, outs, ins, sent)
        if groups % 2 == 0:
            for index in range(1, groups // 2):
                fields[index] = hold(fields[index], token)
                fields.append(lax.ppermute(fields[index], "col", neighbours(groups)))
        for stage in range(1, final):
            totals = product_stage(stage, [fields[piece] for piece in stages[stage]], totals)
        tail = [fields[piece] for piece in stages[final]]
        outgoing = product_last(0, tail, totals[0])
        incoming = lax.ppermute(outgoing, "row", neighbours(row_devices))
        own = product_last(1, tail, totals[1])
        outs.append(outgoing)
        ins.append(incoming)
        sends = {}
        pieces = []
        for shift in range(1, chips):
            pairs = [
                (chip * CORES + core, partner(chip, shift, chips) * CORES + core)
                for chip in range(chips) for core in range(CORES)
            ]
            sends[shift] = pl.pallas_call(
                functools.partial(combine_kernel, shift, chips),
                out_shape=rounded_type,
                in_specs=[in_smem()] + [in_vmem()] * 2,
                out_specs=in_vmem(),
                compiler_params=params(),
                name="combine%d" % shift,
            )(position, own, incoming)
            pieces.append(lax.ppermute(sends[shift], "row", pairs))
        sent += [sends[shift] for shift in range(1, chips)]
        base = pl.pallas_call(
            functools.partial(keep_kernel, chips),
            out_shape=field_type,
            in_specs=[in_smem()] + [in_vmem()] * 4,
            out_specs=in_vmem(),
            compiler_params=params(),
            name="keep",
        )(position, own, incoming, left, sol)
        if step < ITERS - 1:
            sol, left, rounded = pl.pallas_call(
                functools.partial(apply_kernel, len(pieces)),
                out_shape=[field_type, field_type, rounded_type],
                in_specs=[in_vmem()] * (5 + len(pieces)),
                out_specs=[in_vmem()] * 3,
                compiler_params=params(),
                name="apply",
            )(high, low, left, sol, base, *pieces)
    return pl.pallas_call(
        functools.partial(finish_kernel, len(pieces)),
        out_shape=field_type,
        in_specs=[in_vmem()] * (4 + len(pieces)),
        out_specs=in_hbm(),
        scratch_shapes=[
            pltpu.VMEM((owned, rhs, size), jnp.float32),
            pltpu.SemaphoreType.DMA((2 if owned % 2 == 0 else 1,)),
        ],
        compiler_params=params(),
        name="finish",
    )(high, low, sol, base, *pieces)[None]


def solution(mesh):
    placed = (
        P("row", "col", None, None, None),
        P("row", "col", None),
        P("row", "col", None),
        P("row", "col"),
        P("col", "row", None, None),
        P("col", "row", None, None),
    )
    return jax.shard_map(
        per_device,
        mesh=mesh,
        in_specs=placed,
        out_specs=P("col", "row", None, None),
        check_vma=False,
    )
```

time: 290 us -> 92.5 us (0.32)
  waiting for transfers between devices: 127 us -> 27.6 us
  other arithmetic: 52.6 us -> 0.07 us
  blocking collectives: 48.8 us -> 0 us
  Pallas kernels: 0 us -> 39.9 us
  matrix products: 37.6 us -> 0 us
  starting transfers between devices: 0.09 us -> 23.8 us
  between operations: 13.9 us -> 0.81 us
  local copies, waits for them, and re-layouts: 7.91 us -> 0 us
    reduce_scatter x3 -> x0, waiting for transfers between devices: 127 us -> none  [per_device(): lax.psum_scatter(partial_value, 'row', scatter_dimension=0, tiled=True)]
    scatter-add x3 -> x0, other arithmetic: 51.8 us -> none  [per_device(): partial_value = jax.ops.segment_sum(terms, row_local, num_segments=group)]
    all_gather x3 -> x0, blocking collectives: 48.8 us -> none  [per_device(): lax.all_gather(solution.astype(jnp.bfloat16)[None], 'col', axis=1, tiled=...]
    pallas_call x0 -> x35, Pallas kernels: none -> 39.9 us  [the longest x6 9.66 us: product_stage(): pl.pallas_call(functools.partial(stage_kernel, stage, bits, len(pieces)),...]
    dot_general x7 -> x0, matrix products: 37.6 us -> none  [the longest x3 23.5 us: block_terms(): jnp.einsum('ski,soi->sko', gathered, values, preferred_element_type=jnp.f...]
    ppermute x0 -> x21, waiting for transfers between devices: none -> 27.6 us  [the longest x9 13.5 us: per_device(): pieces.append(lax.ppermute(sends[shift], 'row', pairs))]
    ppermute x0 -> x21, starting transfers between devices: none -> 23.8 us  [the longest x9 12.5 us: per_device(): pieces.append(lax.ppermute(sends[shift], 'row', pairs))]
    unnamed x12 -> x0, local copies, waits for them, and re-layouts: 4.48 us -> none
  transfers between devices with their start and end apart: 3 -> 21, of which waited for: 3 -> 17; matrix products, arithmetic and copies ran while one was open for 0% -> 0% of each run, Pallas kernels for 0% -> 32%
where the time goes in v3:
time: 92.5 us; the launch traced here: 92.2 us
  Pallas kernels  39.9 us (43%)
  waiting for transfers between devices  27.6 us (30%)
  starting transfers between devices  23.8 us (26%)
    ppermute x9, waiting for transfers between devices, per_device(): pieces.append(lax.ppermute(sends[shift], 'row', pairs))  13.5 us
    ppermute x9, starting transfers between devices, per_device(): pieces.append(lax.ppermute(sends[shift], 'row', pairs))  12.5 us
    pallas_call x6, Pallas kernels, product_stage(): pl.pallas_call(functools.partial(stage_kernel, stage, bits, len(pieces)),...  9.66 us
    ppermute x3, waiting for transfers between devices, gather(): lax.ppermute(rounded, 'col', ring(2 * step))  8.03 us
    pallas_call x6, Pallas kernels, product_last(): pl.pallas_call(functools.partial(last_kernel, final, half, bits, len(piec...  7.41 us
    pallas_call x3, Pallas kernels, product_first(): pl.pallas_call(functools.partial(first_kernel, len(outs), chips, bits), o...  6.68 us
    ppermute x3, starting transfers between devices, gather(): lax.ppermute(rounded, 'col', ring(2 * step))  6.41 us
    pallas_call x9, Pallas kernels, per_device(): pl.pallas_call(functools.partial(combine_kernel, shift, chips), out_shape...  5.16 us
  transfers between devices with their start and end apart: 21, of which 17 were waited for; matrix products, arithmetic and copies ran while one was open for 0% of the time, Pallas kernels for 32%

profile of v3, /device:TPU:0, one launch (start us, length us, event | category | flops | bytes accessed | tf_op | source)
XLA Modules:
  0.0 92.2 jit_solution(16868820923947941178)
XLA Ops:
  0.0 2.1 %start.1 = (bf16[16,128,128]{2,1,0:T(8,128)(2,1)S(1)}, bf16[16,128,128]{2,1,0:T(8,128)(2,1)S(1)}, f32[16,32,128]{2,1,0:T(8,128)S(1)}, f32[16,32,128]{2,1,0:T(8,128)S(1)}, bf16[16,32,128]{2,1,0:T(8,128)(2,1)S(1)}) custom-call(f32[16,128,128]{2,1,0:T(8,128)} %bitcast.7, f32[16,32,128]{2,1,0:T(8,128)} %bitcast.8), custom_call_target="tpu_custom_call" | custom-call | tf_op jit(solution)/shard_map/start/pallas_call | solution.py:321
  2.2 4.1 %collective-permute-start = (bf16[16,32,128]{2,1,0:T(8,128)(2,1)S(1)}, bf16[16,32,128]{2,1,0:T(8,128)(2,1)S(1)}, u32[]{:S(2)}, u32[]{:S(2)}) collective-permute-start(bf16[16,32,128]{2,1,0:T(8,128)(2,1)S(1)} %get-tuple-element.50.field_ref), channel_id=1, source_target_pairs={{0,2},{1,3},{2,0},{3,1},{4,6},{5,7},{6,4},{7,5},{8,10},{9,11},{10,... | collective-permute-start | bytes 393224 | tf_op jit(solution)/shard_map/ppermute | solution.py:91
  6.3 1.6 %collective-permute-start.2 = (bf16[16,32,128]{2,1,0:T(8,128)(2,1)S(1)}, bf16[16,32,128]{2,1,0:T(8,128)(2,1)S(1)}, u32[]{:S(2)}, u32[]{:S(2)}) collective-permute-start(bf16[16,32,128]{2,1,0:T(8,128)(2,1)S(1)} %get-tuple-element.50.field_ref), channel_id=1, source_target_pairs={{0,1},{1,0},{2,3},{3,2},{4,5},{5,4},{6,7},{7,6},{8,9},{9,8},{10,11... | collective-permute-start | bytes 393224 | tf_op jit(solution)/shard_map/ppermute | solution.py:92
  8.6 4.2 %order.1 = (s32[9,208]{1,0:T(8,128)S(1)}, s32[8]{0:T(128)S(1)}, bf16[192,128,128]{2,1,0:T(8,128)(2,1)S(1)}) custom-call(s32[2]{0:T(128)S(1)} %pad_add_fusion.position_ref, s32[1,1]{1,0:T(1,128)S(6)} %copy.49.count_ref, s32[1,1,192]{2,1,0:T(1,128)} %rows_hbm.1, s32[1,1,192]{2,1,0:T(1,128)} %cols_hbm.1, bf16[192,128,128]{2,1,0:T(8,128)(2,1)} %bitcast.6), custom_call_target="tpu_custom_call" | custom-call | tf_op jit(solution)/shard_map/order/pallas_call | solution.py:334
  12.8 2.2 %stage0.3 = (f32[65,32,128]{2,1,0:T(8,128)S(1)}, f32[65,32,128]{2,1,0:T(8,128)S(1)}, f32[8,128]{1,0:T(8,128)S(1)}) custom-call(s32[2]{0:T(128)S(1)} %pad_add_fusion.position_ref, s32[9,208]{1,0:T(8,128)S(1)} %get-tuple-element.47.list_ref, s32[8]{0:T(128)S(1)} %get-tuple-element.48.total_ref, bf16[192,128,128]{2,1,0:T(8,128)(2,1)S(1)} %get-tuple-element.49.values_ref, ...), custom_call_target="tpu_custom_call" | custom-call | flops 50331648 | bytes 1572864 | tf_op jit(solution)/shard_map/stage0/pallas_call | solution.py:361
  15.9 1.6 %stage1.3 = (f32[65,32,128]{2,1,0:T(8,128)S(1)}, f32[65,32,128]{2,1,0:T(8,128)S(1)}) custom-call(s32[9,208]{1,0:T(8,128)S(1)} %get-tuple-element.47.list_ref, s32[8]{0:T(128)S(1)} %get-tuple-element.48.total_ref, bf16[192,128,128]{2,1,0:T(8,128)(2,1)S(1)} %get-tuple-element.49.values_ref, ...), custom_call_target="tpu_custom_call", output_to_operand_aliasing={{0}: (4, {}), {1}: (5, {})} | custom-call | flops 50331648 | bytes 1572864 | tf_op jit(solution)/shard_map/stage1/pallas_call | solution.py:373
  17.5 1.6 %stage2.3 = (f32[65,32,128]{2,1,0:T(8,128)S(1)}, f32[65,32,128]{2,1,0:T(8,128)S(1)}) custom-call(s32[9,208]{1,0:T(8,128)S(1)} %get-tuple-element.47.list_ref, s32[8]{0:T(128)S(1)} %get-tuple-element.48.total_ref, bf16[192,128,128]{2,1,0:T(8,128)(2,1)S(1)} %get-tuple-element.49.values_ref, ...), custom_call_target="tpu_custom_call", output_to_operand_aliasing={{0}: (4, {}), {1}: (5, {})} | custom-call | flops 50331648 | bytes 1572864 | tf_op jit(solution)/shard_map/stage2/pallas_call | solution.py:373
  20.0 1.3 %last0.3 = (f32[65,32,128]{2,1,0:T(8,128)S(1)}, bf16[64,32,128]{2,1,0:T(8,128)(2,1)S(1)}) custom-call(s32[9,208]{1,0:T(8,128)S(1)} %get-tuple-element.47.list_ref, s32[8]{0:T(128)S(1)} %get-tuple-element.48.total_ref, bf16[192,128,128]{2,1,0:T(8,128)(2,1)S(1)} %get-tuple-element.49.values_ref, ...), custom_call_target="tpu_custom_call", output_to_operand_aliasing={{0}: (4, {})} | custom-call | flops 25165824 | bytes 786432 | tf_op jit(solution)/shard_map/last0/pallas_call | solution.py:387
  21.3 1.2 %last1.3.own_ref = f32[65,32,128]{2,1,0:T(8,128)S(1)} custom-call(s32[9,208]{1,0:T(8,128)S(1)} %get-tuple-element.47.list_ref, s32[8]{0:T(128)S(1)} %get-tuple-element.48.total_ref, bf16[192,128,128]{2,1,0:T(8,128)(2,1)S(1)} %get-tuple-element.49.values_ref, bf16[16,32,128]{2,1,0:T(8,128)(2,1)S(1)} %collective-permute-done.1.refs_0_, ...), custom_call_target="tpu_custom_call", output_to_operand_aliasing={{}: (4, {})} | custom-call | flops 25165824 | bytes 786432 | tf_op jit(solution)/shard_map/last1/pallas_call | solution.py:387
  23.8 4.0 %collective-permute-start.6 = (bf16[16,32,128]{2,1,0:T(8,128)(2,1)S(1)}, bf16[16,32,128]{2,1,0:T(8,128)(2,1)S(1)}, u32[]{:S(2)}, u32[]{:S(2)}) collective-permute-start(bf16[16,32,128]{2,1,0:T(8,128)(2,1)S(1)} %combine3.3.refs_4_.refs_6_), channel_id=1, source_target_pairs={{0,24},{4,28},{8,16},{12,20},{16,8},{20,12},{24,0},{28,4},{1,25},{... | collective-permute-start | bytes 393224 | tf_op jit(solution)/shard_map/ppermute | solution.py:441
  30.3 1.4 %collective-permute-done.6.refs_2_ = bf16[16,32,128]{2,1,0:T(8,128)(2,1)S(1)} collective-permute-done((bf16[16,32,128]{2,1,0:T(8,128)(2,1)S(1)}, bf16[16,32,128]{2,1,0:T(8,128)(2,1)S(1)}, u32[]{:S(2)}, u32[]{:S(2)}) %collective-permute-start.6) | collective-permute-done | bytes 131104 | tf_op jit(solution)/shard_map/ppermute | solution.py:441
  31.7 2.7 %collective-permute-done.5.refs_1_ = bf16[16,32,128]{2,1,0:T(8,128)(2,1)S(1)} collective-permute-done((bf16[16,32,128]{2,1,0:T(8,128)(2,1)S(1)}, bf16[16,32,128]{2,1,0:T(8,128)(2,1)S(1)}, u32[]{:S(2)}, u32[]{:S(2)}) %collective-permute-start.5) | collective-permute-done | bytes 131104 | tf_op jit(solution)/shard_map/ppermute | solution.py:441
  37.2 2.2 %stage0.4 = (f32[65,32,128]{2,1,0:T(8,128)S(1)}, f32[65,32,128]{2,1,0:T(8,128)S(1)}, f32[8,128]{1,0:T(8,128)S(1)}) custom-call(s32[2]{0:T(128)S(1)} %pad_add_fusion.position_ref, s32[9,208]{1,0:T(8,128)S(1)} %get-tuple-element.47.list_ref, s32[8]{0:T(128)S(1)} %get-tuple-element.48.total_ref, bf16[192,128,128]{2,1,0:T(8,128)(2,1)S(1)} %get-tuple-element.49.values_ref, ...), custom_call_target="tpu_custom_call" | custom-call | flops 50331648 | bytes 1572864 | tf_op jit(solution)/shard_map/stage0/pallas_call | solution.py:361
  39.4 4.6 %collective-permute-done.7.piece_ref = bf16[16,32,128]{2,1,0:T(8,128)(2,1)S(1)} collective-permute-done((bf16[16,32,128]{2,1,0:T(8,128)(2,1)S(1)}, bf16[16,32,128]{2,1,0:T(8,128)(2,1)S(1)}, u32[]{:S(2)}, u32[]{:S(2)}) %collective-permute-start.7) | collective-permute-done | bytes 131104 | tf_op jit(solution)/shard_map/ppermute | solution.py:91
  43.9 1.6 %stage1.4 = (f32[65,32,128]{2,1,0:T(8,128)S(1)}, f32[65,32,128]{2,1,0:T(8,128)S(1)}) custom-call(s32[9,208]{1,0:T(8,128)S(1)} %get-tuple-element.47.list_ref, s32[8]{0:T(128)S(1)} %get-tuple-element.48.total_ref, bf16[192,128,128]{2,1,0:T(8,128)(2,1)S(1)} %get-tuple-element.49.values_ref, ...), custom_call_target="tpu_custom_call", output_to_operand_aliasing={{0}: (4, {}), {1}: (5, {})} | custom-call | flops 50331648 | bytes 1572864 | tf_op jit(solution)/shard_map/stage1/pallas_call | solution.py:373
  45.5 1.6 %stage2.4 = (f32[65,32,128]{2,1,0:T(8,128)S(1)}, f32[65,32,128]{2,1,0:T(8,128)S(1)}) custom-call(s32[9,208]{1,0:T(8,128)S(1)} %get-tuple-element.47.list_ref, s32[8]{0:T(128)S(1)} %get-tuple-element.48.total_ref, bf16[192,128,128]{2,1,0:T(8,128)(2,1)S(1)} %get-tuple-element.49.values_ref, ...), custom_call_target="tpu_custom_call", output_to_operand_aliasing={{0}: (4, {}), {1}: (5, {})} | custom-call | flops 50331648 | bytes 1572864 | tf_op jit(solution)/shard_map/stage2/pallas_call | solution.py:373
  47.2 1.7 %collective-permute-done.8.refs_0_ = bf16[16,32,128]{2,1,0:T(8,128)(2,1)S(1)} collective-permute-done((bf16[16,32,128]{2,1,0:T(8,128)(2,1)S(1)}, bf16[16,32,128]{2,1,0:T(8,128)(2,1)S(1)}, u32[]{:S(2)}, u32[]{:S(2)}) %collective-permute-start.8) | collective-permute-done | bytes 131104 | tf_op jit(solution)/shard_map/ppermute | solution.py:417
  48.9 1.3 %last0.4 = (f32[65,32,128]{2,1,0:T(8,128)S(1)}, bf16[64,32,128]{2,1,0:T(8,128)(2,1)S(1)}) custom-call(s32[9,208]{1,0:T(8,128)S(1)} %get-tuple-element.47.list_ref, s32[8]{0:T(128)S(1)} %get-tuple-element.48.total_ref, bf16[192,128,128]{2,1,0:T(8,128)(2,1)S(1)} %get-tuple-element.49.values_ref, ...), custom_call_target="tpu_custom_call", output_to_operand_aliasing={{0}: (4, {})} | custom-call | flops 25165824 | bytes 786432 | tf_op jit(solution)/shard_map/last0/pallas_call | solution.py:387
  50.2 1.2 %last1.4.own_ref = f32[65,32,128]{2,1,0:T(8,128)S(1)} custom-call(s32[9,208]{1,0:T(8,128)S(1)} %get-tuple-element.47.list_ref, s32[8]{0:T(128)S(1)} %get-tuple-element.48.total_ref, bf16[192,128,128]{2,1,0:T(8,128)(2,1)S(1)} %get-tuple-element.49.values_ref, bf16[16,32,128]{2,1,0:T(8,128)(2,1)S(1)} %collective-permute-done.8.refs_0_, ...), custom_call_target="tpu_custom_call", output_to_operand_aliasing={{}: (4, {})} | custom-call | flops 25165824 | bytes 786432 | tf_op jit(solution)/shard_map/last1/pallas_call | solution.py:387
  52.7 2.8 %collective-permute-start.13 = (bf16[16,32,128]{2,1,0:T(8,128)(2,1)S(1)}, bf16[16,32,128]{2,1,0:T(8,128)(2,1)S(1)}, u32[]{:S(2)}, u32[]{:S(2)}) collective-permute-start(bf16[16,32,128]{2,1,0:T(8,128)(2,1)S(1)} %combine3.4.refs_9_), channel_id=1, source_target_pairs={{0,24},{4,28},{8,16},{12,20},{16,8},{20,12},{24,0},{28,4},{1,25},{... | collective-permute-start | bytes 393224 | tf_op jit(solution)/shard_map/ppermute | solution.py:441
  59.4 2.7 %collective-permute-done.12.refs_1_ = bf16[16,32,128]{2,1,0:T(8,128)(2,1)S(1)} collective-permute-done((bf16[16,32,128]{2,1,0:T(8,128)(2,1)S(1)}, bf16[16,32,128]{2,1,0:T(8,128)(2,1)S(1)}, u32[]{:S(2)}, u32[]{:S(2)}) %collective-permute-start.12) | collective-permute-done | bytes 131104 | tf_op jit(solution)/shard_map/ppermute | solution.py:441
  63.5 1.7 %collective-permute-start.14 = (bf16[16,32,128]{2,1,0:T(8,128)(2,1)S(1)}, bf16[16,32,128]{2,1,0:T(8,128)(2,1)S(1)}, u32[]{:S(2)}, u32[]{:S(2)}) collective-permute-start(bf16[16,32,128]{2,1,0:T(8,128)(2,1)S(1)} %get-tuple-element.71.field_ref), channel_id=1, source_target_pairs={{0,2},{1,3},{2,0},{3,1},{4,6},{5,7},{6,4},{7,5},{8,10},{9,11},{10,... | collective-permute-start | bytes 393224 | tf_op jit(solution)/shard_map/ppermute | solution.py:91
  66.1 2.4 %stage0.5 = (f32[65,32,128]{2,1,0:T(8,128)S(1)}, f32[65,32,128]{2,1,0:T(8,128)S(1)}, f32[8,128]{1,0:T(8,128)S(1)}) custom-call(s32[2]{0:T(128)S(1)} %pad_add_fusion.position_ref, s32[9,208]{1,0:T(8,128)S(1)} %get-tuple-element.47.list_ref, s32[8]{0:T(128)S(1)} %get-tuple-element.48.total_ref, bf16[192,128,128]{2,1,0:T(8,128)(2,1)S(1)} %get-tuple-element.49.values_ref, ...), custom_call_target="tpu_custom_call" | custom-call | flops 50331648 | bytes 1572864 | tf_op jit(solution)/shard_map/stage0/pallas_call | solution.py:361
  68.4 3.5 %collective-permute-done.14.piece_ref = bf16[16,32,128]{2,1,0:T(8,128)(2,1)S(1)} collective-permute-done((bf16[16,32,128]{2,1,0:T(8,128)(2,1)S(1)}, bf16[16,32,128]{2,1,0:T(8,128)(2,1)S(1)}, u32[]{:S(2)}, u32[]{:S(2)}) %collective-permute-start.14) | collective-permute-done | bytes 131104 | tf_op jit(solution)/shard_map/ppermute | solution.py:91
  72.2 1.6 %stage1.5 = (f32[65,32,128]{2,1,0:T(8,128)S(1)}, f32[65,32,128]{2,1,0:T(8,128)S(1)}) custom-call(s32[9,208]{1,0:T(8,128)S(1)} %get-tuple-element.47.list_ref, s32[8]{0:T(128)S(1)} %get-tuple-element.48.total_ref, bf16[192,128,128]{2,1,0:T(8,128)(2,1)S(1)} %get-tuple-element.49.values_ref, ...), custom_call_target="tpu_custom_call", output_to_operand_aliasing={{0}: (4, {}), {1}: (5, {})} | custom-call | flops 50331648 | bytes 1572864 | tf_op jit(solution)/shard_map/stage1/pallas_call | solution.py:373
  73.8 1.6 %stage2.5 = (f32[65,32,128]{2,1,0:T(8,128)S(1)}, f32[65,32,128]{2,1,0:T(8,128)S(1)}) custom-call(s32[9,208]{1,0:T(8,128)S(1)} %get-tuple-element.47.list_ref, s32[8]{0:T(128)S(1)} %get-tuple-element.48.total_ref, bf16[192,128,128]{2,1,0:T(8,128)(2,1)S(1)} %get-tuple-element.49.values_ref, ...), custom_call_target="tpu_custom_call", output_to_operand_aliasing={{0}: (4, {}), {1}: (5, {})} | custom-call | flops 50331648 | bytes 1572864 | tf_op jit(solution)/shard_map/stage2/pallas_call | solution.py:373
  75.4 1.4 %collective-permute-done.15.refs_0_ = bf16[16,32,128]{2,1,0:T(8,128)(2,1)S(1)} collective-permute-done((bf16[16,32,128]{2,1,0:T(8,128)(2,1)S(1)}, bf16[16,32,128]{2,1,0:T(8,128)(2,1)S(1)}, u32[]{:S(2)}, u32[]{:S(2)}) %collective-permute-start.15) | collective-permute-done | bytes 131104 | tf_op jit(solution)/shard_map/ppermute | solution.py:417
  76.8 1.3 %last0.5 = (f32[65,32,128]{2,1,0:T(8,128)S(1)}, bf16[64,32,128]{2,1,0:T(8,128)(2,1)S(1)}) custom-call(s32[9,208]{1,0:T(8,128)S(1)} %get-tuple-element.47.list_ref, s32[8]{0:T(128)S(1)} %get-tuple-element.48.total_ref, bf16[192,128,128]{2,1,0:T(8,128)(2,1)S(1)} %get-tuple-element.49.values_ref, ...), custom_call_target="tpu_custom_call", output_to_operand_aliasing={{0}: (4, {})} | custom-call | flops 25165824 | bytes 786432 | tf_op jit(solution)/shard_map/last0/pallas_call | solution.py:387
  78.2 1.2 %last1.5.own_ref = f32[65,32,128]{2,1,0:T(8,128)S(1)} custom-call(s32[9,208]{1,0:T(8,128)S(1)} %get-tuple-element.47.list_ref, s32[8]{0:T(128)S(1)} %get-tuple-element.48.total_ref, bf16[192,128,128]{2,1,0:T(8,128)(2,1)S(1)} %get-tuple-element.49.values_ref, ...), custom_call_target="tpu_custom_call", output_to_operand_aliasing={{}: (4, {})} | custom-call | flops 25165824 | bytes 786432 | tf_op jit(solution)/shard_map/last1/pallas_call | solution.py:387
  80.7 2.9 %collective-permute-start.20 = (bf16[16,32,128]{2,1,0:T(8,128)(2,1)S(1)}, bf16[16,32,128]{2,1,0:T(8,128)(2,1)S(1)}, u32[]{:S(2)}, u32[]{:S(2)}) collective-permute-start(bf16[16,32,128]{2,1,0:T(8,128)(2,1)S(1)} %combine3.5), channel_id=1, source_target_pairs={{0,24},{4,28},{8,16},{12,20},{16,8},{20,12},{24,0},{28,4},{1,25},{... | collective-permute-start | bytes 393224 | tf_op jit(solution)/shard_map/ppermute | solution.py:441
  87.4 2.7 %collective-permute-done.19.refs_1_ = bf16[16,32,128]{2,1,0:T(8,128)(2,1)S(1)} collective-permute-done((bf16[16,32,128]{2,1,0:T(8,128)(2,1)S(1)}, bf16[16,32,128]{2,1,0:T(8,128)(2,1)S(1)}, u32[]{:S(2)}, u32[]{:S(2)}) %collective-permute-start.19) | collective-permute-done | bytes 131104 | tf_op jit(solution)/shard_map/ppermute | solution.py:441
  90.8 1.4 %finish.1 = f32[16,32,128]{2,1,0:T(8,128)} custom-call(bf16[16,128,128]{2,1,0:T(8,128)(2,1)S(1)} %get-tuple-element.43.high_ref, bf16[16,128,128]{2,1,0:T(8,128)(2,1)S(1)} %get-tuple-element.44.low_ref, f32[16,32,128]{2,1,0:T(8,128)S(1)} %get-tuple-element.70.sol_ref, f32[16,32,128]{2,1,0:T(8,128)S(1)} %keep.5.base_ref, ...), custom_call_target="tpu_custom_call" | custom-call | tf_op jit(solution)/shard_map/finish/pallas_call | solution.py:460
  (46 shorter events, 22.2 us)
Async XLA Ops:
  2.2 12.8 %collective-permute-start = (bf16[16,32,128]{2,1,0:T(8,128)(2,1)S(1)}, bf16[16,32,128]{2,1,0:T(8,128)(2,1)S(1)}, u32[]{:S(2)}, u32[]{:S(2)}) collective-permute-start(bf16[16,32,128]{2,1,0:T(8,128)(2,1)S(1)} %get-tuple-element.50.field_ref), channel_id=1, source_target_pairs={{0,2},{1,3},{2,0},{3,1},{4,6},{5,7},{6,4},{7,5},{8,10},{9,11},{10,... | collective-permute-start | bytes 393224 | tf_op jit(solution)/shard_map/ppermute | solution.py:91
  6.3 9.7 %collective-permute-start.2 = (bf16[16,32,128]{2,1,0:T(8,128)(2,1)S(1)}, bf16[16,32,128]{2,1,0:T(8,128)(2,1)S(1)}, u32[]{:S(2)}, u32[]{:S(2)}) collective-permute-start(bf16[16,32,128]{2,1,0:T(8,128)(2,1)S(1)} %get-tuple-element.50.field_ref), channel_id=1, source_target_pairs={{0,1},{1,0},{2,3},{3,2},{4,5},{5,4},{6,7},{7,6},{8,9},{9,8},{10,11... | collective-permute-start | bytes 393224 | tf_op jit(solution)/shard_map/ppermute | solution.py:92
  15.0 5.0 %collective-permute-start.1 = (bf16[16,32,128]{2,1,0:T(8,128)(2,1)S(1)}, bf16[16,32,128]{2,1,0:T(8,128)(2,1)S(1)}, u32[]{:S(2)}, u32[]{:S(2)}) collective-permute-start(bf16[16,32,128]{2,1,0:T(8,128)(2,1)S(1)} %hold.3.refs_0_), channel_id=1, source_target_pairs={{0,1},{1,0},{2,3},{3,2},{4,5},{5,4},{6,7},{7,6},{8,9},{9,8},{10,11... | collective-permute-start | bytes 393224 | tf_op jit(solution)/shard_map/ppermute | solution.py:417
  21.3 2.0 %collective-permute-start.3 = (bf16[64,32,128]{2,1,0:T(8,128)(2,1)S(1)}, bf16[64,32,128]{2,1,0:T(8,128)(2,1)S(1)}, u32[]{:S(2)}, u32[]{:S(2)}) collective-permute-start(bf16[64,32,128]{2,1,0:T(8,128)(2,1)S(1)} %get-tuple-element.58.refs_0_), channel_id=1, source_target_pairs={{0,4},{4,0},{8,12},{12,8},{16,20},{20,16},{24,28},{28,24},{1,5},{5... | collective-permute-start | bytes 1572872 | tf_op jit(solution)/shard_map/ppermute | solution.py:422
  23.8 7.9 %collective-permute-start.6 = (bf16[16,32,128]{2,1,0:T(8,128)(2,1)S(1)}, bf16[16,32,128]{2,1,0:T(8,128)(2,1)S(1)}, u32[]{:S(2)}, u32[]{:S(2)}) collective-permute-start(bf16[16,32,128]{2,1,0:T(8,128)(2,1)S(1)} %combine3.3.refs_4_.refs_6_), channel_id=1, source_target_pairs={{0,24},{4,28},{8,16},{12,20},{16,8},{20,12},{24,0},{28,4},{1,25},{... | collective-permute-start | bytes 393224 | tf_op jit(solution)/shard_map/ppermute | solution.py:441
  28.4 6.0 %collective-permute-start.5 = (bf16[16,32,128]{2,1,0:T(8,128)(2,1)S(1)}, bf16[16,32,128]{2,1,0:T(8,128)(2,1)S(1)}, u32[]{:S(2)}, u32[]{:S(2)}) collective-permute-start(bf16[16,32,128]{2,1,0:T(8,128)(2,1)S(1)} %combine2.3.refs_3_.refs_5_), channel_id=1, source_target_pairs={{0,16},{4,20},{8,24},{12,28},{16,0},{20,4},{24,8},{28,12},{1,17},{... | collective-permute-start | bytes 393224 | tf_op jit(solution)/shard_map/ppermute | solution.py:441
  29.3 5.6 %collective-permute-start.4 = (bf16[16,32,128]{2,1,0:T(8,128)(2,1)S(1)}, bf16[16,32,128]{2,1,0:T(8,128)(2,1)S(1)}, u32[]{:S(2)}, u32[]{:S(2)}) collective-permute-start(bf16[16,32,128]{2,1,0:T(8,128)(2,1)S(1)} %combine1.3.refs_2_.refs_4_), channel_id=1, source_target_pairs={{0,8},{4,12},{8,0},{12,4},{16,24},{20,28},{24,16},{28,20},{1,9},{5... | collective-permute-start | bytes 393224 | tf_op jit(solution)/shard_map/ppermute | solution.py:441
  35.6 8.4 %collective-permute-start.7 = (bf16[16,32,128]{2,1,0:T(8,128)(2,1)S(1)}, bf16[16,32,128]{2,1,0:T(8,128)(2,1)S(1)}, u32[]{:S(2)}, u32[]{:S(2)}) collective-permute-start(bf16[16,32,128]{2,1,0:T(8,128)(2,1)S(1)} %get-tuple-element.61.field_ref), channel_id=1, source_target_pairs={{0,2},{1,3},{2,0},{3,1},{4,6},{5,7},{6,4},{7,5},{8,10},{9,11},{10,... | collective-permute-start | bytes 393224 | tf_op jit(solution)/shard_map/ppermute | solution.py:91
  36.2 7.8 %collective-permute-start.9 = (bf16[16,32,128]{2,1,0:T(8,128)(2,1)S(1)}, bf16[16,32,128]{2,1,0:T(8,128)(2,1)S(1)}, u32[]{:S(2)}, u32[]{:S(2)}) collective-permute-start(bf16[16,32,128]{2,1,0:T(8,128)(2,1)S(1)} %get-tuple-element.61.field_ref), channel_id=1, source_target_pairs={{0,1},{1,0},{2,3},{3,2},{4,5},{5,4},{6,7},{7,6},{8,9},{9,8},{10,11... | collective-permute-start | bytes 393224 | tf_op jit(solution)/shard_map/ppermute | solution.py:92
  43.9 5.0 %collective-permute-start.8 = (bf16[16,32,128]{2,1,0:T(8,128)(2,1)S(1)}, bf16[16,32,128]{2,1,0:T(8,128)(2,1)S(1)}, u32[]{:S(2)}, u32[]{:S(2)}) collective-permute-start(bf16[16,32,128]{2,1,0:T(8,128)(2,1)S(1)} %hold.4.refs_0_), channel_id=1, source_target_pairs={{0,1},{1,0},{2,3},{3,2},{4,5},{5,4},{6,7},{7,6},{8,9},{9,8},{10,11... | collective-permute-start | bytes 393224 | tf_op jit(solution)/shard_map/ppermute | solution.py:417
  50.2 2.0 %collective-permute-start.10 = (bf16[64,32,128]{2,1,0:T(8,128)(2,1)S(1)}, bf16[64,32,128]{2,1,0:T(8,128)(2,1)S(1)}, u32[]{:S(2)}, u32[]{:S(2)}) collective-permute-start(bf16[64,32,128]{2,1,0:T(8,128)(2,1)S(1)} %get-tuple-element.69.refs_1_), channel_id=1, source_target_pairs={{0,4},{4,0},{8,12},{12,8},{16,20},{20,16},{24,28},{28,24},{1,5},{5... | collective-permute-start | bytes 1572872 | tf_op jit(solution)/shard_map/ppermute | solution.py:422
  52.7 6.7 %collective-permute-start.13 = (bf16[16,32,128]{2,1,0:T(8,128)(2,1)S(1)}, bf16[16,32,128]{2,1,0:T(8,128)(2,1)S(1)}, u32[]{:S(2)}, u32[]{:S(2)}) collective-permute-start(bf16[16,32,128]{2,1,0:T(8,128)(2,1)S(1)} %combine3.4.refs_9_), channel_id=1, source_target_pairs={{0,24},{4,28},{8,16},{12,20},{16,8},{20,12},{24,0},{28,4},{1,25},{... | collective-permute-start | bytes 393224 | tf_op jit(solution)/shard_map/ppermute | solution.py:441
  56.1 6.0 %collective-permute-start.12 = (bf16[16,32,128]{2,1,0:T(8,128)(2,1)S(1)}, bf16[16,32,128]{2,1,0:T(8,128)(2,1)S(1)}, u32[]{:S(2)}, u32[]{:S(2)}) collective-permute-start(bf16[16,32,128]{2,1,0:T(8,128)(2,1)S(1)} %combine2.4.refs_8_), channel_id=1, source_target_pairs={{0,16},{4,20},{8,24},{12,28},{16,0},{20,4},{24,8},{28,12},{1,17},{... | collective-permute-start | bytes 393224 | tf_op jit(solution)/shard_map/ppermute | solution.py:441
  57.3 5.6 %collective-permute-start.11 = (bf16[16,32,128]{2,1,0:T(8,128)(2,1)S(1)}, bf16[16,32,128]{2,1,0:T(8,128)(2,1)S(1)}, u32[]{:S(2)}, u32[]{:S(2)}) collective-permute-start(bf16[16,32,128]{2,1,0:T(8,128)(2,1)S(1)} %combine1.4.refs_7_), channel_id=1, source_target_pairs={{0,8},{4,12},{8,0},{12,4},{16,24},{20,28},{24,16},{28,20},{1,9},{5... | collective-permute-start | bytes 393224 | tf_op jit(solution)/shard_map/ppermute | solution.py:441
  63.5 8.3 %collective-permute-start.14 = (bf16[16,32,128]{2,1,0:T(8,128)(2,1)S(1)}, bf16[16,32,128]{2,1,0:T(8,128)(2,1)S(1)}, u32[]{:S(2)}, u32[]{:S(2)}) collective-permute-start(bf16[16,32,128]{2,1,0:T(8,128)(2,1)S(1)} %get-tuple-element.71.field_ref), channel_id=1, source_target_pairs={{0,2},{1,3},{2,0},{3,1},{4,6},{5,7},{6,4},{7,5},{8,10},{9,11},{10,... | collective-permute-start | bytes 393224 | tf_op jit(solution)/shard_map/ppermute | solution.py:91
  65.2 7.0 %collective-permute-start.16 = (bf16[16,32,128]{2,1,0:T(8,128)(2,1)S(1)}, bf16[16,32,128]{2,1,0:T(8,128)(2,1)S(1)}, u32[]{:S(2)}, u32[]{:S(2)}) collective-permute-start(bf16[16,32,128]{2,1,0:T(8,128)(2,1)S(1)} %get-tuple-element.71.field_ref), channel_id=1, source_target_pairs={{0,1},{1,0},{2,3},{3,2},{4,5},{5,4},{6,7},{7,6},{8,9},{9,8},{10,11... | collective-permute-start | bytes 393224 | tf_op jit(solution)/shard_map/ppermute | solution.py:92
  71.9 5.0 %collective-permute-start.15 = (bf16[16,32,128]{2,1,0:T(8,128)(2,1)S(1)}, bf16[16,32,128]{2,1,0:T(8,128)(2,1)S(1)}, u32[]{:S(2)}, u32[]{:S(2)}) collective-permute-start(bf16[16,32,128]{2,1,0:T(8,128)(2,1)S(1)} %hold.5.refs_0_), channel_id=1, source_target_pairs={{0,1},{1,0},{2,3},{3,2},{4,5},{5,4},{6,7},{7,6},{8,9},{9,8},{10,11... | collective-permute-start | bytes 393224 | tf_op jit(solution)/shard_map/ppermute | solution.py:417
  78.1 2.0 %collective-permute-start.17 = (bf16[64,32,128]{2,1,0:T(8,128)(2,1)S(1)}, bf16[64,32,128]{2,1,0:T(8,128)(2,1)S(1)}, u32[]{:S(2)}, u32[]{:S(2)}) collective-permute-start(bf16[64,32,128]{2,1,0:T(8,128)(2,1)S(1)} %get-tuple-element.79), channel_id=1, source_target_pairs={{0,4},{4,0},{8,12},{12,8},{16,20},{20,16},{24,28},{28,24},{1,5},{5... | collective-permute-start | bytes 1572872 | tf_op jit(solution)/shard_map/ppermute | solution.py:422
  80.7 6.8 %collective-permute-start.20 = (bf16[16,32,128]{2,1,0:T(8,128)(2,1)S(1)}, bf16[16,32,128]{2,1,0:T(8,128)(2,1)S(1)}, u32[]{:S(2)}, u32[]{:S(2)}) collective-permute-start(bf16[16,32,128]{2,1,0:T(8,128)(2,1)S(1)} %combine3.5), channel_id=1, source_target_pairs={{0,24},{4,28},{8,16},{12,20},{16,8},{20,12},{24,0},{28,4},{1,25},{... | collective-permute-start | bytes 393224 | tf_op jit(solution)/shard_map/ppermute | solution.py:441
  84.1 6.0 %collective-permute-start.19 = (bf16[16,32,128]{2,1,0:T(8,128)(2,1)S(1)}, bf16[16,32,128]{2,1,0:T(8,128)(2,1)S(1)}, u32[]{:S(2)}, u32[]{:S(2)}) collective-permute-start(bf16[16,32,128]{2,1,0:T(8,128)(2,1)S(1)} %combine2.5), channel_id=1, source_target_pairs={{0,16},{4,20},{8,24},{12,28},{16,0},{20,4},{24,8},{28,12},{1,17},{... | collective-permute-start | bytes 393224 | tf_op jit(solution)/shard_map/ppermute | solution.py:441
  85.2 5.6 %collective-permute-start.18 = (bf16[16,32,128]{2,1,0:T(8,128)(2,1)S(1)}, bf16[16,32,128]{2,1,0:T(8,128)(2,1)S(1)}, u32[]{:S(2)}, u32[]{:S(2)}) collective-permute-start(bf16[16,32,128]{2,1,0:T(8,128)(2,1)S(1)} %combine1.5), channel_id=1, source_target_pairs={{0,8},{4,12},{8,0},{12,4},{16,24},{20,28},{24,16},{28,20},{1,9},{5... | collective-permute-start | bytes 393224 | tf_op jit(solution)/shard_map/ppermute | solution.py:441

commit v4 on v3

--- a/solution.py
+++ b/solution.py
@@ -149,7 +149,7 @@
         store.wait()
 
 
-def order_kernel(group, owned, groups, stages, bits, position_ref, count_ref, rows_hbm, cols_hbm, values_hbm,
+def order_kernel(group, owned, groups, stages, bits, count_ref, rows_hbm, cols_hbm, values_hbm,
                  list_out, total_out, values_out, rows_ref, cols_ref, table_ref, total_ref, sems):
     loads = [
         pltpu.make_async_copy(rows_hbm, rows_ref, sems.at[0]),
@@ -158,9 +158,8 @@
     ]
     for load in loads:
         load.start()
-    core = position_ref[0] & (CORES - 1)
-    mine = position_ref[1]
-    used = count_ref[0, 0]
+    core = lax.axis_index("row") & (CORES - 1)
+    mine = lax.axis_index("col")
     row_bits, col_bits = bits
     lists = len(stages) * CORES
     trash = (group // CORES) << col_bits
@@ -169,8 +168,9 @@
             table_ref[piece] = ((index * CORES) << col_bits) + place * owned
     for index in range(lists + 1):
         total_ref[index] = 0
-    loads[0].wait()
-    loads[1].wait()
+    for load in loads[:2]:
+        load.wait()
+    used = count_ref[0, 0]
 
     def place(chunk, carry):
         entries = []
@@ -230,17 +230,20 @@
 
 
 def join(pieces, field):
+    if len(pieces) == 1:
+        return pieces[0]
     each = pieces[0].shape[0]
     for index, piece in enumerate(pieces):
         field[pl.ds(index * each, each)] = piece[...]
-
-
-def first_kernel(steps, chips, bits, position_ref, list_ref, total_ref, values_ref, field_ref, *refs):
+    return field
+
+
+def first_kernel(steps, chips, bits, list_ref, total_ref, values_ref, field_ref, *refs):
     out_refs, refs = refs[:steps], refs[steps:]
     in_refs, refs = refs[:steps], refs[steps:]
     sent_refs, totals, token_ref = refs[:-CORES - 1], refs[-CORES - 1:-1], refs[-1]
     token_ref[...] = jnp.zeros_like(token_ref)
-    chip = lax.shift_right_logical(position_ref[0], 1)
+    chip = lax.axis_index("row") // CORES
     for half, total in enumerate(totals):
         rows = total.shape[0] - 1
         owned = rows // chips
@@ -262,33 +265,33 @@
 def stage_kernel(stage, bits, pieces, list_ref, total_ref, values_ref, *refs):
     piece_refs, refs = refs[:pieces], refs[pieces + CORES:]
     totals, field = refs[:CORES], refs[-1]
-    join(piece_refs, field)
+    field_ref = join(piece_refs, field)
     for half, total in enumerate(totals):
-        add_products(stage * CORES + half, bits, list_ref, total_ref, values_ref, field, total)
+        add_products(stage * CORES + half, bits, list_ref, total_ref, values_ref, field_ref, total)
 
 
 def last_kernel(stage, half, bits, pieces, list_ref, total_ref, values_ref, *refs):
     piece_refs, refs = refs[:pieces], refs[pieces + 1:]
     total, outs, field = refs[0], refs[1:-1], refs[-1]
-    join(piece_refs, field)
-    add_products(stage * CORES + half, bits, list_ref, total_ref, values_ref, field, total)
+    field_ref = join(piece_refs, field)
+    add_products(stage * CORES + half, bits, list_ref, total_ref, values_ref, field_ref, total)
     for out_ref in outs:
         out_ref[...] = total[pl.ds(0, out_ref.shape[0])].astype(out_ref.dtype)
 
 
-def chip_rows(shift, chips, position_ref, own_ref, other_ref, owned):
-    chip = lax.shift_right_logical(position_ref[0], 1)
+def chip_rows(shift, chips, own_ref, other_ref, owned):
+    chip = lax.axis_index("row") // CORES
     at = pl.ds(partner(chip, shift, chips) * owned, owned)
     return own_ref[at] + other_ref[at].astype(jnp.float32)
 
 
-def combine_kernel(shift, chips, position_ref, own_ref, other_ref, send_ref):
+def combine_kernel(shift, chips, own_ref, other_ref, send_ref):
     send_ref[...] = chip_rows(
-        shift, chips, position_ref, own_ref, other_ref, send_ref.shape[0]).astype(send_ref.dtype)
-
-
-def keep_kernel(chips, position_ref, own_ref, other_ref, left_ref, sol_ref, base_ref):
-    keep = chip_rows(0, chips, position_ref, own_ref, other_ref, base_ref.shape[0])
+        shift, chips, own_ref, other_ref, send_ref.shape[0]).astype(send_ref.dtype)
+
+
+def keep_kernel(chips, own_ref, other_ref, left_ref, sol_ref, base_ref):
+    keep = chip_rows(0, chips, own_ref, other_ref, base_ref.shape[0])
     base_ref[...] = left_ref[...] - sol_ref[...] - keep
 
 
@@ -300,7 +303,6 @@
     group = owned * row_devices
     half_rows = chips * owned
     slots = block_values.shape[2]
-    position = jnp.stack([lax.axis_index("row"), lax.axis_index("col")]).astype(jnp.int32)
 
     stages = gather_stages(groups)
     final = len(stages) - 1
@@ -334,11 +336,11 @@
     *lists, values = pl.pallas_call(
         functools.partial(order_kernel, group, owned, groups, stages, bits),
         out_shape=[
-            jax.ShapeDtypeStruct((lists_total + 1, slots + UNROLL), jnp.int32),
-            jax.ShapeDtypeStruct((lists_total,), jnp.int32),
+            pltpu.SMEM((lists_total + 1, slots + UNROLL), jnp.int32),
+            pltpu.SMEM((lists_total,), jnp.int32),
             pltpu.VMEM(block_values.shape[2:], block_values.dtype),
         ],
-        in_specs=[in_smem()] * 2 + [in_hbm()] * 3,
+        in_specs=[in_smem()] + [in_hbm()] * 3,
         out_specs=[in_smem()] * 2 + [in_vmem()],
         scratch_shapes=[
             index_type, index_type,
@@ -347,7 +349,7 @@
         ],
         compiler_params=params(),
         name="order",
-    )(position, block_counts, *[stay_in_hbm(array) for array in (block_rows, block_cols, block_values[0, 0])])
+    )(block_counts, *[stay_in_hbm(array) for array in (block_rows, block_cols, block_values[0, 0])])
 
     def cost(share):
         return pl.CostEstimate(
@@ -361,12 +363,12 @@
         return pl.pallas_call(
             functools.partial(first_kernel, len(outs), chips, bits),
             out_shape=[total_type] * CORES + [token_type],
-            in_specs=[in_smem()] * 3 + [in_vmem()] * (2 + len(outs) + len(ins) + len(sent)),
+            in_specs=[in_smem()] * 2 + [in_vmem()] * (2 + len(outs) + len(ins) + len(sent)),
             out_specs=[in_vmem()] * (CORES + 1),
             compiler_params=params(),
             cost_estimate=cost(1 / groups),
             name="stage0",
-        )(position, *lists, values, field, *outs, *ins, *sent)
+        )(*lists, values, field, *outs, *ins, *sent)
 
     def product_stage(stage, pieces, totals):
         inputs = 3 + len(pieces)
@@ -433,21 +435,21 @@
             sends[shift] = pl.pallas_call(
                 functools.partial(combine_kernel, shift, chips),
                 out_shape=rounded_type,
-                in_specs=[in_smem()] + [in_vmem()] * 2,
+                in_specs=[in_vmem()] * 2,
                 out_specs=in_vmem(),
                 compiler_params=params(),
                 name="combine%d" % shift,
-            )(position, own, incoming)
+            )(own, incoming)
             pieces.append(lax.ppermute(sends[shift], "row", pairs))
         sent += [sends[shift] for shift in range(1, chips)]
         base = pl.pallas_call(
             functools.partial(keep_kernel, chips),
             out_shape=field_type,
-            in_specs=[in_smem()] + [in_vmem()] * 4,
+            in_specs=[in_vmem()] * 4,
             out_specs=in_vmem(),
             compiler_params=params(),
             name="keep",
-        )(position, own, incoming, left, sol)
+        )(own, incoming, left, sol)
         if step < ITERS - 1:
             sol, left, rounded = pl.pallas_call(
                 functools.partial(apply_kernel, len(pieces)),

time: 92.5 us -> 85.9 us (0.929)
  Pallas kernels: 39.9 us -> 19.7 us
  waiting for transfers between devices: 27.6 us -> 36.4 us
  starting transfers between devices: 23.8 us -> 28.1 us
    pallas_call x6, Pallas kernels: 9.66 us -> 4.72 us  [product_stage(): pl.pallas_call(functools.partial(stage_kernel, stage, bits, len(pieces)),...]
    pallas_call x9, Pallas kernels: 5.16 us -> 0.25 us  [per_device(): pl.pallas_call(functools.partial(combine_kernel, shift, chips), out_shape...]
    pallas_call x6, Pallas kernels: 7.41 us -> 2.54 us  [product_last(): pl.pallas_call(functools.partial(last_kernel, final, half, bits, len(piec...]
    ppermute x9, waiting for transfers between devices: 13.5 us -> 17.9 us  [per_device(): pieces.append(lax.ppermute(sends[shift], 'row', pairs))]
    ppermute x3, waiting for transfers between devices: 3.99 us -> 7.44 us  [per_device(): fields.append(lax.ppermute(fields[index], 'col', neighbours(groups)))]
    ppermute x3, starting transfers between devices: 6.41 us -> 9.17 us  [gather(): lax.ppermute(rounded, 'col', ring(2 * step))]
    pallas_call x3, Pallas kernels: 6.68 us -> 4.21 us  [product_first(): pl.pallas_call(functools.partial(first_kernel, len(outs), chips, bits), o...]
    ppermute x3, waiting for transfers between devices: 2.08 us -> 4.48 us  [per_device(): incoming = lax.ppermute(outgoing, 'row', neighbours(row_devices))]
  transfers between devices with their start and end apart: 21 -> 21, of which waited for: 17 -> 17; matrix products, arithmetic and copies ran while one was open for 0% -> 0% of each run, Pallas kernels for 32% -> 16%
where the time goes in v4:
time: 85.9 us; the launch traced here: 85 us
  waiting for transfers between devices  36.4 us (42%)
  starting transfers between devices  28.1 us (33%)
  Pallas kernels  19.7 us (23%)
    ppermute x9, waiting for transfers between devices, per_device(): pieces.append(lax.ppermute(sends[shift], 'row', pairs))  17.9 us
    ppermute x9, starting transfers between devices, per_device(): pieces.append(lax.ppermute(sends[shift], 'row', pairs))  11.1 us
    ppermute x3, starting transfers between devices, gather(): lax.ppermute(rounded, 'col', ring(2 * step))  9.17 us
    ppermute x3, waiting for transfers between devices, per_device(): fields.append(lax.ppermute(fields[index], 'col', neighbours(groups)))  7.44 us
    ppermute x3, waiting for transfers between devices, gather(): lax.ppermute(rounded, 'col', ring(2 * step))  6.61 us
    pallas_call x6, Pallas kernels, product_stage(): pl.pallas_call(functools.partial(stage_kernel, stage, bits, len(pieces)),...  4.72 us
    ppermute x3, starting transfers between devices, gather(): return [rounded] + far + [lax.ppermute(rounded, 'col', neighbours(groups))]  4.6 us
    ppermute x3, waiting for transfers between devices, per_device(): incoming = lax.ppermute(outgoing, 'row', neighbours(row_devices))  4.48 us
  transfers between devices with their start and end apart: 21, of which 17 were waited for; matrix products, arithmetic and copies ran while one was open for 0% of the time, Pallas kernels for 16%

profile of v4, /device:TPU:0, one launch (start us, length us, event | category | flops | bytes accessed | tf_op | source)
XLA Modules:
  0.0 85.0 jit_solution(12331508310619100762)
XLA Ops:
  0.0 2.1 %start.1 = (bf16[16,128,128]{2,1,0:T(8,128)(2,1)S(1)}, bf16[16,128,128]{2,1,0:T(8,128)(2,1)S(1)}, f32[16,32,128]{2,1,0:T(8,128)S(1)}, f32[16,32,128]{2,1,0:T(8,128)S(1)}, bf16[16,32,128]{2,1,0:T(8,128)(2,1)S(1)}) custom-call(f32[16,128,128]{2,1,0:T(8,128)} %bitcast.5, f32[16,32,128]{2,1,0:T(8,128)} %bitcast.6), custom_call_target="tpu_custom_call" | custom-call | tf_op jit(solution)/shard_map/start/pallas_call | solution.py:323
  2.2 4.1 %collective-permute-start = (bf16[16,32,128]{2,1,0:T(8,128)(2,1)S(1)}, bf16[16,32,128]{2,1,0:T(8,128)(2,1)S(1)}, u32[]{:S(2)}, u32[]{:S(2)}) collective-permute-start(bf16[16,32,128]{2,1,0:T(8,128)(2,1)S(1)} %get-tuple-element.50.field_ref), channel_id=1, source_target_pairs={{0,2},{1,3},{2,0},{3,1},{4,6},{5,7},{6,4},{7,5},{8,10},{9,11},{10,... | collective-permute-start | bytes 393224 | tf_op jit(solution)/shard_map/ppermute | solution.py:91
  6.3 1.6 %collective-permute-start.2 = (bf16[16,32,128]{2,1,0:T(8,128)(2,1)S(1)}, bf16[16,32,128]{2,1,0:T(8,128)(2,1)S(1)}, u32[]{:S(2)}, u32[]{:S(2)}) collective-permute-start(bf16[16,32,128]{2,1,0:T(8,128)(2,1)S(1)} %get-tuple-element.50.field_ref), channel_id=1, source_target_pairs={{0,1},{1,0},{2,3},{3,2},{4,5},{5,4},{6,7},{7,6},{8,9},{9,8},{10,11... | collective-permute-start | bytes 393224 | tf_op jit(solution)/shard_map/ppermute | solution.py:92
  8.5 2.8 %order.1 = (s32[9,208]{1,0:T(8,128)S(4)}, s32[8]{0:T(128)S(4)}, bf16[192,128,128]{2,1,0:T(8,128)(2,1)S(1)}) custom-call(s32[1,1]{1,0:T(1,128)S(6)} %copy.49.count_ref, s32[1,1,192]{2,1,0:T(1,128)} %rows_hbm.1, s32[1,1,192]{2,1,0:T(1,128)} %cols_hbm.1, bf16[192,128,128]{2,1,0:T(8,128)(2,1)} %bitcast.4), custom_call_target="tpu_custom_call" | custom-call | tf_op jit(solution)/shard_map/order/pallas_call | solution.py:336
  11.3 1.3 %stage0.3 = (f32[65,32,128]{2,1,0:T(8,128)S(1)}, f32[65,32,128]{2,1,0:T(8,128)S(1)}, f32[8,128]{1,0:T(8,128)S(1)}) custom-call(s32[9,208]{1,0:T(8,128)S(4)} %get-tuple-element.47.list_ref, s32[8]{0:T(128)S(4)} %get-tuple-element.48.total_ref, bf16[192,128,128]{2,1,0:T(8,128)(2,1)S(1)} %get-tuple-element.49.values_ref, ...), custom_call_target="tpu_custom_call" | custom-call | flops 50331648 | bytes 1572864 | tf_op jit(solution)/shard_map/stage0/pallas_call | solution.py:363
  12.7 2.3 %collective-permute-start.1 = (bf16[16,32,128]{2,1,0:T(8,128)(2,1)S(1)}, bf16[16,32,128]{2,1,0:T(8,128)(2,1)S(1)}, u32[]{:S(2)}, u32[]{:S(2)}) collective-permute-start(bf16[16,32,128]{2,1,0:T(8,128)(2,1)S(1)} %hold.3.refs_0_), channel_id=1, source_target_pairs={{0,1},{1,0},{2,3},{3,2},{4,5},{5,4},{6,7},{7,6},{8,9},{9,8},{10,11... | collective-permute-start | bytes 393224 | tf_op jit(solution)/shard_map/ppermute | solution.py:419
  16.6 1.4 %collective-permute-done.1.refs_0_ = bf16[16,32,128]{2,1,0:T(8,128)(2,1)S(1)} collective-permute-done((bf16[16,32,128]{2,1,0:T(8,128)(2,1)S(1)}, bf16[16,32,128]{2,1,0:T(8,128)(2,1)S(1)}, u32[]{:S(2)}, u32[]{:S(2)}) %collective-permute-start.1) | collective-permute-done | bytes 131104 | tf_op jit(solution)/shard_map/ppermute | solution.py:419
  18.9 1.5 %collective-permute-done.3.other_ref.refs_1_.refs_2_ = bf16[64,32,128]{2,1,0:T(8,128)(2,1)S(1)} collective-permute-done((bf16[64,32,128]{2,1,0:T(8,128)(2,1)S(1)}, bf16[64,32,128]{2,1,0:T(8,128)(2,1)S(1)}, u32[]{:S(2)}, u32[]{:S(2)}) %collective-permute-start.3) | collective-permute-done | bytes 524320 | tf_op jit(solution)/shard_map/ppermute | solution.py:424
  20.4 2.3 %collective-permute-start.6 = (bf16[16,32,128]{2,1,0:T(8,128)(2,1)S(1)}, bf16[16,32,128]{2,1,0:T(8,128)(2,1)S(1)}, u32[]{:S(2)}, u32[]{:S(2)}) collective-permute-start(bf16[16,32,128]{2,1,0:T(8,128)(2,1)S(1)} %combine3.3.refs_4_.refs_6_), channel_id=1, source_target_pairs={{0,24},{4,28},{8,16},{12,20},{16,8},{20,12},{24,0},{28,4},{1,25},{... | collective-permute-start | bytes 393224 | tf_op jit(solution)/shard_map/ppermute | solution.py:443
  24.3 3.0 %collective-permute-done.6.refs_2_ = bf16[16,32,128]{2,1,0:T(8,128)(2,1)S(1)} collective-permute-done((bf16[16,32,128]{2,1,0:T(8,128)(2,1)S(1)}, bf16[16,32,128]{2,1,0:T(8,128)(2,1)S(1)}, u32[]{:S(2)}, u32[]{:S(2)}) %collective-permute-start.6) | collective-permute-done | bytes 131104 | tf_op jit(solution)/shard_map/ppermute | solution.py:443
  27.3 2.5 %collective-permute-done.5.refs_1_ = bf16[16,32,128]{2,1,0:T(8,128)(2,1)S(1)} collective-permute-done((bf16[16,32,128]{2,1,0:T(8,128)(2,1)S(1)}, bf16[16,32,128]{2,1,0:T(8,128)(2,1)S(1)}, u32[]{:S(2)}, u32[]{:S(2)}) %collective-permute-start.5) | collective-permute-done | bytes 131104 | tf_op jit(solution)/shard_map/ppermute | solution.py:443
  31.0 2.3 %collective-permute-start.7 = (bf16[16,32,128]{2,1,0:T(8,128)(2,1)S(1)}, bf16[16,32,128]{2,1,0:T(8,128)(2,1)S(1)}, u32[]{:S(2)}, u32[]{:S(2)}) collective-permute-start(bf16[16,32,128]{2,1,0:T(8,128)(2,1)S(1)} %get-tuple-element.61.field_ref), channel_id=1, source_target_pairs={{0,2},{1,3},{2,0},{3,1},{4,6},{5,7},{6,4},{7,5},{8,10},{9,11},{10,... | collective-permute-start | bytes 393224 | tf_op jit(solution)/shard_map/ppermute | solution.py:91
  33.4 1.6 %collective-permute-start.9 = (bf16[16,32,128]{2,1,0:T(8,128)(2,1)S(1)}, bf16[16,32,128]{2,1,0:T(8,128)(2,1)S(1)}, u32[]{:S(2)}, u32[]{:S(2)}) collective-permute-start(bf16[16,32,128]{2,1,0:T(8,128)(2,1)S(1)} %get-tuple-element.61.field_ref), channel_id=1, source_target_pairs={{0,1},{1,0},{2,3},{3,2},{4,5},{5,4},{6,7},{7,6},{8,9},{9,8},{10,11... | collective-permute-start | bytes 393224 | tf_op jit(solution)/shard_map/ppermute | solution.py:92
  35.0 1.3 %stage0.4 = (f32[65,32,128]{2,1,0:T(8,128)S(1)}, f32[65,32,128]{2,1,0:T(8,128)S(1)}, f32[8,128]{1,0:T(8,128)S(1)}) custom-call(s32[9,208]{1,0:T(8,128)S(4)} %get-tuple-element.47.list_ref, s32[8]{0:T(128)S(4)} %get-tuple-element.48.total_ref, bf16[192,128,128]{2,1,0:T(8,128)(2,1)S(1)} %get-tuple-element.49.values_ref, ...), custom_call_target="tpu_custom_call" | custom-call | flops 50331648 | bytes 1572864 | tf_op jit(solution)/shard_map/stage0/pallas_call | solution.py:363
  36.3 3.4 %collective-permute-done.7.piece_ref = bf16[16,32,128]{2,1,0:T(8,128)(2,1)S(1)} collective-permute-done((bf16[16,32,128]{2,1,0:T(8,128)(2,1)S(1)}, bf16[16,32,128]{2,1,0:T(8,128)(2,1)S(1)}, u32[]{:S(2)}, u32[]{:S(2)}) %collective-permute-start.7) | collective-permute-done | bytes 131104 | tf_op jit(solution)/shard_map/ppermute | solution.py:91
  41.6 3.1 %collective-permute-done.8.refs_0_ = bf16[16,32,128]{2,1,0:T(8,128)(2,1)S(1)} collective-permute-done((bf16[16,32,128]{2,1,0:T(8,128)(2,1)S(1)}, bf16[16,32,128]{2,1,0:T(8,128)(2,1)S(1)}, u32[]{:S(2)}, u32[]{:S(2)}) %collective-permute-start.8) | collective-permute-done | bytes 131104 | tf_op jit(solution)/shard_map/ppermute | solution.py:419
  45.7 1.5 %collective-permute-done.10.other_ref.refs_3_ = bf16[64,32,128]{2,1,0:T(8,128)(2,1)S(1)} collective-permute-done((bf16[64,32,128]{2,1,0:T(8,128)(2,1)S(1)}, bf16[64,32,128]{2,1,0:T(8,128)(2,1)S(1)}, u32[]{:S(2)}, u32[]{:S(2)}) %collective-permute-start.10) | collective-permute-done | bytes 524320 | tf_op jit(solution)/shard_map/ppermute | solution.py:424
  47.2 2.0 %collective-permute-start.13 = (bf16[16,32,128]{2,1,0:T(8,128)(2,1)S(1)}, bf16[16,32,128]{2,1,0:T(8,128)(2,1)S(1)}, u32[]{:S(2)}, u32[]{:S(2)}) collective-permute-start(bf16[16,32,128]{2,1,0:T(8,128)(2,1)S(1)} %combine3.4.refs_9_), channel_id=1, source_target_pairs={{0,24},{4,28},{8,16},{12,20},{16,8},{20,12},{24,0},{28,4},{1,25},{... | collective-permute-start | bytes 393224 | tf_op jit(solution)/shard_map/ppermute | solution.py:443
  49.2 1.1 %collective-permute-start.12 = (bf16[16,32,128]{2,1,0:T(8,128)(2,1)S(1)}, bf16[16,32,128]{2,1,0:T(8,128)(2,1)S(1)}, u32[]{:S(2)}, u32[]{:S(2)}) collective-permute-start(bf16[16,32,128]{2,1,0:T(8,128)(2,1)S(1)} %combine2.4.refs_8_), channel_id=1, source_target_pairs={{0,16},{4,20},{8,24},{12,28},{16,0},{20,4},{24,8},{28,12},{1,17},{... | collective-permute-start | bytes 393224 | tf_op jit(solution)/shard_map/ppermute | solution.py:443
  51.0 3.3 %collective-permute-done.13.refs_2_ = bf16[16,32,128]{2,1,0:T(8,128)(2,1)S(1)} collective-permute-done((bf16[16,32,128]{2,1,0:T(8,128)(2,1)S(1)}, bf16[16,32,128]{2,1,0:T(8,128)(2,1)S(1)}, u32[]{:S(2)}, u32[]{:S(2)}) %collective-permute-start.13) | collective-permute-done | bytes 131104 | tf_op jit(solution)/shard_map/ppermute | solution.py:443
  54.3 2.2 %collective-permute-done.12.refs_1_ = bf16[16,32,128]{2,1,0:T(8,128)(2,1)S(1)} collective-permute-done((bf16[16,32,128]{2,1,0:T(8,128)(2,1)S(1)}, bf16[16,32,128]{2,1,0:T(8,128)(2,1)S(1)}, u32[]{:S(2)}, u32[]{:S(2)}) %collective-permute-start.12) | collective-permute-done | bytes 131104 | tf_op jit(solution)/shard_map/ppermute | solution.py:443
  57.6 2.7 %collective-permute-start.14 = (bf16[16,32,128]{2,1,0:T(8,128)(2,1)S(1)}, bf16[16,32,128]{2,1,0:T(8,128)(2,1)S(1)}, u32[]{:S(2)}, u32[]{:S(2)}) collective-permute-start(bf16[16,32,128]{2,1,0:T(8,128)(2,1)S(1)} %get-tuple-element.71.field_ref), channel_id=1, source_target_pairs={{0,2},{1,3},{2,0},{3,1},{4,6},{5,7},{6,4},{7,5},{8,10},{9,11},{10,... | collective-permute-start | bytes 393224 | tf_op jit(solution)/shard_map/ppermute | solution.py:91
  60.4 1.4 %collective-permute-start.16 = (bf16[16,32,128]{2,1,0:T(8,128)(2,1)S(1)}, bf16[16,32,128]{2,1,0:T(8,128)(2,1)S(1)}, u32[]{:S(2)}, u32[]{:S(2)}) collective-permute-start(bf16[16,32,128]{2,1,0:T(8,128)(2,1)S(1)} %get-tuple-element.71.field_ref), channel_id=1, source_target_pairs={{0,1},{1,0},{2,3},{3,2},{4,5},{5,4},{6,7},{7,6},{8,9},{9,8},{10,11... | collective-permute-start | bytes 393224 | tf_op jit(solution)/shard_map/ppermute | solution.py:92
  61.8 1.5 %stage0.5 = (f32[65,32,128]{2,1,0:T(8,128)S(1)}, f32[65,32,128]{2,1,0:T(8,128)S(1)}, f32[8,128]{1,0:T(8,128)S(1)}) custom-call(s32[9,208]{1,0:T(8,128)S(4)} %get-tuple-element.47.list_ref, s32[8]{0:T(128)S(4)} %get-tuple-element.48.total_ref, bf16[192,128,128]{2,1,0:T(8,128)(2,1)S(1)} %get-tuple-element.49.values_ref, ...), custom_call_target="tpu_custom_call" | custom-call | flops 50331648 | bytes 1572864 | tf_op jit(solution)/shard_map/stage0/pallas_call | solution.py:363
  63.3 3.2 %collective-permute-done.14.piece_ref = bf16[16,32,128]{2,1,0:T(8,128)(2,1)S(1)} collective-permute-done((bf16[16,32,128]{2,1,0:T(8,128)(2,1)S(1)}, bf16[16,32,128]{2,1,0:T(8,128)(2,1)S(1)}, u32[]{:S(2)}, u32[]{:S(2)}) %collective-permute-start.14) | collective-permute-done | bytes 131104 | tf_op jit(solution)/shard_map/ppermute | solution.py:91
  68.5 3.0 %collective-permute-done.15.refs_0_ = bf16[16,32,128]{2,1,0:T(8,128)(2,1)S(1)} collective-permute-done((bf16[16,32,128]{2,1,0:T(8,128)(2,1)S(1)}, bf16[16,32,128]{2,1,0:T(8,128)(2,1)S(1)}, u32[]{:S(2)}, u32[]{:S(2)}) %collective-permute-start.15) | collective-permute-done | bytes 131104 | tf_op jit(solution)/shard_map/ppermute | solution.py:419
  72.4 1.5 %collective-permute-done.17.other_ref = bf16[64,32,128]{2,1,0:T(8,128)(2,1)S(1)} collective-permute-done((bf16[64,32,128]{2,1,0:T(8,128)(2,1)S(1)}, bf16[64,32,128]{2,1,0:T(8,128)(2,1)S(1)}, u32[]{:S(2)}, u32[]{:S(2)}) %collective-permute-start.17) | collective-permute-done | bytes 524320 | tf_op jit(solution)/shard_map/ppermute | solution.py:424
  73.9 2.0 %collective-permute-start.20 = (bf16[16,32,128]{2,1,0:T(8,128)(2,1)S(1)}, bf16[16,32,128]{2,1,0:T(8,128)(2,1)S(1)}, u32[]{:S(2)}, u32[]{:S(2)}) collective-permute-start(bf16[16,32,128]{2,1,0:T(8,128)(2,1)S(1)} %combine3.5), channel_id=1, source_target_pairs={{0,24},{4,28},{8,16},{12,20},{16,8},{20,12},{24,0},{28,4},{1,25},{... | collective-permute-start | bytes 393224 | tf_op jit(solution)/shard_map/ppermute | solution.py:443
  75.9 1.1 %collective-permute-start.19 = (bf16[16,32,128]{2,1,0:T(8,128)(2,1)S(1)}, bf16[16,32,128]{2,1,0:T(8,128)(2,1)S(1)}, u32[]{:S(2)}, u32[]{:S(2)}) collective-permute-start(bf16[16,32,128]{2,1,0:T(8,128)(2,1)S(1)} %combine2.5), channel_id=1, source_target_pairs={{0,16},{4,20},{8,24},{12,28},{16,0},{20,4},{24,8},{28,12},{1,17},{... | collective-permute-start | bytes 393224 | tf_op jit(solution)/shard_map/ppermute | solution.py:443
  77.7 3.3 %collective-permute-done.20.refs_2_ = bf16[16,32,128]{2,1,0:T(8,128)(2,1)S(1)} collective-permute-done((bf16[16,32,128]{2,1,0:T(8,128)(2,1)S(1)}, bf16[16,32,128]{2,1,0:T(8,128)(2,1)S(1)}, u32[]{:S(2)}, u32[]{:S(2)}) %collective-permute-start.20) | collective-permute-done | bytes 131104 | tf_op jit(solution)/shard_map/ppermute | solution.py:443
  81.0 2.2 %collective-permute-done.19.refs_1_ = bf16[16,32,128]{2,1,0:T(8,128)(2,1)S(1)} collective-permute-done((bf16[16,32,128]{2,1,0:T(8,128)(2,1)S(1)}, bf16[16,32,128]{2,1,0:T(8,128)(2,1)S(1)}, u32[]{:S(2)}, u32[]{:S(2)}) %collective-permute-start.19) | collective-permute-done | bytes 131104 | tf_op jit(solution)/shard_map/ppermute | solution.py:443
  83.6 1.4 %finish.1 = f32[16,32,128]{2,1,0:T(8,128)} custom-call(bf16[16,128,128]{2,1,0:T(8,128)(2,1)S(1)} %get-tuple-element.43.high_ref, bf16[16,128,128]{2,1,0:T(8,128)(2,1)S(1)} %get-tuple-element.44.low_ref, f32[16,32,128]{2,1,0:T(8,128)S(1)} %get-tuple-element.70.sol_ref, f32[16,32,128]{2,1,0:T(8,128)S(1)} %keep.5.base_ref, ...), custom_call_target="tpu_custom_call" | custom-call | tf_op jit(solution)/shard_map/finish/pallas_call | solution.py:462
  (45 shorter events, 14.1 us)
Async XLA Ops:
  2.2 10.5 %collective-permute-start = (bf16[16,32,128]{2,1,0:T(8,128)(2,1)S(1)}, bf16[16,32,128]{2,1,0:T(8,128)(2,1)S(1)}, u32[]{:S(2)}, u32[]{:S(2)}) collective-permute-start(bf16[16,32,128]{2,1,0:T(8,128)(2,1)S(1)} %get-tuple-element.50.field_ref), channel_id=1, source_target_pairs={{0,2},{1,3},{2,0},{3,1},{4,6},{5,7},{6,4},{7,5},{8,10},{9,11},{10,... | collective-permute-start | bytes 393224 | tf_op jit(solution)/shard_map/ppermute | solution.py:91
  6.3 8.8 %collective-permute-start.2 = (bf16[16,32,128]{2,1,0:T(8,128)(2,1)S(1)}, bf16[16,32,128]{2,1,0:T(8,128)(2,1)S(1)}, u32[]{:S(2)}, u32[]{:S(2)}) collective-permute-start(bf16[16,32,128]{2,1,0:T(8,128)(2,1)S(1)} %get-tuple-element.50.field_ref), channel_id=1, source_target_pairs={{0,1},{1,0},{2,3},{3,2},{4,5},{5,4},{6,7},{7,6},{8,9},{9,8},{10,11... | collective-permute-start | bytes 393224 | tf_op jit(solution)/shard_map/ppermute | solution.py:92
  12.7 5.3 %collective-permute-start.1 = (bf16[16,32,128]{2,1,0:T(8,128)(2,1)S(1)}, bf16[16,32,128]{2,1,0:T(8,128)(2,1)S(1)}, u32[]{:S(2)}, u32[]{:S(2)}) collective-permute-start(bf16[16,32,128]{2,1,0:T(8,128)(2,1)S(1)} %hold.3.refs_0_), channel_id=1, source_target_pairs={{0,1},{1,0},{2,3},{3,2},{4,5},{5,4},{6,7},{7,6},{8,9},{9,8},{10,11... | collective-permute-start | bytes 393224 | tf_op jit(solution)/shard_map/ppermute | solution.py:419
  18.4 2.0 %collective-permute-start.3 = (bf16[64,32,128]{2,1,0:T(8,128)(2,1)S(1)}, bf16[64,32,128]{2,1,0:T(8,128)(2,1)S(1)}, u32[]{:S(2)}, u32[]{:S(2)}) collective-permute-start(bf16[64,32,128]{2,1,0:T(8,128)(2,1)S(1)} %get-tuple-element.58.refs_0_), channel_id=1, source_target_pairs={{0,4},{4,0},{8,12},{12,8},{16,20},{20,16},{24,28},{28,24},{1,5},{5... | collective-permute-start | bytes 1572872 | tf_op jit(solution)/shard_map/ppermute | solution.py:424
  20.4 6.8 %collective-permute-start.6 = (bf16[16,32,128]{2,1,0:T(8,128)(2,1)S(1)}, bf16[16,32,128]{2,1,0:T(8,128)(2,1)S(1)}, u32[]{:S(2)}, u32[]{:S(2)}) collective-permute-start(bf16[16,32,128]{2,1,0:T(8,128)(2,1)S(1)} %combine3.3.refs_4_.refs_6_), channel_id=1, source_target_pairs={{0,24},{4,28},{8,16},{12,20},{16,8},{20,12},{24,0},{28,4},{1,25},{... | collective-permute-start | bytes 393224 | tf_op jit(solution)/shard_map/ppermute | solution.py:443
  22.7 7.0 %collective-permute-start.5 = (bf16[16,32,128]{2,1,0:T(8,128)(2,1)S(1)}, bf16[16,32,128]{2,1,0:T(8,128)(2,1)S(1)}, u32[]{:S(2)}, u32[]{:S(2)}) collective-permute-start(bf16[16,32,128]{2,1,0:T(8,128)(2,1)S(1)} %combine2.3.refs_3_.refs_5_), channel_id=1, source_target_pairs={{0,16},{4,20},{8,24},{12,28},{16,0},{20,4},{24,8},{28,12},{1,17},{... | collective-permute-start | bytes 393224 | tf_op jit(solution)/shard_map/ppermute | solution.py:443
  23.7 6.6 %collective-permute-start.4 = (bf16[16,32,128]{2,1,0:T(8,128)(2,1)S(1)}, bf16[16,32,128]{2,1,0:T(8,128)(2,1)S(1)}, u32[]{:S(2)}, u32[]{:S(2)}) collective-permute-start(bf16[16,32,128]{2,1,0:T(8,128)(2,1)S(1)} %combine1.3.refs_2_.refs_4_), channel_id=1, source_target_pairs={{0,8},{4,12},{8,0},{12,4},{16,24},{20,28},{24,16},{28,20},{1,9},{5... | collective-permute-start | bytes 393224 | tf_op jit(solution)/shard_map/ppermute | solution.py:443
  31.0 8.7 %collective-permute-start.7 = (bf16[16,32,128]{2,1,0:T(8,128)(2,1)S(1)}, bf16[16,32,128]{2,1,0:T(8,128)(2,1)S(1)}, u32[]{:S(2)}, u32[]{:S(2)}) collective-permute-start(bf16[16,32,128]{2,1,0:T(8,128)(2,1)S(1)} %get-tuple-element.61.field_ref), channel_id=1, source_target_pairs={{0,2},{1,3},{2,0},{3,1},{4,6},{5,7},{6,4},{7,5},{8,10},{9,11},{10,... | collective-permute-start | bytes 393224 | tf_op jit(solution)/shard_map/ppermute | solution.py:91
  33.4 6.7 %collective-permute-start.9 = (bf16[16,32,128]{2,1,0:T(8,128)(2,1)S(1)}, bf16[16,32,128]{2,1,0:T(8,128)(2,1)S(1)}, u32[]{:S(2)}, u32[]{:S(2)}) collective-permute-start(bf16[16,32,128]{2,1,0:T(8,128)(2,1)S(1)} %get-tuple-element.61.field_ref), channel_id=1, source_target_pairs={{0,1},{1,0},{2,3},{3,2},{4,5},{5,4},{6,7},{7,6},{8,9},{9,8},{10,11... | collective-permute-start | bytes 393224 | tf_op jit(solution)/shard_map/ppermute | solution.py:92
  39.8 5.0 %collective-permute-start.8 = (bf16[16,32,128]{2,1,0:T(8,128)(2,1)S(1)}, bf16[16,32,128]{2,1,0:T(8,128)(2,1)S(1)}, u32[]{:S(2)}, u32[]{:S(2)}) collective-permute-start(bf16[16,32,128]{2,1,0:T(8,128)(2,1)S(1)} %hold.4.refs_0_), channel_id=1, source_target_pairs={{0,1},{1,0},{2,3},{3,2},{4,5},{5,4},{6,7},{7,6},{8,9},{9,8},{10,11... | collective-permute-start | bytes 393224 | tf_op jit(solution)/shard_map/ppermute | solution.py:419
  45.2 2.0 %collective-permute-start.10 = (bf16[64,32,128]{2,1,0:T(8,128)(2,1)S(1)}, bf16[64,32,128]{2,1,0:T(8,128)(2,1)S(1)}, u32[]{:S(2)}, u32[]{:S(2)}) collective-permute-start(bf16[64,32,128]{2,1,0:T(8,128)(2,1)S(1)} %get-tuple-element.69.refs_1_), channel_id=1, source_target_pairs={{0,4},{4,0},{8,12},{12,8},{16,20},{20,16},{24,28},{28,24},{1,5},{5... | collective-permute-start | bytes 1572872 | tf_op jit(solution)/shard_map/ppermute | solution.py:424
  47.2 7.2 %collective-permute-start.13 = (bf16[16,32,128]{2,1,0:T(8,128)(2,1)S(1)}, bf16[16,32,128]{2,1,0:T(8,128)(2,1)S(1)}, u32[]{:S(2)}, u32[]{:S(2)}) collective-permute-start(bf16[16,32,128]{2,1,0:T(8,128)(2,1)S(1)} %combine3.4.refs_9_), channel_id=1, source_target_pairs={{0,24},{4,28},{8,16},{12,20},{16,8},{20,12},{24,0},{28,4},{1,25},{... | collective-permute-start | bytes 393224 | tf_op jit(solution)/shard_map/ppermute | solution.py:443
  49.2 7.3 %collective-permute-start.12 = (bf16[16,32,128]{2,1,0:T(8,128)(2,1)S(1)}, bf16[16,32,128]{2,1,0:T(8,128)(2,1)S(1)}, u32[]{:S(2)}, u32[]{:S(2)}) collective-permute-start(bf16[16,32,128]{2,1,0:T(8,128)(2,1)S(1)} %combine2.4.refs_8_), channel_id=1, source_target_pairs={{0,16},{4,20},{8,24},{12,28},{16,0},{20,4},{24,8},{28,12},{1,17},{... | collective-permute-start | bytes 393224 | tf_op jit(solution)/shard_map/ppermute | solution.py:443
  50.3 6.6 %collective-permute-start.11 = (bf16[16,32,128]{2,1,0:T(8,128)(2,1)S(1)}, bf16[16,32,128]{2,1,0:T(8,128)(2,1)S(1)}, u32[]{:S(2)}, u32[]{:S(2)}) collective-permute-start(bf16[16,32,128]{2,1,0:T(8,128)(2,1)S(1)} %combine1.4.refs_7_), channel_id=1, source_target_pairs={{0,8},{4,12},{8,0},{12,4},{16,24},{20,28},{24,16},{28,20},{1,9},{5... | collective-permute-start | bytes 393224 | tf_op jit(solution)/shard_map/ppermute | solution.py:443
  57.6 8.8 %collective-permute-start.14 = (bf16[16,32,128]{2,1,0:T(8,128)(2,1)S(1)}, bf16[16,32,128]{2,1,0:T(8,128)(2,1)S(1)}, u32[]{:S(2)}, u32[]{:S(2)}) collective-permute-start(bf16[16,32,128]{2,1,0:T(8,128)(2,1)S(1)} %get-tuple-element.71.field_ref), channel_id=1, source_target_pairs={{0,2},{1,3},{2,0},{3,1},{4,6},{5,7},{6,4},{7,5},{8,10},{9,11},{10,... | collective-permute-start | bytes 393224 | tf_op jit(solution)/shard_map/ppermute | solution.py:91
  60.4 6.5 %collective-permute-start.16 = (bf16[16,32,128]{2,1,0:T(8,128)(2,1)S(1)}, bf16[16,32,128]{2,1,0:T(8,128)(2,1)S(1)}, u32[]{:S(2)}, u32[]{:S(2)}) collective-permute-start(bf16[16,32,128]{2,1,0:T(8,128)(2,1)S(1)} %get-tuple-element.71.field_ref), channel_id=1, source_target_pairs={{0,1},{1,0},{2,3},{3,2},{4,5},{5,4},{6,7},{7,6},{8,9},{9,8},{10,11... | collective-permute-start | bytes 393224 | tf_op jit(solution)/shard_map/ppermute | solution.py:92
  66.5 5.0 %collective-permute-start.15 = (bf16[16,32,128]{2,1,0:T(8,128)(2,1)S(1)}, bf16[16,32,128]{2,1,0:T(8,128)(2,1)S(1)}, u32[]{:S(2)}, u32[]{:S(2)}) collective-permute-start(bf16[16,32,128]{2,1,0:T(8,128)(2,1)S(1)} %hold.5.refs_0_), channel_id=1, source_target_pairs={{0,1},{1,0},{2,3},{3,2},{4,5},{5,4},{6,7},{7,6},{8,9},{9,8},{10,11... | collective-permute-start | bytes 393224 | tf_op jit(solution)/shard_map/ppermute | solution.py:419
  71.9 2.0 %collective-permute-start.17 = (bf16[64,32,128]{2,1,0:T(8,128)(2,1)S(1)}, bf16[64,32,128]{2,1,0:T(8,128)(2,1)S(1)}, u32[]{:S(2)}, u32[]{:S(2)}) collective-permute-start(bf16[64,32,128]{2,1,0:T(8,128)(2,1)S(1)} %get-tuple-element.79), channel_id=1, source_target_pairs={{0,4},{4,0},{8,12},{12,8},{16,20},{20,16},{24,28},{28,24},{1,5},{5... | collective-permute-start | bytes 1572872 | tf_op jit(solution)/shard_map/ppermute | solution.py:424
  73.9 7.1 %collective-permute-start.20 = (bf16[16,32,128]{2,1,0:T(8,128)(2,1)S(1)}, bf16[16,32,128]{2,1,0:T(8,128)(2,1)S(1)}, u32[]{:S(2)}, u32[]{:S(2)}) collective-permute-start(bf16[16,32,128]{2,1,0:T(8,128)(2,1)S(1)} %combine3.5), channel_id=1, source_target_pairs={{0,24},{4,28},{8,16},{12,20},{16,8},{20,12},{24,0},{28,4},{1,25},{... | collective-permute-start | bytes 393224 | tf_op jit(solution)/shard_map/ppermute | solution.py:443
  75.9 7.3 %collective-permute-start.19 = (bf16[16,32,128]{2,1,0:T(8,128)(2,1)S(1)}, bf16[16,32,128]{2,1,0:T(8,128)(2,1)S(1)}, u32[]{:S(2)}, u32[]{:S(2)}) collective-permute-start(bf16[16,32,128]{2,1,0:T(8,128)(2,1)S(1)} %combine2.5), channel_id=1, source_target_pairs={{0,16},{4,20},{8,24},{12,28},{16,0},{20,4},{24,8},{28,12},{1,17},{... | collective-permute-start | bytes 393224 | tf_op jit(solution)/shard_map/ppermute | solution.py:443
  77.1 6.6 %collective-permute-start.18 = (bf16[16,32,128]{2,1,0:T(8,128)(2,1)S(1)}, bf16[16,32,128]{2,1,0:T(8,128)(2,1)S(1)}, u32[]{:S(2)}, u32[]{:S(2)}) collective-permute-start(bf16[16,32,128]{2,1,0:T(8,128)(2,1)S(1)} %combine1.5), channel_id=1, source_target_pairs={{0,8},{4,12},{8,0},{12,4},{16,24},{20,28},{24,16},{28,20},{1,9},{5... | collective-permute-start | bytes 393224 | tf_op jit(solution)/shard_map/ppermute | solution.py:443

commit v5 on v4

--- a/solution.py
+++ b/solution.py
@@ -11,6 +11,7 @@
 UNROLL = 16
 LANES = 4
 DEPTH = 6
+APPLY_FLOPS = 20_000_000_000
 CORES = 2
 VMEM_LIMIT = 24 * 1024 * 1024
 
@@ -78,18 +79,23 @@
     if groups % 2:
         return [[0], list(range(1, groups))]
     pairs = groups // 2
-    stages = [[0], [pairs], list(range(1, pairs)), list(range(pairs + 1, groups))]
+    stages = [[0], list(range(1, pairs + 1)), list(range(pairs + 1, groups))]
     return [stage for stage in stages if stage]
 
 
-def gather(rounded, groups):
-    def ring(step):
-        return [(c, (c + step) % groups) for c in range(groups)]
-
+def ring(groups, step):
+    return [(c, (c + step) % groups) for c in range(groups)]
+
+
+def gather(whole, rounded, groups):
     if groups % 2:
-        return [rounded] + [lax.ppermute(rounded, "col", ring(step)) for step in range(1, groups)]
-    far = [lax.ppermute(rounded, "col", ring(2 * step)) for step in range(1, groups // 2)]
-    return [rounded] + far + [lax.ppermute(rounded, "col", neighbours(groups))]
+        return {step: [lax.ppermute(whole, "col", ring(groups, step))] for step in range(1, groups)}
+    sets = {
+        step: [lax.ppermute(piece, "col", ring(groups, 2 * step)) for piece in rounded]
+        for step in range(1, groups // 2)
+    }
+    sets[groups // 2] = [lax.ppermute(piece, "col", neighbours(groups)) for piece in rounded]
+    return sets
 
 
 def neighbours(count):
@@ -100,7 +106,8 @@
     pass
 
 
-def start_kernel(precond_hbm, rhs_hbm, high_ref, low_ref, sol_ref, left_ref, rounded_ref, precond_ref, sems):
+def start_kernel(precond_hbm, rhs_hbm, high_ref, low_ref, sol_ref, left_ref, rounded_ref, *refs):
+    part_refs, (precond_ref, sems) = refs[:-2], refs[-2:]
     owned = left_ref.shape[0]
     parts = sems.shape[0] - 1
     each = owned // parts
@@ -119,17 +126,28 @@
             low_ref[p] = low
             value = times_block(left_ref[p], high, low)
             sol_ref[p] = value
-            rounded_ref[p] = value.astype(jnp.bfloat16)
-
-
-def apply_kernel(pieces, high_ref, low_ref, left_ref, sol_ref, base_ref, *refs):
-    piece_refs, (new_ref, new_left_ref, rounded_ref) = refs[:pieces], refs[pieces:]
-    for p in range(sol_ref.shape[0]):
-        received = sum(piece_ref[p].astype(jnp.float32) for piece_ref in piece_refs)
+            rounded = value.astype(jnp.bfloat16)
+            rounded_ref[p] = rounded
+            part_refs[p * len(part_refs) // owned][p % (owned // len(part_refs))] = rounded
+
+
+def apply_kernel(part, earlier, pieces, high_ref, low_ref, left_ref, sol_ref, base_ref, *refs):
+    piece_refs, refs = refs[:pieces], refs[pieces:]
+    earlier_refs, refs = refs[:earlier], refs[earlier:]
+    new_ref, new_left_ref, rounded_ref = refs[:3]
+    each = rounded_ref.shape[0]
+    for whole_ref in refs[3:]:
+        for index, done_ref in enumerate(earlier_refs):
+            whole_ref[pl.ds(index * each, each)] = done_ref[...]
+    for inner in range(each):
+        p = part * each + inner
+        received = sum(piece_ref[inner].astype(jnp.float32) for piece_ref in piece_refs)
         value = sol_ref[p] + times_block(base_ref[p] - received, high_ref[p], low_ref[p])
         new_ref[p] = value
         new_left_ref[p] = left_ref[p] - received
-        rounded_ref[p] = value.astype(jnp.bfloat16)
+        rounded_ref[inner] = value.astype(jnp.bfloat16)
+        for whole_ref in refs[3:]:
+            whole_ref[p] = value.astype(jnp.bfloat16)
 
 
 def finish_kernel(pieces, high_ref, low_ref, sol_ref, base_ref, *refs):
@@ -232,13 +250,14 @@
 def join(pieces, field):
     if len(pieces) == 1:
         return pieces[0]
-    each = pieces[0].shape[0]
-    for index, piece in enumerate(pieces):
-        field[pl.ds(index * each, each)] = piece[...]
+    at = 0
+    for piece in pieces:
+        field[pl.ds(at, piece.shape[0])] = piece[...]
+        at += piece.shape[0]
     return field
 
 
-def first_kernel(steps, chips, bits, list_ref, total_ref, values_ref, field_ref, *refs):
+def first_kernel(steps, parts, chips, bits, list_ref, total_ref, values_ref, field_ref, *refs):
     out_refs, refs = refs[:steps], refs[steps:]
     in_refs, refs = refs[:steps], refs[steps:]
     sent_refs, totals, token_ref = refs[:-CORES - 1], refs[-CORES - 1:-1], refs[-1]
@@ -253,12 +272,15 @@
             total[pl.ds(0, rows)] = -sum(out_ref[...].astype(jnp.float32) for out_ref in out_refs)
         else:
             for shift in range(chips):
-                at = pl.ds(partner(chip, shift, chips) * owned, owned)
-                value = sum(in_ref[at].astype(jnp.float32) for in_ref in in_refs)
-                if shift > 0:
-                    for step in range(steps):
-                        value -= sent_refs[step * (chips - 1) + shift - 1][...].astype(jnp.float32)
-                total[at] = value
+                for part in range(parts):
+                    each = owned // parts
+                    at = pl.ds(partner(chip, shift, chips) * owned + part * each, each)
+                    value = sum(in_ref[at].astype(jnp.float32) for in_ref in in_refs)
+                    if shift > 0:
+                        for step in range(steps):
+                            sent_ref = sent_refs[(step * parts + part) * (chips - 1) + shift - 1]
+                            value -= sent_ref[...].astype(jnp.float32)
+                    total[at] = value
         add_products(half, bits, list_ref, total_ref, values_ref, field_ref, total)
 
 
@@ -279,20 +301,21 @@
         out_ref[...] = total[pl.ds(0, out_ref.shape[0])].astype(out_ref.dtype)
 
 
-def chip_rows(shift, chips, own_ref, other_ref, owned):
+def chip_rows(shift, chips, part, parts, own_ref, other_ref):
     chip = lax.axis_index("row") // CORES
-    at = pl.ds(partner(chip, shift, chips) * owned, owned)
+    owned = other_ref.shape[0] // chips
+    each = owned // parts
+    at = pl.ds(partner(chip, shift, chips) * owned + part * each, each)
     return own_ref[at] + other_ref[at].astype(jnp.float32)
 
 
-def combine_kernel(shift, chips, own_ref, other_ref, send_ref):
-    send_ref[...] = chip_rows(
-        shift, chips, own_ref, other_ref, send_ref.shape[0]).astype(send_ref.dtype)
+def combine_kernel(shifts, chips, part, parts, own_ref, other_ref, *send_refs):
+    for shift, send_ref in zip(shifts, send_refs):
+        send_ref[...] = chip_rows(shift, chips, part, parts, own_ref, other_ref).astype(send_ref.dtype)
 
 
 def keep_kernel(chips, own_ref, other_ref, left_ref, sol_ref, base_ref):
-    keep = chip_rows(0, chips, own_ref, other_ref, base_ref.shape[0])
-    base_ref[...] = left_ref[...] - sol_ref[...] - keep
+    base_ref[...] = left_ref[...] - sol_ref[...] - chip_rows(0, chips, 0, 1, own_ref, other_ref)
 
 
 def per_device(block_values, block_rows, block_cols, block_counts, precond, right_side):
@@ -318,16 +341,18 @@
     total_type = jax.ShapeDtypeStruct((half_rows + 1, rhs, size), jnp.float32)
     index_type = pltpu.SMEM(block_rows.shape, jnp.int32)
     token_type = jax.ShapeDtypeStruct((8, 128), jnp.float32)
-    parts = next(count for count in (4, 2, 1) if owned % count == 0)
-
-    high, low, sol, left, rounded = pl.pallas_call(
+    loads = next(count for count in (4, 2, 1) if owned % count == 0)
+    parts = 2 if owned % 2 == 0 else 1
+    part_type = jax.ShapeDtypeStruct((owned // parts, rhs, size), jnp.bfloat16)
+
+    high, low, sol, left, whole, *rounded = pl.pallas_call(
         start_kernel,
-        out_shape=[matrix_type] * 2 + [field_type] * 2 + [rounded_type],
+        out_shape=[matrix_type] * 2 + [field_type] * 2 + [rounded_type] + [part_type] * parts,
         in_specs=[in_hbm()] * 2,
-        out_specs=[in_vmem()] * 5,
+        out_specs=[in_vmem()] * (5 + parts),
         scratch_shapes=[
             pltpu.VMEM((owned, size, size), jnp.float32),
-            pltpu.SemaphoreType.DMA((parts + 1,)),
+            pltpu.SemaphoreType.DMA((loads + 1,)),
         ],
         compiler_params=params(),
         name="start",
@@ -357,11 +382,11 @@
             bytes_accessed=int(slots * share) * 2 * size * size, transcendentals=0)
 
     def field_scratch(pieces):
-        return pltpu.VMEM((len(pieces) * owned, rhs, size), jnp.bfloat16)
+        return pltpu.VMEM((sum(piece.shape[0] for piece in pieces), rhs, size), jnp.bfloat16)
 
     def product_first(field, outs, ins, sent):
         return pl.pallas_call(
-            functools.partial(first_kernel, len(outs), chips, bits),
+            functools.partial(first_kernel, len(outs), parts, chips, bits),
             out_shape=[total_type] * CORES + [token_type],
             in_specs=[in_smem()] * 2 + [in_vmem()] * (2 + len(outs) + len(ins) + len(sent)),
             out_specs=[in_vmem()] * (CORES + 1),
@@ -401,7 +426,7 @@
     def hold(piece, token):
         return pl.pallas_call(
             hold_kernel,
-            out_shape=rounded_type,
+            out_shape=part_type,
             in_specs=[in_vmem()] * 2,
             out_specs=in_vmem(),
             input_output_aliases={0: 0},
@@ -409,39 +434,63 @@
             name="hold",
         )(piece, token)
 
+    shifts = list(reversed(range(1, chips)))
+
+    def combine(part, parts, own, incoming):
+        send_type = jax.ShapeDtypeStruct((owned // parts, rhs, size), jnp.bfloat16)
+        return pl.pallas_call(
+            functools.partial(combine_kernel, shifts, chips, part, parts),
+            out_shape=[send_type] * len(shifts),
+            in_specs=[in_vmem()] * 2,
+            out_specs=[in_vmem()] * len(shifts),
+            compiler_params=params(),
+            name="combine%d" % part,
+        )(own, incoming)
+
+    def apply(part, sol, left, base, pieces, earlier):
+        last = part == parts - 1
+        return pl.pallas_call(
+            functools.partial(apply_kernel, part, len(earlier), len(pieces)),
+            out_shape=[field_type, field_type, part_type] + [rounded_type] * last,
+            in_specs=[in_vmem()] * (5 + len(pieces) + len(earlier)),
+            out_specs=[in_vmem()] * (3 + last),
+            input_output_aliases={2: 1, 3: 0},
+            compiler_params=params(),
+            cost_estimate=pl.CostEstimate(flops=APPLY_FLOPS, bytes_accessed=0, transcendentals=0),
+            name="apply%d" % part,
+        )(high, low, left, sol, base, *pieces, *earlier)
+
     outs, ins, sent = [], [], []
     for step in range(ITERS):
-        fields = gather(rounded, groups)
-        *totals, token = product_first(rounded, outs, ins, sent)
+        sets = gather(whole, rounded, groups)
+        *totals, token = product_first(whole, outs, ins, sent)
         if groups % 2 == 0:
             for index in range(1, groups // 2):
-                fields[index] = hold(fields[index], token)
-                fields.append(lax.ppermute(fields[index], "col", neighbours(groups)))
+                sets[index] = [hold(piece, token) for piece in sets[index]]
+                sets[groups // 2 + index] = [lax.ppermute(piece, "col", neighbours(groups)) for piece in sets[index]]
+
+        def stage_pieces(stage):
+            return [piece for index in stages[stage] for piece in sets[index]]
+
         for stage in range(1, final):
-            totals = product_stage(stage, [fields[piece] for piece in stages[stage]], totals)
-        tail = [fields[piece] for piece in stages[final]]
-        outgoing = product_last(0, tail, totals[0])
+            totals = product_stage(stage, stage_pieces(stage), totals)
+        outgoing = product_last(0, stage_pieces(final), totals[0])
         incoming = lax.ppermute(outgoing, "row", neighbours(row_devices))
-        own = product_last(1, tail, totals[1])
+        own = product_last(1, stage_pieces(final), totals[1])
         outs.append(outgoing)
         ins.append(incoming)
-        sends = {}
-        pieces = []
-        for shift in range(1, chips):
-            pairs = [
-                (chip * CORES + core, partner(chip, shift, chips) * CORES + core)
-                for chip in range(chips) for core in range(CORES)
-            ]
-            sends[shift] = pl.pallas_call(
-                functools.partial(combine_kernel, shift, chips),
-                out_shape=rounded_type,
-                in_specs=[in_vmem()] * 2,
-                out_specs=in_vmem(),
-                compiler_params=params(),
-                name="combine%d" % shift,
-            )(own, incoming)
-            pieces.append(lax.ppermute(sends[shift], "row", pairs))
-        sent += [sends[shift] for shift in range(1, chips)]
+        parts_now = parts if step < ITERS - 1 else 1
+        received = []
+        for part in range(parts_now):
+            sends = combine(part, parts_now, own, incoming)
+            sent += reversed(sends)
+            received.append([
+                lax.ppermute(send, "row", [
+                    (chip * CORES + core, partner(chip, shift, chips) * CORES + core)
+                    for chip in range(chips) for core in range(CORES)
+                ])
+                for shift, send in zip(shifts, sends)
+            ])
         base = pl.pallas_call(
             functools.partial(keep_kernel, chips),
             out_shape=field_type,
@@ -451,14 +500,12 @@
             name="keep",
         )(own, incoming, left, sol)
         if step < ITERS - 1:
-            sol, left, rounded = pl.pallas_call(
-                functools.partial(apply_kernel, len(pieces)),
-                out_shape=[field_type, field_type, rounded_type],
-                in_specs=[in_vmem()] * (5 + len(pieces)),
-                out_specs=[in_vmem()] * 3,
-                compiler_params=params(),
-                name="apply",
-            )(high, low, left, sol, base, *pieces)
+            rounded = []
+            for part in range(parts):
+                sol, left, new, *rest = apply(part, sol, left, base, received[part], rounded if part == parts - 1 else [])
+                rounded.append(new)
+            whole, = rest
+    pieces = received[0]
     return pl.pallas_call(
         functools.partial(finish_kernel, len(pieces)),
         out_shape=field_type,

time: 85.9 us -> 85.5 us (level)
  waiting for transfers between devices: 36.4 us -> 16.3 us
  starting transfers between devices: 28.1 us -> 42.5 us
  Pallas kernels: 19.7 us -> 25.4 us
    ppermute x18 -> x33, waiting for transfers between devices: 32 us -> 13 us  [the longest x15 8.93 us: per_device(): lax.ppermute(send, 'row', [(chip * CORES + core, partner(chip, shift, chi...]
    ppermute x18 -> x33, starting transfers between devices: 27.9 us -> 42.3 us  [the longest x15 19.2 us: per_device(): lax.ppermute(send, 'row', [(chip * CORES + core, partner(chip, shift, chi...]
    pallas_call x6, Pallas kernels: 2.54 us -> 4.99 us  [product_last(): pl.pallas_call(functools.partial(last_kernel, final, half, bits, len(piec...]
    pallas_call x17 -> x18, Pallas kernels: 5.88 us -> 7.24 us  [the longest x3 5.4 us: product_first(): pl.pallas_call(functools.partial(first_kernel, len(outs), parts, chips, b...]
    pallas_call x6 -> x3, Pallas kernels: 4.72 us -> 5.95 us  [product_stage(): pl.pallas_call(functools.partial(stage_kernel, stage, bits, len(pieces)),...]
    ppermute x3, waiting for transfers between devices: 4.48 us -> 3.28 us  [per_device(): incoming = lax.ppermute(outgoing, 'row', neighbours(row_devices))]
  transfers between devices with their start and end apart: 21 -> 36, of which waited for: 17 -> 18; matrix products, arithmetic and copies ran while one was open for 0% -> 0% of each run, Pallas kernels for 16% -> 22%
where the time goes in v5:
time: 85.5 us; the launch traced here: 85 us
  starting transfers between devices  42.5 us (50%)
  Pallas kernels  25.4 us (30%)
  waiting for transfers between devices  16.3 us (19%)
  between operations  0.86 us (1%)
    ppermute x15, starting transfers between devices, per_device(): lax.ppermute(send, 'row', [(chip * CORES + core, partner(chip, shift, chi...  19.2 us
    ppermute x6, starting transfers between devices, gather(): lax.ppermute(piece, 'col', ring(groups, 2 * step))  11.6 us
    ppermute x15, waiting for transfers between devices, per_device(): lax.ppermute(send, 'row', [(chip * CORES + core, partner(chip, shift, chi...  8.93 us
    ppermute x6, starting transfers between devices, gather(): lax.ppermute(piece, 'col', neighbours(groups))  6.08 us
    pallas_call x3, Pallas kernels, product_stage(): pl.pallas_call(functools.partial(stage_kernel, stage, bits, len(pieces)),...  5.95 us
    ppermute x6, starting transfers between devices, per_device(): lax.ppermute(piece, 'col', neighbours(groups))  5.41 us
    pallas_call x3, Pallas kernels, product_first(): pl.pallas_call(functools.partial(first_kernel, len(outs), parts, chips, b...  5.4 us
    pallas_call x6, Pallas kernels, product_last(): pl.pallas_call(functools.partial(last_kernel, final, half, bits, len(piec...  4.99 us
  transfers between devices with their start and end apart: 36, of which 18 were waited for; matrix products, arithmetic and copies ran while one was open for 0% of the time, Pallas kernels for 22%

profile of v5, /device:TPU:0, one launch (start us, length us, event | category | flops | bytes accessed | tf_op | source)
XLA Modules:
  0.0 85.0 jit_solution(14464265480473735356)
XLA Ops:
  0.0 2.2 %start.1 = (bf16[16,128,128]{2,1,0:T(8,128)(2,1)S(1)}, bf16[16,128,128]{2,1,0:T(8,128)(2,1)S(1)}, f32[16,32,128]{2,1,0:T(8,128)S(1)}, f32[16,32,128]{2,1,0:T(8,1...) custom-call(f32[16,128,128]{2,1,0:T(8,128)} %bitcast.5, ...), custom_call_target="tpu_custom_call" | custom-call | tf_op jit(solution)/shard_map/start/pallas_call | solution.py:348
  2.2 4.1 %collective-permute-start = (bf16[8,32,128]{2,1,0:T(8,128)(2,1)S(1)}, bf16[8,32,128]{2,1,0:T(8,128)(2,1)S(1)}, u32[]{:S(2)}, u32[]{:S(2)}) collective-permute-start(bf16[8,32,128]{2,1,0:T(8,128)(2,1)S(1)} %get-tuple-element.69), channel_id=1, source_target_pairs={{0,2},{1,3},{2,0},{3,1},{4,6},{5,7},{6,4},{7,5},{8,10},{9,11},{10,... | collective-permute-start | bytes 196616 | tf_op jit(solution)/shard_map/ppermute | solution.py:94
  6.3 1.8 %collective-permute-start.4 = (bf16[8,32,128]{2,1,0:T(8,128)(2,1)S(1)}, bf16[8,32,128]{2,1,0:T(8,128)(2,1)S(1)}, u32[]{:S(2)}, u32[]{:S(2)}) collective-permute-start(bf16[8,32,128]{2,1,0:T(8,128)(2,1)S(1)} %get-tuple-element.69), channel_id=1, source_target_pairs={{0,1},{1,0},{2,3},{3,2},{4,5},{5,4},{6,7},{7,6},{8,9},{9,8},{10,11... | collective-permute-start | bytes 196616 | tf_op jit(solution)/shard_map/ppermute | solution.py:97
  9.0 3.4 %order.1 = (s32[7,208]{1,0:T(8,128)S(4)}, s32[6]{0:T(128)S(4)}, bf16[192,128,128]{2,1,0:T(8,128)(2,1)S(1)}) custom-call(s32[1,1]{1,0:T(1,128)S(6)} %copy.59.count_ref, s32[1,1,192]{2,1,0:T(1,128)} %rows_hbm.1, s32[1,1,192]{2,1,0:T(1,128)} %cols_hbm.1, bf16[192,128,128]{2,1,0:T(8,128)(2,1)} %bitcast.4), custom_call_target="tpu_custom_call" | custom-call | tf_op jit(solution)/shard_map/order/pallas_call | solution.py:361
  12.5 1.7 %stage0.3 = (f32[65,32,128]{2,1,0:T(8,128)S(1)}, f32[65,32,128]{2,1,0:T(8,128)S(1)}, f32[8,128]{1,0:T(8,128)S(1)}) custom-call(s32[7,208]{1,0:T(8,128)S(4)} %get-tuple-element.66.list_ref, s32[6]{0:T(128)S(4)} %get-tuple-element.67.total_ref, bf16[192,128,128]{2,1,0:T(8,128)(2,1)S(1)} %get-tuple-element.68.values_ref, ...), custom_call_target="tpu_custom_call" | custom-call | flops 50331648 | bytes 1572864 | tf_op jit(solution)/shard_map/stage0/pallas_call | solution.py:388
  14.8 1.5 %collective-permute-start.3 = (bf16[8,32,128]{2,1,0:T(8,128)(2,1)S(1)}, bf16[8,32,128]{2,1,0:T(8,128)(2,1)S(1)}, u32[]{:S(2)}, u32[]{:S(2)}) collective-permute-start(bf16[8,32,128]{2,1,0:T(8,128)(2,1)S(1)} %hold.7.refs_1_), channel_id=1, source_target_pairs={{0,1},{1,0},{2,3},{3,2},{4,5},{5,4},{6,7},{7,6},{8,9},{9,8},{10,11... | collective-permute-start | bytes 196616 | tf_op jit(solution)/shard_map/ppermute | solution.py:470
  16.3 2.0 %stage1.3 = (f32[65,32,128]{2,1,0:T(8,128)S(1)}, f32[65,32,128]{2,1,0:T(8,128)S(1)}) custom-call(s32[7,208]{1,0:T(8,128)S(4)} %get-tuple-element.66.list_ref, s32[6]{0:T(128)S(4)} %get-tuple-element.67.total_ref, bf16[192,128,128]{2,1,0:T(8,128)(2,1)S(1)} %get-tuple-element.68.values_ref, ...), custom_call_target="tpu_custom_call", output_to_operand_aliasing={{0}: (7, {}), {1}: (8, {})} | custom-call | flops 201326592 | bytes 6291456 | tf_op jit(solution)/shard_map/stage1/pallas_call | solution.py:400
  21.0 1.1 %collective-permute-done.6.other_ref.refs_1_.refs_2_ = bf16[64,32,128]{2,1,0:T(8,128)(2,1)S(1)} collective-permute-done((bf16[64,32,128]{2,1,0:T(8,128)(2,1)S(1)}, bf16[64,32,128]{2,1,0:T(8,128)(2,1)S(1)}, u32[]{:S(2)}, u32[]{:S(2)}) %collective-permute-start.6) | collective-permute-done | bytes 524320 | tf_op jit(solution)/shard_map/ppermute | solution.py:478
  22.1 3.0 %collective-permute-start.7 = (bf16[8,32,128]{2,1,0:T(8,128)(2,1)S(1)}, bf16[8,32,128]{2,1,0:T(8,128)(2,1)S(1)}, u32[]{:S(2)}, u32[]{:S(2)}) collective-permute-start(bf16[8,32,128]{2,1,0:T(8,128)(2,1)S(1)} %get-tuple-element.78.refs_4_.refs_6_), channel_id=1, source_target_pairs={{0,24},{4,28},{8,16},{12,20},{16,8},{20,12},{24,0},{28,4},{1,25},{... | collective-permute-start | bytes 196616 | tf_op jit(solution)/shard_map/ppermute | solution.py:488
  25.1 1.3 %collective-permute-start.8 = (bf16[8,32,128]{2,1,0:T(8,128)(2,1)S(1)}, bf16[8,32,128]{2,1,0:T(8,128)(2,1)S(1)}, u32[]{:S(2)}, u32[]{:S(2)}) collective-permute-start(bf16[8,32,128]{2,1,0:T(8,128)(2,1)S(1)} %get-tuple-element.79.refs_3_.refs_5_), channel_id=1, source_target_pairs={{0,16},{4,20},{8,24},{12,28},{16,0},{20,4},{24,8},{28,12},{1,17},{... | collective-permute-start | bytes 196616 | tf_op jit(solution)/shard_map/ppermute | solution.py:488
  26.5 2.3 %collective-permute-start.10 = (bf16[8,32,128]{2,1,0:T(8,128)(2,1)S(1)}, bf16[8,32,128]{2,1,0:T(8,128)(2,1)S(1)}, u32[]{:S(2)}, u32[]{:S(2)}) collective-permute-start(bf16[8,32,128]{2,1,0:T(8,128)(2,1)S(1)} %get-tuple-element.83.refs_7_.refs_9_), channel_id=1, source_target_pairs={{0,24},{4,28},{8,16},{12,20},{16,8},{20,12},{24,0},{28,4},{1,25},{... | collective-permute-start | bytes 196616 | tf_op jit(solution)/shard_map/ppermute | solution.py:488
  28.7 1.3 %collective-permute-start.11 = (bf16[8,32,128]{2,1,0:T(8,128)(2,1)S(1)}, bf16[8,32,128]{2,1,0:T(8,128)(2,1)S(1)}, u32[]{:S(2)}, u32[]{:S(2)}) collective-permute-start(bf16[8,32,128]{2,1,0:T(8,128)(2,1)S(1)} %get-tuple-element.84.refs_6_.refs_8_), channel_id=1, source_target_pairs={{0,16},{4,20},{8,24},{12,28},{16,0},{20,4},{24,8},{28,12},{1,17},{... | collective-permute-start | bytes 196616 | tf_op jit(solution)/shard_map/ppermute | solution.py:488
  31.1 2.5 %collective-permute-start.13 = (bf16[8,32,128]{2,1,0:T(8,128)(2,1)S(1)}, bf16[8,32,128]{2,1,0:T(8,128)(2,1)S(1)}, u32[]{:S(2)}, u32[]{:S(2)}) collective-permute-start(bf16[8,32,128]{2,1,0:T(8,128)(2,1)S(1)} %get-tuple-element.86.refs_3_), channel_id=1, source_target_pairs={{0,2},{1,3},{2,0},{3,1},{4,6},{5,7},{6,4},{7,5},{8,10},{9,11},{10,... | collective-permute-start | bytes 196616 | tf_op jit(solution)/shard_map/ppermute | solution.py:94
  34.8 2.0 %collective-permute-start.15 = (bf16[8,32,128]{2,1,0:T(8,128)(2,1)S(1)}, bf16[8,32,128]{2,1,0:T(8,128)(2,1)S(1)}, u32[]{:S(2)}, u32[]{:S(2)}) collective-permute-start(bf16[8,32,128]{2,1,0:T(8,128)(2,1)S(1)} %get-tuple-element.91), channel_id=1, source_target_pairs={{0,2},{1,3},{2,0},{3,1},{4,6},{5,7},{6,4},{7,5},{8,10},{9,11},{10,... | collective-permute-start | bytes 196616 | tf_op jit(solution)/shard_map/ppermute | solution.py:94
  37.5 1.4 %collective-permute-start.17 = (bf16[8,32,128]{2,1,0:T(8,128)(2,1)S(1)}, bf16[8,32,128]{2,1,0:T(8,128)(2,1)S(1)}, u32[]{:S(2)}, u32[]{:S(2)}) collective-permute-start(bf16[8,32,128]{2,1,0:T(8,128)(2,1)S(1)} %get-tuple-element.86.refs_3_), channel_id=1, source_target_pairs={{0,1},{1,0},{2,3},{3,2},{4,5},{5,4},{6,7},{7,6},{8,9},{9,8},{10,11... | collective-permute-start | bytes 196616 | tf_op jit(solution)/shard_map/ppermute | solution.py:97
  38.9 1.7 %stage0.4 = (f32[65,32,128]{2,1,0:T(8,128)S(1)}, f32[65,32,128]{2,1,0:T(8,128)S(1)}, f32[8,128]{1,0:T(8,128)S(1)}) custom-call(s32[7,208]{1,0:T(8,128)S(4)} %get-tuple-element.66.list_ref, s32[6]{0:T(128)S(4)} %get-tuple-element.67.total_ref, bf16[192,128,128]{2,1,0:T(8,128)(2,1)S(1)} %get-tuple-element.68.values_ref, ...), custom_call_target="tpu_custom_call" | custom-call | flops 50331648 | bytes 1572864 | tf_op jit(solution)/shard_map/stage0/pallas_call | solution.py:388
  40.8 1.9 %collective-permute-start.16 = (bf16[8,32,128]{2,1,0:T(8,128)(2,1)S(1)}, bf16[8,32,128]{2,1,0:T(8,128)(2,1)S(1)}, u32[]{:S(2)}, u32[]{:S(2)}) collective-permute-start(bf16[8,32,128]{2,1,0:T(8,128)(2,1)S(1)} %hold.9.refs_1_), channel_id=1, source_target_pairs={{0,1},{1,0},{2,3},{3,2},{4,5},{5,4},{6,7},{7,6},{8,9},{9,8},{10,11... | collective-permute-start | bytes 196616 | tf_op jit(solution)/shard_map/ppermute | solution.py:470
  43.2 2.0 %stage1.4 = (f32[65,32,128]{2,1,0:T(8,128)S(1)}, f32[65,32,128]{2,1,0:T(8,128)S(1)}) custom-call(s32[7,208]{1,0:T(8,128)S(4)} %get-tuple-element.66.list_ref, s32[6]{0:T(128)S(4)} %get-tuple-element.67.total_ref, bf16[192,128,128]{2,1,0:T(8,128)(2,1)S(1)} %get-tuple-element.68.values_ref, ...), custom_call_target="tpu_custom_call", output_to_operand_aliasing={{0}: (7, {}), {1}: (8, {})} | custom-call | flops 201326592 | bytes 6291456 | tf_op jit(solution)/shard_map/stage1/pallas_call | solution.py:400
  48.6 2.1 %collective-permute-start.20 = (bf16[8,32,128]{2,1,0:T(8,128)(2,1)S(1)}, bf16[8,32,128]{2,1,0:T(8,128)(2,1)S(1)}, u32[]{:S(2)}, u32[]{:S(2)}) collective-permute-start(bf16[8,32,128]{2,1,0:T(8,128)(2,1)S(1)} %get-tuple-element.97.refs_12_), channel_id=1, source_target_pairs={{0,24},{4,28},{8,16},{12,20},{16,8},{20,12},{24,0},{28,4},{1,25},{... | collective-permute-start | bytes 196616 | tf_op jit(solution)/shard_map/ppermute | solution.py:488
  50.7 1.5 %collective-permute-start.22 = (bf16[8,32,128]{2,1,0:T(8,128)(2,1)S(1)}, bf16[8,32,128]{2,1,0:T(8,128)(2,1)S(1)}, u32[]{:S(2)}, u32[]{:S(2)}) collective-permute-start(bf16[8,32,128]{2,1,0:T(8,128)(2,1)S(1)} %get-tuple-element.99.refs_10_), channel_id=1, source_target_pairs={{0,8},{4,12},{8,0},{12,4},{16,24},{20,28},{24,16},{28,20},{1,9},{5... | collective-permute-start | bytes 196616 | tf_op jit(solution)/shard_map/ppermute | solution.py:488
  52.1 2.1 %collective-permute-start.23 = (bf16[8,32,128]{2,1,0:T(8,128)(2,1)S(1)}, bf16[8,32,128]{2,1,0:T(8,128)(2,1)S(1)}, u32[]{:S(2)}, u32[]{:S(2)}) collective-permute-start(bf16[8,32,128]{2,1,0:T(8,128)(2,1)S(1)} %get-tuple-element.102.refs_15_), channel_id=1, source_target_pairs={{0,24},{4,28},{8,16},{12,20},{16,8},{20,12},{24,0},{28,4},{1,25},{... | collective-permute-start | bytes 196616 | tf_op jit(solution)/shard_map/ppermute | solution.py:488
  54.3 1.5 %collective-permute-start.25 = (bf16[8,32,128]{2,1,0:T(8,128)(2,1)S(1)}, bf16[8,32,128]{2,1,0:T(8,128)(2,1)S(1)}, u32[]{:S(2)}, u32[]{:S(2)}) collective-permute-start(bf16[8,32,128]{2,1,0:T(8,128)(2,1)S(1)} %get-tuple-element.104.refs_13_), channel_id=1, source_target_pairs={{0,8},{4,12},{8,0},{12,4},{16,24},{20,28},{24,16},{28,20},{1,9},{5... | collective-permute-start | bytes 196616 | tf_op jit(solution)/shard_map/ppermute | solution.py:488
  56.3 1.3 %collective-permute-done.23.refs_0_ = bf16[8,32,128]{2,1,0:T(8,128)(2,1)S(1)} collective-permute-done((bf16[8,32,128]{2,1,0:T(8,128)(2,1)S(1)}, bf16[8,32,128]{2,1,0:T(8,128)(2,1)S(1)}, u32[]{:S(2)}, u32[]{:S(2)}) %collective-permute-start.23) | collective-permute-done | bytes 65568 | tf_op jit(solution)/shard_map/ppermute | solution.py:488
  60.0 2.0 %collective-permute-start.26 = (bf16[8,32,128]{2,1,0:T(8,128)(2,1)S(1)}, bf16[8,32,128]{2,1,0:T(8,128)(2,1)S(1)}, u32[]{:S(2)}, u32[]{:S(2)}) collective-permute-start(bf16[8,32,128]{2,1,0:T(8,128)(2,1)S(1)} %get-tuple-element.105.refs_3_), channel_id=1, source_target_pairs={{0,2},{1,3},{2,0},{3,1},{4,6},{5,7},{6,4},{7,5},{8,10},{9,11},{10,... | collective-permute-start | bytes 196616 | tf_op jit(solution)/shard_map/ppermute | solution.py:94
  64.0 1.9 %stage0.5 = (f32[65,32,128]{2,1,0:T(8,128)S(1)}, f32[65,32,128]{2,1,0:T(8,128)S(1)}, f32[8,128]{1,0:T(8,128)S(1)}) custom-call(s32[7,208]{1,0:T(8,128)S(4)} %get-tuple-element.66.list_ref, s32[6]{0:T(128)S(4)} %get-tuple-element.67.total_ref, bf16[192,128,128]{2,1,0:T(8,128)(2,1)S(1)} %get-tuple-element.68.values_ref, ...), custom_call_target="tpu_custom_call" | custom-call | flops 50331648 | bytes 1572864 | tf_op jit(solution)/shard_map/stage0/pallas_call | solution.py:388
  67.1 1.3 %collective-permute-start.27 = (bf16[8,32,128]{2,1,0:T(8,128)(2,1)S(1)}, bf16[8,32,128]{2,1,0:T(8,128)(2,1)S(1)}, u32[]{:S(2)}, u32[]{:S(2)}) collective-permute-start(bf16[8,32,128]{2,1,0:T(8,128)(2,1)S(1)} %hold.10.refs_0_), channel_id=1, source_target_pairs={{0,1},{1,0},{2,3},{3,2},{4,5},{5,4},{6,7},{7,6},{8,9},{9,8},{10,11... | collective-permute-start | bytes 196616 | tf_op jit(solution)/shard_map/ppermute | solution.py:470
  68.9 2.0 %stage1.5 = (f32[65,32,128]{2,1,0:T(8,128)S(1)}, f32[65,32,128]{2,1,0:T(8,128)S(1)}) custom-call(s32[7,208]{1,0:T(8,128)S(4)} %get-tuple-element.66.list_ref, s32[6]{0:T(128)S(4)} %get-tuple-element.67.total_ref, bf16[192,128,128]{2,1,0:T(8,128)(2,1)S(1)} %get-tuple-element.68.values_ref, ...), custom_call_target="tpu_custom_call", output_to_operand_aliasing={{0}: (7, {}), {1}: (8, {})} | custom-call | flops 201326592 | bytes 6291456 | tf_op jit(solution)/shard_map/stage1/pallas_call | solution.py:400
  74.3 1.5 %collective-permute-start.33 = (bf16[16,32,128]{2,1,0:T(8,128)(2,1)S(1)}, bf16[16,32,128]{2,1,0:T(8,128)(2,1)S(1)}, u32[]{:S(2)}, u32[]{:S(2)}) collective-permute-start(bf16[16,32,128]{2,1,0:T(8,128)(2,1)S(1)} %get-tuple-element.116), channel_id=1, source_target_pairs={{0,24},{4,28},{8,16},{12,20},{16,8},{20,12},{24,0},{28,4},{1,25},{... | collective-permute-start | bytes 393224 | tf_op jit(solution)/shard_map/ppermute | solution.py:488
  76.7 1.1 %collective-permute-start.35 = (bf16[16,32,128]{2,1,0:T(8,128)(2,1)S(1)}, bf16[16,32,128]{2,1,0:T(8,128)(2,1)S(1)}, u32[]{:S(2)}, u32[]{:S(2)}) collective-permute-start(bf16[16,32,128]{2,1,0:T(8,128)(2,1)S(1)} %get-tuple-element.118), channel_id=1, source_target_pairs={{0,8},{4,12},{8,0},{12,4},{16,24},{20,28},{24,16},{28,20},{1,9},{5... | collective-permute-start | bytes 393224 | tf_op jit(solution)/shard_map/ppermute | solution.py:488
  77.9 3.7 %collective-permute-done.33.refs_0_ = bf16[16,32,128]{2,1,0:T(8,128)(2,1)S(1)} collective-permute-done((bf16[16,32,128]{2,1,0:T(8,128)(2,1)S(1)}, bf16[16,32,128]{2,1,0:T(8,128)(2,1)S(1)}, u32[]{:S(2)}, u32[]{:S(2)}) %collective-permute-start.33) | collective-permute-done | bytes 131104 | tf_op jit(solution)/shard_map/ppermute | solution.py:488
  81.6 2.0 %collective-permute-done.34.refs_1_ = bf16[16,32,128]{2,1,0:T(8,128)(2,1)S(1)} collective-permute-done((bf16[16,32,128]{2,1,0:T(8,128)(2,1)S(1)}, bf16[16,32,128]{2,1,0:T(8,128)(2,1)S(1)}, u32[]{:S(2)}, u32[]{:S(2)}) %collective-permute-start.34) | collective-permute-done | bytes 131104 | tf_op jit(solution)/shard_map/ppermute | solution.py:488
  83.6 1.4 %finish.1 = f32[16,32,128]{2,1,0:T(8,128)} custom-call(bf16[16,128,128]{2,1,0:T(8,128)(2,1)S(1)} %get-tuple-element.62.high_ref, bf16[16,128,128]{2,1,0:T(8,128)(2,1)S(1)} %get-tuple-element.63.low_ref, f32[16,32,128]{2,1,0:T(8,128)S(1)} %get-tuple-element.106.sol_ref, f32[16,32,128]{2,1,0:T(8,128)S(1)} %keep.5.base_ref, ...), custom_call_target="tpu_custom_call" | custom-call | tf_op jit(solution)/shard_map/finish/pallas_call | solution.py:509
  (73 shorter events, 21.5 us)
Async XLA Ops:
  2.2 12.1 %collective-permute-start = (bf16[8,32,128]{2,1,0:T(8,128)(2,1)S(1)}, bf16[8,32,128]{2,1,0:T(8,128)(2,1)S(1)}, u32[]{:S(2)}, u32[]{:S(2)}) collective-permute-start(bf16[8,32,128]{2,1,0:T(8,128)(2,1)S(1)} %get-tuple-element.69), channel_id=1, source_target_pairs={{0,2},{1,3},{2,0},{3,1},{4,6},{5,7},{6,4},{7,5},{8,10},{9,11},{10,... | collective-permute-start | bytes 196616 | tf_op jit(solution)/shard_map/ppermute | solution.py:94
  6.3 8.6 %collective-permute-start.2 = (bf16[8,32,128]{2,1,0:T(8,128)(2,1)S(1)}, bf16[8,32,128]{2,1,0:T(8,128)(2,1)S(1)}, u32[]{:S(2)}, u32[]{:S(2)}) collective-permute-start(bf16[8,32,128]{2,1,0:T(8,128)(2,1)S(1)} %get-tuple-element.72), channel_id=1, source_target_pairs={{0,2},{1,3},{2,0},{3,1},{4,6},{5,7},{6,4},{7,5},{8,10},{9,11},{10,... | collective-permute-start | bytes 196616 | tf_op jit(solution)/shard_map/ppermute | solution.py:94
  6.3 10.0 %collective-permute-start.4 = (bf16[8,32,128]{2,1,0:T(8,128)(2,1)S(1)}, bf16[8,32,128]{2,1,0:T(8,128)(2,1)S(1)}, u32[]{:S(2)}, u32[]{:S(2)}) collective-permute-start(bf16[8,32,128]{2,1,0:T(8,128)(2,1)S(1)} %get-tuple-element.69), channel_id=1, source_target_pairs={{0,1},{1,0},{2,3},{3,2},{4,5},{5,4},{6,7},{7,6},{8,9},{9,8},{10,11... | collective-permute-start | bytes 196616 | tf_op jit(solution)/shard_map/ppermute | solution.py:97
  8.2 8.2 %collective-permute-start.5 = (bf16[8,32,128]{2,1,0:T(8,128)(2,1)S(1)}, bf16[8,32,128]{2,1,0:T(8,128)(2,1)S(1)}, u32[]{:S(2)}, u32[]{:S(2)}) collective-permute-start(bf16[8,32,128]{2,1,0:T(8,128)(2,1)S(1)} %get-tuple-element.72), channel_id=1, source_target_pairs={{0,1},{1,0},{2,3},{3,2},{4,5},{5,4},{6,7},{7,6},{8,9},{9,8},{10,11... | collective-permute-start | bytes 196616 | tf_op jit(solution)/shard_map/ppermute | solution.py:97
  14.2 4.3 %collective-permute-start.1 = (bf16[8,32,128]{2,1,0:T(8,128)(2,1)S(1)}, bf16[8,32,128]{2,1,0:T(8,128)(2,1)S(1)}, u32[]{:S(2)}, u32[]{:S(2)}) collective-permute-start(bf16[8,32,128]{2,1,0:T(8,128)(2,1)S(1)} %hold.6.refs_0_), channel_id=1, source_target_pairs={{0,1},{1,0},{2,3},{3,2},{4,5},{5,4},{6,7},{7,6},{8,9},{9,8},{10,11... | collective-permute-start | bytes 196616 | tf_op jit(solution)/shard_map/ppermute | solution.py:470
  14.8 4.4 %collective-permute-start.3 = (bf16[8,32,128]{2,1,0:T(8,128)(2,1)S(1)}, bf16[8,32,128]{2,1,0:T(8,128)(2,1)S(1)}, u32[]{:S(2)}, u32[]{:S(2)}) collective-permute-start(bf16[8,32,128]{2,1,0:T(8,128)(2,1)S(1)} %hold.7.refs_1_), channel_id=1, source_target_pairs={{0,1},{1,0},{2,3},{3,2},{4,5},{5,4},{6,7},{7,6},{8,9},{9,8},{10,11... | collective-permute-start | bytes 196616 | tf_op jit(solution)/shard_map/ppermute | solution.py:470
  22.1 7.9 %collective-permute-start.7 = (bf16[8,32,128]{2,1,0:T(8,128)(2,1)S(1)}, bf16[8,32,128]{2,1,0:T(8,128)(2,1)S(1)}, u32[]{:S(2)}, u32[]{:S(2)}) collective-permute-start(bf16[8,32,128]{2,1,0:T(8,128)(2,1)S(1)} %get-tuple-element.78.refs_4_.refs_6_), channel_id=1, source_target_pairs={{0,24},{4,28},{8,16},{12,20},{16,8},{20,12},{24,0},{28,4},{1,25},{... | collective-permute-start | bytes 196616 | tf_op jit(solution)/shard_map/ppermute | solution.py:488
  25.1 5.6 %collective-permute-start.8 = (bf16[8,32,128]{2,1,0:T(8,128)(2,1)S(1)}, bf16[8,32,128]{2,1,0:T(8,128)(2,1)S(1)}, u32[]{:S(2)}, u32[]{:S(2)}) collective-permute-start(bf16[8,32,128]{2,1,0:T(8,128)(2,1)S(1)} %get-tuple-element.79.refs_3_.refs_5_), channel_id=1, source_target_pairs={{0,16},{4,20},{8,24},{12,28},{16,0},{20,4},{24,8},{28,12},{1,17},{... | collective-permute-start | bytes 196616 | tf_op jit(solution)/shard_map/ppermute | solution.py:488
  26.4 4.3 %collective-permute-start.9 = (bf16[8,32,128]{2,1,0:T(8,128)(2,1)S(1)}, bf16[8,32,128]{2,1,0:T(8,128)(2,1)S(1)}, u32[]{:S(2)}, u32[]{:S(2)}) collective-permute-start(bf16[8,32,128]{2,1,0:T(8,128)(2,1)S(1)} %get-tuple-element.80.refs_2_.refs_4_), channel_id=1, source_target_pairs={{0,8},{4,12},{8,0},{12,4},{16,24},{20,28},{24,16},{28,20},{1,9},{5... | collective-permute-start | bytes 196616 | tf_op jit(solution)/shard_map/ppermute | solution.py:488
  26.5 7.1 %collective-permute-start.10 = (bf16[8,32,128]{2,1,0:T(8,128)(2,1)S(1)}, bf16[8,32,128]{2,1,0:T(8,128)(2,1)S(1)}, u32[]{:S(2)}, u32[]{:S(2)}) collective-permute-start(bf16[8,32,128]{2,1,0:T(8,128)(2,1)S(1)} %get-tuple-element.83.refs_7_.refs_9_), channel_id=1, source_target_pairs={{0,24},{4,28},{8,16},{12,20},{16,8},{20,12},{24,0},{28,4},{1,25},{... | collective-permute-start | bytes 196616 | tf_op jit(solution)/shard_map/ppermute | solution.py:488
  28.7 4.9 %collective-permute-start.11 = (bf16[8,32,128]{2,1,0:T(8,128)(2,1)S(1)}, bf16[8,32,128]{2,1,0:T(8,128)(2,1)S(1)}, u32[]{:S(2)}, u32[]{:S(2)}) collective-permute-start(bf16[8,32,128]{2,1,0:T(8,128)(2,1)S(1)} %get-tuple-element.84.refs_6_.refs_8_), channel_id=1, source_target_pairs={{0,16},{4,20},{8,24},{12,28},{16,0},{20,4},{24,8},{28,12},{1,17},{... | collective-permute-start | bytes 196616 | tf_op jit(solution)/shard_map/ppermute | solution.py:488
  30.1 4.3 %collective-permute-start.12 = (bf16[8,32,128]{2,1,0:T(8,128)(2,1)S(1)}, bf16[8,32,128]{2,1,0:T(8,128)(2,1)S(1)}, u32[]{:S(2)}, u32[]{:S(2)}) collective-permute-start(bf16[8,32,128]{2,1,0:T(8,128)(2,1)S(1)} %get-tuple-element.85.refs_5_.refs_7_), channel_id=1, source_target_pairs={{0,8},{4,12},{8,0},{12,4},{16,24},{20,28},{24,16},{28,20},{1,9},{5... | collective-permute-start | bytes 196616 | tf_op jit(solution)/shard_map/ppermute | solution.py:488
  31.1 9.5 %collective-permute-start.13 = (bf16[8,32,128]{2,1,0:T(8,128)(2,1)S(1)}, bf16[8,32,128]{2,1,0:T(8,128)(2,1)S(1)}, u32[]{:S(2)}, u32[]{:S(2)}) collective-permute-start(bf16[8,32,128]{2,1,0:T(8,128)(2,1)S(1)} %get-tuple-element.86.refs_3_), channel_id=1, source_target_pairs={{0,2},{1,3},{2,0},{3,1},{4,6},{5,7},{6,4},{7,5},{8,10},{9,11},{10,... | collective-permute-start | bytes 196616 | tf_op jit(solution)/shard_map/ppermute | solution.py:94
  34.8 6.0 %collective-permute-start.15 = (bf16[8,32,128]{2,1,0:T(8,128)(2,1)S(1)}, bf16[8,32,128]{2,1,0:T(8,128)(2,1)S(1)}, u32[]{:S(2)}, u32[]{:S(2)}) collective-permute-start(bf16[8,32,128]{2,1,0:T(8,128)(2,1)S(1)} %get-tuple-element.91), channel_id=1, source_target_pairs={{0,2},{1,3},{2,0},{3,1},{4,6},{5,7},{6,4},{7,5},{8,10},{9,11},{10,... | collective-permute-start | bytes 196616 | tf_op jit(solution)/shard_map/ppermute | solution.py:94
  36.8 5.9 %collective-permute-start.18 = (bf16[8,32,128]{2,1,0:T(8,128)(2,1)S(1)}, bf16[8,32,128]{2,1,0:T(8,128)(2,1)S(1)}, u32[]{:S(2)}, u32[]{:S(2)}) collective-permute-start(bf16[8,32,128]{2,1,0:T(8,128)(2,1)S(1)} %get-tuple-element.91), channel_id=1, source_target_pairs={{0,1},{1,0},{2,3},{3,2},{4,5},{5,4},{6,7},{7,6},{8,9},{9,8},{10,11... | collective-permute-start | bytes 196616 | tf_op jit(solution)/shard_map/ppermute | solution.py:97
  37.5 5.7 %collective-permute-start.17 = (bf16[8,32,128]{2,1,0:T(8,128)(2,1)S(1)}, bf16[8,32,128]{2,1,0:T(8,128)(2,1)S(1)}, u32[]{:S(2)}, u32[]{:S(2)}) collective-permute-start(bf16[8,32,128]{2,1,0:T(8,128)(2,1)S(1)} %get-tuple-element.86.refs_3_), channel_id=1, source_target_pairs={{0,1},{1,0},{2,3},{3,2},{4,5},{5,4},{6,7},{7,6},{8,9},{9,8},{10,11... | collective-permute-start | bytes 196616 | tf_op jit(solution)/shard_map/ppermute | solution.py:97
  40.6 4.6 %collective-permute-start.14 = (bf16[8,32,128]{2,1,0:T(8,128)(2,1)S(1)}, bf16[8,32,128]{2,1,0:T(8,128)(2,1)S(1)}, u32[]{:S(2)}, u32[]{:S(2)}) collective-permute-start(bf16[8,32,128]{2,1,0:T(8,128)(2,1)S(1)} %hold.8.refs_0_), channel_id=1, source_target_pairs={{0,1},{1,0},{2,3},{3,2},{4,5},{5,4},{6,7},{7,6},{8,9},{9,8},{10,11... | collective-permute-start | bytes 196616 | tf_op jit(solution)/shard_map/ppermute | solution.py:470
  40.8 4.9 %collective-permute-start.16 = (bf16[8,32,128]{2,1,0:T(8,128)(2,1)S(1)}, bf16[8,32,128]{2,1,0:T(8,128)(2,1)S(1)}, u32[]{:S(2)}, u32[]{:S(2)}) collective-permute-start(bf16[8,32,128]{2,1,0:T(8,128)(2,1)S(1)} %hold.9.refs_1_), channel_id=1, source_target_pairs={{0,1},{1,0},{2,3},{3,2},{4,5},{5,4},{6,7},{7,6},{8,9},{9,8},{10,11... | collective-permute-start | bytes 196616 | tf_op jit(solution)/shard_map/ppermute | solution.py:470
  48.6 5.8 %collective-permute-start.20 = (bf16[8,32,128]{2,1,0:T(8,128)(2,1)S(1)}, bf16[8,32,128]{2,1,0:T(8,128)(2,1)S(1)}, u32[]{:S(2)}, u32[]{:S(2)}) collective-permute-start(bf16[8,32,128]{2,1,0:T(8,128)(2,1)S(1)} %get-tuple-element.97.refs_12_), channel_id=1, source_target_pairs={{0,24},{4,28},{8,16},{12,20},{16,8},{20,12},{24,0},{28,4},{1,25},{... | collective-permute-start | bytes 196616 | tf_op jit(solution)/shard_map/ppermute | solution.py:488
  50.6 5.2 %collective-permute-start.21 = (bf16[8,32,128]{2,1,0:T(8,128)(2,1)S(1)}, bf16[8,32,128]{2,1,0:T(8,128)(2,1)S(1)}, u32[]{:S(2)}, u32[]{:S(2)}) collective-permute-start(bf16[8,32,128]{2,1,0:T(8,128)(2,1)S(1)} %get-tuple-element.98.refs_11_), channel_id=1, source_target_pairs={{0,16},{4,20},{8,24},{12,28},{16,0},{20,4},{24,8},{28,12},{1,17},{... | collective-permute-start | bytes 196616 | tf_op jit(solution)/shard_map/ppermute | solution.py:488
  50.7 5.2 %collective-permute-start.22 = (bf16[8,32,128]{2,1,0:T(8,128)(2,1)S(1)}, bf16[8,32,128]{2,1,0:T(8,128)(2,1)S(1)}, u32[]{:S(2)}, u32[]{:S(2)}) collective-permute-start(bf16[8,32,128]{2,1,0:T(8,128)(2,1)S(1)} %get-tuple-element.99.refs_10_), channel_id=1, source_target_pairs={{0,8},{4,12},{8,0},{12,4},{16,24},{20,28},{24,16},{28,20},{1,9},{5... | collective-permute-start | bytes 196616 | tf_op jit(solution)/shard_map/ppermute | solution.py:488
  52.1 5.5 %collective-permute-start.23 = (bf16[8,32,128]{2,1,0:T(8,128)(2,1)S(1)}, bf16[8,32,128]{2,1,0:T(8,128)(2,1)S(1)}, u32[]{:S(2)}, u32[]{:S(2)}) collective-permute-start(bf16[8,32,128]{2,1,0:T(8,128)(2,1)S(1)} %get-tuple-element.102.refs_15_), channel_id=1, source_target_pairs={{0,24},{4,28},{8,16},{12,20},{16,8},{20,12},{24,0},{28,4},{1,25},{... | collective-permute-start | bytes 196616 | tf_op jit(solution)/shard_map/ppermute | solution.py:488
  54.2 4.3 %collective-permute-start.24 = (bf16[8,32,128]{2,1,0:T(8,128)(2,1)S(1)}, bf16[8,32,128]{2,1,0:T(8,128)(2,1)S(1)}, u32[]{:S(2)}, u32[]{:S(2)}) collective-permute-start(bf16[8,32,128]{2,1,0:T(8,128)(2,1)S(1)} %get-tuple-element.103.refs_14_), channel_id=1, source_target_pairs={{0,16},{4,20},{8,24},{12,28},{16,0},{20,4},{24,8},{28,12},{1,17},{... | collective-permute-start | bytes 196616 | tf_op jit(solution)/shard_map/ppermute | solution.py:488
  54.3 4.3 %collective-permute-start.25 = (bf16[8,32,128]{2,1,0:T(8,128)(2,1)S(1)}, bf16[8,32,128]{2,1,0:T(8,128)(2,1)S(1)}, u32[]{:S(2)}, u32[]{:S(2)}) collective-permute-start(bf16[8,32,128]{2,1,0:T(8,128)(2,1)S(1)} %get-tuple-element.104.refs_13_), channel_id=1, source_target_pairs={{0,8},{4,12},{8,0},{12,4},{16,24},{20,28},{24,16},{28,20},{1,9},{5... | collective-permute-start | bytes 196616 | tf_op jit(solution)/shard_map/ppermute | solution.py:488
  59.1 7.4 %collective-permute-start.28 = (bf16[8,32,128]{2,1,0:T(8,128)(2,1)S(1)}, bf16[8,32,128]{2,1,0:T(8,128)(2,1)S(1)}, u32[]{:S(2)}, u32[]{:S(2)}) collective-permute-start(bf16[8,32,128]{2,1,0:T(8,128)(2,1)S(1)} %get-tuple-element.109), channel_id=1, source_target_pairs={{0,2},{1,3},{2,0},{3,1},{4,6},{5,7},{6,4},{7,5},{8,10},{9,11},{10,... | collective-permute-start | bytes 196616 | tf_op jit(solution)/shard_map/ppermute | solution.py:94
  60.0 7.1 %collective-permute-start.26 = (bf16[8,32,128]{2,1,0:T(8,128)(2,1)S(1)}, bf16[8,32,128]{2,1,0:T(8,128)(2,1)S(1)}, u32[]{:S(2)}, u32[]{:S(2)}) collective-permute-start(bf16[8,32,128]{2,1,0:T(8,128)(2,1)S(1)} %get-tuple-element.105.refs_3_), channel_id=1, source_target_pairs={{0,2},{1,3},{2,0},{3,1},{4,6},{5,7},{6,4},{7,5},{8,10},{9,11},{10,... | collective-permute-start | bytes 196616 | tf_op jit(solution)/shard_map/ppermute | solution.py:94
  62.0 6.5 %collective-permute-start.31 = (bf16[8,32,128]{2,1,0:T(8,128)(2,1)S(1)}, bf16[8,32,128]{2,1,0:T(8,128)(2,1)S(1)}, u32[]{:S(2)}, u32[]{:S(2)}) collective-permute-start(bf16[8,32,128]{2,1,0:T(8,128)(2,1)S(1)} %get-tuple-element.109), channel_id=1, source_target_pairs={{0,1},{1,0},{2,3},{3,2},{4,5},{5,4},{6,7},{7,6},{8,9},{9,8},{10,11... | collective-permute-start | bytes 196616 | tf_op jit(solution)/shard_map/ppermute | solution.py:97
  63.1 5.8 %collective-permute-start.30 = (bf16[8,32,128]{2,1,0:T(8,128)(2,1)S(1)}, bf16[8,32,128]{2,1,0:T(8,128)(2,1)S(1)}, u32[]{:S(2)}, u32[]{:S(2)}) collective-permute-start(bf16[8,32,128]{2,1,0:T(8,128)(2,1)S(1)} %get-tuple-element.105.refs_3_), channel_id=1, source_target_pairs={{0,1},{1,0},{2,3},{3,2},{4,5},{5,4},{6,7},{7,6},{8,9},{9,8},{10,11... | collective-permute-start | bytes 196616 | tf_op jit(solution)/shard_map/ppermute | solution.py:97
  66.4 4.5 %collective-permute-start.29 = (bf16[8,32,128]{2,1,0:T(8,128)(2,1)S(1)}, bf16[8,32,128]{2,1,0:T(8,128)(2,1)S(1)}, u32[]{:S(2)}, u32[]{:S(2)}) collective-permute-start(bf16[8,32,128]{2,1,0:T(8,128)(2,1)S(1)} %hold.11.refs_1_), channel_id=1, source_target_pairs={{0,1},{1,0},{2,3},{3,2},{4,5},{5,4},{6,7},{7,6},{8,9},{9,8},{10,11... | collective-permute-start | bytes 196616 | tf_op jit(solution)/shard_map/ppermute | solution.py:470
  74.3 7.3 %collective-permute-start.33 = (bf16[16,32,128]{2,1,0:T(8,128)(2,1)S(1)}, bf16[16,32,128]{2,1,0:T(8,128)(2,1)S(1)}, u32[]{:S(2)}, u32[]{:S(2)}) collective-permute-start(bf16[16,32,128]{2,1,0:T(8,128)(2,1)S(1)} %get-tuple-element.116), channel_id=1, source_target_pairs={{0,24},{4,28},{8,16},{12,20},{16,8},{20,12},{24,0},{28,4},{1,25},{... | collective-permute-start | bytes 393224 | tf_op jit(solution)/shard_map/ppermute | solution.py:488
  75.8 7.8 %collective-permute-start.34 = (bf16[16,32,128]{2,1,0:T(8,128)(2,1)S(1)}, bf16[16,32,128]{2,1,0:T(8,128)(2,1)S(1)}, u32[]{:S(2)}, u32[]{:S(2)}) collective-permute-start(bf16[16,32,128]{2,1,0:T(8,128)(2,1)S(1)} %get-tuple-element.117), channel_id=1, source_target_pairs={{0,16},{4,20},{8,24},{12,28},{16,0},{20,4},{24,8},{28,12},{1,17},{... | collective-permute-start | bytes 393224 | tf_op jit(solution)/shard_map/ppermute | solution.py:488
  76.7 6.9 %collective-permute-start.35 = (bf16[16,32,128]{2,1,0:T(8,128)(2,1)S(1)}, bf16[16,32,128]{2,1,0:T(8,128)(2,1)S(1)}, u32[]{:S(2)}, u32[]{:S(2)}) collective-permute-start(bf16[16,32,128]{2,1,0:T(8,128)(2,1)S(1)} %get-tuple-element.118), channel_id=1, source_target_pairs={{0,8},{4,12},{8,0},{12,4},{16,24},{20,28},{24,16},{28,20},{1,9},{5... | collective-permute-start | bytes 393224 | tf_op jit(solution)/shard_map/ppermute | solution.py:488
  (4 other events, 10.2 us)

commit v6 on v5

--- a/solution.py
+++ b/solution.py
@@ -75,11 +75,19 @@
     return other * (groups // 2) + lax.shift_right_logical(away, 1)
 
 
-def gather_stages(groups):
+def gather_stages(groups, parts):
+    every = range(parts)
+    own = [(0, part) for part in every]
     if groups % 2:
-        return [[0], list(range(1, groups))]
+        return [own, [(index, part) for index in range(1, groups) for part in every]]
     pairs = groups // 2
-    stages = [[0], list(range(1, pairs + 1)), list(range(pairs + 1, groups))]
+    early = range(parts - 1)
+    stages = [
+        own + [(index, part) for part in early for index in range(1, pairs + 1)],
+        [(index, parts - 1) for index in range(1, pairs + 1)]
+        + [(index, part) for part in early for index in range(pairs + 1, groups)],
+        [(index, parts - 1) for index in range(pairs + 1, groups)],
+    ]
     return [stage for stage in stages if stage]
 
 
@@ -87,14 +95,16 @@
     return [(c, (c + step) % groups) for c in range(groups)]
 
 
-def gather(whole, rounded, groups):
-    if groups % 2:
-        return {step: [lax.ppermute(whole, "col", ring(groups, step))] for step in range(1, groups)}
-    sets = {
-        step: [lax.ppermute(piece, "col", ring(groups, 2 * step)) for piece in rounded]
-        for step in range(1, groups // 2)
-    }
-    sets[groups // 2] = [lax.ppermute(piece, "col", neighbours(groups)) for piece in rounded]
+def gather(rounded, groups):
+    sets = {(0, part): piece for part, piece in enumerate(rounded)}
+    for part, piece in enumerate(rounded):
+        if groups % 2:
+            for step in range(1, groups):
+                sets[step, part] = lax.ppermute(piece, "col", ring(groups, step))
+        else:
+            for step in range(1, groups // 2):
+                sets[step, part] = lax.ppermute(piece, "col", ring(groups, 2 * step))
+            sets[groups // 2, part] = lax.ppermute(piece, "col", neighbours(groups))
     return sets
 
 
@@ -106,7 +116,7 @@
     pass
 
 
-def start_kernel(precond_hbm, rhs_hbm, high_ref, low_ref, sol_ref, left_ref, rounded_ref, *refs):
+def start_kernel(precond_hbm, rhs_hbm, high_ref, low_ref, sol_ref, left_ref, *refs):
     part_refs, (precond_ref, sems) = refs[:-2], refs[-2:]
     owned = left_ref.shape[0]
     parts = sems.shape[0] - 1
@@ -126,19 +136,12 @@
             low_ref[p] = low
             value = times_block(left_ref[p], high, low)
             sol_ref[p] = value
-            rounded = value.astype(jnp.bfloat16)
-            rounded_ref[p] = rounded
-            part_refs[p * len(part_refs) // owned][p % (owned // len(part_refs))] = rounded
-
-
-def apply_kernel(part, earlier, pieces, high_ref, low_ref, left_ref, sol_ref, base_ref, *refs):
-    piece_refs, refs = refs[:pieces], refs[pieces:]
-    earlier_refs, refs = refs[:earlier], refs[earlier:]
-    new_ref, new_left_ref, rounded_ref = refs[:3]
+            part_refs[p * len(part_refs) // owned][p % (owned // len(part_refs))] = value.astype(jnp.bfloat16)
+
+
+def apply_kernel(part, pieces, high_ref, low_ref, left_ref, sol_ref, base_ref, *refs):
+    piece_refs, (new_ref, new_left_ref, rounded_ref) = refs[:pieces], refs[pieces:]
     each = rounded_ref.shape[0]
-    for whole_ref in refs[3:]:
-        for index, done_ref in enumerate(earlier_refs):
-            whole_ref[pl.ds(index * each, each)] = done_ref[...]
     for inner in range(each):
         p = part * each + inner
         received = sum(piece_ref[inner].astype(jnp.float32) for piece_ref in piece_refs)
@@ -146,8 +149,6 @@
         new_ref[p] = value
         new_left_ref[p] = left_ref[p] - received
         rounded_ref[inner] = value.astype(jnp.bfloat16)
-        for whole_ref in refs[3:]:
-            whole_ref[p] = value.astype(jnp.bfloat16)
 
 
 def finish_kernel(pieces, high_ref, low_ref, sol_ref, base_ref, *refs):
@@ -167,7 +168,7 @@
         store.wait()
 
 
-def order_kernel(group, owned, groups, stages, bits, count_ref, rows_hbm, cols_hbm, values_hbm,
+def order_kernel(group, owned, groups, parts, stages, bits, count_ref, rows_hbm, cols_hbm, values_hbm,
                  list_out, total_out, values_out, rows_ref, cols_ref, table_ref, total_ref, sems):
     loads = [
         pltpu.make_async_copy(rows_hbm, rows_ref, sems.at[0]),
@@ -180,10 +181,11 @@
     mine = lax.axis_index("col")
     row_bits, col_bits = bits
     lists = len(stages) * CORES
+    each = owned // parts
     trash = (group // CORES) << col_bits
     for index, stage in enumerate(stages):
-        for place, piece in enumerate(stage):
-            table_ref[piece] = ((index * CORES) << col_bits) + place * owned
+        for place, (piece, part) in enumerate(stage):
+            table_ref[piece * parts + part] = ((index * CORES) << col_bits) + place * each
     for index in range(lists + 1):
         total_ref[index] = 0
     for load in loads[:2]:
@@ -197,10 +199,11 @@
             owner, row_inner = halves(halves(rows_ref[0, 0, slot], group)[1], owned)
             source, rest = halves(cols_ref[0, 0, slot], group)
             half = 1 - ((owner & (CORES - 1)) ^ core)
-            first, base = halves(table_ref[relative(mine, source, groups)], 1 << col_bits)
+            part, inner = halves(halves(rest, owned)[1], each)
+            first, base = halves(table_ref[relative(mine, source, groups) * parts + part], 1 << col_bits)
             which = jnp.where(slot < used, first + half, lists)
             row = lax.shift_right_logical(owner, 1) * owned + row_inner
-            col = base + halves(rest, owned)[1]
+            col = base + inner
             entries.append((which, (((slot << row_bits) | row) << col_bits) | col))
         for which, entry in entries:
             at = total_ref[which]
@@ -257,10 +260,12 @@
     return field
 
 
-def first_kernel(steps, parts, chips, bits, list_ref, total_ref, values_ref, field_ref, *refs):
+def first_kernel(pieces, steps, parts, chips, bits, list_ref, total_ref, values_ref, *refs):
+    piece_refs, refs = refs[:pieces], refs[pieces:]
     out_refs, refs = refs[:steps], refs[steps:]
     in_refs, refs = refs[:steps], refs[steps:]
-    sent_refs, totals, token_ref = refs[:-CORES - 1], refs[-CORES - 1:-1], refs[-1]
+    sent_refs, totals, (token_ref, field) = refs[:-CORES - 2], refs[-CORES - 2:-2], refs[-2:]
+    field_ref = join(piece_refs, field)
     token_ref[...] = jnp.zeros_like(token_ref)
     chip = lax.axis_index("row") // CORES
     for half, total in enumerate(totals):
@@ -327,29 +332,28 @@
     half_rows = chips * owned
     slots = block_values.shape[2]
 
-    stages = gather_stages(groups)
+    parts = 2 if owned % 2 == 0 else 1
+    stages = gather_stages(groups, parts)
     final = len(stages) - 1
     lists_total = len(stages) * CORES
-    widest = max(len(stage) for stage in stages) * owned
+    widest = max(len(stage) for stage in stages) * owned // parts
     row_bits, col_bits = bits = half_rows.bit_length(), (widest - 1).bit_length()
     assert (slots - 1).bit_length() + row_bits + col_bits <= 31
     assert slots % LANES == 0
 
     field_type = jax.ShapeDtypeStruct((owned, rhs, size), jnp.float32)
-    rounded_type = jax.ShapeDtypeStruct((owned, rhs, size), jnp.bfloat16)
     matrix_type = jax.ShapeDtypeStruct((owned, size, size), jnp.bfloat16)
     total_type = jax.ShapeDtypeStruct((half_rows + 1, rhs, size), jnp.float32)
     index_type = pltpu.SMEM(block_rows.shape, jnp.int32)
     token_type = jax.ShapeDtypeStruct((8, 128), jnp.float32)
     loads = next(count for count in (4, 2, 1) if owned % count == 0)
-    parts = 2 if owned % 2 == 0 else 1
     part_type = jax.ShapeDtypeStruct((owned // parts, rhs, size), jnp.bfloat16)
 
-    high, low, sol, left, whole, *rounded = pl.pallas_call(
+    high, low, sol, left, *rounded = pl.pallas_call(
         start_kernel,
-        out_shape=[matrix_type] * 2 + [field_type] * 2 + [rounded_type] + [part_type] * parts,
+        out_shape=[matrix_type] * 2 + [field_type] * 2 + [part_type] * parts,
         in_specs=[in_hbm()] * 2,
-        out_specs=[in_vmem()] * (5 + parts),
+        out_specs=[in_vmem()] * (4 + parts),
         scratch_shapes=[
             pltpu.VMEM((owned, size, size), jnp.float32),
             pltpu.SemaphoreType.DMA((loads + 1,)),
@@ -359,7 +363,7 @@
     )(stay_in_hbm(precond[0]), stay_in_hbm(right_side[0]))
 
     *lists, values = pl.pallas_call(
-        functools.partial(order_kernel, group, owned, groups, stages, bits),
+        functools.partial(order_kernel, group, owned, groups, parts, stages, bits),
         out_shape=[
             pltpu.SMEM((lists_total + 1, slots + UNROLL), jnp.int32),
             pltpu.SMEM((lists_total,), jnp.int32),
@@ -369,7 +373,7 @@
         out_specs=[in_smem()] * 2 + [in_vmem()],
         scratch_shapes=[
             index_type, index_type,
-            pltpu.SMEM((groups,), jnp.int32), pltpu.SMEM((lists_total + 1,), jnp.int32),
+            pltpu.SMEM((groups * parts,), jnp.int32), pltpu.SMEM((lists_total + 1,), jnp.int32),
             pltpu.SemaphoreType.DMA((3,)),
         ],
         compiler_params=params(),
@@ -384,16 +388,17 @@
     def field_scratch(pieces):
         return pltpu.VMEM((sum(piece.shape[0] for piece in pieces), rhs, size), jnp.bfloat16)
 
-    def product_first(field, outs, ins, sent):
+    def product_first(pieces, outs, ins, sent):
         return pl.pallas_call(
-            functools.partial(first_kernel, len(outs), parts, chips, bits),
+            functools.partial(first_kernel, len(pieces), len(outs), parts, chips, bits),
             out_shape=[total_type] * CORES + [token_type],
-            in_specs=[in_smem()] * 2 + [in_vmem()] * (2 + len(outs) + len(ins) + len(sent)),
+            in_specs=[in_smem()] * 2 + [in_vmem()] * (1 + len(pieces) + len(outs) + len(ins) + len(sent)),
             out_specs=[in_vmem()] * (CORES + 1),
-            compiler_params=params(),
-            cost_estimate=cost(1 / groups),
+            scratch_shapes=[field_scratch(pieces)],
+            compiler_params=params(),
+            cost_estimate=cost(len(pieces) / groups / parts),
             name="stage0",
-        )(*lists, values, field, *outs, *ins, *sent)
+        )(*lists, values, *pieces, *outs, *ins, *sent)
 
     def product_stage(stage, pieces, totals):
         inputs = 3 + len(pieces)
@@ -405,7 +410,7 @@
             scratch_shapes=[field_scratch(pieces)],
             input_output_aliases={inputs + half: half for half in range(CORES)},
             compiler_params=params(),
-            cost_estimate=cost(len(pieces) / groups),
+            cost_estimate=cost(len(pieces) / groups / parts),
             name="stage%d" % stage,
         )(*lists, values, *pieces, *totals)
 
@@ -419,7 +424,7 @@
             scratch_shapes=[field_scratch(pieces)],
             input_output_aliases={3 + len(pieces): 0},
             compiler_params=params(),
-            cost_estimate=cost(len(pieces) / groups / CORES),
+            cost_estimate=cost(len(pieces) / groups / parts / CORES),
             name="last%d" % half,
         )(*lists, values, *pieces, total)[-1]
 
@@ -447,30 +452,32 @@
             name="combine%d" % part,
         )(own, incoming)
 
-    def apply(part, sol, left, base, pieces, earlier):
-        last = part == parts - 1
+    def apply(part, sol, left, base, pieces):
         return pl.pallas_call(
-            functools.partial(apply_kernel, part, len(earlier), len(pieces)),
-            out_shape=[field_type, field_type, part_type] + [rounded_type] * last,
-            in_specs=[in_vmem()] * (5 + len(pieces) + len(earlier)),
-            out_specs=[in_vmem()] * (3 + last),
+            functools.partial(apply_kernel, part, len(pieces)),
+            out_shape=[field_type, field_type, part_type],
+            in_specs=[in_vmem()] * (5 + len(pieces)),
+            out_specs=[in_vmem()] * 3,
             input_output_aliases={2: 1, 3: 0},
             compiler_params=params(),
             cost_estimate=pl.CostEstimate(flops=APPLY_FLOPS, bytes_accessed=0, transcendentals=0),
             name="apply%d" % part,
-        )(high, low, left, sol, base, *pieces, *earlier)
+        )(high, low, left, sol, base, *pieces)
 
     outs, ins, sent = [], [], []
     for step in range(ITERS):
-        sets = gather(whole, rounded, groups)
-        *totals, token = product_first(whole, outs, ins, sent)
+        sets = gather(rounded, groups)
+
+        def stage_pieces(stage):
+            return [sets[piece] for piece in stages[stage]]
+
+        *totals, token = product_first(stage_pieces(0), outs, ins, sent)
         if groups % 2 == 0:
             for index in range(1, groups // 2):
-                sets[index] = [hold(piece, token) for piece in sets[index]]
-                sets[groups // 2 + index] = [lax.ppermute(piece, "col", neighbours(groups)) for piece in sets[index]]
-
-        def stage_pieces(stage):
-            return [piece for index in stages[stage] for piece in sets[index]]
+                for part in range(parts):
+                    if part == parts - 1:
+                        sets[index, part] = hold(sets[index, part], token)
+                    sets[groups // 2 + index, part] = lax.ppermute(sets[index, part], "col", neighbours(groups))
 
         for stage in range(1, final):
             totals = product_stage(stage, stage_pieces(stage), totals)
@@ -502,9 +509,8 @@
         if step < ITERS - 1:
             rounded = []
             for part in range(parts):
-                sol, left, new, *rest = apply(part, sol, left, base, received[part], rounded if part == parts - 1 else [])
+                sol, left, new = apply(part, sol, left, base, received[part])
                 rounded.append(new)
-            whole, = rest
     pieces = received[0]
     return pl.pallas_call(
         functools.partial(finish_kernel, len(pieces)),

time: 85.5 us -> 86.6 us (1.013)
  waiting for transfers between devices: 16.3 us -> 19.2 us
  Pallas kernels: 25.4 us -> 22.8 us
  starting transfers between devices: 42.5 us -> 43.5 us
    ppermute x18, waiting for transfers between devices: 4.12 us -> 7.99 us  [the longest x6 7.91 us: per_device(): lax.ppermute(sets[index, part], 'col', neighbours(groups))]
    pallas_call x6, Pallas kernels: 4.99 us -> 2.53 us  [product_last(): pl.pallas_call(functools.partial(last_kernel, final, half, bits, len(piec...]
    ppermute x15, waiting for transfers between devices: 8.93 us -> 6.68 us  [per_device(): lax.ppermute(send, 'row', [(chip * CORES + core, partner(chip, shift, chi...]
    ppermute x18, starting transfers between devices: 23.1 us -> 24.7 us  [the longest x6 15.6 us: gather(): sets[step, part] = lax.ppermute(piece, 'col', ring(groups, 2 * step))]
    ppermute x3, waiting for transfers between devices: 3.28 us -> 4.48 us  [per_device(): incoming = lax.ppermute(outgoing, 'row', neighbours(row_devices))]
    pallas_call x3, Pallas kernels: 5.95 us -> 4.77 us  [product_stage(): pl.pallas_call(functools.partial(stage_kernel, stage, bits, len(pieces)),...]
    pallas_call x8, Pallas kernels: 10.5 us -> 11.5 us  [the longest x3 6.63 us: product_first(): pl.pallas_call(functools.partial(first_kernel, len(pieces), len(outs), pa...]
  transfers between devices with their start and end apart: 36 -> 36, of which waited for: 18 -> 13; matrix products, arithmetic and copies ran while one was open for 0% -> 0% of each run, Pallas kernels for 22% -> 21%
where the time goes in v6:
time: 86.6 us; the launch traced here: 86.4 us
  starting transfers between devices  43.5 us (50%)
  Pallas kernels  22.8 us (26%)
  waiting for transfers between devices  19.2 us (22%)
  between operations  0.9 us (1%)
    ppermute x15, starting transfers between devices, per_device(): lax.ppermute(send, 'row', [(chip * CORES + core, partner(chip, shift, chi...  18.6 us
    ppermute x6, starting transfers between devices, gather(): sets[step, part] = lax.ppermute(piece, 'col', ring(groups, 2 * step))  15.6 us
    ppermute x6, waiting for transfers between devices, per_device(): lax.ppermute(sets[index, part], 'col', neighbours(groups))  7.91 us
    ppermute x15, waiting for transfers between devices, per_device(): lax.ppermute(send, 'row', [(chip * CORES + core, partner(chip, shift, chi...  6.68 us
    pallas_call x3, Pallas kernels, product_first(): pl.pallas_call(functools.partial(first_kernel, len(pieces), len(outs), pa...  6.63 us
    ppermute x6, starting transfers between devices, per_device(): lax.ppermute(sets[index, part], 'col', neighbours(groups))  5.75 us
    pallas_call x3, Pallas kernels, product_stage(): pl.pallas_call(functools.partial(stage_kernel, stage, bits, len(pieces)),...  4.77 us
    ppermute x3, waiting for transfers between devices, per_device(): incoming = lax.ppermute(outgoing, 'row', neighbours(row_devices))  4.48 us
  transfers between devices with their start and end apart: 36, of which 13 were waited for; matrix products, arithmetic and copies ran while one was open for 0% of the time, Pallas kernels for 21%

profile of v6, /device:TPU:0, one launch (start us, length us, event | category | flops | bytes accessed | tf_op | source)
XLA Modules:
  0.0 86.4 jit_solution(17177174394050453029)
XLA Ops:
  0.0 2.1 %start.1 = (bf16[16,128,128]{2,1,0:T(8,128)(2,1)S(1)}, bf16[16,128,128]{2,1,0:T(8,128)(2,1)S(1)}, f32[16,32,128]{2,1,0:T(8,128)S(1)}, f32[16,32,128]{2,1,0:T(8,1...) custom-call(f32[16,128,128]{2,1,0:T(8,128)} %bitcast.5, f32[16,32,128]{2,1,0:T(8,128)} %bitcast.6), custom_call_target="tpu_custom_call" | custom-call | tf_op jit(solution)/shard_map/start/pallas_call | solution.py:352
  2.2 4.1 %collective-permute-start.1 = (bf16[8,32,128]{2,1,0:T(8,128)(2,1)S(1)}, bf16[8,32,128]{2,1,0:T(8,128)(2,1)S(1)}, u32[]{:S(2)}, u32[]{:S(2)}) collective-permute-start(bf16[8,32,128]{2,1,0:T(8,128)(2,1)S(1)} %get-tuple-element.67.refs_0_), channel_id=1, source_target_pairs={{0,2},{1,3},{2,0},{3,1},{4,6},{5,7},{6,4},{7,5},{8,10},{9,11},{10,... | collective-permute-start | bytes 196616 | tf_op jit(solution)/shard_map/ppermute | solution.py:106
  6.3 1.6 %collective-permute-start.2 = (bf16[8,32,128]{2,1,0:T(8,128)(2,1)S(1)}, bf16[8,32,128]{2,1,0:T(8,128)(2,1)S(1)}, u32[]{:S(2)}, u32[]{:S(2)}) collective-permute-start(bf16[8,32,128]{2,1,0:T(8,128)(2,1)S(1)} %get-tuple-element.67.refs_0_), channel_id=1, source_target_pairs={{0,1},{1,0},{2,3},{3,2},{4,5},{5,4},{6,7},{7,6},{8,9},{9,8},{10,11... | collective-permute-start | bytes 196616 | tf_op jit(solution)/shard_map/ppermute | solution.py:107
  9.0 3.2 %order.1 = (s32[7,208]{1,0:T(8,128)S(4)}, s32[6]{0:T(128)S(4)}, bf16[192,128,128]{2,1,0:T(8,128)(2,1)S(1)}) custom-call(s32[1,1]{1,0:T(1,128)S(6)} %copy.53.count_ref, s32[1,1,192]{2,1,0:T(1,128)} %rows_hbm.1, s32[1,1,192]{2,1,0:T(1,128)} %cols_hbm.1, bf16[192,128,128]{2,1,0:T(8,128)(2,1)} %bitcast.4), custom_call_target="tpu_custom_call" | custom-call | tf_op jit(solution)/shard_map/order/pallas_call | solution.py:365
  12.3 1.5 %collective-permute-start.5 = (bf16[8,32,128]{2,1,0:T(8,128)(2,1)S(1)}, bf16[8,32,128]{2,1,0:T(8,128)(2,1)S(1)}, u32[]{:S(2)}, u32[]{:S(2)}) collective-permute-start(bf16[8,32,128]{2,1,0:T(8,128)(2,1)S(1)} %collective-permute-done.1.refs_2_), channel_id=1, source_target_pairs={{0,1},{1,0},{2,3},{3,2},{4,5},{5,4},{6,7},{7,6},{8,9},{9,8},{10,11... | collective-permute-start | bytes 196616 | tf_op jit(solution)/shard_map/ppermute | solution.py:480
  13.8 2.1 %stage0.3 = (f32[65,32,128]{2,1,0:T(8,128)S(1)}, f32[65,32,128]{2,1,0:T(8,128)S(1)}, f32[8,128]{1,0:T(8,128)S(1)}) custom-call(s32[7,208]{1,0:T(8,128)S(4)} %get-tuple-element.63.list_ref, s32[6]{0:T(128)S(4)} %get-tuple-element.64.total_ref, bf16[192,128,128]{2,1,0:T(8,128)(2,1)S(1)} %get-tuple-element.65.values_ref, ...), custom_call_target="tpu_custom_call" | custom-call | flops 100663296 | bytes 3145728 | tf_op jit(solution)/shard_map/stage0/pallas_call | solution.py:392
  16.6 1.6 %stage1.3 = (f32[65,32,128]{2,1,0:T(8,128)S(1)}, f32[65,32,128]{2,1,0:T(8,128)S(1)}) custom-call(s32[7,208]{1,0:T(8,128)S(4)} %get-tuple-element.63.list_ref, s32[6]{0:T(128)S(4)} %get-tuple-element.64.total_ref, bf16[192,128,128]{2,1,0:T(8,128)(2,1)S(1)} %get-tuple-element.65.values_ref, ...), custom_call_target="tpu_custom_call", output_to_operand_aliasing={{0}: (6, {}), {1}: (7, {})} | custom-call | flops 75497472 | bytes 2359296 | tf_op jit(solution)/shard_map/stage1/pallas_call | solution.py:405
  18.2 2.1 %collective-permute-done.3.refs_0_ = bf16[8,32,128]{2,1,0:T(8,128)(2,1)S(1)} collective-permute-done((bf16[8,32,128]{2,1,0:T(8,128)(2,1)S(1)}, bf16[8,32,128]{2,1,0:T(8,128)(2,1)S(1)}, u32[]{:S(2)}, u32[]{:S(2)}) %collective-permute-start.3) | collective-permute-done | bytes 65568 | tf_op jit(solution)/shard_map/ppermute | solution.py:480
  21.2 1.5 %collective-permute-done.6.other_ref.refs_5_.refs_6_ = bf16[64,32,128]{2,1,0:T(8,128)(2,1)S(1)} collective-permute-done((bf16[64,32,128]{2,1,0:T(8,128)(2,1)S(1)}, bf16[64,32,128]{2,1,0:T(8,128)(2,1)S(1)}, u32[]{:S(2)}, u32[]{:S(2)}) %collective-permute-start.6) | collective-permute-done | bytes 524320 | tf_op jit(solution)/shard_map/ppermute | solution.py:485
  22.7 3.6 %collective-permute-start.7 = (bf16[8,32,128]{2,1,0:T(8,128)(2,1)S(1)}, bf16[8,32,128]{2,1,0:T(8,128)(2,1)S(1)}, u32[]{:S(2)}, u32[]{:S(2)}) collective-permute-start(bf16[8,32,128]{2,1,0:T(8,128)(2,1)S(1)} %get-tuple-element.74.refs_8_.refs_10_), channel_id=1, source_target_pairs={{0,24},{4,28},{8,16},{12,20},{16,8},{20,12},{24,0},{28,4},{1,25},{... | collective-permute-start | bytes 196616 | tf_op jit(solution)/shard_map/ppermute | solution.py:495
  27.0 2.9 %collective-permute-start.10 = (bf16[8,32,128]{2,1,0:T(8,128)(2,1)S(1)}, bf16[8,32,128]{2,1,0:T(8,128)(2,1)S(1)}, u32[]{:S(2)}, u32[]{:S(2)}) collective-permute-start(bf16[8,32,128]{2,1,0:T(8,128)(2,1)S(1)} %get-tuple-element.79.refs_11_.refs_13_), channel_id=1, source_target_pairs={{0,24},{4,28},{8,16},{12,20},{16,8},{20,12},{24,0},{28,4},{1,25},{... | collective-permute-start | bytes 196616 | tf_op jit(solution)/shard_map/ppermute | solution.py:495
  32.0 3.6 %collective-permute-start.14 = (bf16[8,32,128]{2,1,0:T(8,128)(2,1)S(1)}, bf16[8,32,128]{2,1,0:T(8,128)(2,1)S(1)}, u32[]{:S(2)}, u32[]{:S(2)}) collective-permute-start(bf16[8,32,128]{2,1,0:T(8,128)(2,1)S(1)} %get-tuple-element.85.refs_0_), channel_id=1, source_target_pairs={{0,2},{1,3},{2,0},{3,1},{4,6},{5,7},{6,4},{7,5},{8,10},{9,11},{10,... | collective-permute-start | bytes 196616 | tf_op jit(solution)/shard_map/ppermute | solution.py:106
  36.0 2.1 %collective-permute-start.13 = (bf16[8,32,128]{2,1,0:T(8,128)(2,1)S(1)}, bf16[8,32,128]{2,1,0:T(8,128)(2,1)S(1)}, u32[]{:S(2)}, u32[]{:S(2)}) collective-permute-start(bf16[8,32,128]{2,1,0:T(8,128)(2,1)S(1)} %get-tuple-element.84.refs_1_), channel_id=1, source_target_pairs={{0,2},{1,3},{2,0},{3,1},{4,6},{5,7},{6,4},{7,5},{8,10},{9,11},{10,... | collective-permute-start | bytes 196616 | tf_op jit(solution)/shard_map/ppermute | solution.py:106
  38.9 1.6 %collective-permute-start.18 = (bf16[8,32,128]{2,1,0:T(8,128)(2,1)S(1)}, bf16[8,32,128]{2,1,0:T(8,128)(2,1)S(1)}, u32[]{:S(2)}, u32[]{:S(2)}) collective-permute-start(bf16[8,32,128]{2,1,0:T(8,128)(2,1)S(1)} %collective-permute-done.14.refs_2_), channel_id=1, source_target_pairs={{0,1},{1,0},{2,3},{3,2},{4,5},{5,4},{6,7},{7,6},{8,9},{9,8},{10,11... | collective-permute-start | bytes 196616 | tf_op jit(solution)/shard_map/ppermute | solution.py:480
  40.5 2.2 %stage0.4 = (f32[65,32,128]{2,1,0:T(8,128)S(1)}, f32[65,32,128]{2,1,0:T(8,128)S(1)}, f32[8,128]{1,0:T(8,128)S(1)}) custom-call(s32[7,208]{1,0:T(8,128)S(4)} %get-tuple-element.63.list_ref, s32[6]{0:T(128)S(4)} %get-tuple-element.64.total_ref, bf16[192,128,128]{2,1,0:T(8,128)(2,1)S(1)} %get-tuple-element.65.values_ref, ...), custom_call_target="tpu_custom_call" | custom-call | flops 100663296 | bytes 3145728 | tf_op jit(solution)/shard_map/stage0/pallas_call | solution.py:392
  43.8 1.6 %stage1.4 = (f32[65,32,128]{2,1,0:T(8,128)S(1)}, f32[65,32,128]{2,1,0:T(8,128)S(1)}) custom-call(s32[7,208]{1,0:T(8,128)S(4)} %get-tuple-element.63.list_ref, s32[6]{0:T(128)S(4)} %get-tuple-element.64.total_ref, bf16[192,128,128]{2,1,0:T(8,128)(2,1)S(1)} %get-tuple-element.65.values_ref, ...), custom_call_target="tpu_custom_call", output_to_operand_aliasing={{0}: (6, {}), {1}: (7, {})} | custom-call | flops 75497472 | bytes 2359296 | tf_op jit(solution)/shard_map/stage1/pallas_call | solution.py:405
  45.4 1.6 %collective-permute-done.16.refs_0_ = bf16[8,32,128]{2,1,0:T(8,128)(2,1)S(1)} collective-permute-done((bf16[8,32,128]{2,1,0:T(8,128)(2,1)S(1)}, bf16[8,32,128]{2,1,0:T(8,128)(2,1)S(1)}, u32[]{:S(2)}, u32[]{:S(2)}) %collective-permute-start.16) | collective-permute-done | bytes 65568 | tf_op jit(solution)/shard_map/ppermute | solution.py:480
  47.9 1.5 %collective-permute-done.19.other_ref.refs_7_ = bf16[64,32,128]{2,1,0:T(8,128)(2,1)S(1)} collective-permute-done((bf16[64,32,128]{2,1,0:T(8,128)(2,1)S(1)}, bf16[64,32,128]{2,1,0:T(8,128)(2,1)S(1)}, u32[]{:S(2)}, u32[]{:S(2)}) %collective-permute-start.19) | collective-permute-done | bytes 524320 | tf_op jit(solution)/shard_map/ppermute | solution.py:485
  49.5 2.6 %collective-permute-start.20 = (bf16[8,32,128]{2,1,0:T(8,128)(2,1)S(1)}, bf16[8,32,128]{2,1,0:T(8,128)(2,1)S(1)}, u32[]{:S(2)}, u32[]{:S(2)}) collective-permute-start(bf16[8,32,128]{2,1,0:T(8,128)(2,1)S(1)} %get-tuple-element.92.refs_16_), channel_id=1, source_target_pairs={{0,24},{4,28},{8,16},{12,20},{16,8},{20,12},{24,0},{28,4},{1,25},{... | collective-permute-start | bytes 196616 | tf_op jit(solution)/shard_map/ppermute | solution.py:495
  53.1 2.6 %collective-permute-start.23 = (bf16[8,32,128]{2,1,0:T(8,128)(2,1)S(1)}, bf16[8,32,128]{2,1,0:T(8,128)(2,1)S(1)}, u32[]{:S(2)}, u32[]{:S(2)}) collective-permute-start(bf16[8,32,128]{2,1,0:T(8,128)(2,1)S(1)} %get-tuple-element.97.refs_19_), channel_id=1, source_target_pairs={{0,24},{4,28},{8,16},{12,20},{16,8},{20,12},{24,0},{28,4},{1,25},{... | collective-permute-start | bytes 196616 | tf_op jit(solution)/shard_map/ppermute | solution.py:495
  57.8 3.2 %collective-permute-start.27 = (bf16[8,32,128]{2,1,0:T(8,128)(2,1)S(1)}, bf16[8,32,128]{2,1,0:T(8,128)(2,1)S(1)}, u32[]{:S(2)}, u32[]{:S(2)}) collective-permute-start(bf16[8,32,128]{2,1,0:T(8,128)(2,1)S(1)} %get-tuple-element.102.refs_0_), channel_id=1, source_target_pairs={{0,2},{1,3},{2,0},{3,1},{4,6},{5,7},{6,4},{7,5},{8,10},{9,11},{10,... | collective-permute-start | bytes 196616 | tf_op jit(solution)/shard_map/ppermute | solution.py:106
  61.4 2.3 %collective-permute-start.26 = (bf16[8,32,128]{2,1,0:T(8,128)(2,1)S(1)}, bf16[8,32,128]{2,1,0:T(8,128)(2,1)S(1)}, u32[]{:S(2)}, u32[]{:S(2)}) collective-permute-start(bf16[8,32,128]{2,1,0:T(8,128)(2,1)S(1)} %get-tuple-element.101.refs_1_), channel_id=1, source_target_pairs={{0,2},{1,3},{2,0},{3,1},{4,6},{5,7},{6,4},{7,5},{8,10},{9,11},{10,... | collective-permute-start | bytes 196616 | tf_op jit(solution)/shard_map/ppermute | solution.py:106
  64.0 2.5 %collective-permute-start.31 = (bf16[8,32,128]{2,1,0:T(8,128)(2,1)S(1)}, bf16[8,32,128]{2,1,0:T(8,128)(2,1)S(1)}, u32[]{:S(2)}, u32[]{:S(2)}) collective-permute-start(bf16[8,32,128]{2,1,0:T(8,128)(2,1)S(1)} %collective-permute-done.27.refs_2_), channel_id=1, source_target_pairs={{0,1},{1,0},{2,3},{3,2},{4,5},{5,4},{6,7},{7,6},{8,9},{9,8},{10,11... | collective-permute-start | bytes 196616 | tf_op jit(solution)/shard_map/ppermute | solution.py:480
  66.5 2.3 %stage0.5 = (f32[65,32,128]{2,1,0:T(8,128)S(1)}, f32[65,32,128]{2,1,0:T(8,128)S(1)}, f32[8,128]{1,0:T(8,128)S(1)}) custom-call(s32[7,208]{1,0:T(8,128)S(4)} %get-tuple-element.63.list_ref, s32[6]{0:T(128)S(4)} %get-tuple-element.64.total_ref, bf16[192,128,128]{2,1,0:T(8,128)(2,1)S(1)} %get-tuple-element.65.values_ref, ...), custom_call_target="tpu_custom_call" | custom-call | flops 100663296 | bytes 3145728 | tf_op jit(solution)/shard_map/stage0/pallas_call | solution.py:392
  69.4 1.6 %stage1.5 = (f32[65,32,128]{2,1,0:T(8,128)S(1)}, f32[65,32,128]{2,1,0:T(8,128)S(1)}) custom-call(s32[7,208]{1,0:T(8,128)S(4)} %get-tuple-element.63.list_ref, s32[6]{0:T(128)S(4)} %get-tuple-element.64.total_ref, bf16[192,128,128]{2,1,0:T(8,128)(2,1)S(1)} %get-tuple-element.65.values_ref, ...), custom_call_target="tpu_custom_call", output_to_operand_aliasing={{0}: (6, {}), {1}: (7, {})} | custom-call | flops 75497472 | bytes 2359296 | tf_op jit(solution)/shard_map/stage1/pallas_call | solution.py:405
  71.0 2.2 %collective-permute-done.29.refs_0_ = bf16[8,32,128]{2,1,0:T(8,128)(2,1)S(1)} collective-permute-done((bf16[8,32,128]{2,1,0:T(8,128)(2,1)S(1)}, bf16[8,32,128]{2,1,0:T(8,128)(2,1)S(1)}, u32[]{:S(2)}, u32[]{:S(2)}) %collective-permute-start.29) | collective-permute-done | bytes 65568 | tf_op jit(solution)/shard_map/ppermute | solution.py:480
  74.1 1.5 %collective-permute-done.32.other_ref = bf16[64,32,128]{2,1,0:T(8,128)(2,1)S(1)} collective-permute-done((bf16[64,32,128]{2,1,0:T(8,128)(2,1)S(1)}, bf16[64,32,128]{2,1,0:T(8,128)(2,1)S(1)}, u32[]{:S(2)}, u32[]{:S(2)}) %collective-permute-start.32) | collective-permute-done | bytes 524320 | tf_op jit(solution)/shard_map/ppermute | solution.py:485
  75.7 2.5 %collective-permute-start.33 = (bf16[16,32,128]{2,1,0:T(8,128)(2,1)S(1)}, bf16[16,32,128]{2,1,0:T(8,128)(2,1)S(1)}, u32[]{:S(2)}, u32[]{:S(2)}) collective-permute-start(bf16[16,32,128]{2,1,0:T(8,128)(2,1)S(1)} %get-tuple-element.110), channel_id=1, source_target_pairs={{0,24},{4,28},{8,16},{12,20},{16,8},{20,12},{24,0},{28,4},{1,25},{... | collective-permute-start | bytes 393224 | tf_op jit(solution)/shard_map/ppermute | solution.py:495
  78.2 1.0 %collective-permute-start.35 = (bf16[16,32,128]{2,1,0:T(8,128)(2,1)S(1)}, bf16[16,32,128]{2,1,0:T(8,128)(2,1)S(1)}, u32[]{:S(2)}, u32[]{:S(2)}) collective-permute-start(bf16[16,32,128]{2,1,0:T(8,128)(2,1)S(1)} %get-tuple-element.112), channel_id=1, source_target_pairs={{0,8},{4,12},{8,0},{12,4},{16,24},{20,28},{24,16},{28,20},{1,9},{5... | collective-permute-start | bytes 393224 | tf_op jit(solution)/shard_map/ppermute | solution.py:495
  79.3 3.1 %collective-permute-done.33.refs_0_ = bf16[16,32,128]{2,1,0:T(8,128)(2,1)S(1)} collective-permute-done((bf16[16,32,128]{2,1,0:T(8,128)(2,1)S(1)}, bf16[16,32,128]{2,1,0:T(8,128)(2,1)S(1)}, u32[]{:S(2)}, u32[]{:S(2)}) %collective-permute-start.33) | collective-permute-done | bytes 131104 | tf_op jit(solution)/shard_map/ppermute | solution.py:495
  82.4 2.6 %collective-permute-done.34.refs_1_ = bf16[16,32,128]{2,1,0:T(8,128)(2,1)S(1)} collective-permute-done((bf16[16,32,128]{2,1,0:T(8,128)(2,1)S(1)}, bf16[16,32,128]{2,1,0:T(8,128)(2,1)S(1)}, u32[]{:S(2)}, u32[]{:S(2)}) %collective-permute-start.34) | collective-permute-done | bytes 131104 | tf_op jit(solution)/shard_map/ppermute | solution.py:495
  85.0 1.4 %finish.1 = f32[16,32,128]{2,1,0:T(8,128)} custom-call(bf16[16,128,128]{2,1,0:T(8,128)(2,1)S(1)} %get-tuple-element.59.high_ref, bf16[16,128,128]{2,1,0:T(8,128)(2,1)S(1)} %get-tuple-element.60.low_ref, f32[16,32,128]{2,1,0:T(8,128)S(1)} %get-tuple-element.100.sol_ref, f32[16,32,128]{2,1,0:T(8,128)S(1)} %keep.5.base_ref, ...), custom_call_target="tpu_custom_call" | custom-call | tf_op jit(solution)/shard_map/finish/pallas_call | solution.py:515
  (70 shorter events, 13.6 us)
Async XLA Ops:
  2.2 10.1 %collective-permute-start.1 = (bf16[8,32,128]{2,1,0:T(8,128)(2,1)S(1)}, bf16[8,32,128]{2,1,0:T(8,128)(2,1)S(1)}, u32[]{:S(2)}, u32[]{:S(2)}) collective-permute-start(bf16[8,32,128]{2,1,0:T(8,128)(2,1)S(1)} %get-tuple-element.67.refs_0_), channel_id=1, source_target_pairs={{0,2},{1,3},{2,0},{3,1},{4,6},{5,7},{6,4},{7,5},{8,10},{9,11},{10,... | collective-permute-start | bytes 196616 | tf_op jit(solution)/shard_map/ppermute | solution.py:106
  6.3 7.5 %collective-permute-start.2 = (bf16[8,32,128]{2,1,0:T(8,128)(2,1)S(1)}, bf16[8,32,128]{2,1,0:T(8,128)(2,1)S(1)}, u32[]{:S(2)}, u32[]{:S(2)}) collective-permute-start(bf16[8,32,128]{2,1,0:T(8,128)(2,1)S(1)} %get-tuple-element.67.refs_0_), channel_id=1, source_target_pairs={{0,1},{1,0},{2,3},{3,2},{4,5},{5,4},{6,7},{7,6},{8,9},{9,8},{10,11... | collective-permute-start | bytes 196616 | tf_op jit(solution)/shard_map/ppermute | solution.py:107
  7.8 8.1 %collective-permute-start = (bf16[8,32,128]{2,1,0:T(8,128)(2,1)S(1)}, bf16[8,32,128]{2,1,0:T(8,128)(2,1)S(1)}, u32[]{:S(2)}, u32[]{:S(2)}) collective-permute-start(bf16[8,32,128]{2,1,0:T(8,128)(2,1)S(1)} %get-tuple-element.66.refs_1_), channel_id=1, source_target_pairs={{0,2},{1,3},{2,0},{3,1},{4,6},{5,7},{6,4},{7,5},{8,10},{9,11},{10,... | collective-permute-start | bytes 196616 | tf_op jit(solution)/shard_map/ppermute | solution.py:106
  8.2 7.8 %collective-permute-start.4 = (bf16[8,32,128]{2,1,0:T(8,128)(2,1)S(1)}, bf16[8,32,128]{2,1,0:T(8,128)(2,1)S(1)}, u32[]{:S(2)}, u32[]{:S(2)}) collective-permute-start(bf16[8,32,128]{2,1,0:T(8,128)(2,1)S(1)} %get-tuple-element.66.refs_1_), channel_id=1, source_target_pairs={{0,1},{1,0},{2,3},{3,2},{4,5},{5,4},{6,7},{7,6},{8,9},{9,8},{10,11... | collective-permute-start | bytes 196616 | tf_op jit(solution)/shard_map/ppermute | solution.py:107
  12.3 4.3 %collective-permute-start.5 = (bf16[8,32,128]{2,1,0:T(8,128)(2,1)S(1)}, bf16[8,32,128]{2,1,0:T(8,128)(2,1)S(1)}, u32[]{:S(2)}, u32[]{:S(2)}) collective-permute-start(bf16[8,32,128]{2,1,0:T(8,128)(2,1)S(1)} %collective-permute-done.1.refs_2_), channel_id=1, source_target_pairs={{0,1},{1,0},{2,3},{3,2},{4,5},{5,4},{6,7},{7,6},{8,9},{9,8},{10,11... | collective-permute-start | bytes 196616 | tf_op jit(solution)/shard_map/ppermute | solution.py:480
  15.9 4.3 %collective-permute-start.3 = (bf16[8,32,128]{2,1,0:T(8,128)(2,1)S(1)}, bf16[8,32,128]{2,1,0:T(8,128)(2,1)S(1)}, u32[]{:S(2)}, u32[]{:S(2)}) collective-permute-start(bf16[8,32,128]{2,1,0:T(8,128)(2,1)S(1)} %hold.3.refs_0_), channel_id=1, source_target_pairs={{0,1},{1,0},{2,3},{3,2},{4,5},{5,4},{6,7},{7,6},{8,9},{9,8},{10,11... | collective-permute-start | bytes 196616 | tf_op jit(solution)/shard_map/ppermute | solution.py:480
  22.7 7.3 %collective-permute-start.7 = (bf16[8,32,128]{2,1,0:T(8,128)(2,1)S(1)}, bf16[8,32,128]{2,1,0:T(8,128)(2,1)S(1)}, u32[]{:S(2)}, u32[]{:S(2)}) collective-permute-start(bf16[8,32,128]{2,1,0:T(8,128)(2,1)S(1)} %get-tuple-element.74.refs_8_.refs_10_), channel_id=1, source_target_pairs={{0,24},{4,28},{8,16},{12,20},{16,8},{20,12},{24,0},{28,4},{1,25},{... | collective-permute-start | bytes 196616 | tf_op jit(solution)/shard_map/ppermute | solution.py:495
  26.3 4.4 %collective-permute-start.8 = (bf16[8,32,128]{2,1,0:T(8,128)(2,1)S(1)}, bf16[8,32,128]{2,1,0:T(8,128)(2,1)S(1)}, u32[]{:S(2)}, u32[]{:S(2)}) collective-permute-start(bf16[8,32,128]{2,1,0:T(8,128)(2,1)S(1)} %get-tuple-element.75.refs_7_.refs_9_), channel_id=1, source_target_pairs={{0,16},{4,20},{8,24},{12,28},{16,0},{20,4},{24,8},{28,12},{1,17},{... | collective-permute-start | bytes 196616 | tf_op jit(solution)/shard_map/ppermute | solution.py:495
  26.4 4.8 %collective-permute-start.9 = (bf16[8,32,128]{2,1,0:T(8,128)(2,1)S(1)}, bf16[8,32,128]{2,1,0:T(8,128)(2,1)S(1)}, u32[]{:S(2)}, u32[]{:S(2)}) collective-permute-start(bf16[8,32,128]{2,1,0:T(8,128)(2,1)S(1)} %get-tuple-element.76.refs_6_.refs_8_), channel_id=1, source_target_pairs={{0,8},{4,12},{8,0},{12,4},{16,24},{20,28},{24,16},{28,20},{1,9},{5... | collective-permute-start | bytes 196616 | tf_op jit(solution)/shard_map/ppermute | solution.py:495
  27.0 8.5 %collective-permute-start.10 = (bf16[8,32,128]{2,1,0:T(8,128)(2,1)S(1)}, bf16[8,32,128]{2,1,0:T(8,128)(2,1)S(1)}, u32[]{:S(2)}, u32[]{:S(2)}) collective-permute-start(bf16[8,32,128]{2,1,0:T(8,128)(2,1)S(1)} %get-tuple-element.79.refs_11_.refs_13_), channel_id=1, source_target_pairs={{0,24},{4,28},{8,16},{12,20},{16,8},{20,12},{24,0},{28,4},{1,25},{... | collective-permute-start | bytes 196616 | tf_op jit(solution)/shard_map/ppermute | solution.py:495
  29.9 5.6 %collective-permute-start.11 = (bf16[8,32,128]{2,1,0:T(8,128)(2,1)S(1)}, bf16[8,32,128]{2,1,0:T(8,128)(2,1)S(1)}, u32[]{:S(2)}, u32[]{:S(2)}) collective-permute-start(bf16[8,32,128]{2,1,0:T(8,128)(2,1)S(1)} %get-tuple-element.80.refs_10_.refs_12_), channel_id=1, source_target_pairs={{0,16},{4,20},{8,24},{12,28},{16,0},{20,4},{24,8},{28,12},{1,17},{... | collective-permute-start | bytes 196616 | tf_op jit(solution)/shard_map/ppermute | solution.py:495
  30.0 5.6 %collective-permute-start.12 = (bf16[8,32,128]{2,1,0:T(8,128)(2,1)S(1)}, bf16[8,32,128]{2,1,0:T(8,128)(2,1)S(1)}, u32[]{:S(2)}, u32[]{:S(2)}) collective-permute-start(bf16[8,32,128]{2,1,0:T(8,128)(2,1)S(1)} %get-tuple-element.81.refs_9_.refs_11_), channel_id=1, source_target_pairs={{0,8},{4,12},{8,0},{12,4},{16,24},{20,28},{24,16},{28,20},{1,9},{5... | collective-permute-start | bytes 196616 | tf_op jit(solution)/shard_map/ppermute | solution.py:495
  31.5 9.0 %collective-permute-start.15 = (bf16[8,32,128]{2,1,0:T(8,128)(2,1)S(1)}, bf16[8,32,128]{2,1,0:T(8,128)(2,1)S(1)}, u32[]{:S(2)}, u32[]{:S(2)}) collective-permute-start(bf16[8,32,128]{2,1,0:T(8,128)(2,1)S(1)} %get-tuple-element.85.refs_0_), channel_id=1, source_target_pairs={{0,1},{1,0},{2,3},{3,2},{4,5},{5,4},{6,7},{7,6},{8,9},{9,8},{10,11... | collective-permute-start | bytes 196616 | tf_op jit(solution)/shard_map/ppermute | solution.py:107
  32.0 6.9 %collective-permute-start.14 = (bf16[8,32,128]{2,1,0:T(8,128)(2,1)S(1)}, bf16[8,32,128]{2,1,0:T(8,128)(2,1)S(1)}, u32[]{:S(2)}, u32[]{:S(2)}) collective-permute-start(bf16[8,32,128]{2,1,0:T(8,128)(2,1)S(1)} %get-tuple-element.85.refs_0_), channel_id=1, source_target_pairs={{0,2},{1,3},{2,0},{3,1},{4,6},{5,7},{6,4},{7,5},{8,10},{9,11},{10,... | collective-permute-start | bytes 196616 | tf_op jit(solution)/shard_map/ppermute | solution.py:106
  36.0 6.7 %collective-permute-start.13 = (bf16[8,32,128]{2,1,0:T(8,128)(2,1)S(1)}, bf16[8,32,128]{2,1,0:T(8,128)(2,1)S(1)}, u32[]{:S(2)}, u32[]{:S(2)}) collective-permute-start(bf16[8,32,128]{2,1,0:T(8,128)(2,1)S(1)} %get-tuple-element.84.refs_1_), channel_id=1, source_target_pairs={{0,2},{1,3},{2,0},{3,1},{4,6},{5,7},{6,4},{7,5},{8,10},{9,11},{10,... | collective-permute-start | bytes 196616 | tf_op jit(solution)/shard_map/ppermute | solution.py:106
  38.1 4.7 %collective-permute-start.17 = (bf16[8,32,128]{2,1,0:T(8,128)(2,1)S(1)}, bf16[8,32,128]{2,1,0:T(8,128)(2,1)S(1)}, u32[]{:S(2)}, u32[]{:S(2)}) collective-permute-start(bf16[8,32,128]{2,1,0:T(8,128)(2,1)S(1)} %get-tuple-element.84.refs_1_), channel_id=1, source_target_pairs={{0,1},{1,0},{2,3},{3,2},{4,5},{5,4},{6,7},{7,6},{8,9},{9,8},{10,11... | collective-permute-start | bytes 196616 | tf_op jit(solution)/shard_map/ppermute | solution.py:107
  38.9 4.9 %collective-permute-start.18 = (bf16[8,32,128]{2,1,0:T(8,128)(2,1)S(1)}, bf16[8,32,128]{2,1,0:T(8,128)(2,1)S(1)}, u32[]{:S(2)}, u32[]{:S(2)}) collective-permute-start(bf16[8,32,128]{2,1,0:T(8,128)(2,1)S(1)} %collective-permute-done.14.refs_2_), channel_id=1, source_target_pairs={{0,1},{1,0},{2,3},{3,2},{4,5},{5,4},{6,7},{7,6},{8,9},{9,8},{10,11... | collective-permute-start | bytes 196616 | tf_op jit(solution)/shard_map/ppermute | solution.py:480
  42.7 4.3 %collective-permute-start.16 = (bf16[8,32,128]{2,1,0:T(8,128)(2,1)S(1)}, bf16[8,32,128]{2,1,0:T(8,128)(2,1)S(1)}, u32[]{:S(2)}, u32[]{:S(2)}) collective-permute-start(bf16[8,32,128]{2,1,0:T(8,128)(2,1)S(1)} %hold.4.refs_0_), channel_id=1, source_target_pairs={{0,1},{1,0},{2,3},{3,2},{4,5},{5,4},{6,7},{7,6},{8,9},{9,8},{10,11... | collective-permute-start | bytes 196616 | tf_op jit(solution)/shard_map/ppermute | solution.py:480
  49.5 6.7 %collective-permute-start.20 = (bf16[8,32,128]{2,1,0:T(8,128)(2,1)S(1)}, bf16[8,32,128]{2,1,0:T(8,128)(2,1)S(1)}, u32[]{:S(2)}, u32[]{:S(2)}) collective-permute-start(bf16[8,32,128]{2,1,0:T(8,128)(2,1)S(1)} %get-tuple-element.92.refs_16_), channel_id=1, source_target_pairs={{0,24},{4,28},{8,16},{12,20},{16,8},{20,12},{24,0},{28,4},{1,25},{... | collective-permute-start | bytes 196616 | tf_op jit(solution)/shard_map/ppermute | solution.py:495
  52.1 4.7 %collective-permute-start.21 = (bf16[8,32,128]{2,1,0:T(8,128)(2,1)S(1)}, bf16[8,32,128]{2,1,0:T(8,128)(2,1)S(1)}, u32[]{:S(2)}, u32[]{:S(2)}) collective-permute-start(bf16[8,32,128]{2,1,0:T(8,128)(2,1)S(1)} %get-tuple-element.93.refs_15_), channel_id=1, source_target_pairs={{0,16},{4,20},{8,24},{12,28},{16,0},{20,4},{24,8},{28,12},{1,17},{... | collective-permute-start | bytes 196616 | tf_op jit(solution)/shard_map/ppermute | solution.py:495
  52.5 4.9 %collective-permute-start.22 = (bf16[8,32,128]{2,1,0:T(8,128)(2,1)S(1)}, bf16[8,32,128]{2,1,0:T(8,128)(2,1)S(1)}, u32[]{:S(2)}, u32[]{:S(2)}) collective-permute-start(bf16[8,32,128]{2,1,0:T(8,128)(2,1)S(1)} %get-tuple-element.94.refs_14_), channel_id=1, source_target_pairs={{0,8},{4,12},{8,0},{12,4},{16,24},{20,28},{24,16},{28,20},{1,9},{5... | collective-permute-start | bytes 196616 | tf_op jit(solution)/shard_map/ppermute | solution.py:495
  53.1 7.9 %collective-permute-start.23 = (bf16[8,32,128]{2,1,0:T(8,128)(2,1)S(1)}, bf16[8,32,128]{2,1,0:T(8,128)(2,1)S(1)}, u32[]{:S(2)}, u32[]{:S(2)}) collective-permute-start(bf16[8,32,128]{2,1,0:T(8,128)(2,1)S(1)} %get-tuple-element.97.refs_19_), channel_id=1, source_target_pairs={{0,24},{4,28},{8,16},{12,20},{16,8},{20,12},{24,0},{28,4},{1,25},{... | collective-permute-start | bytes 196616 | tf_op jit(solution)/shard_map/ppermute | solution.py:495
  55.7 5.3 %collective-permute-start.24 = (bf16[8,32,128]{2,1,0:T(8,128)(2,1)S(1)}, bf16[8,32,128]{2,1,0:T(8,128)(2,1)S(1)}, u32[]{:S(2)}, u32[]{:S(2)}) collective-permute-start(bf16[8,32,128]{2,1,0:T(8,128)(2,1)S(1)} %get-tuple-element.98.refs_18_), channel_id=1, source_target_pairs={{0,16},{4,20},{8,24},{12,28},{16,0},{20,4},{24,8},{28,12},{1,17},{... | collective-permute-start | bytes 196616 | tf_op jit(solution)/shard_map/ppermute | solution.py:495
  56.2 4.8 %collective-permute-start.25 = (bf16[8,32,128]{2,1,0:T(8,128)(2,1)S(1)}, bf16[8,32,128]{2,1,0:T(8,128)(2,1)S(1)}, u32[]{:S(2)}, u32[]{:S(2)}) collective-permute-start(bf16[8,32,128]{2,1,0:T(8,128)(2,1)S(1)} %get-tuple-element.99.refs_17_), channel_id=1, source_target_pairs={{0,8},{4,12},{8,0},{12,4},{16,24},{20,28},{24,16},{28,20},{1,9},{5... | collective-permute-start | bytes 196616 | tf_op jit(solution)/shard_map/ppermute | solution.py:495
  57.8 8.7 %collective-permute-start.28 = (bf16[8,32,128]{2,1,0:T(8,128)(2,1)S(1)}, bf16[8,32,128]{2,1,0:T(8,128)(2,1)S(1)}, u32[]{:S(2)}, u32[]{:S(2)}) collective-permute-start(bf16[8,32,128]{2,1,0:T(8,128)(2,1)S(1)} %get-tuple-element.102.refs_0_), channel_id=1, source_target_pairs={{0,1},{1,0},{2,3},{3,2},{4,5},{5,4},{6,7},{7,6},{8,9},{9,8},{10,11... | collective-permute-start | bytes 196616 | tf_op jit(solution)/shard_map/ppermute | solution.py:107
  57.8 6.2 %collective-permute-start.27 = (bf16[8,32,128]{2,1,0:T(8,128)(2,1)S(1)}, bf16[8,32,128]{2,1,0:T(8,128)(2,1)S(1)}, u32[]{:S(2)}, u32[]{:S(2)}) collective-permute-start(bf16[8,32,128]{2,1,0:T(8,128)(2,1)S(1)} %get-tuple-element.102.refs_0_), channel_id=1, source_target_pairs={{0,2},{1,3},{2,0},{3,1},{4,6},{5,7},{6,4},{7,5},{8,10},{9,11},{10,... | collective-permute-start | bytes 196616 | tf_op jit(solution)/shard_map/ppermute | solution.py:106
  61.4 7.4 %collective-permute-start.26 = (bf16[8,32,128]{2,1,0:T(8,128)(2,1)S(1)}, bf16[8,32,128]{2,1,0:T(8,128)(2,1)S(1)}, u32[]{:S(2)}, u32[]{:S(2)}) collective-permute-start(bf16[8,32,128]{2,1,0:T(8,128)(2,1)S(1)} %get-tuple-element.101.refs_1_), channel_id=1, source_target_pairs={{0,2},{1,3},{2,0},{3,1},{4,6},{5,7},{6,4},{7,5},{8,10},{9,11},{10,... | collective-permute-start | bytes 196616 | tf_op jit(solution)/shard_map/ppermute | solution.py:106
  63.6 5.3 %collective-permute-start.30 = (bf16[8,32,128]{2,1,0:T(8,128)(2,1)S(1)}, bf16[8,32,128]{2,1,0:T(8,128)(2,1)S(1)}, u32[]{:S(2)}, u32[]{:S(2)}) collective-permute-start(bf16[8,32,128]{2,1,0:T(8,128)(2,1)S(1)} %get-tuple-element.101.refs_1_), channel_id=1, source_target_pairs={{0,1},{1,0},{2,3},{3,2},{4,5},{5,4},{6,7},{7,6},{8,9},{9,8},{10,11... | collective-permute-start | bytes 196616 | tf_op jit(solution)/shard_map/ppermute | solution.py:107
  64.0 5.4 %collective-permute-start.31 = (bf16[8,32,128]{2,1,0:T(8,128)(2,1)S(1)}, bf16[8,32,128]{2,1,0:T(8,128)(2,1)S(1)}, u32[]{:S(2)}, u32[]{:S(2)}) collective-permute-start(bf16[8,32,128]{2,1,0:T(8,128)(2,1)S(1)} %collective-permute-done.27.refs_2_), channel_id=1, source_target_pairs={{0,1},{1,0},{2,3},{3,2},{4,5},{5,4},{6,7},{7,6},{8,9},{9,8},{10,11... | collective-permute-start | bytes 196616 | tf_op jit(solution)/shard_map/ppermute | solution.py:480
  75.7 6.8 %collective-permute-start.33 = (bf16[16,32,128]{2,1,0:T(8,128)(2,1)S(1)}, bf16[16,32,128]{2,1,0:T(8,128)(2,1)S(1)}, u32[]{:S(2)}, u32[]{:S(2)}) collective-permute-start(bf16[16,32,128]{2,1,0:T(8,128)(2,1)S(1)} %get-tuple-element.110), channel_id=1, source_target_pairs={{0,24},{4,28},{8,16},{12,20},{16,8},{20,12},{24,0},{28,4},{1,25},{... | collective-permute-start | bytes 393224 | tf_op jit(solution)/shard_map/ppermute | solution.py:495
  78.2 6.8 %collective-permute-start.34 = (bf16[16,32,128]{2,1,0:T(8,128)(2,1)S(1)}, bf16[16,32,128]{2,1,0:T(8,128)(2,1)S(1)}, u32[]{:S(2)}, u32[]{:S(2)}) collective-permute-start(bf16[16,32,128]{2,1,0:T(8,128)(2,1)S(1)} %get-tuple-element.111), channel_id=1, source_target_pairs={{0,16},{4,20},{8,24},{12,28},{16,0},{20,4},{24,8},{28,12},{1,17},{... | collective-permute-start | bytes 393224 | tf_op jit(solution)/shard_map/ppermute | solution.py:495
  78.2 6.8 %collective-permute-start.35 = (bf16[16,32,128]{2,1,0:T(8,128)(2,1)S(1)}, bf16[16,32,128]{2,1,0:T(8,128)(2,1)S(1)}, u32[]{:S(2)}, u32[]{:S(2)}) collective-permute-start(bf16[16,32,128]{2,1,0:T(8,128)(2,1)S(1)} %get-tuple-element.112), channel_id=1, source_target_pairs={{0,8},{4,12},{8,0},{12,4},{16,24},{20,28},{24,16},{28,20},{1,9},{5... | collective-permute-start | bytes 393224 | tf_op jit(solution)/shard_map/ppermute | solution.py:495
  (4 other events, 10.3 us)

commit v7 on v6

--- a/solution.py
+++ b/solution.py
@@ -223,6 +223,14 @@
     lax.fori_loop(0, lists, close, 0)
     loads[2].wait()
 
+    def turn(chunk, carry):
+        blocks = [values_out[chunk * LANES + lane] for lane in range(LANES)]
+        for lane, block in enumerate(blocks):
+            values_out[chunk * LANES + lane] = block.T
+        return carry
+
+    lax.fori_loop(0, lax.div(used + LANES - 1, LANES), turn, 0)
+
 
 def add_products(which, bits, list_ref, total_ref, values_ref, field_ref, total):
     row_bits, col_bits = bits
@@ -238,8 +246,7 @@
             col = entry & ((1 << col_bits) - 1)
             row = lax.shift_right_logical(entry, col_bits) & ((1 << row_bits) - 1)
             slot = lax.shift_right_logical(entry, col_bits + row_bits)
-            term = lax.dot_general(
-                field_ref[col], values_ref[slot], NT, preferred_element_type=jnp.float32)
+            term = jnp.dot(field_ref[col], values_ref[slot], preferred_element_type=jnp.float32)
             terms.append((row, term))
             if len(terms) > DEPTH:
                 store(*terms.pop(0))

time: 86.6 us -> 87 us (level)
  waiting for transfers between devices: 19.2 us -> 22.7 us
  Pallas kernels: 22.8 us -> 19.7 us
    ppermute x6, waiting for transfers between devices: 0.02 us -> 4.42 us  [gather(): sets[step, part] = lax.ppermute(piece, 'col', ring(groups, 2 * step))]
    ppermute x6, starting transfers between devices: 15.6 us -> 11.7 us  [gather(): sets[step, part] = lax.ppermute(piece, 'col', ring(groups, 2 * step))]
    pallas_call x3, Pallas kernels: 4.77 us -> 2.38 us  [product_stage(): pl.pallas_call(functools.partial(stage_kernel, stage, bits, len(pieces)),...]
    pallas_call x1, Pallas kernels: 3.24 us -> 5.34 us  [per_device(): pl.pallas_call(functools.partial(order_kernel, group, owned, groups, part...]
    pallas_call x3, Pallas kernels: 6.63 us -> 4.59 us  [product_first(): pl.pallas_call(functools.partial(first_kernel, len(pieces), len(outs), pa...]
    ppermute x15, starting transfers between devices: 18.6 us -> 20.6 us  [per_device(): lax.ppermute(send, 'row', [(chip * CORES + core, partner(chip, shift, chi...]
    ppermute x6, starting transfers between devices: 3.38 us -> 5.21 us  [gather(): sets[groups // 2, part] = lax.ppermute(piece, 'col', neighbours(groups))]
    ppermute x6, waiting for transfers between devices: 7.91 us -> 6.96 us  [per_device(): lax.ppermute(sets[index, part], 'col', neighbours(groups))]
  transfers between devices with their start and end apart: 36 -> 36, of which waited for: 13 -> 15; matrix products, arithmetic and copies ran while one was open for 0% -> 0% of each run, Pallas kernels for 21% -> 17%
where the time goes in v7:
time: 87 us; the launch traced here: 86.9 us
  starting transfers between devices  43.6 us (50%)
  waiting for transfers between devices  22.7 us (26%)
  Pallas kernels  19.7 us (23%)
  between operations  0.87 us (1%)
    ppermute x15, starting transfers between devices, per_device(): lax.ppermute(send, 'row', [(chip * CORES + core, partner(chip, shift, chi...  20.6 us
    ppermute x6, starting transfers between devices, gather(): sets[step, part] = lax.ppermute(piece, 'col', ring(groups, 2 * step))  11.7 us
    ppermute x6, waiting for transfers between devices, per_device(): lax.ppermute(sets[index, part], 'col', neighbours(groups))  6.96 us
    ppermute x15, waiting for transfers between devices, per_device(): lax.ppermute(send, 'row', [(chip * CORES + core, partner(chip, shift, chi...  6.48 us
    ppermute x6, starting transfers between devices, per_device(): lax.ppermute(sets[index, part], 'col', neighbours(groups))  5.95 us
    pallas_call x1, Pallas kernels, per_device(): pl.pallas_call(functools.partial(order_kernel, group, owned, groups, part...  5.34 us
    ppermute x6, starting transfers between devices, gather(): sets[groups // 2, part] = lax.ppermute(piece, 'col', neighbours(groups))  5.21 us
    ppermute x3, waiting for transfers between devices, per_device(): incoming = lax.ppermute(outgoing, 'row', neighbours(row_devices))  4.86 us
  transfers between devices with their start and end apart: 36, of which 15 were waited for; matrix products, arithmetic and copies ran while one was open for 0% of the time, Pallas kernels for 17%

profile of v7, /device:TPU:0, one launch (start us, length us, event | category | flops | bytes accessed | tf_op | source)
XLA Modules:
  0.0 86.9 jit_solution(17089206303664182177)
XLA Ops:
  0.0 2.1 %start.1 = (bf16[16,128,128]{2,1,0:T(8,128)(2,1)S(1)}, bf16[16,128,128]{2,1,0:T(8,128)(2,1)S(1)}, f32[16,32,128]{2,1,0:T(8,128)S(1)}, f32[16,32,128]{2,1,0:T(8,1...) custom-call(f32[16,128,128]{2,1,0:T(8,128)} %bitcast.5, f32[16,32,128]{2,1,0:T(8,128)} %bitcast.6), custom_call_target="tpu_custom_call" | custom-call | tf_op jit(solution)/shard_map/start/pallas_call | solution.py:359
  2.2 4.1 %collective-permute-start.1 = (bf16[8,32,128]{2,1,0:T(8,128)(2,1)S(1)}, bf16[8,32,128]{2,1,0:T(8,128)(2,1)S(1)}, u32[]{:S(2)}, u32[]{:S(2)}) collective-permute-start(bf16[8,32,128]{2,1,0:T(8,128)(2,1)S(1)} %get-tuple-element.67.refs_0_), channel_id=1, source_target_pairs={{0,2},{1,3},{2,0},{3,1},{4,6},{5,7},{6,4},{7,5},{8,10},{9,11},{10,... | collective-permute-start | bytes 196616 | tf_op jit(solution)/shard_map/ppermute | solution.py:106
  6.3 1.6 %collective-permute-start.2 = (bf16[8,32,128]{2,1,0:T(8,128)(2,1)S(1)}, bf16[8,32,128]{2,1,0:T(8,128)(2,1)S(1)}, u32[]{:S(2)}, u32[]{:S(2)}) collective-permute-start(bf16[8,32,128]{2,1,0:T(8,128)(2,1)S(1)} %get-tuple-element.67.refs_0_), channel_id=1, source_target_pairs={{0,1},{1,0},{2,3},{3,2},{4,5},{5,4},{6,7},{7,6},{8,9},{9,8},{10,11... | collective-permute-start | bytes 196616 | tf_op jit(solution)/shard_map/ppermute | solution.py:107
  9.0 5.3 %order.1 = (s32[7,208]{1,0:T(8,128)S(4)}, s32[6]{0:T(128)S(4)}, bf16[192,128,128]{2,1,0:T(8,128)(2,1)S(1)}) custom-call(s32[1,1]{1,0:T(1,128)S(6)} %copy.53.count_ref, s32[1,1,192]{2,1,0:T(1,128)} %rows_hbm.1, s32[1,1,192]{2,1,0:T(1,128)} %cols_hbm.1, bf16[192,128,128]{2,1,0:T(8,128)(2,1)} %bitcast.4), custom_call_target="tpu_custom_call" | custom-call | tf_op jit(solution)/shard_map/order/pallas_call | solution.py:372
  14.4 2.2 %collective-permute-start.5 = (bf16[8,32,128]{2,1,0:T(8,128)(2,1)S(1)}, bf16[8,32,128]{2,1,0:T(8,128)(2,1)S(1)}, u32[]{:S(2)}, u32[]{:S(2)}) collective-permute-start(bf16[8,32,128]{2,1,0:T(8,128)(2,1)S(1)} %collective-permute-done.1.refs_2_), channel_id=1, source_target_pairs={{0,1},{1,0},{2,3},{3,2},{4,5},{5,4},{6,7},{7,6},{8,9},{9,8},{10,11... | collective-permute-start | bytes 196616 | tf_op jit(solution)/shard_map/ppermute | solution.py:487
  16.6 1.4 %stage0.3 = (f32[65,32,128]{2,1,0:T(8,128)S(1)}, f32[65,32,128]{2,1,0:T(8,128)S(1)}, f32[8,128]{1,0:T(8,128)S(1)}) custom-call(s32[7,208]{1,0:T(8,128)S(4)} %get-tuple-element.63.list_ref, s32[6]{0:T(128)S(4)} %get-tuple-element.64.total_ref, bf16[192,128,128]{2,1,0:T(8,128)(2,1)S(1)} %get-tuple-element.65.values_ref, ...), custom_call_target="tpu_custom_call" | custom-call | flops 100663296 | bytes 3145728 | tf_op jit(solution)/shard_map/stage0/pallas_call | solution.py:399
  19.6 2.8 %collective-permute-done.3.refs_0_ = bf16[8,32,128]{2,1,0:T(8,128)(2,1)S(1)} collective-permute-done((bf16[8,32,128]{2,1,0:T(8,128)(2,1)S(1)}, bf16[8,32,128]{2,1,0:T(8,128)(2,1)S(1)}, u32[]{:S(2)}, u32[]{:S(2)}) %collective-permute-start.3) | collective-permute-done | bytes 65568 | tf_op jit(solution)/shard_map/ppermute | solution.py:487
  23.1 1.6 %collective-permute-done.6.other_ref.refs_5_.refs_6_ = bf16[64,32,128]{2,1,0:T(8,128)(2,1)S(1)} collective-permute-done((bf16[64,32,128]{2,1,0:T(8,128)(2,1)S(1)}, bf16[64,32,128]{2,1,0:T(8,128)(2,1)S(1)}, u32[]{:S(2)}, u32[]{:S(2)}) %collective-permute-start.6) | collective-permute-done | bytes 524320 | tf_op jit(solution)/shard_map/ppermute | solution.py:492
  25.1 4.3 %collective-permute-start.8 = (bf16[8,32,128]{2,1,0:T(8,128)(2,1)S(1)}, bf16[8,32,128]{2,1,0:T(8,128)(2,1)S(1)}, u32[]{:S(2)}, u32[]{:S(2)}) collective-permute-start(bf16[8,32,128]{2,1,0:T(8,128)(2,1)S(1)} %get-tuple-element.75.refs_7_.refs_9_), channel_id=1, source_target_pairs={{0,16},{4,20},{8,24},{12,28},{16,0},{20,4},{24,8},{28,12},{1,17},{... | collective-permute-start | bytes 196616 | tf_op jit(solution)/shard_map/ppermute | solution.py:502
  29.4 1.4 %collective-permute-start.9 = (bf16[8,32,128]{2,1,0:T(8,128)(2,1)S(1)}, bf16[8,32,128]{2,1,0:T(8,128)(2,1)S(1)}, u32[]{:S(2)}, u32[]{:S(2)}) collective-permute-start(bf16[8,32,128]{2,1,0:T(8,128)(2,1)S(1)} %get-tuple-element.76.refs_6_.refs_8_), channel_id=1, source_target_pairs={{0,8},{4,12},{8,0},{12,4},{16,24},{20,28},{24,16},{28,20},{1,9},{5... | collective-permute-start | bytes 196616 | tf_op jit(solution)/shard_map/ppermute | solution.py:502
  30.9 1.5 %collective-permute-start.10 = (bf16[8,32,128]{2,1,0:T(8,128)(2,1)S(1)}, bf16[8,32,128]{2,1,0:T(8,128)(2,1)S(1)}, u32[]{:S(2)}, u32[]{:S(2)}) collective-permute-start(bf16[8,32,128]{2,1,0:T(8,128)(2,1)S(1)} %get-tuple-element.79.refs_11_.refs_13_), channel_id=1, source_target_pairs={{0,24},{4,28},{8,16},{12,20},{16,8},{20,12},{24,0},{28,4},{1,25},{... | collective-permute-start | bytes 196616 | tf_op jit(solution)/shard_map/ppermute | solution.py:502
  33.1 1.5 %collective-permute-start.12 = (bf16[8,32,128]{2,1,0:T(8,128)(2,1)S(1)}, bf16[8,32,128]{2,1,0:T(8,128)(2,1)S(1)}, u32[]{:S(2)}, u32[]{:S(2)}) collective-permute-start(bf16[8,32,128]{2,1,0:T(8,128)(2,1)S(1)} %get-tuple-element.81.refs_9_.refs_11_), channel_id=1, source_target_pairs={{0,8},{4,12},{8,0},{12,4},{16,24},{20,28},{24,16},{28,20},{1,9},{5... | collective-permute-start | bytes 196616 | tf_op jit(solution)/shard_map/ppermute | solution.py:502
  35.6 2.2 %collective-permute-start.14 = (bf16[8,32,128]{2,1,0:T(8,128)(2,1)S(1)}, bf16[8,32,128]{2,1,0:T(8,128)(2,1)S(1)}, u32[]{:S(2)}, u32[]{:S(2)}) collective-permute-start(bf16[8,32,128]{2,1,0:T(8,128)(2,1)S(1)} %get-tuple-element.85.refs_0_), channel_id=1, source_target_pairs={{0,2},{1,3},{2,0},{3,1},{4,6},{5,7},{6,4},{7,5},{8,10},{9,11},{10,... | collective-permute-start | bytes 196616 | tf_op jit(solution)/shard_map/ppermute | solution.py:106
  38.1 1.9 %collective-permute-start.13 = (bf16[8,32,128]{2,1,0:T(8,128)(2,1)S(1)}, bf16[8,32,128]{2,1,0:T(8,128)(2,1)S(1)}, u32[]{:S(2)}, u32[]{:S(2)}) collective-permute-start(bf16[8,32,128]{2,1,0:T(8,128)(2,1)S(1)} %get-tuple-element.84.refs_1_), channel_id=1, source_target_pairs={{0,2},{1,3},{2,0},{3,1},{4,6},{5,7},{6,4},{7,5},{8,10},{9,11},{10,... | collective-permute-start | bytes 196616 | tf_op jit(solution)/shard_map/ppermute | solution.py:106
  40.9 1.9 %collective-permute-done.14.refs_2_ = bf16[8,32,128]{2,1,0:T(8,128)(2,1)S(1)} collective-permute-done((bf16[8,32,128]{2,1,0:T(8,128)(2,1)S(1)}, bf16[8,32,128]{2,1,0:T(8,128)(2,1)S(1)}, u32[]{:S(2)}, u32[]{:S(2)}) %collective-permute-start.14) | collective-permute-done | bytes 65568 | tf_op jit(solution)/shard_map/ppermute | solution.py:106
  42.9 1.5 %stage0.4 = (f32[65,32,128]{2,1,0:T(8,128)S(1)}, f32[65,32,128]{2,1,0:T(8,128)S(1)}, f32[8,128]{1,0:T(8,128)S(1)}) custom-call(s32[7,208]{1,0:T(8,128)S(4)} %get-tuple-element.63.list_ref, s32[6]{0:T(128)S(4)} %get-tuple-element.64.total_ref, bf16[192,128,128]{2,1,0:T(8,128)(2,1)S(1)} %get-tuple-element.65.values_ref, ...), custom_call_target="tpu_custom_call" | custom-call | flops 100663296 | bytes 3145728 | tf_op jit(solution)/shard_map/stage0/pallas_call | solution.py:399
  44.4 1.7 %collective-permute-start.16 = (bf16[8,32,128]{2,1,0:T(8,128)(2,1)S(1)}, bf16[8,32,128]{2,1,0:T(8,128)(2,1)S(1)}, u32[]{:S(2)}, u32[]{:S(2)}) collective-permute-start(bf16[8,32,128]{2,1,0:T(8,128)(2,1)S(1)} %hold.4.refs_0_), channel_id=1, source_target_pairs={{0,1},{1,0},{2,3},{3,2},{4,5},{5,4},{6,7},{7,6},{8,9},{9,8},{10,11... | collective-permute-start | bytes 196616 | tf_op jit(solution)/shard_map/ppermute | solution.py:487
  49.4 1.6 %collective-permute-done.19.other_ref.refs_7_ = bf16[64,32,128]{2,1,0:T(8,128)(2,1)S(1)} collective-permute-done((bf16[64,32,128]{2,1,0:T(8,128)(2,1)S(1)}, bf16[64,32,128]{2,1,0:T(8,128)(2,1)S(1)}, u32[]{:S(2)}, u32[]{:S(2)}) %collective-permute-start.19) | collective-permute-done | bytes 524320 | tf_op jit(solution)/shard_map/ppermute | solution.py:492
  51.0 2.3 %collective-permute-start.20 = (bf16[8,32,128]{2,1,0:T(8,128)(2,1)S(1)}, bf16[8,32,128]{2,1,0:T(8,128)(2,1)S(1)}, u32[]{:S(2)}, u32[]{:S(2)}) collective-permute-start(bf16[8,32,128]{2,1,0:T(8,128)(2,1)S(1)} %get-tuple-element.92.refs_16_), channel_id=1, source_target_pairs={{0,24},{4,28},{8,16},{12,20},{16,8},{20,12},{24,0},{28,4},{1,25},{... | collective-permute-start | bytes 196616 | tf_op jit(solution)/shard_map/ppermute | solution.py:502
  54.7 2.2 %collective-permute-start.23 = (bf16[8,32,128]{2,1,0:T(8,128)(2,1)S(1)}, bf16[8,32,128]{2,1,0:T(8,128)(2,1)S(1)}, u32[]{:S(2)}, u32[]{:S(2)}) collective-permute-start(bf16[8,32,128]{2,1,0:T(8,128)(2,1)S(1)} %get-tuple-element.97.refs_19_), channel_id=1, source_target_pairs={{0,24},{4,28},{8,16},{12,20},{16,8},{20,12},{24,0},{28,4},{1,25},{... | collective-permute-start | bytes 196616 | tf_op jit(solution)/shard_map/ppermute | solution.py:502
  58.8 1.6 %collective-permute-start.28 = (bf16[8,32,128]{2,1,0:T(8,128)(2,1)S(1)}, bf16[8,32,128]{2,1,0:T(8,128)(2,1)S(1)}, u32[]{:S(2)}, u32[]{:S(2)}) collective-permute-start(bf16[8,32,128]{2,1,0:T(8,128)(2,1)S(1)} %get-tuple-element.102.refs_0_), channel_id=1, source_target_pairs={{0,1},{1,0},{2,3},{3,2},{4,5},{5,4},{6,7},{7,6},{8,9},{9,8},{10,11... | collective-permute-start | bytes 196616 | tf_op jit(solution)/shard_map/ppermute | solution.py:107
  60.4 1.1 %collective-permute-start.27 = (bf16[8,32,128]{2,1,0:T(8,128)(2,1)S(1)}, bf16[8,32,128]{2,1,0:T(8,128)(2,1)S(1)}, u32[]{:S(2)}, u32[]{:S(2)}) collective-permute-start(bf16[8,32,128]{2,1,0:T(8,128)(2,1)S(1)} %get-tuple-element.102.refs_0_), channel_id=1, source_target_pairs={{0,2},{1,3},{2,0},{3,1},{4,6},{5,7},{6,4},{7,5},{8,10},{9,11},{10,... | collective-permute-start | bytes 196616 | tf_op jit(solution)/shard_map/ppermute | solution.py:106
  62.1 2.1 %collective-permute-start.26 = (bf16[8,32,128]{2,1,0:T(8,128)(2,1)S(1)}, bf16[8,32,128]{2,1,0:T(8,128)(2,1)S(1)}, u32[]{:S(2)}, u32[]{:S(2)}) collective-permute-start(bf16[8,32,128]{2,1,0:T(8,128)(2,1)S(1)} %get-tuple-element.101.refs_1_), channel_id=1, source_target_pairs={{0,2},{1,3},{2,0},{3,1},{4,6},{5,7},{6,4},{7,5},{8,10},{9,11},{10,... | collective-permute-start | bytes 196616 | tf_op jit(solution)/shard_map/ppermute | solution.py:106
  64.6 2.5 %collective-permute-done.27.refs_2_ = bf16[8,32,128]{2,1,0:T(8,128)(2,1)S(1)} collective-permute-done((bf16[8,32,128]{2,1,0:T(8,128)(2,1)S(1)}, bf16[8,32,128]{2,1,0:T(8,128)(2,1)S(1)}, u32[]{:S(2)}, u32[]{:S(2)}) %collective-permute-start.27) | collective-permute-done | bytes 65568 | tf_op jit(solution)/shard_map/ppermute | solution.py:106
  67.1 1.7 %stage0.5 = (f32[65,32,128]{2,1,0:T(8,128)S(1)}, f32[65,32,128]{2,1,0:T(8,128)S(1)}, f32[8,128]{1,0:T(8,128)S(1)}) custom-call(s32[7,208]{1,0:T(8,128)S(4)} %get-tuple-element.63.list_ref, s32[6]{0:T(128)S(4)} %get-tuple-element.64.total_ref, bf16[192,128,128]{2,1,0:T(8,128)(2,1)S(1)} %get-tuple-element.65.values_ref, ...), custom_call_target="tpu_custom_call" | custom-call | flops 100663296 | bytes 3145728 | tf_op jit(solution)/shard_map/stage0/pallas_call | solution.py:399
  68.8 1.8 %collective-permute-start.29 = (bf16[8,32,128]{2,1,0:T(8,128)(2,1)S(1)}, bf16[8,32,128]{2,1,0:T(8,128)(2,1)S(1)}, u32[]{:S(2)}, u32[]{:S(2)}) collective-permute-start(bf16[8,32,128]{2,1,0:T(8,128)(2,1)S(1)} %hold.5.refs_0_), channel_id=1, source_target_pairs={{0,1},{1,0},{2,3},{3,2},{4,5},{5,4},{6,7},{7,6},{8,9},{9,8},{10,11... | collective-permute-start | bytes 196616 | tf_op jit(solution)/shard_map/ppermute | solution.py:487
  73.8 1.6 %collective-permute-done.32.other_ref = bf16[64,32,128]{2,1,0:T(8,128)(2,1)S(1)} collective-permute-done((bf16[64,32,128]{2,1,0:T(8,128)(2,1)S(1)}, bf16[64,32,128]{2,1,0:T(8,128)(2,1)S(1)}, u32[]{:S(2)}, u32[]{:S(2)}) %collective-permute-start.32) | collective-permute-done | bytes 524320 | tf_op jit(solution)/shard_map/ppermute | solution.py:492
  75.5 1.8 %collective-permute-start.33 = (bf16[16,32,128]{2,1,0:T(8,128)(2,1)S(1)}, bf16[16,32,128]{2,1,0:T(8,128)(2,1)S(1)}, u32[]{:S(2)}, u32[]{:S(2)}) collective-permute-start(bf16[16,32,128]{2,1,0:T(8,128)(2,1)S(1)} %get-tuple-element.110), channel_id=1, source_target_pairs={{0,24},{4,28},{8,16},{12,20},{16,8},{20,12},{24,0},{28,4},{1,25},{... | collective-permute-start | bytes 393224 | tf_op jit(solution)/shard_map/ppermute | solution.py:502
  77.9 1.2 %collective-permute-start.35 = (bf16[16,32,128]{2,1,0:T(8,128)(2,1)S(1)}, bf16[16,32,128]{2,1,0:T(8,128)(2,1)S(1)}, u32[]{:S(2)}, u32[]{:S(2)}) collective-permute-start(bf16[16,32,128]{2,1,0:T(8,128)(2,1)S(1)} %get-tuple-element.112), channel_id=1, source_target_pairs={{0,8},{4,12},{8,0},{12,4},{16,24},{20,28},{24,16},{28,20},{1,9},{5... | collective-permute-start | bytes 393224 | tf_op jit(solution)/shard_map/ppermute | solution.py:502
  79.2 3.6 %collective-permute-done.33.refs_0_ = bf16[16,32,128]{2,1,0:T(8,128)(2,1)S(1)} collective-permute-done((bf16[16,32,128]{2,1,0:T(8,128)(2,1)S(1)}, bf16[16,32,128]{2,1,0:T(8,128)(2,1)S(1)}, u32[]{:S(2)}, u32[]{:S(2)}) %collective-permute-start.33) | collective-permute-done | bytes 131104 | tf_op jit(solution)/shard_map/ppermute | solution.py:502
  82.8 2.0 %collective-permute-done.34.refs_1_ = bf16[16,32,128]{2,1,0:T(8,128)(2,1)S(1)} collective-permute-done((bf16[16,32,128]{2,1,0:T(8,128)(2,1)S(1)}, bf16[16,32,128]{2,1,0:T(8,128)(2,1)S(1)}, u32[]{:S(2)}, u32[]{:S(2)}) %collective-permute-start.34) | collective-permute-done | bytes 131104 | tf_op jit(solution)/shard_map/ppermute | solution.py:502
  85.5 1.4 %finish.1 = f32[16,32,128]{2,1,0:T(8,128)} custom-call(bf16[16,128,128]{2,1,0:T(8,128)(2,1)S(1)} %get-tuple-element.59.high_ref, bf16[16,128,128]{2,1,0:T(8,128)(2,1)S(1)} %get-tuple-element.60.low_ref, f32[16,32,128]{2,1,0:T(8,128)S(1)} %get-tuple-element.100.sol_ref, f32[16,32,128]{2,1,0:T(8,128)S(1)} %keep.5.base_ref, ...), custom_call_target="tpu_custom_call" | custom-call | tf_op jit(solution)/shard_map/finish/pallas_call | solution.py:522
  (70 shorter events, 18.4 us)
Async XLA Ops:
  2.2 12.2 %collective-permute-start.1 = (bf16[8,32,128]{2,1,0:T(8,128)(2,1)S(1)}, bf16[8,32,128]{2,1,0:T(8,128)(2,1)S(1)}, u32[]{:S(2)}, u32[]{:S(2)}) collective-permute-start(bf16[8,32,128]{2,1,0:T(8,128)(2,1)S(1)} %get-tuple-element.67.refs_0_), channel_id=1, source_target_pairs={{0,2},{1,3},{2,0},{3,1},{4,6},{5,7},{6,4},{7,5},{8,10},{9,11},{10,... | collective-permute-start | bytes 196616 | tf_op jit(solution)/shard_map/ppermute | solution.py:106
  6.3 10.3 %collective-permute-start.2 = (bf16[8,32,128]{2,1,0:T(8,128)(2,1)S(1)}, bf16[8,32,128]{2,1,0:T(8,128)(2,1)S(1)}, u32[]{:S(2)}, u32[]{:S(2)}) collective-permute-start(bf16[8,32,128]{2,1,0:T(8,128)(2,1)S(1)} %get-tuple-element.67.refs_0_), channel_id=1, source_target_pairs={{0,1},{1,0},{2,3},{3,2},{4,5},{5,4},{6,7},{7,6},{8,9},{9,8},{10,11... | collective-permute-start | bytes 196616 | tf_op jit(solution)/shard_map/ppermute | solution.py:107
  7.8 10.2 %collective-permute-start = (bf16[8,32,128]{2,1,0:T(8,128)(2,1)S(1)}, bf16[8,32,128]{2,1,0:T(8,128)(2,1)S(1)}, u32[]{:S(2)}, u32[]{:S(2)}) collective-permute-start(bf16[8,32,128]{2,1,0:T(8,128)(2,1)S(1)} %get-tuple-element.66.refs_1_), channel_id=1, source_target_pairs={{0,2},{1,3},{2,0},{3,1},{4,6},{5,7},{6,4},{7,5},{8,10},{9,11},{10,... | collective-permute-start | bytes 196616 | tf_op jit(solution)/shard_map/ppermute | solution.py:106
  8.2 10.0 %collective-permute-start.4 = (bf16[8,32,128]{2,1,0:T(8,128)(2,1)S(1)}, bf16[8,32,128]{2,1,0:T(8,128)(2,1)S(1)}, u32[]{:S(2)}, u32[]{:S(2)}) collective-permute-start(bf16[8,32,128]{2,1,0:T(8,128)(2,1)S(1)} %get-tuple-element.66.refs_1_), channel_id=1, source_target_pairs={{0,1},{1,0},{2,3},{3,2},{4,5},{5,4},{6,7},{7,6},{8,9},{9,8},{10,11... | collective-permute-start | bytes 196616 | tf_op jit(solution)/shard_map/ppermute | solution.py:107
  14.4 4.5 %collective-permute-start.5 = (bf16[8,32,128]{2,1,0:T(8,128)(2,1)S(1)}, bf16[8,32,128]{2,1,0:T(8,128)(2,1)S(1)}, u32[]{:S(2)}, u32[]{:S(2)}) collective-permute-start(bf16[8,32,128]{2,1,0:T(8,128)(2,1)S(1)} %collective-permute-done.1.refs_2_), channel_id=1, source_target_pairs={{0,1},{1,0},{2,3},{3,2},{4,5},{5,4},{6,7},{7,6},{8,9},{9,8},{10,11... | collective-permute-start | bytes 196616 | tf_op jit(solution)/shard_map/ppermute | solution.py:487
  18.1 4.3 %collective-permute-start.3 = (bf16[8,32,128]{2,1,0:T(8,128)(2,1)S(1)}, bf16[8,32,128]{2,1,0:T(8,128)(2,1)S(1)}, u32[]{:S(2)}, u32[]{:S(2)}) collective-permute-start(bf16[8,32,128]{2,1,0:T(8,128)(2,1)S(1)} %hold.3.refs_0_), channel_id=1, source_target_pairs={{0,1},{1,0},{2,3},{3,2},{4,5},{5,4},{6,7},{7,6},{8,9},{9,8},{10,11... | collective-permute-start | bytes 196616 | tf_op jit(solution)/shard_map/ppermute | solution.py:487
  24.7 8.4 %collective-permute-start.7 = (bf16[8,32,128]{2,1,0:T(8,128)(2,1)S(1)}, bf16[8,32,128]{2,1,0:T(8,128)(2,1)S(1)}, u32[]{:S(2)}, u32[]{:S(2)}) collective-permute-start(bf16[8,32,128]{2,1,0:T(8,128)(2,1)S(1)} %get-tuple-element.74.refs_8_.refs_10_), channel_id=1, source_target_pairs={{0,24},{4,28},{8,16},{12,20},{16,8},{20,12},{24,0},{28,4},{1,25},{... | collective-permute-start | bytes 196616 | tf_op jit(solution)/shard_map/ppermute | solution.py:502
  25.1 9.5 %collective-permute-start.8 = (bf16[8,32,128]{2,1,0:T(8,128)(2,1)S(1)}, bf16[8,32,128]{2,1,0:T(8,128)(2,1)S(1)}, u32[]{:S(2)}, u32[]{:S(2)}) collective-permute-start(bf16[8,32,128]{2,1,0:T(8,128)(2,1)S(1)} %get-tuple-element.75.refs_7_.refs_9_), channel_id=1, source_target_pairs={{0,16},{4,20},{8,24},{12,28},{16,0},{20,4},{24,8},{28,12},{1,17},{... | collective-permute-start | bytes 196616 | tf_op jit(solution)/shard_map/ppermute | solution.py:502
  29.4 5.1 %collective-permute-start.9 = (bf16[8,32,128]{2,1,0:T(8,128)(2,1)S(1)}, bf16[8,32,128]{2,1,0:T(8,128)(2,1)S(1)}, u32[]{:S(2)}, u32[]{:S(2)}) collective-permute-start(bf16[8,32,128]{2,1,0:T(8,128)(2,1)S(1)} %get-tuple-element.76.refs_6_.refs_8_), channel_id=1, source_target_pairs={{0,8},{4,12},{8,0},{12,4},{16,24},{20,28},{24,16},{28,20},{1,9},{5... | collective-permute-start | bytes 196616 | tf_op jit(solution)/shard_map/ppermute | solution.py:502
  30.9 6.8 %collective-permute-start.10 = (bf16[8,32,128]{2,1,0:T(8,128)(2,1)S(1)}, bf16[8,32,128]{2,1,0:T(8,128)(2,1)S(1)}, u32[]{:S(2)}, u32[]{:S(2)}) collective-permute-start(bf16[8,32,128]{2,1,0:T(8,128)(2,1)S(1)} %get-tuple-element.79.refs_11_.refs_13_), channel_id=1, source_target_pairs={{0,24},{4,28},{8,16},{12,20},{16,8},{20,12},{24,0},{28,4},{1,25},{... | collective-permute-start | bytes 196616 | tf_op jit(solution)/shard_map/ppermute | solution.py:502
  32.4 5.3 %collective-permute-start.11 = (bf16[8,32,128]{2,1,0:T(8,128)(2,1)S(1)}, bf16[8,32,128]{2,1,0:T(8,128)(2,1)S(1)}, u32[]{:S(2)}, u32[]{:S(2)}) collective-permute-start(bf16[8,32,128]{2,1,0:T(8,128)(2,1)S(1)} %get-tuple-element.80.refs_10_.refs_12_), channel_id=1, source_target_pairs={{0,16},{4,20},{8,24},{12,28},{16,0},{20,4},{24,8},{28,12},{1,17},{... | collective-permute-start | bytes 196616 | tf_op jit(solution)/shard_map/ppermute | solution.py:502
  33.1 4.6 %collective-permute-start.12 = (bf16[8,32,128]{2,1,0:T(8,128)(2,1)S(1)}, bf16[8,32,128]{2,1,0:T(8,128)(2,1)S(1)}, u32[]{:S(2)}, u32[]{:S(2)}) collective-permute-start(bf16[8,32,128]{2,1,0:T(8,128)(2,1)S(1)} %get-tuple-element.81.refs_9_.refs_11_), channel_id=1, source_target_pairs={{0,8},{4,12},{8,0},{12,4},{16,24},{20,28},{24,16},{28,20},{1,9},{5... | collective-permute-start | bytes 196616 | tf_op jit(solution)/shard_map/ppermute | solution.py:502
  35.0 7.9 %collective-permute-start.15 = (bf16[8,32,128]{2,1,0:T(8,128)(2,1)S(1)}, bf16[8,32,128]{2,1,0:T(8,128)(2,1)S(1)}, u32[]{:S(2)}, u32[]{:S(2)}) collective-permute-start(bf16[8,32,128]{2,1,0:T(8,128)(2,1)S(1)} %get-tuple-element.85.refs_0_), channel_id=1, source_target_pairs={{0,1},{1,0},{2,3},{3,2},{4,5},{5,4},{6,7},{7,6},{8,9},{9,8},{10,11... | collective-permute-start | bytes 196616 | tf_op jit(solution)/shard_map/ppermute | solution.py:107
  35.6 7.2 %collective-permute-start.14 = (bf16[8,32,128]{2,1,0:T(8,128)(2,1)S(1)}, bf16[8,32,128]{2,1,0:T(8,128)(2,1)S(1)}, u32[]{:S(2)}, u32[]{:S(2)}) collective-permute-start(bf16[8,32,128]{2,1,0:T(8,128)(2,1)S(1)} %get-tuple-element.85.refs_0_), channel_id=1, source_target_pairs={{0,2},{1,3},{2,0},{3,1},{4,6},{5,7},{6,4},{7,5},{8,10},{9,11},{10,... | collective-permute-start | bytes 196616 | tf_op jit(solution)/shard_map/ppermute | solution.py:106
  38.1 6.2 %collective-permute-start.13 = (bf16[8,32,128]{2,1,0:T(8,128)(2,1)S(1)}, bf16[8,32,128]{2,1,0:T(8,128)(2,1)S(1)}, u32[]{:S(2)}, u32[]{:S(2)}) collective-permute-start(bf16[8,32,128]{2,1,0:T(8,128)(2,1)S(1)} %get-tuple-element.84.refs_1_), channel_id=1, source_target_pairs={{0,2},{1,3},{2,0},{3,1},{4,6},{5,7},{6,4},{7,5},{8,10},{9,11},{10,... | collective-permute-start | bytes 196616 | tf_op jit(solution)/shard_map/ppermute | solution.py:106
  40.0 6.1 %collective-permute-start.17 = (bf16[8,32,128]{2,1,0:T(8,128)(2,1)S(1)}, bf16[8,32,128]{2,1,0:T(8,128)(2,1)S(1)}, u32[]{:S(2)}, u32[]{:S(2)}) collective-permute-start(bf16[8,32,128]{2,1,0:T(8,128)(2,1)S(1)} %get-tuple-element.84.refs_1_), channel_id=1, source_target_pairs={{0,1},{1,0},{2,3},{3,2},{4,5},{5,4},{6,7},{7,6},{8,9},{9,8},{10,11... | collective-permute-start | bytes 196616 | tf_op jit(solution)/shard_map/ppermute | solution.py:107
  42.8 4.3 %collective-permute-start.18 = (bf16[8,32,128]{2,1,0:T(8,128)(2,1)S(1)}, bf16[8,32,128]{2,1,0:T(8,128)(2,1)S(1)}, u32[]{:S(2)}, u32[]{:S(2)}) collective-permute-start(bf16[8,32,128]{2,1,0:T(8,128)(2,1)S(1)} %collective-permute-done.14.refs_2_), channel_id=1, source_target_pairs={{0,1},{1,0},{2,3},{3,2},{4,5},{5,4},{6,7},{7,6},{8,9},{9,8},{10,11... | collective-permute-start | bytes 196616 | tf_op jit(solution)/shard_map/ppermute | solution.py:487
  44.4 4.3 %collective-permute-start.16 = (bf16[8,32,128]{2,1,0:T(8,128)(2,1)S(1)}, bf16[8,32,128]{2,1,0:T(8,128)(2,1)S(1)}, u32[]{:S(2)}, u32[]{:S(2)}) collective-permute-start(bf16[8,32,128]{2,1,0:T(8,128)(2,1)S(1)} %hold.4.refs_0_), channel_id=1, source_target_pairs={{0,1},{1,0},{2,3},{3,2},{4,5},{5,4},{6,7},{7,6},{8,9},{9,8},{10,11... | collective-permute-start | bytes 196616 | tf_op jit(solution)/shard_map/ppermute | solution.py:487
  51.0 6.3 %collective-permute-start.20 = (bf16[8,32,128]{2,1,0:T(8,128)(2,1)S(1)}, bf16[8,32,128]{2,1,0:T(8,128)(2,1)S(1)}, u32[]{:S(2)}, u32[]{:S(2)}) collective-permute-start(bf16[8,32,128]{2,1,0:T(8,128)(2,1)S(1)} %get-tuple-element.92.refs_16_), channel_id=1, source_target_pairs={{0,24},{4,28},{8,16},{12,20},{16,8},{20,12},{24,0},{28,4},{1,25},{... | collective-permute-start | bytes 196616 | tf_op jit(solution)/shard_map/ppermute | solution.py:502
  53.3 5.1 %collective-permute-start.21 = (bf16[8,32,128]{2,1,0:T(8,128)(2,1)S(1)}, bf16[8,32,128]{2,1,0:T(8,128)(2,1)S(1)}, u32[]{:S(2)}, u32[]{:S(2)}) collective-permute-start(bf16[8,32,128]{2,1,0:T(8,128)(2,1)S(1)} %get-tuple-element.93.refs_15_), channel_id=1, source_target_pairs={{0,16},{4,20},{8,24},{12,28},{16,0},{20,4},{24,8},{28,12},{1,17},{... | collective-permute-start | bytes 196616 | tf_op jit(solution)/shard_map/ppermute | solution.py:502
  53.7 4.7 %collective-permute-start.22 = (bf16[8,32,128]{2,1,0:T(8,128)(2,1)S(1)}, bf16[8,32,128]{2,1,0:T(8,128)(2,1)S(1)}, u32[]{:S(2)}, u32[]{:S(2)}) collective-permute-start(bf16[8,32,128]{2,1,0:T(8,128)(2,1)S(1)} %get-tuple-element.94.refs_14_), channel_id=1, source_target_pairs={{0,8},{4,12},{8,0},{12,4},{16,24},{20,28},{24,16},{28,20},{1,9},{5... | collective-permute-start | bytes 196616 | tf_op jit(solution)/shard_map/ppermute | solution.py:502
  54.7 6.8 %collective-permute-start.23 = (bf16[8,32,128]{2,1,0:T(8,128)(2,1)S(1)}, bf16[8,32,128]{2,1,0:T(8,128)(2,1)S(1)}, u32[]{:S(2)}, u32[]{:S(2)}) collective-permute-start(bf16[8,32,128]{2,1,0:T(8,128)(2,1)S(1)} %get-tuple-element.97.refs_19_), channel_id=1, source_target_pairs={{0,24},{4,28},{8,16},{12,20},{16,8},{20,12},{24,0},{28,4},{1,25},{... | collective-permute-start | bytes 196616 | tf_op jit(solution)/shard_map/ppermute | solution.py:502
  56.9 4.6 %collective-permute-start.24 = (bf16[8,32,128]{2,1,0:T(8,128)(2,1)S(1)}, bf16[8,32,128]{2,1,0:T(8,128)(2,1)S(1)}, u32[]{:S(2)}, u32[]{:S(2)}) collective-permute-start(bf16[8,32,128]{2,1,0:T(8,128)(2,1)S(1)} %get-tuple-element.98.refs_18_), channel_id=1, source_target_pairs={{0,16},{4,20},{8,24},{12,28},{16,0},{20,4},{24,8},{28,12},{1,17},{... | collective-permute-start | bytes 196616 | tf_op jit(solution)/shard_map/ppermute | solution.py:502
  57.3 4.3 %collective-permute-start.25 = (bf16[8,32,128]{2,1,0:T(8,128)(2,1)S(1)}, bf16[8,32,128]{2,1,0:T(8,128)(2,1)S(1)}, u32[]{:S(2)}, u32[]{:S(2)}) collective-permute-start(bf16[8,32,128]{2,1,0:T(8,128)(2,1)S(1)} %get-tuple-element.99.refs_17_), channel_id=1, source_target_pairs={{0,8},{4,12},{8,0},{12,4},{16,24},{20,28},{24,16},{28,20},{1,9},{5... | collective-permute-start | bytes 196616 | tf_op jit(solution)/shard_map/ppermute | solution.py:502
  58.8 8.3 %collective-permute-start.28 = (bf16[8,32,128]{2,1,0:T(8,128)(2,1)S(1)}, bf16[8,32,128]{2,1,0:T(8,128)(2,1)S(1)}, u32[]{:S(2)}, u32[]{:S(2)}) collective-permute-start(bf16[8,32,128]{2,1,0:T(8,128)(2,1)S(1)} %get-tuple-element.102.refs_0_), channel_id=1, source_target_pairs={{0,1},{1,0},{2,3},{3,2},{4,5},{5,4},{6,7},{7,6},{8,9},{9,8},{10,11... | collective-permute-start | bytes 196616 | tf_op jit(solution)/shard_map/ppermute | solution.py:107
  60.4 6.7 %collective-permute-start.27 = (bf16[8,32,128]{2,1,0:T(8,128)(2,1)S(1)}, bf16[8,32,128]{2,1,0:T(8,128)(2,1)S(1)}, u32[]{:S(2)}, u32[]{:S(2)}) collective-permute-start(bf16[8,32,128]{2,1,0:T(8,128)(2,1)S(1)} %get-tuple-element.102.refs_0_), channel_id=1, source_target_pairs={{0,2},{1,3},{2,0},{3,1},{4,6},{5,7},{6,4},{7,5},{8,10},{9,11},{10,... | collective-permute-start | bytes 196616 | tf_op jit(solution)/shard_map/ppermute | solution.py:106
  62.1 6.7 %collective-permute-start.26 = (bf16[8,32,128]{2,1,0:T(8,128)(2,1)S(1)}, bf16[8,32,128]{2,1,0:T(8,128)(2,1)S(1)}, u32[]{:S(2)}, u32[]{:S(2)}) collective-permute-start(bf16[8,32,128]{2,1,0:T(8,128)(2,1)S(1)} %get-tuple-element.101.refs_1_), channel_id=1, source_target_pairs={{0,2},{1,3},{2,0},{3,1},{4,6},{5,7},{6,4},{7,5},{8,10},{9,11},{10,... | collective-permute-start | bytes 196616 | tf_op jit(solution)/shard_map/ppermute | solution.py:106
  64.2 6.4 %collective-permute-start.30 = (bf16[8,32,128]{2,1,0:T(8,128)(2,1)S(1)}, bf16[8,32,128]{2,1,0:T(8,128)(2,1)S(1)}, u32[]{:S(2)}, u32[]{:S(2)}) collective-permute-start(bf16[8,32,128]{2,1,0:T(8,128)(2,1)S(1)} %get-tuple-element.101.refs_1_), channel_id=1, source_target_pairs={{0,1},{1,0},{2,3},{3,2},{4,5},{5,4},{6,7},{7,6},{8,9},{9,8},{10,11... | collective-permute-start | bytes 196616 | tf_op jit(solution)/shard_map/ppermute | solution.py:107
  68.8 4.3 %collective-permute-start.29 = (bf16[8,32,128]{2,1,0:T(8,128)(2,1)S(1)}, bf16[8,32,128]{2,1,0:T(8,128)(2,1)S(1)}, u32[]{:S(2)}, u32[]{:S(2)}) collective-permute-start(bf16[8,32,128]{2,1,0:T(8,128)(2,1)S(1)} %hold.5.refs_0_), channel_id=1, source_target_pairs={{0,1},{1,0},{2,3},{3,2},{4,5},{5,4},{6,7},{7,6},{8,9},{9,8},{10,11... | collective-permute-start | bytes 196616 | tf_op jit(solution)/shard_map/ppermute | solution.py:487
  75.5 7.3 %collective-permute-start.33 = (bf16[16,32,128]{2,1,0:T(8,128)(2,1)S(1)}, bf16[16,32,128]{2,1,0:T(8,128)(2,1)S(1)}, u32[]{:S(2)}, u32[]{:S(2)}) collective-permute-start(bf16[16,32,128]{2,1,0:T(8,128)(2,1)S(1)} %get-tuple-element.110), channel_id=1, source_target_pairs={{0,24},{4,28},{8,16},{12,20},{16,8},{20,12},{24,0},{28,4},{1,25},{... | collective-permute-start | bytes 393224 | tf_op jit(solution)/shard_map/ppermute | solution.py:502
  77.3 7.5 %collective-permute-start.34 = (bf16[16,32,128]{2,1,0:T(8,128)(2,1)S(1)}, bf16[16,32,128]{2,1,0:T(8,128)(2,1)S(1)}, u32[]{:S(2)}, u32[]{:S(2)}) collective-permute-start(bf16[16,32,128]{2,1,0:T(8,128)(2,1)S(1)} %get-tuple-element.111), channel_id=1, source_target_pairs={{0,16},{4,20},{8,24},{12,28},{16,0},{20,4},{24,8},{28,12},{1,17},{... | collective-permute-start | bytes 393224 | tf_op jit(solution)/shard_map/ppermute | solution.py:502
  77.9 7.6 %collective-permute-start.35 = (bf16[16,32,128]{2,1,0:T(8,128)(2,1)S(1)}, bf16[16,32,128]{2,1,0:T(8,128)(2,1)S(1)}, u32[]{:S(2)}, u32[]{:S(2)}) collective-permute-start(bf16[16,32,128]{2,1,0:T(8,128)(2,1)S(1)} %get-tuple-element.112), channel_id=1, source_target_pairs={{0,8},{4,12},{8,0},{12,4},{16,24},{20,28},{24,16},{28,20},{1,9},{5... | collective-permute-start | bytes 393224 | tf_op jit(solution)/shard_map/ppermute | solution.py:502
  (4 other events, 10.2 us)

commit v8 on v7

--- a/solution.py
+++ b/solution.py
@@ -11,7 +11,6 @@
 UNROLL = 16
 LANES = 4
 DEPTH = 6
-APPLY_FLOPS = 20_000_000_000
 CORES = 2
 VMEM_LIMIT = 24 * 1024 * 1024
 
@@ -82,11 +81,12 @@
         return [own, [(index, part) for index in range(1, groups) for part in every]]
     pairs = groups // 2
     early = range(parts - 1)
+    far, forwarded = range(1, pairs), range(pairs + 1, groups)
     stages = [
-        own + [(index, part) for part in early for index in range(1, pairs + 1)],
-        [(index, parts - 1) for index in range(1, pairs + 1)]
-        + [(index, part) for part in early for index in range(pairs + 1, groups)],
-        [(index, parts - 1) for index in range(pairs + 1, groups)],
+        own + [(index, part) for part in early for index in far],
+        [(pairs, part) for part in every] + [(index, parts - 1) for index in far]
+        + [(index, part) for part in early for index in forwarded],
+        [(index, parts - 1) for index in forwarded],
     ]
     return [stage for stage in stages if stage]
 
@@ -95,16 +95,16 @@
     return [(c, (c + step) % groups) for c in range(groups)]
 
 
-def gather(rounded, groups):
-    sets = {(0, part): piece for part, piece in enumerate(rounded)}
+def gather(whole, rounded, groups):
+    sets = {(0, 0): whole}
+    if groups % 2:
+        for step in range(1, groups):
+            sets[step, 0] = lax.ppermute(whole, "col", ring(groups, step))
+        return sets
     for part, piece in enumerate(rounded):
-        if groups % 2:
-            for step in range(1, groups):
-                sets[step, part] = lax.ppermute(piece, "col", ring(groups, step))
-        else:
-            for step in range(1, groups // 2):
-                sets[step, part] = lax.ppermute(piece, "col", ring(groups, 2 * step))
-            sets[groups // 2, part] = lax.ppermute(piece, "col", neighbours(groups))
+        for step in range(1, groups // 2):
+            sets[step, part] = lax.ppermute(piece, "col", ring(groups, 2 * step))
+    sets[groups // 2, 0] = lax.ppermute(whole, "col", neighbours(groups))
     return sets
 
 
@@ -116,7 +116,14 @@
     pass
 
 
-def start_kernel(precond_hbm, rhs_hbm, high_ref, low_ref, sol_ref, left_ref, *refs):
+def put_rounded(p, value, whole_ref, part_refs):
+    part, inner = divmod(p, part_refs[0].shape[0])
+    rounded = value.astype(jnp.bfloat16)
+    whole_ref[p] = rounded
+    part_refs[part][inner] = rounded
+
+
+def start_kernel(precond_hbm, rhs_hbm, high_ref, low_ref, sol_ref, left_ref, whole_ref, *refs):
     part_refs, (precond_ref, sems) = refs[:-2], refs[-2:]
     owned = left_ref.shape[0]
     parts = sems.shape[0] - 1
@@ -136,19 +143,17 @@
             low_ref[p] = low
             value = times_block(left_ref[p], high, low)
             sol_ref[p] = value
-            part_refs[p * len(part_refs) // owned][p % (owned // len(part_refs))] = value.astype(jnp.bfloat16)
-
-
-def apply_kernel(part, pieces, high_ref, low_ref, left_ref, sol_ref, base_ref, *refs):
-    piece_refs, (new_ref, new_left_ref, rounded_ref) = refs[:pieces], refs[pieces:]
-    each = rounded_ref.shape[0]
-    for inner in range(each):
-        p = part * each + inner
-        received = sum(piece_ref[inner].astype(jnp.float32) for piece_ref in piece_refs)
+            put_rounded(p, value, whole_ref, part_refs)
+
+
+def apply_kernel(pieces, high_ref, low_ref, left_ref, sol_ref, base_ref, *refs):
+    piece_refs, (new_ref, new_left_ref, whole_ref, *part_refs) = refs[:pieces], refs[pieces:]
+    for p in range(sol_ref.shape[0]):
+        received = sum(piece_ref[p].astype(jnp.float32) for piece_ref in piece_refs)
         value = sol_ref[p] + times_block(base_ref[p] - received, high_ref[p], low_ref[p])
         new_ref[p] = value
         new_left_ref[p] = left_ref[p] - received
-        rounded_ref[inner] = value.astype(jnp.bfloat16)
+        put_rounded(p, value, whole_ref, part_refs)
 
 
 def finish_kernel(pieces, high_ref, low_ref, sol_ref, base_ref, *refs):
@@ -267,7 +272,7 @@
     return field
 
 
-def first_kernel(pieces, steps, parts, chips, bits, list_ref, total_ref, values_ref, *refs):
+def first_kernel(pieces, steps, chips, bits, list_ref, total_ref, values_ref, *refs):
     piece_refs, refs = refs[:pieces], refs[pieces:]
     out_refs, refs = refs[:steps], refs[steps:]
     in_refs, refs = refs[:steps], refs[steps:]
@@ -284,15 +289,12 @@
             total[pl.ds(0, rows)] = -sum(out_ref[...].astype(jnp.float32) for out_ref in out_refs)
         else:
             for shift in range(chips):
-                for part in range(parts):
-                    each = owned // parts
-                    at = pl.ds(partner(chip, shift, chips) * owned + part * each, each)
-                    value = sum(in_ref[at].astype(jnp.float32) for in_ref in in_refs)
-                    if shift > 0:
-                        for step in range(steps):
-                            sent_ref = sent_refs[(step * parts + part) * (chips - 1) + shift - 1]
-                            value -= sent_ref[...].astype(jnp.float32)
-                    total[at] = value
+                at = pl.ds(partner(chip, shift, chips) * owned, owned)
+                value = sum(in_ref[at].astype(jnp.float32) for in_ref in in_refs)
+                if shift > 0:
+                    for step in range(steps):
+                        value -= sent_refs[step * (chips - 1) + shift - 1][...].astype(jnp.float32)
+                total[at] = value
         add_products(half, bits, list_ref, total_ref, values_ref, field_ref, total)
 
 
@@ -313,21 +315,20 @@
         out_ref[...] = total[pl.ds(0, out_ref.shape[0])].astype(out_ref.dtype)
 
 
-def chip_rows(shift, chips, part, parts, own_ref, other_ref):
+def chip_rows(shift, chips, own_ref, other_ref):
     chip = lax.axis_index("row") // CORES
     owned = other_ref.shape[0] // chips
-    each = owned // parts
-    at = pl.ds(partner(chip, shift, chips) * owned + part * each, each)
+    at = pl.ds(partner(chip, shift, chips) * owned, owned)
     return own_ref[at] + other_ref[at].astype(jnp.float32)
 
 
-def combine_kernel(shifts, chips, part, parts, own_ref, other_ref, *send_refs):
+def combine_kernel(shifts, chips, own_ref, other_ref, *send_refs):
     for shift, send_ref in zip(shifts, send_refs):
-        send_ref[...] = chip_rows(shift, chips, part, parts, own_ref, other_ref).astype(send_ref.dtype)
+        send_ref[...] = chip_rows(shift, chips, own_ref, other_ref).astype(send_ref.dtype)
 
 
 def keep_kernel(chips, own_ref, other_ref, left_ref, sol_ref, base_ref):
-    base_ref[...] = left_ref[...] - sol_ref[...] - chip_rows(0, chips, 0, 1, own_ref, other_ref)
+    base_ref[...] = left_ref[...] - sol_ref[...] - chip_rows(0, chips, own_ref, other_ref)
 
 
 def per_device(block_values, block_rows, block_cols, block_counts, precond, right_side):
@@ -354,13 +355,14 @@
     index_type = pltpu.SMEM(block_rows.shape, jnp.int32)
     token_type = jax.ShapeDtypeStruct((8, 128), jnp.float32)
     loads = next(count for count in (4, 2, 1) if owned % count == 0)
+    rounded_type = jax.ShapeDtypeStruct((owned, rhs, size), jnp.bfloat16)
     part_type = jax.ShapeDtypeStruct((owned // parts, rhs, size), jnp.bfloat16)
 
-    high, low, sol, left, *rounded = pl.pallas_call(
+    high, low, sol, left, whole, *rounded = pl.pallas_call(
         start_kernel,
-        out_shape=[matrix_type] * 2 + [field_type] * 2 + [part_type] * parts,
+        out_shape=[matrix_type] * 2 + [field_type] * 2 + [rounded_type] + [part_type] * parts,
         in_specs=[in_hbm()] * 2,
-        out_specs=[in_vmem()] * (4 + parts),
+        out_specs=[in_vmem()] * (5 + parts),
         scratch_shapes=[
             pltpu.VMEM((owned, size, size), jnp.float32),
             pltpu.SemaphoreType.DMA((loads + 1,)),
@@ -397,13 +399,13 @@
 
     def product_first(pieces, outs, ins, sent):
         return pl.pallas_call(
-            functools.partial(first_kernel, len(pieces), len(outs), parts, chips, bits),
+            functools.partial(first_kernel, len(pieces), len(outs), chips, bits),
             out_shape=[total_type] * CORES + [token_type],
             in_specs=[in_smem()] * 2 + [in_vmem()] * (1 + len(pieces) + len(outs) + len(ins) + len(sent)),
             out_specs=[in_vmem()] * (CORES + 1),
+            compiler_params=params(),
             scratch_shapes=[field_scratch(pieces)],
-            compiler_params=params(),
-            cost_estimate=cost(len(pieces) / groups / parts),
+            cost_estimate=cost(len(stages[0]) / groups / parts),
             name="stage0",
         )(*lists, values, *pieces, *outs, *ins, *sent)
 
@@ -417,7 +419,7 @@
             scratch_shapes=[field_scratch(pieces)],
             input_output_aliases={inputs + half: half for half in range(CORES)},
             compiler_params=params(),
-            cost_estimate=cost(len(pieces) / groups / parts),
+            cost_estimate=cost(len(stages[stage]) / groups / parts),
             name="stage%d" % stage,
         )(*lists, values, *pieces, *totals)
 
@@ -431,7 +433,7 @@
             scratch_shapes=[field_scratch(pieces)],
             input_output_aliases={3 + len(pieces): 0},
             compiler_params=params(),
-            cost_estimate=cost(len(pieces) / groups / parts / CORES),
+            cost_estimate=cost(len(stages[final]) / groups / parts / CORES),
             name="last%d" % half,
         )(*lists, values, *pieces, total)[-1]
 
@@ -448,43 +450,35 @@
 
     shifts = list(reversed(range(1, chips)))
 
-    def combine(part, parts, own, incoming):
-        send_type = jax.ShapeDtypeStruct((owned // parts, rhs, size), jnp.bfloat16)
+    def combine(own, incoming):
         return pl.pallas_call(
-            functools.partial(combine_kernel, shifts, chips, part, parts),
-            out_shape=[send_type] * len(shifts),
+            functools.partial(combine_kernel, shifts, chips),
+            out_shape=[rounded_type] * len(shifts),
             in_specs=[in_vmem()] * 2,
             out_specs=[in_vmem()] * len(shifts),
             compiler_params=params(),
-            name="combine%d" % part,
+            name="combine",
         )(own, incoming)
-
-    def apply(part, sol, left, base, pieces):
-        return pl.pallas_call(
-            functools.partial(apply_kernel, part, len(pieces)),
-            out_shape=[field_type, field_type, part_type],
-            in_specs=[in_vmem()] * (5 + len(pieces)),
-            out_specs=[in_vmem()] * 3,
-            input_output_aliases={2: 1, 3: 0},
-            compiler_params=params(),
-            cost_estimate=pl.CostEstimate(flops=APPLY_FLOPS, bytes_accessed=0, transcendentals=0),
-            name="apply%d" % part,
-        )(high, low, left, sol, base, *pieces)
 
     outs, ins, sent = [], [], []
     for step in range(ITERS):
-        sets = gather(rounded, groups)
+        sets = gather(whole, rounded, groups)
 
         def stage_pieces(stage):
-            return [sets[piece] for piece in stages[stage]]
-
+            return [sets[piece] for piece in stages[stage] if piece in sets]
+
+        def forward(part, token=None):
+            for index in range(1, groups // 2):
+                if token is not None:
+                    sets[index, part] = hold(sets[index, part], token)
+                sets[groups // 2 + index, part] = lax.ppermute(sets[index, part], "col", neighbours(groups))
+
+        if groups % 2 == 0:
+            for part in range(parts - 1):
+                forward(part)
         *totals, token = product_first(stage_pieces(0), outs, ins, sent)
         if groups % 2 == 0:
-            for index in range(1, groups // 2):
-                for part in range(parts):
-                    if part == parts - 1:
-                        sets[index, part] = hold(sets[index, part], token)
-                    sets[groups // 2 + index, part] = lax.ppermute(sets[index, part], "col", neighbours(groups))
+            forward(parts - 1, token)
 
         for stage in range(1, final):
             totals = product_stage(stage, stage_pieces(stage), totals)
@@ -493,18 +487,15 @@
         own = product_last(1, stage_pieces(final), totals[1])
         outs.append(outgoing)
         ins.append(incoming)
-        parts_now = parts if step < ITERS - 1 else 1
-        received = []
-        for part in range(parts_now):
-            sends = combine(part, parts_now, own, incoming)
-            sent += reversed(sends)
-            received.append([
-                lax.ppermute(send, "row", [
-                    (chip * CORES + core, partner(chip, shift, chips) * CORES + core)
-                    for chip in range(chips) for core in range(CORES)
-                ])
-                for shift, send in zip(shifts, sends)
+        sends = combine(own, incoming)
+        sent += reversed(sends)
+        pieces = [
+            lax.ppermute(send, "row", [
+                (chip * CORES + core, partner(chip, shift, chips) * CORES + core)
+                for chip in range(chips) for core in range(CORES)
             ])
+            for shift, send in zip(shifts, sends)
+        ]
         base = pl.pallas_call(
             functools.partial(keep_kernel, chips),
             out_shape=field_type,
@@ -514,11 +505,14 @@
             name="keep",
         )(own, incoming, left, sol)
         if step < ITERS - 1:
-            rounded = []
-            for part in range(parts):
-                sol, left, new = apply(part, sol, left, base, received[part])
-                rounded.append(new)
-    pieces = received[0]
+            sol, left, whole, *rounded = pl.pallas_call(
+                functools.partial(apply_kernel, len(pieces)),
+                out_shape=[field_type, field_type, rounded_type] + [part_type] * parts,
+                in_specs=[in_vmem()] * (5 + len(pieces)),
+                out_specs=[in_vmem()] * (3 + parts),
+                compiler_params=params(),
+                name="apply",
+            )(high, low, left, sol, base, *pieces)
     return pl.pallas_call(
         functools.partial(finish_kernel, len(pieces)),
         out_shape=field_type,

time: 87 us -> 90.5 us (1.040)
  waiting for transfers between devices: 22.7 us -> 40.3 us
  starting transfers between devices: 43.6 us -> 32.8 us
  Pallas kernels: 19.7 us -> 17 us
    ppermute x15 -> x9, waiting for transfers between devices: 6.48 us -> 17.7 us  [per_device(): lax.ppermute(send, 'row', [(chip * CORES + core, partner(chip, shift, chi...]
    ppermute x15 -> x9, starting transfers between devices: 20.6 us -> 12.6 us  [per_device(): lax.ppermute(send, 'row', [(chip * CORES + core, partner(chip, shift, chi...]
    ppermute x6, waiting for transfers between devices: 4.42 us -> 10.5 us  [gather(): sets[step, part] = lax.ppermute(piece, 'col', ring(groups, 2 * step))]
    ppermute x12 -> x9, starting transfers between devices: 11.2 us -> 7.81 us  [the longest x6 5.23 us: forward(): lax.ppermute(sets[index, part], 'col', neighbours(groups))]
    pallas_call x12 -> x8, Pallas kernels: 6.44 us -> 4.69 us  [the longest x3 3.06 us: product_first(): pl.pallas_call(functools.partial(first_kernel, len(pieces), len(outs), ch...]
    ppermute x12 -> x9, waiting for transfers between devices: 6.98 us -> 7.6 us  [the longest x6 7.59 us: forward(): lax.ppermute(sets[index, part], 'col', neighbours(groups))]
  transfers between devices with their start and end apart: 36 -> 27, of which waited for: 15 -> 20; matrix products, arithmetic and copies ran while one was open for 0% -> 0% of each run, Pallas kernels for 17% -> 12%
where the time goes in v8:
time: 90.5 us; the launch traced here: 90.9 us
  waiting for transfers between devices  40.3 us (45%)
  starting transfers between devices  32.8 us (36%)
  Pallas kernels  17 us (19%)
    ppermute x9, waiting for transfers between devices, per_device(): lax.ppermute(send, 'row', [(chip * CORES + core, partner(chip, shift, chi...  17.7 us
    ppermute x9, starting transfers between devices, per_device(): lax.ppermute(send, 'row', [(chip * CORES + core, partner(chip, shift, chi...  12.6 us
    ppermute x6, starting transfers between devices, gather(): sets[step, part] = lax.ppermute(piece, 'col', ring(groups, 2 * step))  11.6 us
    ppermute x6, waiting for transfers between devices, gather(): sets[step, part] = lax.ppermute(piece, 'col', ring(groups, 2 * step))  10.5 us
    ppermute x6, waiting for transfers between devices, forward(): lax.ppermute(sets[index, part], 'col', neighbours(groups))  7.59 us
    ppermute x6, starting transfers between devices, forward(): lax.ppermute(sets[index, part], 'col', neighbours(groups))  5.23 us
    ppermute x3, waiting for transfers between devices, per_device(): incoming = lax.ppermute(outgoing, 'row', neighbours(row_devices))  4.52 us
    pallas_call x1, Pallas kernels, per_device(): pl.pallas_call(functools.partial(order_kernel, group, owned, groups, part...  4.49 us
  transfers between devices with their start and end apart: 27, of which 20 were waited for; matrix products, arithmetic and copies ran while one was open for 0% of the time, Pallas kernels for 12%

profile of v8, /device:TPU:0, one launch (start us, length us, event | category | flops | bytes accessed | tf_op | source)
XLA Modules:
  0.0 90.9 jit_solution(3516131269431587872)
XLA Ops:
  0.0 2.2 %start.1 = (bf16[16,128,128]{2,1,0:T(8,128)(2,1)S(1)}, bf16[16,128,128]{2,1,0:T(8,128)(2,1)S(1)}, f32[16,32,128]{2,1,0:T(8,128)S(1)}, f32[16,32,128]{2,1,0:T(8,1...) custom-call(f32[16,128,128]{2,1,0:T(8,128)} %bitcast.5, ...), custom_call_target="tpu_custom_call" | custom-call | tf_op jit(solution)/shard_map/start/pallas_call | solution.py:361
  2.2 4.1 %collective-permute-start.1 = (bf16[8,32,128]{2,1,0:T(8,128)(2,1)S(1)}, bf16[8,32,128]{2,1,0:T(8,128)(2,1)S(1)}, u32[]{:S(2)}, u32[]{:S(2)}) collective-permute-start(bf16[8,32,128]{2,1,0:T(8,128)(2,1)S(1)} %get-tuple-element.61), channel_id=1, source_target_pairs={{0,2},{1,3},{2,0},{3,1},{4,6},{5,7},{6,4},{7,5},{8,10},{9,11},{10,... | collective-permute-start | bytes 196616 | tf_op jit(solution)/shard_map/ppermute | solution.py:106
  6.3 1.6 %collective-permute-start.3 = (bf16[16,32,128]{2,1,0:T(8,128)(2,1)S(1)}, bf16[16,32,128]{2,1,0:T(8,128)(2,1)S(1)}, u32[]{:S(2)}, u32[]{:S(2)}) collective-permute-start(bf16[16,32,128]{2,1,0:T(8,128)(2,1)S(1)} %get-tuple-element.60.refs_0_), channel_id=1, source_target_pairs={{0,1},{1,0},{2,3},{3,2},{4,5},{5,4},{6,7},{7,6},{8,9},{9,8},{10,11... | collective-permute-start | bytes 393224 | tf_op jit(solution)/shard_map/ppermute | solution.py:107
  9.3 1.8 %collective-permute-start.4 = (bf16[8,32,128]{2,1,0:T(8,128)(2,1)S(1)}, bf16[8,32,128]{2,1,0:T(8,128)(2,1)S(1)}, u32[]{:S(2)}, u32[]{:S(2)}) collective-permute-start(bf16[8,32,128]{2,1,0:T(8,128)(2,1)S(1)} %collective-permute-done.1.refs_1_), channel_id=1, source_target_pairs={{0,1},{1,0},{2,3},{3,2},{4,5},{5,4},{6,7},{7,6},{8,9},{9,8},{10,11... | collective-permute-start | bytes 196616 | tf_op jit(solution)/shard_map/ppermute | solution.py:474
  11.8 4.5 %order.1 = (s32[7,208]{1,0:T(8,128)S(4)}, s32[6]{0:T(128)S(4)}, bf16[192,128,128]{2,1,0:T(8,128)(2,1)S(1)}) custom-call(s32[1,1]{1,0:T(1,128)S(6)} %copy.37.count_ref, s32[1,1,192]{2,1,0:T(1,128)} %rows_hbm.1, s32[1,1,192]{2,1,0:T(1,128)} %cols_hbm.1, bf16[192,128,128]{2,1,0:T(8,128)(2,1)} %bitcast.4), custom_call_target="tpu_custom_call" | custom-call | tf_op jit(solution)/shard_map/order/pallas_call | solution.py:374
  19.2 2.4 %collective-permute-done.2.refs_0_ = bf16[8,32,128]{2,1,0:T(8,128)(2,1)S(1)} collective-permute-done((bf16[8,32,128]{2,1,0:T(8,128)(2,1)S(1)}, bf16[8,32,128]{2,1,0:T(8,128)(2,1)S(1)}, u32[]{:S(2)}, u32[]{:S(2)}) %collective-permute-start.2) | collective-permute-done | bytes 65568 | tf_op jit(solution)/shard_map/ppermute | solution.py:474
  22.8 1.3 %collective-permute-done.5.other_ref.refs_3_.refs_4_ = bf16[64,32,128]{2,1,0:T(8,128)(2,1)S(1)} collective-permute-done((bf16[64,32,128]{2,1,0:T(8,128)(2,1)S(1)}, bf16[64,32,128]{2,1,0:T(8,128)(2,1)S(1)}, u32[]{:S(2)}, u32[]{:S(2)}) %collective-permute-start.5) | collective-permute-done | bytes 524320 | tf_op jit(solution)/shard_map/ppermute | solution.py:486
  24.1 4.9 %collective-permute-start.6 = (bf16[16,32,128]{2,1,0:T(8,128)(2,1)S(1)}, bf16[16,32,128]{2,1,0:T(8,128)(2,1)S(1)}, u32[]{:S(2)}, u32[]{:S(2)}) collective-permute-start(bf16[16,32,128]{2,1,0:T(8,128)(2,1)S(1)} %get-tuple-element.68.refs_6_.refs_8_), channel_id=1, source_target_pairs={{0,24},{4,28},{8,16},{12,20},{16,8},{20,12},{24,0},{28,4},{1,25},{... | collective-permute-start | bytes 393224 | tf_op jit(solution)/shard_map/ppermute | solution.py:493
  29.7 3.2 %collective-permute-done.6.refs_0_ = bf16[16,32,128]{2,1,0:T(8,128)(2,1)S(1)} collective-permute-done((bf16[16,32,128]{2,1,0:T(8,128)(2,1)S(1)}, bf16[16,32,128]{2,1,0:T(8,128)(2,1)S(1)}, u32[]{:S(2)}, u32[]{:S(2)}) %collective-permute-start.6) | collective-permute-done | bytes 131104 | tf_op jit(solution)/shard_map/ppermute | solution.py:493
  32.9 2.7 %collective-permute-done.7.refs_1_ = bf16[16,32,128]{2,1,0:T(8,128)(2,1)S(1)} collective-permute-done((bf16[16,32,128]{2,1,0:T(8,128)(2,1)S(1)}, bf16[16,32,128]{2,1,0:T(8,128)(2,1)S(1)}, u32[]{:S(2)}, u32[]{:S(2)}) %collective-permute-start.7) | collective-permute-done | bytes 131104 | tf_op jit(solution)/shard_map/ppermute | solution.py:493
  36.7 3.9 %collective-permute-start.10 = (bf16[8,32,128]{2,1,0:T(8,128)(2,1)S(1)}, bf16[8,32,128]{2,1,0:T(8,128)(2,1)S(1)}, u32[]{:S(2)}, u32[]{:S(2)}) collective-permute-start(bf16[8,32,128]{2,1,0:T(8,128)(2,1)S(1)} %get-tuple-element.75), channel_id=1, source_target_pairs={{0,2},{1,3},{2,0},{3,1},{4,6},{5,7},{6,4},{7,5},{8,10},{9,11},{10,... | collective-permute-start | bytes 196616 | tf_op jit(solution)/shard_map/ppermute | solution.py:106
  41.7 2.6 %collective-permute-done.10.refs_1_ = bf16[8,32,128]{2,1,0:T(8,128)(2,1)S(1)} collective-permute-done((bf16[8,32,128]{2,1,0:T(8,128)(2,1)S(1)}, bf16[8,32,128]{2,1,0:T(8,128)(2,1)S(1)}, u32[]{:S(2)}, u32[]{:S(2)}) %collective-permute-start.10) | collective-permute-done | bytes 65568 | tf_op jit(solution)/shard_map/ppermute | solution.py:106
  45.8 2.2 %collective-permute-done.9.piece_ref = bf16[8,32,128]{2,1,0:T(8,128)(2,1)S(1)} collective-permute-done((bf16[8,32,128]{2,1,0:T(8,128)(2,1)S(1)}, bf16[8,32,128]{2,1,0:T(8,128)(2,1)S(1)}, u32[]{:S(2)}, u32[]{:S(2)}) %collective-permute-start.9) | collective-permute-done | bytes 65568 | tf_op jit(solution)/shard_map/ppermute | solution.py:106
  48.2 1.6 %collective-permute-done.13.refs_2_ = bf16[8,32,128]{2,1,0:T(8,128)(2,1)S(1)} collective-permute-done((bf16[8,32,128]{2,1,0:T(8,128)(2,1)S(1)}, bf16[8,32,128]{2,1,0:T(8,128)(2,1)S(1)}, u32[]{:S(2)}, u32[]{:S(2)}) %collective-permute-start.13) | collective-permute-done | bytes 65568 | tf_op jit(solution)/shard_map/ppermute | solution.py:474
  50.6 1.6 %collective-permute-done.11.refs_0_ = bf16[8,32,128]{2,1,0:T(8,128)(2,1)S(1)} collective-permute-done((bf16[8,32,128]{2,1,0:T(8,128)(2,1)S(1)}, bf16[8,32,128]{2,1,0:T(8,128)(2,1)S(1)}, u32[]{:S(2)}, u32[]{:S(2)}) %collective-permute-start.11) | collective-permute-done | bytes 65568 | tf_op jit(solution)/shard_map/ppermute | solution.py:474
  53.0 1.6 %collective-permute-done.14.other_ref.refs_5_ = bf16[64,32,128]{2,1,0:T(8,128)(2,1)S(1)} collective-permute-done((bf16[64,32,128]{2,1,0:T(8,128)(2,1)S(1)}, bf16[64,32,128]{2,1,0:T(8,128)(2,1)S(1)}, u32[]{:S(2)}, u32[]{:S(2)}) %collective-permute-start.14) | collective-permute-done | bytes 524320 | tf_op jit(solution)/shard_map/ppermute | solution.py:486
  54.7 1.2 %collective-permute-start.15 = (bf16[16,32,128]{2,1,0:T(8,128)(2,1)S(1)}, bf16[16,32,128]{2,1,0:T(8,128)(2,1)S(1)}, u32[]{:S(2)}, u32[]{:S(2)}) collective-permute-start(bf16[16,32,128]{2,1,0:T(8,128)(2,1)S(1)} %get-tuple-element.82.refs_11_), channel_id=1, source_target_pairs={{0,24},{4,28},{8,16},{12,20},{16,8},{20,12},{24,0},{28,4},{1,25},{... | collective-permute-start | bytes 393224 | tf_op jit(solution)/shard_map/ppermute | solution.py:493
  56.5 1.7 %collective-permute-start.17 = (bf16[16,32,128]{2,1,0:T(8,128)(2,1)S(1)}, bf16[16,32,128]{2,1,0:T(8,128)(2,1)S(1)}, u32[]{:S(2)}, u32[]{:S(2)}) collective-permute-start(bf16[16,32,128]{2,1,0:T(8,128)(2,1)S(1)} %get-tuple-element.84.refs_9_), channel_id=1, source_target_pairs={{0,8},{4,12},{8,0},{12,4},{16,24},{20,28},{24,16},{28,20},{1,9},{5... | collective-permute-start | bytes 393224 | tf_op jit(solution)/shard_map/ppermute | solution.py:493
  58.3 3.7 %collective-permute-done.15.refs_0_ = bf16[16,32,128]{2,1,0:T(8,128)(2,1)S(1)} collective-permute-done((bf16[16,32,128]{2,1,0:T(8,128)(2,1)S(1)}, bf16[16,32,128]{2,1,0:T(8,128)(2,1)S(1)}, u32[]{:S(2)}, u32[]{:S(2)}) %collective-permute-start.15) | collective-permute-done | bytes 131104 | tf_op jit(solution)/shard_map/ppermute | solution.py:493
  62.0 1.9 %collective-permute-done.16.refs_1_ = bf16[16,32,128]{2,1,0:T(8,128)(2,1)S(1)} collective-permute-done((bf16[16,32,128]{2,1,0:T(8,128)(2,1)S(1)}, bf16[16,32,128]{2,1,0:T(8,128)(2,1)S(1)}, u32[]{:S(2)}, u32[]{:S(2)}) %collective-permute-start.16) | collective-permute-done | bytes 131104 | tf_op jit(solution)/shard_map/ppermute | solution.py:493
  64.7 2.6 %collective-permute-start.19 = (bf16[8,32,128]{2,1,0:T(8,128)(2,1)S(1)}, bf16[8,32,128]{2,1,0:T(8,128)(2,1)S(1)}, u32[]{:S(2)}, u32[]{:S(2)}) collective-permute-start(bf16[8,32,128]{2,1,0:T(8,128)(2,1)S(1)} %get-tuple-element.88), channel_id=1, source_target_pairs={{0,2},{1,3},{2,0},{3,1},{4,6},{5,7},{6,4},{7,5},{8,10},{9,11},{10,... | collective-permute-start | bytes 196616 | tf_op jit(solution)/shard_map/ppermute | solution.py:106
  67.9 3.1 %collective-permute-done.19.refs_1_ = bf16[8,32,128]{2,1,0:T(8,128)(2,1)S(1)} collective-permute-done((bf16[8,32,128]{2,1,0:T(8,128)(2,1)S(1)}, bf16[8,32,128]{2,1,0:T(8,128)(2,1)S(1)}, u32[]{:S(2)}, u32[]{:S(2)}) %collective-permute-start.19) | collective-permute-done | bytes 65568 | tf_op jit(solution)/shard_map/ppermute | solution.py:106
  71.0 1.2 %stage0.5 = (f32[65,32,128]{2,1,0:T(8,128)S(1)}, f32[65,32,128]{2,1,0:T(8,128)S(1)}, f32[8,128]{1,0:T(8,128)S(1)}) custom-call(s32[7,208]{1,0:T(8,128)S(4)} %get-tuple-element.56.list_ref, s32[6]{0:T(128)S(4)} %get-tuple-element.57.total_ref, bf16[192,128,128]{2,1,0:T(8,128)(2,1)S(1)} %get-tuple-element.58.values_ref, ...), custom_call_target="tpu_custom_call" | custom-call | flops 75497472 | bytes 2359296 | tf_op jit(solution)/shard_map/stage0/pallas_call | solution.py:401
  72.1 1.5 %collective-permute-done.18.piece_ref = bf16[8,32,128]{2,1,0:T(8,128)(2,1)S(1)} collective-permute-done((bf16[8,32,128]{2,1,0:T(8,128)(2,1)S(1)}, bf16[8,32,128]{2,1,0:T(8,128)(2,1)S(1)}, u32[]{:S(2)}, u32[]{:S(2)}) %collective-permute-start.18) | collective-permute-done | bytes 65568 | tf_op jit(solution)/shard_map/ppermute | solution.py:106
  73.6 1.5 %collective-permute-start.20 = (bf16[8,32,128]{2,1,0:T(8,128)(2,1)S(1)}, bf16[8,32,128]{2,1,0:T(8,128)(2,1)S(1)}, u32[]{:S(2)}, u32[]{:S(2)}) collective-permute-start(bf16[8,32,128]{2,1,0:T(8,128)(2,1)S(1)} %hold.5.refs_1_), channel_id=1, source_target_pairs={{0,1},{1,0},{2,3},{3,2},{4,5},{5,4},{6,7},{7,6},{8,9},{9,8},{10,11... | collective-permute-start | bytes 196616 | tf_op jit(solution)/shard_map/ppermute | solution.py:474
  75.1 1.2 %collective-permute-done.22.refs_2_ = bf16[8,32,128]{2,1,0:T(8,128)(2,1)S(1)} collective-permute-done((bf16[8,32,128]{2,1,0:T(8,128)(2,1)S(1)}, bf16[8,32,128]{2,1,0:T(8,128)(2,1)S(1)}, u32[]{:S(2)}, u32[]{:S(2)}) %collective-permute-start.22) | collective-permute-done | bytes 65568 | tf_op jit(solution)/shard_map/ppermute | solution.py:474
  78.5 1.6 %collective-permute-done.23.other_ref = bf16[64,32,128]{2,1,0:T(8,128)(2,1)S(1)} collective-permute-done((bf16[64,32,128]{2,1,0:T(8,128)(2,1)S(1)}, bf16[64,32,128]{2,1,0:T(8,128)(2,1)S(1)}, u32[]{:S(2)}, u32[]{:S(2)}) %collective-permute-start.23) | collective-permute-done | bytes 524320 | tf_op jit(solution)/shard_map/ppermute | solution.py:486
  80.2 1.5 %collective-permute-start.24 = (bf16[16,32,128]{2,1,0:T(8,128)(2,1)S(1)}, bf16[16,32,128]{2,1,0:T(8,128)(2,1)S(1)}, u32[]{:S(2)}, u32[]{:S(2)}) collective-permute-start(bf16[16,32,128]{2,1,0:T(8,128)(2,1)S(1)} %get-tuple-element.96), channel_id=1, source_target_pairs={{0,24},{4,28},{8,16},{12,20},{16,8},{20,12},{24,0},{28,4},{1,25},{... | collective-permute-start | bytes 393224 | tf_op jit(solution)/shard_map/ppermute | solution.py:493
  81.7 1.3 %collective-permute-start.25 = (bf16[16,32,128]{2,1,0:T(8,128)(2,1)S(1)}, bf16[16,32,128]{2,1,0:T(8,128)(2,1)S(1)}, u32[]{:S(2)}, u32[]{:S(2)}) collective-permute-start(bf16[16,32,128]{2,1,0:T(8,128)(2,1)S(1)} %get-tuple-element.97), channel_id=1, source_target_pairs={{0,16},{4,20},{8,24},{12,28},{16,0},{20,4},{24,8},{28,12},{1,17},{... | collective-permute-start | bytes 393224 | tf_op jit(solution)/shard_map/ppermute | solution.py:493
  83.9 3.7 %collective-permute-done.24.refs_0_ = bf16[16,32,128]{2,1,0:T(8,128)(2,1)S(1)} collective-permute-done((bf16[16,32,128]{2,1,0:T(8,128)(2,1)S(1)}, bf16[16,32,128]{2,1,0:T(8,128)(2,1)S(1)}, u32[]{:S(2)}, u32[]{:S(2)}) %collective-permute-start.24) | collective-permute-done | bytes 131104 | tf_op jit(solution)/shard_map/ppermute | solution.py:493
  87.6 2.0 %collective-permute-done.25.refs_1_ = bf16[16,32,128]{2,1,0:T(8,128)(2,1)S(1)} collective-permute-done((bf16[16,32,128]{2,1,0:T(8,128)(2,1)S(1)}, bf16[16,32,128]{2,1,0:T(8,128)(2,1)S(1)}, u32[]{:S(2)}, u32[]{:S(2)}) %collective-permute-start.25) | collective-permute-done | bytes 131104 | tf_op jit(solution)/shard_map/ppermute | solution.py:493
  89.5 1.4 %finish.1 = f32[16,32,128]{2,1,0:T(8,128)} custom-call(bf16[16,128,128]{2,1,0:T(8,128)(2,1)S(1)} %get-tuple-element.52.high_ref, bf16[16,128,128]{2,1,0:T(8,128)(2,1)S(1)} %get-tuple-element.53.low_ref, f32[16,32,128]{2,1,0:T(8,128)S(1)} %get-tuple-element.85.sol_ref, f32[16,32,128]{2,1,0:T(8,128)S(1)} %keep.5.base_ref, ...), custom_call_target="tpu_custom_call" | custom-call | tf_op jit(solution)/shard_map/finish/pallas_call | solution.py:516
  (48 shorter events, 16.8 us)
Async XLA Ops:
  2.2 7.2 %collective-permute-start.1 = (bf16[8,32,128]{2,1,0:T(8,128)(2,1)S(1)}, bf16[8,32,128]{2,1,0:T(8,128)(2,1)S(1)}, u32[]{:S(2)}, u32[]{:S(2)}) collective-permute-start(bf16[8,32,128]{2,1,0:T(8,128)(2,1)S(1)} %get-tuple-element.61), channel_id=1, source_target_pairs={{0,2},{1,3},{2,0},{3,1},{4,6},{5,7},{6,4},{7,5},{8,10},{9,11},{10,... | collective-permute-start | bytes 196616 | tf_op jit(solution)/shard_map/ppermute | solution.py:106
  6.3 12.1 %collective-permute-start.3 = (bf16[16,32,128]{2,1,0:T(8,128)(2,1)S(1)}, bf16[16,32,128]{2,1,0:T(8,128)(2,1)S(1)}, u32[]{:S(2)}, u32[]{:S(2)}) collective-permute-start(bf16[16,32,128]{2,1,0:T(8,128)(2,1)S(1)} %get-tuple-element.60.refs_0_), channel_id=1, source_target_pairs={{0,1},{1,0},{2,3},{3,2},{4,5},{5,4},{6,7},{7,6},{8,9},{9,8},{10,11... | collective-permute-start | bytes 393224 | tf_op jit(solution)/shard_map/ppermute | solution.py:107
  7.8 9.4 %collective-permute-start = (bf16[8,32,128]{2,1,0:T(8,128)(2,1)S(1)}, bf16[8,32,128]{2,1,0:T(8,128)(2,1)S(1)}, u32[]{:S(2)}, u32[]{:S(2)}) collective-permute-start(bf16[8,32,128]{2,1,0:T(8,128)(2,1)S(1)} %get-tuple-element.59), channel_id=1, source_target_pairs={{0,2},{1,3},{2,0},{3,1},{4,6},{5,7},{6,4},{7,5},{8,10},{9,11},{10,... | collective-permute-start | bytes 196616 | tf_op jit(solution)/shard_map/ppermute | solution.py:106
  9.3 9.1 %collective-permute-start.4 = (bf16[8,32,128]{2,1,0:T(8,128)(2,1)S(1)}, bf16[8,32,128]{2,1,0:T(8,128)(2,1)S(1)}, u32[]{:S(2)}, u32[]{:S(2)}) collective-permute-start(bf16[8,32,128]{2,1,0:T(8,128)(2,1)S(1)} %collective-permute-done.1.refs_1_), channel_id=1, source_target_pairs={{0,1},{1,0},{2,3},{3,2},{4,5},{5,4},{6,7},{7,6},{8,9},{9,8},{10,11... | collective-permute-start | bytes 196616 | tf_op jit(solution)/shard_map/ppermute | solution.py:474
  17.2 4.3 %collective-permute-start.2 = (bf16[8,32,128]{2,1,0:T(8,128)(2,1)S(1)}, bf16[8,32,128]{2,1,0:T(8,128)(2,1)S(1)}, u32[]{:S(2)}, u32[]{:S(2)}) collective-permute-start(bf16[8,32,128]{2,1,0:T(8,128)(2,1)S(1)} %hold.3.refs_1_), channel_id=1, source_target_pairs={{0,1},{1,0},{2,3},{3,2},{4,5},{5,4},{6,7},{7,6},{8,9},{9,8},{10,11... | collective-permute-start | bytes 196616 | tf_op jit(solution)/shard_map/ppermute | solution.py:474
  21.9 2.2 %collective-permute-start.5 = (bf16[64,32,128]{2,1,0:T(8,128)(2,1)S(1)}, bf16[64,32,128]{2,1,0:T(8,128)(2,1)S(1)}, u32[]{:S(2)}, u32[]{:S(2)}) collective-permute-start(bf16[64,32,128]{2,1,0:T(8,128)(2,1)S(1)} %get-tuple-element.67.refs_2_), channel_id=1, source_target_pairs={{0,4},{4,0},{8,12},{12,8},{16,20},{20,16},{24,28},{28,24},{1,5},{5... | collective-permute-start | bytes 1572872 | tf_op jit(solution)/shard_map/ppermute | solution.py:486
  24.1 8.8 %collective-permute-start.6 = (bf16[16,32,128]{2,1,0:T(8,128)(2,1)S(1)}, bf16[16,32,128]{2,1,0:T(8,128)(2,1)S(1)}, u32[]{:S(2)}, u32[]{:S(2)}) collective-permute-start(bf16[16,32,128]{2,1,0:T(8,128)(2,1)S(1)} %get-tuple-element.68.refs_6_.refs_8_), channel_id=1, source_target_pairs={{0,24},{4,28},{8,16},{12,20},{16,8},{20,12},{24,0},{28,4},{1,25},{... | collective-permute-start | bytes 393224 | tf_op jit(solution)/shard_map/ppermute | solution.py:493
  29.0 6.6 %collective-permute-start.7 = (bf16[16,32,128]{2,1,0:T(8,128)(2,1)S(1)}, bf16[16,32,128]{2,1,0:T(8,128)(2,1)S(1)}, u32[]{:S(2)}, u32[]{:S(2)}) collective-permute-start(bf16[16,32,128]{2,1,0:T(8,128)(2,1)S(1)} %get-tuple-element.69.refs_5_.refs_7_), channel_id=1, source_target_pairs={{0,16},{4,20},{8,24},{12,28},{16,0},{20,4},{24,8},{28,12},{1,17},{... | collective-permute-start | bytes 393224 | tf_op jit(solution)/shard_map/ppermute | solution.py:493
  29.0 7.0 %collective-permute-start.8 = (bf16[16,32,128]{2,1,0:T(8,128)(2,1)S(1)}, bf16[16,32,128]{2,1,0:T(8,128)(2,1)S(1)}, u32[]{:S(2)}, u32[]{:S(2)}) collective-permute-start(bf16[16,32,128]{2,1,0:T(8,128)(2,1)S(1)} %get-tuple-element.70.refs_4_.refs_6_), channel_id=1, source_target_pairs={{0,8},{4,12},{8,0},{12,4},{16,24},{20,28},{24,16},{28,20},{1,9},{5... | collective-permute-start | bytes 393224 | tf_op jit(solution)/shard_map/ppermute | solution.py:493
  36.7 7.6 %collective-permute-start.10 = (bf16[8,32,128]{2,1,0:T(8,128)(2,1)S(1)}, bf16[8,32,128]{2,1,0:T(8,128)(2,1)S(1)}, u32[]{:S(2)}, u32[]{:S(2)}) collective-permute-start(bf16[8,32,128]{2,1,0:T(8,128)(2,1)S(1)} %get-tuple-element.75), channel_id=1, source_target_pairs={{0,2},{1,3},{2,0},{3,1},{4,6},{5,7},{6,4},{7,5},{8,10},{9,11},{10,... | collective-permute-start | bytes 196616 | tf_op jit(solution)/shard_map/ppermute | solution.py:106
  40.6 9.2 %collective-permute-start.12 = (bf16[16,32,128]{2,1,0:T(8,128)(2,1)S(1)}, bf16[16,32,128]{2,1,0:T(8,128)(2,1)S(1)}, u32[]{:S(2)}, u32[]{:S(2)}) collective-permute-start(bf16[16,32,128]{2,1,0:T(8,128)(2,1)S(1)} %get-tuple-element.74.refs_0_), channel_id=1, source_target_pairs={{0,1},{1,0},{2,3},{3,2},{4,5},{5,4},{6,7},{7,6},{8,9},{9,8},{10,11... | collective-permute-start | bytes 393224 | tf_op jit(solution)/shard_map/ppermute | solution.py:107
  41.6 6.4 %collective-permute-start.9 = (bf16[8,32,128]{2,1,0:T(8,128)(2,1)S(1)}, bf16[8,32,128]{2,1,0:T(8,128)(2,1)S(1)}, u32[]{:S(2)}, u32[]{:S(2)}) collective-permute-start(bf16[8,32,128]{2,1,0:T(8,128)(2,1)S(1)} %get-tuple-element.73), channel_id=1, source_target_pairs={{0,2},{1,3},{2,0},{3,1},{4,6},{5,7},{6,4},{7,5},{8,10},{9,11},{10,... | collective-permute-start | bytes 196616 | tf_op jit(solution)/shard_map/ppermute | solution.py:106
  44.3 5.6 %collective-permute-start.13 = (bf16[8,32,128]{2,1,0:T(8,128)(2,1)S(1)}, bf16[8,32,128]{2,1,0:T(8,128)(2,1)S(1)}, u32[]{:S(2)}, u32[]{:S(2)}) collective-permute-start(bf16[8,32,128]{2,1,0:T(8,128)(2,1)S(1)} %collective-permute-done.10.refs_1_), channel_id=1, source_target_pairs={{0,1},{1,0},{2,3},{3,2},{4,5},{5,4},{6,7},{7,6},{8,9},{9,8},{10,11... | collective-permute-start | bytes 196616 | tf_op jit(solution)/shard_map/ppermute | solution.py:474
  48.0 4.3 %collective-permute-start.11 = (bf16[8,32,128]{2,1,0:T(8,128)(2,1)S(1)}, bf16[8,32,128]{2,1,0:T(8,128)(2,1)S(1)}, u32[]{:S(2)}, u32[]{:S(2)}) collective-permute-start(bf16[8,32,128]{2,1,0:T(8,128)(2,1)S(1)} %hold.4.refs_1_), channel_id=1, source_target_pairs={{0,1},{1,0},{2,3},{3,2},{4,5},{5,4},{6,7},{7,6},{8,9},{9,8},{10,11... | collective-permute-start | bytes 196616 | tf_op jit(solution)/shard_map/ppermute | solution.py:474
  52.6 2.0 %collective-permute-start.14 = (bf16[64,32,128]{2,1,0:T(8,128)(2,1)S(1)}, bf16[64,32,128]{2,1,0:T(8,128)(2,1)S(1)}, u32[]{:S(2)}, u32[]{:S(2)}) collective-permute-start(bf16[64,32,128]{2,1,0:T(8,128)(2,1)S(1)} %get-tuple-element.81.refs_3_), channel_id=1, source_target_pairs={{0,4},{4,0},{8,12},{12,8},{16,20},{20,16},{24,28},{28,24},{1,5},{5... | collective-permute-start | bytes 1572872 | tf_op jit(solution)/shard_map/ppermute | solution.py:486
  54.7 7.4 %collective-permute-start.15 = (bf16[16,32,128]{2,1,0:T(8,128)(2,1)S(1)}, bf16[16,32,128]{2,1,0:T(8,128)(2,1)S(1)}, u32[]{:S(2)}, u32[]{:S(2)}) collective-permute-start(bf16[16,32,128]{2,1,0:T(8,128)(2,1)S(1)} %get-tuple-element.82.refs_11_), channel_id=1, source_target_pairs={{0,24},{4,28},{8,16},{12,20},{16,8},{20,12},{24,0},{28,4},{1,25},{... | collective-permute-start | bytes 393224 | tf_op jit(solution)/shard_map/ppermute | solution.py:493
  55.9 8.1 %collective-permute-start.16 = (bf16[16,32,128]{2,1,0:T(8,128)(2,1)S(1)}, bf16[16,32,128]{2,1,0:T(8,128)(2,1)S(1)}, u32[]{:S(2)}, u32[]{:S(2)}) collective-permute-start(bf16[16,32,128]{2,1,0:T(8,128)(2,1)S(1)} %get-tuple-element.83.refs_10_), channel_id=1, source_target_pairs={{0,16},{4,20},{8,24},{12,28},{16,0},{20,4},{24,8},{28,12},{1,17},{... | collective-permute-start | bytes 393224 | tf_op jit(solution)/shard_map/ppermute | solution.py:493
  56.5 7.5 %collective-permute-start.17 = (bf16[16,32,128]{2,1,0:T(8,128)(2,1)S(1)}, bf16[16,32,128]{2,1,0:T(8,128)(2,1)S(1)}, u32[]{:S(2)}, u32[]{:S(2)}) collective-permute-start(bf16[16,32,128]{2,1,0:T(8,128)(2,1)S(1)} %get-tuple-element.84.refs_9_), channel_id=1, source_target_pairs={{0,8},{4,12},{8,0},{12,4},{16,24},{20,28},{24,16},{28,20},{1,9},{5... | collective-permute-start | bytes 393224 | tf_op jit(solution)/shard_map/ppermute | solution.py:493
  64.7 6.3 %collective-permute-start.19 = (bf16[8,32,128]{2,1,0:T(8,128)(2,1)S(1)}, bf16[8,32,128]{2,1,0:T(8,128)(2,1)S(1)}, u32[]{:S(2)}, u32[]{:S(2)}) collective-permute-start(bf16[8,32,128]{2,1,0:T(8,128)(2,1)S(1)} %get-tuple-element.88), channel_id=1, source_target_pairs={{0,2},{1,3},{2,0},{3,1},{4,6},{5,7},{6,4},{7,5},{8,10},{9,11},{10,... | collective-permute-start | bytes 196616 | tf_op jit(solution)/shard_map/ppermute | solution.py:106
  67.3 9.0 %collective-permute-start.21 = (bf16[16,32,128]{2,1,0:T(8,128)(2,1)S(1)}, bf16[16,32,128]{2,1,0:T(8,128)(2,1)S(1)}, u32[]{:S(2)}, u32[]{:S(2)}) collective-permute-start(bf16[16,32,128]{2,1,0:T(8,128)(2,1)S(1)} %get-tuple-element.87.refs_0_), channel_id=1, source_target_pairs={{0,1},{1,0},{2,3},{3,2},{4,5},{5,4},{6,7},{7,6},{8,9},{9,8},{10,11... | collective-permute-start | bytes 393224 | tf_op jit(solution)/shard_map/ppermute | solution.py:107
  67.3 6.3 %collective-permute-start.18 = (bf16[8,32,128]{2,1,0:T(8,128)(2,1)S(1)}, bf16[8,32,128]{2,1,0:T(8,128)(2,1)S(1)}, u32[]{:S(2)}, u32[]{:S(2)}) collective-permute-start(bf16[8,32,128]{2,1,0:T(8,128)(2,1)S(1)} %get-tuple-element.86), channel_id=1, source_target_pairs={{0,2},{1,3},{2,0},{3,1},{4,6},{5,7},{6,4},{7,5},{8,10},{9,11},{10,... | collective-permute-start | bytes 196616 | tf_op jit(solution)/shard_map/ppermute | solution.py:106
  71.0 5.4 %collective-permute-start.22 = (bf16[8,32,128]{2,1,0:T(8,128)(2,1)S(1)}, bf16[8,32,128]{2,1,0:T(8,128)(2,1)S(1)}, u32[]{:S(2)}, u32[]{:S(2)}) collective-permute-start(bf16[8,32,128]{2,1,0:T(8,128)(2,1)S(1)} %collective-permute-done.19.refs_1_), channel_id=1, source_target_pairs={{0,1},{1,0},{2,3},{3,2},{4,5},{5,4},{6,7},{7,6},{8,9},{9,8},{10,11... | collective-permute-start | bytes 196616 | tf_op jit(solution)/shard_map/ppermute | solution.py:474
  73.6 4.3 %collective-permute-start.20 = (bf16[8,32,128]{2,1,0:T(8,128)(2,1)S(1)}, bf16[8,32,128]{2,1,0:T(8,128)(2,1)S(1)}, u32[]{:S(2)}, u32[]{:S(2)}) collective-permute-start(bf16[8,32,128]{2,1,0:T(8,128)(2,1)S(1)} %hold.5.refs_1_), channel_id=1, source_target_pairs={{0,1},{1,0},{2,3},{3,2},{4,5},{5,4},{6,7},{7,6},{8,9},{9,8},{10,11... | collective-permute-start | bytes 196616 | tf_op jit(solution)/shard_map/ppermute | solution.py:474
  78.2 2.0 %collective-permute-start.23 = (bf16[64,32,128]{2,1,0:T(8,128)(2,1)S(1)}, bf16[64,32,128]{2,1,0:T(8,128)(2,1)S(1)}, u32[]{:S(2)}, u32[]{:S(2)}) collective-permute-start(bf16[64,32,128]{2,1,0:T(8,128)(2,1)S(1)} %get-tuple-element.94), channel_id=1, source_target_pairs={{0,4},{4,0},{8,12},{12,8},{16,20},{20,16},{24,28},{28,24},{1,5},{5... | collective-permute-start | bytes 1572872 | tf_op jit(solution)/shard_map/ppermute | solution.py:486
  80.2 7.3 %collective-permute-start.24 = (bf16[16,32,128]{2,1,0:T(8,128)(2,1)S(1)}, bf16[16,32,128]{2,1,0:T(8,128)(2,1)S(1)}, u32[]{:S(2)}, u32[]{:S(2)}) collective-permute-start(bf16[16,32,128]{2,1,0:T(8,128)(2,1)S(1)} %get-tuple-element.96), channel_id=1, source_target_pairs={{0,24},{4,28},{8,16},{12,20},{16,8},{20,12},{24,0},{28,4},{1,25},{... | collective-permute-start | bytes 393224 | tf_op jit(solution)/shard_map/ppermute | solution.py:493
  81.7 7.8 %collective-permute-start.25 = (bf16[16,32,128]{2,1,0:T(8,128)(2,1)S(1)}, bf16[16,32,128]{2,1,0:T(8,128)(2,1)S(1)}, u32[]{:S(2)}, u32[]{:S(2)}) collective-permute-start(bf16[16,32,128]{2,1,0:T(8,128)(2,1)S(1)} %get-tuple-element.97), channel_id=1, source_target_pairs={{0,16},{4,20},{8,24},{12,28},{16,0},{20,4},{24,8},{28,12},{1,17},{... | collective-permute-start | bytes 393224 | tf_op jit(solution)/shard_map/ppermute | solution.py:493
  83.0 6.6 %collective-permute-start.26 = (bf16[16,32,128]{2,1,0:T(8,128)(2,1)S(1)}, bf16[16,32,128]{2,1,0:T(8,128)(2,1)S(1)}, u32[]{:S(2)}, u32[]{:S(2)}) collective-permute-start(bf16[16,32,128]{2,1,0:T(8,128)(2,1)S(1)} %get-tuple-element.98), channel_id=1, source_target_pairs={{0,8},{4,12},{8,0},{12,4},{16,24},{20,28},{24,16},{28,20},{1,9},{5... | collective-permute-start | bytes 393224 | tf_op jit(solution)/shard_map/ppermute | solution.py:493

commit v9 on v8

--- a/solution.py
+++ b/solution.py
@@ -11,6 +11,7 @@
 UNROLL = 16
 LANES = 4
 DEPTH = 6
+LAST_FLOPS = 20_000_000_000
 CORES = 2
 VMEM_LIMIT = 24 * 1024 * 1024
 
@@ -174,7 +175,8 @@
 
 
 def order_kernel(group, owned, groups, parts, stages, bits, count_ref, rows_hbm, cols_hbm, values_hbm,
-                 list_out, total_out, values_out, rows_ref, cols_ref, table_ref, total_ref, sems):
+                 list_out, total_out, values_out, token_ref, rows_ref, cols_ref, table_ref, total_ref, sems):
+    token_ref[...] = jnp.zeros_like(token_ref)
     loads = [
         pltpu.make_async_copy(rows_hbm, rows_ref, sems.at[0]),
         pltpu.make_async_copy(cols_hbm, cols_ref, sems.at[1]),
@@ -228,10 +230,15 @@
     lax.fori_loop(0, lists, close, 0)
     loads[2].wait()
 
+
+def turn_kernel(total_ref, values_ref, turned_ref, token_ref):
+    token_ref[...] = jnp.zeros_like(token_ref)
+    used = sum(total_ref[index] for index in range(total_ref.shape[0]))
+
     def turn(chunk, carry):
-        blocks = [values_out[chunk * LANES + lane] for lane in range(LANES)]
+        blocks = [values_ref[chunk * LANES + lane] for lane in range(LANES)]
         for lane, block in enumerate(blocks):
-            values_out[chunk * LANES + lane] = block.T
+            turned_ref[chunk * LANES + lane] = block.T
         return carry
 
     lax.fori_loop(0, lax.div(used + LANES - 1, LANES), turn, 0)
@@ -272,10 +279,25 @@
     return field
 
 
+def swap_order(chips):
+    return list(reversed(range(chips)))
+
+
+def swapped_early(chips):
+    return chips // 2
+
+
+def swapped_rows(index, chips, owned, first_ref, rest_ref):
+    early = swapped_early(chips)
+    if index < early:
+        return first_ref[pl.ds(index * owned, owned)]
+    return rest_ref[pl.ds((index - early) * owned, owned)]
+
+
 def first_kernel(pieces, steps, chips, bits, list_ref, total_ref, values_ref, *refs):
     piece_refs, refs = refs[:pieces], refs[pieces:]
-    out_refs, refs = refs[:steps], refs[steps:]
-    in_refs, refs = refs[:steps], refs[steps:]
+    out_refs, refs = refs[:2 * steps], refs[2 * steps:]
+    in_refs, refs = refs[:2 * steps], refs[2 * steps:]
     sent_refs, totals, (token_ref, field) = refs[:-CORES - 2], refs[-CORES - 2:-2], refs[-2:]
     field_ref = join(piece_refs, field)
     token_ref[...] = jnp.zeros_like(token_ref)
@@ -285,16 +307,18 @@
         owned = rows // chips
         if steps == 0:
             total[...] = jnp.zeros(total.shape, jnp.float32)
-        elif half == 0:
-            total[pl.ds(0, rows)] = -sum(out_ref[...].astype(jnp.float32) for out_ref in out_refs)
         else:
-            for shift in range(chips):
-                at = pl.ds(partner(chip, shift, chips) * owned, owned)
-                value = sum(in_ref[at].astype(jnp.float32) for in_ref in in_refs)
-                if shift > 0:
+            for index, shift in enumerate(swap_order(chips)):
+                swapped = in_refs if half else out_refs
+                value = sum(
+                    swapped_rows(index, chips, owned, *swapped[2 * step:2 * step + 2]).astype(jnp.float32)
+                    for step in range(steps))
+                if half == 0:
+                    value = -value
+                elif shift > 0:
                     for step in range(steps):
-                        value -= sent_refs[step * (chips - 1) + shift - 1][...].astype(jnp.float32)
-                total[at] = value
+                        value -= sent_refs[step * (chips - 1) + index][...].astype(jnp.float32)
+                total[pl.ds(partner(chip, shift, chips) * owned, owned)] = value
         add_products(half, bits, list_ref, total_ref, values_ref, field_ref, total)
 
 
@@ -306,29 +330,42 @@
         add_products(stage * CORES + half, bits, list_ref, total_ref, values_ref, field_ref, total)
 
 
-def last_kernel(stage, half, bits, pieces, list_ref, total_ref, values_ref, *refs):
+def last_kernel(stage, half, bits, pieces, chips, list_ref, total_ref, values_ref, *refs):
     piece_refs, refs = refs[:pieces], refs[pieces + 1:]
-    total, outs, field = refs[0], refs[1:-1], refs[-1]
+    if half == 0:
+        total, out_ref, field = refs
+        other = total
+    else:
+        other, total, out_ref, field = refs
     field_ref = join(piece_refs, field)
     add_products(stage * CORES + half, bits, list_ref, total_ref, values_ref, field_ref, total)
-    for out_ref in outs:
-        out_ref[...] = total[pl.ds(0, out_ref.shape[0])].astype(out_ref.dtype)
-
-
-def chip_rows(shift, chips, own_ref, other_ref):
     chip = lax.axis_index("row") // CORES
-    owned = other_ref.shape[0] // chips
-    at = pl.ds(partner(chip, shift, chips) * owned, owned)
-    return own_ref[at] + other_ref[at].astype(jnp.float32)
-
-
-def combine_kernel(shifts, chips, own_ref, other_ref, *send_refs):
-    for shift, send_ref in zip(shifts, send_refs):
-        send_ref[...] = chip_rows(shift, chips, own_ref, other_ref).astype(send_ref.dtype)
-
-
-def keep_kernel(chips, own_ref, other_ref, left_ref, sol_ref, base_ref):
-    base_ref[...] = left_ref[...] - sol_ref[...] - chip_rows(0, chips, own_ref, other_ref)
+    owned = (other.shape[0] - 1) // chips
+    shifts, early = swap_order(chips), swapped_early(chips)
+    for index, shift in enumerate(shifts[early:] if half else shifts[:early]):
+        rows = other[pl.ds(partner(chip, shift, chips) * owned, owned)]
+        out_ref[pl.ds(index * owned, owned)] = rows.astype(out_ref.dtype)
+
+
+def chip_rows(index, chips, owned, own_ref, *other_refs):
+    chip = lax.axis_index("row") // CORES
+    at = pl.ds(partner(chip, swap_order(chips)[index], chips) * owned, owned)
+    return own_ref[at] + swapped_rows(index, chips, owned, *other_refs).astype(jnp.float32)
+
+
+def combine_first_kernel(chips, own_ref, first_ref, *send_refs):
+    for index, send_ref in enumerate(send_refs):
+        rows = chip_rows(index, chips, send_ref.shape[0], own_ref, first_ref, None)
+        send_ref[...] = rows.astype(send_ref.dtype)
+
+
+def combine_rest_kernel(chips, own_ref, rest_ref, left_ref, sol_ref, base_ref, *send_refs):
+    owned = base_ref.shape[0]
+    for index, send_ref in enumerate(send_refs):
+        rows = chip_rows(swapped_early(chips) + index, chips, owned, own_ref, None, rest_ref)
+        send_ref[...] = rows.astype(send_ref.dtype)
+    keep = chip_rows(chips - 1, chips, owned, own_ref, None, rest_ref)
+    base_ref[...] = left_ref[...] - sol_ref[...] - keep
 
 
 def per_device(block_values, block_rows, block_cols, block_counts, precond, right_side):
@@ -371,15 +408,16 @@
         name="start",
     )(stay_in_hbm(precond[0]), stay_in_hbm(right_side[0]))
 
-    *lists, values = pl.pallas_call(
+    *lists, values, order_token = pl.pallas_call(
         functools.partial(order_kernel, group, owned, groups, parts, stages, bits),
         out_shape=[
             pltpu.SMEM((lists_total + 1, slots + UNROLL), jnp.int32),
             pltpu.SMEM((lists_total,), jnp.int32),
             pltpu.VMEM(block_values.shape[2:], block_values.dtype),
+            token_type,
         ],
         in_specs=[in_smem()] + [in_hbm()] * 3,
-        out_specs=[in_smem()] * 2 + [in_vmem()],
+        out_specs=[in_smem()] * 2 + [in_vmem()] * 2,
         scratch_shapes=[
             index_type, index_type,
             pltpu.SMEM((groups * parts,), jnp.int32), pltpu.SMEM((lists_total + 1,), jnp.int32),
@@ -389,6 +427,16 @@
         name="order",
     )(block_counts, *[stay_in_hbm(array) for array in (block_rows, block_cols, block_values[0, 0])])
 
+    values, turn_token = pl.pallas_call(
+        turn_kernel,
+        out_shape=[pltpu.VMEM(values.shape, values.dtype), token_type],
+        in_specs=[in_smem(), in_vmem()],
+        out_specs=[in_vmem()] * 2,
+        input_output_aliases={1: 0},
+        compiler_params=params(),
+        name="turn",
+    )(lists[1], values)
+
     def cost(share):
         return pl.CostEstimate(
             flops=int(slots * share) * 2 * rhs * size * size,
@@ -399,7 +447,7 @@
 
     def product_first(pieces, outs, ins, sent):
         return pl.pallas_call(
-            functools.partial(first_kernel, len(pieces), len(outs), chips, bits),
+            functools.partial(first_kernel, len(pieces), len(outs) // 2, chips, bits),
             out_shape=[total_type] * CORES + [token_type],
             in_specs=[in_smem()] * 2 + [in_vmem()] * (1 + len(pieces) + len(outs) + len(ins) + len(sent)),
             out_specs=[in_vmem()] * (CORES + 1),
@@ -423,19 +471,20 @@
             name="stage%d" % stage,
         )(*lists, values, *pieces, *totals)
 
-    def product_last(half, pieces, total):
-        send = [jax.ShapeDtypeStruct((half_rows, rhs, size), jnp.bfloat16)] if half == 0 else []
+    def product_last(half, pieces, total, *other):
+        send_chips = chips - swapped_early(chips) if half else swapped_early(chips)
         return pl.pallas_call(
-            functools.partial(last_kernel, final, half, bits, len(pieces)),
-            out_shape=[total_type] + send,
-            in_specs=[in_smem()] * 2 + [in_vmem()] * (2 + len(pieces)),
-            out_specs=[in_vmem()] * (1 + len(send)),
+            functools.partial(last_kernel, final, half, bits, len(pieces), chips),
+            out_shape=[total_type, jax.ShapeDtypeStruct((send_chips * owned, rhs, size), jnp.bfloat16)],
+            in_specs=[in_smem()] * 2 + [in_vmem()] * (2 + len(pieces) + len(other)),
+            out_specs=[in_vmem()] * 2,
             scratch_shapes=[field_scratch(pieces)],
             input_output_aliases={3 + len(pieces): 0},
             compiler_params=params(),
-            cost_estimate=cost(len(stages[final]) / groups / parts / CORES),
+            cost_estimate=pl.CostEstimate(
+                flops=LAST_FLOPS if half else 0, bytes_accessed=0, transcendentals=0),
             name="last%d" % half,
-        )(*lists, values, *pieces, total)[-1]
+        )(*lists, values, *pieces, total, *other)
 
     def hold(piece, token):
         return pl.pallas_call(
@@ -448,17 +497,27 @@
             name="hold",
         )(piece, token)
 
-    shifts = list(reversed(range(1, chips)))
-
-    def combine(own, incoming):
+    early = swapped_early(chips)
+
+    def combine_first(own, first):
         return pl.pallas_call(
-            functools.partial(combine_kernel, shifts, chips),
-            out_shape=[rounded_type] * len(shifts),
+            functools.partial(combine_first_kernel, chips),
+            out_shape=[rounded_type] * early,
             in_specs=[in_vmem()] * 2,
-            out_specs=[in_vmem()] * len(shifts),
+            out_specs=[in_vmem()] * early,
             compiler_params=params(),
-            name="combine",
-        )(own, incoming)
+            name="combine0",
+        )(own, first)
+
+    def combine_rest(own, rest, left, sol):
+        return pl.pallas_call(
+            functools.partial(combine_rest_kernel, chips),
+            out_shape=[field_type] + [rounded_type] * (chips - 1 - early),
+            in_specs=[in_vmem()] * 4,
+            out_specs=[in_vmem()] * (chips - early),
+            compiler_params=params(),
+            name="combine1",
+        )(own, rest, left, sol)
 
     outs, ins, sent = [], [], []
     for step in range(ITERS):
@@ -475,35 +534,30 @@
 
         if groups % 2 == 0:
             for part in range(parts - 1):
-                forward(part)
+                forward(part, order_token if step == 0 else None)
         *totals, token = product_first(stage_pieces(0), outs, ins, sent)
         if groups % 2 == 0:
-            forward(parts - 1, token)
+            forward(parts - 1, turn_token if step == 0 else token)
 
         for stage in range(1, final):
             totals = product_stage(stage, stage_pieces(stage), totals)
-        outgoing = product_last(0, stage_pieces(final), totals[0])
-        incoming = lax.ppermute(outgoing, "row", neighbours(row_devices))
-        own = product_last(1, stage_pieces(final), totals[1])
-        outs.append(outgoing)
-        ins.append(incoming)
-        sends = combine(own, incoming)
-        sent += reversed(sends)
+        other, out_first = product_last(0, stage_pieces(final), totals[0])
+        own, out_rest = product_last(1, stage_pieces(final), totals[1], other)
+        outgoing = [out_first, out_rest]
+        incoming = [lax.ppermute(rows, "row", neighbours(row_devices)) for rows in outgoing]
+        outs += outgoing
+        ins += incoming
+        first = combine_first(own, incoming[0])
+        base, *rest = combine_rest(own, incoming[1], left, sol)
+        sends = list(first) + rest
+        sent += sends
         pieces = [
             lax.ppermute(send, "row", [
                 (chip * CORES + core, partner(chip, shift, chips) * CORES + core)
                 for chip in range(chips) for core in range(CORES)
             ])
-            for shift, send in zip(shifts, sends)
+            for shift, send in zip(swap_order(chips), sends)
         ]
-        base = pl.pallas_call(
-            functools.partial(keep_kernel, chips),
-            out_shape=field_type,
-            in_specs=[in_vmem()] * 4,
-            out_specs=in_vmem(),
-            compiler_params=params(),
-            name="keep",
-        )(own, incoming, left, sol)
         if step < ITERS - 1:
             sol, left, whole, *rounded = pl.pallas_call(
                 functools.partial(apply_kernel, len(pieces)),

time: 90.5 us -> 85.9 us (0.949)
  waiting for transfers between devices: 40.3 us -> 26.7 us
  Pallas kernels: 17 us -> 22 us
  starting transfers between devices: 32.8 us -> 36.2 us
    ppermute x6, waiting for transfers between devices: 10.5 us -> 4.74 us  [gather(): sets[step, part] = lax.ppermute(piece, 'col', ring(groups, 2 * step))]
    ppermute x6, waiting for transfers between devices: 7.59 us -> 1.86 us  [forward(): lax.ppermute(sets[index, part], 'col', neighbours(groups))]
    pallas_call x9 -> x10, Pallas kernels: 3.45 us -> 7.84 us  [the longest x3 4.42 us: product_first(): pl.pallas_call(functools.partial(first_kernel, len(pieces), len(outs) //...]
    ppermute x6, starting transfers between devices: 5.23 us -> 8.44 us  [forward(): lax.ppermute(sets[index, part], 'col', neighbours(groups))]
    ppermute x3 -> x6, waiting for transfers between devices: 4.52 us -> 1.99 us  [per_device(): lax.ppermute(rows, 'row', neighbours(row_devices))]
    pallas_call x3, Pallas kernels: 2.39 us -> 3.93 us  [product_stage(): pl.pallas_call(functools.partial(stage_kernel, stage, bits, len(pieces)),...]
    ppermute x3 -> x6, starting transfers between devices: 0.77 us -> 1.84 us  [per_device(): lax.ppermute(rows, 'row', neighbours(row_devices))]
    pallas_call x1, Pallas kernels: 4.49 us -> 3.45 us  [per_device(): pl.pallas_call(functools.partial(order_kernel, group, owned, groups, part...]
  transfers between devices with their start and end apart: 27 -> 30, of which waited for: 20 -> 19; matrix products, arithmetic and copies ran while one was open for 0% -> 0% of each run, Pallas kernels for 12% -> 19%
where the time goes in v9:
time: 85.9 us; the launch traced here: 85.8 us
  starting transfers between devices  36.2 us (42%)
  waiting for transfers between devices  26.7 us (31%)
  Pallas kernels  22 us (26%)
  between operations  0.86 us (1%)
    ppermute x9, waiting for transfers between devices, per_device(): lax.ppermute(send, 'row', [(chip * CORES + core, partner(chip, shift, chi...  18.1 us
    ppermute x9, starting transfers between devices, per_device(): lax.ppermute(send, 'row', [(chip * CORES + core, partner(chip, shift, chi...  12.2 us
    ppermute x6, starting transfers between devices, gather(): sets[step, part] = lax.ppermute(piece, 'col', ring(groups, 2 * step))  11.1 us
    ppermute x6, starting transfers between devices, forward(): lax.ppermute(sets[index, part], 'col', neighbours(groups))  8.44 us
    ppermute x6, waiting for transfers between devices, gather(): sets[step, part] = lax.ppermute(piece, 'col', ring(groups, 2 * step))  4.74 us
    pallas_call x3, Pallas kernels, product_first(): pl.pallas_call(functools.partial(first_kernel, len(pieces), len(outs) //...  4.42 us
    pallas_call x3, Pallas kernels, product_stage(): pl.pallas_call(functools.partial(stage_kernel, stage, bits, len(pieces)),...  3.93 us
    pallas_call x1, Pallas kernels, per_device(): pl.pallas_call(functools.partial(order_kernel, group, owned, groups, part...  3.45 us
  transfers between devices with their start and end apart: 30, of which 19 were waited for; matrix products, arithmetic and copies ran while one was open for 0% of the time, Pallas kernels for 19%

profile of v9, /device:TPU:0, one launch (start us, length us, event | category | flops | bytes accessed | tf_op | source)
XLA Modules:
  0.0 85.8 jit_solution(5101958821999718456)
XLA Ops:
  0.0 2.2 %start.1 = (bf16[16,128,128]{2,1,0:T(8,128)(2,1)S(1)}, bf16[16,128,128]{2,1,0:T(8,128)(2,1)S(1)}, f32[16,32,128]{2,1,0:T(8,128)S(1)}, f32[16,32,128]{2,1,0:T(8,1...) custom-call(f32[16,128,128]{2,1,0:T(8,128)} %bitcast.5, ...), custom_call_target="tpu_custom_call" | custom-call | tf_op jit(solution)/shard_map/start/pallas_call | solution.py:398
  2.2 4.1 %collective-permute-start.3 = (bf16[8,32,128]{2,1,0:T(8,128)(2,1)S(1)}, bf16[8,32,128]{2,1,0:T(8,128)(2,1)S(1)}, u32[]{:S(2)}, u32[]{:S(2)}) collective-permute-start(bf16[8,32,128]{2,1,0:T(8,128)(2,1)S(1)} %get-tuple-element.77), channel_id=1, source_target_pairs={{0,2},{1,3},{2,0},{3,1},{4,6},{5,7},{6,4},{7,5},{8,10},{9,11},{10,... | collective-permute-start | bytes 196616 | tf_op jit(solution)/shard_map/ppermute | solution.py:107
  6.3 1.6 %collective-permute-start.2 = (bf16[16,32,128]{2,1,0:T(8,128)(2,1)S(1)}, bf16[16,32,128]{2,1,0:T(8,128)(2,1)S(1)}, u32[]{:S(2)}, u32[]{:S(2)}) collective-permute-start(bf16[16,32,128]{2,1,0:T(8,128)(2,1)S(1)} %get-tuple-element.76.refs_0_), channel_id=1, source_target_pairs={{0,1},{1,0},{2,3},{3,2},{4,5},{5,4},{6,7},{7,6},{8,9},{9,8},{10,11... | collective-permute-start | bytes 393224 | tf_op jit(solution)/shard_map/ppermute | solution.py:108
  8.8 3.5 %order.1 = (s32[7,208]{1,0:T(8,128)S(4)}, s32[6]{0:T(128)S(4)}, bf16[192,128,128]{2,1,0:T(8,128)(2,1)S(1)}, f32[8,128]{1,0:T(8,128)S(1)}) custom-call(s32[1,1]{1,0:T(1,128)S(6)} %copy.41.count_ref, s32[1,1,192]{2,1,0:T(1,128)} %rows_hbm.1, s32[1,1,192]{2,1,0:T(1,128)} %cols_hbm.1, bf16[192,128,128]{2,1,0:T(8,128)(2,1)} %bitcast.4), custom_call_target="tpu_custom_call" | custom-call | tf_op jit(solution)/shard_map/order/pallas_call | solution.py:411
  12.7 3.0 %turn.1 = (bf16[192,128,128]{2,1,0:T(8,128)(2,1)S(1)}, f32[8,128]{1,0:T(8,128)S(1)}) custom-call(s32[6]{0:T(128)S(4)} %get-tuple-element.71.total_ref, bf16[192,128,128]{2,1,0:T(8,128)(2,1)S(1)} %get-tuple-element.72.values_ref), custom_call_target="tpu_custom_call", output_to_operand_aliasing={{0}: (1, {})} | custom-call | tf_op jit(solution)/shard_map/turn/pallas_call | solution.py:430
  15.7 1.9 %collective-permute-start.1 = (bf16[8,32,128]{2,1,0:T(8,128)(2,1)S(1)}, bf16[8,32,128]{2,1,0:T(8,128)(2,1)S(1)}, u32[]{:S(2)}, u32[]{:S(2)}) collective-permute-start(bf16[8,32,128]{2,1,0:T(8,128)(2,1)S(1)} %hold.4.refs_1_), channel_id=1, source_target_pairs={{0,1},{1,0},{2,3},{3,2},{4,5},{5,4},{6,7},{7,6},{8,9},{9,8},{10,11... | collective-permute-start | bytes 196616 | tf_op jit(solution)/shard_map/ppermute | solution.py:533
  17.7 1.8 %stage0.3 = (f32[65,32,128]{2,1,0:T(8,128)S(1)}, f32[65,32,128]{2,1,0:T(8,128)S(1)}, f32[8,128]{1,0:T(8,128)}) custom-call(s32[7,208]{1,0:T(8,128)S(4)} %get-tuple-element.70.list_ref, s32[6]{0:T(128)S(4)} %get-tuple-element.71.total_ref, bf16[192,128,128]{2,1,0:T(8,128)(2,1)S(1)} %get-tuple-element.73.values_ref, ...), custom_call_target="tpu_custom_call" | custom-call | flops 75497472 | bytes 2359296 | tf_op jit(solution)/shard_map/stage0/pallas_call | solution.py:449
  19.4 1.3 %stage1.3 = (f32[65,32,128]{2,1,0:T(8,128)S(1)}, f32[65,32,128]{2,1,0:T(8,128)S(1)}) custom-call(s32[7,208]{1,0:T(8,128)S(4)} %get-tuple-element.70.list_ref, s32[6]{0:T(128)S(4)} %get-tuple-element.71.total_ref, bf16[192,128,128]{2,1,0:T(8,128)(2,1)S(1)} %get-tuple-element.73.values_ref, ...), custom_call_target="tpu_custom_call", output_to_operand_aliasing={{0}: (6, {}), {1}: (7, {})} | custom-call | flops 100663296 | bytes 3145728 | tf_op jit(solution)/shard_map/stage1/pallas_call | solution.py:462
  23.6 2.6 %collective-permute-start.8 = (bf16[16,32,128]{2,1,0:T(8,128)(2,1)S(1)}, bf16[16,32,128]{2,1,0:T(8,128)(2,1)S(1)}, u32[]{:S(2)}, u32[]{:S(2)}) collective-permute-start(bf16[16,32,128]{2,1,0:T(8,128)(2,1)S(1)} %get-tuple-element.89.refs_7_.refs_11_), channel_id=1, source_target_pairs={{0,16},{4,20},{8,24},{12,28},{16,0},{20,4},{24,8},{28,12},{1,17},{... | collective-permute-start | bytes 393224 | tf_op jit(solution)/shard_map/ppermute | solution.py:555
  26.3 1.5 %collective-permute-start.9 = (bf16[16,32,128]{2,1,0:T(8,128)(2,1)S(1)}, bf16[16,32,128]{2,1,0:T(8,128)(2,1)S(1)}, u32[]{:S(2)}, u32[]{:S(2)}) collective-permute-start(bf16[16,32,128]{2,1,0:T(8,128)(2,1)S(1)} %get-tuple-element.90.refs_8_.refs_12_), channel_id=1, source_target_pairs={{0,8},{4,12},{8,0},{12,4},{16,24},{20,28},{24,16},{28,20},{1,9},{5... | collective-permute-start | bytes 393224 | tf_op jit(solution)/shard_map/ppermute | solution.py:555
  27.7 1.6 %collective-permute-done.7.refs_0_ = bf16[16,32,128]{2,1,0:T(8,128)(2,1)S(1)} collective-permute-done((bf16[16,32,128]{2,1,0:T(8,128)(2,1)S(1)}, bf16[16,32,128]{2,1,0:T(8,128)(2,1)S(1)}, u32[]{:S(2)}, u32[]{:S(2)}) %collective-permute-start.7) | collective-permute-done | bytes 131104 | tf_op jit(solution)/shard_map/ppermute | solution.py:555
  29.4 2.7 %collective-permute-done.8.refs_1_ = bf16[16,32,128]{2,1,0:T(8,128)(2,1)S(1)} collective-permute-done((bf16[16,32,128]{2,1,0:T(8,128)(2,1)S(1)}, bf16[16,32,128]{2,1,0:T(8,128)(2,1)S(1)}, u32[]{:S(2)}, u32[]{:S(2)}) %collective-permute-start.8) | collective-permute-done | bytes 131104 | tf_op jit(solution)/shard_map/ppermute | solution.py:555
  32.1 1.9 %collective-permute-done.9.refs_2_ = bf16[16,32,128]{2,1,0:T(8,128)(2,1)S(1)} collective-permute-done((bf16[16,32,128]{2,1,0:T(8,128)(2,1)S(1)}, bf16[16,32,128]{2,1,0:T(8,128)(2,1)S(1)}, u32[]{:S(2)}, u32[]{:S(2)}) %collective-permute-start.9) | collective-permute-done | bytes 131104 | tf_op jit(solution)/shard_map/ppermute | solution.py:555
  34.6 1.4 %collective-permute-start.11 = (bf16[8,32,128]{2,1,0:T(8,128)(2,1)S(1)}, bf16[8,32,128]{2,1,0:T(8,128)(2,1)S(1)}, u32[]{:S(2)}, u32[]{:S(2)}) collective-permute-start(bf16[8,32,128]{2,1,0:T(8,128)(2,1)S(1)} %get-tuple-element.95), channel_id=1, source_target_pairs={{0,2},{1,3},{2,0},{3,1},{4,6},{5,7},{6,4},{7,5},{8,10},{9,11},{10,... | collective-permute-start | bytes 196616 | tf_op jit(solution)/shard_map/ppermute | solution.py:107
  37.9 3.2 %collective-permute-done.11.refs_1_ = bf16[8,32,128]{2,1,0:T(8,128)(2,1)S(1)} collective-permute-done((bf16[8,32,128]{2,1,0:T(8,128)(2,1)S(1)}, bf16[8,32,128]{2,1,0:T(8,128)(2,1)S(1)}, u32[]{:S(2)}, u32[]{:S(2)}) %collective-permute-start.11) | collective-permute-done | bytes 65568 | tf_op jit(solution)/shard_map/ppermute | solution.py:107
  41.1 1.2 %stage0.4 = (f32[65,32,128]{2,1,0:T(8,128)S(1)}, f32[65,32,128]{2,1,0:T(8,128)S(1)}, f32[8,128]{1,0:T(8,128)S(1)}) custom-call(s32[7,208]{1,0:T(8,128)S(4)} %get-tuple-element.70.list_ref, s32[6]{0:T(128)S(4)} %get-tuple-element.71.total_ref, bf16[192,128,128]{2,1,0:T(8,128)(2,1)S(1)} %get-tuple-element.73.values_ref, ...), custom_call_target="tpu_custom_call" | custom-call | flops 75497472 | bytes 2359296 | tf_op jit(solution)/shard_map/stage0/pallas_call | solution.py:449
  42.7 2.2 %collective-permute-start.12 = (bf16[8,32,128]{2,1,0:T(8,128)(2,1)S(1)}, bf16[8,32,128]{2,1,0:T(8,128)(2,1)S(1)}, u32[]{:S(2)}, u32[]{:S(2)}) collective-permute-start(bf16[8,32,128]{2,1,0:T(8,128)(2,1)S(1)} %hold.6.refs_1_), channel_id=1, source_target_pairs={{0,1},{1,0},{2,3},{3,2},{4,5},{5,4},{6,7},{7,6},{8,9},{9,8},{10,11... | collective-permute-start | bytes 196616 | tf_op jit(solution)/shard_map/ppermute | solution.py:533
  45.6 1.3 %stage1.4 = (f32[65,32,128]{2,1,0:T(8,128)S(1)}, f32[65,32,128]{2,1,0:T(8,128)S(1)}) custom-call(s32[7,208]{1,0:T(8,128)S(4)} %get-tuple-element.70.list_ref, s32[6]{0:T(128)S(4)} %get-tuple-element.71.total_ref, bf16[192,128,128]{2,1,0:T(8,128)(2,1)S(1)} %get-tuple-element.73.values_ref, ...), custom_call_target="tpu_custom_call", output_to_operand_aliasing={{0}: (6, {}), {1}: (7, {})} | custom-call | flops 100663296 | bytes 3145728 | tf_op jit(solution)/shard_map/stage1/pallas_call | solution.py:462
  49.0 1.9 %collective-permute-start.17 = (bf16[16,32,128]{2,1,0:T(8,128)(2,1)S(1)}, bf16[16,32,128]{2,1,0:T(8,128)(2,1)S(1)}, u32[]{:S(2)}, u32[]{:S(2)}) collective-permute-start(bf16[16,32,128]{2,1,0:T(8,128)(2,1)S(1)} %get-tuple-element.106.refs_13_), channel_id=1, source_target_pairs={{0,24},{4,28},{8,16},{12,20},{16,8},{20,12},{24,0},{28,4},{1,25},{... | collective-permute-start | bytes 393224 | tf_op jit(solution)/shard_map/ppermute | solution.py:555
  51.3 1.4 %collective-permute-start.19 = (bf16[16,32,128]{2,1,0:T(8,128)(2,1)S(1)}, bf16[16,32,128]{2,1,0:T(8,128)(2,1)S(1)}, u32[]{:S(2)}, u32[]{:S(2)}) collective-permute-start(bf16[16,32,128]{2,1,0:T(8,128)(2,1)S(1)} %get-tuple-element.108.refs_15_), channel_id=1, source_target_pairs={{0,8},{4,12},{8,0},{12,4},{16,24},{20,28},{24,16},{28,20},{1,9},{5... | collective-permute-start | bytes 393224 | tf_op jit(solution)/shard_map/ppermute | solution.py:555
  52.8 3.6 %collective-permute-done.17.refs_0_ = bf16[16,32,128]{2,1,0:T(8,128)(2,1)S(1)} collective-permute-done((bf16[16,32,128]{2,1,0:T(8,128)(2,1)S(1)}, bf16[16,32,128]{2,1,0:T(8,128)(2,1)S(1)}, u32[]{:S(2)}, u32[]{:S(2)}) %collective-permute-start.17) | collective-permute-done | bytes 131104 | tf_op jit(solution)/shard_map/ppermute | solution.py:555
  56.3 2.0 %collective-permute-done.18.refs_1_ = bf16[16,32,128]{2,1,0:T(8,128)(2,1)S(1)} collective-permute-done((bf16[16,32,128]{2,1,0:T(8,128)(2,1)S(1)}, bf16[16,32,128]{2,1,0:T(8,128)(2,1)S(1)}, u32[]{:S(2)}, u32[]{:S(2)}) %collective-permute-start.18) | collective-permute-done | bytes 131104 | tf_op jit(solution)/shard_map/ppermute | solution.py:555
  59.2 2.7 %collective-permute-start.21 = (bf16[8,32,128]{2,1,0:T(8,128)(2,1)S(1)}, bf16[8,32,128]{2,1,0:T(8,128)(2,1)S(1)}, u32[]{:S(2)}, u32[]{:S(2)}) collective-permute-start(bf16[8,32,128]{2,1,0:T(8,128)(2,1)S(1)} %get-tuple-element.112), channel_id=1, source_target_pairs={{0,2},{1,3},{2,0},{3,1},{4,6},{5,7},{6,4},{7,5},{8,10},{9,11},{10,... | collective-permute-start | bytes 196616 | tf_op jit(solution)/shard_map/ppermute | solution.py:107
  61.9 1.8 %collective-permute-start.20 = (bf16[8,32,128]{2,1,0:T(8,128)(2,1)S(1)}, bf16[8,32,128]{2,1,0:T(8,128)(2,1)S(1)}, u32[]{:S(2)}, u32[]{:S(2)}) collective-permute-start(bf16[8,32,128]{2,1,0:T(8,128)(2,1)S(1)} %get-tuple-element.110), channel_id=1, source_target_pairs={{0,2},{1,3},{2,0},{3,1},{4,6},{5,7},{6,4},{7,5},{8,10},{9,11},{10,... | collective-permute-start | bytes 196616 | tf_op jit(solution)/shard_map/ppermute | solution.py:107
  64.9 1.8 %collective-permute-start.24 = (bf16[8,32,128]{2,1,0:T(8,128)(2,1)S(1)}, bf16[8,32,128]{2,1,0:T(8,128)(2,1)S(1)}, u32[]{:S(2)}, u32[]{:S(2)}) collective-permute-start(bf16[8,32,128]{2,1,0:T(8,128)(2,1)S(1)} %collective-permute-done.21.refs_1_), channel_id=1, source_target_pairs={{0,1},{1,0},{2,3},{3,2},{4,5},{5,4},{6,7},{7,6},{8,9},{9,8},{10,11... | collective-permute-start | bytes 196616 | tf_op jit(solution)/shard_map/ppermute | solution.py:533
  66.7 1.4 %stage0.5 = (f32[65,32,128]{2,1,0:T(8,128)S(1)}, f32[65,32,128]{2,1,0:T(8,128)S(1)}, f32[8,128]{1,0:T(8,128)S(1)}) custom-call(s32[7,208]{1,0:T(8,128)S(4)} %get-tuple-element.70.list_ref, s32[6]{0:T(128)S(4)} %get-tuple-element.71.total_ref, bf16[192,128,128]{2,1,0:T(8,128)(2,1)S(1)} %get-tuple-element.73.values_ref, ...), custom_call_target="tpu_custom_call" | custom-call | flops 75497472 | bytes 2359296 | tf_op jit(solution)/shard_map/stage0/pallas_call | solution.py:449
  68.1 2.2 %collective-permute-start.22 = (bf16[8,32,128]{2,1,0:T(8,128)(2,1)S(1)}, bf16[8,32,128]{2,1,0:T(8,128)(2,1)S(1)}, u32[]{:S(2)}, u32[]{:S(2)}) collective-permute-start(bf16[8,32,128]{2,1,0:T(8,128)(2,1)S(1)} %hold.7.refs_1_), channel_id=1, source_target_pairs={{0,1},{1,0},{2,3},{3,2},{4,5},{5,4},{6,7},{7,6},{8,9},{9,8},{10,11... | collective-permute-start | bytes 196616 | tf_op jit(solution)/shard_map/ppermute | solution.py:533
  70.8 1.3 %stage1.5 = (f32[65,32,128]{2,1,0:T(8,128)S(1)}, f32[65,32,128]{2,1,0:T(8,128)S(1)}) custom-call(s32[7,208]{1,0:T(8,128)S(4)} %get-tuple-element.70.list_ref, s32[6]{0:T(128)S(4)} %get-tuple-element.71.total_ref, bf16[192,128,128]{2,1,0:T(8,128)(2,1)S(1)} %get-tuple-element.73.values_ref, ...), custom_call_target="tpu_custom_call", output_to_operand_aliasing={{0}: (6, {}), {1}: (7, {})} | custom-call | flops 100663296 | bytes 3145728 | tf_op jit(solution)/shard_map/stage1/pallas_call | solution.py:462
  74.5 1.6 %collective-permute-start.27 = (bf16[16,32,128]{2,1,0:T(8,128)(2,1)S(1)}, bf16[16,32,128]{2,1,0:T(8,128)(2,1)S(1)}, u32[]{:S(2)}, u32[]{:S(2)}) collective-permute-start(bf16[16,32,128]{2,1,0:T(8,128)(2,1)S(1)} %get-tuple-element.124), channel_id=1, source_target_pairs={{0,24},{4,28},{8,16},{12,20},{16,8},{20,12},{24,0},{28,4},{1,25},{... | collective-permute-start | bytes 393224 | tf_op jit(solution)/shard_map/ppermute | solution.py:555
  78.2 3.6 %collective-permute-done.27.refs_0_ = bf16[16,32,128]{2,1,0:T(8,128)(2,1)S(1)} collective-permute-done((bf16[16,32,128]{2,1,0:T(8,128)(2,1)S(1)}, bf16[16,32,128]{2,1,0:T(8,128)(2,1)S(1)}, u32[]{:S(2)}, u32[]{:S(2)}) %collective-permute-start.27) | collective-permute-done | bytes 131104 | tf_op jit(solution)/shard_map/ppermute | solution.py:555
  81.8 2.0 %collective-permute-done.28.refs_1_ = bf16[16,32,128]{2,1,0:T(8,128)(2,1)S(1)} collective-permute-done((bf16[16,32,128]{2,1,0:T(8,128)(2,1)S(1)}, bf16[16,32,128]{2,1,0:T(8,128)(2,1)S(1)}, u32[]{:S(2)}, u32[]{:S(2)}) %collective-permute-start.28) | collective-permute-done | bytes 131104 | tf_op jit(solution)/shard_map/ppermute | solution.py:555
  84.4 1.4 %finish.1 = f32[16,32,128]{2,1,0:T(8,128)} custom-call(bf16[16,128,128]{2,1,0:T(8,128)(2,1)S(1)} %get-tuple-element.66.high_ref, bf16[16,128,128]{2,1,0:T(8,128)(2,1)S(1)} %get-tuple-element.67.low_ref, f32[16,32,128]{2,1,0:T(8,128)S(1)} %get-tuple-element.109.sol_ref, f32[16,32,128]{2,1,0:T(8,128)S(1)} %get-tuple-element.122.base_ref, ...), custom_call_target="tpu_custom_call" | custom-call | tf_op jit(solution)/shard_map/finish/pallas_call | solution.py:570
  (56 shorter events, 17.5 us)
Async XLA Ops:
  2.2 10.1 %collective-permute-start.3 = (bf16[8,32,128]{2,1,0:T(8,128)(2,1)S(1)}, bf16[8,32,128]{2,1,0:T(8,128)(2,1)S(1)}, u32[]{:S(2)}, u32[]{:S(2)}) collective-permute-start(bf16[8,32,128]{2,1,0:T(8,128)(2,1)S(1)} %get-tuple-element.77), channel_id=1, source_target_pairs={{0,2},{1,3},{2,0},{3,1},{4,6},{5,7},{6,4},{7,5},{8,10},{9,11},{10,... | collective-permute-start | bytes 196616 | tf_op jit(solution)/shard_map/ppermute | solution.py:107
  6.3 13.2 %collective-permute-start.2 = (bf16[16,32,128]{2,1,0:T(8,128)(2,1)S(1)}, bf16[16,32,128]{2,1,0:T(8,128)(2,1)S(1)}, u32[]{:S(2)}, u32[]{:S(2)}) collective-permute-start(bf16[16,32,128]{2,1,0:T(8,128)(2,1)S(1)} %get-tuple-element.76.refs_0_), channel_id=1, source_target_pairs={{0,1},{1,0},{2,3},{3,2},{4,5},{5,4},{6,7},{7,6},{8,9},{9,8},{10,11... | collective-permute-start | bytes 393224 | tf_op jit(solution)/shard_map/ppermute | solution.py:108
  7.8 7.9 %collective-permute-start = (bf16[8,32,128]{2,1,0:T(8,128)(2,1)S(1)}, bf16[8,32,128]{2,1,0:T(8,128)(2,1)S(1)}, u32[]{:S(2)}, u32[]{:S(2)}) collective-permute-start(bf16[8,32,128]{2,1,0:T(8,128)(2,1)S(1)} %get-tuple-element.74), channel_id=1, source_target_pairs={{0,2},{1,3},{2,0},{3,1},{4,6},{5,7},{6,4},{7,5},{8,10},{9,11},{10,... | collective-permute-start | bytes 196616 | tf_op jit(solution)/shard_map/ppermute | solution.py:107
  12.3 7.1 %collective-permute-start.4 = (bf16[8,32,128]{2,1,0:T(8,128)(2,1)S(1)}, bf16[8,32,128]{2,1,0:T(8,128)(2,1)S(1)}, u32[]{:S(2)}, u32[]{:S(2)}) collective-permute-start(bf16[8,32,128]{2,1,0:T(8,128)(2,1)S(1)} %hold.5.refs_1_), channel_id=1, source_target_pairs={{0,1},{1,0},{2,3},{3,2},{4,5},{5,4},{6,7},{7,6},{8,9},{9,8},{10,11... | collective-permute-start | bytes 196616 | tf_op jit(solution)/shard_map/ppermute | solution.py:533
  15.7 5.0 %collective-permute-start.1 = (bf16[8,32,128]{2,1,0:T(8,128)(2,1)S(1)}, bf16[8,32,128]{2,1,0:T(8,128)(2,1)S(1)}, u32[]{:S(2)}, u32[]{:S(2)}) collective-permute-start(bf16[8,32,128]{2,1,0:T(8,128)(2,1)S(1)} %hold.4.refs_1_), channel_id=1, source_target_pairs={{0,1},{1,0},{2,3},{3,2},{4,5},{5,4},{6,7},{7,6},{8,9},{9,8},{10,11... | collective-permute-start | bytes 196616 | tf_op jit(solution)/shard_map/ppermute | solution.py:533
  21.1 1.6 %collective-permute-start.6 = (bf16[32,32,128]{2,1,0:T(8,128)(2,1)S(1)}, bf16[32,32,128]{2,1,0:T(8,128)(2,1)S(1)}, u32[]{:S(2)}, u32[]{:S(2)}) collective-permute-start(bf16[32,32,128]{2,1,0:T(8,128)(2,1)S(1)} %get-tuple-element.87.refs_2_), channel_id=1, source_target_pairs={{0,4},{4,0},{8,12},{12,8},{16,20},{20,16},{24,28},{28,24},{1,5},{5... | collective-permute-start | bytes 786440 | tf_op jit(solution)/shard_map/ppermute | solution.py:547
  21.5 4.7 %collective-permute-start.5 = (bf16[32,32,128]{2,1,0:T(8,128)(2,1)S(1)}, bf16[32,32,128]{2,1,0:T(8,128)(2,1)S(1)}, u32[]{:S(2)}, u32[]{:S(2)}) collective-permute-start(bf16[32,32,128]{2,1,0:T(8,128)(2,1)S(1)} %get-tuple-element.85.refs_3_), channel_id=1, source_target_pairs={{0,4},{4,0},{8,12},{12,8},{16,20},{20,16},{24,28},{28,24},{1,5},{5... | collective-permute-start | bytes 786440 | tf_op jit(solution)/shard_map/ppermute | solution.py:547
  22.8 6.6 %collective-permute-start.7 = (bf16[16,32,128]{2,1,0:T(8,128)(2,1)S(1)}, bf16[16,32,128]{2,1,0:T(8,128)(2,1)S(1)}, u32[]{:S(2)}, u32[]{:S(2)}) collective-permute-start(bf16[16,32,128]{2,1,0:T(8,128)(2,1)S(1)} %get-tuple-element.88.refs_6_.refs_10_), channel_id=1, source_target_pairs={{0,24},{4,28},{8,16},{12,20},{16,8},{20,12},{24,0},{28,4},{1,25},{... | collective-permute-start | bytes 393224 | tf_op jit(solution)/shard_map/ppermute | solution.py:555
  23.6 8.5 %collective-permute-start.8 = (bf16[16,32,128]{2,1,0:T(8,128)(2,1)S(1)}, bf16[16,32,128]{2,1,0:T(8,128)(2,1)S(1)}, u32[]{:S(2)}, u32[]{:S(2)}) collective-permute-start(bf16[16,32,128]{2,1,0:T(8,128)(2,1)S(1)} %get-tuple-element.89.refs_7_.refs_11_), channel_id=1, source_target_pairs={{0,16},{4,20},{8,24},{12,28},{16,0},{20,4},{24,8},{28,12},{1,17},{... | collective-permute-start | bytes 393224 | tf_op jit(solution)/shard_map/ppermute | solution.py:555
  26.3 7.7 %collective-permute-start.9 = (bf16[16,32,128]{2,1,0:T(8,128)(2,1)S(1)}, bf16[16,32,128]{2,1,0:T(8,128)(2,1)S(1)}, u32[]{:S(2)}, u32[]{:S(2)}) collective-permute-start(bf16[16,32,128]{2,1,0:T(8,128)(2,1)S(1)} %get-tuple-element.90.refs_8_.refs_12_), channel_id=1, source_target_pairs={{0,8},{4,12},{8,0},{12,4},{16,24},{20,28},{24,16},{28,20},{1,9},{5... | collective-permute-start | bytes 393224 | tf_op jit(solution)/shard_map/ppermute | solution.py:555
  34.6 6.4 %collective-permute-start.11 = (bf16[8,32,128]{2,1,0:T(8,128)(2,1)S(1)}, bf16[8,32,128]{2,1,0:T(8,128)(2,1)S(1)}, u32[]{:S(2)}, u32[]{:S(2)}) collective-permute-start(bf16[8,32,128]{2,1,0:T(8,128)(2,1)S(1)} %get-tuple-element.95), channel_id=1, source_target_pairs={{0,2},{1,3},{2,0},{3,1},{4,6},{5,7},{6,4},{7,5},{8,10},{9,11},{10,... | collective-permute-start | bytes 196616 | tf_op jit(solution)/shard_map/ppermute | solution.py:107
  36.0 9.5 %collective-permute-start.13 = (bf16[16,32,128]{2,1,0:T(8,128)(2,1)S(1)}, bf16[16,32,128]{2,1,0:T(8,128)(2,1)S(1)}, u32[]{:S(2)}, u32[]{:S(2)}) collective-permute-start(bf16[16,32,128]{2,1,0:T(8,128)(2,1)S(1)} %get-tuple-element.94.refs_0_), channel_id=1, source_target_pairs={{0,1},{1,0},{2,3},{3,2},{4,5},{5,4},{6,7},{7,6},{8,9},{9,8},{10,11... | collective-permute-start | bytes 393224 | tf_op jit(solution)/shard_map/ppermute | solution.py:108
  37.1 5.5 %collective-permute-start.10 = (bf16[8,32,128]{2,1,0:T(8,128)(2,1)S(1)}, bf16[8,32,128]{2,1,0:T(8,128)(2,1)S(1)}, u32[]{:S(2)}, u32[]{:S(2)}) collective-permute-start(bf16[8,32,128]{2,1,0:T(8,128)(2,1)S(1)} %get-tuple-element.93), channel_id=1, source_target_pairs={{0,2},{1,3},{2,0},{3,1},{4,6},{5,7},{6,4},{7,5},{8,10},{9,11},{10,... | collective-permute-start | bytes 196616 | tf_op jit(solution)/shard_map/ppermute | solution.py:107
  41.1 4.5 %collective-permute-start.14 = (bf16[8,32,128]{2,1,0:T(8,128)(2,1)S(1)}, bf16[8,32,128]{2,1,0:T(8,128)(2,1)S(1)}, u32[]{:S(2)}, u32[]{:S(2)}) collective-permute-start(bf16[8,32,128]{2,1,0:T(8,128)(2,1)S(1)} %collective-permute-done.11.refs_1_), channel_id=1, source_target_pairs={{0,1},{1,0},{2,3},{3,2},{4,5},{5,4},{6,7},{7,6},{8,9},{9,8},{10,11... | collective-permute-start | bytes 196616 | tf_op jit(solution)/shard_map/ppermute | solution.py:533
  42.7 4.4 %collective-permute-start.12 = (bf16[8,32,128]{2,1,0:T(8,128)(2,1)S(1)}, bf16[8,32,128]{2,1,0:T(8,128)(2,1)S(1)}, u32[]{:S(2)}, u32[]{:S(2)}) collective-permute-start(bf16[8,32,128]{2,1,0:T(8,128)(2,1)S(1)} %hold.6.refs_1_), channel_id=1, source_target_pairs={{0,1},{1,0},{2,3},{3,2},{4,5},{5,4},{6,7},{7,6},{8,9},{9,8},{10,11... | collective-permute-start | bytes 196616 | tf_op jit(solution)/shard_map/ppermute | solution.py:533
  47.4 1.6 %collective-permute-start.16 = (bf16[32,32,128]{2,1,0:T(8,128)(2,1)S(1)}, bf16[32,32,128]{2,1,0:T(8,128)(2,1)S(1)}, u32[]{:S(2)}, u32[]{:S(2)}) collective-permute-start(bf16[32,32,128]{2,1,0:T(8,128)(2,1)S(1)} %get-tuple-element.105.refs_4_), channel_id=1, source_target_pairs={{0,4},{4,0},{8,12},{12,8},{16,20},{20,16},{24,28},{28,24},{1,5},{5... | collective-permute-start | bytes 786440 | tf_op jit(solution)/shard_map/ppermute | solution.py:547
  47.8 3.5 %collective-permute-start.15 = (bf16[32,32,128]{2,1,0:T(8,128)(2,1)S(1)}, bf16[32,32,128]{2,1,0:T(8,128)(2,1)S(1)}, u32[]{:S(2)}, u32[]{:S(2)}) collective-permute-start(bf16[32,32,128]{2,1,0:T(8,128)(2,1)S(1)} %get-tuple-element.103.refs_5_), channel_id=1, source_target_pairs={{0,4},{4,0},{8,12},{12,8},{16,20},{20,16},{24,28},{28,24},{1,5},{5... | collective-permute-start | bytes 786440 | tf_op jit(solution)/shard_map/ppermute | solution.py:547
  49.0 7.3 %collective-permute-start.17 = (bf16[16,32,128]{2,1,0:T(8,128)(2,1)S(1)}, bf16[16,32,128]{2,1,0:T(8,128)(2,1)S(1)}, u32[]{:S(2)}, u32[]{:S(2)}) collective-permute-start(bf16[16,32,128]{2,1,0:T(8,128)(2,1)S(1)} %get-tuple-element.106.refs_13_), channel_id=1, source_target_pairs={{0,24},{4,28},{8,16},{12,20},{16,8},{20,12},{24,0},{28,4},{1,25},{... | collective-permute-start | bytes 393224 | tf_op jit(solution)/shard_map/ppermute | solution.py:555
  50.9 7.4 %collective-permute-start.18 = (bf16[16,32,128]{2,1,0:T(8,128)(2,1)S(1)}, bf16[16,32,128]{2,1,0:T(8,128)(2,1)S(1)}, u32[]{:S(2)}, u32[]{:S(2)}) collective-permute-start(bf16[16,32,128]{2,1,0:T(8,128)(2,1)S(1)} %get-tuple-element.107.refs_14_), channel_id=1, source_target_pairs={{0,16},{4,20},{8,24},{12,28},{16,0},{20,4},{24,8},{28,12},{1,17},{... | collective-permute-start | bytes 393224 | tf_op jit(solution)/shard_map/ppermute | solution.py:555
  51.3 7.1 %collective-permute-start.19 = (bf16[16,32,128]{2,1,0:T(8,128)(2,1)S(1)}, bf16[16,32,128]{2,1,0:T(8,128)(2,1)S(1)}, u32[]{:S(2)}, u32[]{:S(2)}) collective-permute-start(bf16[16,32,128]{2,1,0:T(8,128)(2,1)S(1)} %get-tuple-element.108.refs_15_), channel_id=1, source_target_pairs={{0,8},{4,12},{8,0},{12,4},{16,24},{20,28},{24,16},{28,20},{1,9},{5... | collective-permute-start | bytes 393224 | tf_op jit(solution)/shard_map/ppermute | solution.py:555
  59.2 5.7 %collective-permute-start.21 = (bf16[8,32,128]{2,1,0:T(8,128)(2,1)S(1)}, bf16[8,32,128]{2,1,0:T(8,128)(2,1)S(1)}, u32[]{:S(2)}, u32[]{:S(2)}) collective-permute-start(bf16[8,32,128]{2,1,0:T(8,128)(2,1)S(1)} %get-tuple-element.112), channel_id=1, source_target_pairs={{0,2},{1,3},{2,0},{3,1},{4,6},{5,7},{6,4},{7,5},{8,10},{9,11},{10,... | collective-permute-start | bytes 196616 | tf_op jit(solution)/shard_map/ppermute | solution.py:107
  61.9 8.4 %collective-permute-start.23 = (bf16[16,32,128]{2,1,0:T(8,128)(2,1)S(1)}, bf16[16,32,128]{2,1,0:T(8,128)(2,1)S(1)}, u32[]{:S(2)}, u32[]{:S(2)}) collective-permute-start(bf16[16,32,128]{2,1,0:T(8,128)(2,1)S(1)} %get-tuple-element.111.refs_0_), channel_id=1, source_target_pairs={{0,1},{1,0},{2,3},{3,2},{4,5},{5,4},{6,7},{7,6},{8,9},{9,8},{10,11... | collective-permute-start | bytes 393224 | tf_op jit(solution)/shard_map/ppermute | solution.py:108
  61.9 6.2 %collective-permute-start.20 = (bf16[8,32,128]{2,1,0:T(8,128)(2,1)S(1)}, bf16[8,32,128]{2,1,0:T(8,128)(2,1)S(1)}, u32[]{:S(2)}, u32[]{:S(2)}) collective-permute-start(bf16[8,32,128]{2,1,0:T(8,128)(2,1)S(1)} %get-tuple-element.110), channel_id=1, source_target_pairs={{0,2},{1,3},{2,0},{3,1},{4,6},{5,7},{6,4},{7,5},{8,10},{9,11},{10,... | collective-permute-start | bytes 196616 | tf_op jit(solution)/shard_map/ppermute | solution.py:107
  64.9 6.0 %collective-permute-start.24 = (bf16[8,32,128]{2,1,0:T(8,128)(2,1)S(1)}, bf16[8,32,128]{2,1,0:T(8,128)(2,1)S(1)}, u32[]{:S(2)}, u32[]{:S(2)}) collective-permute-start(bf16[8,32,128]{2,1,0:T(8,128)(2,1)S(1)} %collective-permute-done.21.refs_1_), channel_id=1, source_target_pairs={{0,1},{1,0},{2,3},{3,2},{4,5},{5,4},{6,7},{7,6},{8,9},{9,8},{10,11... | collective-permute-start | bytes 196616 | tf_op jit(solution)/shard_map/ppermute | solution.py:533
  68.1 4.4 %collective-permute-start.22 = (bf16[8,32,128]{2,1,0:T(8,128)(2,1)S(1)}, bf16[8,32,128]{2,1,0:T(8,128)(2,1)S(1)}, u32[]{:S(2)}, u32[]{:S(2)}) collective-permute-start(bf16[8,32,128]{2,1,0:T(8,128)(2,1)S(1)} %hold.7.refs_1_), channel_id=1, source_target_pairs={{0,1},{1,0},{2,3},{3,2},{4,5},{5,4},{6,7},{7,6},{8,9},{9,8},{10,11... | collective-permute-start | bytes 196616 | tf_op jit(solution)/shard_map/ppermute | solution.py:533
  72.8 1.6 %collective-permute-start.26 = (bf16[32,32,128]{2,1,0:T(8,128)(2,1)S(1)}, bf16[32,32,128]{2,1,0:T(8,128)(2,1)S(1)}, u32[]{:S(2)}, u32[]{:S(2)}) collective-permute-start(bf16[32,32,128]{2,1,0:T(8,128)(2,1)S(1)} %get-tuple-element.123), channel_id=1, source_target_pairs={{0,4},{4,0},{8,12},{12,8},{16,20},{20,16},{24,28},{28,24},{1,5},{5... | collective-permute-start | bytes 786440 | tf_op jit(solution)/shard_map/ppermute | solution.py:547
  73.2 4.0 %collective-permute-start.25 = (bf16[32,32,128]{2,1,0:T(8,128)(2,1)S(1)}, bf16[32,32,128]{2,1,0:T(8,128)(2,1)S(1)}, u32[]{:S(2)}, u32[]{:S(2)}) collective-permute-start(bf16[32,32,128]{2,1,0:T(8,128)(2,1)S(1)} %get-tuple-element.120), channel_id=1, source_target_pairs={{0,4},{4,0},{8,12},{12,8},{16,20},{20,16},{24,28},{28,24},{1,5},{5... | collective-permute-start | bytes 786440 | tf_op jit(solution)/shard_map/ppermute | solution.py:547
  74.5 7.3 %collective-permute-start.27 = (bf16[16,32,128]{2,1,0:T(8,128)(2,1)S(1)}, bf16[16,32,128]{2,1,0:T(8,128)(2,1)S(1)}, u32[]{:S(2)}, u32[]{:S(2)}) collective-permute-start(bf16[16,32,128]{2,1,0:T(8,128)(2,1)S(1)} %get-tuple-element.124), channel_id=1, source_target_pairs={{0,24},{4,28},{8,16},{12,20},{16,8},{20,12},{24,0},{28,4},{1,25},{... | collective-permute-start | bytes 393224 | tf_op jit(solution)/shard_map/ppermute | solution.py:555
  76.1 7.7 %collective-permute-start.28 = (bf16[16,32,128]{2,1,0:T(8,128)(2,1)S(1)}, bf16[16,32,128]{2,1,0:T(8,128)(2,1)S(1)}, u32[]{:S(2)}, u32[]{:S(2)}) collective-permute-start(bf16[16,32,128]{2,1,0:T(8,128)(2,1)S(1)} %get-tuple-element.125), channel_id=1, source_target_pairs={{0,16},{4,20},{8,24},{12,28},{16,0},{20,4},{24,8},{28,12},{1,17},{... | collective-permute-start | bytes 393224 | tf_op jit(solution)/shard_map/ppermute | solution.py:555
  77.3 7.1 %collective-permute-start.29 = (bf16[16,32,128]{2,1,0:T(8,128)(2,1)S(1)}, bf16[16,32,128]{2,1,0:T(8,128)(2,1)S(1)}, u32[]{:S(2)}, u32[]{:S(2)}) collective-permute-start(bf16[16,32,128]{2,1,0:T(8,128)(2,1)S(1)} %get-tuple-element.126), channel_id=1, source_target_pairs={{0,8},{4,12},{8,0},{12,4},{16,24},{20,28},{24,16},{28,20},{1,9},{5... | collective-permute-start | bytes 393224 | tf_op jit(solution)/shard_map/ppermute | solution.py:555

commit v10 on v9

--- a/solution.py
+++ b/solution.py
@@ -11,11 +11,12 @@
 UNROLL = 16
 LANES = 4
 DEPTH = 6
-LAST_FLOPS = 20_000_000_000
+HIDE_FLOPS = 20_000_000_000
 CORES = 2
 VMEM_LIMIT = 24 * 1024 * 1024
 
 NT = (((1,), (1,)), ((), ()))
+NN = (((1,), (0,)), ((), ()))
 
 
 def in_vmem():
@@ -147,14 +148,22 @@
             put_rounded(p, value, whole_ref, part_refs)
 
 
-def apply_kernel(pieces, high_ref, low_ref, left_ref, sol_ref, base_ref, *refs):
-    piece_refs, (new_ref, new_left_ref, whole_ref, *part_refs) = refs[:pieces], refs[pieces:]
-    for p in range(sol_ref.shape[0]):
+def apply_kernel(part, parts, pieces, high_ref, low_ref, left_ref, sol_ref, base_ref, *refs):
+    piece_refs, refs = refs[:pieces], refs[pieces:]
+    earlier_refs, refs = refs[:-3 - (part == parts - 1)], refs[-3 - (part == parts - 1):]
+    new_ref, new_left_ref, rounded_ref, *whole_refs = refs
+    each = rounded_ref.shape[0]
+    for whole_ref in whole_refs:
+        for index, earlier_ref in enumerate(earlier_refs):
+            whole_ref[pl.ds(index * each, each)] = earlier_ref[...]
+    for inner in range(each):
+        p = part * each + inner
         received = sum(piece_ref[p].astype(jnp.float32) for piece_ref in piece_refs)
         value = sol_ref[p] + times_block(base_ref[p] - received, high_ref[p], low_ref[p])
         new_ref[p] = value
         new_left_ref[p] = left_ref[p] - received
-        put_rounded(p, value, whole_ref, part_refs)
+        for out_ref, at in [(rounded_ref, inner)] + [(whole_ref, p) for whole_ref in whole_refs]:
+            out_ref[at] = value.astype(jnp.bfloat16)
 
 
 def finish_kernel(pieces, high_ref, low_ref, sol_ref, base_ref, *refs):
@@ -231,20 +240,18 @@
     loads[2].wait()
 
 
-def turn_kernel(total_ref, values_ref, turned_ref, token_ref):
-    token_ref[...] = jnp.zeros_like(token_ref)
+def turn_kernel(total_ref, values_ref, base_ref, turned_ref, same_ref):
     used = sum(total_ref[index] for index in range(total_ref.shape[0]))
 
     def turn(chunk, carry):
-        blocks = [values_ref[chunk * LANES + lane] for lane in range(LANES)]
-        for lane, block in enumerate(blocks):
-            turned_ref[chunk * LANES + lane] = block.T
+        for lane in range(LANES):
+            turned_ref[chunk * LANES + lane] = values_ref[chunk * LANES + lane].T
         return carry
 
     lax.fori_loop(0, lax.div(used + LANES - 1, LANES), turn, 0)
 
 
-def add_products(which, bits, list_ref, total_ref, values_ref, field_ref, total):
+def add_products(which, bits, dims, list_ref, total_ref, values_ref, field_ref, total):
     row_bits, col_bits = bits
 
     def step(chunk, carry):
@@ -258,7 +265,7 @@
             col = entry & ((1 << col_bits) - 1)
             row = lax.shift_right_logical(entry, col_bits) & ((1 << row_bits) - 1)
             slot = lax.shift_right_logical(entry, col_bits + row_bits)
-            term = jnp.dot(field_ref[col], values_ref[slot], preferred_element_type=jnp.float32)
+            term = lax.dot_general(field_ref[col], values_ref[slot], dims, preferred_element_type=jnp.float32)
             terms.append((row, term))
             if len(terms) > DEPTH:
                 store(*terms.pop(0))
@@ -284,7 +291,7 @@
 
 
 def swapped_early(chips):
-    return chips // 2
+    return chips - 1
 
 
 def swapped_rows(index, chips, owned, first_ref, rest_ref):
@@ -294,7 +301,7 @@
     return rest_ref[pl.ds((index - early) * owned, owned)]
 
 
-def first_kernel(pieces, steps, chips, bits, list_ref, total_ref, values_ref, *refs):
+def first_kernel(pieces, steps, chips, bits, dims, list_ref, total_ref, values_ref, *refs):
     piece_refs, refs = refs[:pieces], refs[pieces:]
     out_refs, refs = refs[:2 * steps], refs[2 * steps:]
     in_refs, refs = refs[:2 * steps], refs[2 * steps:]
@@ -319,18 +326,18 @@
                     for step in range(steps):
                         value -= sent_refs[step * (chips - 1) + index][...].astype(jnp.float32)
                 total[pl.ds(partner(chip, shift, chips) * owned, owned)] = value
-        add_products(half, bits, list_ref, total_ref, values_ref, field_ref, total)
-
-
-def stage_kernel(stage, bits, pieces, list_ref, total_ref, values_ref, *refs):
+        add_products(half, bits, dims, list_ref, total_ref, values_ref, field_ref, total)
+
+
+def stage_kernel(stage, bits, dims, pieces, list_ref, total_ref, values_ref, *refs):
     piece_refs, refs = refs[:pieces], refs[pieces + CORES:]
     totals, field = refs[:CORES], refs[-1]
     field_ref = join(piece_refs, field)
     for half, total in enumerate(totals):
-        add_products(stage * CORES + half, bits, list_ref, total_ref, values_ref, field_ref, total)
-
-
-def last_kernel(stage, half, bits, pieces, chips, list_ref, total_ref, values_ref, *refs):
+        add_products(stage * CORES + half, bits, dims, list_ref, total_ref, values_ref, field_ref, total)
+
+
+def last_kernel(stage, half, bits, dims, pieces, chips, list_ref, total_ref, values_ref, *refs):
     piece_refs, refs = refs[:pieces], refs[pieces + 1:]
     if half == 0:
         total, out_ref, field = refs
@@ -338,7 +345,7 @@
     else:
         other, total, out_ref, field = refs
     field_ref = join(piece_refs, field)
-    add_products(stage * CORES + half, bits, list_ref, total_ref, values_ref, field_ref, total)
+    add_products(stage * CORES + half, bits, dims, list_ref, total_ref, values_ref, field_ref, total)
     chip = lax.axis_index("row") // CORES
     owned = (other.shape[0] - 1) // chips
     shifts, early = swap_order(chips), swapped_early(chips)
@@ -359,7 +366,7 @@
         send_ref[...] = rows.astype(send_ref.dtype)
 
 
-def combine_rest_kernel(chips, own_ref, rest_ref, left_ref, sol_ref, base_ref, *send_refs):
+def combine_rest_kernel(chips, own_ref, rest_ref, left_ref, sol_ref, before_ref, base_ref, *send_refs):
     owned = base_ref.shape[0]
     for index, send_ref in enumerate(send_refs):
         rows = chip_rows(swapped_early(chips) + index, chips, owned, own_ref, None, rest_ref)
@@ -427,15 +434,17 @@
         name="order",
     )(block_counts, *[stay_in_hbm(array) for array in (block_rows, block_cols, block_values[0, 0])])
 
-    values, turn_token = pl.pallas_call(
-        turn_kernel,
-        out_shape=[pltpu.VMEM(values.shape, values.dtype), token_type],
-        in_specs=[in_smem(), in_vmem()],
-        out_specs=[in_vmem()] * 2,
-        input_output_aliases={1: 0},
-        compiler_params=params(),
-        name="turn",
-    )(lists[1], values)
+    def turn(values, base):
+        return pl.pallas_call(
+            turn_kernel,
+            out_shape=[pltpu.VMEM(values.shape, values.dtype), field_type],
+            in_specs=[in_smem()] + [in_vmem()] * 2,
+            out_specs=[in_vmem()] * 2,
+            input_output_aliases={2: 1},
+            compiler_params=params(),
+            cost_estimate=pl.CostEstimate(flops=HIDE_FLOPS, bytes_accessed=0, transcendentals=0),
+            name="turn",
+        )(lists[1], values, base)
 
     def cost(share):
         return pl.CostEstimate(
@@ -445,9 +454,9 @@
     def field_scratch(pieces):
         return pltpu.VMEM((sum(piece.shape[0] for piece in pieces), rhs, size), jnp.bfloat16)
 
-    def product_first(pieces, outs, ins, sent):
-        return pl.pallas_call(
-            functools.partial(first_kernel, len(pieces), len(outs) // 2, chips, bits),
+    def product_first(values, dims, pieces, outs, ins, sent):
+        return pl.pallas_call(
+            functools.partial(first_kernel, len(pieces), len(outs) // 2, chips, bits, dims),
             out_shape=[total_type] * CORES + [token_type],
             in_specs=[in_smem()] * 2 + [in_vmem()] * (1 + len(pieces) + len(outs) + len(ins) + len(sent)),
             out_specs=[in_vmem()] * (CORES + 1),
@@ -457,10 +466,10 @@
             name="stage0",
         )(*lists, values, *pieces, *outs, *ins, *sent)
 
-    def product_stage(stage, pieces, totals):
+    def product_stage(values, dims, stage, pieces, totals):
         inputs = 3 + len(pieces)
         return pl.pallas_call(
-            functools.partial(stage_kernel, stage, bits, len(pieces)),
+            functools.partial(stage_kernel, stage, bits, dims, len(pieces)),
             out_shape=[total_type] * CORES,
             in_specs=[in_smem()] * 2 + [in_vmem()] * (1 + len(pieces) + CORES),
             out_specs=[in_vmem()] * CORES,
@@ -471,10 +480,10 @@
             name="stage%d" % stage,
         )(*lists, values, *pieces, *totals)
 
-    def product_last(half, pieces, total, *other):
+    def product_last(values, dims, half, pieces, total, *other):
         send_chips = chips - swapped_early(chips) if half else swapped_early(chips)
         return pl.pallas_call(
-            functools.partial(last_kernel, final, half, bits, len(pieces), chips),
+            functools.partial(last_kernel, final, half, bits, dims, len(pieces), chips),
             out_shape=[total_type, jax.ShapeDtypeStruct((send_chips * owned, rhs, size), jnp.bfloat16)],
             in_specs=[in_smem()] * 2 + [in_vmem()] * (2 + len(pieces) + len(other)),
             out_specs=[in_vmem()] * 2,
@@ -482,7 +491,7 @@
             input_output_aliases={3 + len(pieces): 0},
             compiler_params=params(),
             cost_estimate=pl.CostEstimate(
-                flops=LAST_FLOPS if half else 0, bytes_accessed=0, transcendentals=0),
+                flops=HIDE_FLOPS if half else 0, bytes_accessed=0, transcendentals=0),
             name="last%d" % half,
         )(*lists, values, *pieces, total, *other)
 
@@ -509,16 +518,30 @@
             name="combine0",
         )(own, first)
 
-    def combine_rest(own, rest, left, sol):
+    def combine_rest(own, rest, left, sol, before):
         return pl.pallas_call(
             functools.partial(combine_rest_kernel, chips),
             out_shape=[field_type] + [rounded_type] * (chips - 1 - early),
-            in_specs=[in_vmem()] * 4,
+            in_specs=[in_vmem()] * 5,
             out_specs=[in_vmem()] * (chips - early),
             compiler_params=params(),
             name="combine1",
-        )(own, rest, left, sol)
-
+        )(own, rest, left, sol, before)
+
+    def apply(part, sol, left, base, pieces, earlier):
+        last = part == parts - 1
+        return pl.pallas_call(
+            functools.partial(apply_kernel, part, parts, len(pieces)),
+            out_shape=[field_type, field_type, part_type] + [rounded_type] * last,
+            in_specs=[in_vmem()] * (5 + len(pieces) + len(earlier)),
+            out_specs=[in_vmem()] * (3 + last),
+            input_output_aliases={2: 1, 3: 0},
+            compiler_params=params(),
+            cost_estimate=pl.CostEstimate(flops=HIDE_FLOPS, bytes_accessed=0, transcendentals=0),
+            name="apply%d" % part,
+        )(high, low, left, sol, base, *pieces, *earlier)
+
+    blocks = values, NT
     outs, ins, sent = [], [], []
     for step in range(ITERS):
         sets = gather(whole, rounded, groups)
@@ -535,20 +558,20 @@
         if groups % 2 == 0:
             for part in range(parts - 1):
                 forward(part, order_token if step == 0 else None)
-        *totals, token = product_first(stage_pieces(0), outs, ins, sent)
+        *totals, token = product_first(*blocks, stage_pieces(0), outs, ins, sent)
         if groups % 2 == 0:
-            forward(parts - 1, turn_token if step == 0 else token)
+            forward(parts - 1, order_token if step == 0 else token)
 
         for stage in range(1, final):
-            totals = product_stage(stage, stage_pieces(stage), totals)
-        other, out_first = product_last(0, stage_pieces(final), totals[0])
-        own, out_rest = product_last(1, stage_pieces(final), totals[1], other)
+            totals = product_stage(*blocks, stage, stage_pieces(stage), totals)
+        other, out_first = product_last(*blocks, 0, stage_pieces(final), totals[0])
+        own, out_rest = product_last(*blocks, 1, stage_pieces(final), totals[1], other)
         outgoing = [out_first, out_rest]
         incoming = [lax.ppermute(rows, "row", neighbours(row_devices)) for rows in outgoing]
         outs += outgoing
         ins += incoming
         first = combine_first(own, incoming[0])
-        base, *rest = combine_rest(own, incoming[1], left, sol)
+        base, *rest = combine_rest(own, incoming[1], left, sol, first[-1])
         sends = list(first) + rest
         sent += sends
         pieces = [
@@ -558,15 +581,15 @@
             ])
             for shift, send in zip(swap_order(chips), sends)
         ]
+        if step == 0:
+            turned, base = turn(values, base)
+            blocks = turned, NN
         if step < ITERS - 1:
-            sol, left, whole, *rounded = pl.pallas_call(
-                functools.partial(apply_kernel, len(pieces)),
-                out_shape=[field_type, field_type, rounded_type] + [part_type] * parts,
-                in_specs=[in_vmem()] * (5 + len(pieces)),
-                out_specs=[in_vmem()] * (3 + parts),
-                compiler_params=params(),
-                name="apply",
-            )(high, low, left, sol, base, *pieces)
+            rounded = []
+            for part in range(parts):
+                sol, left, new, *done = apply(part, sol, left, base, pieces, rounded if part == parts - 1 else [])
+                rounded.append(new)
+            whole, = done
     return pl.pallas_call(
         functools.partial(finish_kernel, len(pieces)),
         out_shape=field_type,

time: 85.9 us -> 84.6 us (0.985)
  Pallas kernels: 22 us -> 28.5 us
  waiting for transfers between devices: 26.7 us -> 21.3 us
  starting transfers between devices: 36.2 us -> 34.3 us
    ppermute x9, waiting for transfers between devices: 18.1 us -> 12.9 us  [per_device(): lax.ppermute(send, 'row', [(chip * CORES + core, partner(chip, shift, chi...]
    pallas_call x12 -> x14, Pallas kernels: 10.2 us -> 14.3 us  [the longest x3 6.43 us: product_stage(): pl.pallas_call(functools.partial(stage_kernel, stage, bits, dims, len(pie...]
    ppermute x3, starting transfers between devices: 2.72 us -> 4.57 us  [gather(): sets[groups // 2, 0] = lax.ppermute(whole, 'col', neighbours(groups))]
    ppermute x9, starting transfers between devices: 12.2 us -> 10.7 us  [per_device(): lax.ppermute(send, 'row', [(chip * CORES + core, partner(chip, shift, chi...]
    pallas_call x3, Pallas kernels: 4.42 us -> 5.87 us  [product_first(): pl.pallas_call(functools.partial(first_kernel, len(pieces), len(outs) //...]
    ppermute x6, starting transfers between devices: 8.44 us -> 7.24 us  [forward(): lax.ppermute(sets[index, part], 'col', neighbours(groups))]
    ppermute x6, starting transfers between devices: 11.1 us -> 9.99 us  [gather(): sets[step, part] = lax.ppermute(piece, 'col', ring(groups, 2 * step))]
    pallas_call x1, Pallas kernels: 3.45 us -> 4.37 us  [per_device(): pl.pallas_call(functools.partial(order_kernel, group, owned, groups, part...]
  transfers between devices with their start and end apart: 30 -> 30, of which waited for: 19 -> 14; matrix products, arithmetic and copies ran while one was open for 0% -> 0% of each run, Pallas kernels for 19% -> 27%
where the time goes in v10:
time: 84.6 us; the launch traced here: 85 us
  starting transfers between devices  34.3 us (41%)
  Pallas kernels  28.5 us (34%)
  waiting for transfers between devices  21.3 us (25%)
  between operations  0.88 us (1%)
    ppermute x9, waiting for transfers between devices, per_device(): lax.ppermute(send, 'row', [(chip * CORES + core, partner(chip, shift, chi...  12.9 us
    ppermute x9, starting transfers between devices, per_device(): lax.ppermute(send, 'row', [(chip * CORES + core, partner(chip, shift, chi...  10.7 us
    ppermute x6, starting transfers between devices, gather(): sets[step, part] = lax.ppermute(piece, 'col', ring(groups, 2 * step))  9.99 us
    ppermute x6, starting transfers between devices, forward(): lax.ppermute(sets[index, part], 'col', neighbours(groups))  7.24 us
    pallas_call x3, Pallas kernels, product_stage(): pl.pallas_call(functools.partial(stage_kernel, stage, bits, dims, len(pie...  6.43 us
    pallas_call x3, Pallas kernels, product_first(): pl.pallas_call(functools.partial(first_kernel, len(pieces), len(outs) //...  5.87 us
    ppermute x6, waiting for transfers between devices, gather(): sets[step, part] = lax.ppermute(piece, 'col', ring(groups, 2 * step))  4.9 us
    ppermute x3, starting transfers between devices, gather(): sets[groups // 2, 0] = lax.ppermute(whole, 'col', neighbours(groups))  4.57 us
  transfers between devices with their start and end apart: 30, of which 14 were waited for; matrix products, arithmetic and copies ran while one was open for 0% of the time, Pallas kernels for 27%

profile of v10, /device:TPU:0, one launch (start us, length us, event | category | flops | bytes accessed | tf_op | source)
XLA Modules:
  0.0 85.0 jit_solution(13234976399992087136)
XLA Ops:
  0.0 2.2 %start.1 = (bf16[16,128,128]{2,1,0:T(8,128)(2,1)S(1)}, bf16[16,128,128]{2,1,0:T(8,128)(2,1)S(1)}, f32[16,32,128]{2,1,0:T(8,128)S(1)}, f32[16,32,128]{2,1,0:T(8,1...) custom-call(f32[16,128,128]{2,1,0:T(8,128)} %bitcast.5, ...), custom_call_target="tpu_custom_call" | custom-call | tf_op jit(solution)/shard_map/start/pallas_call | solution.py:405
  2.2 4.1 %collective-permute-start.3 = (bf16[8,32,128]{2,1,0:T(8,128)(2,1)S(1)}, bf16[8,32,128]{2,1,0:T(8,128)(2,1)S(1)}, u32[]{:S(2)}, u32[]{:S(2)}) collective-permute-start(bf16[8,32,128]{2,1,0:T(8,128)(2,1)S(1)} %get-tuple-element.77), channel_id=1, source_target_pairs={{0,2},{1,3},{2,0},{3,1},{4,6},{5,7},{6,4},{7,5},{8,10},{9,11},{10,... | collective-permute-start | bytes 196616 | tf_op jit(solution)/shard_map/ppermute | solution.py:108
  6.3 1.6 %collective-permute-start.2 = (bf16[16,32,128]{2,1,0:T(8,128)(2,1)S(1)}, bf16[16,32,128]{2,1,0:T(8,128)(2,1)S(1)}, u32[]{:S(2)}, u32[]{:S(2)}) collective-permute-start(bf16[16,32,128]{2,1,0:T(8,128)(2,1)S(1)} %get-tuple-element.76.refs_0_), channel_id=1, source_target_pairs={{0,1},{1,0},{2,3},{3,2},{4,5},{5,4},{6,7},{7,6},{8,9},{9,8},{10,11... | collective-permute-start | bytes 393224 | tf_op jit(solution)/shard_map/ppermute | solution.py:109
  8.8 4.4 %order.1 = (s32[7,208]{1,0:T(8,128)S(4)}, s32[6]{0:T(128)S(4)}, bf16[192,128,128]{2,1,0:T(8,128)(2,1)S(1)}, f32[8,128]{1,0:T(8,128)S(1)}) custom-call(s32[1,1]{1,0:T(1,128)S(6)} %copy.57.count_ref, s32[1,1,192]{2,1,0:T(1,128)} %rows_hbm.1, s32[1,1,192]{2,1,0:T(1,128)} %cols_hbm.1, bf16[192,128,128]{2,1,0:T(8,128)(2,1)} %bitcast.4), custom_call_target="tpu_custom_call" | custom-call | tf_op jit(solution)/shard_map/order/pallas_call | solution.py:418
  13.8 1.5 %collective-permute-start.1 = (bf16[8,32,128]{2,1,0:T(8,128)(2,1)S(1)}, bf16[8,32,128]{2,1,0:T(8,128)(2,1)S(1)}, u32[]{:S(2)}, u32[]{:S(2)}) collective-permute-start(bf16[8,32,128]{2,1,0:T(8,128)(2,1)S(1)} %hold.4.refs_1_), channel_id=1, source_target_pairs={{0,1},{1,0},{2,3},{3,2},{4,5},{5,4},{6,7},{7,6},{8,9},{9,8},{10,11... | collective-permute-start | bytes 196616 | tf_op jit(solution)/shard_map/ppermute | solution.py:556
  15.3 2.7 %stage0.3 = (f32[65,32,128]{2,1,0:T(8,128)S(1)}, f32[65,32,128]{2,1,0:T(8,128)S(1)}, f32[8,128]{1,0:T(8,128)}) custom-call(s32[7,208]{1,0:T(8,128)S(4)} %get-tuple-element.73.list_ref, s32[6]{0:T(128)S(4)} %get-tuple-element.71.total_ref, bf16[192,128,128]{2,1,0:T(8,128)(2,1)S(1)} %get-tuple-element.72.values_ref, ...), custom_call_target="tpu_custom_call" | custom-call | flops 75497472 | bytes 2359296 | tf_op jit(solution)/shard_map/stage0/pallas_call | solution.py:458
  18.1 2.8 %stage1.3 = (f32[65,32,128]{2,1,0:T(8,128)S(1)}, f32[65,32,128]{2,1,0:T(8,128)S(1)}) custom-call(s32[7,208]{1,0:T(8,128)S(4)} %get-tuple-element.73.list_ref, s32[6]{0:T(128)S(4)} %get-tuple-element.71.total_ref, bf16[192,128,128]{2,1,0:T(8,128)(2,1)S(1)} %get-tuple-element.72.values_ref, ...), custom_call_target="tpu_custom_call", output_to_operand_aliasing={{0}: (6, {}), {1}: (7, {})} | custom-call | flops 100663296 | bytes 3145728 | tf_op jit(solution)/shard_map/stage1/pallas_call | solution.py:471
  23.3 3.4 %collective-permute-start.8 = (bf16[16,32,128]{2,1,0:T(8,128)(2,1)S(1)}, bf16[16,32,128]{2,1,0:T(8,128)(2,1)S(1)}, u32[]{:S(2)}, u32[]{:S(2)}) collective-permute-start(bf16[16,32,128]{2,1,0:T(8,128)(2,1)S(1)} %get-tuple-element.89.refs_7_.refs_11_), channel_id=1, source_target_pairs={{0,16},{4,20},{8,24},{12,28},{16,0},{20,4},{24,8},{28,12},{1,17},{... | collective-permute-start | bytes 393224 | tf_op jit(solution)/shard_map/ppermute | solution.py:578
  26.8 4.1 %turn.1 = (bf16[192,128,128]{2,1,0:T(8,128)(2,1)S(1)}, f32[16,32,128]{2,1,0:T(8,128)S(1)}) custom-call(s32[6]{0:T(128)S(4)} %get-tuple-element.71.total_ref, bf16[192,128,128]{2,1,0:T(8,128)(2,1)S(1)} %get-tuple-element.72.values_ref, f32[16,32,128]{2,1,0:T(8,128)S(1)} %combine1.3.base_ref), custom_call_target="tpu_custom_call", output_to_operand_aliasing={{1}: (2, {})} | custom-call | flops 20000000000 | tf_op jit(solution)/shard_map/turn/pallas_call | solution.py:438
  31.0 1.5 %collective-permute-done.8.refs_1_ = bf16[16,32,128]{2,1,0:T(8,128)(2,1)S(1)} collective-permute-done((bf16[16,32,128]{2,1,0:T(8,128)(2,1)S(1)}, bf16[16,32,128]{2,1,0:T(8,128)(2,1)S(1)}, u32[]{:S(2)}, u32[]{:S(2)}) %collective-permute-start.8) | collective-permute-done | bytes 131104 | tf_op jit(solution)/shard_map/ppermute | solution.py:578
  33.4 2.4 %collective-permute-start.13 = (bf16[16,32,128]{2,1,0:T(8,128)(2,1)S(1)}, bf16[16,32,128]{2,1,0:T(8,128)(2,1)S(1)}, u32[]{:S(2)}, u32[]{:S(2)}) collective-permute-start(bf16[16,32,128]{2,1,0:T(8,128)(2,1)S(1)} %get-tuple-element.97.refs_0_), channel_id=1, source_target_pairs={{0,1},{1,0},{2,3},{3,2},{4,5},{5,4},{6,7},{7,6},{8,9},{9,8},{10,11... | collective-permute-start | bytes 393224 | tf_op jit(solution)/shard_map/ppermute | solution.py:109
  35.8 1.3 %collective-permute-start.10 = (bf16[8,32,128]{2,1,0:T(8,128)(2,1)S(1)}, bf16[8,32,128]{2,1,0:T(8,128)(2,1)S(1)}, u32[]{:S(2)}, u32[]{:S(2)}) collective-permute-start(bf16[8,32,128]{2,1,0:T(8,128)(2,1)S(1)} %get-tuple-element.96), channel_id=1, source_target_pairs={{0,2},{1,3},{2,0},{3,1},{4,6},{5,7},{6,4},{7,5},{8,10},{9,11},{10,... | collective-permute-start | bytes 196616 | tf_op jit(solution)/shard_map/ppermute | solution.py:108
  37.1 2.6 %collective-permute-done.11.refs_1_ = bf16[8,32,128]{2,1,0:T(8,128)(2,1)S(1)} collective-permute-done((bf16[8,32,128]{2,1,0:T(8,128)(2,1)S(1)}, bf16[8,32,128]{2,1,0:T(8,128)(2,1)S(1)}, u32[]{:S(2)}, u32[]{:S(2)}) %collective-permute-start.11) | collective-permute-done | bytes 65568 | tf_op jit(solution)/shard_map/ppermute | solution.py:108
  39.7 1.5 %stage0.4 = (f32[65,32,128]{2,1,0:T(8,128)S(1)}, f32[65,32,128]{2,1,0:T(8,128)S(1)}, f32[8,128]{1,0:T(8,128)S(1)}) custom-call(s32[7,208]{1,0:T(8,128)S(4)} %get-tuple-element.73.list_ref, s32[6]{0:T(128)S(4)} %get-tuple-element.71.total_ref, bf16[192,128,128]{2,1,0:T(8,128)(2,1)S(1)} %get-tuple-element.95.values_ref, ...), custom_call_target="tpu_custom_call" | custom-call | flops 75497472 | bytes 2359296 | tf_op jit(solution)/shard_map/stage0/pallas_call | solution.py:458
  41.6 2.2 %collective-permute-start.12 = (bf16[8,32,128]{2,1,0:T(8,128)(2,1)S(1)}, bf16[8,32,128]{2,1,0:T(8,128)(2,1)S(1)}, u32[]{:S(2)}, u32[]{:S(2)}) collective-permute-start(bf16[8,32,128]{2,1,0:T(8,128)(2,1)S(1)} %hold.6.refs_1_), channel_id=1, source_target_pairs={{0,1},{1,0},{2,3},{3,2},{4,5},{5,4},{6,7},{7,6},{8,9},{9,8},{10,11... | collective-permute-start | bytes 196616 | tf_op jit(solution)/shard_map/ppermute | solution.py:556
  44.4 1.8 %stage1.4 = (f32[65,32,128]{2,1,0:T(8,128)S(1)}, f32[65,32,128]{2,1,0:T(8,128)S(1)}) custom-call(s32[7,208]{1,0:T(8,128)S(4)} %get-tuple-element.73.list_ref, s32[6]{0:T(128)S(4)} %get-tuple-element.71.total_ref, bf16[192,128,128]{2,1,0:T(8,128)(2,1)S(1)} %get-tuple-element.95.values_ref, ...), custom_call_target="tpu_custom_call", output_to_operand_aliasing={{0}: (6, {}), {1}: (7, {})} | custom-call | flops 100663296 | bytes 3145728 | tf_op jit(solution)/shard_map/stage1/pallas_call | solution.py:471
  48.4 1.9 %collective-permute-start.17 = (bf16[16,32,128]{2,1,0:T(8,128)(2,1)S(1)}, bf16[16,32,128]{2,1,0:T(8,128)(2,1)S(1)}, u32[]{:S(2)}, u32[]{:S(2)}) collective-permute-start(bf16[16,32,128]{2,1,0:T(8,128)(2,1)S(1)} %get-tuple-element.108.refs_13_), channel_id=1, source_target_pairs={{0,24},{4,28},{8,16},{12,20},{16,8},{20,12},{24,0},{28,4},{1,25},{... | collective-permute-start | bytes 393224 | tf_op jit(solution)/shard_map/ppermute | solution.py:578
  50.4 0.9 %collective-permute-start.18 = (bf16[16,32,128]{2,1,0:T(8,128)(2,1)S(1)}, bf16[16,32,128]{2,1,0:T(8,128)(2,1)S(1)}, u32[]{:S(2)}, u32[]{:S(2)}) collective-permute-start(bf16[16,32,128]{2,1,0:T(8,128)(2,1)S(1)} %get-tuple-element.109.refs_14_), channel_id=1, source_target_pairs={{0,16},{4,20},{8,24},{12,28},{16,0},{20,4},{24,8},{28,12},{1,17},{... | collective-permute-start | bytes 393224 | tf_op jit(solution)/shard_map/ppermute | solution.py:578
  52.1 3.7 %collective-permute-done.17.refs_0_ = bf16[16,32,128]{2,1,0:T(8,128)(2,1)S(1)} collective-permute-done((bf16[16,32,128]{2,1,0:T(8,128)(2,1)S(1)}, bf16[16,32,128]{2,1,0:T(8,128)(2,1)S(1)}, u32[]{:S(2)}, u32[]{:S(2)}) %collective-permute-start.17) | collective-permute-done | bytes 131104 | tf_op jit(solution)/shard_map/ppermute | solution.py:578
  55.7 2.0 %collective-permute-done.18.refs_1_ = bf16[16,32,128]{2,1,0:T(8,128)(2,1)S(1)} collective-permute-done((bf16[16,32,128]{2,1,0:T(8,128)(2,1)S(1)}, bf16[16,32,128]{2,1,0:T(8,128)(2,1)S(1)}, u32[]{:S(2)}, u32[]{:S(2)}) %collective-permute-start.18) | collective-permute-done | bytes 131104 | tf_op jit(solution)/shard_map/ppermute | solution.py:578
  58.2 1.6 %collective-permute-start.21 = (bf16[8,32,128]{2,1,0:T(8,128)(2,1)S(1)}, bf16[8,32,128]{2,1,0:T(8,128)(2,1)S(1)}, u32[]{:S(2)}, u32[]{:S(2)}) collective-permute-start(bf16[8,32,128]{2,1,0:T(8,128)(2,1)S(1)} %get-tuple-element.112.refs_3_), channel_id=1, source_target_pairs={{0,2},{1,3},{2,0},{3,1},{4,6},{5,7},{6,4},{7,5},{8,10},{9,11},{10,... | collective-permute-start | bytes 196616 | tf_op jit(solution)/shard_map/ppermute | solution.py:108
  60.7 2.6 %collective-permute-start.20 = (bf16[8,32,128]{2,1,0:T(8,128)(2,1)S(1)}, bf16[8,32,128]{2,1,0:T(8,128)(2,1)S(1)}, u32[]{:S(2)}, u32[]{:S(2)}) collective-permute-start(bf16[8,32,128]{2,1,0:T(8,128)(2,1)S(1)} %get-tuple-element.114), channel_id=1, source_target_pairs={{0,2},{1,3},{2,0},{3,1},{4,6},{5,7},{6,4},{7,5},{8,10},{9,11},{10,... | collective-permute-start | bytes 196616 | tf_op jit(solution)/shard_map/ppermute | solution.py:108
  63.4 1.4 %collective-permute-done.21.refs_1_ = bf16[8,32,128]{2,1,0:T(8,128)(2,1)S(1)} collective-permute-done((bf16[8,32,128]{2,1,0:T(8,128)(2,1)S(1)}, bf16[8,32,128]{2,1,0:T(8,128)(2,1)S(1)}, u32[]{:S(2)}, u32[]{:S(2)}) %collective-permute-start.21) | collective-permute-done | bytes 65568 | tf_op jit(solution)/shard_map/ppermute | solution.py:108
  64.7 1.1 %collective-permute-start.24 = (bf16[8,32,128]{2,1,0:T(8,128)(2,1)S(1)}, bf16[8,32,128]{2,1,0:T(8,128)(2,1)S(1)}, u32[]{:S(2)}, u32[]{:S(2)}) collective-permute-start(bf16[8,32,128]{2,1,0:T(8,128)(2,1)S(1)} %collective-permute-done.21.refs_1_), channel_id=1, source_target_pairs={{0,1},{1,0},{2,3},{3,2},{4,5},{5,4},{6,7},{7,6},{8,9},{9,8},{10,11... | collective-permute-start | bytes 196616 | tf_op jit(solution)/shard_map/ppermute | solution.py:556
  65.9 1.7 %stage0.5 = (f32[65,32,128]{2,1,0:T(8,128)S(1)}, f32[65,32,128]{2,1,0:T(8,128)S(1)}, f32[8,128]{1,0:T(8,128)S(1)}) custom-call(s32[7,208]{1,0:T(8,128)S(4)} %get-tuple-element.73.list_ref, s32[6]{0:T(128)S(4)} %get-tuple-element.71.total_ref, bf16[192,128,128]{2,1,0:T(8,128)(2,1)S(1)} %get-tuple-element.95.values_ref, ...), custom_call_target="tpu_custom_call" | custom-call | flops 75497472 | bytes 2359296 | tf_op jit(solution)/shard_map/stage0/pallas_call | solution.py:458
  67.5 2.3 %collective-permute-start.22 = (bf16[8,32,128]{2,1,0:T(8,128)(2,1)S(1)}, bf16[8,32,128]{2,1,0:T(8,128)(2,1)S(1)}, u32[]{:S(2)}, u32[]{:S(2)}) collective-permute-start(bf16[8,32,128]{2,1,0:T(8,128)(2,1)S(1)} %hold.7.refs_1_), channel_id=1, source_target_pairs={{0,1},{1,0},{2,3},{3,2},{4,5},{5,4},{6,7},{7,6},{8,9},{9,8},{10,11... | collective-permute-start | bytes 196616 | tf_op jit(solution)/shard_map/ppermute | solution.py:556
  69.9 1.8 %stage1.5 = (f32[65,32,128]{2,1,0:T(8,128)S(1)}, f32[65,32,128]{2,1,0:T(8,128)S(1)}) custom-call(s32[7,208]{1,0:T(8,128)S(4)} %get-tuple-element.73.list_ref, s32[6]{0:T(128)S(4)} %get-tuple-element.71.total_ref, bf16[192,128,128]{2,1,0:T(8,128)(2,1)S(1)} %get-tuple-element.95.values_ref, ...), custom_call_target="tpu_custom_call", output_to_operand_aliasing={{0}: (6, {}), {1}: (7, {})} | custom-call | flops 100663296 | bytes 3145728 | tf_op jit(solution)/shard_map/stage1/pallas_call | solution.py:471
  74.3 1.1 %collective-permute-start.27 = (bf16[16,32,128]{2,1,0:T(8,128)(2,1)S(1)}, bf16[16,32,128]{2,1,0:T(8,128)(2,1)S(1)}, u32[]{:S(2)}, u32[]{:S(2)}) collective-permute-start(bf16[16,32,128]{2,1,0:T(8,128)(2,1)S(1)} %get-tuple-element.127), channel_id=1, source_target_pairs={{0,24},{4,28},{8,16},{12,20},{16,8},{20,12},{24,0},{28,4},{1,25},{... | collective-permute-start | bytes 393224 | tf_op jit(solution)/shard_map/ppermute | solution.py:578
  75.3 2.1 %collective-permute-start.28 = (bf16[16,32,128]{2,1,0:T(8,128)(2,1)S(1)}, bf16[16,32,128]{2,1,0:T(8,128)(2,1)S(1)}, u32[]{:S(2)}, u32[]{:S(2)}) collective-permute-start(bf16[16,32,128]{2,1,0:T(8,128)(2,1)S(1)} %get-tuple-element.128), channel_id=1, source_target_pairs={{0,16},{4,20},{8,24},{12,28},{16,0},{20,4},{24,8},{28,12},{1,17},{... | collective-permute-start | bytes 393224 | tf_op jit(solution)/shard_map/ppermute | solution.py:578
  77.9 3.7 %collective-permute-done.27.refs_0_ = bf16[16,32,128]{2,1,0:T(8,128)(2,1)S(1)} collective-permute-done((bf16[16,32,128]{2,1,0:T(8,128)(2,1)S(1)}, bf16[16,32,128]{2,1,0:T(8,128)(2,1)S(1)}, u32[]{:S(2)}, u32[]{:S(2)}) %collective-permute-start.27) | collective-permute-done | bytes 131104 | tf_op jit(solution)/shard_map/ppermute | solution.py:578
  81.6 2.0 %collective-permute-done.28.refs_1_ = bf16[16,32,128]{2,1,0:T(8,128)(2,1)S(1)} collective-permute-done((bf16[16,32,128]{2,1,0:T(8,128)(2,1)S(1)}, bf16[16,32,128]{2,1,0:T(8,128)(2,1)S(1)}, u32[]{:S(2)}, u32[]{:S(2)}) %collective-permute-start.28) | collective-permute-done | bytes 131104 | tf_op jit(solution)/shard_map/ppermute | solution.py:578
  83.6 1.4 %finish.1 = f32[16,32,128]{2,1,0:T(8,128)} custom-call(bf16[16,128,128]{2,1,0:T(8,128)(2,1)S(1)} %get-tuple-element.67.high_ref, bf16[16,128,128]{2,1,0:T(8,128)(2,1)S(1)} %get-tuple-element.68.low_ref, f32[16,32,128]{2,1,0:T(8,128)S(1)} %get-tuple-element.113.sol_ref, f32[16,32,128]{2,1,0:T(8,128)S(1)} %combine1.5.base_ref, ...), custom_call_target="tpu_custom_call" | custom-call | tf_op jit(solution)/shard_map/finish/pallas_call | solution.py:593
  (58 shorter events, 12.7 us)
Async XLA Ops:
  2.2 11.1 %collective-permute-start.3 = (bf16[8,32,128]{2,1,0:T(8,128)(2,1)S(1)}, bf16[8,32,128]{2,1,0:T(8,128)(2,1)S(1)}, u32[]{:S(2)}, u32[]{:S(2)}) collective-permute-start(bf16[8,32,128]{2,1,0:T(8,128)(2,1)S(1)} %get-tuple-element.77), channel_id=1, source_target_pairs={{0,2},{1,3},{2,0},{3,1},{4,6},{5,7},{6,4},{7,5},{8,10},{9,11},{10,... | collective-permute-start | bytes 196616 | tf_op jit(solution)/shard_map/ppermute | solution.py:108
  6.3 11.8 %collective-permute-start.2 = (bf16[16,32,128]{2,1,0:T(8,128)(2,1)S(1)}, bf16[16,32,128]{2,1,0:T(8,128)(2,1)S(1)}, u32[]{:S(2)}, u32[]{:S(2)}) collective-permute-start(bf16[16,32,128]{2,1,0:T(8,128)(2,1)S(1)} %get-tuple-element.76.refs_0_), channel_id=1, source_target_pairs={{0,1},{1,0},{2,3},{3,2},{4,5},{5,4},{6,7},{7,6},{8,9},{9,8},{10,11... | collective-permute-start | bytes 393224 | tf_op jit(solution)/shard_map/ppermute | solution.py:109
  7.8 6.0 %collective-permute-start = (bf16[8,32,128]{2,1,0:T(8,128)(2,1)S(1)}, bf16[8,32,128]{2,1,0:T(8,128)(2,1)S(1)}, u32[]{:S(2)}, u32[]{:S(2)}) collective-permute-start(bf16[8,32,128]{2,1,0:T(8,128)(2,1)S(1)} %get-tuple-element.74), channel_id=1, source_target_pairs={{0,2},{1,3},{2,0},{3,1},{4,6},{5,7},{6,4},{7,5},{8,10},{9,11},{10,... | collective-permute-start | bytes 196616 | tf_op jit(solution)/shard_map/ppermute | solution.py:108
  13.2 4.8 %collective-permute-start.4 = (bf16[8,32,128]{2,1,0:T(8,128)(2,1)S(1)}, bf16[8,32,128]{2,1,0:T(8,128)(2,1)S(1)}, u32[]{:S(2)}, u32[]{:S(2)}) collective-permute-start(bf16[8,32,128]{2,1,0:T(8,128)(2,1)S(1)} %hold.5.refs_1_), channel_id=1, source_target_pairs={{0,1},{1,0},{2,3},{3,2},{4,5},{5,4},{6,7},{7,6},{8,9},{9,8},{10,11... | collective-permute-start | bytes 196616 | tf_op jit(solution)/shard_map/ppermute | solution.py:556
  13.8 7.1 %collective-permute-start.1 = (bf16[8,32,128]{2,1,0:T(8,128)(2,1)S(1)}, bf16[8,32,128]{2,1,0:T(8,128)(2,1)S(1)}, u32[]{:S(2)}, u32[]{:S(2)}) collective-permute-start(bf16[8,32,128]{2,1,0:T(8,128)(2,1)S(1)} %hold.4.refs_1_), channel_id=1, source_target_pairs={{0,1},{1,0},{2,3},{3,2},{4,5},{5,4},{6,7},{7,6},{8,9},{9,8},{10,11... | collective-permute-start | bytes 196616 | tf_op jit(solution)/shard_map/ppermute | solution.py:556
  21.3 1.8 %collective-permute-start.6 = (bf16[48,32,128]{2,1,0:T(8,128)(2,1)S(1)}, bf16[48,32,128]{2,1,0:T(8,128)(2,1)S(1)}, u32[]{:S(2)}, u32[]{:S(2)}) collective-permute-start(bf16[48,32,128]{2,1,0:T(8,128)(2,1)S(1)} %get-tuple-element.85.refs_2_), channel_id=1, source_target_pairs={{0,4},{4,0},{8,12},{12,8},{16,20},{20,16},{24,28},{28,24},{1,5},{5... | collective-permute-start | bytes 1179656 | tf_op jit(solution)/shard_map/ppermute | solution.py:570
  21.8 4.9 %collective-permute-start.5 = (bf16[16,32,128]{2,1,0:T(8,128)(2,1)S(1)}, bf16[16,32,128]{2,1,0:T(8,128)(2,1)S(1)}, u32[]{:S(2)}, u32[]{:S(2)}) collective-permute-start(bf16[16,32,128]{2,1,0:T(8,128)(2,1)S(1)} %get-tuple-element.84.refs_3_), channel_id=1, source_target_pairs={{0,4},{4,0},{8,12},{12,8},{16,20},{20,16},{24,28},{28,24},{1,5},{5... | collective-permute-start | bytes 393224 | tf_op jit(solution)/shard_map/ppermute | solution.py:570
  23.2 7.8 %collective-permute-start.7 = (bf16[16,32,128]{2,1,0:T(8,128)(2,1)S(1)}, bf16[16,32,128]{2,1,0:T(8,128)(2,1)S(1)}, u32[]{:S(2)}, u32[]{:S(2)}) collective-permute-start(bf16[16,32,128]{2,1,0:T(8,128)(2,1)S(1)} %get-tuple-element.88.refs_6_.refs_10_), channel_id=1, source_target_pairs={{0,24},{4,28},{8,16},{12,20},{16,8},{20,12},{24,0},{28,4},{1,25},{... | collective-permute-start | bytes 393224 | tf_op jit(solution)/shard_map/ppermute | solution.py:578
  23.3 9.2 %collective-permute-start.8 = (bf16[16,32,128]{2,1,0:T(8,128)(2,1)S(1)}, bf16[16,32,128]{2,1,0:T(8,128)(2,1)S(1)}, u32[]{:S(2)}, u32[]{:S(2)}) collective-permute-start(bf16[16,32,128]{2,1,0:T(8,128)(2,1)S(1)} %get-tuple-element.89.refs_7_.refs_11_), channel_id=1, source_target_pairs={{0,16},{4,20},{8,24},{12,28},{16,0},{20,4},{24,8},{28,12},{1,17},{... | collective-permute-start | bytes 393224 | tf_op jit(solution)/shard_map/ppermute | solution.py:578
  26.7 5.8 %collective-permute-start.9 = (bf16[16,32,128]{2,1,0:T(8,128)(2,1)S(1)}, bf16[16,32,128]{2,1,0:T(8,128)(2,1)S(1)}, u32[]{:S(2)}, u32[]{:S(2)}) collective-permute-start(bf16[16,32,128]{2,1,0:T(8,128)(2,1)S(1)} %get-tuple-element.86.before_ref.refs_8_.refs_12_), channel_id=1, source_target_pairs={{0,8},{4,12},{8,0},{12,4},{16,24},{20,28},{24,16},{28,20},{1,9},{5... | collective-permute-start | bytes 393224 | tf_op jit(solution)/shard_map/ppermute | solution.py:578
  32.9 6.7 %collective-permute-start.11 = (bf16[8,32,128]{2,1,0:T(8,128)(2,1)S(1)}, bf16[8,32,128]{2,1,0:T(8,128)(2,1)S(1)}, u32[]{:S(2)}, u32[]{:S(2)}) collective-permute-start(bf16[8,32,128]{2,1,0:T(8,128)(2,1)S(1)} %get-tuple-element.92.refs_3_), channel_id=1, source_target_pairs={{0,2},{1,3},{2,0},{3,1},{4,6},{5,7},{6,4},{7,5},{8,10},{9,11},{10,... | collective-permute-start | bytes 196616 | tf_op jit(solution)/shard_map/ppermute | solution.py:108
  33.4 11.0 %collective-permute-start.13 = (bf16[16,32,128]{2,1,0:T(8,128)(2,1)S(1)}, bf16[16,32,128]{2,1,0:T(8,128)(2,1)S(1)}, u32[]{:S(2)}, u32[]{:S(2)}) collective-permute-start(bf16[16,32,128]{2,1,0:T(8,128)(2,1)S(1)} %get-tuple-element.97.refs_0_), channel_id=1, source_target_pairs={{0,1},{1,0},{2,3},{3,2},{4,5},{5,4},{6,7},{7,6},{8,9},{9,8},{10,11... | collective-permute-start | bytes 393224 | tf_op jit(solution)/shard_map/ppermute | solution.py:109
  35.8 5.8 %collective-permute-start.10 = (bf16[8,32,128]{2,1,0:T(8,128)(2,1)S(1)}, bf16[8,32,128]{2,1,0:T(8,128)(2,1)S(1)}, u32[]{:S(2)}, u32[]{:S(2)}) collective-permute-start(bf16[8,32,128]{2,1,0:T(8,128)(2,1)S(1)} %get-tuple-element.96), channel_id=1, source_target_pairs={{0,2},{1,3},{2,0},{3,1},{4,6},{5,7},{6,4},{7,5},{8,10},{9,11},{10,... | collective-permute-start | bytes 196616 | tf_op jit(solution)/shard_map/ppermute | solution.py:108
  39.6 4.7 %collective-permute-start.14 = (bf16[8,32,128]{2,1,0:T(8,128)(2,1)S(1)}, bf16[8,32,128]{2,1,0:T(8,128)(2,1)S(1)}, u32[]{:S(2)}, u32[]{:S(2)}) collective-permute-start(bf16[8,32,128]{2,1,0:T(8,128)(2,1)S(1)} %collective-permute-done.11.refs_1_), channel_id=1, source_target_pairs={{0,1},{1,0},{2,3},{3,2},{4,5},{5,4},{6,7},{7,6},{8,9},{9,8},{10,11... | collective-permute-start | bytes 196616 | tf_op jit(solution)/shard_map/ppermute | solution.py:556
  41.6 4.6 %collective-permute-start.12 = (bf16[8,32,128]{2,1,0:T(8,128)(2,1)S(1)}, bf16[8,32,128]{2,1,0:T(8,128)(2,1)S(1)}, u32[]{:S(2)}, u32[]{:S(2)}) collective-permute-start(bf16[8,32,128]{2,1,0:T(8,128)(2,1)S(1)} %hold.6.refs_1_), channel_id=1, source_target_pairs={{0,1},{1,0},{2,3},{3,2},{4,5},{5,4},{6,7},{7,6},{8,9},{9,8},{10,11... | collective-permute-start | bytes 196616 | tf_op jit(solution)/shard_map/ppermute | solution.py:556
  46.6 1.8 %collective-permute-start.16 = (bf16[48,32,128]{2,1,0:T(8,128)(2,1)S(1)}, bf16[48,32,128]{2,1,0:T(8,128)(2,1)S(1)}, u32[]{:S(2)}, u32[]{:S(2)}) collective-permute-start(bf16[48,32,128]{2,1,0:T(8,128)(2,1)S(1)} %get-tuple-element.106.refs_4_), channel_id=1, source_target_pairs={{0,4},{4,0},{8,12},{12,8},{16,20},{20,16},{24,28},{28,24},{1,5},{5... | collective-permute-start | bytes 1179656 | tf_op jit(solution)/shard_map/ppermute | solution.py:570
  46.9 5.0 %collective-permute-start.15 = (bf16[16,32,128]{2,1,0:T(8,128)(2,1)S(1)}, bf16[16,32,128]{2,1,0:T(8,128)(2,1)S(1)}, u32[]{:S(2)}, u32[]{:S(2)}) collective-permute-start(bf16[16,32,128]{2,1,0:T(8,128)(2,1)S(1)} %get-tuple-element.105.refs_5_), channel_id=1, source_target_pairs={{0,4},{4,0},{8,12},{12,8},{16,20},{20,16},{24,28},{28,24},{1,5},{5... | collective-permute-start | bytes 393224 | tf_op jit(solution)/shard_map/ppermute | solution.py:570
  48.4 7.3 %collective-permute-start.17 = (bf16[16,32,128]{2,1,0:T(8,128)(2,1)S(1)}, bf16[16,32,128]{2,1,0:T(8,128)(2,1)S(1)}, u32[]{:S(2)}, u32[]{:S(2)}) collective-permute-start(bf16[16,32,128]{2,1,0:T(8,128)(2,1)S(1)} %get-tuple-element.108.refs_13_), channel_id=1, source_target_pairs={{0,24},{4,28},{8,16},{12,20},{16,8},{20,12},{24,0},{28,4},{1,25},{... | collective-permute-start | bytes 393224 | tf_op jit(solution)/shard_map/ppermute | solution.py:578
  50.4 7.4 %collective-permute-start.18 = (bf16[16,32,128]{2,1,0:T(8,128)(2,1)S(1)}, bf16[16,32,128]{2,1,0:T(8,128)(2,1)S(1)}, u32[]{:S(2)}, u32[]{:S(2)}) collective-permute-start(bf16[16,32,128]{2,1,0:T(8,128)(2,1)S(1)} %get-tuple-element.109.refs_14_), channel_id=1, source_target_pairs={{0,16},{4,20},{8,24},{12,28},{16,0},{20,4},{24,8},{28,12},{1,17},{... | collective-permute-start | bytes 393224 | tf_op jit(solution)/shard_map/ppermute | solution.py:578
  51.3 6.5 %collective-permute-start.19 = (bf16[16,32,128]{2,1,0:T(8,128)(2,1)S(1)}, bf16[16,32,128]{2,1,0:T(8,128)(2,1)S(1)}, u32[]{:S(2)}, u32[]{:S(2)}) collective-permute-start(bf16[16,32,128]{2,1,0:T(8,128)(2,1)S(1)} %get-tuple-element.107.before_ref.refs_15_), channel_id=1, source_target_pairs={{0,8},{4,12},{8,0},{12,4},{16,24},{20,28},{24,16},{28,20},{1,9},{5... | collective-permute-start | bytes 393224 | tf_op jit(solution)/shard_map/ppermute | solution.py:578
  58.2 6.6 %collective-permute-start.21 = (bf16[8,32,128]{2,1,0:T(8,128)(2,1)S(1)}, bf16[8,32,128]{2,1,0:T(8,128)(2,1)S(1)}, u32[]{:S(2)}, u32[]{:S(2)}) collective-permute-start(bf16[8,32,128]{2,1,0:T(8,128)(2,1)S(1)} %get-tuple-element.112.refs_3_), channel_id=1, source_target_pairs={{0,2},{1,3},{2,0},{3,1},{4,6},{5,7},{6,4},{7,5},{8,10},{9,11},{10,... | collective-permute-start | bytes 196616 | tf_op jit(solution)/shard_map/ppermute | solution.py:108
  60.2 9.7 %collective-permute-start.23 = (bf16[16,32,128]{2,1,0:T(8,128)(2,1)S(1)}, bf16[16,32,128]{2,1,0:T(8,128)(2,1)S(1)}, u32[]{:S(2)}, u32[]{:S(2)}) collective-permute-start(bf16[16,32,128]{2,1,0:T(8,128)(2,1)S(1)} %get-tuple-element.115.refs_0_), channel_id=1, source_target_pairs={{0,1},{1,0},{2,3},{3,2},{4,5},{5,4},{6,7},{7,6},{8,9},{9,8},{10,11... | collective-permute-start | bytes 393224 | tf_op jit(solution)/shard_map/ppermute | solution.py:109
  60.7 6.8 %collective-permute-start.20 = (bf16[8,32,128]{2,1,0:T(8,128)(2,1)S(1)}, bf16[8,32,128]{2,1,0:T(8,128)(2,1)S(1)}, u32[]{:S(2)}, u32[]{:S(2)}) collective-permute-start(bf16[8,32,128]{2,1,0:T(8,128)(2,1)S(1)} %get-tuple-element.114), channel_id=1, source_target_pairs={{0,2},{1,3},{2,0},{3,1},{4,6},{5,7},{6,4},{7,5},{8,10},{9,11},{10,... | collective-permute-start | bytes 196616 | tf_op jit(solution)/shard_map/ppermute | solution.py:108
  64.7 5.1 %collective-permute-start.24 = (bf16[8,32,128]{2,1,0:T(8,128)(2,1)S(1)}, bf16[8,32,128]{2,1,0:T(8,128)(2,1)S(1)}, u32[]{:S(2)}, u32[]{:S(2)}) collective-permute-start(bf16[8,32,128]{2,1,0:T(8,128)(2,1)S(1)} %collective-permute-done.21.refs_1_), channel_id=1, source_target_pairs={{0,1},{1,0},{2,3},{3,2},{4,5},{5,4},{6,7},{7,6},{8,9},{9,8},{10,11... | collective-permute-start | bytes 196616 | tf_op jit(solution)/shard_map/ppermute | solution.py:556
  67.5 4.6 %collective-permute-start.22 = (bf16[8,32,128]{2,1,0:T(8,128)(2,1)S(1)}, bf16[8,32,128]{2,1,0:T(8,128)(2,1)S(1)}, u32[]{:S(2)}, u32[]{:S(2)}) collective-permute-start(bf16[8,32,128]{2,1,0:T(8,128)(2,1)S(1)} %hold.7.refs_1_), channel_id=1, source_target_pairs={{0,1},{1,0},{2,3},{3,2},{4,5},{5,4},{6,7},{7,6},{8,9},{9,8},{10,11... | collective-permute-start | bytes 196616 | tf_op jit(solution)/shard_map/ppermute | solution.py:556
  72.4 1.8 %collective-permute-start.26 = (bf16[48,32,128]{2,1,0:T(8,128)(2,1)S(1)}, bf16[48,32,128]{2,1,0:T(8,128)(2,1)S(1)}, u32[]{:S(2)}, u32[]{:S(2)}) collective-permute-start(bf16[48,32,128]{2,1,0:T(8,128)(2,1)S(1)} %get-tuple-element.125), channel_id=1, source_target_pairs={{0,4},{4,0},{8,12},{12,8},{16,20},{20,16},{24,28},{28,24},{1,5},{5... | collective-permute-start | bytes 1179656 | tf_op jit(solution)/shard_map/ppermute | solution.py:570
  72.8 5.0 %collective-permute-start.25 = (bf16[16,32,128]{2,1,0:T(8,128)(2,1)S(1)}, bf16[16,32,128]{2,1,0:T(8,128)(2,1)S(1)}, u32[]{:S(2)}, u32[]{:S(2)}) collective-permute-start(bf16[16,32,128]{2,1,0:T(8,128)(2,1)S(1)} %get-tuple-element.123), channel_id=1, source_target_pairs={{0,4},{4,0},{8,12},{12,8},{16,20},{20,16},{24,28},{28,24},{1,5},{5... | collective-permute-start | bytes 393224 | tf_op jit(solution)/shard_map/ppermute | solution.py:570
  74.3 7.3 %collective-permute-start.27 = (bf16[16,32,128]{2,1,0:T(8,128)(2,1)S(1)}, bf16[16,32,128]{2,1,0:T(8,128)(2,1)S(1)}, u32[]{:S(2)}, u32[]{:S(2)}) collective-permute-start(bf16[16,32,128]{2,1,0:T(8,128)(2,1)S(1)} %get-tuple-element.127), channel_id=1, source_target_pairs={{0,24},{4,28},{8,16},{12,20},{16,8},{20,12},{24,0},{28,4},{1,25},{... | collective-permute-start | bytes 393224 | tf_op jit(solution)/shard_map/ppermute | solution.py:578
  75.3 8.2 %collective-permute-start.28 = (bf16[16,32,128]{2,1,0:T(8,128)(2,1)S(1)}, bf16[16,32,128]{2,1,0:T(8,128)(2,1)S(1)}, u32[]{:S(2)}, u32[]{:S(2)}) collective-permute-start(bf16[16,32,128]{2,1,0:T(8,128)(2,1)S(1)} %get-tuple-element.128), channel_id=1, source_target_pairs={{0,16},{4,20},{8,24},{12,28},{16,0},{20,4},{24,8},{28,12},{1,17},{... | collective-permute-start | bytes 393224 | tf_op jit(solution)/shard_map/ppermute | solution.py:578
  77.4 6.2 %collective-permute-start.29 = (bf16[16,32,128]{2,1,0:T(8,128)(2,1)S(1)}, bf16[16,32,128]{2,1,0:T(8,128)(2,1)S(1)}, u32[]{:S(2)}, u32[]{:S(2)}) collective-permute-start(bf16[16,32,128]{2,1,0:T(8,128)(2,1)S(1)} %get-tuple-element.126.before_ref), channel_id=1, source_target_pairs={{0,8},{4,12},{8,0},{12,4},{16,24},{20,28},{24,16},{28,20},{1,9},{5... | collective-permute-start | bytes 393224 | tf_op jit(solution)/shard_map/ppermute | solution.py:578

commit v11 on v10

--- a/solution.py
+++ b/solution.py
@@ -118,8 +118,19 @@
     pass
 
 
+def part_sizes(owned):
+    if owned % 8 == 0:
+        return [owned - 3 * owned // 8, 3 * owned // 8]
+    return [owned]
+
+
+def part_starts(sizes):
+    return [sum(sizes[:part]) for part in range(len(sizes))]
+
+
 def put_rounded(p, value, whole_ref, part_refs):
-    part, inner = divmod(p, part_refs[0].shape[0])
+    first = part_refs[0].shape[0]
+    part, inner = (0, p) if p < first else (1, p - first)
     rounded = value.astype(jnp.bfloat16)
     whole_ref[p] = rounded
     part_refs[part][inner] = rounded
@@ -148,16 +159,16 @@
             put_rounded(p, value, whole_ref, part_refs)
 
 
-def apply_kernel(part, parts, pieces, high_ref, low_ref, left_ref, sol_ref, base_ref, *refs):
+def apply_kernel(start, pieces, earlier, high_ref, low_ref, left_ref, sol_ref, base_ref, *refs):
     piece_refs, refs = refs[:pieces], refs[pieces:]
-    earlier_refs, refs = refs[:-3 - (part == parts - 1)], refs[-3 - (part == parts - 1):]
-    new_ref, new_left_ref, rounded_ref, *whole_refs = refs
-    each = rounded_ref.shape[0]
+    earlier_refs, (new_ref, new_left_ref, rounded_ref, *whole_refs) = refs[:earlier], refs[earlier:]
     for whole_ref in whole_refs:
-        for index, earlier_ref in enumerate(earlier_refs):
-            whole_ref[pl.ds(index * each, each)] = earlier_ref[...]
-    for inner in range(each):
-        p = part * each + inner
+        at = 0
+        for earlier_ref in earlier_refs:
+            whole_ref[pl.ds(at, earlier_ref.shape[0])] = earlier_ref[...]
+            at += earlier_ref.shape[0]
+    for inner in range(rounded_ref.shape[0]):
+        p = start + inner
         received = sum(piece_ref[p].astype(jnp.float32) for piece_ref in piece_refs)
         value = sol_ref[p] + times_block(base_ref[p] - received, high_ref[p], low_ref[p])
         new_ref[p] = value
@@ -197,11 +208,13 @@
     mine = lax.axis_index("col")
     row_bits, col_bits = bits
     lists = len(stages) * CORES
-    each = owned // parts
+    sizes = part_sizes(owned)
     trash = (group // CORES) << col_bits
     for index, stage in enumerate(stages):
-        for place, (piece, part) in enumerate(stage):
-            table_ref[piece * parts + part] = ((index * CORES) << col_bits) + place * each
+        base = 0
+        for piece, part in stage:
+            table_ref[piece * parts + part] = ((index * CORES) << col_bits) + base
+            base += sizes[part]
     for index in range(lists + 1):
         total_ref[index] = 0
     for load in loads[:2]:
@@ -215,7 +228,9 @@
             owner, row_inner = halves(halves(rows_ref[0, 0, slot], group)[1], owned)
             source, rest = halves(cols_ref[0, 0, slot], group)
             half = 1 - ((owner & (CORES - 1)) ^ core)
-            part, inner = halves(halves(rest, owned)[1], each)
+            inner = halves(rest, owned)[1]
+            part = jnp.where(inner >= sizes[0], parts - 1, 0)
+            inner = jnp.where(inner >= sizes[0], inner - sizes[0], inner)
             first, base = halves(table_ref[relative(mine, source, groups) * parts + part], 1 << col_bits)
             which = jnp.where(slot < used, first + half, lists)
             row = lax.shift_right_logical(owner, 1) * owned + row_inner
@@ -384,11 +399,12 @@
     half_rows = chips * owned
     slots = block_values.shape[2]
 
-    parts = 2 if owned % 2 == 0 else 1
+    sizes = part_sizes(owned)
+    parts = len(sizes)
     stages = gather_stages(groups, parts)
     final = len(stages) - 1
     lists_total = len(stages) * CORES
-    widest = max(len(stage) for stage in stages) * owned // parts
+    widest = max(sum(sizes[part] for _, part in stage) for stage in stages)
     row_bits, col_bits = bits = half_rows.bit_length(), (widest - 1).bit_length()
     assert (slots - 1).bit_length() + row_bits + col_bits <= 31
     assert slots % LANES == 0
@@ -400,11 +416,11 @@
     token_type = jax.ShapeDtypeStruct((8, 128), jnp.float32)
     loads = next(count for count in (4, 2, 1) if owned % count == 0)
     rounded_type = jax.ShapeDtypeStruct((owned, rhs, size), jnp.bfloat16)
-    part_type = jax.ShapeDtypeStruct((owned // parts, rhs, size), jnp.bfloat16)
+    part_types = [jax.ShapeDtypeStruct((part, rhs, size), jnp.bfloat16) for part in sizes]
 
     high, low, sol, left, whole, *rounded = pl.pallas_call(
         start_kernel,
-        out_shape=[matrix_type] * 2 + [field_type] * 2 + [rounded_type] + [part_type] * parts,
+        out_shape=[matrix_type] * 2 + [field_type] * 2 + [rounded_type] + part_types,
         in_specs=[in_hbm()] * 2,
         out_specs=[in_vmem()] * (5 + parts),
         scratch_shapes=[
@@ -498,7 +514,7 @@
     def hold(piece, token):
         return pl.pallas_call(
             hold_kernel,
-            out_shape=part_type,
+            out_shape=jax.ShapeDtypeStruct(piece.shape, piece.dtype),
             in_specs=[in_vmem()] * 2,
             out_specs=in_vmem(),
             input_output_aliases={0: 0},
@@ -531,8 +547,8 @@
     def apply(part, sol, left, base, pieces, earlier):
         last = part == parts - 1
         return pl.pallas_call(
-            functools.partial(apply_kernel, part, parts, len(pieces)),
-            out_shape=[field_type, field_type, part_type] + [rounded_type] * last,
+            functools.partial(apply_kernel, part_starts(sizes)[part], len(pieces), len(earlier)),
+            out_shape=[field_type, field_type, part_types[part]] + [rounded_type] * last,
             in_specs=[in_vmem()] * (5 + len(pieces) + len(earlier)),
             out_specs=[in_vmem()] * (3 + last),
             input_output_aliases={2: 1, 3: 0},

time: 84.6 us -> 84 us (level); the launches traced: 85 us -> 83.5 us
  Pallas kernels: 28.5 us -> 18.7 us
  waiting for transfers between devices: 21.3 us -> 28.3 us
  starting transfers between devices: 34.3 us -> 35.7 us
    pallas_call x3, Pallas kernels: 6.43 us -> 2.81 us  [product_stage(): pl.pallas_call(functools.partial(stage_kernel, stage, bits, dims, len(pie...]
    ppermute x9, waiting for transfers between devices: 12.9 us -> 16 us  [per_device(): lax.ppermute(send, 'row', [(chip * CORES + core, partner(chip, shift, chi...]
    pallas_call x1, Pallas kernels: 4.14 us -> 1.24 us  [turn(): pl.pallas_call(turn_kernel, out_shape=[pltpu.VMEM(values.shape, values.dt...]
    ppermute x6, waiting for transfers between devices: 0.99 us -> 3.36 us  [forward(): lax.ppermute(sets[index, part], 'col', neighbours(groups))]
    ppermute x9, starting transfers between devices: 10.7 us -> 12.7 us  [per_device(): lax.ppermute(send, 'row', [(chip * CORES + core, partner(chip, shift, chi...]
    pallas_call x3, Pallas kernels: 5.87 us -> 4.06 us  [product_first(): pl.pallas_call(functools.partial(first_kernel, len(pieces), len(outs) //...]
    pallas_call x1, Pallas kernels: 4.37 us -> 2.82 us  [per_device(): pl.pallas_call(functools.partial(order_kernel, group, owned, groups, part...]
    ppermute x6, waiting for transfers between devices: 4.9 us -> 6.43 us  [gather(): sets[step, part] = lax.ppermute(piece, 'col', ring(groups, 2 * step))]
  transfers between devices with their start and end apart: 30 -> 30, of which waited for: 14 -> 16; matrix products, arithmetic and copies ran while one was open for 0% -> 0% of each run, Pallas kernels for 27% -> 16%
where the time goes in v11:
time: 84 us; the launch traced here: 83.5 us
  starting transfers between devices  35.7 us (43%)
  waiting for transfers between devices  28.3 us (34%)
  Pallas kernels  18.7 us (22%)
  between operations  0.85 us (1%)
    ppermute x9, waiting for transfers between devices, per_device(): lax.ppermute(send, 'row', [(chip * CORES + core, partner(chip, shift, chi...  16 us
    ppermute x9, starting transfers between devices, per_device(): lax.ppermute(send, 'row', [(chip * CORES + core, partner(chip, shift, chi...  12.7 us
    ppermute x6, starting transfers between devices, gather(): sets[step, part] = lax.ppermute(piece, 'col', ring(groups, 2 * step))  8.78 us
    ppermute x6, starting transfers between devices, forward(): lax.ppermute(sets[index, part], 'col', neighbours(groups))  7.26 us
    ppermute x6, waiting for transfers between devices, gather(): sets[step, part] = lax.ppermute(piece, 'col', ring(groups, 2 * step))  6.43 us
    ppermute x3, starting transfers between devices, gather(): sets[groups // 2, 0] = lax.ppermute(whole, 'col', neighbours(groups))  5.12 us
    pallas_call x3, Pallas kernels, product_first(): pl.pallas_call(functools.partial(first_kernel, len(pieces), len(outs) //...  4.06 us
    ppermute x6, waiting for transfers between devices, forward(): lax.ppermute(sets[index, part], 'col', neighbours(groups))  3.36 us
  transfers between devices with their start and end apart: 30, of which 16 were waited for; matrix products, arithmetic and copies ran while one was open for 0% of the time, Pallas kernels for 16%

profile of v11, /device:TPU:0, one launch (start us, length us, event | category | flops | bytes accessed | tf_op | source)
XLA Modules:
  0.0 83.5 jit_solution(7287438704772672889)
XLA Ops:
  0.0 2.2 %start.1 = (bf16[16,128,128]{2,1,0:T(8,128)(2,1)S(1)}, bf16[16,128,128]{2,1,0:T(8,128)(2,1)S(1)}, f32[16,32,128]{2,1,0:T(8,128)S(1)}, f32[16,32,128]{2,1,0:T(8,1...) custom-call(f32[16,128,128]{2,1,0:T(8,128)} %bitcast.5, ...), custom_call_target="tpu_custom_call" | custom-call | tf_op jit(solution)/shard_map/start/pallas_call | solution.py:421
  2.2 4.1 %collective-permute-start.3 = (bf16[10,32,128]{2,1,0:T(8,128)(2,1)S(1)}, bf16[10,32,128]{2,1,0:T(8,128)(2,1)S(1)}, u32[]{:S(2)}, u32[]{:S(2)}) collective-permute-start(bf16[10,32,128]{2,1,0:T(8,128)(2,1)S(1)} %get-tuple-element.77), channel_id=1, source_target_pairs={{0,2},{1,3},{2,0},{3,1},{4,6},{5,7},{6,4},{7,5},{8,10},{9,11},{10,... | collective-permute-start | bytes 245768 | tf_op jit(solution)/shard_map/ppermute | solution.py:108
  6.3 1.6 %collective-permute-start.2 = (bf16[16,32,128]{2,1,0:T(8,128)(2,1)S(1)}, bf16[16,32,128]{2,1,0:T(8,128)(2,1)S(1)}, u32[]{:S(2)}, u32[]{:S(2)}) collective-permute-start(bf16[16,32,128]{2,1,0:T(8,128)(2,1)S(1)} %get-tuple-element.76.refs_0_), channel_id=1, source_target_pairs={{0,1},{1,0},{2,3},{3,2},{4,5},{5,4},{6,7},{7,6},{8,9},{9,8},{10,11... | collective-permute-start | bytes 393224 | tf_op jit(solution)/shard_map/ppermute | solution.py:109
  8.8 2.8 %order.1 = (s32[7,208]{1,0:T(8,128)S(4)}, s32[6]{0:T(128)S(4)}, bf16[192,128,128]{2,1,0:T(8,128)(2,1)S(1)}, f32[8,128]{1,0:T(8,128)S(1)}) custom-call(s32[1,1]{1,0:T(1,128)S(6)} %copy.57.count_ref, s32[1,1,192]{2,1,0:T(1,128)} %rows_hbm.1, s32[1,1,192]{2,1,0:T(1,128)} %cols_hbm.1, bf16[192,128,128]{2,1,0:T(8,128)(2,1)} %bitcast.4), custom_call_target="tpu_custom_call" | custom-call | tf_op jit(solution)/shard_map/order/pallas_call | solution.py:434
  11.7 1.5 %collective-permute-start.4 = (bf16[10,32,128]{2,1,0:T(8,128)(2,1)S(1)}, bf16[10,32,128]{2,1,0:T(8,128)(2,1)S(1)}, u32[]{:S(2)}, u32[]{:S(2)}) collective-permute-start(bf16[10,32,128]{2,1,0:T(8,128)(2,1)S(1)} %hold.5.refs_1_), channel_id=1, source_target_pairs={{0,1},{1,0},{2,3},{3,2},{4,5},{5,4},{6,7},{7,6},{8,9},{9,8},{10,11... | collective-permute-start | bytes 245768 | tf_op jit(solution)/shard_map/ppermute | solution.py:572
  13.2 1.0 %collective-permute-start.1 = (bf16[6,32,128]{2,1,0:T(8,128)(2,1)S(1)}, bf16[6,32,128]{2,1,0:T(8,128)(2,1)S(1)}, u32[]{:S(2)}, u32[]{:S(2)}) collective-permute-start(bf16[6,32,128]{2,1,0:T(8,128)(2,1)S(1)} %hold.4.refs_1_), channel_id=1, source_target_pairs={{0,1},{1,0},{2,3},{3,2},{4,5},{5,4},{6,7},{7,6},{8,9},{9,8},{10,11... | collective-permute-start | bytes 147464 | tf_op jit(solution)/shard_map/ppermute | solution.py:572
  14.2 1.9 %stage0.3 = (f32[65,32,128]{2,1,0:T(8,128)S(1)}, f32[65,32,128]{2,1,0:T(8,128)S(1)}, f32[8,128]{1,0:T(8,128)}) custom-call(s32[7,208]{1,0:T(8,128)S(4)} %get-tuple-element.73.list_ref, s32[6]{0:T(128)S(4)} %get-tuple-element.71.total_ref, bf16[192,128,128]{2,1,0:T(8,128)(2,1)S(1)} %get-tuple-element.72.values_ref, ...), custom_call_target="tpu_custom_call" | custom-call | flops 75497472 | bytes 2359296 | tf_op jit(solution)/shard_map/stage0/pallas_call | solution.py:474
  16.7 1.2 %stage1.3 = (f32[65,32,128]{2,1,0:T(8,128)S(1)}, f32[65,32,128]{2,1,0:T(8,128)S(1)}) custom-call(s32[7,208]{1,0:T(8,128)S(4)} %get-tuple-element.73.list_ref, s32[6]{0:T(128)S(4)} %get-tuple-element.71.total_ref, bf16[192,128,128]{2,1,0:T(8,128)(2,1)S(1)} %get-tuple-element.72.values_ref, ...), custom_call_target="tpu_custom_call", output_to_operand_aliasing={{0}: (6, {}), {1}: (7, {})} | custom-call | flops 100663296 | bytes 3145728 | tf_op jit(solution)/shard_map/stage1/pallas_call | solution.py:487
  20.3 5.0 %collective-permute-start.7 = (bf16[16,32,128]{2,1,0:T(8,128)(2,1)S(1)}, bf16[16,32,128]{2,1,0:T(8,128)(2,1)S(1)}, u32[]{:S(2)}, u32[]{:S(2)}) collective-permute-start(bf16[16,32,128]{2,1,0:T(8,128)(2,1)S(1)} %get-tuple-element.88.refs_6_.refs_10_), channel_id=1, source_target_pairs={{0,24},{4,28},{8,16},{12,20},{16,8},{20,12},{24,0},{28,4},{1,25},{... | collective-permute-start | bytes 393224 | tf_op jit(solution)/shard_map/ppermute | solution.py:594
  26.0 1.2 %turn.1 = (bf16[192,128,128]{2,1,0:T(8,128)(2,1)S(1)}, f32[16,32,128]{2,1,0:T(8,128)S(1)}) custom-call(s32[6]{0:T(128)S(4)} %get-tuple-element.71.total_ref, bf16[192,128,128]{2,1,0:T(8,128)(2,1)S(1)} %get-tuple-element.72.values_ref, f32[16,32,128]{2,1,0:T(8,128)S(1)} %combine1.3.base_ref), custom_call_target="tpu_custom_call", output_to_operand_aliasing={{1}: (2, {})} | custom-call | flops 20000000000 | tf_op jit(solution)/shard_map/turn/pallas_call | solution.py:454
  27.2 1.9 %collective-permute-done.7.refs_0_ = bf16[16,32,128]{2,1,0:T(8,128)(2,1)S(1)} collective-permute-done((bf16[16,32,128]{2,1,0:T(8,128)(2,1)S(1)}, bf16[16,32,128]{2,1,0:T(8,128)(2,1)S(1)}, u32[]{:S(2)}, u32[]{:S(2)}) %collective-permute-start.7) | collective-permute-done | bytes 131104 | tf_op jit(solution)/shard_map/ppermute | solution.py:594
  29.1 2.7 %collective-permute-done.8.refs_1_ = bf16[16,32,128]{2,1,0:T(8,128)(2,1)S(1)} collective-permute-done((bf16[16,32,128]{2,1,0:T(8,128)(2,1)S(1)}, bf16[16,32,128]{2,1,0:T(8,128)(2,1)S(1)}, u32[]{:S(2)}, u32[]{:S(2)}) %collective-permute-start.8) | collective-permute-done | bytes 131104 | tf_op jit(solution)/shard_map/ppermute | solution.py:594
  33.4 2.5 %collective-permute-start.13 = (bf16[16,32,128]{2,1,0:T(8,128)(2,1)S(1)}, bf16[16,32,128]{2,1,0:T(8,128)(2,1)S(1)}, u32[]{:S(2)}, u32[]{:S(2)}) collective-permute-start(bf16[16,32,128]{2,1,0:T(8,128)(2,1)S(1)} %get-tuple-element.97.refs_0_), channel_id=1, source_target_pairs={{0,1},{1,0},{2,3},{3,2},{4,5},{5,4},{6,7},{7,6},{8,9},{9,8},{10,11... | collective-permute-start | bytes 393224 | tf_op jit(solution)/shard_map/ppermute | solution.py:109
  36.0 3.7 %collective-permute-done.11.refs_1_ = bf16[10,32,128]{2,1,0:T(8,128)(2,1)S(1)} collective-permute-done((bf16[10,32,128]{2,1,0:T(8,128)(2,1)S(1)}, bf16[10,32,128]{2,1,0:T(8,128)(2,1)S(1)}, u32[]{:S(2)}, u32[]{:S(2)}) %collective-permute-start.11) | collective-permute-done | bytes 81952 | tf_op jit(solution)/shard_map/ppermute | solution.py:108
  39.6 1.0 %stage0.4 = (f32[65,32,128]{2,1,0:T(8,128)S(1)}, f32[65,32,128]{2,1,0:T(8,128)S(1)}, f32[8,128]{1,0:T(8,128)S(1)}) custom-call(s32[7,208]{1,0:T(8,128)S(4)} %get-tuple-element.73.list_ref, s32[6]{0:T(128)S(4)} %get-tuple-element.71.total_ref, bf16[192,128,128]{2,1,0:T(8,128)(2,1)S(1)} %get-tuple-element.95.values_ref, ...), custom_call_target="tpu_custom_call" | custom-call | flops 75497472 | bytes 2359296 | tf_op jit(solution)/shard_map/stage0/pallas_call | solution.py:474
  41.1 2.1 %collective-permute-start.12 = (bf16[6,32,128]{2,1,0:T(8,128)(2,1)S(1)}, bf16[6,32,128]{2,1,0:T(8,128)(2,1)S(1)}, u32[]{:S(2)}, u32[]{:S(2)}) collective-permute-start(bf16[6,32,128]{2,1,0:T(8,128)(2,1)S(1)} %hold.6.refs_1_), channel_id=1, source_target_pairs={{0,1},{1,0},{2,3},{3,2},{4,5},{5,4},{6,7},{7,6},{8,9},{9,8},{10,11... | collective-permute-start | bytes 147464 | tf_op jit(solution)/shard_map/ppermute | solution.py:572
  43.2 1.4 %collective-permute-done.14.refs_2_ = bf16[10,32,128]{2,1,0:T(8,128)(2,1)S(1)} collective-permute-done((bf16[10,32,128]{2,1,0:T(8,128)(2,1)S(1)}, bf16[10,32,128]{2,1,0:T(8,128)(2,1)S(1)}, u32[]{:S(2)}, u32[]{:S(2)}) %collective-permute-start.14) | collective-permute-done | bytes 81952 | tf_op jit(solution)/shard_map/ppermute | solution.py:572
  47.6 2.4 %collective-permute-start.17 = (bf16[16,32,128]{2,1,0:T(8,128)(2,1)S(1)}, bf16[16,32,128]{2,1,0:T(8,128)(2,1)S(1)}, u32[]{:S(2)}, u32[]{:S(2)}) collective-permute-start(bf16[16,32,128]{2,1,0:T(8,128)(2,1)S(1)} %get-tuple-element.108.refs_13_), channel_id=1, source_target_pairs={{0,24},{4,28},{8,16},{12,20},{16,8},{20,12},{24,0},{28,4},{1,25},{... | collective-permute-start | bytes 393224 | tf_op jit(solution)/shard_map/ppermute | solution.py:594
  50.2 1.0 %collective-permute-start.19 = (bf16[16,32,128]{2,1,0:T(8,128)(2,1)S(1)}, bf16[16,32,128]{2,1,0:T(8,128)(2,1)S(1)}, u32[]{:S(2)}, u32[]{:S(2)}) collective-permute-start(bf16[16,32,128]{2,1,0:T(8,128)(2,1)S(1)} %get-tuple-element.107.before_ref.refs_15_), channel_id=1, source_target_pairs={{0,8},{4,12},{8,0},{12,4},{16,24},{20,28},{24,16},{28,20},{1,9},{5... | collective-permute-start | bytes 393224 | tf_op jit(solution)/shard_map/ppermute | solution.py:594
  51.2 3.3 %collective-permute-done.17.refs_0_ = bf16[16,32,128]{2,1,0:T(8,128)(2,1)S(1)} collective-permute-done((bf16[16,32,128]{2,1,0:T(8,128)(2,1)S(1)}, bf16[16,32,128]{2,1,0:T(8,128)(2,1)S(1)}, u32[]{:S(2)}, u32[]{:S(2)}) %collective-permute-start.17) | collective-permute-done | bytes 131104 | tf_op jit(solution)/shard_map/ppermute | solution.py:594
  54.5 2.4 %collective-permute-done.18.refs_1_ = bf16[16,32,128]{2,1,0:T(8,128)(2,1)S(1)} collective-permute-done((bf16[16,32,128]{2,1,0:T(8,128)(2,1)S(1)}, bf16[16,32,128]{2,1,0:T(8,128)(2,1)S(1)}, u32[]{:S(2)}, u32[]{:S(2)}) %collective-permute-start.18) | collective-permute-done | bytes 131104 | tf_op jit(solution)/shard_map/ppermute | solution.py:594
  57.4 1.9 %collective-permute-start.21 = (bf16[10,32,128]{2,1,0:T(8,128)(2,1)S(1)}, bf16[10,32,128]{2,1,0:T(8,128)(2,1)S(1)}, u32[]{:S(2)}, u32[]{:S(2)}) collective-permute-start(bf16[10,32,128]{2,1,0:T(8,128)(2,1)S(1)} %get-tuple-element.112.refs_3_), channel_id=1, source_target_pairs={{0,2},{1,3},{2,0},{3,1},{4,6},{5,7},{6,4},{7,5},{8,10},{9,11},{10,... | collective-permute-start | bytes 245768 | tf_op jit(solution)/shard_map/ppermute | solution.py:108
  59.6 1.0 %collective-permute-start.23 = (bf16[16,32,128]{2,1,0:T(8,128)(2,1)S(1)}, bf16[16,32,128]{2,1,0:T(8,128)(2,1)S(1)}, u32[]{:S(2)}, u32[]{:S(2)}) collective-permute-start(bf16[16,32,128]{2,1,0:T(8,128)(2,1)S(1)} %get-tuple-element.115.refs_0_), channel_id=1, source_target_pairs={{0,1},{1,0},{2,3},{3,2},{4,5},{5,4},{6,7},{7,6},{8,9},{9,8},{10,11... | collective-permute-start | bytes 393224 | tf_op jit(solution)/shard_map/ppermute | solution.py:109
  60.6 1.7 %collective-permute-start.20 = (bf16[6,32,128]{2,1,0:T(8,128)(2,1)S(1)}, bf16[6,32,128]{2,1,0:T(8,128)(2,1)S(1)}, u32[]{:S(2)}, u32[]{:S(2)}) collective-permute-start(bf16[6,32,128]{2,1,0:T(8,128)(2,1)S(1)} %get-tuple-element.114), channel_id=1, source_target_pairs={{0,2},{1,3},{2,0},{3,1},{4,6},{5,7},{6,4},{7,5},{8,10},{9,11},{10,... | collective-permute-start | bytes 147464 | tf_op jit(solution)/shard_map/ppermute | solution.py:108
  62.3 2.3 %collective-permute-done.21.refs_1_ = bf16[10,32,128]{2,1,0:T(8,128)(2,1)S(1)} collective-permute-done((bf16[10,32,128]{2,1,0:T(8,128)(2,1)S(1)}, bf16[10,32,128]{2,1,0:T(8,128)(2,1)S(1)}, u32[]{:S(2)}, u32[]{:S(2)}) %collective-permute-start.21) | collective-permute-done | bytes 81952 | tf_op jit(solution)/shard_map/ppermute | solution.py:108
  65.3 1.1 %stage0.5 = (f32[65,32,128]{2,1,0:T(8,128)S(1)}, f32[65,32,128]{2,1,0:T(8,128)S(1)}, f32[8,128]{1,0:T(8,128)S(1)}) custom-call(s32[7,208]{1,0:T(8,128)S(4)} %get-tuple-element.73.list_ref, s32[6]{0:T(128)S(4)} %get-tuple-element.71.total_ref, bf16[192,128,128]{2,1,0:T(8,128)(2,1)S(1)} %get-tuple-element.95.values_ref, ...), custom_call_target="tpu_custom_call" | custom-call | flops 75497472 | bytes 2359296 | tf_op jit(solution)/shard_map/stage0/pallas_call | solution.py:474
  66.4 1.9 %collective-permute-start.22 = (bf16[6,32,128]{2,1,0:T(8,128)(2,1)S(1)}, bf16[6,32,128]{2,1,0:T(8,128)(2,1)S(1)}, u32[]{:S(2)}, u32[]{:S(2)}) collective-permute-start(bf16[6,32,128]{2,1,0:T(8,128)(2,1)S(1)} %hold.7.refs_1_), channel_id=1, source_target_pairs={{0,1},{1,0},{2,3},{3,2},{4,5},{5,4},{6,7},{7,6},{8,9},{9,8},{10,11... | collective-permute-start | bytes 147464 | tf_op jit(solution)/shard_map/ppermute | solution.py:572
  72.8 1.8 %collective-permute-start.27 = (bf16[16,32,128]{2,1,0:T(8,128)(2,1)S(1)}, bf16[16,32,128]{2,1,0:T(8,128)(2,1)S(1)}, u32[]{:S(2)}, u32[]{:S(2)}) collective-permute-start(bf16[16,32,128]{2,1,0:T(8,128)(2,1)S(1)} %get-tuple-element.127), channel_id=1, source_target_pairs={{0,24},{4,28},{8,16},{12,20},{16,8},{20,12},{24,0},{28,4},{1,25},{... | collective-permute-start | bytes 393224 | tf_op jit(solution)/shard_map/ppermute | solution.py:594
  74.6 0.9 %collective-permute-start.28 = (bf16[16,32,128]{2,1,0:T(8,128)(2,1)S(1)}, bf16[16,32,128]{2,1,0:T(8,128)(2,1)S(1)}, u32[]{:S(2)}, u32[]{:S(2)}) collective-permute-start(bf16[16,32,128]{2,1,0:T(8,128)(2,1)S(1)} %get-tuple-element.128), channel_id=1, source_target_pairs={{0,16},{4,20},{8,24},{12,28},{16,0},{20,4},{24,8},{28,12},{1,17},{... | collective-permute-start | bytes 393224 | tf_op jit(solution)/shard_map/ppermute | solution.py:594
  76.4 3.7 %collective-permute-done.27.refs_0_ = bf16[16,32,128]{2,1,0:T(8,128)(2,1)S(1)} collective-permute-done((bf16[16,32,128]{2,1,0:T(8,128)(2,1)S(1)}, bf16[16,32,128]{2,1,0:T(8,128)(2,1)S(1)}, u32[]{:S(2)}, u32[]{:S(2)}) %collective-permute-start.27) | collective-permute-done | bytes 131104 | tf_op jit(solution)/shard_map/ppermute | solution.py:594
  80.1 2.0 %collective-permute-done.28.refs_1_ = bf16[16,32,128]{2,1,0:T(8,128)(2,1)S(1)} collective-permute-done((bf16[16,32,128]{2,1,0:T(8,128)(2,1)S(1)}, bf16[16,32,128]{2,1,0:T(8,128)(2,1)S(1)}, u32[]{:S(2)}, u32[]{:S(2)}) %collective-permute-start.28) | collective-permute-done | bytes 131104 | tf_op jit(solution)/shard_map/ppermute | solution.py:594
  82.1 1.4 %finish.1 = f32[16,32,128]{2,1,0:T(8,128)} custom-call(bf16[16,128,128]{2,1,0:T(8,128)(2,1)S(1)} %get-tuple-element.67.high_ref, bf16[16,128,128]{2,1,0:T(8,128)(2,1)S(1)} %get-tuple-element.68.low_ref, f32[16,32,128]{2,1,0:T(8,128)S(1)} %get-tuple-element.113.sol_ref, f32[16,32,128]{2,1,0:T(8,128)S(1)} %combine1.5.base_ref, ...), custom_call_target="tpu_custom_call" | custom-call | tf_op jit(solution)/shard_map/finish/pallas_call | solution.py:609
  (58 shorter events, 16.1 us)
Async XLA Ops:
  2.2 9.5 %collective-permute-start.3 = (bf16[10,32,128]{2,1,0:T(8,128)(2,1)S(1)}, bf16[10,32,128]{2,1,0:T(8,128)(2,1)S(1)}, u32[]{:S(2)}, u32[]{:S(2)}) collective-permute-start(bf16[10,32,128]{2,1,0:T(8,128)(2,1)S(1)} %get-tuple-element.77), channel_id=1, source_target_pairs={{0,2},{1,3},{2,0},{3,1},{4,6},{5,7},{6,4},{7,5},{8,10},{9,11},{10,... | collective-permute-start | bytes 245768 | tf_op jit(solution)/shard_map/ppermute | solution.py:108
  6.3 9.9 %collective-permute-start.2 = (bf16[16,32,128]{2,1,0:T(8,128)(2,1)S(1)}, bf16[16,32,128]{2,1,0:T(8,128)(2,1)S(1)}, u32[]{:S(2)}, u32[]{:S(2)}) collective-permute-start(bf16[16,32,128]{2,1,0:T(8,128)(2,1)S(1)} %get-tuple-element.76.refs_0_), channel_id=1, source_target_pairs={{0,1},{1,0},{2,3},{3,2},{4,5},{5,4},{6,7},{7,6},{8,9},{9,8},{10,11... | collective-permute-start | bytes 393224 | tf_op jit(solution)/shard_map/ppermute | solution.py:109
  7.8 5.4 %collective-permute-start = (bf16[6,32,128]{2,1,0:T(8,128)(2,1)S(1)}, bf16[6,32,128]{2,1,0:T(8,128)(2,1)S(1)}, u32[]{:S(2)}, u32[]{:S(2)}) collective-permute-start(bf16[6,32,128]{2,1,0:T(8,128)(2,1)S(1)} %get-tuple-element.74), channel_id=1, source_target_pairs={{0,2},{1,3},{2,0},{3,1},{4,6},{5,7},{6,4},{7,5},{8,10},{9,11},{10,... | collective-permute-start | bytes 147464 | tf_op jit(solution)/shard_map/ppermute | solution.py:108
  11.7 5.0 %collective-permute-start.4 = (bf16[10,32,128]{2,1,0:T(8,128)(2,1)S(1)}, bf16[10,32,128]{2,1,0:T(8,128)(2,1)S(1)}, u32[]{:S(2)}, u32[]{:S(2)}) collective-permute-start(bf16[10,32,128]{2,1,0:T(8,128)(2,1)S(1)} %hold.5.refs_1_), channel_id=1, source_target_pairs={{0,1},{1,0},{2,3},{3,2},{4,5},{5,4},{6,7},{7,6},{8,9},{9,8},{10,11... | collective-permute-start | bytes 245768 | tf_op jit(solution)/shard_map/ppermute | solution.py:572
  13.2 4.7 %collective-permute-start.1 = (bf16[6,32,128]{2,1,0:T(8,128)(2,1)S(1)}, bf16[6,32,128]{2,1,0:T(8,128)(2,1)S(1)}, u32[]{:S(2)}, u32[]{:S(2)}) collective-permute-start(bf16[6,32,128]{2,1,0:T(8,128)(2,1)S(1)} %hold.4.refs_1_), channel_id=1, source_target_pairs={{0,1},{1,0},{2,3},{3,2},{4,5},{5,4},{6,7},{7,6},{8,9},{9,8},{10,11... | collective-permute-start | bytes 147464 | tf_op jit(solution)/shard_map/ppermute | solution.py:572
  18.4 1.8 %collective-permute-start.6 = (bf16[48,32,128]{2,1,0:T(8,128)(2,1)S(1)}, bf16[48,32,128]{2,1,0:T(8,128)(2,1)S(1)}, u32[]{:S(2)}, u32[]{:S(2)}) collective-permute-start(bf16[48,32,128]{2,1,0:T(8,128)(2,1)S(1)} %get-tuple-element.85.refs_2_), channel_id=1, source_target_pairs={{0,4},{4,0},{8,12},{12,8},{16,20},{20,16},{24,28},{28,24},{1,5},{5... | collective-permute-start | bytes 1179656 | tf_op jit(solution)/shard_map/ppermute | solution.py:586
  18.9 7.0 %collective-permute-start.5 = (bf16[16,32,128]{2,1,0:T(8,128)(2,1)S(1)}, bf16[16,32,128]{2,1,0:T(8,128)(2,1)S(1)}, u32[]{:S(2)}, u32[]{:S(2)}) collective-permute-start(bf16[16,32,128]{2,1,0:T(8,128)(2,1)S(1)} %get-tuple-element.84.refs_3_), channel_id=1, source_target_pairs={{0,4},{4,0},{8,12},{12,8},{16,20},{20,16},{24,28},{28,24},{1,5},{5... | collective-permute-start | bytes 393224 | tf_op jit(solution)/shard_map/ppermute | solution.py:586
  20.3 8.9 %collective-permute-start.7 = (bf16[16,32,128]{2,1,0:T(8,128)(2,1)S(1)}, bf16[16,32,128]{2,1,0:T(8,128)(2,1)S(1)}, u32[]{:S(2)}, u32[]{:S(2)}) collective-permute-start(bf16[16,32,128]{2,1,0:T(8,128)(2,1)S(1)} %get-tuple-element.88.refs_6_.refs_10_), channel_id=1, source_target_pairs={{0,24},{4,28},{8,16},{12,20},{16,8},{20,12},{24,0},{28,4},{1,25},{... | collective-permute-start | bytes 393224 | tf_op jit(solution)/shard_map/ppermute | solution.py:594
  25.2 6.6 %collective-permute-start.8 = (bf16[16,32,128]{2,1,0:T(8,128)(2,1)S(1)}, bf16[16,32,128]{2,1,0:T(8,128)(2,1)S(1)}, u32[]{:S(2)}, u32[]{:S(2)}) collective-permute-start(bf16[16,32,128]{2,1,0:T(8,128)(2,1)S(1)} %get-tuple-element.89.refs_7_.refs_11_), channel_id=1, source_target_pairs={{0,16},{4,20},{8,24},{12,28},{16,0},{20,4},{24,8},{28,12},{1,17},{... | collective-permute-start | bytes 393224 | tf_op jit(solution)/shard_map/ppermute | solution.py:594
  25.2 6.6 %collective-permute-start.9 = (bf16[16,32,128]{2,1,0:T(8,128)(2,1)S(1)}, bf16[16,32,128]{2,1,0:T(8,128)(2,1)S(1)}, u32[]{:S(2)}, u32[]{:S(2)}) collective-permute-start(bf16[16,32,128]{2,1,0:T(8,128)(2,1)S(1)} %get-tuple-element.86.before_ref.refs_8_.refs_12_), channel_id=1, source_target_pairs={{0,8},{4,12},{8,0},{12,4},{16,24},{20,28},{24,16},{28,20},{1,9},{5... | collective-permute-start | bytes 393224 | tf_op jit(solution)/shard_map/ppermute | solution.py:594
  32.3 7.3 %collective-permute-start.11 = (bf16[10,32,128]{2,1,0:T(8,128)(2,1)S(1)}, bf16[10,32,128]{2,1,0:T(8,128)(2,1)S(1)}, u32[]{:S(2)}, u32[]{:S(2)}) collective-permute-start(bf16[10,32,128]{2,1,0:T(8,128)(2,1)S(1)} %get-tuple-element.92.refs_3_), channel_id=1, source_target_pairs={{0,2},{1,3},{2,0},{3,1},{4,6},{5,7},{6,4},{7,5},{8,10},{9,11},{10,... | collective-permute-start | bytes 245768 | tf_op jit(solution)/shard_map/ppermute | solution.py:108
  33.4 9.8 %collective-permute-start.13 = (bf16[16,32,128]{2,1,0:T(8,128)(2,1)S(1)}, bf16[16,32,128]{2,1,0:T(8,128)(2,1)S(1)}, u32[]{:S(2)}, u32[]{:S(2)}) collective-permute-start(bf16[16,32,128]{2,1,0:T(8,128)(2,1)S(1)} %get-tuple-element.97.refs_0_), channel_id=1, source_target_pairs={{0,1},{1,0},{2,3},{3,2},{4,5},{5,4},{6,7},{7,6},{8,9},{9,8},{10,11... | collective-permute-start | bytes 393224 | tf_op jit(solution)/shard_map/ppermute | solution.py:109
  35.9 5.2 %collective-permute-start.10 = (bf16[6,32,128]{2,1,0:T(8,128)(2,1)S(1)}, bf16[6,32,128]{2,1,0:T(8,128)(2,1)S(1)}, u32[]{:S(2)}, u32[]{:S(2)}) collective-permute-start(bf16[6,32,128]{2,1,0:T(8,128)(2,1)S(1)} %get-tuple-element.96), channel_id=1, source_target_pairs={{0,2},{1,3},{2,0},{3,1},{4,6},{5,7},{6,4},{7,5},{8,10},{9,11},{10,... | collective-permute-start | bytes 147464 | tf_op jit(solution)/shard_map/ppermute | solution.py:108
  39.6 5.0 %collective-permute-start.14 = (bf16[10,32,128]{2,1,0:T(8,128)(2,1)S(1)}, bf16[10,32,128]{2,1,0:T(8,128)(2,1)S(1)}, u32[]{:S(2)}, u32[]{:S(2)}) collective-permute-start(bf16[10,32,128]{2,1,0:T(8,128)(2,1)S(1)} %collective-permute-done.11.refs_1_), channel_id=1, source_target_pairs={{0,1},{1,0},{2,3},{3,2},{4,5},{5,4},{6,7},{7,6},{8,9},{9,8},{10,11... | collective-permute-start | bytes 245768 | tf_op jit(solution)/shard_map/ppermute | solution.py:572
  41.1 4.3 %collective-permute-start.12 = (bf16[6,32,128]{2,1,0:T(8,128)(2,1)S(1)}, bf16[6,32,128]{2,1,0:T(8,128)(2,1)S(1)}, u32[]{:S(2)}, u32[]{:S(2)}) collective-permute-start(bf16[6,32,128]{2,1,0:T(8,128)(2,1)S(1)} %hold.6.refs_1_), channel_id=1, source_target_pairs={{0,1},{1,0},{2,3},{3,2},{4,5},{5,4},{6,7},{7,6},{8,9},{9,8},{10,11... | collective-permute-start | bytes 147464 | tf_op jit(solution)/shard_map/ppermute | solution.py:572
  45.7 1.8 %collective-permute-start.16 = (bf16[48,32,128]{2,1,0:T(8,128)(2,1)S(1)}, bf16[48,32,128]{2,1,0:T(8,128)(2,1)S(1)}, u32[]{:S(2)}, u32[]{:S(2)}) collective-permute-start(bf16[48,32,128]{2,1,0:T(8,128)(2,1)S(1)} %get-tuple-element.106.refs_4_), channel_id=1, source_target_pairs={{0,4},{4,0},{8,12},{12,8},{16,20},{20,16},{24,28},{28,24},{1,5},{5... | collective-permute-start | bytes 1179656 | tf_op jit(solution)/shard_map/ppermute | solution.py:586
  46.1 5.0 %collective-permute-start.15 = (bf16[16,32,128]{2,1,0:T(8,128)(2,1)S(1)}, bf16[16,32,128]{2,1,0:T(8,128)(2,1)S(1)}, u32[]{:S(2)}, u32[]{:S(2)}) collective-permute-start(bf16[16,32,128]{2,1,0:T(8,128)(2,1)S(1)} %get-tuple-element.105.refs_5_), channel_id=1, source_target_pairs={{0,4},{4,0},{8,12},{12,8},{16,20},{20,16},{24,28},{28,24},{1,5},{5... | collective-permute-start | bytes 393224 | tf_op jit(solution)/shard_map/ppermute | solution.py:586
  47.6 6.9 %collective-permute-start.17 = (bf16[16,32,128]{2,1,0:T(8,128)(2,1)S(1)}, bf16[16,32,128]{2,1,0:T(8,128)(2,1)S(1)}, u32[]{:S(2)}, u32[]{:S(2)}) collective-permute-start(bf16[16,32,128]{2,1,0:T(8,128)(2,1)S(1)} %get-tuple-element.108.refs_13_), channel_id=1, source_target_pairs={{0,24},{4,28},{8,16},{12,20},{16,8},{20,12},{24,0},{28,4},{1,25},{... | collective-permute-start | bytes 393224 | tf_op jit(solution)/shard_map/ppermute | solution.py:594
  50.0 6.9 %collective-permute-start.18 = (bf16[16,32,128]{2,1,0:T(8,128)(2,1)S(1)}, bf16[16,32,128]{2,1,0:T(8,128)(2,1)S(1)}, u32[]{:S(2)}, u32[]{:S(2)}) collective-permute-start(bf16[16,32,128]{2,1,0:T(8,128)(2,1)S(1)} %get-tuple-element.109.refs_14_), channel_id=1, source_target_pairs={{0,16},{4,20},{8,24},{12,28},{16,0},{20,4},{24,8},{28,12},{1,17},{... | collective-permute-start | bytes 393224 | tf_op jit(solution)/shard_map/ppermute | solution.py:594
  50.2 6.7 %collective-permute-start.19 = (bf16[16,32,128]{2,1,0:T(8,128)(2,1)S(1)}, bf16[16,32,128]{2,1,0:T(8,128)(2,1)S(1)}, u32[]{:S(2)}, u32[]{:S(2)}) collective-permute-start(bf16[16,32,128]{2,1,0:T(8,128)(2,1)S(1)} %get-tuple-element.107.before_ref.refs_15_), channel_id=1, source_target_pairs={{0,8},{4,12},{8,0},{12,4},{16,24},{20,28},{24,16},{28,20},{1,9},{5... | collective-permute-start | bytes 393224 | tf_op jit(solution)/shard_map/ppermute | solution.py:594
  57.4 7.2 %collective-permute-start.21 = (bf16[10,32,128]{2,1,0:T(8,128)(2,1)S(1)}, bf16[10,32,128]{2,1,0:T(8,128)(2,1)S(1)}, u32[]{:S(2)}, u32[]{:S(2)}) collective-permute-start(bf16[10,32,128]{2,1,0:T(8,128)(2,1)S(1)} %get-tuple-element.112.refs_3_), channel_id=1, source_target_pairs={{0,2},{1,3},{2,0},{3,1},{4,6},{5,7},{6,4},{7,5},{8,10},{9,11},{10,... | collective-permute-start | bytes 245768 | tf_op jit(solution)/shard_map/ppermute | solution.py:108
  59.6 8.7 %collective-permute-start.23 = (bf16[16,32,128]{2,1,0:T(8,128)(2,1)S(1)}, bf16[16,32,128]{2,1,0:T(8,128)(2,1)S(1)}, u32[]{:S(2)}, u32[]{:S(2)}) collective-permute-start(bf16[16,32,128]{2,1,0:T(8,128)(2,1)S(1)} %get-tuple-element.115.refs_0_), channel_id=1, source_target_pairs={{0,1},{1,0},{2,3},{3,2},{4,5},{5,4},{6,7},{7,6},{8,9},{9,8},{10,11... | collective-permute-start | bytes 393224 | tf_op jit(solution)/shard_map/ppermute | solution.py:109
  60.6 5.8 %collective-permute-start.20 = (bf16[6,32,128]{2,1,0:T(8,128)(2,1)S(1)}, bf16[6,32,128]{2,1,0:T(8,128)(2,1)S(1)}, u32[]{:S(2)}, u32[]{:S(2)}) collective-permute-start(bf16[6,32,128]{2,1,0:T(8,128)(2,1)S(1)} %get-tuple-element.114), channel_id=1, source_target_pairs={{0,2},{1,3},{2,0},{3,1},{4,6},{5,7},{6,4},{7,5},{8,10},{9,11},{10,... | collective-permute-start | bytes 147464 | tf_op jit(solution)/shard_map/ppermute | solution.py:108
  64.6 4.4 %collective-permute-start.24 = (bf16[10,32,128]{2,1,0:T(8,128)(2,1)S(1)}, bf16[10,32,128]{2,1,0:T(8,128)(2,1)S(1)}, u32[]{:S(2)}, u32[]{:S(2)}) collective-permute-start(bf16[10,32,128]{2,1,0:T(8,128)(2,1)S(1)} %collective-permute-done.21.refs_1_), channel_id=1, source_target_pairs={{0,1},{1,0},{2,3},{3,2},{4,5},{5,4},{6,7},{7,6},{8,9},{9,8},{10,11... | collective-permute-start | bytes 245768 | tf_op jit(solution)/shard_map/ppermute | solution.py:572
  66.4 4.2 %collective-permute-start.22 = (bf16[6,32,128]{2,1,0:T(8,128)(2,1)S(1)}, bf16[6,32,128]{2,1,0:T(8,128)(2,1)S(1)}, u32[]{:S(2)}, u32[]{:S(2)}) collective-permute-start(bf16[6,32,128]{2,1,0:T(8,128)(2,1)S(1)} %hold.7.refs_1_), channel_id=1, source_target_pairs={{0,1},{1,0},{2,3},{3,2},{4,5},{5,4},{6,7},{7,6},{8,9},{9,8},{10,11... | collective-permute-start | bytes 147464 | tf_op jit(solution)/shard_map/ppermute | solution.py:572
  70.9 1.8 %collective-permute-start.26 = (bf16[48,32,128]{2,1,0:T(8,128)(2,1)S(1)}, bf16[48,32,128]{2,1,0:T(8,128)(2,1)S(1)}, u32[]{:S(2)}, u32[]{:S(2)}) collective-permute-start(bf16[48,32,128]{2,1,0:T(8,128)(2,1)S(1)} %get-tuple-element.125), channel_id=1, source_target_pairs={{0,4},{4,0},{8,12},{12,8},{16,20},{20,16},{24,28},{28,24},{1,5},{5... | collective-permute-start | bytes 1179656 | tf_op jit(solution)/shard_map/ppermute | solution.py:586
  71.3 5.0 %collective-permute-start.25 = (bf16[16,32,128]{2,1,0:T(8,128)(2,1)S(1)}, bf16[16,32,128]{2,1,0:T(8,128)(2,1)S(1)}, u32[]{:S(2)}, u32[]{:S(2)}) collective-permute-start(bf16[16,32,128]{2,1,0:T(8,128)(2,1)S(1)} %get-tuple-element.123), channel_id=1, source_target_pairs={{0,4},{4,0},{8,12},{12,8},{16,20},{20,16},{24,28},{28,24},{1,5},{5... | collective-permute-start | bytes 393224 | tf_op jit(solution)/shard_map/ppermute | solution.py:586
  72.8 7.3 %collective-permute-start.27 = (bf16[16,32,128]{2,1,0:T(8,128)(2,1)S(1)}, bf16[16,32,128]{2,1,0:T(8,128)(2,1)S(1)}, u32[]{:S(2)}, u32[]{:S(2)}) collective-permute-start(bf16[16,32,128]{2,1,0:T(8,128)(2,1)S(1)} %get-tuple-element.127), channel_id=1, source_target_pairs={{0,24},{4,28},{8,16},{12,20},{16,8},{20,12},{24,0},{28,4},{1,25},{... | collective-permute-start | bytes 393224 | tf_op jit(solution)/shard_map/ppermute | solution.py:594
  74.6 7.5 %collective-permute-start.28 = (bf16[16,32,128]{2,1,0:T(8,128)(2,1)S(1)}, bf16[16,32,128]{2,1,0:T(8,128)(2,1)S(1)}, u32[]{:S(2)}, u32[]{:S(2)}) collective-permute-start(bf16[16,32,128]{2,1,0:T(8,128)(2,1)S(1)} %get-tuple-element.128), channel_id=1, source_target_pairs={{0,16},{4,20},{8,24},{12,28},{16,0},{20,4},{24,8},{28,12},{1,17},{... | collective-permute-start | bytes 393224 | tf_op jit(solution)/shard_map/ppermute | solution.py:594
  75.5 6.6 %collective-permute-start.29 = (bf16[16,32,128]{2,1,0:T(8,128)(2,1)S(1)}, bf16[16,32,128]{2,1,0:T(8,128)(2,1)S(1)}, u32[]{:S(2)}, u32[]{:S(2)}) collective-permute-start(bf16[16,32,128]{2,1,0:T(8,128)(2,1)S(1)} %get-tuple-element.126.before_ref), channel_id=1, source_target_pairs={{0,8},{4,12},{8,0},{12,4},{16,24},{20,28},{24,16},{28,20},{1,9},{5... | collective-permute-start | bytes 393224 | tf_op jit(solution)/shard_map/ppermute | solution.py:594

commit v12 on v10

--- a/solution.py
+++ b/solution.py
@@ -184,7 +184,8 @@
 
 
 def order_kernel(group, owned, groups, parts, stages, bits, count_ref, rows_hbm, cols_hbm, values_hbm,
-                 list_out, total_out, values_out, token_ref, rows_ref, cols_ref, table_ref, total_ref, sems):
+                 list_out, total_out, values_out, token_ref, rows_ref, cols_ref, first_ref, base_ref, total_ref,
+                 sems):
     token_ref[...] = jnp.zeros_like(token_ref)
     loads = [
         pltpu.make_async_copy(rows_hbm, rows_ref, sems.at[0]),
@@ -193,15 +194,26 @@
     ]
     for load in loads:
         load.start()
-    core = lax.axis_index("row") & (CORES - 1)
+    other = 1 - (lax.axis_index("row") & (CORES - 1))
     mine = lax.axis_index("col")
     row_bits, col_bits = bits
     lists = len(stages) * CORES
     each = owned // parts
     trash = (group // CORES) << col_bits
-    for index, stage in enumerate(stages):
-        for place, (piece, part) in enumerate(stage):
-            table_ref[piece * parts + part] = ((index * CORES) << col_bits) + place * each
+    places = {
+        piece: (index * CORES, place * each) for index, stage in enumerate(stages) for place, piece in enumerate(stage)
+    }
+    own_rows = lax.axis_index("row") * owned
+    for source in range(groups):
+        piece = relative(mine, source, groups)
+        for part in range(parts):
+            first, base = places[0, part]
+            for index in range(1, groups):
+                first = jnp.where(piece == index, places[index, part][0], first)
+                base = jnp.where(piece == index, places[index, part][1], base)
+            at = halves(source * group + own_rows + part * each, each)[0]
+            first_ref[at] = first
+            base_ref[at] = base
     for index in range(lists + 1):
         total_ref[index] = 0
     for load in loads[:2]:
@@ -213,13 +225,11 @@
         for lane in range(LANES):
             slot = chunk * LANES + lane
             owner, row_inner = halves(halves(rows_ref[0, 0, slot], group)[1], owned)
-            source, rest = halves(cols_ref[0, 0, slot], group)
-            half = 1 - ((owner & (CORES - 1)) ^ core)
-            part, inner = halves(halves(rest, owned)[1], each)
-            first, base = halves(table_ref[relative(mine, source, groups) * parts + part], 1 << col_bits)
-            which = jnp.where(slot < used, first + half, lists)
+            at, inner = halves(cols_ref[0, 0, slot], each)
+            half = (owner & (CORES - 1)) ^ other
+            which = jnp.where(slot < used, first_ref[at] + half, lists)
             row = lax.shift_right_logical(owner, 1) * owned + row_inner
-            col = base + inner
+            col = base_ref[at] + inner
             entries.append((which, (((slot << row_bits) | row) << col_bits) | col))
         for which, entry in entries:
             at = total_ref[which]
@@ -427,7 +437,9 @@
         out_specs=[in_smem()] * 2 + [in_vmem()] * 2,
         scratch_shapes=[
             index_type, index_type,
-            pltpu.SMEM((groups * parts,), jnp.int32), pltpu.SMEM((lists_total + 1,), jnp.int32),
+            pltpu.SMEM((groups * row_devices * parts,), jnp.int32),
+            pltpu.SMEM((groups * row_devices * parts,), jnp.int32),
+            pltpu.SMEM((lists_total + 1,), jnp.int32),
             pltpu.SemaphoreType.DMA((3,)),
         ],
         compiler_params=params(),

time: 84.6 us -> 84.1 us (level)
  waiting for transfers between devices: 21.3 us -> 28.5 us
  Pallas kernels: 28.5 us -> 23 us
  starting transfers between devices: 34.3 us -> 31.5 us
    ppermute x6, waiting for transfers between devices: 4.9 us -> 8.89 us  [gather(): sets[step, part] = lax.ppermute(piece, 'col', ring(groups, 2 * step))]
    ppermute x6, starting transfers between devices: 7.24 us -> 4.53 us  [forward(): lax.ppermute(sets[index, part], 'col', neighbours(groups))]
    ppermute x3, starting transfers between devices: 4.57 us -> 2.05 us  [gather(): sets[groups // 2, 0] = lax.ppermute(whole, 'col', neighbours(groups))]
    ppermute x6, starting transfers between devices: 9.99 us -> 12.2 us  [gather(): sets[step, part] = lax.ppermute(piece, 'col', ring(groups, 2 * step))]
    ppermute x9, waiting for transfers between devices: 12.9 us -> 14.8 us  [per_device(): lax.ppermute(send, 'row', [(chip * CORES + core, partner(chip, shift, chi...]
    pallas_call x3, Pallas kernels: 6.43 us -> 4.62 us  [product_stage(): pl.pallas_call(functools.partial(stage_kernel, stage, bits, dims, len(pie...]
    pallas_call x1, Pallas kernels: 4.37 us -> 2.82 us  [per_device(): pl.pallas_call(functools.partial(order_kernel, group, owned, groups, part...]
    ppermute x6, waiting for transfers between devices: 0.99 us -> 2.4 us  [forward(): lax.ppermute(sets[index, part], 'col', neighbours(groups))]
  transfers between devices with their start and end apart: 30 -> 30, of which waited for: 14 -> 17; matrix products, arithmetic and copies ran while one was open for 0% -> 0% of each run, Pallas kernels for 27% -> 21%
where the time goes in v12:
time: 84.1 us; the launch traced here: 83.9 us
  starting transfers between devices  31.5 us (37%)
  waiting for transfers between devices  28.5 us (34%)
  Pallas kernels  23 us (27%)
  between operations  0.85 us (1%)
    ppermute x9, waiting for transfers between devices, per_device(): lax.ppermute(send, 'row', [(chip * CORES + core, partner(chip, shift, chi...  14.8 us
    ppermute x6, starting transfers between devices, gather(): sets[step, part] = lax.ppermute(piece, 'col', ring(groups, 2 * step))  12.2 us
    ppermute x9, starting transfers between devices, per_device(): lax.ppermute(send, 'row', [(chip * CORES + core, partner(chip, shift, chi...  10.9 us
    ppermute x6, waiting for transfers between devices, gather(): sets[step, part] = lax.ppermute(piece, 'col', ring(groups, 2 * step))  8.89 us
    pallas_call x3, Pallas kernels, product_first(): pl.pallas_call(functools.partial(first_kernel, len(pieces), len(outs) //...  4.96 us
    pallas_call x3, Pallas kernels, product_stage(): pl.pallas_call(functools.partial(stage_kernel, stage, bits, dims, len(pie...  4.62 us
    ppermute x6, starting transfers between devices, forward(): lax.ppermute(sets[index, part], 'col', neighbours(groups))  4.53 us
    pallas_call x1, Pallas kernels, turn(): pl.pallas_call(turn_kernel, out_shape=[pltpu.VMEM(values.shape, values.dt...  2.91 us
  transfers between devices with their start and end apart: 30, of which 17 were waited for; matrix products, arithmetic and copies ran while one was open for 0% of the time, Pallas kernels for 21%

profile of v12, /device:TPU:0, one launch (start us, length us, event | category | flops | bytes accessed | tf_op | source)
XLA Modules:
  0.0 83.9 jit_solution(2992092273150679687)
XLA Ops:
  0.0 2.2 %start.1 = (bf16[16,128,128]{2,1,0:T(8,128)(2,1)S(1)}, bf16[16,128,128]{2,1,0:T(8,128)(2,1)S(1)}, f32[16,32,128]{2,1,0:T(8,128)S(1)}, f32[16,32,128]{2,1,0:T(8,1...) custom-call(f32[16,128,128]{2,1,0:T(8,128)} %bitcast.5, ...), custom_call_target="tpu_custom_call" | custom-call | tf_op jit(solution)/shard_map/start/pallas_call | solution.py:415
  2.2 4.1 %collective-permute-start.3 = (bf16[8,32,128]{2,1,0:T(8,128)(2,1)S(1)}, bf16[8,32,128]{2,1,0:T(8,128)(2,1)S(1)}, u32[]{:S(2)}, u32[]{:S(2)}) collective-permute-start(bf16[8,32,128]{2,1,0:T(8,128)(2,1)S(1)} %get-tuple-element.77), channel_id=1, source_target_pairs={{0,2},{1,3},{2,0},{3,1},{4,6},{5,7},{6,4},{7,5},{8,10},{9,11},{10,... | collective-permute-start | bytes 196616 | tf_op jit(solution)/shard_map/ppermute | solution.py:108
  6.3 1.6 %collective-permute-start.2 = (bf16[16,32,128]{2,1,0:T(8,128)(2,1)S(1)}, bf16[16,32,128]{2,1,0:T(8,128)(2,1)S(1)}, u32[]{:S(2)}, u32[]{:S(2)}) collective-permute-start(bf16[16,32,128]{2,1,0:T(8,128)(2,1)S(1)} %get-tuple-element.76.refs_0_), channel_id=1, source_target_pairs={{0,1},{1,0},{2,3},{3,2},{4,5},{5,4},{6,7},{7,6},{8,9},{9,8},{10,11... | collective-permute-start | bytes 393224 | tf_op jit(solution)/shard_map/ppermute | solution.py:109
  8.8 2.8 %order.1 = (s32[7,208]{1,0:T(8,128)S(4)}, s32[6]{0:T(128)S(4)}, bf16[192,128,128]{2,1,0:T(8,128)(2,1)S(1)}, f32[8,128]{1,0:T(8,128)S(1)}) custom-call(s32[1,1]{1,0:T(1,128)S(6)} %copy.57.count_ref, s32[1,1,192]{2,1,0:T(1,128)} %rows_hbm.1, s32[1,1,192]{2,1,0:T(1,128)} %cols_hbm.1, bf16[192,128,128]{2,1,0:T(8,128)(2,1)} %bitcast.4), custom_call_target="tpu_custom_call" | custom-call | tf_op jit(solution)/shard_map/order/pallas_call | solution.py:428
  11.9 2.0 %collective-permute-done.piece_ref = bf16[8,32,128]{2,1,0:T(8,128)(2,1)S(1)} collective-permute-done((bf16[8,32,128]{2,1,0:T(8,128)(2,1)S(1)}, bf16[8,32,128]{2,1,0:T(8,128)(2,1)S(1)}, u32[]{:S(2)}, u32[]{:S(2)}) %collective-permute-start) | collective-permute-done | bytes 65568 | tf_op jit(solution)/shard_map/ppermute | solution.py:108
  14.3 2.3 %stage0.3 = (f32[65,32,128]{2,1,0:T(8,128)S(1)}, f32[65,32,128]{2,1,0:T(8,128)S(1)}, f32[8,128]{1,0:T(8,128)}) custom-call(s32[7,208]{1,0:T(8,128)S(4)} %get-tuple-element.73.list_ref, s32[6]{0:T(128)S(4)} %get-tuple-element.71.total_ref, bf16[192,128,128]{2,1,0:T(8,128)(2,1)S(1)} %get-tuple-element.72.values_ref, ...), custom_call_target="tpu_custom_call" | custom-call | flops 75497472 | bytes 2359296 | tf_op jit(solution)/shard_map/stage0/pallas_call | solution.py:470
  16.6 2.0 %stage1.3 = (f32[65,32,128]{2,1,0:T(8,128)S(1)}, f32[65,32,128]{2,1,0:T(8,128)S(1)}) custom-call(s32[7,208]{1,0:T(8,128)S(4)} %get-tuple-element.73.list_ref, s32[6]{0:T(128)S(4)} %get-tuple-element.71.total_ref, bf16[192,128,128]{2,1,0:T(8,128)(2,1)S(1)} %get-tuple-element.72.values_ref, ...), custom_call_target="tpu_custom_call", output_to_operand_aliasing={{0}: (6, {}), {1}: (7, {})} | custom-call | flops 100663296 | bytes 3145728 | tf_op jit(solution)/shard_map/stage1/pallas_call | solution.py:483
  21.0 2.9 %collective-permute-start.7 = (bf16[16,32,128]{2,1,0:T(8,128)(2,1)S(1)}, bf16[16,32,128]{2,1,0:T(8,128)(2,1)S(1)}, u32[]{:S(2)}, u32[]{:S(2)}) collective-permute-start(bf16[16,32,128]{2,1,0:T(8,128)(2,1)S(1)} %get-tuple-element.88.refs_6_.refs_10_), channel_id=1, source_target_pairs={{0,24},{4,28},{8,16},{12,20},{16,8},{20,12},{24,0},{28,4},{1,25},{... | collective-permute-start | bytes 393224 | tf_op jit(solution)/shard_map/ppermute | solution.py:590
  24.9 2.9 %turn.1 = (bf16[192,128,128]{2,1,0:T(8,128)(2,1)S(1)}, f32[16,32,128]{2,1,0:T(8,128)S(1)}) custom-call(s32[6]{0:T(128)S(4)} %get-tuple-element.71.total_ref, bf16[192,128,128]{2,1,0:T(8,128)(2,1)S(1)} %get-tuple-element.72.values_ref, f32[16,32,128]{2,1,0:T(8,128)S(1)} %combine1.3.base_ref), custom_call_target="tpu_custom_call", output_to_operand_aliasing={{1}: (2, {})} | custom-call | flops 20000000000 | tf_op jit(solution)/shard_map/turn/pallas_call | solution.py:450
  27.8 2.7 %collective-permute-done.8.refs_1_ = bf16[16,32,128]{2,1,0:T(8,128)(2,1)S(1)} collective-permute-done((bf16[16,32,128]{2,1,0:T(8,128)(2,1)S(1)}, bf16[16,32,128]{2,1,0:T(8,128)(2,1)S(1)}, u32[]{:S(2)}, u32[]{:S(2)}) %collective-permute-start.8) | collective-permute-done | bytes 131104 | tf_op jit(solution)/shard_map/ppermute | solution.py:590
  31.6 2.8 %collective-permute-start.11 = (bf16[8,32,128]{2,1,0:T(8,128)(2,1)S(1)}, bf16[8,32,128]{2,1,0:T(8,128)(2,1)S(1)}, u32[]{:S(2)}, u32[]{:S(2)}) collective-permute-start(bf16[8,32,128]{2,1,0:T(8,128)(2,1)S(1)} %get-tuple-element.92.refs_3_), channel_id=1, source_target_pairs={{0,2},{1,3},{2,0},{3,1},{4,6},{5,7},{6,4},{7,5},{8,10},{9,11},{10,... | collective-permute-start | bytes 196616 | tf_op jit(solution)/shard_map/ppermute | solution.py:108
  35.7 2.4 %collective-permute-done.11.refs_1_ = bf16[8,32,128]{2,1,0:T(8,128)(2,1)S(1)} collective-permute-done((bf16[8,32,128]{2,1,0:T(8,128)(2,1)S(1)}, bf16[8,32,128]{2,1,0:T(8,128)(2,1)S(1)}, u32[]{:S(2)}, u32[]{:S(2)}) %collective-permute-start.11) | collective-permute-done | bytes 65568 | tf_op jit(solution)/shard_map/ppermute | solution.py:108
  38.1 1.2 %stage0.4 = (f32[65,32,128]{2,1,0:T(8,128)S(1)}, f32[65,32,128]{2,1,0:T(8,128)S(1)}, f32[8,128]{1,0:T(8,128)S(1)}) custom-call(s32[7,208]{1,0:T(8,128)S(4)} %get-tuple-element.73.list_ref, s32[6]{0:T(128)S(4)} %get-tuple-element.71.total_ref, bf16[192,128,128]{2,1,0:T(8,128)(2,1)S(1)} %get-tuple-element.95.values_ref, ...), custom_call_target="tpu_custom_call" | custom-call | flops 75497472 | bytes 2359296 | tf_op jit(solution)/shard_map/stage0/pallas_call | solution.py:470
  39.4 1.6 %collective-permute-done.10.piece_ref = bf16[8,32,128]{2,1,0:T(8,128)(2,1)S(1)} collective-permute-done((bf16[8,32,128]{2,1,0:T(8,128)(2,1)S(1)}, bf16[8,32,128]{2,1,0:T(8,128)(2,1)S(1)}, u32[]{:S(2)}, u32[]{:S(2)}) %collective-permute-start.10) | collective-permute-done | bytes 65568 | tf_op jit(solution)/shard_map/ppermute | solution.py:108
  40.9 1.5 %collective-permute-start.12 = (bf16[8,32,128]{2,1,0:T(8,128)(2,1)S(1)}, bf16[8,32,128]{2,1,0:T(8,128)(2,1)S(1)}, u32[]{:S(2)}, u32[]{:S(2)}) collective-permute-start(bf16[8,32,128]{2,1,0:T(8,128)(2,1)S(1)} %hold.6.refs_1_), channel_id=1, source_target_pairs={{0,1},{1,0},{2,3},{3,2},{4,5},{5,4},{6,7},{7,6},{8,9},{9,8},{10,11... | collective-permute-start | bytes 196616 | tf_op jit(solution)/shard_map/ppermute | solution.py:568
  42.5 1.3 %collective-permute-done.14.refs_2_ = bf16[8,32,128]{2,1,0:T(8,128)(2,1)S(1)} collective-permute-done((bf16[8,32,128]{2,1,0:T(8,128)(2,1)S(1)}, bf16[8,32,128]{2,1,0:T(8,128)(2,1)S(1)}, u32[]{:S(2)}, u32[]{:S(2)}) %collective-permute-start.14) | collective-permute-done | bytes 65568 | tf_op jit(solution)/shard_map/ppermute | solution.py:568
  43.8 1.3 %stage1.4 = (f32[65,32,128]{2,1,0:T(8,128)S(1)}, f32[65,32,128]{2,1,0:T(8,128)S(1)}) custom-call(s32[7,208]{1,0:T(8,128)S(4)} %get-tuple-element.73.list_ref, s32[6]{0:T(128)S(4)} %get-tuple-element.71.total_ref, bf16[192,128,128]{2,1,0:T(8,128)(2,1)S(1)} %get-tuple-element.95.values_ref, ...), custom_call_target="tpu_custom_call", output_to_operand_aliasing={{0}: (6, {}), {1}: (7, {})} | custom-call | flops 100663296 | bytes 3145728 | tf_op jit(solution)/shard_map/stage1/pallas_call | solution.py:483
  47.4 1.5 %collective-permute-start.17 = (bf16[16,32,128]{2,1,0:T(8,128)(2,1)S(1)}, bf16[16,32,128]{2,1,0:T(8,128)(2,1)S(1)}, u32[]{:S(2)}, u32[]{:S(2)}) collective-permute-start(bf16[16,32,128]{2,1,0:T(8,128)(2,1)S(1)} %get-tuple-element.108.refs_13_), channel_id=1, source_target_pairs={{0,24},{4,28},{8,16},{12,20},{16,8},{20,12},{24,0},{28,4},{1,25},{... | collective-permute-start | bytes 393224 | tf_op jit(solution)/shard_map/ppermute | solution.py:590
  48.9 1.4 %collective-permute-start.18 = (bf16[16,32,128]{2,1,0:T(8,128)(2,1)S(1)}, bf16[16,32,128]{2,1,0:T(8,128)(2,1)S(1)}, u32[]{:S(2)}, u32[]{:S(2)}) collective-permute-start(bf16[16,32,128]{2,1,0:T(8,128)(2,1)S(1)} %get-tuple-element.109.refs_14_), channel_id=1, source_target_pairs={{0,16},{4,20},{8,24},{12,28},{16,0},{20,4},{24,8},{28,12},{1,17},{... | collective-permute-start | bytes 393224 | tf_op jit(solution)/shard_map/ppermute | solution.py:590
  51.0 3.7 %collective-permute-done.17.refs_0_ = bf16[16,32,128]{2,1,0:T(8,128)(2,1)S(1)} collective-permute-done((bf16[16,32,128]{2,1,0:T(8,128)(2,1)S(1)}, bf16[16,32,128]{2,1,0:T(8,128)(2,1)S(1)}, u32[]{:S(2)}, u32[]{:S(2)}) %collective-permute-start.17) | collective-permute-done | bytes 131104 | tf_op jit(solution)/shard_map/ppermute | solution.py:590
  54.7 2.0 %collective-permute-done.18.refs_1_ = bf16[16,32,128]{2,1,0:T(8,128)(2,1)S(1)} collective-permute-done((bf16[16,32,128]{2,1,0:T(8,128)(2,1)S(1)}, bf16[16,32,128]{2,1,0:T(8,128)(2,1)S(1)}, u32[]{:S(2)}, u32[]{:S(2)}) %collective-permute-start.18) | collective-permute-done | bytes 131104 | tf_op jit(solution)/shard_map/ppermute | solution.py:590
  57.1 3.2 %collective-permute-start.21 = (bf16[8,32,128]{2,1,0:T(8,128)(2,1)S(1)}, bf16[8,32,128]{2,1,0:T(8,128)(2,1)S(1)}, u32[]{:S(2)}, u32[]{:S(2)}) collective-permute-start(bf16[8,32,128]{2,1,0:T(8,128)(2,1)S(1)} %get-tuple-element.112.refs_3_), channel_id=1, source_target_pairs={{0,2},{1,3},{2,0},{3,1},{4,6},{5,7},{6,4},{7,5},{8,10},{9,11},{10,... | collective-permute-start | bytes 196616 | tf_op jit(solution)/shard_map/ppermute | solution.py:108
  60.8 1.2 %collective-permute-start.20 = (bf16[8,32,128]{2,1,0:T(8,128)(2,1)S(1)}, bf16[8,32,128]{2,1,0:T(8,128)(2,1)S(1)}, u32[]{:S(2)}, u32[]{:S(2)}) collective-permute-start(bf16[8,32,128]{2,1,0:T(8,128)(2,1)S(1)} %get-tuple-element.114), channel_id=1, source_target_pairs={{0,2},{1,3},{2,0},{3,1},{4,6},{5,7},{6,4},{7,5},{8,10},{9,11},{10,... | collective-permute-start | bytes 196616 | tf_op jit(solution)/shard_map/ppermute | solution.py:108
  62.0 2.0 %collective-permute-done.21.refs_1_ = bf16[8,32,128]{2,1,0:T(8,128)(2,1)S(1)} collective-permute-done((bf16[8,32,128]{2,1,0:T(8,128)(2,1)S(1)}, bf16[8,32,128]{2,1,0:T(8,128)(2,1)S(1)}, u32[]{:S(2)}, u32[]{:S(2)}) %collective-permute-start.21) | collective-permute-done | bytes 65568 | tf_op jit(solution)/shard_map/ppermute | solution.py:108
  64.4 1.4 %stage0.5 = (f32[65,32,128]{2,1,0:T(8,128)S(1)}, f32[65,32,128]{2,1,0:T(8,128)S(1)}, f32[8,128]{1,0:T(8,128)S(1)}) custom-call(s32[7,208]{1,0:T(8,128)S(4)} %get-tuple-element.73.list_ref, s32[6]{0:T(128)S(4)} %get-tuple-element.71.total_ref, bf16[192,128,128]{2,1,0:T(8,128)(2,1)S(1)} %get-tuple-element.95.values_ref, ...), custom_call_target="tpu_custom_call" | custom-call | flops 75497472 | bytes 2359296 | tf_op jit(solution)/shard_map/stage0/pallas_call | solution.py:470
  66.7 2.0 %collective-permute-start.22 = (bf16[8,32,128]{2,1,0:T(8,128)(2,1)S(1)}, bf16[8,32,128]{2,1,0:T(8,128)(2,1)S(1)}, u32[]{:S(2)}, u32[]{:S(2)}) collective-permute-start(bf16[8,32,128]{2,1,0:T(8,128)(2,1)S(1)} %hold.7.refs_1_), channel_id=1, source_target_pairs={{0,1},{1,0},{2,3},{3,2},{4,5},{5,4},{6,7},{7,6},{8,9},{9,8},{10,11... | collective-permute-start | bytes 196616 | tf_op jit(solution)/shard_map/ppermute | solution.py:568
  69.7 1.3 %stage1.5 = (f32[65,32,128]{2,1,0:T(8,128)S(1)}, f32[65,32,128]{2,1,0:T(8,128)S(1)}) custom-call(s32[7,208]{1,0:T(8,128)S(4)} %get-tuple-element.73.list_ref, s32[6]{0:T(128)S(4)} %get-tuple-element.71.total_ref, bf16[192,128,128]{2,1,0:T(8,128)(2,1)S(1)} %get-tuple-element.95.values_ref, ...), custom_call_target="tpu_custom_call", output_to_operand_aliasing={{0}: (6, {}), {1}: (7, {})} | custom-call | flops 100663296 | bytes 3145728 | tf_op jit(solution)/shard_map/stage1/pallas_call | solution.py:483
  73.2 1.4 %collective-permute-start.27 = (bf16[16,32,128]{2,1,0:T(8,128)(2,1)S(1)}, bf16[16,32,128]{2,1,0:T(8,128)(2,1)S(1)}, u32[]{:S(2)}, u32[]{:S(2)}) collective-permute-start(bf16[16,32,128]{2,1,0:T(8,128)(2,1)S(1)} %get-tuple-element.127), channel_id=1, source_target_pairs={{0,24},{4,28},{8,16},{12,20},{16,8},{20,12},{24,0},{28,4},{1,25},{... | collective-permute-start | bytes 393224 | tf_op jit(solution)/shard_map/ppermute | solution.py:590
  74.6 1.2 %collective-permute-start.28 = (bf16[16,32,128]{2,1,0:T(8,128)(2,1)S(1)}, bf16[16,32,128]{2,1,0:T(8,128)(2,1)S(1)}, u32[]{:S(2)}, u32[]{:S(2)}) collective-permute-start(bf16[16,32,128]{2,1,0:T(8,128)(2,1)S(1)} %get-tuple-element.128), channel_id=1, source_target_pairs={{0,16},{4,20},{8,24},{12,28},{16,0},{20,4},{24,8},{28,12},{1,17},{... | collective-permute-start | bytes 393224 | tf_op jit(solution)/shard_map/ppermute | solution.py:590
  76.8 3.7 %collective-permute-done.27.refs_0_ = bf16[16,32,128]{2,1,0:T(8,128)(2,1)S(1)} collective-permute-done((bf16[16,32,128]{2,1,0:T(8,128)(2,1)S(1)}, bf16[16,32,128]{2,1,0:T(8,128)(2,1)S(1)}, u32[]{:S(2)}, u32[]{:S(2)}) %collective-permute-start.27) | collective-permute-done | bytes 131104 | tf_op jit(solution)/shard_map/ppermute | solution.py:590
  80.5 2.0 %collective-permute-done.28.refs_1_ = bf16[16,32,128]{2,1,0:T(8,128)(2,1)S(1)} collective-permute-done((bf16[16,32,128]{2,1,0:T(8,128)(2,1)S(1)}, bf16[16,32,128]{2,1,0:T(8,128)(2,1)S(1)}, u32[]{:S(2)}, u32[]{:S(2)}) %collective-permute-start.28) | collective-permute-done | bytes 131104 | tf_op jit(solution)/shard_map/ppermute | solution.py:590
  82.5 1.4 %finish.1 = f32[16,32,128]{2,1,0:T(8,128)} custom-call(bf16[16,128,128]{2,1,0:T(8,128)(2,1)S(1)} %get-tuple-element.67.high_ref, bf16[16,128,128]{2,1,0:T(8,128)(2,1)S(1)} %get-tuple-element.68.low_ref, f32[16,32,128]{2,1,0:T(8,128)S(1)} %get-tuple-element.113.sol_ref, f32[16,32,128]{2,1,0:T(8,128)S(1)} %combine1.5.base_ref, ...), custom_call_target="tpu_custom_call" | custom-call | tf_op jit(solution)/shard_map/finish/pallas_call | solution.py:605
  (58 shorter events, 16.1 us)
Async XLA Ops:
  2.2 9.5 %collective-permute-start.3 = (bf16[8,32,128]{2,1,0:T(8,128)(2,1)S(1)}, bf16[8,32,128]{2,1,0:T(8,128)(2,1)S(1)}, u32[]{:S(2)}, u32[]{:S(2)}) collective-permute-start(bf16[8,32,128]{2,1,0:T(8,128)(2,1)S(1)} %get-tuple-element.77), channel_id=1, source_target_pairs={{0,2},{1,3},{2,0},{3,1},{4,6},{5,7},{6,4},{7,5},{8,10},{9,11},{10,... | collective-permute-start | bytes 196616 | tf_op jit(solution)/shard_map/ppermute | solution.py:108
  6.3 10.4 %collective-permute-start.2 = (bf16[16,32,128]{2,1,0:T(8,128)(2,1)S(1)}, bf16[16,32,128]{2,1,0:T(8,128)(2,1)S(1)}, u32[]{:S(2)}, u32[]{:S(2)}) collective-permute-start(bf16[16,32,128]{2,1,0:T(8,128)(2,1)S(1)} %get-tuple-element.76.refs_0_), channel_id=1, source_target_pairs={{0,1},{1,0},{2,3},{3,2},{4,5},{5,4},{6,7},{7,6},{8,9},{9,8},{10,11... | collective-permute-start | bytes 393224 | tf_op jit(solution)/shard_map/ppermute | solution.py:109
  7.8 6.1 %collective-permute-start = (bf16[8,32,128]{2,1,0:T(8,128)(2,1)S(1)}, bf16[8,32,128]{2,1,0:T(8,128)(2,1)S(1)}, u32[]{:S(2)}, u32[]{:S(2)}) collective-permute-start(bf16[8,32,128]{2,1,0:T(8,128)(2,1)S(1)} %get-tuple-element.74), channel_id=1, source_target_pairs={{0,2},{1,3},{2,0},{3,1},{4,6},{5,7},{6,4},{7,5},{8,10},{9,11},{10,... | collective-permute-start | bytes 196616 | tf_op jit(solution)/shard_map/ppermute | solution.py:108
  11.7 5.0 %collective-permute-start.4 = (bf16[8,32,128]{2,1,0:T(8,128)(2,1)S(1)}, bf16[8,32,128]{2,1,0:T(8,128)(2,1)S(1)}, u32[]{:S(2)}, u32[]{:S(2)}) collective-permute-start(bf16[8,32,128]{2,1,0:T(8,128)(2,1)S(1)} %hold.5.refs_1_), channel_id=1, source_target_pairs={{0,1},{1,0},{2,3},{3,2},{4,5},{5,4},{6,7},{7,6},{8,9},{9,8},{10,11... | collective-permute-start | bytes 196616 | tf_op jit(solution)/shard_map/ppermute | solution.py:568
  13.9 4.7 %collective-permute-start.1 = (bf16[8,32,128]{2,1,0:T(8,128)(2,1)S(1)}, bf16[8,32,128]{2,1,0:T(8,128)(2,1)S(1)}, u32[]{:S(2)}, u32[]{:S(2)}) collective-permute-start(bf16[8,32,128]{2,1,0:T(8,128)(2,1)S(1)} %hold.4.refs_1_), channel_id=1, source_target_pairs={{0,1},{1,0},{2,3},{3,2},{4,5},{5,4},{6,7},{7,6},{8,9},{9,8},{10,11... | collective-permute-start | bytes 196616 | tf_op jit(solution)/shard_map/ppermute | solution.py:568
  19.1 1.8 %collective-permute-start.6 = (bf16[48,32,128]{2,1,0:T(8,128)(2,1)S(1)}, bf16[48,32,128]{2,1,0:T(8,128)(2,1)S(1)}, u32[]{:S(2)}, u32[]{:S(2)}) collective-permute-start(bf16[48,32,128]{2,1,0:T(8,128)(2,1)S(1)} %get-tuple-element.85.refs_2_), channel_id=1, source_target_pairs={{0,4},{4,0},{8,12},{12,8},{16,20},{20,16},{24,28},{28,24},{1,5},{5... | collective-permute-start | bytes 1179656 | tf_op jit(solution)/shard_map/ppermute | solution.py:582
  19.6 5.2 %collective-permute-start.5 = (bf16[16,32,128]{2,1,0:T(8,128)(2,1)S(1)}, bf16[16,32,128]{2,1,0:T(8,128)(2,1)S(1)}, u32[]{:S(2)}, u32[]{:S(2)}) collective-permute-start(bf16[16,32,128]{2,1,0:T(8,128)(2,1)S(1)} %get-tuple-element.84.refs_3_), channel_id=1, source_target_pairs={{0,4},{4,0},{8,12},{12,8},{16,20},{20,16},{24,28},{28,24},{1,5},{5... | collective-permute-start | bytes 393224 | tf_op jit(solution)/shard_map/ppermute | solution.py:582
  21.0 6.8 %collective-permute-start.7 = (bf16[16,32,128]{2,1,0:T(8,128)(2,1)S(1)}, bf16[16,32,128]{2,1,0:T(8,128)(2,1)S(1)}, u32[]{:S(2)}, u32[]{:S(2)}) collective-permute-start(bf16[16,32,128]{2,1,0:T(8,128)(2,1)S(1)} %get-tuple-element.88.refs_6_.refs_10_), channel_id=1, source_target_pairs={{0,24},{4,28},{8,16},{12,20},{16,8},{20,12},{24,0},{28,4},{1,25},{... | collective-permute-start | bytes 393224 | tf_op jit(solution)/shard_map/ppermute | solution.py:590
  23.9 6.6 %collective-permute-start.8 = (bf16[16,32,128]{2,1,0:T(8,128)(2,1)S(1)}, bf16[16,32,128]{2,1,0:T(8,128)(2,1)S(1)}, u32[]{:S(2)}, u32[]{:S(2)}) collective-permute-start(bf16[16,32,128]{2,1,0:T(8,128)(2,1)S(1)} %get-tuple-element.89.refs_7_.refs_11_), channel_id=1, source_target_pairs={{0,16},{4,20},{8,24},{12,28},{16,0},{20,4},{24,8},{28,12},{1,17},{... | collective-permute-start | bytes 393224 | tf_op jit(solution)/shard_map/ppermute | solution.py:590
  24.0 7.2 %collective-permute-start.9 = (bf16[16,32,128]{2,1,0:T(8,128)(2,1)S(1)}, bf16[16,32,128]{2,1,0:T(8,128)(2,1)S(1)}, u32[]{:S(2)}, u32[]{:S(2)}) collective-permute-start(bf16[16,32,128]{2,1,0:T(8,128)(2,1)S(1)} %get-tuple-element.86.before_ref.refs_8_.refs_12_), channel_id=1, source_target_pairs={{0,8},{4,12},{8,0},{12,4},{16,24},{20,28},{24,16},{28,20},{1,9},{5... | collective-permute-start | bytes 393224 | tf_op jit(solution)/shard_map/ppermute | solution.py:590
  31.6 6.5 %collective-permute-start.11 = (bf16[8,32,128]{2,1,0:T(8,128)(2,1)S(1)}, bf16[8,32,128]{2,1,0:T(8,128)(2,1)S(1)}, u32[]{:S(2)}, u32[]{:S(2)}) collective-permute-start(bf16[8,32,128]{2,1,0:T(8,128)(2,1)S(1)} %get-tuple-element.92.refs_3_), channel_id=1, source_target_pairs={{0,2},{1,3},{2,0},{3,1},{4,6},{5,7},{6,4},{7,5},{8,10},{9,11},{10,... | collective-permute-start | bytes 196616 | tf_op jit(solution)/shard_map/ppermute | solution.py:108
  34.7 9.0 %collective-permute-start.13 = (bf16[16,32,128]{2,1,0:T(8,128)(2,1)S(1)}, bf16[16,32,128]{2,1,0:T(8,128)(2,1)S(1)}, u32[]{:S(2)}, u32[]{:S(2)}) collective-permute-start(bf16[16,32,128]{2,1,0:T(8,128)(2,1)S(1)} %get-tuple-element.97.refs_0_), channel_id=1, source_target_pairs={{0,1},{1,0},{2,3},{3,2},{4,5},{5,4},{6,7},{7,6},{8,9},{9,8},{10,11... | collective-permute-start | bytes 393224 | tf_op jit(solution)/shard_map/ppermute | solution.py:109
  35.1 5.8 %collective-permute-start.10 = (bf16[8,32,128]{2,1,0:T(8,128)(2,1)S(1)}, bf16[8,32,128]{2,1,0:T(8,128)(2,1)S(1)}, u32[]{:S(2)}, u32[]{:S(2)}) collective-permute-start(bf16[8,32,128]{2,1,0:T(8,128)(2,1)S(1)} %get-tuple-element.96), channel_id=1, source_target_pairs={{0,2},{1,3},{2,0},{3,1},{4,6},{5,7},{6,4},{7,5},{8,10},{9,11},{10,... | collective-permute-start | bytes 196616 | tf_op jit(solution)/shard_map/ppermute | solution.py:108
  38.1 5.6 %collective-permute-start.14 = (bf16[8,32,128]{2,1,0:T(8,128)(2,1)S(1)}, bf16[8,32,128]{2,1,0:T(8,128)(2,1)S(1)}, u32[]{:S(2)}, u32[]{:S(2)}) collective-permute-start(bf16[8,32,128]{2,1,0:T(8,128)(2,1)S(1)} %collective-permute-done.11.refs_1_), channel_id=1, source_target_pairs={{0,1},{1,0},{2,3},{3,2},{4,5},{5,4},{6,7},{7,6},{8,9},{9,8},{10,11... | collective-permute-start | bytes 196616 | tf_op jit(solution)/shard_map/ppermute | solution.py:568
  40.9 4.3 %collective-permute-start.12 = (bf16[8,32,128]{2,1,0:T(8,128)(2,1)S(1)}, bf16[8,32,128]{2,1,0:T(8,128)(2,1)S(1)}, u32[]{:S(2)}, u32[]{:S(2)}) collective-permute-start(bf16[8,32,128]{2,1,0:T(8,128)(2,1)S(1)} %hold.6.refs_1_), channel_id=1, source_target_pairs={{0,1},{1,0},{2,3},{3,2},{4,5},{5,4},{6,7},{7,6},{8,9},{9,8},{10,11... | collective-permute-start | bytes 196616 | tf_op jit(solution)/shard_map/ppermute | solution.py:568
  45.5 1.8 %collective-permute-start.16 = (bf16[48,32,128]{2,1,0:T(8,128)(2,1)S(1)}, bf16[48,32,128]{2,1,0:T(8,128)(2,1)S(1)}, u32[]{:S(2)}, u32[]{:S(2)}) collective-permute-start(bf16[48,32,128]{2,1,0:T(8,128)(2,1)S(1)} %get-tuple-element.106.refs_4_), channel_id=1, source_target_pairs={{0,4},{4,0},{8,12},{12,8},{16,20},{20,16},{24,28},{28,24},{1,5},{5... | collective-permute-start | bytes 1179656 | tf_op jit(solution)/shard_map/ppermute | solution.py:582
  45.9 5.0 %collective-permute-start.15 = (bf16[16,32,128]{2,1,0:T(8,128)(2,1)S(1)}, bf16[16,32,128]{2,1,0:T(8,128)(2,1)S(1)}, u32[]{:S(2)}, u32[]{:S(2)}) collective-permute-start(bf16[16,32,128]{2,1,0:T(8,128)(2,1)S(1)} %get-tuple-element.105.refs_5_), channel_id=1, source_target_pairs={{0,4},{4,0},{8,12},{12,8},{16,20},{20,16},{24,28},{28,24},{1,5},{5... | collective-permute-start | bytes 393224 | tf_op jit(solution)/shard_map/ppermute | solution.py:582
  47.4 7.3 %collective-permute-start.17 = (bf16[16,32,128]{2,1,0:T(8,128)(2,1)S(1)}, bf16[16,32,128]{2,1,0:T(8,128)(2,1)S(1)}, u32[]{:S(2)}, u32[]{:S(2)}) collective-permute-start(bf16[16,32,128]{2,1,0:T(8,128)(2,1)S(1)} %get-tuple-element.108.refs_13_), channel_id=1, source_target_pairs={{0,24},{4,28},{8,16},{12,20},{16,8},{20,12},{24,0},{28,4},{1,25},{... | collective-permute-start | bytes 393224 | tf_op jit(solution)/shard_map/ppermute | solution.py:590
  48.9 7.8 %collective-permute-start.18 = (bf16[16,32,128]{2,1,0:T(8,128)(2,1)S(1)}, bf16[16,32,128]{2,1,0:T(8,128)(2,1)S(1)}, u32[]{:S(2)}, u32[]{:S(2)}) collective-permute-start(bf16[16,32,128]{2,1,0:T(8,128)(2,1)S(1)} %get-tuple-element.109.refs_14_), channel_id=1, source_target_pairs={{0,16},{4,20},{8,24},{12,28},{16,0},{20,4},{24,8},{28,12},{1,17},{... | collective-permute-start | bytes 393224 | tf_op jit(solution)/shard_map/ppermute | solution.py:590
  50.3 6.4 %collective-permute-start.19 = (bf16[16,32,128]{2,1,0:T(8,128)(2,1)S(1)}, bf16[16,32,128]{2,1,0:T(8,128)(2,1)S(1)}, u32[]{:S(2)}, u32[]{:S(2)}) collective-permute-start(bf16[16,32,128]{2,1,0:T(8,128)(2,1)S(1)} %get-tuple-element.107.before_ref.refs_15_), channel_id=1, source_target_pairs={{0,8},{4,12},{8,0},{12,4},{16,24},{20,28},{24,16},{28,20},{1,9},{5... | collective-permute-start | bytes 393224 | tf_op jit(solution)/shard_map/ppermute | solution.py:590
  57.1 6.9 %collective-permute-start.21 = (bf16[8,32,128]{2,1,0:T(8,128)(2,1)S(1)}, bf16[8,32,128]{2,1,0:T(8,128)(2,1)S(1)}, u32[]{:S(2)}, u32[]{:S(2)}) collective-permute-start(bf16[8,32,128]{2,1,0:T(8,128)(2,1)S(1)} %get-tuple-element.112.refs_3_), channel_id=1, source_target_pairs={{0,2},{1,3},{2,0},{3,1},{4,6},{5,7},{6,4},{7,5},{8,10},{9,11},{10,... | collective-permute-start | bytes 196616 | tf_op jit(solution)/shard_map/ppermute | solution.py:108
  60.7 8.0 %collective-permute-start.23 = (bf16[16,32,128]{2,1,0:T(8,128)(2,1)S(1)}, bf16[16,32,128]{2,1,0:T(8,128)(2,1)S(1)}, u32[]{:S(2)}, u32[]{:S(2)}) collective-permute-start(bf16[16,32,128]{2,1,0:T(8,128)(2,1)S(1)} %get-tuple-element.115.refs_0_), channel_id=1, source_target_pairs={{0,1},{1,0},{2,3},{3,2},{4,5},{5,4},{6,7},{7,6},{8,9},{9,8},{10,11... | collective-permute-start | bytes 393224 | tf_op jit(solution)/shard_map/ppermute | solution.py:109
  60.8 5.9 %collective-permute-start.20 = (bf16[8,32,128]{2,1,0:T(8,128)(2,1)S(1)}, bf16[8,32,128]{2,1,0:T(8,128)(2,1)S(1)}, u32[]{:S(2)}, u32[]{:S(2)}) collective-permute-start(bf16[8,32,128]{2,1,0:T(8,128)(2,1)S(1)} %get-tuple-element.114), channel_id=1, source_target_pairs={{0,2},{1,3},{2,0},{3,1},{4,6},{5,7},{6,4},{7,5},{8,10},{9,11},{10,... | collective-permute-start | bytes 196616 | tf_op jit(solution)/shard_map/ppermute | solution.py:108
  64.0 5.7 %collective-permute-start.24 = (bf16[8,32,128]{2,1,0:T(8,128)(2,1)S(1)}, bf16[8,32,128]{2,1,0:T(8,128)(2,1)S(1)}, u32[]{:S(2)}, u32[]{:S(2)}) collective-permute-start(bf16[8,32,128]{2,1,0:T(8,128)(2,1)S(1)} %collective-permute-done.21.refs_1_), channel_id=1, source_target_pairs={{0,1},{1,0},{2,3},{3,2},{4,5},{5,4},{6,7},{7,6},{8,9},{9,8},{10,11... | collective-permute-start | bytes 196616 | tf_op jit(solution)/shard_map/ppermute | solution.py:568
  66.7 4.3 %collective-permute-start.22 = (bf16[8,32,128]{2,1,0:T(8,128)(2,1)S(1)}, bf16[8,32,128]{2,1,0:T(8,128)(2,1)S(1)}, u32[]{:S(2)}, u32[]{:S(2)}) collective-permute-start(bf16[8,32,128]{2,1,0:T(8,128)(2,1)S(1)} %hold.7.refs_1_), channel_id=1, source_target_pairs={{0,1},{1,0},{2,3},{3,2},{4,5},{5,4},{6,7},{7,6},{8,9},{9,8},{10,11... | collective-permute-start | bytes 196616 | tf_op jit(solution)/shard_map/ppermute | solution.py:568
  71.3 1.8 %collective-permute-start.26 = (bf16[48,32,128]{2,1,0:T(8,128)(2,1)S(1)}, bf16[48,32,128]{2,1,0:T(8,128)(2,1)S(1)}, u32[]{:S(2)}, u32[]{:S(2)}) collective-permute-start(bf16[48,32,128]{2,1,0:T(8,128)(2,1)S(1)} %get-tuple-element.125), channel_id=1, source_target_pairs={{0,4},{4,0},{8,12},{12,8},{16,20},{20,16},{24,28},{28,24},{1,5},{5... | collective-permute-start | bytes 1179656 | tf_op jit(solution)/shard_map/ppermute | solution.py:582
  71.7 5.0 %collective-permute-start.25 = (bf16[16,32,128]{2,1,0:T(8,128)(2,1)S(1)}, bf16[16,32,128]{2,1,0:T(8,128)(2,1)S(1)}, u32[]{:S(2)}, u32[]{:S(2)}) collective-permute-start(bf16[16,32,128]{2,1,0:T(8,128)(2,1)S(1)} %get-tuple-element.123), channel_id=1, source_target_pairs={{0,4},{4,0},{8,12},{12,8},{16,20},{20,16},{24,28},{28,24},{1,5},{5... | collective-permute-start | bytes 393224 | tf_op jit(solution)/shard_map/ppermute | solution.py:582
  73.2 7.3 %collective-permute-start.27 = (bf16[16,32,128]{2,1,0:T(8,128)(2,1)S(1)}, bf16[16,32,128]{2,1,0:T(8,128)(2,1)S(1)}, u32[]{:S(2)}, u32[]{:S(2)}) collective-permute-start(bf16[16,32,128]{2,1,0:T(8,128)(2,1)S(1)} %get-tuple-element.127), channel_id=1, source_target_pairs={{0,24},{4,28},{8,16},{12,20},{16,8},{20,12},{24,0},{28,4},{1,25},{... | collective-permute-start | bytes 393224 | tf_op jit(solution)/shard_map/ppermute | solution.py:590
  74.6 7.9 %collective-permute-start.28 = (bf16[16,32,128]{2,1,0:T(8,128)(2,1)S(1)}, bf16[16,32,128]{2,1,0:T(8,128)(2,1)S(1)}, u32[]{:S(2)}, u32[]{:S(2)}) collective-permute-start(bf16[16,32,128]{2,1,0:T(8,128)(2,1)S(1)} %get-tuple-element.128), channel_id=1, source_target_pairs={{0,16},{4,20},{8,24},{12,28},{16,0},{20,4},{24,8},{28,12},{1,17},{... | collective-permute-start | bytes 393224 | tf_op jit(solution)/shard_map/ppermute | solution.py:590
  75.8 6.7 %collective-permute-start.29 = (bf16[16,32,128]{2,1,0:T(8,128)(2,1)S(1)}, bf16[16,32,128]{2,1,0:T(8,128)(2,1)S(1)}, u32[]{:S(2)}, u32[]{:S(2)}) collective-permute-start(bf16[16,32,128]{2,1,0:T(8,128)(2,1)S(1)} %get-tuple-element.126.before_ref), channel_id=1, source_target_pairs={{0,8},{4,12},{8,0},{12,4},{16,24},{20,28},{24,16},{28,20},{1,9},{5... | collective-permute-start | bytes 393224 | tf_op jit(solution)/shard_map/ppermute | solution.py:590

commit v13 on v12

--- a/solution.py
+++ b/solution.py
@@ -107,6 +107,9 @@
         for step in range(1, groups // 2):
             sets[step, part] = lax.ppermute(piece, "col", ring(groups, 2 * step))
     sets[groups // 2, 0] = lax.ppermute(whole, "col", neighbours(groups))
+    for step in range(1, groups // 2):
+        across = [(c, ((c + 2 * step) % groups) ^ 1) for c in range(groups)]
+        sets[groups // 2 + step, len(rounded) - 1] = lax.ppermute(rounded[-1], "col", across)
     return sets
 
 
@@ -570,9 +573,7 @@
         if groups % 2 == 0:
             for part in range(parts - 1):
                 forward(part, order_token if step == 0 else None)
-        *totals, token = product_first(*blocks, stage_pieces(0), outs, ins, sent)
-        if groups % 2 == 0:
-            forward(parts - 1, order_token if step == 0 else token)
+        *totals, _ = product_first(*blocks, stage_pieces(0), outs, ins, sent)
 
         for stage in range(1, final):
             totals = product_stage(*blocks, stage, stage_pieces(stage), totals)

time: 84.1 us -> 83.4 us (level)
  waiting for transfers between devices: 28.5 us -> 21.3 us
  Pallas kernels: 23 us -> 29.8 us
    ppermute x0 -> x3, starting transfers between devices: none -> 6.45 us  [gather(): lax.ppermute(rounded[-1], 'col', across)]
    ppermute x6, waiting for transfers between devices: 8.89 us -> 4.51 us  [gather(): sets[step, part] = lax.ppermute(piece, 'col', ring(groups, 2 * step))]
    ppermute x6 -> x3, starting transfers between devices: 4.53 us -> 0.23 us  [forward(): lax.ppermute(sets[index, part], 'col', neighbours(groups))]
    ppermute x6, starting transfers between devices: 12.2 us -> 8.64 us  [gather(): sets[step, part] = lax.ppermute(piece, 'col', ring(groups, 2 * step))]
    pallas_call x3, Pallas kernels: 4.96 us -> 7.98 us  [product_first(): pl.pallas_call(functools.partial(first_kernel, len(pieces), len(outs) //...]
    pallas_call x3, Pallas kernels: 4.62 us -> 6.44 us  [product_stage(): pl.pallas_call(functools.partial(stage_kernel, stage, bits, dims, len(pie...]
    ppermute x9, waiting for transfers between devices: 14.8 us -> 13 us  [per_device(): lax.ppermute(send, 'row', [(chip * CORES + core, partner(chip, shift, chi...]
    ppermute x3, starting transfers between devices: 2.05 us -> 3.84 us  [gather(): sets[groups // 2, 0] = lax.ppermute(whole, 'col', neighbours(groups))]
  transfers between devices with their start and end apart: 30 -> 30, of which waited for: 17 -> 15; matrix products, arithmetic and copies ran while one was open for 0% -> 0% of each run, Pallas kernels for 21% -> 29%
where the time goes in v13:
time: 83.4 us; the launch traced here: 83.7 us
  starting transfers between devices  31.7 us (38%)
  Pallas kernels  29.8 us (36%)
  waiting for transfers between devices  21.3 us (26%)
  between operations  0.87 us (1%)
    ppermute x9, waiting for transfers between devices, per_device(): lax.ppermute(send, 'row', [(chip * CORES + core, partner(chip, shift, chi...  13 us
    ppermute x9, starting transfers between devices, per_device(): lax.ppermute(send, 'row', [(chip * CORES + core, partner(chip, shift, chi...  10.7 us
    ppermute x6, starting transfers between devices, gather(): sets[step, part] = lax.ppermute(piece, 'col', ring(groups, 2 * step))  8.64 us
    pallas_call x3, Pallas kernels, product_first(): pl.pallas_call(functools.partial(first_kernel, len(pieces), len(outs) //...  7.98 us
    ppermute x3, starting transfers between devices, gather(): lax.ppermute(rounded[-1], 'col', across)  6.45 us
    pallas_call x3, Pallas kernels, product_stage(): pl.pallas_call(functools.partial(stage_kernel, stage, bits, dims, len(pie...  6.44 us
    ppermute x6, waiting for transfers between devices, gather(): sets[step, part] = lax.ppermute(piece, 'col', ring(groups, 2 * step))  4.51 us
    pallas_call x1, Pallas kernels, turn(): pl.pallas_call(turn_kernel, out_shape=[pltpu.VMEM(values.shape, values.dt...  4.23 us
  transfers between devices with their start and end apart: 30, of which 15 were waited for; matrix products, arithmetic and copies ran while one was open for 0% of the time, Pallas kernels for 29%

profile of v13, /device:TPU:0, one launch (start us, length us, event | category | flops | bytes accessed | tf_op | source)
XLA Modules:
  0.0 83.7 jit_solution(7796493363618200831)
XLA Ops:
  0.0 2.2 %start.1 = (bf16[16,128,128]{2,1,0:T(8,128)(2,1)S(1)}, bf16[16,128,128]{2,1,0:T(8,128)(2,1)S(1)}, f32[16,32,128]{2,1,0:T(8,128)S(1)}, f32[16,32,128]{2,1,0:T(8,1...) custom-call(f32[16,128,128]{2,1,0:T(8,128)} %bitcast.5, ...), custom_call_target="tpu_custom_call" | custom-call | tf_op jit(solution)/shard_map/start/pallas_call | solution.py:418
  2.2 4.1 %collective-permute-start.3 = (bf16[8,32,128]{2,1,0:T(8,128)(2,1)S(1)}, bf16[8,32,128]{2,1,0:T(8,128)(2,1)S(1)}, u32[]{:S(2)}, u32[]{:S(2)}) collective-permute-start(bf16[8,32,128]{2,1,0:T(8,128)(2,1)S(1)} %get-tuple-element.74), channel_id=1, source_target_pairs={{0,2},{1,3},{2,0},{3,1},{4,6},{5,7},{6,4},{7,5},{8,10},{9,11},{10,... | collective-permute-start | bytes 196616 | tf_op jit(solution)/shard_map/ppermute | solution.py:108
  6.3 1.6 %collective-permute-start.1 = (bf16[16,32,128]{2,1,0:T(8,128)(2,1)S(1)}, bf16[16,32,128]{2,1,0:T(8,128)(2,1)S(1)}, u32[]{:S(2)}, u32[]{:S(2)}) collective-permute-start(bf16[16,32,128]{2,1,0:T(8,128)(2,1)S(1)} %get-tuple-element.73.refs_0_), channel_id=1, source_target_pairs={{0,1},{1,0},{2,3},{3,2},{4,5},{5,4},{6,7},{7,6},{8,9},{9,8},{10,11... | collective-permute-start | bytes 393224 | tf_op jit(solution)/shard_map/ppermute | solution.py:109
  8.8 3.4 %order.1 = (s32[7,208]{1,0:T(8,128)S(4)}, s32[6]{0:T(128)S(4)}, bf16[192,128,128]{2,1,0:T(8,128)(2,1)S(1)}, f32[8,128]{1,0:T(8,128)S(1)}) custom-call(s32[1,1]{1,0:T(1,128)S(6)} %copy.51.count_ref, s32[1,1,192]{2,1,0:T(1,128)} %rows_hbm.1, s32[1,1,192]{2,1,0:T(1,128)} %cols_hbm.1, bf16[192,128,128]{2,1,0:T(8,128)(2,1)} %bitcast.4), custom_call_target="tpu_custom_call" | custom-call | tf_op jit(solution)/shard_map/order/pallas_call | solution.py:431
  12.4 3.4 %collective-permute-start = (bf16[8,32,128]{2,1,0:T(8,128)(2,1)S(1)}, bf16[8,32,128]{2,1,0:T(8,128)(2,1)S(1)}, u32[]{:S(2)}, u32[]{:S(2)}) collective-permute-start(bf16[8,32,128]{2,1,0:T(8,128)(2,1)S(1)} %get-tuple-element.72), channel_id=1, source_target_pairs={{0,3},{1,2},{2,1},{3,0},{4,7},{5,6},{6,5},{7,4},{8,11},{9,10},{10,... | collective-permute-start | bytes 196616 | tf_op jit(solution)/shard_map/ppermute | solution.py:112
  15.8 3.1 %stage0.3 = (f32[65,32,128]{2,1,0:T(8,128)S(1)}, f32[65,32,128]{2,1,0:T(8,128)S(1)}, f32[8,128]{1,0:T(8,128)}) custom-call(s32[7,208]{1,0:T(8,128)S(4)} %get-tuple-element.71.list_ref, s32[6]{0:T(128)S(4)} %get-tuple-element.69.total_ref, bf16[192,128,128]{2,1,0:T(8,128)(2,1)S(1)} %get-tuple-element.70.values_ref, ...), custom_call_target="tpu_custom_call" | custom-call | flops 75497472 | bytes 2359296 | tf_op jit(solution)/shard_map/stage0/pallas_call | solution.py:473
  18.9 2.8 %stage1.3 = (f32[65,32,128]{2,1,0:T(8,128)S(1)}, f32[65,32,128]{2,1,0:T(8,128)S(1)}) custom-call(s32[7,208]{1,0:T(8,128)S(4)} %get-tuple-element.71.list_ref, s32[6]{0:T(128)S(4)} %get-tuple-element.69.total_ref, bf16[192,128,128]{2,1,0:T(8,128)(2,1)S(1)} %get-tuple-element.70.values_ref, ...), custom_call_target="tpu_custom_call", output_to_operand_aliasing={{0}: (6, {}), {1}: (7, {})} | custom-call | flops 100663296 | bytes 3145728 | tf_op jit(solution)/shard_map/stage1/pallas_call | solution.py:486
  24.5 2.1 %collective-permute-start.8 = (bf16[16,32,128]{2,1,0:T(8,128)(2,1)S(1)}, bf16[16,32,128]{2,1,0:T(8,128)(2,1)S(1)}, u32[]{:S(2)}, u32[]{:S(2)}) collective-permute-start(bf16[16,32,128]{2,1,0:T(8,128)(2,1)S(1)} %get-tuple-element.87.refs_7_.refs_11_), channel_id=1, source_target_pairs={{0,16},{4,20},{8,24},{12,28},{16,0},{20,4},{24,8},{28,12},{1,17},{... | collective-permute-start | bytes 393224 | tf_op jit(solution)/shard_map/ppermute | solution.py:591
  26.5 1.1 %collective-permute-start.9 = (bf16[16,32,128]{2,1,0:T(8,128)(2,1)S(1)}, bf16[16,32,128]{2,1,0:T(8,128)(2,1)S(1)}, u32[]{:S(2)}, u32[]{:S(2)}) collective-permute-start(bf16[16,32,128]{2,1,0:T(8,128)(2,1)S(1)} %get-tuple-element.84.before_ref.refs_8_.refs_12_), channel_id=1, source_target_pairs={{0,8},{4,12},{8,0},{12,4},{16,24},{20,28},{24,16},{28,20},{1,9},{5... | collective-permute-start | bytes 393224 | tf_op jit(solution)/shard_map/ppermute | solution.py:591
  27.7 4.2 %turn.1 = (bf16[192,128,128]{2,1,0:T(8,128)(2,1)S(1)}, f32[16,32,128]{2,1,0:T(8,128)S(1)}) custom-call(s32[6]{0:T(128)S(4)} %get-tuple-element.69.total_ref, bf16[192,128,128]{2,1,0:T(8,128)(2,1)S(1)} %get-tuple-element.70.values_ref, f32[16,32,128]{2,1,0:T(8,128)S(1)} %combine1.3.base_ref), custom_call_target="tpu_custom_call", output_to_operand_aliasing={{1}: (2, {})} | custom-call | flops 20000000000 | tf_op jit(solution)/shard_map/turn/pallas_call | solution.py:453
  31.9 0.9 %collective-permute-done.8.refs_1_ = bf16[16,32,128]{2,1,0:T(8,128)(2,1)S(1)} collective-permute-done((bf16[16,32,128]{2,1,0:T(8,128)(2,1)S(1)}, bf16[16,32,128]{2,1,0:T(8,128)(2,1)S(1)}, u32[]{:S(2)}, u32[]{:S(2)}) %collective-permute-start.8) | collective-permute-done | bytes 131104 | tf_op jit(solution)/shard_map/ppermute | solution.py:591
  35.0 2.3 %collective-permute-start.12 = (bf16[8,32,128]{2,1,0:T(8,128)(2,1)S(1)}, bf16[8,32,128]{2,1,0:T(8,128)(2,1)S(1)}, u32[]{:S(2)}, u32[]{:S(2)}) collective-permute-start(bf16[8,32,128]{2,1,0:T(8,128)(2,1)S(1)} %get-tuple-element.94), channel_id=1, source_target_pairs={{0,2},{1,3},{2,0},{3,1},{4,6},{5,7},{6,4},{7,5},{8,10},{9,11},{10,... | collective-permute-start | bytes 196616 | tf_op jit(solution)/shard_map/ppermute | solution.py:108
  37.3 2.2 %collective-permute-done.13.refs_1_ = bf16[8,32,128]{2,1,0:T(8,128)(2,1)S(1)} collective-permute-done((bf16[8,32,128]{2,1,0:T(8,128)(2,1)S(1)}, bf16[8,32,128]{2,1,0:T(8,128)(2,1)S(1)}, u32[]{:S(2)}, u32[]{:S(2)}) %collective-permute-start.13) | collective-permute-done | bytes 65568 | tf_op jit(solution)/shard_map/ppermute | solution.py:108
  39.5 1.7 %collective-permute-start.10 = (bf16[8,32,128]{2,1,0:T(8,128)(2,1)S(1)}, bf16[8,32,128]{2,1,0:T(8,128)(2,1)S(1)}, u32[]{:S(2)}, u32[]{:S(2)}) collective-permute-start(bf16[8,32,128]{2,1,0:T(8,128)(2,1)S(1)} %get-tuple-element.94), channel_id=1, source_target_pairs={{0,3},{1,2},{2,1},{3,0},{4,7},{5,6},{6,5},{7,4},{8,11},{9,10},{10,... | collective-permute-start | bytes 196616 | tf_op jit(solution)/shard_map/ppermute | solution.py:112
  41.2 2.3 %stage0.4 = (f32[65,32,128]{2,1,0:T(8,128)S(1)}, f32[65,32,128]{2,1,0:T(8,128)S(1)}, f32[8,128]{1,0:T(8,128)}) custom-call(s32[7,208]{1,0:T(8,128)S(4)} %get-tuple-element.71.list_ref, s32[6]{0:T(128)S(4)} %get-tuple-element.69.total_ref, bf16[192,128,128]{2,1,0:T(8,128)(2,1)S(1)} %get-tuple-element.93.values_ref, ...), custom_call_target="tpu_custom_call" | custom-call | flops 75497472 | bytes 2359296 | tf_op jit(solution)/shard_map/stage0/pallas_call | solution.py:473
  44.1 1.8 %stage1.4 = (f32[65,32,128]{2,1,0:T(8,128)S(1)}, f32[65,32,128]{2,1,0:T(8,128)S(1)}) custom-call(s32[7,208]{1,0:T(8,128)S(4)} %get-tuple-element.71.list_ref, s32[6]{0:T(128)S(4)} %get-tuple-element.69.total_ref, bf16[192,128,128]{2,1,0:T(8,128)(2,1)S(1)} %get-tuple-element.93.values_ref, ...), custom_call_target="tpu_custom_call", output_to_operand_aliasing={{0}: (6, {}), {1}: (7, {})} | custom-call | flops 100663296 | bytes 3145728 | tf_op jit(solution)/shard_map/stage1/pallas_call | solution.py:486
  49.0 1.7 %collective-permute-start.18 = (bf16[16,32,128]{2,1,0:T(8,128)(2,1)S(1)}, bf16[16,32,128]{2,1,0:T(8,128)(2,1)S(1)}, u32[]{:S(2)}, u32[]{:S(2)}) collective-permute-start(bf16[16,32,128]{2,1,0:T(8,128)(2,1)S(1)} %get-tuple-element.106.refs_14_), channel_id=1, source_target_pairs={{0,16},{4,20},{8,24},{12,28},{16,0},{20,4},{24,8},{28,12},{1,17},{... | collective-permute-start | bytes 393224 | tf_op jit(solution)/shard_map/ppermute | solution.py:591
  50.7 1.0 %collective-permute-start.19 = (bf16[16,32,128]{2,1,0:T(8,128)(2,1)S(1)}, bf16[16,32,128]{2,1,0:T(8,128)(2,1)S(1)}, u32[]{:S(2)}, u32[]{:S(2)}) collective-permute-start(bf16[16,32,128]{2,1,0:T(8,128)(2,1)S(1)} %get-tuple-element.104.before_ref.refs_15_), channel_id=1, source_target_pairs={{0,8},{4,12},{8,0},{12,4},{16,24},{20,28},{24,16},{28,20},{1,9},{5... | collective-permute-start | bytes 393224 | tf_op jit(solution)/shard_map/ppermute | solution.py:591
  51.8 3.7 %collective-permute-done.17.refs_0_ = bf16[16,32,128]{2,1,0:T(8,128)(2,1)S(1)} collective-permute-done((bf16[16,32,128]{2,1,0:T(8,128)(2,1)S(1)}, bf16[16,32,128]{2,1,0:T(8,128)(2,1)S(1)}, u32[]{:S(2)}, u32[]{:S(2)}) %collective-permute-start.17) | collective-permute-done | bytes 131104 | tf_op jit(solution)/shard_map/ppermute | solution.py:591
  55.5 1.6 %collective-permute-done.18.refs_1_ = bf16[16,32,128]{2,1,0:T(8,128)(2,1)S(1)} collective-permute-done((bf16[16,32,128]{2,1,0:T(8,128)(2,1)S(1)}, bf16[16,32,128]{2,1,0:T(8,128)(2,1)S(1)}, u32[]{:S(2)}, u32[]{:S(2)}) %collective-permute-start.18) | collective-permute-done | bytes 131104 | tf_op jit(solution)/shard_map/ppermute | solution.py:591
  58.6 1.6 %collective-permute-start.21 = (bf16[16,32,128]{2,1,0:T(8,128)(2,1)S(1)}, bf16[16,32,128]{2,1,0:T(8,128)(2,1)S(1)}, u32[]{:S(2)}, u32[]{:S(2)}) collective-permute-start(bf16[16,32,128]{2,1,0:T(8,128)(2,1)S(1)} %get-tuple-element.112.refs_0_), channel_id=1, source_target_pairs={{0,1},{1,0},{2,3},{3,2},{4,5},{5,4},{6,7},{7,6},{8,9},{9,8},{10,11... | collective-permute-start | bytes 393224 | tf_op jit(solution)/shard_map/ppermute | solution.py:109
  60.2 1.5 %collective-permute-start.22 = (bf16[8,32,128]{2,1,0:T(8,128)(2,1)S(1)}, bf16[8,32,128]{2,1,0:T(8,128)(2,1)S(1)}, u32[]{:S(2)}, u32[]{:S(2)}) collective-permute-start(bf16[8,32,128]{2,1,0:T(8,128)(2,1)S(1)} %get-tuple-element.111), channel_id=1, source_target_pairs={{0,2},{1,3},{2,0},{3,1},{4,6},{5,7},{6,4},{7,5},{8,10},{9,11},{10,... | collective-permute-start | bytes 196616 | tf_op jit(solution)/shard_map/ppermute | solution.py:108
  61.7 2.3 %collective-permute-done.23.refs_1_ = bf16[8,32,128]{2,1,0:T(8,128)(2,1)S(1)} collective-permute-done((bf16[8,32,128]{2,1,0:T(8,128)(2,1)S(1)}, bf16[8,32,128]{2,1,0:T(8,128)(2,1)S(1)}, u32[]{:S(2)}, u32[]{:S(2)}) %collective-permute-start.23) | collective-permute-done | bytes 65568 | tf_op jit(solution)/shard_map/ppermute | solution.py:108
  64.2 1.3 %collective-permute-start.20 = (bf16[8,32,128]{2,1,0:T(8,128)(2,1)S(1)}, bf16[8,32,128]{2,1,0:T(8,128)(2,1)S(1)}, u32[]{:S(2)}, u32[]{:S(2)}) collective-permute-start(bf16[8,32,128]{2,1,0:T(8,128)(2,1)S(1)} %get-tuple-element.111), channel_id=1, source_target_pairs={{0,3},{1,2},{2,1},{3,0},{4,7},{5,6},{6,5},{7,4},{8,11},{9,10},{10,... | collective-permute-start | bytes 196616 | tf_op jit(solution)/shard_map/ppermute | solution.py:112
  65.5 2.5 %stage0.5 = (f32[65,32,128]{2,1,0:T(8,128)S(1)}, f32[65,32,128]{2,1,0:T(8,128)S(1)}, f32[8,128]{1,0:T(8,128)}) custom-call(s32[7,208]{1,0:T(8,128)S(4)} %get-tuple-element.71.list_ref, s32[6]{0:T(128)S(4)} %get-tuple-element.69.total_ref, bf16[192,128,128]{2,1,0:T(8,128)(2,1)S(1)} %get-tuple-element.93.values_ref, ...), custom_call_target="tpu_custom_call" | custom-call | flops 75497472 | bytes 2359296 | tf_op jit(solution)/shard_map/stage0/pallas_call | solution.py:473
  68.8 1.8 %stage1.5 = (f32[65,32,128]{2,1,0:T(8,128)S(1)}, f32[65,32,128]{2,1,0:T(8,128)S(1)}) custom-call(s32[7,208]{1,0:T(8,128)S(4)} %get-tuple-element.71.list_ref, s32[6]{0:T(128)S(4)} %get-tuple-element.69.total_ref, bf16[192,128,128]{2,1,0:T(8,128)(2,1)S(1)} %get-tuple-element.93.values_ref, ...), custom_call_target="tpu_custom_call", output_to_operand_aliasing={{0}: (6, {}), {1}: (7, {})} | custom-call | flops 100663296 | bytes 3145728 | tf_op jit(solution)/shard_map/stage1/pallas_call | solution.py:486
  72.9 1.1 %collective-permute-start.27 = (bf16[16,32,128]{2,1,0:T(8,128)(2,1)S(1)}, bf16[16,32,128]{2,1,0:T(8,128)(2,1)S(1)}, u32[]{:S(2)}, u32[]{:S(2)}) collective-permute-start(bf16[16,32,128]{2,1,0:T(8,128)(2,1)S(1)} %get-tuple-element.123), channel_id=1, source_target_pairs={{0,24},{4,28},{8,16},{12,20},{16,8},{20,12},{24,0},{28,4},{1,25},{... | collective-permute-start | bytes 393224 | tf_op jit(solution)/shard_map/ppermute | solution.py:591
  74.0 0.9 %collective-permute-start.28 = (bf16[16,32,128]{2,1,0:T(8,128)(2,1)S(1)}, bf16[16,32,128]{2,1,0:T(8,128)(2,1)S(1)}, u32[]{:S(2)}, u32[]{:S(2)}) collective-permute-start(bf16[16,32,128]{2,1,0:T(8,128)(2,1)S(1)} %get-tuple-element.124), channel_id=1, source_target_pairs={{0,16},{4,20},{8,24},{12,28},{16,0},{20,4},{24,8},{28,12},{1,17},{... | collective-permute-start | bytes 393224 | tf_op jit(solution)/shard_map/ppermute | solution.py:591
  74.9 1.6 %collective-permute-start.29 = (bf16[16,32,128]{2,1,0:T(8,128)(2,1)S(1)}, bf16[16,32,128]{2,1,0:T(8,128)(2,1)S(1)}, u32[]{:S(2)}, u32[]{:S(2)}) collective-permute-start(bf16[16,32,128]{2,1,0:T(8,128)(2,1)S(1)} %get-tuple-element.122.before_ref), channel_id=1, source_target_pairs={{0,8},{4,12},{8,0},{12,4},{16,24},{20,28},{24,16},{28,20},{1,9},{5... | collective-permute-start | bytes 393224 | tf_op jit(solution)/shard_map/ppermute | solution.py:591
  76.5 3.7 %collective-permute-done.27.refs_0_ = bf16[16,32,128]{2,1,0:T(8,128)(2,1)S(1)} collective-permute-done((bf16[16,32,128]{2,1,0:T(8,128)(2,1)S(1)}, bf16[16,32,128]{2,1,0:T(8,128)(2,1)S(1)}, u32[]{:S(2)}, u32[]{:S(2)}) %collective-permute-start.27) | collective-permute-done | bytes 131104 | tf_op jit(solution)/shard_map/ppermute | solution.py:591
  80.2 1.8 %collective-permute-done.28.refs_1_ = bf16[16,32,128]{2,1,0:T(8,128)(2,1)S(1)} collective-permute-done((bf16[16,32,128]{2,1,0:T(8,128)(2,1)S(1)}, bf16[16,32,128]{2,1,0:T(8,128)(2,1)S(1)}, u32[]{:S(2)}, u32[]{:S(2)}) %collective-permute-start.28) | collective-permute-done | bytes 131104 | tf_op jit(solution)/shard_map/ppermute | solution.py:591
  82.3 1.4 %finish.1 = f32[16,32,128]{2,1,0:T(8,128)} custom-call(bf16[16,128,128]{2,1,0:T(8,128)(2,1)S(1)} %get-tuple-element.65.high_ref, bf16[16,128,128]{2,1,0:T(8,128)(2,1)S(1)} %get-tuple-element.66.low_ref, f32[16,32,128]{2,1,0:T(8,128)S(1)} %get-tuple-element.110.sol_ref, f32[16,32,128]{2,1,0:T(8,128)S(1)} %combine1.5.base_ref, ...), custom_call_target="tpu_custom_call" | custom-call | tf_op jit(solution)/shard_map/finish/pallas_call | solution.py:606
  (55 shorter events, 13.9 us)
Async XLA Ops:
  2.2 10.1 %collective-permute-start.3 = (bf16[8,32,128]{2,1,0:T(8,128)(2,1)S(1)}, bf16[8,32,128]{2,1,0:T(8,128)(2,1)S(1)}, u32[]{:S(2)}, u32[]{:S(2)}) collective-permute-start(bf16[8,32,128]{2,1,0:T(8,128)(2,1)S(1)} %get-tuple-element.74), channel_id=1, source_target_pairs={{0,2},{1,3},{2,0},{3,1},{4,6},{5,7},{6,4},{7,5},{8,10},{9,11},{10,... | collective-permute-start | bytes 196616 | tf_op jit(solution)/shard_map/ppermute | solution.py:108
  6.3 12.7 %collective-permute-start.1 = (bf16[16,32,128]{2,1,0:T(8,128)(2,1)S(1)}, bf16[16,32,128]{2,1,0:T(8,128)(2,1)S(1)}, u32[]{:S(2)}, u32[]{:S(2)}) collective-permute-start(bf16[16,32,128]{2,1,0:T(8,128)(2,1)S(1)} %get-tuple-element.73.refs_0_), channel_id=1, source_target_pairs={{0,1},{1,0},{2,3},{3,2},{4,5},{5,4},{6,7},{7,6},{8,9},{9,8},{10,11... | collective-permute-start | bytes 393224 | tf_op jit(solution)/shard_map/ppermute | solution.py:109
  7.8 11.1 %collective-permute-start.2 = (bf16[8,32,128]{2,1,0:T(8,128)(2,1)S(1)}, bf16[8,32,128]{2,1,0:T(8,128)(2,1)S(1)}, u32[]{:S(2)}, u32[]{:S(2)}) collective-permute-start(bf16[8,32,128]{2,1,0:T(8,128)(2,1)S(1)} %get-tuple-element.72), channel_id=1, source_target_pairs={{0,2},{1,3},{2,0},{3,1},{4,6},{5,7},{6,4},{7,5},{8,10},{9,11},{10,... | collective-permute-start | bytes 196616 | tf_op jit(solution)/shard_map/ppermute | solution.py:108
  12.3 6.6 %collective-permute-start.4 = (bf16[8,32,128]{2,1,0:T(8,128)(2,1)S(1)}, bf16[8,32,128]{2,1,0:T(8,128)(2,1)S(1)}, u32[]{:S(2)}, u32[]{:S(2)}) collective-permute-start(bf16[8,32,128]{2,1,0:T(8,128)(2,1)S(1)} %hold.1.refs_1_), channel_id=1, source_target_pairs={{0,1},{1,0},{2,3},{3,2},{4,5},{5,4},{6,7},{7,6},{8,9},{9,8},{10,11... | collective-permute-start | bytes 196616 | tf_op jit(solution)/shard_map/ppermute | solution.py:571
  12.4 9.3 %collective-permute-start = (bf16[8,32,128]{2,1,0:T(8,128)(2,1)S(1)}, bf16[8,32,128]{2,1,0:T(8,128)(2,1)S(1)}, u32[]{:S(2)}, u32[]{:S(2)}) collective-permute-start(bf16[8,32,128]{2,1,0:T(8,128)(2,1)S(1)} %get-tuple-element.72), channel_id=1, source_target_pairs={{0,3},{1,2},{2,1},{3,0},{4,7},{5,6},{6,5},{7,4},{8,11},{9,10},{10,... | collective-permute-start | bytes 196616 | tf_op jit(solution)/shard_map/ppermute | solution.py:112
  22.2 1.8 %collective-permute-start.6 = (bf16[48,32,128]{2,1,0:T(8,128)(2,1)S(1)}, bf16[48,32,128]{2,1,0:T(8,128)(2,1)S(1)}, u32[]{:S(2)}, u32[]{:S(2)}) collective-permute-start(bf16[48,32,128]{2,1,0:T(8,128)(2,1)S(1)} %get-tuple-element.83.refs_2_), channel_id=1, source_target_pairs={{0,4},{4,0},{8,12},{12,8},{16,20},{20,16},{24,28},{28,24},{1,5},{5... | collective-permute-start | bytes 1179656 | tf_op jit(solution)/shard_map/ppermute | solution.py:583
  22.7 4.9 %collective-permute-start.5 = (bf16[16,32,128]{2,1,0:T(8,128)(2,1)S(1)}, bf16[16,32,128]{2,1,0:T(8,128)(2,1)S(1)}, u32[]{:S(2)}, u32[]{:S(2)}) collective-permute-start(bf16[16,32,128]{2,1,0:T(8,128)(2,1)S(1)} %get-tuple-element.82.refs_3_), channel_id=1, source_target_pairs={{0,4},{4,0},{8,12},{12,8},{16,20},{20,16},{24,28},{28,24},{1,5},{5... | collective-permute-start | bytes 393224 | tf_op jit(solution)/shard_map/ppermute | solution.py:583
  24.1 7.9 %collective-permute-start.7 = (bf16[16,32,128]{2,1,0:T(8,128)(2,1)S(1)}, bf16[16,32,128]{2,1,0:T(8,128)(2,1)S(1)}, u32[]{:S(2)}, u32[]{:S(2)}) collective-permute-start(bf16[16,32,128]{2,1,0:T(8,128)(2,1)S(1)} %get-tuple-element.86.refs_6_.refs_10_), channel_id=1, source_target_pairs={{0,24},{4,28},{8,16},{12,20},{16,8},{20,12},{24,0},{28,4},{1,25},{... | collective-permute-start | bytes 393224 | tf_op jit(solution)/shard_map/ppermute | solution.py:591
  24.5 8.4 %collective-permute-start.8 = (bf16[16,32,128]{2,1,0:T(8,128)(2,1)S(1)}, bf16[16,32,128]{2,1,0:T(8,128)(2,1)S(1)}, u32[]{:S(2)}, u32[]{:S(2)}) collective-permute-start(bf16[16,32,128]{2,1,0:T(8,128)(2,1)S(1)} %get-tuple-element.87.refs_7_.refs_11_), channel_id=1, source_target_pairs={{0,16},{4,20},{8,24},{12,28},{16,0},{20,4},{24,8},{28,12},{1,17},{... | collective-permute-start | bytes 393224 | tf_op jit(solution)/shard_map/ppermute | solution.py:591
  26.5 7.0 %collective-permute-start.9 = (bf16[16,32,128]{2,1,0:T(8,128)(2,1)S(1)}, bf16[16,32,128]{2,1,0:T(8,128)(2,1)S(1)}, u32[]{:S(2)}, u32[]{:S(2)}) collective-permute-start(bf16[16,32,128]{2,1,0:T(8,128)(2,1)S(1)} %get-tuple-element.84.before_ref.refs_8_.refs_12_), channel_id=1, source_target_pairs={{0,8},{4,12},{8,0},{12,4},{16,24},{20,28},{24,16},{28,20},{1,9},{5... | collective-permute-start | bytes 393224 | tf_op jit(solution)/shard_map/ppermute | solution.py:591
  33.9 5.6 %collective-permute-start.13 = (bf16[8,32,128]{2,1,0:T(8,128)(2,1)S(1)}, bf16[8,32,128]{2,1,0:T(8,128)(2,1)S(1)}, u32[]{:S(2)}, u32[]{:S(2)}) collective-permute-start(bf16[8,32,128]{2,1,0:T(8,128)(2,1)S(1)} %get-tuple-element.90.refs_3_), channel_id=1, source_target_pairs={{0,2},{1,3},{2,0},{3,1},{4,6},{5,7},{6,4},{7,5},{8,10},{9,11},{10,... | collective-permute-start | bytes 196616 | tf_op jit(solution)/shard_map/ppermute | solution.py:108
  34.3 9.8 %collective-permute-start.11 = (bf16[16,32,128]{2,1,0:T(8,128)(2,1)S(1)}, bf16[16,32,128]{2,1,0:T(8,128)(2,1)S(1)}, u32[]{:S(2)}, u32[]{:S(2)}) collective-permute-start(bf16[16,32,128]{2,1,0:T(8,128)(2,1)S(1)} %get-tuple-element.95.refs_0_), channel_id=1, source_target_pairs={{0,1},{1,0},{2,3},{3,2},{4,5},{5,4},{6,7},{7,6},{8,9},{9,8},{10,11... | collective-permute-start | bytes 393224 | tf_op jit(solution)/shard_map/ppermute | solution.py:109
  35.0 8.6 %collective-permute-start.12 = (bf16[8,32,128]{2,1,0:T(8,128)(2,1)S(1)}, bf16[8,32,128]{2,1,0:T(8,128)(2,1)S(1)}, u32[]{:S(2)}, u32[]{:S(2)}) collective-permute-start(bf16[8,32,128]{2,1,0:T(8,128)(2,1)S(1)} %get-tuple-element.94), channel_id=1, source_target_pairs={{0,2},{1,3},{2,0},{3,1},{4,6},{5,7},{6,4},{7,5},{8,10},{9,11},{10,... | collective-permute-start | bytes 196616 | tf_op jit(solution)/shard_map/ppermute | solution.py:108
  39.5 4.6 %collective-permute-start.14 = (bf16[8,32,128]{2,1,0:T(8,128)(2,1)S(1)}, bf16[8,32,128]{2,1,0:T(8,128)(2,1)S(1)}, u32[]{:S(2)}, u32[]{:S(2)}) collective-permute-start(bf16[8,32,128]{2,1,0:T(8,128)(2,1)S(1)} %collective-permute-done.13.refs_1_), channel_id=1, source_target_pairs={{0,1},{1,0},{2,3},{3,2},{4,5},{5,4},{6,7},{7,6},{8,9},{9,8},{10,11... | collective-permute-start | bytes 196616 | tf_op jit(solution)/shard_map/ppermute | solution.py:571
  39.5 6.5 %collective-permute-start.10 = (bf16[8,32,128]{2,1,0:T(8,128)(2,1)S(1)}, bf16[8,32,128]{2,1,0:T(8,128)(2,1)S(1)}, u32[]{:S(2)}, u32[]{:S(2)}) collective-permute-start(bf16[8,32,128]{2,1,0:T(8,128)(2,1)S(1)} %get-tuple-element.94), channel_id=1, source_target_pairs={{0,3},{1,2},{2,1},{3,0},{4,7},{5,6},{6,5},{7,4},{8,11},{9,10},{10,... | collective-permute-start | bytes 196616 | tf_op jit(solution)/shard_map/ppermute | solution.py:112
  46.3 1.8 %collective-permute-start.16 = (bf16[48,32,128]{2,1,0:T(8,128)(2,1)S(1)}, bf16[48,32,128]{2,1,0:T(8,128)(2,1)S(1)}, u32[]{:S(2)}, u32[]{:S(2)}) collective-permute-start(bf16[48,32,128]{2,1,0:T(8,128)(2,1)S(1)} %get-tuple-element.103.refs_4_), channel_id=1, source_target_pairs={{0,4},{4,0},{8,12},{12,8},{16,20},{20,16},{24,28},{28,24},{1,5},{5... | collective-permute-start | bytes 1179656 | tf_op jit(solution)/shard_map/ppermute | solution.py:583
  46.7 5.0 %collective-permute-start.15 = (bf16[16,32,128]{2,1,0:T(8,128)(2,1)S(1)}, bf16[16,32,128]{2,1,0:T(8,128)(2,1)S(1)}, u32[]{:S(2)}, u32[]{:S(2)}) collective-permute-start(bf16[16,32,128]{2,1,0:T(8,128)(2,1)S(1)} %get-tuple-element.102.refs_5_), channel_id=1, source_target_pairs={{0,4},{4,0},{8,12},{12,8},{16,20},{20,16},{24,28},{28,24},{1,5},{5... | collective-permute-start | bytes 393224 | tf_op jit(solution)/shard_map/ppermute | solution.py:583
  48.1 7.3 %collective-permute-start.17 = (bf16[16,32,128]{2,1,0:T(8,128)(2,1)S(1)}, bf16[16,32,128]{2,1,0:T(8,128)(2,1)S(1)}, u32[]{:S(2)}, u32[]{:S(2)}) collective-permute-start(bf16[16,32,128]{2,1,0:T(8,128)(2,1)S(1)} %get-tuple-element.105.refs_13_), channel_id=1, source_target_pairs={{0,24},{4,28},{8,16},{12,20},{16,8},{20,12},{24,0},{28,4},{1,25},{... | collective-permute-start | bytes 393224 | tf_op jit(solution)/shard_map/ppermute | solution.py:591
  49.0 8.1 %collective-permute-start.18 = (bf16[16,32,128]{2,1,0:T(8,128)(2,1)S(1)}, bf16[16,32,128]{2,1,0:T(8,128)(2,1)S(1)}, u32[]{:S(2)}, u32[]{:S(2)}) collective-permute-start(bf16[16,32,128]{2,1,0:T(8,128)(2,1)S(1)} %get-tuple-element.106.refs_14_), channel_id=1, source_target_pairs={{0,16},{4,20},{8,24},{12,28},{16,0},{20,4},{24,8},{28,12},{1,17},{... | collective-permute-start | bytes 393224 | tf_op jit(solution)/shard_map/ppermute | solution.py:591
  50.7 6.7 %collective-permute-start.19 = (bf16[16,32,128]{2,1,0:T(8,128)(2,1)S(1)}, bf16[16,32,128]{2,1,0:T(8,128)(2,1)S(1)}, u32[]{:S(2)}, u32[]{:S(2)}) collective-permute-start(bf16[16,32,128]{2,1,0:T(8,128)(2,1)S(1)} %get-tuple-element.104.before_ref.refs_15_), channel_id=1, source_target_pairs={{0,8},{4,12},{8,0},{12,4},{16,24},{20,28},{24,16},{28,20},{1,9},{5... | collective-permute-start | bytes 393224 | tf_op jit(solution)/shard_map/ppermute | solution.py:591
  57.9 6.2 %collective-permute-start.23 = (bf16[8,32,128]{2,1,0:T(8,128)(2,1)S(1)}, bf16[8,32,128]{2,1,0:T(8,128)(2,1)S(1)}, u32[]{:S(2)}, u32[]{:S(2)}) collective-permute-start(bf16[8,32,128]{2,1,0:T(8,128)(2,1)S(1)} %get-tuple-element.109.refs_3_), channel_id=1, source_target_pairs={{0,2},{1,3},{2,0},{3,1},{4,6},{5,7},{6,4},{7,5},{8,10},{9,11},{10,... | collective-permute-start | bytes 196616 | tf_op jit(solution)/shard_map/ppermute | solution.py:108
  58.6 9.4 %collective-permute-start.21 = (bf16[16,32,128]{2,1,0:T(8,128)(2,1)S(1)}, bf16[16,32,128]{2,1,0:T(8,128)(2,1)S(1)}, u32[]{:S(2)}, u32[]{:S(2)}) collective-permute-start(bf16[16,32,128]{2,1,0:T(8,128)(2,1)S(1)} %get-tuple-element.112.refs_0_), channel_id=1, source_target_pairs={{0,1},{1,0},{2,3},{3,2},{4,5},{5,4},{6,7},{7,6},{8,9},{9,8},{10,11... | collective-permute-start | bytes 393224 | tf_op jit(solution)/shard_map/ppermute | solution.py:109
  60.2 7.8 %collective-permute-start.22 = (bf16[8,32,128]{2,1,0:T(8,128)(2,1)S(1)}, bf16[8,32,128]{2,1,0:T(8,128)(2,1)S(1)}, u32[]{:S(2)}, u32[]{:S(2)}) collective-permute-start(bf16[8,32,128]{2,1,0:T(8,128)(2,1)S(1)} %get-tuple-element.111), channel_id=1, source_target_pairs={{0,2},{1,3},{2,0},{3,1},{4,6},{5,7},{6,4},{7,5},{8,10},{9,11},{10,... | collective-permute-start | bytes 196616 | tf_op jit(solution)/shard_map/ppermute | solution.py:108
  64.1 4.8 %collective-permute-start.24 = (bf16[8,32,128]{2,1,0:T(8,128)(2,1)S(1)}, bf16[8,32,128]{2,1,0:T(8,128)(2,1)S(1)}, u32[]{:S(2)}, u32[]{:S(2)}) collective-permute-start(bf16[8,32,128]{2,1,0:T(8,128)(2,1)S(1)} %collective-permute-done.23.refs_1_), channel_id=1, source_target_pairs={{0,1},{1,0},{2,3},{3,2},{4,5},{5,4},{6,7},{7,6},{8,9},{9,8},{10,11... | collective-permute-start | bytes 196616 | tf_op jit(solution)/shard_map/ppermute | solution.py:571
  64.2 6.5 %collective-permute-start.20 = (bf16[8,32,128]{2,1,0:T(8,128)(2,1)S(1)}, bf16[8,32,128]{2,1,0:T(8,128)(2,1)S(1)}, u32[]{:S(2)}, u32[]{:S(2)}) collective-permute-start(bf16[8,32,128]{2,1,0:T(8,128)(2,1)S(1)} %get-tuple-element.111), channel_id=1, source_target_pairs={{0,3},{1,2},{2,1},{3,0},{4,7},{5,6},{6,5},{7,4},{8,11},{9,10},{10,... | collective-permute-start | bytes 196616 | tf_op jit(solution)/shard_map/ppermute | solution.py:112
  71.0 1.8 %collective-permute-start.26 = (bf16[48,32,128]{2,1,0:T(8,128)(2,1)S(1)}, bf16[48,32,128]{2,1,0:T(8,128)(2,1)S(1)}, u32[]{:S(2)}, u32[]{:S(2)}) collective-permute-start(bf16[48,32,128]{2,1,0:T(8,128)(2,1)S(1)} %get-tuple-element.121), channel_id=1, source_target_pairs={{0,4},{4,0},{8,12},{12,8},{16,20},{20,16},{24,28},{28,24},{1,5},{5... | collective-permute-start | bytes 1179656 | tf_op jit(solution)/shard_map/ppermute | solution.py:583
  71.4 5.0 %collective-permute-start.25 = (bf16[16,32,128]{2,1,0:T(8,128)(2,1)S(1)}, bf16[16,32,128]{2,1,0:T(8,128)(2,1)S(1)}, u32[]{:S(2)}, u32[]{:S(2)}) collective-permute-start(bf16[16,32,128]{2,1,0:T(8,128)(2,1)S(1)} %get-tuple-element.119), channel_id=1, source_target_pairs={{0,4},{4,0},{8,12},{12,8},{16,20},{20,16},{24,28},{28,24},{1,5},{5... | collective-permute-start | bytes 393224 | tf_op jit(solution)/shard_map/ppermute | solution.py:583
  72.9 7.3 %collective-permute-start.27 = (bf16[16,32,128]{2,1,0:T(8,128)(2,1)S(1)}, bf16[16,32,128]{2,1,0:T(8,128)(2,1)S(1)}, u32[]{:S(2)}, u32[]{:S(2)}) collective-permute-start(bf16[16,32,128]{2,1,0:T(8,128)(2,1)S(1)} %get-tuple-element.123), channel_id=1, source_target_pairs={{0,24},{4,28},{8,16},{12,20},{16,8},{20,12},{24,0},{28,4},{1,25},{... | collective-permute-start | bytes 393224 | tf_op jit(solution)/shard_map/ppermute | solution.py:591
  74.0 8.1 %collective-permute-start.28 = (bf16[16,32,128]{2,1,0:T(8,128)(2,1)S(1)}, bf16[16,32,128]{2,1,0:T(8,128)(2,1)S(1)}, u32[]{:S(2)}, u32[]{:S(2)}) collective-permute-start(bf16[16,32,128]{2,1,0:T(8,128)(2,1)S(1)} %get-tuple-element.124), channel_id=1, source_target_pairs={{0,16},{4,20},{8,24},{12,28},{16,0},{20,4},{24,8},{28,12},{1,17},{... | collective-permute-start | bytes 393224 | tf_op jit(solution)/shard_map/ppermute | solution.py:591
  74.9 7.4 %collective-permute-start.29 = (bf16[16,32,128]{2,1,0:T(8,128)(2,1)S(1)}, bf16[16,32,128]{2,1,0:T(8,128)(2,1)S(1)}, u32[]{:S(2)}, u32[]{:S(2)}) collective-permute-start(bf16[16,32,128]{2,1,0:T(8,128)(2,1)S(1)} %get-tuple-element.122.before_ref), channel_id=1, source_target_pairs={{0,8},{4,12},{8,0},{12,4},{16,24},{20,28},{24,16},{28,20},{1,9},{5... | collective-permute-start | bytes 393224 | tf_op jit(solution)/shard_map/ppermute | solution.py:591

commit v14 on v13

--- a/solution.py
+++ b/solution.py
@@ -85,7 +85,8 @@
     early = range(parts - 1)
     far, forwarded = range(1, pairs), range(pairs + 1, groups)
     stages = [
-        own + [(index, part) for part in early for index in far],
+        own,
+        [(index, part) for part in early for index in far],
         [(pairs, part) for part in every] + [(index, parts - 1) for index in far]
         + [(index, part) for part in early for index in forwarded],
         [(index, parts - 1) for index in forwarded],
@@ -564,17 +565,12 @@
         def stage_pieces(stage):
             return [sets[piece] for piece in stages[stage] if piece in sets]
 
-        def forward(part, token=None):
-            for index in range(1, groups // 2):
-                if token is not None:
-                    sets[index, part] = hold(sets[index, part], token)
-                sets[groups // 2 + index, part] = lax.ppermute(sets[index, part], "col", neighbours(groups))
-
+        *totals, token = product_first(*blocks, stage_pieces(0), outs, ins, sent)
         if groups % 2 == 0:
             for part in range(parts - 1):
-                forward(part, order_token if step == 0 else None)
-        *totals, _ = product_first(*blocks, stage_pieces(0), outs, ins, sent)
-
+                for index in range(1, groups // 2):
+                    sets[index, part] = hold(sets[index, part], token)
+                    sets[groups // 2 + index, part] = lax.ppermute(sets[index, part], "col", neighbours(groups))
         for stage in range(1, final):
             totals = product_stage(*blocks, stage, stage_pieces(stage), totals)
         other, out_first = product_last(*blocks, 0, stage_pieces(final), totals[0])

time: 83.4 us -> 85.6 us (1.026)
  starting transfers between devices: 31.7 us -> 34 us
    pallas_call x3 -> x6, Pallas kernels: 6.44 us -> 10.1 us  [product_stage(): pl.pallas_call(functools.partial(stage_kernel, stage, bits, dims, len(pie...]
    pallas_call x3, Pallas kernels: 7.98 us -> 4.35 us  [product_first(): pl.pallas_call(functools.partial(first_kernel, len(pieces), len(outs) //...]
    ppermute x3, starting transfers between devices: 6.45 us -> 9.13 us  [gather(): lax.ppermute(rounded[-1], 'col', across)]
    ppermute x6, starting transfers between devices: 8.64 us -> 6.39 us  [gather(): sets[step, part] = lax.ppermute(piece, 'col', ring(groups, 2 * step))]
    ppermute x3, starting transfers between devices: 3.84 us -> 5.75 us  [gather(): sets[groups // 2, 0] = lax.ppermute(whole, 'col', neighbours(groups))]
    ppermute x6, waiting for transfers between devices: 4.51 us -> 2.87 us  [gather(): sets[step, part] = lax.ppermute(piece, 'col', ring(groups, 2 * step))]
    ppermute x3, waiting for transfers between devices: 1.35 us -> 2.89 us  [per_device(): lax.ppermute(sets[index, part], 'col', neighbours(groups))]
  transfers between devices with their start and end apart: 30 -> 30, of which waited for: 15 -> 12; matrix products, arithmetic and copies ran while one was open for 0% -> 0% of each run, Pallas kernels for 29% -> 29%
where the time goes in v14:
time: 85.6 us; the launch traced here: 86 us
  starting transfers between devices  34 us (40%)
  Pallas kernels  30.4 us (36%)
  waiting for transfers between devices  20.8 us (24%)
  between operations  0.91 us (1%)
    ppermute x9, waiting for transfers between devices, per_device(): lax.ppermute(send, 'row', [(chip * CORES + core, partner(chip, shift, chi...  12.5 us
    ppermute x9, starting transfers between devices, per_device(): lax.ppermute(send, 'row', [(chip * CORES + core, partner(chip, shift, chi...  10.7 us
    pallas_call x6, Pallas kernels, product_stage(): pl.pallas_call(functools.partial(stage_kernel, stage, bits, dims, len(pie...  10.1 us
    ppermute x3, starting transfers between devices, gather(): lax.ppermute(rounded[-1], 'col', across)  9.13 us
    ppermute x6, starting transfers between devices, gather(): sets[step, part] = lax.ppermute(piece, 'col', ring(groups, 2 * step))  6.39 us
    ppermute x3, starting transfers between devices, gather(): sets[groups // 2, 0] = lax.ppermute(whole, 'col', neighbours(groups))  5.75 us
    pallas_call x3, Pallas kernels, product_first(): pl.pallas_call(functools.partial(first_kernel, len(pieces), len(outs) //...  4.35 us
    pallas_call x1, Pallas kernels, turn(): pl.pallas_call(turn_kernel, out_shape=[pltpu.VMEM(values.shape, values.dt...  4.14 us
  transfers between devices with their start and end apart: 30, of which 12 were waited for; matrix products, arithmetic and copies ran while one was open for 0% of the time, Pallas kernels for 29%

profile of v14, /device:TPU:0, one launch (start us, length us, event | category | flops | bytes accessed | tf_op | source)
XLA Modules:
  0.0 86.0 jit_solution(2842813328756982565)
XLA Ops:
  0.0 2.2 %start.1 = (bf16[16,128,128]{2,1,0:T(8,128)(2,1)S(1)}, bf16[16,128,128]{2,1,0:T(8,128)(2,1)S(1)}, f32[16,32,128]{2,1,0:T(8,128)S(1)}, f32[16,32,128]{2,1,0:T(8,1...) custom-call(f32[16,128,128]{2,1,0:T(8,128)} %bitcast.5, ...), custom_call_target="tpu_custom_call" | custom-call | tf_op jit(solution)/shard_map/start/pallas_call | solution.py:419
  2.2 4.1 %collective-permute-start.3 = (bf16[8,32,128]{2,1,0:T(8,128)(2,1)S(1)}, bf16[8,32,128]{2,1,0:T(8,128)(2,1)S(1)}, u32[]{:S(2)}, u32[]{:S(2)}) collective-permute-start(bf16[8,32,128]{2,1,0:T(8,128)(2,1)S(1)} %get-tuple-element.82), channel_id=1, source_target_pairs={{0,2},{1,3},{2,0},{3,1},{4,6},{5,7},{6,4},{7,5},{8,10},{9,11},{10,... | collective-permute-start | bytes 196616 | tf_op jit(solution)/shard_map/ppermute | solution.py:109
  6.3 1.6 %collective-permute-start.1 = (bf16[16,32,128]{2,1,0:T(8,128)(2,1)S(1)}, bf16[16,32,128]{2,1,0:T(8,128)(2,1)S(1)}, u32[]{:S(2)}, u32[]{:S(2)}) collective-permute-start(bf16[16,32,128]{2,1,0:T(8,128)(2,1)S(1)} %get-tuple-element.81.refs_0_), channel_id=1, source_target_pairs={{0,1},{1,0},{2,3},{3,2},{4,5},{5,4},{6,7},{7,6},{8,9},{9,8},{10,11... | collective-permute-start | bytes 393224 | tf_op jit(solution)/shard_map/ppermute | solution.py:110
  8.8 4.1 %order.1 = (s32[9,208]{1,0:T(8,128)S(4)}, s32[8]{0:T(128)S(4)}, bf16[192,128,128]{2,1,0:T(8,128)(2,1)S(1)}, f32[8,128]{1,0:T(8,128)}) custom-call(s32[1,1]{1,0:T(1,128)S(6)} %copy.67.count_ref, s32[1,1,192]{2,1,0:T(1,128)} %rows_hbm.1, s32[1,1,192]{2,1,0:T(1,128)} %cols_hbm.1, bf16[192,128,128]{2,1,0:T(8,128)(2,1)} %bitcast.4), custom_call_target="tpu_custom_call" | custom-call | tf_op jit(solution)/shard_map/order/pallas_call | solution.py:432
  12.9 1.7 %stage0.3 = (f32[65,32,128]{2,1,0:T(8,128)S(1)}, f32[65,32,128]{2,1,0:T(8,128)S(1)}, f32[8,128]{1,0:T(8,128)S(1)}) custom-call(s32[9,208]{1,0:T(8,128)S(4)} %get-tuple-element.79.list_ref, s32[8]{0:T(128)S(4)} %get-tuple-element.77.total_ref, bf16[192,128,128]{2,1,0:T(8,128)(2,1)S(1)} %get-tuple-element.78.values_ref, ...), custom_call_target="tpu_custom_call" | custom-call | flops 50331648 | bytes 1572864 | tf_op jit(solution)/shard_map/stage0/pallas_call | solution.py:474
  14.7 3.8 %collective-permute-start = (bf16[8,32,128]{2,1,0:T(8,128)(2,1)S(1)}, bf16[8,32,128]{2,1,0:T(8,128)(2,1)S(1)}, u32[]{:S(2)}, u32[]{:S(2)}) collective-permute-start(bf16[8,32,128]{2,1,0:T(8,128)(2,1)S(1)} %get-tuple-element.80), channel_id=1, source_target_pairs={{0,3},{1,2},{2,1},{3,0},{4,7},{5,6},{6,5},{7,4},{8,11},{9,10},{10,... | collective-permute-start | bytes 196616 | tf_op jit(solution)/shard_map/ppermute | solution.py:113
  18.6 1.2 %stage1.3 = (f32[65,32,128]{2,1,0:T(8,128)S(1)}, f32[65,32,128]{2,1,0:T(8,128)S(1)}) custom-call(s32[9,208]{1,0:T(8,128)S(4)} %get-tuple-element.79.list_ref, s32[8]{0:T(128)S(4)} %get-tuple-element.77.total_ref, bf16[192,128,128]{2,1,0:T(8,128)(2,1)S(1)} %get-tuple-element.78.values_ref, ...), custom_call_target="tpu_custom_call", output_to_operand_aliasing={{0}: (4, {}), {1}: (5, {})} | custom-call | flops 25165824 | bytes 786432 | tf_op jit(solution)/shard_map/stage1/pallas_call | solution.py:487
  19.8 3.2 %stage2.3 = (f32[65,32,128]{2,1,0:T(8,128)S(1)}, f32[65,32,128]{2,1,0:T(8,128)S(1)}) custom-call(s32[9,208]{1,0:T(8,128)S(4)} %get-tuple-element.79.list_ref, s32[8]{0:T(128)S(4)} %get-tuple-element.77.total_ref, bf16[192,128,128]{2,1,0:T(8,128)(2,1)S(1)} %get-tuple-element.78.values_ref, ...), custom_call_target="tpu_custom_call", output_to_operand_aliasing={{0}: (6, {}), {1}: (7, {})} | custom-call | flops 100663296 | bytes 3145728 | tf_op jit(solution)/shard_map/stage2/pallas_call | solution.py:487
  25.3 1.6 %collective-permute-start.7 = (bf16[16,32,128]{2,1,0:T(8,128)(2,1)S(1)}, bf16[16,32,128]{2,1,0:T(8,128)(2,1)S(1)}, u32[]{:S(2)}, u32[]{:S(2)}) collective-permute-start(bf16[16,32,128]{2,1,0:T(8,128)(2,1)S(1)} %get-tuple-element.96.refs_5_.refs_9_), channel_id=1, source_target_pairs={{0,24},{4,28},{8,16},{12,20},{16,8},{20,12},{24,0},{28,4},{1,25},{... | collective-permute-start | bytes 393224 | tf_op jit(solution)/shard_map/ppermute | solution.py:587
  27.1 1.8 %collective-permute-start.9 = (bf16[16,32,128]{2,1,0:T(8,128)(2,1)S(1)}, bf16[16,32,128]{2,1,0:T(8,128)(2,1)S(1)}, u32[]{:S(2)}, u32[]{:S(2)}) collective-permute-start(bf16[16,32,128]{2,1,0:T(8,128)(2,1)S(1)} %get-tuple-element.94.before_ref.refs_7_.refs_11_), channel_id=1, source_target_pairs={{0,8},{4,12},{8,0},{12,4},{16,24},{20,28},{24,16},{28,20},{1,9},{5... | collective-permute-start | bytes 393224 | tf_op jit(solution)/shard_map/ppermute | solution.py:587
  29.0 4.1 %turn.1 = (bf16[192,128,128]{2,1,0:T(8,128)(2,1)S(1)}, f32[16,32,128]{2,1,0:T(8,128)S(1)}) custom-call(s32[8]{0:T(128)S(4)} %get-tuple-element.77.total_ref, bf16[192,128,128]{2,1,0:T(8,128)(2,1)S(1)} %get-tuple-element.78.values_ref, f32[16,32,128]{2,1,0:T(8,128)S(1)} %combine1.3.base_ref), custom_call_target="tpu_custom_call", output_to_operand_aliasing={{1}: (2, {})} | custom-call | flops 20000000000 | tf_op jit(solution)/shard_map/turn/pallas_call | solution.py:454
  33.1 1.5 %collective-permute-done.8.refs_1_ = bf16[16,32,128]{2,1,0:T(8,128)(2,1)S(1)} collective-permute-done((bf16[16,32,128]{2,1,0:T(8,128)(2,1)S(1)}, bf16[16,32,128]{2,1,0:T(8,128)(2,1)S(1)}, u32[]{:S(2)}, u32[]{:S(2)}) %collective-permute-start.8) | collective-permute-done | bytes 131104 | tf_op jit(solution)/shard_map/ppermute | solution.py:587
  36.3 2.2 %collective-permute-start.11 = (bf16[16,32,128]{2,1,0:T(8,128)(2,1)S(1)}, bf16[16,32,128]{2,1,0:T(8,128)(2,1)S(1)}, u32[]{:S(2)}, u32[]{:S(2)}) collective-permute-start(bf16[16,32,128]{2,1,0:T(8,128)(2,1)S(1)} %get-tuple-element.105.refs_0_), channel_id=1, source_target_pairs={{0,1},{1,0},{2,3},{3,2},{4,5},{5,4},{6,7},{7,6},{8,9},{9,8},{10,11... | collective-permute-start | bytes 393224 | tf_op jit(solution)/shard_map/ppermute | solution.py:110
  38.5 1.2 %stage0.4 = (f32[65,32,128]{2,1,0:T(8,128)S(1)}, f32[65,32,128]{2,1,0:T(8,128)S(1)}, f32[8,128]{1,0:T(8,128)S(1)}) custom-call(s32[9,208]{1,0:T(8,128)S(4)} %get-tuple-element.79.list_ref, s32[8]{0:T(128)S(4)} %get-tuple-element.77.total_ref, bf16[192,128,128]{2,1,0:T(8,128)(2,1)S(1)} %get-tuple-element.103.values_ref, ...), custom_call_target="tpu_custom_call" | custom-call | flops 50331648 | bytes 1572864 | tf_op jit(solution)/shard_map/stage0/pallas_call | solution.py:474
  39.7 1.6 %collective-permute-done.13.piece_ref = bf16[8,32,128]{2,1,0:T(8,128)(2,1)S(1)} collective-permute-done((bf16[8,32,128]{2,1,0:T(8,128)(2,1)S(1)}, bf16[8,32,128]{2,1,0:T(8,128)(2,1)S(1)}, u32[]{:S(2)}, u32[]{:S(2)}) %collective-permute-start.13) | collective-permute-done | bytes 65568 | tf_op jit(solution)/shard_map/ppermute | solution.py:109
  41.3 2.9 %collective-permute-start.10 = (bf16[8,32,128]{2,1,0:T(8,128)(2,1)S(1)}, bf16[8,32,128]{2,1,0:T(8,128)(2,1)S(1)}, u32[]{:S(2)}, u32[]{:S(2)}) collective-permute-start(bf16[8,32,128]{2,1,0:T(8,128)(2,1)S(1)} %get-tuple-element.104), channel_id=1, source_target_pairs={{0,3},{1,2},{2,1},{3,0},{4,7},{5,6},{6,5},{7,4},{8,11},{9,10},{10,... | collective-permute-start | bytes 196616 | tf_op jit(solution)/shard_map/ppermute | solution.py:113
  45.0 1.6 %collective-permute-done.14.refs_2_ = bf16[8,32,128]{2,1,0:T(8,128)(2,1)S(1)} collective-permute-done((bf16[8,32,128]{2,1,0:T(8,128)(2,1)S(1)}, bf16[8,32,128]{2,1,0:T(8,128)(2,1)S(1)}, u32[]{:S(2)}, u32[]{:S(2)}) %collective-permute-start.14) | collective-permute-done | bytes 65568 | tf_op jit(solution)/shard_map/ppermute | solution.py:573
  46.5 2.1 %stage2.4 = (f32[65,32,128]{2,1,0:T(8,128)S(1)}, f32[65,32,128]{2,1,0:T(8,128)S(1)}) custom-call(s32[9,208]{1,0:T(8,128)S(4)} %get-tuple-element.79.list_ref, s32[8]{0:T(128)S(4)} %get-tuple-element.77.total_ref, bf16[192,128,128]{2,1,0:T(8,128)(2,1)S(1)} %get-tuple-element.103.values_ref, ...), custom_call_target="tpu_custom_call", output_to_operand_aliasing={{0}: (6, {}), {1}: (7, {})} | custom-call | flops 100663296 | bytes 3145728 | tf_op jit(solution)/shard_map/stage2/pallas_call | solution.py:487
  50.8 1.1 %collective-permute-start.17 = (bf16[16,32,128]{2,1,0:T(8,128)(2,1)S(1)}, bf16[16,32,128]{2,1,0:T(8,128)(2,1)S(1)}, u32[]{:S(2)}, u32[]{:S(2)}) collective-permute-start(bf16[16,32,128]{2,1,0:T(8,128)(2,1)S(1)} %get-tuple-element.118.refs_12_), channel_id=1, source_target_pairs={{0,24},{4,28},{8,16},{12,20},{16,8},{20,12},{24,0},{28,4},{1,25},{... | collective-permute-start | bytes 393224 | tf_op jit(solution)/shard_map/ppermute | solution.py:587
  52.4 2.0 %collective-permute-start.19 = (bf16[16,32,128]{2,1,0:T(8,128)(2,1)S(1)}, bf16[16,32,128]{2,1,0:T(8,128)(2,1)S(1)}, u32[]{:S(2)}, u32[]{:S(2)}) collective-permute-start(bf16[16,32,128]{2,1,0:T(8,128)(2,1)S(1)} %get-tuple-element.117.before_ref.refs_14_), channel_id=1, source_target_pairs={{0,8},{4,12},{8,0},{12,4},{16,24},{20,28},{24,16},{28,20},{1,9},{5... | collective-permute-start | bytes 393224 | tf_op jit(solution)/shard_map/ppermute | solution.py:587
  54.5 3.7 %collective-permute-done.17.refs_0_ = bf16[16,32,128]{2,1,0:T(8,128)(2,1)S(1)} collective-permute-done((bf16[16,32,128]{2,1,0:T(8,128)(2,1)S(1)}, bf16[16,32,128]{2,1,0:T(8,128)(2,1)S(1)}, u32[]{:S(2)}, u32[]{:S(2)}) %collective-permute-start.17) | collective-permute-done | bytes 131104 | tf_op jit(solution)/shard_map/ppermute | solution.py:587
  58.2 1.8 %collective-permute-done.18.refs_1_ = bf16[16,32,128]{2,1,0:T(8,128)(2,1)S(1)} collective-permute-done((bf16[16,32,128]{2,1,0:T(8,128)(2,1)S(1)}, bf16[16,32,128]{2,1,0:T(8,128)(2,1)S(1)}, u32[]{:S(2)}, u32[]{:S(2)}) %collective-permute-start.18) | collective-permute-done | bytes 131104 | tf_op jit(solution)/shard_map/ppermute | solution.py:587
  61.3 2.0 %collective-permute-start.21 = (bf16[16,32,128]{2,1,0:T(8,128)(2,1)S(1)}, bf16[16,32,128]{2,1,0:T(8,128)(2,1)S(1)}, u32[]{:S(2)}, u32[]{:S(2)}) collective-permute-start(bf16[16,32,128]{2,1,0:T(8,128)(2,1)S(1)} %get-tuple-element.125.refs_0_), channel_id=1, source_target_pairs={{0,1},{1,0},{2,3},{3,2},{4,5},{5,4},{6,7},{7,6},{8,9},{9,8},{10,11... | collective-permute-start | bytes 393224 | tf_op jit(solution)/shard_map/ppermute | solution.py:110
  63.9 1.4 %stage0.5 = (f32[65,32,128]{2,1,0:T(8,128)S(1)}, f32[65,32,128]{2,1,0:T(8,128)S(1)}, f32[8,128]{1,0:T(8,128)S(1)}) custom-call(s32[9,208]{1,0:T(8,128)S(4)} %get-tuple-element.79.list_ref, s32[8]{0:T(128)S(4)} %get-tuple-element.77.total_ref, bf16[192,128,128]{2,1,0:T(8,128)(2,1)S(1)} %get-tuple-element.103.values_ref, ...), custom_call_target="tpu_custom_call" | custom-call | flops 50331648 | bytes 1572864 | tf_op jit(solution)/shard_map/stage0/pallas_call | solution.py:474
  65.3 1.3 %collective-permute-done.23.piece_ref = bf16[8,32,128]{2,1,0:T(8,128)(2,1)S(1)} collective-permute-done((bf16[8,32,128]{2,1,0:T(8,128)(2,1)S(1)}, bf16[8,32,128]{2,1,0:T(8,128)(2,1)S(1)}, u32[]{:S(2)}, u32[]{:S(2)}) %collective-permute-start.23) | collective-permute-done | bytes 65568 | tf_op jit(solution)/shard_map/ppermute | solution.py:109
  66.7 2.4 %collective-permute-start.20 = (bf16[8,32,128]{2,1,0:T(8,128)(2,1)S(1)}, bf16[8,32,128]{2,1,0:T(8,128)(2,1)S(1)}, u32[]{:S(2)}, u32[]{:S(2)}) collective-permute-start(bf16[8,32,128]{2,1,0:T(8,128)(2,1)S(1)} %get-tuple-element.124), channel_id=1, source_target_pairs={{0,3},{1,2},{2,1},{3,0},{4,7},{5,6},{6,5},{7,4},{8,11},{9,10},{10,... | collective-permute-start | bytes 196616 | tf_op jit(solution)/shard_map/ppermute | solution.py:113
  69.9 1.3 %collective-permute-done.24.refs_2_ = bf16[8,32,128]{2,1,0:T(8,128)(2,1)S(1)} collective-permute-done((bf16[8,32,128]{2,1,0:T(8,128)(2,1)S(1)}, bf16[8,32,128]{2,1,0:T(8,128)(2,1)S(1)}, u32[]{:S(2)}, u32[]{:S(2)}) %collective-permute-start.24) | collective-permute-done | bytes 65568 | tf_op jit(solution)/shard_map/ppermute | solution.py:573
  71.3 2.1 %stage2.5 = (f32[65,32,128]{2,1,0:T(8,128)S(1)}, f32[65,32,128]{2,1,0:T(8,128)S(1)}) custom-call(s32[9,208]{1,0:T(8,128)S(4)} %get-tuple-element.79.list_ref, s32[8]{0:T(128)S(4)} %get-tuple-element.77.total_ref, bf16[192,128,128]{2,1,0:T(8,128)(2,1)S(1)} %get-tuple-element.103.values_ref, ...), custom_call_target="tpu_custom_call", output_to_operand_aliasing={{0}: (6, {}), {1}: (7, {})} | custom-call | flops 100663296 | bytes 3145728 | tf_op jit(solution)/shard_map/stage2/pallas_call | solution.py:487
  77.1 2.0 %collective-permute-start.29 = (bf16[16,32,128]{2,1,0:T(8,128)(2,1)S(1)}, bf16[16,32,128]{2,1,0:T(8,128)(2,1)S(1)}, u32[]{:S(2)}, u32[]{:S(2)}) collective-permute-start(bf16[16,32,128]{2,1,0:T(8,128)(2,1)S(1)} %get-tuple-element.138.before_ref), channel_id=1, source_target_pairs={{0,8},{4,12},{8,0},{12,4},{16,24},{20,28},{24,16},{28,20},{1,9},{5... | collective-permute-start | bytes 393224 | tf_op jit(solution)/shard_map/ppermute | solution.py:587
  79.2 3.7 %collective-permute-done.27.refs_0_ = bf16[16,32,128]{2,1,0:T(8,128)(2,1)S(1)} collective-permute-done((bf16[16,32,128]{2,1,0:T(8,128)(2,1)S(1)}, bf16[16,32,128]{2,1,0:T(8,128)(2,1)S(1)}, u32[]{:S(2)}, u32[]{:S(2)}) %collective-permute-start.27) | collective-permute-done | bytes 131104 | tf_op jit(solution)/shard_map/ppermute | solution.py:587
  82.9 1.7 %collective-permute-done.28.refs_1_ = bf16[16,32,128]{2,1,0:T(8,128)(2,1)S(1)} collective-permute-done((bf16[16,32,128]{2,1,0:T(8,128)(2,1)S(1)}, bf16[16,32,128]{2,1,0:T(8,128)(2,1)S(1)}, u32[]{:S(2)}, u32[]{:S(2)}) %collective-permute-start.28) | collective-permute-done | bytes 131104 | tf_op jit(solution)/shard_map/ppermute | solution.py:587
  84.6 1.4 %finish.1 = f32[16,32,128]{2,1,0:T(8,128)} custom-call(bf16[16,128,128]{2,1,0:T(8,128)(2,1)S(1)} %get-tuple-element.73.high_ref, bf16[16,128,128]{2,1,0:T(8,128)(2,1)S(1)} %get-tuple-element.74.low_ref, f32[16,32,128]{2,1,0:T(8,128)S(1)} %get-tuple-element.123.sol_ref, f32[16,32,128]{2,1,0:T(8,128)S(1)} %combine1.5.base_ref, ...), custom_call_target="tpu_custom_call" | custom-call | tf_op jit(solution)/shard_map/finish/pallas_call | solution.py:602
  (60 shorter events, 14.7 us)
Async XLA Ops:
  2.2 12.5 %collective-permute-start.3 = (bf16[8,32,128]{2,1,0:T(8,128)(2,1)S(1)}, bf16[8,32,128]{2,1,0:T(8,128)(2,1)S(1)}, u32[]{:S(2)}, u32[]{:S(2)}) collective-permute-start(bf16[8,32,128]{2,1,0:T(8,128)(2,1)S(1)} %get-tuple-element.82), channel_id=1, source_target_pairs={{0,2},{1,3},{2,0},{3,1},{4,6},{5,7},{6,4},{7,5},{8,10},{9,11},{10,... | collective-permute-start | bytes 196616 | tf_op jit(solution)/shard_map/ppermute | solution.py:109
  6.3 13.5 %collective-permute-start.1 = (bf16[16,32,128]{2,1,0:T(8,128)(2,1)S(1)}, bf16[16,32,128]{2,1,0:T(8,128)(2,1)S(1)}, u32[]{:S(2)}, u32[]{:S(2)}) collective-permute-start(bf16[16,32,128]{2,1,0:T(8,128)(2,1)S(1)} %get-tuple-element.81.refs_0_), channel_id=1, source_target_pairs={{0,1},{1,0},{2,3},{3,2},{4,5},{5,4},{6,7},{7,6},{8,9},{9,8},{10,11... | collective-permute-start | bytes 393224 | tf_op jit(solution)/shard_map/ppermute | solution.py:110
  7.8 11.9 %collective-permute-start.2 = (bf16[8,32,128]{2,1,0:T(8,128)(2,1)S(1)}, bf16[8,32,128]{2,1,0:T(8,128)(2,1)S(1)}, u32[]{:S(2)}, u32[]{:S(2)}) collective-permute-start(bf16[8,32,128]{2,1,0:T(8,128)(2,1)S(1)} %get-tuple-element.80), channel_id=1, source_target_pairs={{0,2},{1,3},{2,0},{3,1},{4,6},{5,7},{6,4},{7,5},{8,10},{9,11},{10,... | collective-permute-start | bytes 196616 | tf_op jit(solution)/shard_map/ppermute | solution.py:109
  14.7 5.1 %collective-permute-start.4 = (bf16[8,32,128]{2,1,0:T(8,128)(2,1)S(1)}, bf16[8,32,128]{2,1,0:T(8,128)(2,1)S(1)}, u32[]{:S(2)}, u32[]{:S(2)}) collective-permute-start(bf16[8,32,128]{2,1,0:T(8,128)(2,1)S(1)} %hold.3.refs_0_), channel_id=1, source_target_pairs={{0,1},{1,0},{2,3},{3,2},{4,5},{5,4},{6,7},{7,6},{8,9},{9,8},{10,11... | collective-permute-start | bytes 196616 | tf_op jit(solution)/shard_map/ppermute | solution.py:573
  14.7 8.2 %collective-permute-start = (bf16[8,32,128]{2,1,0:T(8,128)(2,1)S(1)}, bf16[8,32,128]{2,1,0:T(8,128)(2,1)S(1)}, u32[]{:S(2)}, u32[]{:S(2)}) collective-permute-start(bf16[8,32,128]{2,1,0:T(8,128)(2,1)S(1)} %get-tuple-element.80), channel_id=1, source_target_pairs={{0,3},{1,2},{2,1},{3,0},{4,7},{5,6},{6,5},{7,4},{8,11},{9,10},{10,... | collective-permute-start | bytes 196616 | tf_op jit(solution)/shard_map/ppermute | solution.py:113
  23.5 1.8 %collective-permute-start.6 = (bf16[48,32,128]{2,1,0:T(8,128)(2,1)S(1)}, bf16[48,32,128]{2,1,0:T(8,128)(2,1)S(1)}, u32[]{:S(2)}, u32[]{:S(2)}) collective-permute-start(bf16[48,32,128]{2,1,0:T(8,128)(2,1)S(1)} %get-tuple-element.93.refs_1_), channel_id=1, source_target_pairs={{0,4},{4,0},{8,12},{12,8},{16,20},{20,16},{24,28},{28,24},{1,5},{5... | collective-permute-start | bytes 1179656 | tf_op jit(solution)/shard_map/ppermute | solution.py:579
  24.0 4.9 %collective-permute-start.5 = (bf16[16,32,128]{2,1,0:T(8,128)(2,1)S(1)}, bf16[16,32,128]{2,1,0:T(8,128)(2,1)S(1)}, u32[]{:S(2)}, u32[]{:S(2)}) collective-permute-start(bf16[16,32,128]{2,1,0:T(8,128)(2,1)S(1)} %get-tuple-element.92.refs_2_), channel_id=1, source_target_pairs={{0,4},{4,0},{8,12},{12,8},{16,20},{20,16},{24,28},{28,24},{1,5},{5... | collective-permute-start | bytes 393224 | tf_op jit(solution)/shard_map/ppermute | solution.py:579
  25.3 7.8 %collective-permute-start.7 = (bf16[16,32,128]{2,1,0:T(8,128)(2,1)S(1)}, bf16[16,32,128]{2,1,0:T(8,128)(2,1)S(1)}, u32[]{:S(2)}, u32[]{:S(2)}) collective-permute-start(bf16[16,32,128]{2,1,0:T(8,128)(2,1)S(1)} %get-tuple-element.96.refs_5_.refs_9_), channel_id=1, source_target_pairs={{0,24},{4,28},{8,16},{12,20},{16,8},{20,12},{24,0},{28,4},{1,25},{... | collective-permute-start | bytes 393224 | tf_op jit(solution)/shard_map/ppermute | solution.py:587
  26.9 7.8 %collective-permute-start.8 = (bf16[16,32,128]{2,1,0:T(8,128)(2,1)S(1)}, bf16[16,32,128]{2,1,0:T(8,128)(2,1)S(1)}, u32[]{:S(2)}, u32[]{:S(2)}) collective-permute-start(bf16[16,32,128]{2,1,0:T(8,128)(2,1)S(1)} %get-tuple-element.97.refs_6_.refs_10_), channel_id=1, source_target_pairs={{0,16},{4,20},{8,24},{12,28},{16,0},{20,4},{24,8},{28,12},{1,17},{... | collective-permute-start | bytes 393224 | tf_op jit(solution)/shard_map/ppermute | solution.py:587
  27.1 7.6 %collective-permute-start.9 = (bf16[16,32,128]{2,1,0:T(8,128)(2,1)S(1)}, bf16[16,32,128]{2,1,0:T(8,128)(2,1)S(1)}, u32[]{:S(2)}, u32[]{:S(2)}) collective-permute-start(bf16[16,32,128]{2,1,0:T(8,128)(2,1)S(1)} %get-tuple-element.94.before_ref.refs_7_.refs_11_), channel_id=1, source_target_pairs={{0,8},{4,12},{8,0},{12,4},{16,24},{20,28},{24,16},{28,20},{1,9},{5... | collective-permute-start | bytes 393224 | tf_op jit(solution)/shard_map/ppermute | solution.py:587
  35.1 6.2 %collective-permute-start.13 = (bf16[8,32,128]{2,1,0:T(8,128)(2,1)S(1)}, bf16[8,32,128]{2,1,0:T(8,128)(2,1)S(1)}, u32[]{:S(2)}, u32[]{:S(2)}) collective-permute-start(bf16[8,32,128]{2,1,0:T(8,128)(2,1)S(1)} %get-tuple-element.100.refs_3_), channel_id=1, source_target_pairs={{0,2},{1,3},{2,0},{3,1},{4,6},{5,7},{6,4},{7,5},{8,10},{9,11},{10,... | collective-permute-start | bytes 196616 | tf_op jit(solution)/shard_map/ppermute | solution.py:109
  36.3 10.3 %collective-permute-start.11 = (bf16[16,32,128]{2,1,0:T(8,128)(2,1)S(1)}, bf16[16,32,128]{2,1,0:T(8,128)(2,1)S(1)}, u32[]{:S(2)}, u32[]{:S(2)}) collective-permute-start(bf16[16,32,128]{2,1,0:T(8,128)(2,1)S(1)} %get-tuple-element.105.refs_0_), channel_id=1, source_target_pairs={{0,1},{1,0},{2,3},{3,2},{4,5},{5,4},{6,7},{7,6},{8,9},{9,8},{10,11... | collective-permute-start | bytes 393224 | tf_op jit(solution)/shard_map/ppermute | solution.py:110
  38.5 6.5 %collective-permute-start.12 = (bf16[8,32,128]{2,1,0:T(8,128)(2,1)S(1)}, bf16[8,32,128]{2,1,0:T(8,128)(2,1)S(1)}, u32[]{:S(2)}, u32[]{:S(2)}) collective-permute-start(bf16[8,32,128]{2,1,0:T(8,128)(2,1)S(1)} %get-tuple-element.104), channel_id=1, source_target_pairs={{0,2},{1,3},{2,0},{3,1},{4,6},{5,7},{6,4},{7,5},{8,10},{9,11},{10,... | collective-permute-start | bytes 196616 | tf_op jit(solution)/shard_map/ppermute | solution.py:109
  41.3 5.2 %collective-permute-start.14 = (bf16[8,32,128]{2,1,0:T(8,128)(2,1)S(1)}, bf16[8,32,128]{2,1,0:T(8,128)(2,1)S(1)}, u32[]{:S(2)}, u32[]{:S(2)}) collective-permute-start(bf16[8,32,128]{2,1,0:T(8,128)(2,1)S(1)} %hold.4.refs_0_), channel_id=1, source_target_pairs={{0,1},{1,0},{2,3},{3,2},{4,5},{5,4},{6,7},{7,6},{8,9},{9,8},{10,11... | collective-permute-start | bytes 196616 | tf_op jit(solution)/shard_map/ppermute | solution.py:573
  41.3 7.3 %collective-permute-start.10 = (bf16[8,32,128]{2,1,0:T(8,128)(2,1)S(1)}, bf16[8,32,128]{2,1,0:T(8,128)(2,1)S(1)}, u32[]{:S(2)}, u32[]{:S(2)}) collective-permute-start(bf16[8,32,128]{2,1,0:T(8,128)(2,1)S(1)} %get-tuple-element.104), channel_id=1, source_target_pairs={{0,3},{1,2},{2,1},{3,0},{4,7},{5,6},{6,5},{7,4},{8,11},{9,10},{10,... | collective-permute-start | bytes 196616 | tf_op jit(solution)/shard_map/ppermute | solution.py:113
  49.0 1.8 %collective-permute-start.16 = (bf16[48,32,128]{2,1,0:T(8,128)(2,1)S(1)}, bf16[48,32,128]{2,1,0:T(8,128)(2,1)S(1)}, u32[]{:S(2)}, u32[]{:S(2)}) collective-permute-start(bf16[48,32,128]{2,1,0:T(8,128)(2,1)S(1)} %get-tuple-element.116.refs_3_), channel_id=1, source_target_pairs={{0,4},{4,0},{8,12},{12,8},{16,20},{20,16},{24,28},{28,24},{1,5},{5... | collective-permute-start | bytes 1179656 | tf_op jit(solution)/shard_map/ppermute | solution.py:579
  49.3 5.0 %collective-permute-start.15 = (bf16[16,32,128]{2,1,0:T(8,128)(2,1)S(1)}, bf16[16,32,128]{2,1,0:T(8,128)(2,1)S(1)}, u32[]{:S(2)}, u32[]{:S(2)}) collective-permute-start(bf16[16,32,128]{2,1,0:T(8,128)(2,1)S(1)} %get-tuple-element.115.refs_4_), channel_id=1, source_target_pairs={{0,4},{4,0},{8,12},{12,8},{16,20},{20,16},{24,28},{28,24},{1,5},{5... | collective-permute-start | bytes 393224 | tf_op jit(solution)/shard_map/ppermute | solution.py:579
  50.8 7.3 %collective-permute-start.17 = (bf16[16,32,128]{2,1,0:T(8,128)(2,1)S(1)}, bf16[16,32,128]{2,1,0:T(8,128)(2,1)S(1)}, u32[]{:S(2)}, u32[]{:S(2)}) collective-permute-start(bf16[16,32,128]{2,1,0:T(8,128)(2,1)S(1)} %get-tuple-element.118.refs_12_), channel_id=1, source_target_pairs={{0,24},{4,28},{8,16},{12,20},{16,8},{20,12},{24,0},{28,4},{1,25},{... | collective-permute-start | bytes 393224 | tf_op jit(solution)/shard_map/ppermute | solution.py:587
  51.9 8.1 %collective-permute-start.18 = (bf16[16,32,128]{2,1,0:T(8,128)(2,1)S(1)}, bf16[16,32,128]{2,1,0:T(8,128)(2,1)S(1)}, u32[]{:S(2)}, u32[]{:S(2)}) collective-permute-start(bf16[16,32,128]{2,1,0:T(8,128)(2,1)S(1)} %get-tuple-element.119.refs_13_), channel_id=1, source_target_pairs={{0,16},{4,20},{8,24},{12,28},{16,0},{20,4},{24,8},{28,12},{1,17},{... | collective-permute-start | bytes 393224 | tf_op jit(solution)/shard_map/ppermute | solution.py:587
  52.4 7.6 %collective-permute-start.19 = (bf16[16,32,128]{2,1,0:T(8,128)(2,1)S(1)}, bf16[16,32,128]{2,1,0:T(8,128)(2,1)S(1)}, u32[]{:S(2)}, u32[]{:S(2)}) collective-permute-start(bf16[16,32,128]{2,1,0:T(8,128)(2,1)S(1)} %get-tuple-element.117.before_ref.refs_14_), channel_id=1, source_target_pairs={{0,8},{4,12},{8,0},{12,4},{16,24},{20,28},{24,16},{28,20},{1,9},{5... | collective-permute-start | bytes 393224 | tf_op jit(solution)/shard_map/ppermute | solution.py:587
  60.4 6.2 %collective-permute-start.23 = (bf16[8,32,128]{2,1,0:T(8,128)(2,1)S(1)}, bf16[8,32,128]{2,1,0:T(8,128)(2,1)S(1)}, u32[]{:S(2)}, u32[]{:S(2)}) collective-permute-start(bf16[8,32,128]{2,1,0:T(8,128)(2,1)S(1)} %get-tuple-element.122.refs_3_), channel_id=1, source_target_pairs={{0,2},{1,3},{2,0},{3,1},{4,6},{5,7},{6,4},{7,5},{8,10},{9,11},{10,... | collective-permute-start | bytes 196616 | tf_op jit(solution)/shard_map/ppermute | solution.py:109
  61.3 8.6 %collective-permute-start.21 = (bf16[16,32,128]{2,1,0:T(8,128)(2,1)S(1)}, bf16[16,32,128]{2,1,0:T(8,128)(2,1)S(1)}, u32[]{:S(2)}, u32[]{:S(2)}) collective-permute-start(bf16[16,32,128]{2,1,0:T(8,128)(2,1)S(1)} %get-tuple-element.125.refs_0_), channel_id=1, source_target_pairs={{0,1},{1,0},{2,3},{3,2},{4,5},{5,4},{6,7},{7,6},{8,9},{9,8},{10,11... | collective-permute-start | bytes 393224 | tf_op jit(solution)/shard_map/ppermute | solution.py:110
  63.3 6.6 %collective-permute-start.22 = (bf16[8,32,128]{2,1,0:T(8,128)(2,1)S(1)}, bf16[8,32,128]{2,1,0:T(8,128)(2,1)S(1)}, u32[]{:S(2)}, u32[]{:S(2)}) collective-permute-start(bf16[8,32,128]{2,1,0:T(8,128)(2,1)S(1)} %get-tuple-element.124), channel_id=1, source_target_pairs={{0,2},{1,3},{2,0},{3,1},{4,6},{5,7},{6,4},{7,5},{8,10},{9,11},{10,... | collective-permute-start | bytes 196616 | tf_op jit(solution)/shard_map/ppermute | solution.py:109
  66.6 4.7 %collective-permute-start.24 = (bf16[8,32,128]{2,1,0:T(8,128)(2,1)S(1)}, bf16[8,32,128]{2,1,0:T(8,128)(2,1)S(1)}, u32[]{:S(2)}, u32[]{:S(2)}) collective-permute-start(bf16[8,32,128]{2,1,0:T(8,128)(2,1)S(1)} %hold.5.refs_0_), channel_id=1, source_target_pairs={{0,1},{1,0},{2,3},{3,2},{4,5},{5,4},{6,7},{7,6},{8,9},{9,8},{10,11... | collective-permute-start | bytes 196616 | tf_op jit(solution)/shard_map/ppermute | solution.py:573
  66.7 6.6 %collective-permute-start.20 = (bf16[8,32,128]{2,1,0:T(8,128)(2,1)S(1)}, bf16[8,32,128]{2,1,0:T(8,128)(2,1)S(1)}, u32[]{:S(2)}, u32[]{:S(2)}) collective-permute-start(bf16[8,32,128]{2,1,0:T(8,128)(2,1)S(1)} %get-tuple-element.124), channel_id=1, source_target_pairs={{0,3},{1,2},{2,1},{3,0},{4,7},{5,6},{6,5},{7,4},{8,11},{9,10},{10,... | collective-permute-start | bytes 196616 | tf_op jit(solution)/shard_map/ppermute | solution.py:113
  73.7 1.8 %collective-permute-start.26 = (bf16[48,32,128]{2,1,0:T(8,128)(2,1)S(1)}, bf16[48,32,128]{2,1,0:T(8,128)(2,1)S(1)}, u32[]{:S(2)}, u32[]{:S(2)}) collective-permute-start(bf16[48,32,128]{2,1,0:T(8,128)(2,1)S(1)} %get-tuple-element.137), channel_id=1, source_target_pairs={{0,4},{4,0},{8,12},{12,8},{16,20},{20,16},{24,28},{28,24},{1,5},{5... | collective-permute-start | bytes 1179656 | tf_op jit(solution)/shard_map/ppermute | solution.py:579
  74.1 5.0 %collective-permute-start.25 = (bf16[16,32,128]{2,1,0:T(8,128)(2,1)S(1)}, bf16[16,32,128]{2,1,0:T(8,128)(2,1)S(1)}, u32[]{:S(2)}, u32[]{:S(2)}) collective-permute-start(bf16[16,32,128]{2,1,0:T(8,128)(2,1)S(1)} %get-tuple-element.135), channel_id=1, source_target_pairs={{0,4},{4,0},{8,12},{12,8},{16,20},{20,16},{24,28},{28,24},{1,5},{5... | collective-permute-start | bytes 393224 | tf_op jit(solution)/shard_map/ppermute | solution.py:579
  75.6 7.3 %collective-permute-start.27 = (bf16[16,32,128]{2,1,0:T(8,128)(2,1)S(1)}, bf16[16,32,128]{2,1,0:T(8,128)(2,1)S(1)}, u32[]{:S(2)}, u32[]{:S(2)}) collective-permute-start(bf16[16,32,128]{2,1,0:T(8,128)(2,1)S(1)} %get-tuple-element.139), channel_id=1, source_target_pairs={{0,24},{4,28},{8,16},{12,20},{16,8},{20,12},{24,0},{28,4},{1,25},{... | collective-permute-start | bytes 393224 | tf_op jit(solution)/shard_map/ppermute | solution.py:587
  76.6 8.1 %collective-permute-start.28 = (bf16[16,32,128]{2,1,0:T(8,128)(2,1)S(1)}, bf16[16,32,128]{2,1,0:T(8,128)(2,1)S(1)}, u32[]{:S(2)}, u32[]{:S(2)}) collective-permute-start(bf16[16,32,128]{2,1,0:T(8,128)(2,1)S(1)} %get-tuple-element.140), channel_id=1, source_target_pairs={{0,16},{4,20},{8,24},{12,28},{16,0},{20,4},{24,8},{28,12},{1,17},{... | collective-permute-start | bytes 393224 | tf_op jit(solution)/shard_map/ppermute | solution.py:587
  77.1 7.6 %collective-permute-start.29 = (bf16[16,32,128]{2,1,0:T(8,128)(2,1)S(1)}, bf16[16,32,128]{2,1,0:T(8,128)(2,1)S(1)}, u32[]{:S(2)}, u32[]{:S(2)}) collective-permute-start(bf16[16,32,128]{2,1,0:T(8,128)(2,1)S(1)} %get-tuple-element.138.before_ref), channel_id=1, source_target_pairs={{0,8},{4,12},{8,0},{12,4},{16,24},{20,28},{24,16},{28,20},{1,9},{5... | collective-permute-start | bytes 393224 | tf_op jit(solution)/shard_map/ppermute | solution.py:587

commit v15 on v13

--- a/solution.py
+++ b/solution.py
@@ -86,8 +86,8 @@
     far, forwarded = range(1, pairs), range(pairs + 1, groups)
     stages = [
         own + [(index, part) for part in early for index in far],
-        [(pairs, part) for part in every] + [(index, parts - 1) for index in far]
-        + [(index, part) for part in early for index in forwarded],
+        [(index, parts - 1) for index in far],
+        [(pairs, part) for part in every] + [(index, part) for part in early for index in forwarded],
         [(index, parts - 1) for index in forwarded],
     ]
     return [stage for stage in stages if stage]
@@ -610,7 +610,7 @@
         out_specs=in_hbm(),
         scratch_shapes=[
             pltpu.VMEM((owned, rhs, size), jnp.float32),
-            pltpu.SemaphoreType.DMA((2 if owned % 2 == 0 else 1,)),
+            pltpu.SemaphoreType.DMA((4 if owned % 4 == 0 else 1,)),
         ],
         compiler_params=params(),
         name="finish",

time: 83.4 us -> 82.7 us (level)
  Pallas kernels: 29.8 us -> 24.8 us
  starting transfers between devices: 31.7 us -> 33.9 us
  waiting for transfers between devices: 21.3 us -> 23.2 us
    ppermute x3, starting transfers between devices: 6.45 us -> 8.54 us  [gather(): lax.ppermute(rounded[-1], 'col', across)]
    pallas_call x3, Pallas kernels: 7.98 us -> 6.16 us  [product_first(): pl.pallas_call(functools.partial(first_kernel, len(pieces), len(outs) //...]
    pallas_call x1, Pallas kernels: 4.23 us -> 2.56 us  [turn(): pl.pallas_call(turn_kernel, out_shape=[pltpu.VMEM(values.shape, values.dt...]
    ppermute x3, starting transfers between devices: 3.84 us -> 5.06 us  [gather(): sets[groups // 2, 0] = lax.ppermute(whole, 'col', neighbours(groups))]
    ppermute x6, starting transfers between devices: 8.64 us -> 7.42 us  [gather(): sets[step, part] = lax.ppermute(piece, 'col', ring(groups, 2 * step))]
    ppermute x9, waiting for transfers between devices: 13 us -> 14.2 us  [per_device(): lax.ppermute(send, 'row', [(chip * CORES + core, partner(chip, shift, chi...]
    ppermute x3, waiting for transfers between devices: 0.01 us -> 0.98 us  [gather(): lax.ppermute(rounded[-1], 'col', across)]
    pallas_call x3 -> x6, Pallas kernels: 6.44 us -> 5.53 us  [product_stage(): pl.pallas_call(functools.partial(stage_kernel, stage, bits, dims, len(pie...]
  transfers between devices with their start and end apart: 30 -> 30, of which waited for: 15 -> 15; matrix products, arithmetic and copies ran while one was open for 0% -> 0% of each run, Pallas kernels for 29% -> 23%
where the time goes in v15:
time: 82.7 us
  starting transfers between devices  33.9 us (41%)
  Pallas kernels  24.8 us (30%)
  waiting for transfers between devices  23.2 us (28%)
  between operations  0.86 us (1%)
    ppermute x9, waiting for transfers between devices, per_device(): lax.ppermute(send, 'row', [(chip * CORES + core, partner(chip, shift, chi...  14.2 us
    ppermute x9, starting transfers between devices, per_device(): lax.ppermute(send, 'row', [(chip * CORES + core, partner(chip, shift, chi...  10.7 us
    ppermute x3, starting transfers between devices, gather(): lax.ppermute(rounded[-1], 'col', across)  8.54 us
    ppermute x6, starting transfers between devices, gather(): sets[step, part] = lax.ppermute(piece, 'col', ring(groups, 2 * step))  7.42 us
    pallas_call x3, Pallas kernels, product_first(): pl.pallas_call(functools.partial(first_kernel, len(pieces), len(outs) //...  6.16 us
    pallas_call x6, Pallas kernels, product_stage(): pl.pallas_call(functools.partial(stage_kernel, stage, bits, dims, len(pie...  5.53 us
    ppermute x3, starting transfers between devices, gather(): sets[groups // 2, 0] = lax.ppermute(whole, 'col', neighbours(groups))  5.06 us
    ppermute x6, waiting for transfers between devices, gather(): sets[step, part] = lax.ppermute(piece, 'col', ring(groups, 2 * step))  4.58 us
  transfers between devices with their start and end apart: 30, of which 15 were waited for; matrix products, arithmetic and copies ran while one was open for 0% of the time, Pallas kernels for 23%

profile of v15, /device:TPU:0, one launch (start us, length us, event | category | flops | bytes accessed | tf_op | source)
XLA Modules:
  0.0 82.7 jit_solution(10738685303679171809)
XLA Ops:
  0.0 2.2 %start.1 = (bf16[16,128,128]{2,1,0:T(8,128)(2,1)S(1)}, bf16[16,128,128]{2,1,0:T(8,128)(2,1)S(1)}, f32[16,32,128]{2,1,0:T(8,128)S(1)}, f32[16,32,128]{2,1,0:T(8,1...) custom-call(f32[16,128,128]{2,1,0:T(8,128)} %bitcast.5, ...), custom_call_target="tpu_custom_call" | custom-call | tf_op jit(solution)/shard_map/start/pallas_call | solution.py:418
  2.2 4.1 %collective-permute-start.2 = (bf16[8,32,128]{2,1,0:T(8,128)(2,1)S(1)}, bf16[8,32,128]{2,1,0:T(8,128)(2,1)S(1)}, u32[]{:S(2)}, u32[]{:S(2)}) collective-permute-start(bf16[8,32,128]{2,1,0:T(8,128)(2,1)S(1)} %get-tuple-element.80), channel_id=1, source_target_pairs={{0,2},{1,3},{2,0},{3,1},{4,6},{5,7},{6,4},{7,5},{8,10},{9,11},{10,... | collective-permute-start | bytes 196616 | tf_op jit(solution)/shard_map/ppermute | solution.py:108
  6.3 1.6 %collective-permute-start.1 = (bf16[16,32,128]{2,1,0:T(8,128)(2,1)S(1)}, bf16[16,32,128]{2,1,0:T(8,128)(2,1)S(1)}, u32[]{:S(2)}, u32[]{:S(2)}) collective-permute-start(bf16[16,32,128]{2,1,0:T(8,128)(2,1)S(1)} %get-tuple-element.79.refs_0_), channel_id=1, source_target_pairs={{0,1},{1,0},{2,3},{3,2},{4,5},{5,4},{6,7},{7,6},{8,9},{9,8},{10,11... | collective-permute-start | bytes 393224 | tf_op jit(solution)/shard_map/ppermute | solution.py:109
  8.8 2.8 %order.1 = (s32[9,208]{1,0:T(8,128)S(4)}, s32[8]{0:T(128)S(4)}, bf16[192,128,128]{2,1,0:T(8,128)(2,1)S(1)}, f32[8,128]{1,0:T(8,128)S(1)}) custom-call(s32[1,1]{1,0:T(1,128)S(6)} %copy.63.count_ref, s32[1,1,192]{2,1,0:T(1,128)} %rows_hbm.1, s32[1,1,192]{2,1,0:T(1,128)} %cols_hbm.1, bf16[192,128,128]{2,1,0:T(8,128)(2,1)} %bitcast.4), custom_call_target="tpu_custom_call" | custom-call | tf_op jit(solution)/shard_map/order/pallas_call | solution.py:431
  11.9 4.5 %collective-permute-start = (bf16[8,32,128]{2,1,0:T(8,128)(2,1)S(1)}, bf16[8,32,128]{2,1,0:T(8,128)(2,1)S(1)}, u32[]{:S(2)}, u32[]{:S(2)}) collective-permute-start(bf16[8,32,128]{2,1,0:T(8,128)(2,1)S(1)} %get-tuple-element.78), channel_id=1, source_target_pairs={{0,3},{1,2},{2,1},{3,0},{4,7},{5,6},{6,5},{7,4},{8,11},{9,10},{10,... | collective-permute-start | bytes 196616 | tf_op jit(solution)/shard_map/ppermute | solution.py:112
  16.5 2.3 %stage0.3 = (f32[65,32,128]{2,1,0:T(8,128)S(1)}, f32[65,32,128]{2,1,0:T(8,128)S(1)}, f32[8,128]{1,0:T(8,128)}) custom-call(s32[9,208]{1,0:T(8,128)S(4)} %get-tuple-element.77.list_ref, s32[8]{0:T(128)S(4)} %get-tuple-element.75.total_ref, bf16[192,128,128]{2,1,0:T(8,128)(2,1)S(1)} %get-tuple-element.76.values_ref, ...), custom_call_target="tpu_custom_call" | custom-call | flops 75497472 | bytes 2359296 | tf_op jit(solution)/shard_map/stage0/pallas_call | solution.py:473
  19.6 1.6 %stage2.3 = (f32[65,32,128]{2,1,0:T(8,128)S(1)}, f32[65,32,128]{2,1,0:T(8,128)S(1)}) custom-call(s32[9,208]{1,0:T(8,128)S(4)} %get-tuple-element.77.list_ref, s32[8]{0:T(128)S(4)} %get-tuple-element.75.total_ref, bf16[192,128,128]{2,1,0:T(8,128)(2,1)S(1)} %get-tuple-element.76.values_ref, ...), custom_call_target="tpu_custom_call", output_to_operand_aliasing={{0}: (5, {}), {1}: (6, {})} | custom-call | flops 75497472 | bytes 2359296 | tf_op jit(solution)/shard_map/stage2/pallas_call | solution.py:486
  23.6 1.1 %collective-permute-start.7 = (bf16[16,32,128]{2,1,0:T(8,128)(2,1)S(1)}, bf16[16,32,128]{2,1,0:T(8,128)(2,1)S(1)}, u32[]{:S(2)}, u32[]{:S(2)}) collective-permute-start(bf16[16,32,128]{2,1,0:T(8,128)(2,1)S(1)} %get-tuple-element.94.refs_6_.refs_10_), channel_id=1, source_target_pairs={{0,24},{4,28},{8,16},{12,20},{16,8},{20,12},{24,0},{28,4},{1,25},{... | collective-permute-start | bytes 393224 | tf_op jit(solution)/shard_map/ppermute | solution.py:591
  24.6 2.0 %collective-permute-start.8 = (bf16[16,32,128]{2,1,0:T(8,128)(2,1)S(1)}, bf16[16,32,128]{2,1,0:T(8,128)(2,1)S(1)}, u32[]{:S(2)}, u32[]{:S(2)}) collective-permute-start(bf16[16,32,128]{2,1,0:T(8,128)(2,1)S(1)} %get-tuple-element.95.refs_7_.refs_11_), channel_id=1, source_target_pairs={{0,16},{4,20},{8,24},{12,28},{16,0},{20,4},{24,8},{28,12},{1,17},{... | collective-permute-start | bytes 393224 | tf_op jit(solution)/shard_map/ppermute | solution.py:591
  27.2 2.6 %turn.1 = (bf16[192,128,128]{2,1,0:T(8,128)(2,1)S(1)}, f32[16,32,128]{2,1,0:T(8,128)S(1)}) custom-call(s32[8]{0:T(128)S(4)} %get-tuple-element.75.total_ref, bf16[192,128,128]{2,1,0:T(8,128)(2,1)S(1)} %get-tuple-element.76.values_ref, f32[16,32,128]{2,1,0:T(8,128)S(1)} %combine1.3.base_ref), custom_call_target="tpu_custom_call", output_to_operand_aliasing={{1}: (2, {})} | custom-call | flops 20000000000 | tf_op jit(solution)/shard_map/turn/pallas_call | solution.py:453
  29.7 1.2 %collective-permute-done.7.refs_0_ = bf16[16,32,128]{2,1,0:T(8,128)(2,1)S(1)} collective-permute-done((bf16[16,32,128]{2,1,0:T(8,128)(2,1)S(1)}, bf16[16,32,128]{2,1,0:T(8,128)(2,1)S(1)}, u32[]{:S(2)}, u32[]{:S(2)}) %collective-permute-start.7) | collective-permute-done | bytes 131104 | tf_op jit(solution)/shard_map/ppermute | solution.py:591
  30.9 2.0 %collective-permute-done.8.refs_1_ = bf16[16,32,128]{2,1,0:T(8,128)(2,1)S(1)} collective-permute-done((bf16[16,32,128]{2,1,0:T(8,128)(2,1)S(1)}, bf16[16,32,128]{2,1,0:T(8,128)(2,1)S(1)}, u32[]{:S(2)}, u32[]{:S(2)}) %collective-permute-start.8) | collective-permute-done | bytes 131104 | tf_op jit(solution)/shard_map/ppermute | solution.py:591
  33.9 1.8 %collective-permute-start.11 = (bf16[16,32,128]{2,1,0:T(8,128)(2,1)S(1)}, bf16[16,32,128]{2,1,0:T(8,128)(2,1)S(1)}, u32[]{:S(2)}, u32[]{:S(2)}) collective-permute-start(bf16[16,32,128]{2,1,0:T(8,128)(2,1)S(1)} %get-tuple-element.103.refs_0_), channel_id=1, source_target_pairs={{0,1},{1,0},{2,3},{3,2},{4,5},{5,4},{6,7},{7,6},{8,9},{9,8},{10,11... | collective-permute-start | bytes 393224 | tf_op jit(solution)/shard_map/ppermute | solution.py:109
  36.7 1.8 %collective-permute-done.12.refs_1_ = bf16[8,32,128]{2,1,0:T(8,128)(2,1)S(1)} collective-permute-done((bf16[8,32,128]{2,1,0:T(8,128)(2,1)S(1)}, bf16[8,32,128]{2,1,0:T(8,128)(2,1)S(1)}, u32[]{:S(2)}, u32[]{:S(2)}) %collective-permute-start.12) | collective-permute-done | bytes 65568 | tf_op jit(solution)/shard_map/ppermute | solution.py:108
  38.7 2.3 %collective-permute-start.10 = (bf16[8,32,128]{2,1,0:T(8,128)(2,1)S(1)}, bf16[8,32,128]{2,1,0:T(8,128)(2,1)S(1)}, u32[]{:S(2)}, u32[]{:S(2)}) collective-permute-start(bf16[8,32,128]{2,1,0:T(8,128)(2,1)S(1)} %get-tuple-element.102), channel_id=1, source_target_pairs={{0,3},{1,2},{2,1},{3,0},{4,7},{5,6},{6,5},{7,4},{8,11},{9,10},{10,... | collective-permute-start | bytes 196616 | tf_op jit(solution)/shard_map/ppermute | solution.py:112
  40.9 1.8 %stage0.4 = (f32[65,32,128]{2,1,0:T(8,128)S(1)}, f32[65,32,128]{2,1,0:T(8,128)S(1)}, f32[8,128]{1,0:T(8,128)}) custom-call(s32[9,208]{1,0:T(8,128)S(4)} %get-tuple-element.77.list_ref, s32[8]{0:T(128)S(4)} %get-tuple-element.75.total_ref, bf16[192,128,128]{2,1,0:T(8,128)(2,1)S(1)} %get-tuple-element.101.values_ref, ...), custom_call_target="tpu_custom_call" | custom-call | flops 75497472 | bytes 2359296 | tf_op jit(solution)/shard_map/stage0/pallas_call | solution.py:473
  43.6 1.1 %stage2.4 = (f32[65,32,128]{2,1,0:T(8,128)S(1)}, f32[65,32,128]{2,1,0:T(8,128)S(1)}) custom-call(s32[9,208]{1,0:T(8,128)S(4)} %get-tuple-element.77.list_ref, s32[8]{0:T(128)S(4)} %get-tuple-element.75.total_ref, bf16[192,128,128]{2,1,0:T(8,128)(2,1)S(1)} %get-tuple-element.101.values_ref, ...), custom_call_target="tpu_custom_call", output_to_operand_aliasing={{0}: (5, {}), {1}: (6, {})} | custom-call | flops 75497472 | bytes 2359296 | tf_op jit(solution)/shard_map/stage2/pallas_call | solution.py:486
  47.7 1.1 %collective-permute-start.17 = (bf16[16,32,128]{2,1,0:T(8,128)(2,1)S(1)}, bf16[16,32,128]{2,1,0:T(8,128)(2,1)S(1)}, u32[]{:S(2)}, u32[]{:S(2)}) collective-permute-start(bf16[16,32,128]{2,1,0:T(8,128)(2,1)S(1)} %get-tuple-element.115.refs_13_), channel_id=1, source_target_pairs={{0,24},{4,28},{8,16},{12,20},{16,8},{20,12},{24,0},{28,4},{1,25},{... | collective-permute-start | bytes 393224 | tf_op jit(solution)/shard_map/ppermute | solution.py:591
  49.8 1.4 %collective-permute-start.19 = (bf16[16,32,128]{2,1,0:T(8,128)(2,1)S(1)}, bf16[16,32,128]{2,1,0:T(8,128)(2,1)S(1)}, u32[]{:S(2)}, u32[]{:S(2)}) collective-permute-start(bf16[16,32,128]{2,1,0:T(8,128)(2,1)S(1)} %get-tuple-element.114.before_ref.refs_15_), channel_id=1, source_target_pairs={{0,8},{4,12},{8,0},{12,4},{16,24},{20,28},{24,16},{28,20},{1,9},{5... | collective-permute-start | bytes 393224 | tf_op jit(solution)/shard_map/ppermute | solution.py:591
  51.3 3.7 %collective-permute-done.17.refs_0_ = bf16[16,32,128]{2,1,0:T(8,128)(2,1)S(1)} collective-permute-done((bf16[16,32,128]{2,1,0:T(8,128)(2,1)S(1)}, bf16[16,32,128]{2,1,0:T(8,128)(2,1)S(1)}, u32[]{:S(2)}, u32[]{:S(2)}) %collective-permute-start.17) | collective-permute-done | bytes 131104 | tf_op jit(solution)/shard_map/ppermute | solution.py:591
  55.0 1.8 %collective-permute-done.18.refs_1_ = bf16[16,32,128]{2,1,0:T(8,128)(2,1)S(1)} collective-permute-done((bf16[16,32,128]{2,1,0:T(8,128)(2,1)S(1)}, bf16[16,32,128]{2,1,0:T(8,128)(2,1)S(1)}, u32[]{:S(2)}, u32[]{:S(2)}) %collective-permute-start.18) | collective-permute-done | bytes 131104 | tf_op jit(solution)/shard_map/ppermute | solution.py:591
  57.3 1.2 %collective-permute-start.22 = (bf16[8,32,128]{2,1,0:T(8,128)(2,1)S(1)}, bf16[8,32,128]{2,1,0:T(8,128)(2,1)S(1)}, u32[]{:S(2)}, u32[]{:S(2)}) collective-permute-start(bf16[8,32,128]{2,1,0:T(8,128)(2,1)S(1)} %get-tuple-element.119.refs_3_), channel_id=1, source_target_pairs={{0,2},{1,3},{2,0},{3,1},{4,6},{5,7},{6,4},{7,5},{8,10},{9,11},{10,... | collective-permute-start | bytes 196616 | tf_op jit(solution)/shard_map/ppermute | solution.py:108
  58.8 1.7 %collective-permute-start.21 = (bf16[16,32,128]{2,1,0:T(8,128)(2,1)S(1)}, bf16[16,32,128]{2,1,0:T(8,128)(2,1)S(1)}, u32[]{:S(2)}, u32[]{:S(2)}) collective-permute-start(bf16[16,32,128]{2,1,0:T(8,128)(2,1)S(1)} %get-tuple-element.122.refs_0_), channel_id=1, source_target_pairs={{0,1},{1,0},{2,3},{3,2},{4,5},{5,4},{6,7},{7,6},{8,9},{9,8},{10,11... | collective-permute-start | bytes 393224 | tf_op jit(solution)/shard_map/ppermute | solution.py:109
  61.1 2.8 %collective-permute-done.22.refs_1_ = bf16[8,32,128]{2,1,0:T(8,128)(2,1)S(1)} collective-permute-done((bf16[8,32,128]{2,1,0:T(8,128)(2,1)S(1)}, bf16[8,32,128]{2,1,0:T(8,128)(2,1)S(1)}, u32[]{:S(2)}, u32[]{:S(2)}) %collective-permute-start.22) | collective-permute-done | bytes 65568 | tf_op jit(solution)/shard_map/ppermute | solution.py:108
  63.9 1.8 %collective-permute-start.20 = (bf16[8,32,128]{2,1,0:T(8,128)(2,1)S(1)}, bf16[8,32,128]{2,1,0:T(8,128)(2,1)S(1)}, u32[]{:S(2)}, u32[]{:S(2)}) collective-permute-start(bf16[8,32,128]{2,1,0:T(8,128)(2,1)S(1)} %get-tuple-element.121), channel_id=1, source_target_pairs={{0,3},{1,2},{2,1},{3,0},{4,7},{5,6},{6,5},{7,4},{8,11},{9,10},{10,... | collective-permute-start | bytes 196616 | tf_op jit(solution)/shard_map/ppermute | solution.py:112
  65.7 2.0 %stage0.5 = (f32[65,32,128]{2,1,0:T(8,128)S(1)}, f32[65,32,128]{2,1,0:T(8,128)S(1)}, f32[8,128]{1,0:T(8,128)}) custom-call(s32[9,208]{1,0:T(8,128)S(4)} %get-tuple-element.77.list_ref, s32[8]{0:T(128)S(4)} %get-tuple-element.75.total_ref, bf16[192,128,128]{2,1,0:T(8,128)(2,1)S(1)} %get-tuple-element.101.values_ref, ...), custom_call_target="tpu_custom_call" | custom-call | flops 75497472 | bytes 2359296 | tf_op jit(solution)/shard_map/stage0/pallas_call | solution.py:473
  68.9 1.1 %stage2.5 = (f32[65,32,128]{2,1,0:T(8,128)S(1)}, f32[65,32,128]{2,1,0:T(8,128)S(1)}) custom-call(s32[9,208]{1,0:T(8,128)S(4)} %get-tuple-element.77.list_ref, s32[8]{0:T(128)S(4)} %get-tuple-element.75.total_ref, bf16[192,128,128]{2,1,0:T(8,128)(2,1)S(1)} %get-tuple-element.101.values_ref, ...), custom_call_target="tpu_custom_call", output_to_operand_aliasing={{0}: (5, {}), {1}: (6, {})} | custom-call | flops 75497472 | bytes 2359296 | tf_op jit(solution)/shard_map/stage2/pallas_call | solution.py:486
  73.3 1.2 %collective-permute-start.28 = (bf16[16,32,128]{2,1,0:T(8,128)(2,1)S(1)}, bf16[16,32,128]{2,1,0:T(8,128)(2,1)S(1)}, u32[]{:S(2)}, u32[]{:S(2)}) collective-permute-start(bf16[16,32,128]{2,1,0:T(8,128)(2,1)S(1)} %get-tuple-element.136), channel_id=1, source_target_pairs={{0,16},{4,20},{8,24},{12,28},{16,0},{20,4},{24,8},{28,12},{1,17},{... | collective-permute-start | bytes 393224 | tf_op jit(solution)/shard_map/ppermute | solution.py:591
  74.5 1.3 %collective-permute-start.29 = (bf16[16,32,128]{2,1,0:T(8,128)(2,1)S(1)}, bf16[16,32,128]{2,1,0:T(8,128)(2,1)S(1)}, u32[]{:S(2)}, u32[]{:S(2)}) collective-permute-start(bf16[16,32,128]{2,1,0:T(8,128)(2,1)S(1)} %get-tuple-element.134.before_ref), channel_id=1, source_target_pairs={{0,8},{4,12},{8,0},{12,4},{16,24},{20,28},{24,16},{28,20},{1,9},{5... | collective-permute-start | bytes 393224 | tf_op jit(solution)/shard_map/ppermute | solution.py:591
  75.9 3.7 %collective-permute-done.27.refs_0_ = bf16[16,32,128]{2,1,0:T(8,128)(2,1)S(1)} collective-permute-done((bf16[16,32,128]{2,1,0:T(8,128)(2,1)S(1)}, bf16[16,32,128]{2,1,0:T(8,128)(2,1)S(1)}, u32[]{:S(2)}, u32[]{:S(2)}) %collective-permute-start.27) | collective-permute-done | bytes 131104 | tf_op jit(solution)/shard_map/ppermute | solution.py:591
  79.6 1.7 %collective-permute-done.28.refs_1_ = bf16[16,32,128]{2,1,0:T(8,128)(2,1)S(1)} collective-permute-done((bf16[16,32,128]{2,1,0:T(8,128)(2,1)S(1)}, bf16[16,32,128]{2,1,0:T(8,128)(2,1)S(1)}, u32[]{:S(2)}, u32[]{:S(2)}) %collective-permute-start.28) | collective-permute-done | bytes 131104 | tf_op jit(solution)/shard_map/ppermute | solution.py:591
  81.3 1.4 %finish.1 = f32[16,32,128]{2,1,0:T(8,128)} custom-call(bf16[16,128,128]{2,1,0:T(8,128)(2,1)S(1)} %get-tuple-element.71.high_ref, bf16[16,128,128]{2,1,0:T(8,128)(2,1)S(1)} %get-tuple-element.72.low_ref, f32[16,32,128]{2,1,0:T(8,128)S(1)} %get-tuple-element.120.sol_ref, f32[16,32,128]{2,1,0:T(8,128)S(1)} %combine1.5.base_ref, ...), custom_call_target="tpu_custom_call" | custom-call | tf_op jit(solution)/shard_map/finish/pallas_call | solution.py:606
  (58 shorter events, 17.4 us)
Async XLA Ops:
  2.2 9.5 %collective-permute-start.2 = (bf16[8,32,128]{2,1,0:T(8,128)(2,1)S(1)}, bf16[8,32,128]{2,1,0:T(8,128)(2,1)S(1)}, u32[]{:S(2)}, u32[]{:S(2)}) collective-permute-start(bf16[8,32,128]{2,1,0:T(8,128)(2,1)S(1)} %get-tuple-element.80), channel_id=1, source_target_pairs={{0,2},{1,3},{2,0},{3,1},{4,6},{5,7},{6,4},{7,5},{8,10},{9,11},{10,... | collective-permute-start | bytes 196616 | tf_op jit(solution)/shard_map/ppermute | solution.py:108
  6.3 13.3 %collective-permute-start.1 = (bf16[16,32,128]{2,1,0:T(8,128)(2,1)S(1)}, bf16[16,32,128]{2,1,0:T(8,128)(2,1)S(1)}, u32[]{:S(2)}, u32[]{:S(2)}) collective-permute-start(bf16[16,32,128]{2,1,0:T(8,128)(2,1)S(1)} %get-tuple-element.79.refs_0_), channel_id=1, source_target_pairs={{0,1},{1,0},{2,3},{3,2},{4,5},{5,4},{6,7},{7,6},{8,9},{9,8},{10,11... | collective-permute-start | bytes 393224 | tf_op jit(solution)/shard_map/ppermute | solution.py:109
  7.8 11.0 %collective-permute-start.4 = (bf16[8,32,128]{2,1,0:T(8,128)(2,1)S(1)}, bf16[8,32,128]{2,1,0:T(8,128)(2,1)S(1)}, u32[]{:S(2)}, u32[]{:S(2)}) collective-permute-start(bf16[8,32,128]{2,1,0:T(8,128)(2,1)S(1)} %get-tuple-element.78), channel_id=1, source_target_pairs={{0,2},{1,3},{2,0},{3,1},{4,6},{5,7},{6,4},{7,5},{8,10},{9,11},{10,... | collective-permute-start | bytes 196616 | tf_op jit(solution)/shard_map/ppermute | solution.py:108
  11.7 7.9 %collective-permute-start.3 = (bf16[8,32,128]{2,1,0:T(8,128)(2,1)S(1)}, bf16[8,32,128]{2,1,0:T(8,128)(2,1)S(1)}, u32[]{:S(2)}, u32[]{:S(2)}) collective-permute-start(bf16[8,32,128]{2,1,0:T(8,128)(2,1)S(1)} %hold.1.refs_1_), channel_id=1, source_target_pairs={{0,1},{1,0},{2,3},{3,2},{4,5},{5,4},{6,7},{7,6},{8,9},{9,8},{10,11... | collective-permute-start | bytes 196616 | tf_op jit(solution)/shard_map/ppermute | solution.py:571
  11.9 9.3 %collective-permute-start = (bf16[8,32,128]{2,1,0:T(8,128)(2,1)S(1)}, bf16[8,32,128]{2,1,0:T(8,128)(2,1)S(1)}, u32[]{:S(2)}, u32[]{:S(2)}) collective-permute-start(bf16[8,32,128]{2,1,0:T(8,128)(2,1)S(1)} %get-tuple-element.78), channel_id=1, source_target_pairs={{0,3},{1,2},{2,1},{3,0},{4,7},{5,6},{6,5},{7,4},{8,11},{9,10},{10,... | collective-permute-start | bytes 196616 | tf_op jit(solution)/shard_map/ppermute | solution.py:112
  21.7 1.8 %collective-permute-start.6 = (bf16[48,32,128]{2,1,0:T(8,128)(2,1)S(1)}, bf16[48,32,128]{2,1,0:T(8,128)(2,1)S(1)}, u32[]{:S(2)}, u32[]{:S(2)}) collective-permute-start(bf16[48,32,128]{2,1,0:T(8,128)(2,1)S(1)} %get-tuple-element.91.refs_2_), channel_id=1, source_target_pairs={{0,4},{4,0},{8,12},{12,8},{16,20},{20,16},{24,28},{28,24},{1,5},{5... | collective-permute-start | bytes 1179656 | tf_op jit(solution)/shard_map/ppermute | solution.py:583
  22.2 4.9 %collective-permute-start.5 = (bf16[16,32,128]{2,1,0:T(8,128)(2,1)S(1)}, bf16[16,32,128]{2,1,0:T(8,128)(2,1)S(1)}, u32[]{:S(2)}, u32[]{:S(2)}) collective-permute-start(bf16[16,32,128]{2,1,0:T(8,128)(2,1)S(1)} %get-tuple-element.90.refs_3_), channel_id=1, source_target_pairs={{0,4},{4,0},{8,12},{12,8},{16,20},{20,16},{24,28},{28,24},{1,5},{5... | collective-permute-start | bytes 393224 | tf_op jit(solution)/shard_map/ppermute | solution.py:583
  23.6 7.3 %collective-permute-start.7 = (bf16[16,32,128]{2,1,0:T(8,128)(2,1)S(1)}, bf16[16,32,128]{2,1,0:T(8,128)(2,1)S(1)}, u32[]{:S(2)}, u32[]{:S(2)}) collective-permute-start(bf16[16,32,128]{2,1,0:T(8,128)(2,1)S(1)} %get-tuple-element.94.refs_6_.refs_10_), channel_id=1, source_target_pairs={{0,24},{4,28},{8,16},{12,20},{16,8},{20,12},{24,0},{28,4},{1,25},{... | collective-permute-start | bytes 393224 | tf_op jit(solution)/shard_map/ppermute | solution.py:591
  24.6 8.3 %collective-permute-start.8 = (bf16[16,32,128]{2,1,0:T(8,128)(2,1)S(1)}, bf16[16,32,128]{2,1,0:T(8,128)(2,1)S(1)}, u32[]{:S(2)}, u32[]{:S(2)}) collective-permute-start(bf16[16,32,128]{2,1,0:T(8,128)(2,1)S(1)} %get-tuple-element.95.refs_7_.refs_11_), channel_id=1, source_target_pairs={{0,16},{4,20},{8,24},{12,28},{16,0},{20,4},{24,8},{28,12},{1,17},{... | collective-permute-start | bytes 393224 | tf_op jit(solution)/shard_map/ppermute | solution.py:591
  26.6 6.3 %collective-permute-start.9 = (bf16[16,32,128]{2,1,0:T(8,128)(2,1)S(1)}, bf16[16,32,128]{2,1,0:T(8,128)(2,1)S(1)}, u32[]{:S(2)}, u32[]{:S(2)}) collective-permute-start(bf16[16,32,128]{2,1,0:T(8,128)(2,1)S(1)} %get-tuple-element.92.before_ref.refs_8_.refs_12_), channel_id=1, source_target_pairs={{0,8},{4,12},{8,0},{12,4},{16,24},{20,28},{24,16},{28,20},{1,9},{5... | collective-permute-start | bytes 393224 | tf_op jit(solution)/shard_map/ppermute | solution.py:591
  33.3 5.2 %collective-permute-start.12 = (bf16[8,32,128]{2,1,0:T(8,128)(2,1)S(1)}, bf16[8,32,128]{2,1,0:T(8,128)(2,1)S(1)}, u32[]{:S(2)}, u32[]{:S(2)}) collective-permute-start(bf16[8,32,128]{2,1,0:T(8,128)(2,1)S(1)} %get-tuple-element.98.refs_3_), channel_id=1, source_target_pairs={{0,2},{1,3},{2,0},{3,1},{4,6},{5,7},{6,4},{7,5},{8,10},{9,11},{10,... | collective-permute-start | bytes 196616 | tf_op jit(solution)/shard_map/ppermute | solution.py:108
  33.9 9.7 %collective-permute-start.11 = (bf16[16,32,128]{2,1,0:T(8,128)(2,1)S(1)}, bf16[16,32,128]{2,1,0:T(8,128)(2,1)S(1)}, u32[]{:S(2)}, u32[]{:S(2)}) collective-permute-start(bf16[16,32,128]{2,1,0:T(8,128)(2,1)S(1)} %get-tuple-element.103.refs_0_), channel_id=1, source_target_pairs={{0,1},{1,0},{2,3},{3,2},{4,5},{5,4},{6,7},{7,6},{8,9},{9,8},{10,11... | collective-permute-start | bytes 393224 | tf_op jit(solution)/shard_map/ppermute | solution.py:109
  35.7 7.0 %collective-permute-start.14 = (bf16[8,32,128]{2,1,0:T(8,128)(2,1)S(1)}, bf16[8,32,128]{2,1,0:T(8,128)(2,1)S(1)}, u32[]{:S(2)}, u32[]{:S(2)}) collective-permute-start(bf16[8,32,128]{2,1,0:T(8,128)(2,1)S(1)} %get-tuple-element.102), channel_id=1, source_target_pairs={{0,2},{1,3},{2,0},{3,1},{4,6},{5,7},{6,4},{7,5},{8,10},{9,11},{10,... | collective-permute-start | bytes 196616 | tf_op jit(solution)/shard_map/ppermute | solution.py:108
  38.5 5.1 %collective-permute-start.13 = (bf16[8,32,128]{2,1,0:T(8,128)(2,1)S(1)}, bf16[8,32,128]{2,1,0:T(8,128)(2,1)S(1)}, u32[]{:S(2)}, u32[]{:S(2)}) collective-permute-start(bf16[8,32,128]{2,1,0:T(8,128)(2,1)S(1)} %collective-permute-done.12.refs_1_), channel_id=1, source_target_pairs={{0,1},{1,0},{2,3},{3,2},{4,5},{5,4},{6,7},{7,6},{8,9},{9,8},{10,11... | collective-permute-start | bytes 196616 | tf_op jit(solution)/shard_map/ppermute | solution.py:571
  38.7 6.8 %collective-permute-start.10 = (bf16[8,32,128]{2,1,0:T(8,128)(2,1)S(1)}, bf16[8,32,128]{2,1,0:T(8,128)(2,1)S(1)}, u32[]{:S(2)}, u32[]{:S(2)}) collective-permute-start(bf16[8,32,128]{2,1,0:T(8,128)(2,1)S(1)} %get-tuple-element.102), channel_id=1, source_target_pairs={{0,3},{1,2},{2,1},{3,0},{4,7},{5,6},{6,5},{7,4},{8,11},{9,10},{10,... | collective-permute-start | bytes 196616 | tf_op jit(solution)/shard_map/ppermute | solution.py:112
  45.8 1.8 %collective-permute-start.16 = (bf16[48,32,128]{2,1,0:T(8,128)(2,1)S(1)}, bf16[48,32,128]{2,1,0:T(8,128)(2,1)S(1)}, u32[]{:S(2)}, u32[]{:S(2)}) collective-permute-start(bf16[48,32,128]{2,1,0:T(8,128)(2,1)S(1)} %get-tuple-element.113.refs_4_), channel_id=1, source_target_pairs={{0,4},{4,0},{8,12},{12,8},{16,20},{20,16},{24,28},{28,24},{1,5},{5... | collective-permute-start | bytes 1179656 | tf_op jit(solution)/shard_map/ppermute | solution.py:583
  46.2 5.0 %collective-permute-start.15 = (bf16[16,32,128]{2,1,0:T(8,128)(2,1)S(1)}, bf16[16,32,128]{2,1,0:T(8,128)(2,1)S(1)}, u32[]{:S(2)}, u32[]{:S(2)}) collective-permute-start(bf16[16,32,128]{2,1,0:T(8,128)(2,1)S(1)} %get-tuple-element.112.refs_5_), channel_id=1, source_target_pairs={{0,4},{4,0},{8,12},{12,8},{16,20},{20,16},{24,28},{28,24},{1,5},{5... | collective-permute-start | bytes 393224 | tf_op jit(solution)/shard_map/ppermute | solution.py:583
  47.7 7.3 %collective-permute-start.17 = (bf16[16,32,128]{2,1,0:T(8,128)(2,1)S(1)}, bf16[16,32,128]{2,1,0:T(8,128)(2,1)S(1)}, u32[]{:S(2)}, u32[]{:S(2)}) collective-permute-start(bf16[16,32,128]{2,1,0:T(8,128)(2,1)S(1)} %get-tuple-element.115.refs_13_), channel_id=1, source_target_pairs={{0,24},{4,28},{8,16},{12,20},{16,8},{20,12},{24,0},{28,4},{1,25},{... | collective-permute-start | bytes 393224 | tf_op jit(solution)/shard_map/ppermute | solution.py:591
  48.8 8.1 %collective-permute-start.18 = (bf16[16,32,128]{2,1,0:T(8,128)(2,1)S(1)}, bf16[16,32,128]{2,1,0:T(8,128)(2,1)S(1)}, u32[]{:S(2)}, u32[]{:S(2)}) collective-permute-start(bf16[16,32,128]{2,1,0:T(8,128)(2,1)S(1)} %get-tuple-element.116.refs_14_), channel_id=1, source_target_pairs={{0,16},{4,20},{8,24},{12,28},{16,0},{20,4},{24,8},{28,12},{1,17},{... | collective-permute-start | bytes 393224 | tf_op jit(solution)/shard_map/ppermute | solution.py:591
  49.8 7.0 %collective-permute-start.19 = (bf16[16,32,128]{2,1,0:T(8,128)(2,1)S(1)}, bf16[16,32,128]{2,1,0:T(8,128)(2,1)S(1)}, u32[]{:S(2)}, u32[]{:S(2)}) collective-permute-start(bf16[16,32,128]{2,1,0:T(8,128)(2,1)S(1)} %get-tuple-element.114.before_ref.refs_15_), channel_id=1, source_target_pairs={{0,8},{4,12},{8,0},{12,4},{16,24},{20,28},{24,16},{28,20},{1,9},{5... | collective-permute-start | bytes 393224 | tf_op jit(solution)/shard_map/ppermute | solution.py:591
  57.3 6.6 %collective-permute-start.22 = (bf16[8,32,128]{2,1,0:T(8,128)(2,1)S(1)}, bf16[8,32,128]{2,1,0:T(8,128)(2,1)S(1)}, u32[]{:S(2)}, u32[]{:S(2)}) collective-permute-start(bf16[8,32,128]{2,1,0:T(8,128)(2,1)S(1)} %get-tuple-element.119.refs_3_), channel_id=1, source_target_pairs={{0,2},{1,3},{2,0},{3,1},{4,6},{5,7},{6,4},{7,5},{8,10},{9,11},{10,... | collective-permute-start | bytes 196616 | tf_op jit(solution)/shard_map/ppermute | solution.py:108
  58.8 9.3 %collective-permute-start.21 = (bf16[16,32,128]{2,1,0:T(8,128)(2,1)S(1)}, bf16[16,32,128]{2,1,0:T(8,128)(2,1)S(1)}, u32[]{:S(2)}, u32[]{:S(2)}) collective-permute-start(bf16[16,32,128]{2,1,0:T(8,128)(2,1)S(1)} %get-tuple-element.122.refs_0_), channel_id=1, source_target_pairs={{0,1},{1,0},{2,3},{3,2},{4,5},{5,4},{6,7},{7,6},{8,9},{9,8},{10,11... | collective-permute-start | bytes 393224 | tf_op jit(solution)/shard_map/ppermute | solution.py:109
  60.5 7.1 %collective-permute-start.24 = (bf16[8,32,128]{2,1,0:T(8,128)(2,1)S(1)}, bf16[8,32,128]{2,1,0:T(8,128)(2,1)S(1)}, u32[]{:S(2)}, u32[]{:S(2)}) collective-permute-start(bf16[8,32,128]{2,1,0:T(8,128)(2,1)S(1)} %get-tuple-element.121), channel_id=1, source_target_pairs={{0,2},{1,3},{2,0},{3,1},{4,6},{5,7},{6,4},{7,5},{8,10},{9,11},{10,... | collective-permute-start | bytes 196616 | tf_op jit(solution)/shard_map/ppermute | solution.py:108
  63.9 5.0 %collective-permute-start.23 = (bf16[8,32,128]{2,1,0:T(8,128)(2,1)S(1)}, bf16[8,32,128]{2,1,0:T(8,128)(2,1)S(1)}, u32[]{:S(2)}, u32[]{:S(2)}) collective-permute-start(bf16[8,32,128]{2,1,0:T(8,128)(2,1)S(1)} %collective-permute-done.22.refs_1_), channel_id=1, source_target_pairs={{0,1},{1,0},{2,3},{3,2},{4,5},{5,4},{6,7},{7,6},{8,9},{9,8},{10,11... | collective-permute-start | bytes 196616 | tf_op jit(solution)/shard_map/ppermute | solution.py:571
  63.9 6.2 %collective-permute-start.20 = (bf16[8,32,128]{2,1,0:T(8,128)(2,1)S(1)}, bf16[8,32,128]{2,1,0:T(8,128)(2,1)S(1)}, u32[]{:S(2)}, u32[]{:S(2)}) collective-permute-start(bf16[8,32,128]{2,1,0:T(8,128)(2,1)S(1)} %get-tuple-element.121), channel_id=1, source_target_pairs={{0,3},{1,2},{2,1},{3,0},{4,7},{5,6},{6,5},{7,4},{8,11},{9,10},{10,... | collective-permute-start | bytes 196616 | tf_op jit(solution)/shard_map/ppermute | solution.py:112
  70.4 1.8 %collective-permute-start.26 = (bf16[48,32,128]{2,1,0:T(8,128)(2,1)S(1)}, bf16[48,32,128]{2,1,0:T(8,128)(2,1)S(1)}, u32[]{:S(2)}, u32[]{:S(2)}) collective-permute-start(bf16[48,32,128]{2,1,0:T(8,128)(2,1)S(1)} %get-tuple-element.133), channel_id=1, source_target_pairs={{0,4},{4,0},{8,12},{12,8},{16,20},{20,16},{24,28},{28,24},{1,5},{5... | collective-permute-start | bytes 1179656 | tf_op jit(solution)/shard_map/ppermute | solution.py:583
  70.8 5.0 %collective-permute-start.25 = (bf16[16,32,128]{2,1,0:T(8,128)(2,1)S(1)}, bf16[16,32,128]{2,1,0:T(8,128)(2,1)S(1)}, u32[]{:S(2)}, u32[]{:S(2)}) collective-permute-start(bf16[16,32,128]{2,1,0:T(8,128)(2,1)S(1)} %get-tuple-element.131), channel_id=1, source_target_pairs={{0,4},{4,0},{8,12},{12,8},{16,20},{20,16},{24,28},{28,24},{1,5},{5... | collective-permute-start | bytes 393224 | tf_op jit(solution)/shard_map/ppermute | solution.py:583
  72.2 7.3 %collective-permute-start.27 = (bf16[16,32,128]{2,1,0:T(8,128)(2,1)S(1)}, bf16[16,32,128]{2,1,0:T(8,128)(2,1)S(1)}, u32[]{:S(2)}, u32[]{:S(2)}) collective-permute-start(bf16[16,32,128]{2,1,0:T(8,128)(2,1)S(1)} %get-tuple-element.135), channel_id=1, source_target_pairs={{0,24},{4,28},{8,16},{12,20},{16,8},{20,12},{24,0},{28,4},{1,25},{... | collective-permute-start | bytes 393224 | tf_op jit(solution)/shard_map/ppermute | solution.py:591
  73.3 8.1 %collective-permute-start.28 = (bf16[16,32,128]{2,1,0:T(8,128)(2,1)S(1)}, bf16[16,32,128]{2,1,0:T(8,128)(2,1)S(1)}, u32[]{:S(2)}, u32[]{:S(2)}) collective-permute-start(bf16[16,32,128]{2,1,0:T(8,128)(2,1)S(1)} %get-tuple-element.136), channel_id=1, source_target_pairs={{0,16},{4,20},{8,24},{12,28},{16,0},{20,4},{24,8},{28,12},{1,17},{... | collective-permute-start | bytes 393224 | tf_op jit(solution)/shard_map/ppermute | solution.py:591
  74.5 6.8 %collective-permute-start.29 = (bf16[16,32,128]{2,1,0:T(8,128)(2,1)S(1)}, bf16[16,32,128]{2,1,0:T(8,128)(2,1)S(1)}, u32[]{:S(2)}, u32[]{:S(2)}) collective-permute-start(bf16[16,32,128]{2,1,0:T(8,128)(2,1)S(1)} %get-tuple-element.134.before_ref), channel_id=1, source_target_pairs={{0,8},{4,12},{8,0},{12,4},{16,24},{20,28},{24,16},{28,20},{1,9},{5... | collective-permute-start | bytes 393224 | tf_op jit(solution)/shard_map/ppermute | solution.py:591

commit v16 on v15

--- a/solution.py
+++ b/solution.py
@@ -8,7 +8,7 @@
 from jax.sharding import PartitionSpec as P
 
 ITERS = 3
-UNROLL = 16
+UNROLL = 8
 LANES = 4
 DEPTH = 6
 HIDE_FLOPS = 20_000_000_000

time: 82.7 us -> 86.2 us (1.042)
  waiting for transfers between devices: 23.2 us -> 26 us
  starting transfers between devices: 33.9 us -> 36.1 us
  Pallas kernels: 24.8 us -> 22.6 us
    ppermute x6, starting transfers between devices: 7.42 us -> 11.3 us  [gather(): sets[step, part] = lax.ppermute(piece, 'col', ring(groups, 2 * step))]
    ppermute x3, starting transfers between devices: 5.06 us -> 1.86 us  [gather(): sets[groups // 2, 0] = lax.ppermute(whole, 'col', neighbours(groups))]
    ppermute x9, starting transfers between devices: 10.7 us -> 13 us  [per_device(): lax.ppermute(send, 'row', [(chip * CORES + core, partner(chip, shift, chi...]
    ppermute x9, waiting for transfers between devices: 14.2 us -> 16.3 us  [per_device(): lax.ppermute(send, 'row', [(chip * CORES + core, partner(chip, shift, chi...]
    ppermute x3, starting transfers between devices: 8.54 us -> 6.87 us  [gather(): lax.ppermute(rounded[-1], 'col', across)]
    ppermute x3, starting transfers between devices: 0.42 us -> 1.54 us  [forward(): lax.ppermute(sets[index, part], 'col', neighbours(groups))]
    pallas_call x3, Pallas kernels: 6.16 us -> 5.05 us  [product_first(): pl.pallas_call(functools.partial(first_kernel, len(pieces), len(outs) //...]
    ppermute x3, waiting for transfers between devices: 0.98 us -> 1.92 us  [forward(): lax.ppermute(sets[index, part], 'col', neighbours(groups))]
  transfers between devices with their start and end apart: 30 -> 30, of which waited for: 15 -> 17; matrix products, arithmetic and copies ran while one was open for 0% -> 0% of each run, Pallas kernels for 23% -> 20%
where the time goes in v16:
time: 86.2 us; the launch traced here: 85.5 us
  starting transfers between devices  36.1 us (42%)
  waiting for transfers between devices  26 us (30%)
  Pallas kernels  22.6 us (26%)
  between operations  0.9 us (1%)
    ppermute x9, waiting for transfers between devices, per_device(): lax.ppermute(send, 'row', [(chip * CORES + core, partner(chip, shift, chi...  16.3 us
    ppermute x9, starting transfers between devices, per_device(): lax.ppermute(send, 'row', [(chip * CORES + core, partner(chip, shift, chi...  13 us
    ppermute x6, starting transfers between devices, gather(): sets[step, part] = lax.ppermute(piece, 'col', ring(groups, 2 * step))  11.3 us
    ppermute x3, starting transfers between devices, gather(): lax.ppermute(rounded[-1], 'col', across)  6.87 us
    pallas_call x6, Pallas kernels, product_stage(): pl.pallas_call(functools.partial(stage_kernel, stage, bits, dims, len(pie...  5.12 us
    pallas_call x3, Pallas kernels, product_first(): pl.pallas_call(functools.partial(first_kernel, len(pieces), len(outs) //...  5.05 us
    ppermute x6, waiting for transfers between devices, gather(): sets[step, part] = lax.ppermute(piece, 'col', ring(groups, 2 * step))  4.49 us
    pallas_call x1, Pallas kernels, per_device(): pl.pallas_call(functools.partial(order_kernel, group, owned, groups, part...  2.82 us
  transfers between devices with their start and end apart: 30, of which 17 were waited for; matrix products, arithmetic and copies ran while one was open for 0% of the time, Pallas kernels for 20%

profile of v16, /device:TPU:0, one launch (start us, length us, event | category | flops | bytes accessed | tf_op | source)
XLA Modules:
  0.0 85.5 jit_solution(106848337934741364)
XLA Ops:
  0.0 2.2 %start.1 = (bf16[16,128,128]{2,1,0:T(8,128)(2,1)S(1)}, bf16[16,128,128]{2,1,0:T(8,128)(2,1)S(1)}, f32[16,32,128]{2,1,0:T(8,128)S(1)}, f32[16,32,128]{2,1,0:T(8,1...) custom-call(f32[16,128,128]{2,1,0:T(8,128)} %bitcast.5, ...), custom_call_target="tpu_custom_call" | custom-call | tf_op jit(solution)/shard_map/start/pallas_call | solution.py:418
  2.2 4.1 %collective-permute-start.2 = (bf16[8,32,128]{2,1,0:T(8,128)(2,1)S(1)}, bf16[8,32,128]{2,1,0:T(8,128)(2,1)S(1)}, u32[]{:S(2)}, u32[]{:S(2)}) collective-permute-start(bf16[8,32,128]{2,1,0:T(8,128)(2,1)S(1)} %get-tuple-element.80), channel_id=1, source_target_pairs={{0,2},{1,3},{2,0},{3,1},{4,6},{5,7},{6,4},{7,5},{8,10},{9,11},{10,... | collective-permute-start | bytes 196616 | tf_op jit(solution)/shard_map/ppermute | solution.py:108
  6.3 1.6 %collective-permute-start.1 = (bf16[16,32,128]{2,1,0:T(8,128)(2,1)S(1)}, bf16[16,32,128]{2,1,0:T(8,128)(2,1)S(1)}, u32[]{:S(2)}, u32[]{:S(2)}) collective-permute-start(bf16[16,32,128]{2,1,0:T(8,128)(2,1)S(1)} %get-tuple-element.79.refs_0_), channel_id=1, source_target_pairs={{0,1},{1,0},{2,3},{3,2},{4,5},{5,4},{6,7},{7,6},{8,9},{9,8},{10,11... | collective-permute-start | bytes 393224 | tf_op jit(solution)/shard_map/ppermute | solution.py:109
  8.8 2.8 %order.1 = (s32[9,200]{1,0:T(8,128)S(4)}, s32[8]{0:T(128)S(4)}, bf16[192,128,128]{2,1,0:T(8,128)(2,1)S(1)}, f32[8,128]{1,0:T(8,128)S(1)}) custom-call(s32[1,1]{1,0:T(1,128)S(6)} %copy.63.count_ref, s32[1,1,192]{2,1,0:T(1,128)} %rows_hbm.1, s32[1,1,192]{2,1,0:T(1,128)} %cols_hbm.1, bf16[192,128,128]{2,1,0:T(8,128)(2,1)} %bitcast.4), custom_call_target="tpu_custom_call" | custom-call | tf_op jit(solution)/shard_map/order/pallas_call | solution.py:431
  12.3 3.6 %collective-permute-start = (bf16[8,32,128]{2,1,0:T(8,128)(2,1)S(1)}, bf16[8,32,128]{2,1,0:T(8,128)(2,1)S(1)}, u32[]{:S(2)}, u32[]{:S(2)}) collective-permute-start(bf16[8,32,128]{2,1,0:T(8,128)(2,1)S(1)} %get-tuple-element.78), channel_id=1, source_target_pairs={{0,3},{1,2},{2,1},{3,0},{4,7},{5,6},{6,5},{7,4},{8,11},{9,10},{10,... | collective-permute-start | bytes 196616 | tf_op jit(solution)/shard_map/ppermute | solution.py:112
  15.9 1.8 %stage0.3 = (f32[65,32,128]{2,1,0:T(8,128)S(1)}, f32[65,32,128]{2,1,0:T(8,128)S(1)}, f32[8,128]{1,0:T(8,128)}) custom-call(s32[9,200]{1,0:T(8,128)S(4)} %get-tuple-element.77.list_ref, s32[8]{0:T(128)S(4)} %get-tuple-element.75.total_ref, bf16[192,128,128]{2,1,0:T(8,128)(2,1)S(1)} %get-tuple-element.76.values_ref, ...), custom_call_target="tpu_custom_call" | custom-call | flops 75497472 | bytes 2359296 | tf_op jit(solution)/shard_map/stage0/pallas_call | solution.py:473
  18.5 1.3 %stage2.3 = (f32[65,32,128]{2,1,0:T(8,128)S(1)}, f32[65,32,128]{2,1,0:T(8,128)S(1)}) custom-call(s32[9,200]{1,0:T(8,128)S(4)} %get-tuple-element.77.list_ref, s32[8]{0:T(128)S(4)} %get-tuple-element.75.total_ref, bf16[192,128,128]{2,1,0:T(8,128)(2,1)S(1)} %get-tuple-element.76.values_ref, ...), custom_call_target="tpu_custom_call", output_to_operand_aliasing={{0}: (5, {}), {1}: (6, {})} | custom-call | flops 75497472 | bytes 2359296 | tf_op jit(solution)/shard_map/stage2/pallas_call | solution.py:486
  22.2 5.0 %collective-permute-start.7 = (bf16[16,32,128]{2,1,0:T(8,128)(2,1)S(1)}, bf16[16,32,128]{2,1,0:T(8,128)(2,1)S(1)}, u32[]{:S(2)}, u32[]{:S(2)}) collective-permute-start(bf16[16,32,128]{2,1,0:T(8,128)(2,1)S(1)} %get-tuple-element.94.refs_6_.refs_10_), channel_id=1, source_target_pairs={{0,24},{4,28},{8,16},{12,20},{16,8},{20,12},{24,0},{28,4},{1,25},{... | collective-permute-start | bytes 393224 | tf_op jit(solution)/shard_map/ppermute | solution.py:591
  27.9 1.9 %turn.1 = (bf16[192,128,128]{2,1,0:T(8,128)(2,1)S(1)}, f32[16,32,128]{2,1,0:T(8,128)S(1)}) custom-call(s32[8]{0:T(128)S(4)} %get-tuple-element.75.total_ref, bf16[192,128,128]{2,1,0:T(8,128)(2,1)S(1)} %get-tuple-element.76.values_ref, f32[16,32,128]{2,1,0:T(8,128)S(1)} %combine1.3.base_ref), custom_call_target="tpu_custom_call", output_to_operand_aliasing={{1}: (2, {})} | custom-call | flops 20000000000 | tf_op jit(solution)/shard_map/turn/pallas_call | solution.py:453
  29.8 1.3 %collective-permute-done.7.refs_0_ = bf16[16,32,128]{2,1,0:T(8,128)(2,1)S(1)} collective-permute-done((bf16[16,32,128]{2,1,0:T(8,128)(2,1)S(1)}, bf16[16,32,128]{2,1,0:T(8,128)(2,1)S(1)}, u32[]{:S(2)}, u32[]{:S(2)}) %collective-permute-start.7) | collective-permute-done | bytes 131104 | tf_op jit(solution)/shard_map/ppermute | solution.py:591
  31.1 2.7 %collective-permute-done.8.refs_1_ = bf16[16,32,128]{2,1,0:T(8,128)(2,1)S(1)} collective-permute-done((bf16[16,32,128]{2,1,0:T(8,128)(2,1)S(1)}, bf16[16,32,128]{2,1,0:T(8,128)(2,1)S(1)}, u32[]{:S(2)}, u32[]{:S(2)}) %collective-permute-start.8) | collective-permute-done | bytes 131104 | tf_op jit(solution)/shard_map/ppermute | solution.py:591
  34.9 2.7 %collective-permute-start.14 = (bf16[8,32,128]{2,1,0:T(8,128)(2,1)S(1)}, bf16[8,32,128]{2,1,0:T(8,128)(2,1)S(1)}, u32[]{:S(2)}, u32[]{:S(2)}) collective-permute-start(bf16[8,32,128]{2,1,0:T(8,128)(2,1)S(1)} %get-tuple-element.102), channel_id=1, source_target_pairs={{0,2},{1,3},{2,0},{3,1},{4,6},{5,7},{6,4},{7,5},{8,10},{9,11},{10,... | collective-permute-start | bytes 196616 | tf_op jit(solution)/shard_map/ppermute | solution.py:108
  37.6 2.8 %collective-permute-done.12.refs_1_ = bf16[8,32,128]{2,1,0:T(8,128)(2,1)S(1)} collective-permute-done((bf16[8,32,128]{2,1,0:T(8,128)(2,1)S(1)}, bf16[8,32,128]{2,1,0:T(8,128)(2,1)S(1)}, u32[]{:S(2)}, u32[]{:S(2)}) %collective-permute-start.12) | collective-permute-done | bytes 65568 | tf_op jit(solution)/shard_map/ppermute | solution.py:108
  40.5 1.0 %collective-permute-start.10 = (bf16[8,32,128]{2,1,0:T(8,128)(2,1)S(1)}, bf16[8,32,128]{2,1,0:T(8,128)(2,1)S(1)}, u32[]{:S(2)}, u32[]{:S(2)}) collective-permute-start(bf16[8,32,128]{2,1,0:T(8,128)(2,1)S(1)} %get-tuple-element.102), channel_id=1, source_target_pairs={{0,3},{1,2},{2,1},{3,0},{4,7},{5,6},{6,5},{7,4},{8,11},{9,10},{10,... | collective-permute-start | bytes 196616 | tf_op jit(solution)/shard_map/ppermute | solution.py:112
  41.5 1.6 %stage0.4 = (f32[65,32,128]{2,1,0:T(8,128)S(1)}, f32[65,32,128]{2,1,0:T(8,128)S(1)}, f32[8,128]{1,0:T(8,128)}) custom-call(s32[9,200]{1,0:T(8,128)S(4)} %get-tuple-element.77.list_ref, s32[8]{0:T(128)S(4)} %get-tuple-element.75.total_ref, bf16[192,128,128]{2,1,0:T(8,128)(2,1)S(1)} %get-tuple-element.101.values_ref, ...), custom_call_target="tpu_custom_call" | custom-call | flops 75497472 | bytes 2359296 | tf_op jit(solution)/shard_map/stage0/pallas_call | solution.py:473
  43.6 1.8 %collective-permute-done.13.refs_1_ = bf16[8,32,128]{2,1,0:T(8,128)(2,1)S(1)} collective-permute-done((bf16[8,32,128]{2,1,0:T(8,128)(2,1)S(1)}, bf16[8,32,128]{2,1,0:T(8,128)(2,1)S(1)}, u32[]{:S(2)}, u32[]{:S(2)}) %collective-permute-start.13) | collective-permute-done | bytes 65568 | tf_op jit(solution)/shard_map/ppermute | solution.py:571
  45.4 1.0 %stage2.4 = (f32[65,32,128]{2,1,0:T(8,128)S(1)}, f32[65,32,128]{2,1,0:T(8,128)S(1)}) custom-call(s32[9,200]{1,0:T(8,128)S(4)} %get-tuple-element.77.list_ref, s32[8]{0:T(128)S(4)} %get-tuple-element.75.total_ref, bf16[192,128,128]{2,1,0:T(8,128)(2,1)S(1)} %get-tuple-element.101.values_ref, ...), custom_call_target="tpu_custom_call", output_to_operand_aliasing={{0}: (5, {}), {1}: (6, {})} | custom-call | flops 75497472 | bytes 2359296 | tf_op jit(solution)/shard_map/stage2/pallas_call | solution.py:486
  47.7 0.9 %collective-permute-done.16.first_ref.refs_8_ = bf16[48,32,128]{2,1,0:T(8,128)(2,1)S(1)} collective-permute-done((bf16[48,32,128]{2,1,0:T(8,128)(2,1)S(1)}, bf16[48,32,128]{2,1,0:T(8,128)(2,1)S(1)}, u32[]{:S(2)}, u32[]{:S(2)}) %collective-permute-start.16) | collective-permute-done | bytes 393248 | tf_op jit(solution)/shard_map/ppermute | solution.py:583
  48.8 2.1 %collective-permute-start.17 = (bf16[16,32,128]{2,1,0:T(8,128)(2,1)S(1)}, bf16[16,32,128]{2,1,0:T(8,128)(2,1)S(1)}, u32[]{:S(2)}, u32[]{:S(2)}) collective-permute-start(bf16[16,32,128]{2,1,0:T(8,128)(2,1)S(1)} %get-tuple-element.115.refs_13_), channel_id=1, source_target_pairs={{0,24},{4,28},{8,16},{12,20},{16,8},{20,12},{24,0},{28,4},{1,25},{... | collective-permute-start | bytes 393224 | tf_op jit(solution)/shard_map/ppermute | solution.py:591
  50.8 1.0 %collective-permute-start.18 = (bf16[16,32,128]{2,1,0:T(8,128)(2,1)S(1)}, bf16[16,32,128]{2,1,0:T(8,128)(2,1)S(1)}, u32[]{:S(2)}, u32[]{:S(2)}) collective-permute-start(bf16[16,32,128]{2,1,0:T(8,128)(2,1)S(1)} %get-tuple-element.116.refs_14_), channel_id=1, source_target_pairs={{0,16},{4,20},{8,24},{12,28},{16,0},{20,4},{24,8},{28,12},{1,17},{... | collective-permute-start | bytes 393224 | tf_op jit(solution)/shard_map/ppermute | solution.py:591
  52.4 3.7 %collective-permute-done.17.refs_0_ = bf16[16,32,128]{2,1,0:T(8,128)(2,1)S(1)} collective-permute-done((bf16[16,32,128]{2,1,0:T(8,128)(2,1)S(1)}, bf16[16,32,128]{2,1,0:T(8,128)(2,1)S(1)}, u32[]{:S(2)}, u32[]{:S(2)}) %collective-permute-start.17) | collective-permute-done | bytes 131104 | tf_op jit(solution)/shard_map/ppermute | solution.py:591
  56.1 2.0 %collective-permute-done.18.refs_1_ = bf16[16,32,128]{2,1,0:T(8,128)(2,1)S(1)} collective-permute-done((bf16[16,32,128]{2,1,0:T(8,128)(2,1)S(1)}, bf16[16,32,128]{2,1,0:T(8,128)(2,1)S(1)}, u32[]{:S(2)}, u32[]{:S(2)}) %collective-permute-start.18) | collective-permute-done | bytes 131104 | tf_op jit(solution)/shard_map/ppermute | solution.py:591
  58.7 2.0 %collective-permute-start.22 = (bf16[8,32,128]{2,1,0:T(8,128)(2,1)S(1)}, bf16[8,32,128]{2,1,0:T(8,128)(2,1)S(1)}, u32[]{:S(2)}, u32[]{:S(2)}) collective-permute-start(bf16[8,32,128]{2,1,0:T(8,128)(2,1)S(1)} %get-tuple-element.119.refs_3_), channel_id=1, source_target_pairs={{0,2},{1,3},{2,0},{3,1},{4,6},{5,7},{6,4},{7,5},{8,10},{9,11},{10,... | collective-permute-start | bytes 196616 | tf_op jit(solution)/shard_map/ppermute | solution.py:108
  61.1 2.1 %collective-permute-start.24 = (bf16[8,32,128]{2,1,0:T(8,128)(2,1)S(1)}, bf16[8,32,128]{2,1,0:T(8,128)(2,1)S(1)}, u32[]{:S(2)}, u32[]{:S(2)}) collective-permute-start(bf16[8,32,128]{2,1,0:T(8,128)(2,1)S(1)} %get-tuple-element.121), channel_id=1, source_target_pairs={{0,2},{1,3},{2,0},{3,1},{4,6},{5,7},{6,4},{7,5},{8,10},{9,11},{10,... | collective-permute-start | bytes 196616 | tf_op jit(solution)/shard_map/ppermute | solution.py:108
  63.2 1.6 %collective-permute-done.22.refs_1_ = bf16[8,32,128]{2,1,0:T(8,128)(2,1)S(1)} collective-permute-done((bf16[8,32,128]{2,1,0:T(8,128)(2,1)S(1)}, bf16[8,32,128]{2,1,0:T(8,128)(2,1)S(1)}, u32[]{:S(2)}, u32[]{:S(2)}) %collective-permute-start.22) | collective-permute-done | bytes 65568 | tf_op jit(solution)/shard_map/ppermute | solution.py:108
  65.8 2.3 %collective-permute-start.20 = (bf16[8,32,128]{2,1,0:T(8,128)(2,1)S(1)}, bf16[8,32,128]{2,1,0:T(8,128)(2,1)S(1)}, u32[]{:S(2)}, u32[]{:S(2)}) collective-permute-start(bf16[8,32,128]{2,1,0:T(8,128)(2,1)S(1)} %get-tuple-element.121), channel_id=1, source_target_pairs={{0,3},{1,2},{2,1},{3,0},{4,7},{5,6},{6,5},{7,4},{8,11},{9,10},{10,... | collective-permute-start | bytes 196616 | tf_op jit(solution)/shard_map/ppermute | solution.py:112
  68.0 1.7 %stage0.5 = (f32[65,32,128]{2,1,0:T(8,128)S(1)}, f32[65,32,128]{2,1,0:T(8,128)S(1)}, f32[8,128]{1,0:T(8,128)}) custom-call(s32[9,200]{1,0:T(8,128)S(4)} %get-tuple-element.77.list_ref, s32[8]{0:T(128)S(4)} %get-tuple-element.75.total_ref, bf16[192,128,128]{2,1,0:T(8,128)(2,1)S(1)} %get-tuple-element.101.values_ref, ...), custom_call_target="tpu_custom_call" | custom-call | flops 75497472 | bytes 2359296 | tf_op jit(solution)/shard_map/stage0/pallas_call | solution.py:473
  70.5 1.0 %stage2.5 = (f32[65,32,128]{2,1,0:T(8,128)S(1)}, f32[65,32,128]{2,1,0:T(8,128)S(1)}) custom-call(s32[9,200]{1,0:T(8,128)S(4)} %get-tuple-element.77.list_ref, s32[8]{0:T(128)S(4)} %get-tuple-element.75.total_ref, bf16[192,128,128]{2,1,0:T(8,128)(2,1)S(1)} %get-tuple-element.101.values_ref, ...), custom_call_target="tpu_custom_call", output_to_operand_aliasing={{0}: (5, {}), {1}: (6, {})} | custom-call | flops 75497472 | bytes 2359296 | tf_op jit(solution)/shard_map/stage2/pallas_call | solution.py:486
  73.9 3.1 %collective-permute-start.27 = (bf16[16,32,128]{2,1,0:T(8,128)(2,1)S(1)}, bf16[16,32,128]{2,1,0:T(8,128)(2,1)S(1)}, u32[]{:S(2)}, u32[]{:S(2)}) collective-permute-start(bf16[16,32,128]{2,1,0:T(8,128)(2,1)S(1)} %get-tuple-element.135), channel_id=1, source_target_pairs={{0,24},{4,28},{8,16},{12,20},{16,8},{20,12},{24,0},{28,4},{1,25},{... | collective-permute-start | bytes 393224 | tf_op jit(solution)/shard_map/ppermute | solution.py:591
  77.8 3.2 %collective-permute-done.27.refs_0_ = bf16[16,32,128]{2,1,0:T(8,128)(2,1)S(1)} collective-permute-done((bf16[16,32,128]{2,1,0:T(8,128)(2,1)S(1)}, bf16[16,32,128]{2,1,0:T(8,128)(2,1)S(1)}, u32[]{:S(2)}, u32[]{:S(2)}) %collective-permute-start.27) | collective-permute-done | bytes 131104 | tf_op jit(solution)/shard_map/ppermute | solution.py:591
  81.0 2.7 %collective-permute-done.28.refs_1_ = bf16[16,32,128]{2,1,0:T(8,128)(2,1)S(1)} collective-permute-done((bf16[16,32,128]{2,1,0:T(8,128)(2,1)S(1)}, bf16[16,32,128]{2,1,0:T(8,128)(2,1)S(1)}, u32[]{:S(2)}, u32[]{:S(2)}) %collective-permute-start.28) | collective-permute-done | bytes 131104 | tf_op jit(solution)/shard_map/ppermute | solution.py:591
  84.1 1.4 %finish.1 = f32[16,32,128]{2,1,0:T(8,128)} custom-call(bf16[16,128,128]{2,1,0:T(8,128)(2,1)S(1)} %get-tuple-element.71.high_ref, bf16[16,128,128]{2,1,0:T(8,128)(2,1)S(1)} %get-tuple-element.72.low_ref, f32[16,32,128]{2,1,0:T(8,128)S(1)} %get-tuple-element.120.sol_ref, f32[16,32,128]{2,1,0:T(8,128)S(1)} %combine1.5.base_ref, ...), custom_call_target="tpu_custom_call" | custom-call | tf_op jit(solution)/shard_map/finish/pallas_call | solution.py:606
  (58 shorter events, 14.9 us)
Async XLA Ops:
  2.2 9.5 %collective-permute-start.2 = (bf16[8,32,128]{2,1,0:T(8,128)(2,1)S(1)}, bf16[8,32,128]{2,1,0:T(8,128)(2,1)S(1)}, u32[]{:S(2)}, u32[]{:S(2)}) collective-permute-start(bf16[8,32,128]{2,1,0:T(8,128)(2,1)S(1)} %get-tuple-element.80), channel_id=1, source_target_pairs={{0,2},{1,3},{2,0},{3,1},{4,6},{5,7},{6,4},{7,5},{8,10},{9,11},{10,... | collective-permute-start | bytes 196616 | tf_op jit(solution)/shard_map/ppermute | solution.py:108
  6.3 12.2 %collective-permute-start.1 = (bf16[16,32,128]{2,1,0:T(8,128)(2,1)S(1)}, bf16[16,32,128]{2,1,0:T(8,128)(2,1)S(1)}, u32[]{:S(2)}, u32[]{:S(2)}) collective-permute-start(bf16[16,32,128]{2,1,0:T(8,128)(2,1)S(1)} %get-tuple-element.79.refs_0_), channel_id=1, source_target_pairs={{0,1},{1,0},{2,3},{3,2},{4,5},{5,4},{6,7},{7,6},{8,9},{9,8},{10,11... | collective-permute-start | bytes 393224 | tf_op jit(solution)/shard_map/ppermute | solution.py:109
  7.8 9.9 %collective-permute-start.4 = (bf16[8,32,128]{2,1,0:T(8,128)(2,1)S(1)}, bf16[8,32,128]{2,1,0:T(8,128)(2,1)S(1)}, u32[]{:S(2)}, u32[]{:S(2)}) collective-permute-start(bf16[8,32,128]{2,1,0:T(8,128)(2,1)S(1)} %get-tuple-element.78), channel_id=1, source_target_pairs={{0,2},{1,3},{2,0},{3,1},{4,6},{5,7},{6,4},{7,5},{8,10},{9,11},{10,... | collective-permute-start | bytes 196616 | tf_op jit(solution)/shard_map/ppermute | solution.py:108
  11.7 6.8 %collective-permute-start.3 = (bf16[8,32,128]{2,1,0:T(8,128)(2,1)S(1)}, bf16[8,32,128]{2,1,0:T(8,128)(2,1)S(1)}, u32[]{:S(2)}, u32[]{:S(2)}) collective-permute-start(bf16[8,32,128]{2,1,0:T(8,128)(2,1)S(1)} %hold.1.refs_1_), channel_id=1, source_target_pairs={{0,1},{1,0},{2,3},{3,2},{4,5},{5,4},{6,7},{7,6},{8,9},{9,8},{10,11... | collective-permute-start | bytes 196616 | tf_op jit(solution)/shard_map/ppermute | solution.py:571
  12.3 7.5 %collective-permute-start = (bf16[8,32,128]{2,1,0:T(8,128)(2,1)S(1)}, bf16[8,32,128]{2,1,0:T(8,128)(2,1)S(1)}, u32[]{:S(2)}, u32[]{:S(2)}) collective-permute-start(bf16[8,32,128]{2,1,0:T(8,128)(2,1)S(1)} %get-tuple-element.78), channel_id=1, source_target_pairs={{0,3},{1,2},{2,1},{3,0},{4,7},{5,6},{6,5},{7,4},{8,11},{9,10},{10,... | collective-permute-start | bytes 196616 | tf_op jit(solution)/shard_map/ppermute | solution.py:112
  20.1 2.0 %collective-permute-start.6 = (bf16[48,32,128]{2,1,0:T(8,128)(2,1)S(1)}, bf16[48,32,128]{2,1,0:T(8,128)(2,1)S(1)}, u32[]{:S(2)}, u32[]{:S(2)}) collective-permute-start(bf16[48,32,128]{2,1,0:T(8,128)(2,1)S(1)} %get-tuple-element.91.refs_2_), channel_id=1, source_target_pairs={{0,4},{4,0},{8,12},{12,8},{16,20},{20,16},{24,28},{28,24},{1,5},{5... | collective-permute-start | bytes 1179656 | tf_op jit(solution)/shard_map/ppermute | solution.py:583
  21.3 6.5 %collective-permute-start.5 = (bf16[16,32,128]{2,1,0:T(8,128)(2,1)S(1)}, bf16[16,32,128]{2,1,0:T(8,128)(2,1)S(1)}, u32[]{:S(2)}, u32[]{:S(2)}) collective-permute-start(bf16[16,32,128]{2,1,0:T(8,128)(2,1)S(1)} %get-tuple-element.90.refs_3_), channel_id=1, source_target_pairs={{0,4},{4,0},{8,12},{12,8},{16,20},{20,16},{24,28},{28,24},{1,5},{5... | collective-permute-start | bytes 393224 | tf_op jit(solution)/shard_map/ppermute | solution.py:583
  22.2 8.9 %collective-permute-start.7 = (bf16[16,32,128]{2,1,0:T(8,128)(2,1)S(1)}, bf16[16,32,128]{2,1,0:T(8,128)(2,1)S(1)}, u32[]{:S(2)}, u32[]{:S(2)}) collective-permute-start(bf16[16,32,128]{2,1,0:T(8,128)(2,1)S(1)} %get-tuple-element.94.refs_6_.refs_10_), channel_id=1, source_target_pairs={{0,24},{4,28},{8,16},{12,20},{16,8},{20,12},{24,0},{28,4},{1,25},{... | collective-permute-start | bytes 393224 | tf_op jit(solution)/shard_map/ppermute | solution.py:591
  27.2 6.6 %collective-permute-start.8 = (bf16[16,32,128]{2,1,0:T(8,128)(2,1)S(1)}, bf16[16,32,128]{2,1,0:T(8,128)(2,1)S(1)}, u32[]{:S(2)}, u32[]{:S(2)}) collective-permute-start(bf16[16,32,128]{2,1,0:T(8,128)(2,1)S(1)} %get-tuple-element.95.refs_7_.refs_11_), channel_id=1, source_target_pairs={{0,16},{4,20},{8,24},{12,28},{16,0},{20,4},{24,8},{28,12},{1,17},{... | collective-permute-start | bytes 393224 | tf_op jit(solution)/shard_map/ppermute | solution.py:591
  27.2 6.6 %collective-permute-start.9 = (bf16[16,32,128]{2,1,0:T(8,128)(2,1)S(1)}, bf16[16,32,128]{2,1,0:T(8,128)(2,1)S(1)}, u32[]{:S(2)}, u32[]{:S(2)}) collective-permute-start(bf16[16,32,128]{2,1,0:T(8,128)(2,1)S(1)} %get-tuple-element.92.before_ref.refs_8_.refs_12_), channel_id=1, source_target_pairs={{0,8},{4,12},{8,0},{12,4},{16,24},{20,28},{24,16},{28,20},{1,9},{5... | collective-permute-start | bytes 393224 | tf_op jit(solution)/shard_map/ppermute | solution.py:591
  34.2 6.3 %collective-permute-start.12 = (bf16[8,32,128]{2,1,0:T(8,128)(2,1)S(1)}, bf16[8,32,128]{2,1,0:T(8,128)(2,1)S(1)}, u32[]{:S(2)}, u32[]{:S(2)}) collective-permute-start(bf16[8,32,128]{2,1,0:T(8,128)(2,1)S(1)} %get-tuple-element.98.refs_3_), channel_id=1, source_target_pairs={{0,2},{1,3},{2,0},{3,1},{4,6},{5,7},{6,4},{7,5},{8,10},{9,11},{10,... | collective-permute-start | bytes 196616 | tf_op jit(solution)/shard_map/ppermute | solution.py:108
  34.6 10.8 %collective-permute-start.11 = (bf16[16,32,128]{2,1,0:T(8,128)(2,1)S(1)}, bf16[16,32,128]{2,1,0:T(8,128)(2,1)S(1)}, u32[]{:S(2)}, u32[]{:S(2)}) collective-permute-start(bf16[16,32,128]{2,1,0:T(8,128)(2,1)S(1)} %get-tuple-element.103.refs_0_), channel_id=1, source_target_pairs={{0,1},{1,0},{2,3},{3,2},{4,5},{5,4},{6,7},{7,6},{8,9},{9,8},{10,11... | collective-permute-start | bytes 393224 | tf_op jit(solution)/shard_map/ppermute | solution.py:109
  34.9 8.2 %collective-permute-start.14 = (bf16[8,32,128]{2,1,0:T(8,128)(2,1)S(1)}, bf16[8,32,128]{2,1,0:T(8,128)(2,1)S(1)}, u32[]{:S(2)}, u32[]{:S(2)}) collective-permute-start(bf16[8,32,128]{2,1,0:T(8,128)(2,1)S(1)} %get-tuple-element.102), channel_id=1, source_target_pairs={{0,2},{1,3},{2,0},{3,1},{4,6},{5,7},{6,4},{7,5},{8,10},{9,11},{10,... | collective-permute-start | bytes 196616 | tf_op jit(solution)/shard_map/ppermute | solution.py:108
  40.5 4.9 %collective-permute-start.13 = (bf16[8,32,128]{2,1,0:T(8,128)(2,1)S(1)}, bf16[8,32,128]{2,1,0:T(8,128)(2,1)S(1)}, u32[]{:S(2)}, u32[]{:S(2)}) collective-permute-start(bf16[8,32,128]{2,1,0:T(8,128)(2,1)S(1)} %collective-permute-done.12.refs_1_), channel_id=1, source_target_pairs={{0,1},{1,0},{2,3},{3,2},{4,5},{5,4},{6,7},{7,6},{8,9},{9,8},{10,11... | collective-permute-start | bytes 196616 | tf_op jit(solution)/shard_map/ppermute | solution.py:571
  40.5 6.2 %collective-permute-start.10 = (bf16[8,32,128]{2,1,0:T(8,128)(2,1)S(1)}, bf16[8,32,128]{2,1,0:T(8,128)(2,1)S(1)}, u32[]{:S(2)}, u32[]{:S(2)}) collective-permute-start(bf16[8,32,128]{2,1,0:T(8,128)(2,1)S(1)} %get-tuple-element.102), channel_id=1, source_target_pairs={{0,3},{1,2},{2,1},{3,0},{4,7},{5,6},{6,5},{7,4},{8,11},{9,10},{10,... | collective-permute-start | bytes 196616 | tf_op jit(solution)/shard_map/ppermute | solution.py:112
  46.9 1.8 %collective-permute-start.16 = (bf16[48,32,128]{2,1,0:T(8,128)(2,1)S(1)}, bf16[48,32,128]{2,1,0:T(8,128)(2,1)S(1)}, u32[]{:S(2)}, u32[]{:S(2)}) collective-permute-start(bf16[48,32,128]{2,1,0:T(8,128)(2,1)S(1)} %get-tuple-element.113.refs_4_), channel_id=1, source_target_pairs={{0,4},{4,0},{8,12},{12,8},{16,20},{20,16},{24,28},{28,24},{1,5},{5... | collective-permute-start | bytes 1179656 | tf_op jit(solution)/shard_map/ppermute | solution.py:583
  47.4 4.9 %collective-permute-start.15 = (bf16[16,32,128]{2,1,0:T(8,128)(2,1)S(1)}, bf16[16,32,128]{2,1,0:T(8,128)(2,1)S(1)}, u32[]{:S(2)}, u32[]{:S(2)}) collective-permute-start(bf16[16,32,128]{2,1,0:T(8,128)(2,1)S(1)} %get-tuple-element.112.refs_5_), channel_id=1, source_target_pairs={{0,4},{4,0},{8,12},{12,8},{16,20},{20,16},{24,28},{28,24},{1,5},{5... | collective-permute-start | bytes 393224 | tf_op jit(solution)/shard_map/ppermute | solution.py:583
  48.8 7.3 %collective-permute-start.17 = (bf16[16,32,128]{2,1,0:T(8,128)(2,1)S(1)}, bf16[16,32,128]{2,1,0:T(8,128)(2,1)S(1)}, u32[]{:S(2)}, u32[]{:S(2)}) collective-permute-start(bf16[16,32,128]{2,1,0:T(8,128)(2,1)S(1)} %get-tuple-element.115.refs_13_), channel_id=1, source_target_pairs={{0,24},{4,28},{8,16},{12,20},{16,8},{20,12},{24,0},{28,4},{1,25},{... | collective-permute-start | bytes 393224 | tf_op jit(solution)/shard_map/ppermute | solution.py:591
  50.8 7.2 %collective-permute-start.18 = (bf16[16,32,128]{2,1,0:T(8,128)(2,1)S(1)}, bf16[16,32,128]{2,1,0:T(8,128)(2,1)S(1)}, u32[]{:S(2)}, u32[]{:S(2)}) collective-permute-start(bf16[16,32,128]{2,1,0:T(8,128)(2,1)S(1)} %get-tuple-element.116.refs_14_), channel_id=1, source_target_pairs={{0,16},{4,20},{8,24},{12,28},{16,0},{20,4},{24,8},{28,12},{1,17},{... | collective-permute-start | bytes 393224 | tf_op jit(solution)/shard_map/ppermute | solution.py:591
  51.8 6.6 %collective-permute-start.19 = (bf16[16,32,128]{2,1,0:T(8,128)(2,1)S(1)}, bf16[16,32,128]{2,1,0:T(8,128)(2,1)S(1)}, u32[]{:S(2)}, u32[]{:S(2)}) collective-permute-start(bf16[16,32,128]{2,1,0:T(8,128)(2,1)S(1)} %get-tuple-element.114.before_ref.refs_15_), channel_id=1, source_target_pairs={{0,8},{4,12},{8,0},{12,4},{16,24},{20,28},{24,16},{28,20},{1,9},{5... | collective-permute-start | bytes 393224 | tf_op jit(solution)/shard_map/ppermute | solution.py:591
  58.7 6.1 %collective-permute-start.22 = (bf16[8,32,128]{2,1,0:T(8,128)(2,1)S(1)}, bf16[8,32,128]{2,1,0:T(8,128)(2,1)S(1)}, u32[]{:S(2)}, u32[]{:S(2)}) collective-permute-start(bf16[8,32,128]{2,1,0:T(8,128)(2,1)S(1)} %get-tuple-element.119.refs_3_), channel_id=1, source_target_pairs={{0,2},{1,3},{2,0},{3,1},{4,6},{5,7},{6,4},{7,5},{8,10},{9,11},{10,... | collective-permute-start | bytes 196616 | tf_op jit(solution)/shard_map/ppermute | solution.py:108
  61.1 9.2 %collective-permute-start.21 = (bf16[16,32,128]{2,1,0:T(8,128)(2,1)S(1)}, bf16[16,32,128]{2,1,0:T(8,128)(2,1)S(1)}, u32[]{:S(2)}, u32[]{:S(2)}) collective-permute-start(bf16[16,32,128]{2,1,0:T(8,128)(2,1)S(1)} %get-tuple-element.122.refs_0_), channel_id=1, source_target_pairs={{0,1},{1,0},{2,3},{3,2},{4,5},{5,4},{6,7},{7,6},{8,9},{9,8},{10,11... | collective-permute-start | bytes 393224 | tf_op jit(solution)/shard_map/ppermute | solution.py:109
  61.1 8.6 %collective-permute-start.24 = (bf16[8,32,128]{2,1,0:T(8,128)(2,1)S(1)}, bf16[8,32,128]{2,1,0:T(8,128)(2,1)S(1)}, u32[]{:S(2)}, u32[]{:S(2)}) collective-permute-start(bf16[8,32,128]{2,1,0:T(8,128)(2,1)S(1)} %get-tuple-element.121), channel_id=1, source_target_pairs={{0,2},{1,3},{2,0},{3,1},{4,6},{5,7},{6,4},{7,5},{8,10},{9,11},{10,... | collective-permute-start | bytes 196616 | tf_op jit(solution)/shard_map/ppermute | solution.py:108
  64.9 5.6 %collective-permute-start.23 = (bf16[8,32,128]{2,1,0:T(8,128)(2,1)S(1)}, bf16[8,32,128]{2,1,0:T(8,128)(2,1)S(1)}, u32[]{:S(2)}, u32[]{:S(2)}) collective-permute-start(bf16[8,32,128]{2,1,0:T(8,128)(2,1)S(1)} %collective-permute-done.22.refs_1_), channel_id=1, source_target_pairs={{0,1},{1,0},{2,3},{3,2},{4,5},{5,4},{6,7},{7,6},{8,9},{9,8},{10,11... | collective-permute-start | bytes 196616 | tf_op jit(solution)/shard_map/ppermute | solution.py:571
  65.8 6.1 %collective-permute-start.20 = (bf16[8,32,128]{2,1,0:T(8,128)(2,1)S(1)}, bf16[8,32,128]{2,1,0:T(8,128)(2,1)S(1)}, u32[]{:S(2)}, u32[]{:S(2)}) collective-permute-start(bf16[8,32,128]{2,1,0:T(8,128)(2,1)S(1)} %get-tuple-element.121), channel_id=1, source_target_pairs={{0,3},{1,2},{2,1},{3,0},{4,7},{5,6},{6,5},{7,4},{8,11},{9,10},{10,... | collective-permute-start | bytes 196616 | tf_op jit(solution)/shard_map/ppermute | solution.py:112
  72.1 1.8 %collective-permute-start.26 = (bf16[48,32,128]{2,1,0:T(8,128)(2,1)S(1)}, bf16[48,32,128]{2,1,0:T(8,128)(2,1)S(1)}, u32[]{:S(2)}, u32[]{:S(2)}) collective-permute-start(bf16[48,32,128]{2,1,0:T(8,128)(2,1)S(1)} %get-tuple-element.133), channel_id=1, source_target_pairs={{0,4},{4,0},{8,12},{12,8},{16,20},{20,16},{24,28},{28,24},{1,5},{5... | collective-permute-start | bytes 1179656 | tf_op jit(solution)/shard_map/ppermute | solution.py:583
  72.6 5.2 %collective-permute-start.25 = (bf16[16,32,128]{2,1,0:T(8,128)(2,1)S(1)}, bf16[16,32,128]{2,1,0:T(8,128)(2,1)S(1)}, u32[]{:S(2)}, u32[]{:S(2)}) collective-permute-start(bf16[16,32,128]{2,1,0:T(8,128)(2,1)S(1)} %get-tuple-element.131), channel_id=1, source_target_pairs={{0,4},{4,0},{8,12},{12,8},{16,20},{20,16},{24,28},{28,24},{1,5},{5... | collective-permute-start | bytes 393224 | tf_op jit(solution)/shard_map/ppermute | solution.py:583
  73.9 7.1 %collective-permute-start.27 = (bf16[16,32,128]{2,1,0:T(8,128)(2,1)S(1)}, bf16[16,32,128]{2,1,0:T(8,128)(2,1)S(1)}, u32[]{:S(2)}, u32[]{:S(2)}) collective-permute-start(bf16[16,32,128]{2,1,0:T(8,128)(2,1)S(1)} %get-tuple-element.135), channel_id=1, source_target_pairs={{0,24},{4,28},{8,16},{12,20},{16,8},{20,12},{24,0},{28,4},{1,25},{... | collective-permute-start | bytes 393224 | tf_op jit(solution)/shard_map/ppermute | solution.py:591
  77.1 6.6 %collective-permute-start.28 = (bf16[16,32,128]{2,1,0:T(8,128)(2,1)S(1)}, bf16[16,32,128]{2,1,0:T(8,128)(2,1)S(1)}, u32[]{:S(2)}, u32[]{:S(2)}) collective-permute-start(bf16[16,32,128]{2,1,0:T(8,128)(2,1)S(1)} %get-tuple-element.136), channel_id=1, source_target_pairs={{0,16},{4,20},{8,24},{12,28},{16,0},{20,4},{24,8},{28,12},{1,17},{... | collective-permute-start | bytes 393224 | tf_op jit(solution)/shard_map/ppermute | solution.py:591
  77.1 7.0 %collective-permute-start.29 = (bf16[16,32,128]{2,1,0:T(8,128)(2,1)S(1)}, bf16[16,32,128]{2,1,0:T(8,128)(2,1)S(1)}, u32[]{:S(2)}, u32[]{:S(2)}) collective-permute-start(bf16[16,32,128]{2,1,0:T(8,128)(2,1)S(1)} %get-tuple-element.134.before_ref), channel_id=1, source_target_pairs={{0,8},{4,12},{8,0},{12,4},{16,24},{20,28},{24,16},{28,20},{1,9},{5... | collective-permute-start | bytes 393224 | tf_op jit(solution)/shard_map/ppermute | solution.py:591
